TPU v7x, 32 devices: a whole 2x2x4 slice. The times are simulated.
32 devices in a mesh: rows: 16 (over z, x, core), cols: 2 (over y).
Axes of the slice: x: 2, y: 2, z: 4, core: 2. Of those that a mesh axis runs over, the one named last changes fastest.
Arguments:
- tokens: bfloat16 [49152, 1024], P('rows', 'cols'), may hold values from -6 to 6
- doc_lengths: int32 [16, 2, 4], replicated, may hold values from 1 to 512, 1024 in all within a row
- match_picks: int32 [512, 128, 32], P('rows', 'cols'), may hold values from 0 to 4095
- labels: int32 [512], P('rows'), may hold values from 0 to 127
- w_qkv: bfloat16 [3, 1024, 1024], P(None, None, 'cols'), may hold values from -0.1875 to 0.1875
- b_qkv: float32 [3, 1024], P(None, 'cols'), may hold values from -3 to 3
- w_out: bfloat16 [1024, 1024], P('cols'), may hold values from -1.5 to 1.5
- b_out: float32 [1024], P('cols'), may hold values from -3 to 3
- ln1_gain: float32 [1024], P('cols'), may hold values from 0.5 to 1.5
- ln1_bias: float32 [1024], P('cols'), may hold values from -3 to 3
- w_up: bfloat16 [1024, 4096], P(None, 'cols'), may hold values from -0.1875 to 0.1875
- b_up: float32 [4096], P('cols'), may hold values from -3 to 3
- w_down: bfloat16 [4096, 1024], P('cols'), may hold values from -0.125 to 0.125
- b_down: float32 [1024], P('cols'), may hold values from -3 to 3
- ln2_gain: float32 [1024], P('cols'), may hold values from 0.5 to 1.5
- ln2_bias: float32 [1024], P('cols'), may hold values from -3 to 3
- w_proj: bfloat16 [1024, 128], P('cols'), may hold values from -0.1875 to 0.1875
- log_scale: float32 [1], replicated, may hold values from 1 to 1.8
Outputs:
- scores: float32 [512, 128], P('rows', 'cols')
- contrastive_loss: float32 [512], P('rows')
- tokens_grad: float32 [49152, 1024], P('rows', 'cols')
- w_qkv_grad: float32 [3, 1024, 1024], P(None, 'rows', 'cols')
- b_qkv_grad: float32 [3, 1024], P(None, ('cols', 'rows'))
- w_out_grad: float32 [1024, 1024], P('cols', 'rows')
- b_out_grad: float32 [1024], P(('cols', 'rows'))
- ln1_gain_grad: float32 [1024], P(('cols', 'rows'))
- ln1_bias_grad: float32 [1024], P(('cols', 'rows'))
- w_up_grad: float32 [1024, 4096], P('rows', 'cols')
- b_up_grad: float32 [4096], P(('cols', 'rows'))
- w_down_grad: float32 [4096, 1024], P('cols', 'rows')
- b_down_grad: float32 [1024], P(('cols', 'rows'))
- ln2_gain_grad: float32 [1024], P(('cols', 'rows'))
- ln2_bias_grad: float32 [1024], P(('cols', 'rows'))
- w_proj_grad: float32 [1024, 128], P('cols', 'rows')
- log_scale_grad: float32 [1], replicated
Inputs may be any that keep to these rules, and one draw needn't show every extreme that they name: `doc_lengths`: in each block the 4 lengths sum to 1024, and the largest of them is exactly 512.
All inputs are finite; a program needn't handle non-finite values.
Results may differ from a plain program's by a relative error of at most 0.018.
The roundings to bfloat16 on the way count: a program that leaves them out, or rounds other values in their place, can miss the bound.
Values may be sent and summed in bfloat16 or wider, within the bound.
A program may use at most 384 MiB of HBM per device.

v0:
```python
import math

import jax
import jax.numpy as jnp
from jax import lax
from jax.sharding import PartitionSpec as P

DH = 64
QLEN = 32
ROW_LEN = 1024
ABLK = 512


def combined_all(value, axis, join):
    pieces = jax.tree.map(lambda part: lax.all_gather(part, axis), value)
    head = jax.tree.map(lambda part: part[0], pieces)
    tail = jax.tree.map(lambda part: part[1:], pieces)
    subtotal, _ = lax.scan(lambda subtotal, slab: (join(subtotal, slab), None), head, tail)
    return subtotal


def full_features(part_rows):
    return lax.all_gather(part_rows, "cols", axis=1, tiled=True)


def summed_part(product_rows):
    return lax.psum_scatter(product_rows, "cols", scatter_dimension=1, tiled=True)


def row_totals(pair):
    return lax.psum(pair, "cols")


def exact_gelu(values):
    return jax.nn.gelu(values, approximate=False)


def rotary_tables(positions, head_size):
    half_size = head_size // 2
    frequency = jnp.exp(
        jnp.arange(half_size, dtype=jnp.float32) * (-2.0 * math.log(10000.0) / head_size)
    )
    angles = positions.astype(jnp.float32)[:, None] * frequency[None, :]
    return (jnp.cos(angles), jnp.sin(angles))


def rotate(values, cosine, sine_table, turn_sign):
    half_size = values.shape[-1] // 2
    first_half = values[..., :half_size]
    second = values[..., half_size:]
    cos_rows = cosine[:, None, :]
    sin_rows = turn_sign * sine_table[:, None, :]
    return jnp.concatenate(
        [first_half * cos_rows - second * sin_rows, second * cos_rows + first_half * sin_rows],
        axis=-1,
    )


def group_layout(lengths_group, row_length, query_length, shard_rows):
    query_places = jnp.arange(row_length, dtype=jnp.int32)
    doc_ends = jnp.cumsum(lengths_group, axis=1, dtype=jnp.int32)
    places = jnp.arange(shard_rows, dtype=jnp.int32)
    passed = places[None, :, None] >= doc_ends[:, None, :]
    doc_slot = jnp.sum(passed.astype(jnp.int32), axis=2, dtype=jnp.int32)
    doc_begin = jnp.sum(jnp.where(passed, lengths_group[:, None, :], 0), axis=2, dtype=jnp.int32)
    block_count = lengths_group.shape[0]
    doc_count = lengths_group.shape[1]
    doc_segment = (
        row_length // query_length
        + jnp.arange(block_count, dtype=jnp.int32)[:, None] * doc_count
        + doc_slot
    )
    segment = jnp.concatenate([query_places // query_length, doc_segment.reshape(-1)])
    position = jnp.concatenate(
        [query_places % query_length, (places[None, :] - doc_begin).reshape(-1)]
    )
    return (segment, position)


def padded_keys(keys, values, segment):
    padding = jnp.zeros((ABLK,) + keys.shape[1:], keys.dtype)
    nothing = jnp.full((ABLK,), -1, jnp.int32)
    return (
        jnp.concatenate([padding, keys, padding]),
        jnp.concatenate([padding, values, padding]),
        jnp.concatenate([nothing, segment, nothing]),
    )


def block_logits(queries, key_pad, segment, segment_pad, first_row):
    query_block = lax.dynamic_slice_in_dim(queries, first_row, ABLK, 0)
    query_segment = lax.dynamic_slice_in_dim(segment, first_row, ABLK, 0)
    key_window = lax.dynamic_slice_in_dim(key_pad, first_row, 3 * ABLK, 0)
    key_segment = lax.dynamic_slice_in_dim(segment_pad, first_row, 3 * ABLK, 0)
    logits = jnp.einsum(
        "qhd,khd->hqk", query_block, key_window, preferred_element_type=jnp.float32
    ) * DH ** (-0.5)
    logits = jnp.where((query_segment[:, None] == key_segment[None, :])[None], logits, -1e30)
    return (logits, query_block, key_window)


def attention_forward(queries, keys, values, segment):
    row_count, head_count, head_size = queries.shape
    key_pad, value_pad, segment_pad = padded_keys(keys, values, segment)

    def one_block(block_index):
        first_row = block_index * ABLK
        logits, query_block, key_window = block_logits(
            queries, key_pad, segment, segment_pad, first_row
        )
        value_window = lax.dynamic_slice_in_dim(value_pad, first_row, 3 * ABLK, 0)
        row_top = jnp.max(logits, axis=2, keepdims=True)
        weights = jnp.exp(logits - row_top)
        row_mass = jnp.sum(weights, axis=2, keepdims=True)
        result = jnp.einsum(
            "hqk,khd->qhd",
            (weights / row_mass).astype(jnp.bfloat16),
            value_window,
            preferred_element_type=jnp.float32,
        )
        return (result, (row_top + jnp.log(row_mass))[:, :, 0])

    result, log_mass = lax.map(one_block, jnp.arange(row_count // ABLK, dtype=jnp.int32))
    return (result.reshape(row_count, head_count, head_size), log_mass)


def attention_backward(queries, keys, values, segment, grad_out, log_mass):
    row_count, head_count, head_size = queries.shape
    key_pad, value_pad, segment_pad = padded_keys(keys, values, segment)
    zeros = jnp.zeros((row_count + 2 * ABLK, head_count, head_size), jnp.float32)

    def one_block(carry, block_item):
        key_grad, value_grad = carry
        block_index, block_mass = block_item
        first_row = block_index * ABLK
        logits, query_block, key_window = block_logits(
            queries, key_pad, segment, segment_pad, first_row
        )
        value_window = lax.dynamic_slice_in_dim(value_pad, first_row, 3 * ABLK, 0)
        grad_block = lax.dynamic_slice_in_dim(grad_out, first_row, ABLK, 0)
        weights = jnp.exp(logits - block_mass[:, :, None])
        flow = jnp.einsum(
            "qhd,khd->hqk", grad_block, value_window, preferred_element_type=jnp.float32
        )
        inner = jnp.sum(weights * flow, axis=2, keepdims=True)
        logit_grad = (weights * (flow - inner)).astype(jnp.bfloat16)
        query_part = jnp.einsum(
            "hqk,khd->qhd", logit_grad, key_window, preferred_element_type=jnp.float32
        ) * DH ** (-0.5)
        key_part = jnp.einsum(
            "hqk,qhd->khd", logit_grad, query_block, preferred_element_type=jnp.float32
        ) * DH ** (-0.5)
        value_part = jnp.einsum(
            "hqk,qhd->khd",
            weights.astype(jnp.bfloat16),
            grad_block,
            preferred_element_type=jnp.float32,
        )
        key_grad = lax.dynamic_update_slice_in_dim(
            key_grad,
            lax.dynamic_slice_in_dim(key_grad, first_row, 3 * ABLK, 0) + key_part,
            first_row,
            0,
        )
        value_grad = lax.dynamic_update_slice_in_dim(
            value_grad,
            lax.dynamic_slice_in_dim(value_grad, first_row, 3 * ABLK, 0) + value_part,
            first_row,
            0,
        )
        return ((key_grad, value_grad), query_part)

    (key_grad, value_grad), query_grad = lax.scan(
        one_block, (zeros, zeros), (jnp.arange(row_count // ABLK, dtype=jnp.int32), log_mass)
    )
    return (
        query_grad.reshape(row_count, head_count, head_size),
        key_grad[ABLK : ABLK + row_count],
        value_grad[ABLK : ABLK + row_count],
    )


def norm_forward(residual, norm_gain, norm_bias, full_width):
    row_sums = row_totals((jnp.sum(residual, axis=1), jnp.sum(residual * residual, axis=1)))
    row_mean = row_sums[0] / full_width
    row_var = row_sums[1] / full_width - row_mean * row_mean
    inverse = lax.rsqrt(row_var + 1e-05)
    normed = (residual - row_mean[:, None]) * inverse[:, None]
    return (normed * norm_gain + norm_bias, normed, inverse)


def norm_backward(grad_rows, normed, inverse, norm_gain, full_width):
    scaled = grad_rows * norm_gain
    row_sums = row_totals((jnp.sum(scaled, axis=1), jnp.sum(scaled * normed, axis=1)))
    residual_grad = inverse[:, None] * (
        scaled - row_sums[0][:, None] / full_width - normed * row_sums[1][:, None] / full_width
    )
    return (residual_grad, jnp.sum(grad_rows * normed, axis=0), jnp.sum(grad_rows, axis=0))


def unit_forward(embedding):
    inverse = lax.rsqrt(jnp.sum(embedding * embedding, axis=1, keepdims=True) + 1e-06)
    return (embedding * inverse, inverse)


def unit_backward(grad_rows, unit_rows, inverse):
    return inverse * (grad_rows - unit_rows * jnp.sum(grad_rows * unit_rows, axis=1, keepdims=True))


def on_device(
    tokens,
    doc_lengths,
    match_picks,
    labels,
    w_qkv,
    b_qkv,
    w_out,
    b_out,
    ln1_gain,
    ln1_bias,
    w_up,
    b_up,
    w_down,
    b_down,
    ln2_gain,
    ln2_bias,
    w_proj,
    log_scale,
):
    group_rows = tokens.shape[0]
    col_count = lax.axis_size("cols")
    row_groups = lax.axis_size("rows")
    own_width = tokens.shape[1]
    full_width = own_width * col_count
    col_index = lax.axis_index("cols")
    row_index = lax.axis_index("rows")
    local_width = w_qkv.shape[2]
    token_shape = (group_rows, local_width // DH, DH)
    shard_rows = (group_rows - ROW_LEN) // col_count
    own_lengths = lax.dynamic_index_in_dim(doc_lengths, row_index, 0, keepdims=False)
    segment, position = group_layout(own_lengths, ROW_LEN, QLEN, shard_rows)
    cosine, sine_table = rotary_tables(position, DH)
    inputs_full = full_features(tokens)
    mixed_qkv = (
        jnp.einsum("nd,tde->tne", inputs_full, w_qkv, preferred_element_type=jnp.float32)
        + b_qkv[:, None, :]
    )
    queries = rotate(mixed_qkv[0].reshape(token_shape), cosine, sine_table, 1.0).astype(
        jnp.bfloat16
    )
    keys = rotate(mixed_qkv[1].reshape(token_shape), cosine, sine_table, 1.0).astype(jnp.bfloat16)
    values = mixed_qkv[2].reshape(token_shape).astype(jnp.bfloat16)
    attended, log_mass = attention_forward(queries, keys, values, segment)
    attended_low = attended.reshape(group_rows, local_width).astype(jnp.bfloat16)
    attention_rows = jnp.dot(attended_low, w_out, preferred_element_type=jnp.float32)
    resid_one = tokens.astype(jnp.float32) + summed_part(attention_rows) + b_out
    hidden, normed_one, inverse_one = norm_forward(resid_one, ln1_gain, ln1_bias, full_width)
    hidden_low = hidden.astype(jnp.bfloat16)
    hidden_full = full_features(hidden_low)
    pre_act = jnp.dot(hidden_full, w_up, preferred_element_type=jnp.float32) + b_up
    active, gelu_pull = jax.vjp(exact_gelu, pre_act)
    active_low = active.astype(jnp.bfloat16)
    resid_two = (
        hidden
        + summed_part(jnp.dot(active_low, w_down, preferred_element_type=jnp.float32))
        + b_down
    )
    normed_out, normed_two, inverse_two = norm_forward(resid_two, ln2_gain, ln2_bias, full_width)
    output_low = normed_out.astype(jnp.bfloat16)
    embed_rows = jnp.dot(output_low, w_proj, preferred_element_type=jnp.float32)
    query_embed, doc_embed = (
        lax.psum_scatter(embed_rows[:ROW_LEN], "cols", scatter_dimension=0, tiled=True),
        lax.psum_scatter(embed_rows[ROW_LEN:], "cols", scatter_dimension=0, tiled=True),
    )
    query_unit, query_inverse = unit_forward(query_embed)
    doc_unit, doc_inverse = unit_forward(doc_embed)
    query_tile = lax.all_gather(query_unit.astype(jnp.bfloat16), "cols", axis=0, tiled=True)
    doc_tile = lax.all_gather(doc_unit.astype(jnp.bfloat16), "rows", axis=0, tiled=True)
    query_count = match_picks.shape[0]
    tile_docs = match_picks.shape[1]
    tile_rows = doc_tile.shape[0]
    doc_sizes = lax.dynamic_index_in_dim(doc_lengths, col_index, 1, keepdims=False)
    offsets = (jnp.arange(doc_sizes.shape[0], dtype=jnp.int32) * shard_rows)[:, None]
    begins = jnp.cumsum(doc_sizes, axis=1, dtype=jnp.int32) - doc_sizes + offsets
    begin_flat = begins.reshape(-1)
    size_flat = doc_sizes.reshape(-1)
    places = begin_flat[None, :, None] + match_picks % size_flat[None, :, None]
    row_ids = jnp.arange(tile_rows, dtype=jnp.int32)
    member = (row_ids[None, :] >= begin_flat[:, None]) & (
        row_ids[None, :] < (begin_flat + size_flat)[:, None]
    )
    member_float = member.astype(jnp.float32)
    member_low = member.astype(jnp.bfloat16)
    per_block = min(query_count, ABLK // QLEN)
    block_total = query_count // per_block
    block_rows = per_block * QLEN
    query_blocks = query_tile.reshape(block_total, block_rows, -1)
    place_blocks = jnp.transpose(places, (0, 2, 1)).reshape(block_total, block_rows, tile_docs)

    def match_table(matched):
        spread_match = jnp.dot(
            matched.astype(jnp.float32), member_float, precision=lax.Precision.HIGHEST
        )
        return spread_match.astype(jnp.int32) == row_ids[None, :]

    def score_block(block_item):
        vectors, matched = block_item
        sim = jnp.einsum("tp,jp->tj", vectors, doc_tile, preferred_element_type=jnp.float32)
        masked = jnp.where(match_table(matched), sim, 0.0)
        picked = jnp.einsum("tj,dj->td", masked, member_float, precision=lax.Precision.HIGHEST)
        return jnp.sum(picked.reshape(per_block, QLEN, tile_docs), axis=1)

    scores = lax.map(score_block, (query_blocks, place_blocks)).reshape(query_count, tile_docs)
    score_scale = jnp.exp(log_scale[0])
    scaled = score_scale * scores
    row_top = jnp.max(scaled, axis=1)
    row_mass = jnp.sum(jnp.exp(scaled - row_top[:, None]), axis=1)
    local_label = labels - col_index * tile_docs
    is_label = jnp.arange(tile_docs, dtype=jnp.int32)[None, :] == local_label[:, None]
    chosen = jnp.sum(jnp.where(is_label, scaled, 0.0), axis=1)

    def combine_rows(first_part, second_part):
        larger = jnp.maximum(first_part[0], second_part[0])
        joined_mass = first_part[1] * jnp.exp(first_part[0] - larger) + second_part[1] * jnp.exp(
            second_part[0] - larger
        )
        return (larger, joined_mass, first_part[2] + second_part[2])

    row_top, row_mass, chosen = combined_all((row_top, row_mass, chosen), "cols", combine_rows)
    log_total = row_top + jnp.log(row_mass)
    query_total = query_count * row_groups
    scaled_grad = (
        jnp.exp(scaled - log_total[:, None]) - is_label.astype(jnp.float32)
    ) / query_total
    score_grad = score_scale * scaled_grad
    scale_sum = lax.psum(jnp.sum(scaled_grad * scaled), ("rows", "cols"))

    def grad_block(doc_running, block_item):
        vectors, matched, weight_rows = block_item
        spread = (
            jnp.broadcast_to(weight_rows[:, None, :], (per_block, QLEN, tile_docs))
            .reshape(block_rows, tile_docs)
            .astype(jnp.bfloat16)
        )
        spread_rows = jnp.dot(spread, member_low, preferred_element_type=jnp.float32).astype(
            jnp.bfloat16
        )
        sparse = jnp.where(match_table(matched), spread_rows, jnp.zeros((), jnp.bfloat16))
        query_part = jnp.einsum("tj,jp->tp", sparse, doc_tile, preferred_element_type=jnp.float32)
        doc_running = doc_running + jnp.einsum(
            "tj,tp->jp", sparse, vectors, preferred_element_type=jnp.float32
        )
        return (doc_running, query_part)

    doc_start = jnp.zeros((tile_rows, doc_tile.shape[1]), jnp.float32)
    doc_tile_grad, query_tile_grad = lax.scan(
        grad_block,
        doc_start,
        (query_blocks, place_blocks, score_grad.reshape(block_total, per_block, tile_docs)),
    )
    query_unit_grad = lax.psum_scatter(
        query_tile_grad.reshape(query_count * QLEN, -1), "cols", scatter_dimension=0, tiled=True
    )
    doc_unit_grad = lax.psum_scatter(doc_tile_grad, "rows", scatter_dimension=0, tiled=True)
    query_embed_grad = unit_backward(query_unit_grad, query_unit, query_inverse).astype(
        jnp.bfloat16
    )
    doc_embed_grad = unit_backward(doc_unit_grad, doc_unit, doc_inverse).astype(jnp.bfloat16)
    query_full_grad, doc_full_grad = (
        lax.all_gather(query_embed_grad, "cols", axis=0, tiled=True),
        lax.all_gather(doc_embed_grad, "cols", axis=0, tiled=True),
    )
    embed_grad = jnp.concatenate([query_full_grad, doc_full_grad], axis=0)
    w_proj_grad = jnp.einsum(
        "nd,np->dp", output_low, embed_grad, preferred_element_type=jnp.float32
    )
    output_grad = jnp.einsum("np,dp->nd", embed_grad, w_proj, preferred_element_type=jnp.float32)
    resid_two_grad, gain_two_grad, bias_two_grad = norm_backward(
        output_grad, normed_two, inverse_two, ln2_gain, full_width
    )
    b_down_grad = jnp.sum(resid_two_grad, axis=0)
    down_full = full_features(resid_two_grad.astype(jnp.bfloat16))
    w_down_grad = jnp.einsum("nf,nd->fd", active_low, down_full, preferred_element_type=jnp.float32)
    pre_grad = gelu_pull(
        jnp.einsum("nd,fd->nf", down_full, w_down, preferred_element_type=jnp.float32)
    )[0].astype(jnp.bfloat16)
    b_up_grad = jnp.sum(pre_grad, axis=0, dtype=jnp.float32)
    up_inputs = full_features(hidden_low)
    w_up_grad = jnp.einsum("nd,nf->df", up_inputs, pre_grad, preferred_element_type=jnp.float32)
    hidden_grad = resid_two_grad + summed_part(
        jnp.einsum("nf,df->nd", pre_grad, w_up, preferred_element_type=jnp.float32)
    )
    resid_one_grad, gain_one_grad, bias_one_grad = norm_backward(
        hidden_grad, normed_one, inverse_one, ln1_gain, full_width
    )
    b_out_grad = jnp.sum(resid_one_grad, axis=0)
    branch_full = full_features(resid_one_grad.astype(jnp.bfloat16))
    w_out_grad = jnp.einsum(
        "ne,nd->ed", attended_low, branch_full, preferred_element_type=jnp.float32
    )
    attended_grad = (
        jnp.einsum("nd,ed->ne", branch_full, w_out, preferred_element_type=jnp.float32)
        .astype(jnp.bfloat16)
        .reshape(token_shape)
    )
    query_grad, key_grad, value_grad = attention_backward(
        queries, keys, values, segment, attended_grad, log_mass
    )
    mixed_grad = jnp.stack(
        [
            rotate(query_grad, cosine, sine_table, -1.0).reshape(group_rows, local_width),
            rotate(key_grad, cosine, sine_table, -1.0).reshape(group_rows, local_width),
            value_grad.reshape(group_rows, local_width),
        ]
    ).astype(jnp.bfloat16)
    b_qkv_grad = jnp.sum(mixed_grad, axis=1, dtype=jnp.float32)
    qkv_inputs = full_features(tokens)
    w_qkv_grad = jnp.einsum(
        "nd,tne->tde", qkv_inputs, mixed_grad, preferred_element_type=jnp.float32
    )
    tokens_grad = resid_one_grad + summed_part(
        jnp.einsum("tne,tde->nd", mixed_grad, w_qkv, preferred_element_type=jnp.float32)
    )
    summed = (
        lax.psum_scatter(w_qkv_grad, "rows", scatter_dimension=1, tiled=True),
        lax.psum_scatter(b_qkv_grad, "rows", scatter_dimension=1, tiled=True),
        lax.psum_scatter(w_out_grad, "rows", scatter_dimension=1, tiled=True),
        lax.psum_scatter(b_out_grad, "rows", scatter_dimension=0, tiled=True),
        lax.psum_scatter(gain_one_grad, "rows", scatter_dimension=0, tiled=True),
        lax.psum_scatter(bias_one_grad, "rows", scatter_dimension=0, tiled=True),
        lax.psum_scatter(w_up_grad, "rows", scatter_dimension=0, tiled=True),
        lax.psum_scatter(b_up_grad, "rows", scatter_dimension=0, tiled=True),
        lax.psum_scatter(w_down_grad, "rows", scatter_dimension=1, tiled=True),
        lax.psum_scatter(b_down_grad, "rows", scatter_dimension=0, tiled=True),
        lax.psum_scatter(gain_two_grad, "rows", scatter_dimension=0, tiled=True),
        lax.psum_scatter(bias_two_grad, "rows", scatter_dimension=0, tiled=True),
        lax.psum_scatter(w_proj_grad, "rows", scatter_dimension=1, tiled=True),
    )
    return (scores, log_total - chosen, tokens_grad) + tuple(summed) + (scale_sum.reshape(1),)


def solution(mesh):
    in_specs = (
        P("rows", "cols"),
        P(),
        P("rows", "cols", None),
        P("rows"),
        P(None, None, "cols"),
        P(None, "cols"),
        P("cols", None),
        P("cols"),
        P("cols"),
        P("cols"),
        P(None, "cols"),
        P("cols"),
        P("cols", None),
        P("cols"),
        P("cols"),
        P("cols"),
        P("cols", None),
        P(),
    )
    out_specs = (
        P("rows", "cols"),
        P("rows"),
        P("rows", "cols"),
        P(None, "rows", "cols"),
        P(None, ("cols", "rows")),
        P("cols", "rows"),
        P(("cols", "rows")),
        P(("cols", "rows")),
        P(("cols", "rows")),
        P("rows", "cols"),
        P(("cols", "rows")),
        P("cols", "rows"),
        P(("cols", "rows")),
        P(("cols", "rows")),
        P(("cols", "rows")),
        P("cols", "rows"),
        P(),
    )
    return jax.shard_map(
        on_device, mesh=mesh, in_specs=in_specs, out_specs=out_specs, check_vma=False
    )
```

profile of v0, /device:TPU:0, one launch (start us, length us, event | category | flops | bytes accessed | tf_op | source)
XLA Modules:
  0.0 3321.6 jit_solution(4974390324088313125)
XLA Ops:
  12.4 80.3 %all-gather.9.cloned.1.call-done = bf16[3072,1024]{1,0:T(8,128)(2,1)} async-done(((bf16[3072,512]{1,0:T(8,128)(2,1)}), bf16[3072,1024]{1,0:T(8,128)(2,1)}) %all-gather.9.cloned.1.call-update) | async-done | bytes 6291472 | tf_op jit(solution)/shard_map/all_gather | solution.py:23
  92.7 18.2 add_bitcast_fusion
  136.0 251.0 %while.62 = (s32[]{:T(128)}, bf16[6,512,8,64]{1,3,2,0:T(8,128)(2,1)}, f32[6,8,512]{2,1,0:T(8,128)}, s32[6]{0:T(128)S(1)}, bf16[4096,8,64]{0,2,1:T(8,128)(2,1)}, ...) while((s32[]{:T(128)}, ...), condition=%wide.region_6.7_spmd.clone, body=%wide.region_3.6_spmd.sunk.clone | while | flops 1686892544 | bytes 83518664 | solution.py:123
  138.8 14.1 fusion.258
  180.5 14.1 fusion.258
  222.3 14.1 fusion.258
  264.1 14.2 fusion.258
  305.9 14.2 fusion.258
  347.6 14.1 fusion.258
  401.0 144.5 %reduce-scatter.16.cloned.1.call-done = f32[3072,512]{1,0:T(8,128)} async-done(((f32[3072,1024]{1,0:T(8,128)}), f32[3072,512]{1,0:T(8,128)}) %reduce-scatter.16.cloned.1.call-update) | async-done | bytes 6291472 | tf_op jit(solution)/shard_map/reduce_scatter | solution.py:27
  565.5 81.6 %all-gather.11.cloned.1.call-done = bf16[3072,1024]{1,0:T(8,128)(2,1)} async-done(((bf16[3072,512]{1,0:T(8,128)(2,1)}), bf16[3072,1024]{1,0:T(8,128)(2,1)}) %all-gather.11.cloned.1.call-update) | async-done | bytes 6291472 | tf_op jit(solution)/shard_map/all_gather | solution.py:23
  647.1 70.7 %multiply_convert_fusion.1 = (bf16[3072,2048]{1,0:T(8,128)(2,1)S(1)}, f32[3072,2048]{1,0:T(8,128)}, f32[3072,2048]{1,0:T(8,128)}) fusion(f32[2048]{0:T(1024)S(1)} %copy-done.61, bf16[3072,1024]{1,0:T(8,128)(2,1)} %all-gather.11.cloned.1.call-done, bf16[1024,2048]{1,0:T(8,128)(2,1)} %param.36), kind=kOutput, calls=%fused_computation.106 | convolution fusion | flops 13300137984 | bytes 73408512 | tf_op jit(solution)/shard_map/dot_general | solution.py:260
  722.3 15.5 fusion.146
  737.8 144.5 %reduce-scatter.18.cloned.1.call-done = f32[3072,512]{1,0:T(8,128)} async-done(((f32[3072,1024]{1,0:T(8,128)}), f32[3072,512]{1,0:T(8,128)}) %reduce-scatter.18.cloned.1.call-update) | async-done | bytes 6291472 | tf_op jit(solution)/shard_map/reduce_scatter | solution.py:27
  908.3 19.6 reduce-scatter.22.cloned.1.call-done
  954.0 44.1 %all-gather.13.cloned.1.call-done = bf16[16384,128]{1,0:T(8,128)(2,1)} async-done(((bf16[1024,128]{1,0:T(8,128)(2,1)}), bf16[16384,128]{1,0:T(8,128)(2,1)}) %all-gather.13.cloned.1.call-update) | async-done | bytes 4194320 | tf_op jit(solution)/shard_map/all_gather | solution.py:278
  998.1 163.7 %while.64 = (s32[]{:T(128)}, f32[2,16,64]{2,1,0:T(8,128)S(1)}, s32[2,512,64]{2,1,0:T(8,128)}, bf16[2,512,128]{2,1,0:T(8,128)(2,1)S(1)}, bf16[16384,128]{1,0:T(8,128)(2,1)}, /*index=5*/s32[64]{0:T(128)S(1)}, s32[64]{0:T(128)S(1)}) while((s32[]{:T(128)}, f32[2,16,64]{2,1,0:T(8,128)S(1)}, s32[2,512,64]{2,1,0:T(8,128)}, ...), condition=%wide.region_24.25_spmd.clone.clone, body=%wide.region_22.24_spmd.clone.sunk.clone | while | flops 15066004480 | bytes 155604592 | solution.py:313
  998.5 34.0 %fusion.280 = f32[512,16384]{1,0:T(8,128)} fusion(s32[64]{0:T(128)S(1)} %get-tuple-element.969, s32[64]{0:T(128)S(1)} %get-tuple-element.968, s32[2,512,64]{2,1,0:T(8,128)} %get-tuple-element.965, s32[]{:T(128)} %get-tuple-element.956), kind=kOutput, calls=%fused_computation.58.clone.1.clone | convolution fusion | flops 6446678016 | bytes 33817600 | tf_op jit(solution)/shard_map/while/body/eval_jaxpr/dot_general | solution.py:301
  1045.6 34.5 %bitcast_reduce_fusion.3 = f32[16,64]{1,0:T(8,128)S(1)} fusion(s32[64]{0:T(128)S(1)} %get-tuple-element.969, s32[64]{0:T(128)S(1)} %get-tuple-element.968, f32[512,16384]{1,0:T(8,128)} %fusion.279, f32[512,16384]{1,0:T(8,128)} %fusion.280), kind=kOutput, calls=%fused_computation.67.clone.1.clone | convolution fusion | flops 6471842816 | bytes 67113472 | tf_op jit(solution)/shard_map/while/body/eval_jaxpr/tj,dj->td/dot_general | solution.py:310
  1080.1 34.0 %fusion.280 = f32[512,16384]{1,0:T(8,128)} fusion(s32[64]{0:T(128)S(1)} %get-tuple-element.969, s32[64]{0:T(128)S(1)} %get-tuple-element.968, s32[2,512,64]{2,1,0:T(8,128)} %get-tuple-element.965, s32[]{:T(128)} %get-tuple-element.956), kind=kOutput, calls=%fused_computation.58.clone.1.clone | convolution fusion | flops 6446678016 | bytes 33817600 | tf_op jit(solution)/shard_map/while/body/eval_jaxpr/dot_general | solution.py:301
  1127.2 34.5 %bitcast_reduce_fusion.3 = f32[16,64]{1,0:T(8,128)S(1)} fusion(s32[64]{0:T(128)S(1)} %get-tuple-element.969, s32[64]{0:T(128)S(1)} %get-tuple-element.968, f32[512,16384]{1,0:T(8,128)} %fusion.279, f32[512,16384]{1,0:T(8,128)} %fusion.280), kind=kOutput, calls=%fused_computation.67.clone.1.clone | convolution fusion | flops 6471842816 | bytes 67113472 | tf_op jit(solution)/shard_map/while/body/eval_jaxpr/tj,dj->td/dot_general | solution.py:310
  1172.0 130.1 %while.65 = (s32[]{:T(128)}, f32[16384,128]{1,0:T(8,128)}, f32[2,512,128]{2,1,0:T(8,128)}, s32[2,512,64]{2,1,0:T(8,128)}, bf16[2,16,64]{2,1,0:T(8,128)(2,1)S(1)}...) while((s32[]{:T(128)}, f32[16384,128]{1,0:T(8,128)}, ...), condition=%wide.region_29.30_spmd.clone.clone.clone.clone, body=%wide.region_28.29_spmd.clone.clone.clone.sunk.clone | while | flops 11857330176 | bytes 123478184 | solution.py:356
  1177.2 36.1 %fusion.290 = bf16[512,16384]{1,0:T(8,128)(2,1)} fusion(bf16[512,16384]{1,0:T(8,128)(2,1)S(1)} %convolution_convert_fusion.4, s32[64]{0:T(128)S(1)} %get-tuple-element.996, s32[64]{0:T(128)S(1)} %get-tuple-element.995, s32[2,512,64]{2,1,0:T(8,128)S(1)} %copy-done.8, s32[]{:T(128)} %get-tuple-element.979), kind=kOutput, calls=%fused_computation.79.clone.1.clone | convolution fusion | flops 6471843840 | bytes 33817604 | tf_op jit(solution)/shard_map/while/body/eval_jaxpr/dot_general | solution.py:301
  1213.2 13.7 convolution_add_fusion.3
  1240.7 36.1 %fusion.290 = bf16[512,16384]{1,0:T(8,128)(2,1)} fusion(bf16[512,16384]{1,0:T(8,128)(2,1)S(1)} %convolution_convert_fusion.4, s32[64]{0:T(128)S(1)} %get-tuple-element.996, s32[64]{0:T(128)S(1)} %get-tuple-element.995, s32[2,512,64]{2,1,0:T(8,128)S(1)} %copy-done.8, s32[]{:T(128)} %get-tuple-element.979), kind=kOutput, calls=%fused_computation.79.clone.1.clone | convolution fusion | flops 6471843840 | bytes 33817604 | tf_op jit(solution)/shard_map/while/body/eval_jaxpr/dot_general | solution.py:301
  1276.8 16.1 convolution_add_fusion.3
  1324.3 100.3 %reduce-scatter.26.cloned.1.call-done = f32[1024,128]{1,0:T(8,128)} async-done(((f32[16384,128]{1,0:T(8,128)}), f32[1024,128]{1,0:T(8,128)}) %reduce-scatter.26.cloned.1.call-update) | async-done | bytes 524304 | tf_op jit(solution)/shard_map/reduce_scatter | solution.py:364
  1465.9 79.5 %all-gather.15.cloned.1.call-done = bf16[3072,1024]{1,0:T(8,128)(2,1)} async-done(((bf16[3072,512]{1,0:T(8,128)(2,1)}), bf16[3072,1024]{1,0:T(8,128)(2,1)}) %all-gather.15.cloned.1.call-update) | async-done | bytes 6291472 | tf_op jit(solution)/shard_map/all_gather | solution.py:23
  1545.4 35.0 %convert_reduce_fusion = (f32[2048]{0:T(1024)}, bf16[3072,2048]{1,0:T(8,128)(2,1)}) fusion(f32[3072,2048]{1,0:T(8,128)} %get-tuple-element.550, bf16[3072,1024]{1,0:T(8,128)(2,1)} %all-gather.15.cloned.1.call-done, bf16[2048,1024]{1,0:T(8,128)(2,1)} %param.38, f32[3072,2048]{1,0:T(8,128)} %get-tuple-element.580, f32[2048]{0:T(1024)S(1)} %copy-done.62), kind=kOutput, calls=%fused_computation.104 | convolution fusion | flops 12991854592 | bytes 73416704 | tf_op jit(solution)/shard_map/nd,fd->nf/dot_general | solution.py:385
  1580.5 19.0 fusion.148
  1599.6 144.6 %reduce-scatter.28.cloned.1.call-done = f32[3072,512]{1,0:T(8,128)} async-done(((f32[3072,1024]{1,0:T(8,128)}), f32[3072,512]{1,0:T(8,128)}) %reduce-scatter.28.cloned.1.call-update) | async-done | bytes 6291472 | tf_op jit(solution)/shard_map/reduce_scatter | solution.py:27
  1773.7 81.6 %all-gather.17.cloned.1.call-done = bf16[3072,1024]{1,0:T(8,128)(2,1)} async-done(((bf16[3072,512]{1,0:T(8,128)(2,1)}), bf16[3072,1024]{1,0:T(8,128)(2,1)}) %all-gather.17.cloned.1.call-update) | async-done | bytes 6291472 | tf_op jit(solution)/shard_map/all_gather | solution.py:23
  1872.0 677.2 %while.63 = (s32[]{:T(128)}, f32[4096,8,64]{0,2,1:T(8,128)}, f32[4096,8,64]{0,2,1:T(8,128)}, f32[6,512,8,64]{1,0,3,2:T(8,128)}, s32[6]{0:T(128)S(1)}, /*index=5*...) while((s32[]{:T(128)}, f32[4096,8,64]{0,2,1:T(8,128)}, ...), condition=%wide.region_45.46_spmd.clone, body=%wide.region_43.45_spmd.sunk.clone | while | flops 4086558720 | bytes 215064816 | solution.py:173
  1889.5 18.3 multiply_reduce_fusion.17
  1907.8 21.4 multiply_convert_fusion.8
  1940.2 21.9 dynamic_update_slice.53
  1986.0 13.3 fusion.269
  2002.3 18.2 multiply_reduce_fusion.17
  2020.6 21.4 multiply_convert_fusion.8
  2053.0 21.9 dynamic_update_slice.53
  2115.2 18.2 multiply_reduce_fusion.17
  2133.5 21.4 multiply_convert_fusion.8
  2165.9 21.9 dynamic_update_slice.53
  2228.0 18.3 multiply_reduce_fusion.17
  2246.3 21.4 multiply_convert_fusion.8
  2278.7 21.9 dynamic_update_slice.53
  2340.8 18.2 multiply_reduce_fusion.17
  2359.0 21.4 multiply_convert_fusion.8
  2391.4 21.9 dynamic_update_slice.53
  2453.5 18.2 multiply_reduce_fusion.17
  2471.8 21.4 multiply_convert_fusion.8
  2504.2 21.9 dynamic_update_slice.53
  2596.3 16.7 fusion.116
  2622.4 15.4 convolution_bitcast_fusion.1
  2641.4 19.1 fusion.151
  2660.6 19.1 fusion.150
  2692.2 41.2 %psum.71 = f32[1]{0:T(128)} all-reduce(f32[1]{0:T(128)} %bitcast.34), channel_id=1, replica_groups=mesh['rows'=16,'cols'=2] {'rows','cols'}, use_global_device_ids=true, to_apply=%region_69.70 | all-reduce | flops 1 | bytes 8 | tf_op jit(solution)/shard_map/psum | solution.py:336
  2738.7 59.2 %all-reduce.8 = (f32[512]{0:T(512)S(1)}, f32[512]{0:T(512)S(1)}, f32[512]{0:T(512)S(1)}, f32[2048]{0:T(1024)S(1)}, f32[512]{0:T(512)S(1)}, /*index=5*/f32[512]{0:T(512)S(1)}, f32[512]{0:T(512)S(1)}) all-reduce(f32[512]{0:T(512)S(1)} %copy-done.46, f32[512]{0:T(512)S(1)} %copy-done.44, ...), channel_id=13, replica_groups=mesh['rows'=16,'cols'=2] {'rows'}, use_global_device_ids=true, to_apply=%region_52.53.clone | all-reduce | flops 5120 | bytes 40960
  2803.3 23.1 all-reduce.15.cloned.1.call-done
  2828.4 144.5 %reduce-scatter.30.cloned.1.call-done = f32[3072,512]{1,0:T(8,128)} async-done(((f32[3072,1024]{1,0:T(8,128)}), f32[3072,512]{1,0:T(8,128)}) %reduce-scatter.30.cloned.1.call-update) | async-done | bytes 6291472 | tf_op jit(solution)/shard_map/reduce_scatter | solution.py:27
  2981.8 50.4 %reduce-scatter.38.cloned.1.call-done = f32[512,8]{0,1:T(8,128)} async-done(((f32[512,128]{0,1:T(8,128)}), f32[512,8]{0,1:T(8,128)}) %reduce-scatter.38.cloned.1.call-update) | async-done | bytes 16400 | tf_op jit(solution)/shard_map/reduce_scatter | solution.py:437
  3032.2 108.2 %reduce-scatter.36.cloned.1.call-done = f32[2048,64]{0,1:T(8,128)} async-done(((f32[2048,1024]{0,1:T(8,128)}), f32[2048,64]{0,1:T(8,128)}) %reduce-scatter.36.cloned.1.call-update) | async-done | bytes 524304 | tf_op jit(solution)/shard_map/reduce_scatter | solution.py:433
  3140.3 108.9 %reduce-scatter.34.cloned.1.call-done = f32[64,2048]{1,0:T(8,128)} async-done(((f32[1024,2048]{1,0:T(8,128)}), f32[64,2048]{1,0:T(8,128)}) %reduce-scatter.34.cloned.1.call-update) | async-done | bytes 524304 | tf_op jit(solution)/shard_map/reduce_scatter | solution.py:431
  3249.2 65.6 %reduce-scatter.32.cloned.1.call-done = f32[512,64]{0,1:T(8,128)} async-done(((f32[512,1024]{0,1:T(8,128)}), f32[512,64]{0,1:T(8,128)}) %reduce-scatter.32.cloned.1.call-update) | async-done | bytes 131088 | tf_op jit(solution)/shard_map/reduce_scatter | solution.py:427
  (421 shorter events, 836.9 us)
Async XLA Ops:
  7.2 85.5 %copy-start = (bf16[3,1024,512]{2,1,0:T(8,128)(2,1)S(1)}, bf16[3,1024,512]{2,1,0:T(8,128)(2,1)}, u32[]{:S(2)}) copy-start(bf16[3,1024,512]{2,1,0:T(8,128)(2,1)} %param.30) | copy-start | bytes 9437188
  7.2 85.5 %all-gather.9.cloned.1.call-start = ((), (), s32[]{:S(2)}) async-start(), calls=%async_computation.13 | async-start | bytes 9437184 | tf_op jit(solution)/shard_map/all_gather | solution.py:23
  7.9 537.6 %reduce-scatter.16.cloned.1.call-start = ((), (), s32[]{:S(2)}) async-start(), calls=%async_computation.14 | async-start | bytes 18874368 | tf_op jit(solution)/shard_map/reduce_scatter | solution.py:27
  12.4 112.9 %copy-start.10 = (f32[3072,32]{0,1:T(8,128)}, f32[3072,32]{0,1:T(8,128)S(1)}, u32[]{:S(2)}) copy-start(f32[3072,32]{0,1:T(8,128)S(1)} %get-tuple-element.574) | copy-start | bytes 1179652
  110.9 14.4 copy-start.13
  400.9 144.6 %copy-start.54 = (f32[512]{0:T(512)S(1)}, f32[512]{0:T(512)}, u32[]{:S(2)}) copy-start(f32[512]{0:T(512)} %param.33) | copy-start | bytes 6148
  400.9 159.6 %copy-start.32 = (f32[512]{0:T(512)S(1)}, f32[512]{0:T(512)}, u32[]{:S(2)}) copy-start(f32[512]{0:T(512)} %param.34) | copy-start | bytes 6148
  400.9 159.6 %copy-start.39 = (f32[512]{0:T(512)S(1)}, f32[512]{0:T(512)}, u32[]{:S(2)}) copy-start(f32[512]{0:T(512)} %param.35) | copy-start | bytes 6148
  401.0 246.1 %all-gather.11.cloned.1.call-start = ((), (), s32[]{:S(2)}) async-start(), calls=%async_computation.15 | async-start | bytes 9437184 | tf_op jit(solution)/shard_map/all_gather | solution.py:23
  560.5 86.5 %copy-start.61 = (f32[2048]{0:T(1024)S(1)}, f32[2048]{0:T(1024)}, u32[]{:S(2)}) copy-start(f32[2048]{0:T(1024)} %param.37) | copy-start | bytes 24580
  565.4 317.0 %reduce-scatter.18.cloned.1.call-start = ((), (), s32[]{:S(2)}) async-start(), calls=%async_computation.16 | async-start | bytes 18874368 | tf_op jit(solution)/shard_map/reduce_scatter | solution.py:27
  647.1 75.2 %copy-start.59 = (bf16[2048,1024]{1,0:T(8,128)(2,1)S(1)}, bf16[2048,1024]{1,0:T(8,128)(2,1)}, u32[]{:S(2)}) copy-start(bf16[2048,1024]{1,0:T(8,128)(2,1)} %param.38) | copy-start | bytes 12582916
  737.7 144.7 %copy-start.17 = (f32[3072]{0:T(1024)S(1)}, f32[3072]{0:T(1024)}, u32[]{:S(2)}) copy-start(f32[3072]{0:T(1024)} %copy-done.16) | copy-start | bytes 36868
  737.7 144.7 %copy-start.20 = (f32[3072]{0:T(1024)S(1)}, f32[3072]{0:T(1024)}, u32[]{:S(2)}) copy-start(f32[3072]{0:T(1024)} %copy-done.19) | copy-start | bytes 36868
  737.7 144.7 %copy-start.33 = (f32[512]{0:T(512)S(1)}, f32[512]{0:T(512)}, u32[]{:S(2)}) copy-start(f32[512]{0:T(512)} %param.34) | copy-start | bytes 6148
  737.7 144.7 %copy-start.40 = (f32[512]{0:T(512)S(1)}, f32[512]{0:T(512)}, u32[]{:S(2)}) copy-start(f32[512]{0:T(512)} %param.35) | copy-start | bytes 6148
  737.7 144.7 %copy-start.55 = (f32[512]{0:T(512)S(1)}, f32[512]{0:T(512)}, u32[]{:S(2)}) copy-start(f32[512]{0:T(512)} %param.39) | copy-start | bytes 6148
  737.8 159.9 %copy-start.41 = (f32[512]{0:T(512)S(1)}, f32[512]{0:T(512)}, u32[]{:S(2)}) copy-start(f32[512]{0:T(512)} %param.40) | copy-start | bytes 6148
  737.8 159.9 %copy-start.56 = (f32[512]{0:T(512)S(1)}, f32[512]{0:T(512)}, u32[]{:S(2)}) copy-start(f32[512]{0:T(512)} %param.41) | copy-start | bytes 6148
  737.8 190.2 %reduce-scatter.22.cloned.1.call-start = ((), (), s32[]{:S(2)}) async-start(), calls=%async_computation.18 | async-start | bytes 1572864 | tf_op jit(solution)/shard_map/reduce_scatter | solution.py:273
  890.4 12.7 copy-start.24
  903.1 28.8 copy-start.36
  903.1 30.1 copy-start.63
  906.3 38.9 %reduce-scatter.20.cloned.1.call-start = ((), (), s32[]{:S(2)}) async-start(), calls=%async_computation.17 | async-start | bytes 786432 | tf_op jit(solution)/shard_map/reduce_scatter | solution.py:272
  908.3 89.8 %all-gather.13.cloned.1.call-start = ((), (), s32[]{:S(2)}) async-start(), calls=%async_computation.19 | async-start | bytes 4456448 | tf_op jit(solution)/shard_map/all_gather | solution.py:278
  931.8 383.5 %reduce-scatter.24.cloned.1.call-start = ((), (), s32[]{:S(2)}) async-start(), calls=%async_computation.20 | async-start | bytes 786432 | tf_op jit(solution)/shard_map/reduce_scatter | solution.py:361
  998.1 173.8 %copy-start.48 = (s32[2,16]{1,0:T(2,128)S(1)}, s32[2,16]{1,0:T(2,128)}, u32[]{:S(2)}) copy-start(s32[2,16]{1,0:T(2,128)} %eq.84) | copy-start | bytes 388
  998.4 34.0 %copy-start.1 = (bf16[16384,128]{1,0:T(8,128)(2,1)S(1)}, bf16[16384,128]{1,0:T(8,128)(2,1)}, u32[]{:S(2)}) copy-start(bf16[16384,128]{1,0:T(8,128)(2,1)} %get-tuple-element.967) | copy-start | bytes 12582916 | tf_op jit(solution)/shard_map/while
  1080.1 34.0 %copy-start.1 = (bf16[16384,128]{1,0:T(8,128)(2,1)S(1)}, bf16[16384,128]{1,0:T(8,128)(2,1)}, u32[]{:S(2)}) copy-start(bf16[16384,128]{1,0:T(8,128)(2,1)} %get-tuple-element.967) | copy-start | bytes 12582916 | tf_op jit(solution)/shard_map/while
  1213.2 13.7 copy-start.2
  1276.8 16.1 copy-start.2
  1302.1 13.2 copy-start.9
  1302.1 122.5 %copy-start.31 = (f32[1024]{0:T(1024)S(1)}, f32[1024]{0:T(1024)}, u32[]{:S(2)}) copy-start(f32[1024]{0:T(1024)} %copy-done.30) | copy-start | bytes 12292
  1302.1 122.5 %reduce-scatter.26.cloned.1.call-start = ((), (), s32[]{:S(2)}) async-start(), calls=%async_computation.21 | async-start | bytes 8912896 | tf_op jit(solution)/shard_map/reduce_scatter | solution.py:364
  1302.2 135.2 %copy-start.25 = (bf16[512,128]{1,0:T(8,128)(2,1)S(1)}, bf16[512,128]{1,0:T(8,128)(2,1)}, u32[]{:S(2)}) copy-start(bf16[512,128]{1,0:T(8,128)(2,1)} %param.42) | copy-start | bytes 393220
  1302.2 135.2 %copy-start.27 = (f32[3072]{0:T(1024)S(1)}, f32[3072]{0:T(1024)}, u32[]{:S(2)}) copy-start(f32[3072]{0:T(1024)} %copy-done.26) | copy-start | bytes 36868
  1302.9 242.5 %all-gather.15.cloned.1.call-start = ((), (), s32[]{:S(2)}) async-start(), calls=%async_computation.22 | async-start | bytes 9437184 | tf_op jit(solution)/shard_map/all_gather | solution.py:23
  1437.4 17.1 copy-start.29
  1437.4 17.1 copy-start.42
  1463.8 81.6 %copy-start.62 = (f32[2048]{0:T(1024)S(1)}, f32[2048]{0:T(1024)}, u32[]{:S(2)}) copy-start(f32[2048]{0:T(1024)} %param.37) | copy-start | bytes 24580
  1465.9 278.3 %reduce-scatter.28.cloned.1.call-start = ((), (), s32[]{:S(2)}) async-start(), calls=%async_computation.23 | async-start | bytes 18874368 | tf_op jit(solution)/shard_map/reduce_scatter | solution.py:27
  1599.5 144.7 %copy-start.18 = (f32[3072]{0:T(1024)S(1)}, f32[3072]{0:T(1024)}, u32[]{:S(2)}) copy-start(f32[3072]{0:T(1024)} %copy-done.16) | copy-start | bytes 36868
  1599.5 144.7 %copy-start.21 = (f32[3072]{0:T(1024)S(1)}, f32[3072]{0:T(1024)}, u32[]{:S(2)}) copy-start(f32[3072]{0:T(1024)} %copy-done.19) | copy-start | bytes 36868
  1599.5 144.7 %copy-start.34 = (f32[512]{0:T(512)S(1)}, f32[512]{0:T(512)}, u32[]{:S(2)}) copy-start(f32[512]{0:T(512)} %param.34) | copy-start | bytes 6148
  1599.5 255.7 %all-gather.17.cloned.1.call-start = ((), (), s32[]{:S(2)}) async-start(), calls=%async_computation.24 | async-start | bytes 9437184 | tf_op jit(solution)/shard_map/all_gather | solution.py:23
  1773.6 1028.3 %reduce-scatter.40.cloned.1.call-start = ((), (), s32[]{:S(2)}) async-start(), calls=%async_computation.30 | async-start | bytes 278528
  2596.2 230.2 %all-reduce.15.cloned.1.call-start = ((), (), s32[]{:S(2)}) async-start(), calls=%async_computation.31 | async-start | bytes 16777216
  2622.4 350.6 %reduce-scatter.30.cloned.1.call-start = ((), (), s32[]{:S(2)}) async-start(), calls=%async_computation.25 | async-start | bytes 18874368 | tf_op jit(solution)/shard_map/reduce_scatter | solution.py:27
  2637.9 394.3 %reduce-scatter.38.cloned.1.call-start = ((), (), s32[]{:S(2)}) async-start(), calls=%async_computation.29 | async-start | bytes 278528 | tf_op jit(solution)/shard_map/reduce_scatter | solution.py:437
  2641.4 498.9 %reduce-scatter.36.cloned.1.call-start = ((), (), s32[]{:S(2)}) async-start(), calls=%async_computation.28 | async-start | bytes 8912896 | tf_op jit(solution)/shard_map/reduce_scatter | solution.py:433
  2660.5 588.7 %reduce-scatter.34.cloned.1.call-start = ((), (), s32[]{:S(2)}) async-start(), calls=%async_computation.27 | async-start | bytes 8912896 | tf_op jit(solution)/shard_map/reduce_scatter | solution.py:431
  2679.8 11.8 copy-start.23
  2679.8 11.8 copy-start.38
  2679.8 11.8 copy-start.49
  2679.8 58.3 %copy-start.51 = (f32[2,1,32]{2,1,0:T(1,128)S(1)}, f32[2,1,32]{2,1,0:T(1,128)}, u32[]{:S(2)}) copy-start(f32[2,1,32]{2,1,0:T(1,128)} %copy-done.50) | copy-start | bytes 772
  2679.8 58.3 %copy-start.53 = (f32[2,1,32]{2,1,0:T(1,128)S(1)}, f32[2,1,32]{2,1,0:T(1,128)}, u32[]{:S(2)}) copy-start(f32[2,1,32]{2,1,0:T(1,128)} %copy-done.52) | copy-start | bytes 772
  2679.8 58.8 %copy-start.43 = (f32[512]{0:T(512)S(1)}, f32[512]{0:T(512)}, u32[]{:S(2)}) copy-start(f32[512]{0:T(512)} %get-tuple-element.541) | copy-start | bytes 6148
  2679.8 58.8 %copy-start.44 = (f32[512]{0:T(512)S(1)}, f32[512]{0:T(512)}, u32[]{:S(2)}) copy-start(f32[512]{0:T(512)} %get-tuple-element.434) | copy-start | bytes 6148
  2679.8 58.8 %copy-start.45 = (f32[512]{0:T(512)S(1)}, f32[512]{0:T(512)}, u32[]{:S(2)}) copy-start(f32[512]{0:T(512)} %get-tuple-element.439) | copy-start | bytes 6148
  2679.8 58.8 %copy-start.46 = (f32[512]{0:T(512)S(1)}, f32[512]{0:T(512)}, u32[]{:S(2)}) copy-start(f32[512]{0:T(512)} %get-tuple-element.543) | copy-start | bytes 6148
  2679.9 58.8 %copy-start.47 = (f32[2048]{0:T(1024)S(1)}, f32[2048]{0:T(1024)}, u32[]{:S(2)}) copy-start(f32[2048]{0:T(1024)} %get-tuple-element.582) | copy-start | bytes 24580
  2679.9 58.8 %copy-start.57 = (f32[512]{0:T(512)S(1)}, f32[512]{0:T(512)}, u32[]{:S(2)}) copy-start(f32[512]{0:T(512)} %get-tuple-element.432) | copy-start | bytes 6148
  2679.9 58.8 %copy-start.58 = (f32[512]{0:T(512)S(1)}, f32[512]{0:T(512)}, u32[]{:S(2)}) copy-start(f32[512]{0:T(512)} %get-tuple-element.438) | copy-start | bytes 6148
  2679.9 635.0 %reduce-scatter.32.cloned.1.call-start = ((), (), s32[]{:S(2)}) async-start(), calls=%async_computation.26 | async-start | bytes 2228224 | tf_op jit(solution)/shard_map/reduce_scatter | solution.py:427
  (24 other events, 96.1 us)
Sparse Core Ops, SparseCore 0:
  9.6 83.0 all-gather.8
  401.1 144.4 reduce-scatter.15
  565.5 81.5 all-gather.10
  737.9 144.4 reduce-scatter.17
  906.5 21.4 reduce-scatter.21
  930.7 14.5 reduce-scatter.19
  947.5 50.5 all-gather.12
  1302.3 13.0 reduce-scatter.23
  1320.0 104.6 reduce-scatter.25
  1466.0 79.3 all-gather.14
  1599.7 144.4 reduce-scatter.27
  1773.7 81.4 all-gather.16
  2596.4 55.2 reduce-scatter.39
  2655.7 170.6 all-reduce.14
  2828.6 144.3 reduce-scatter.29
  2976.9 55.2 reduce-scatter.37
  3036.7 103.6 reduce-scatter.35
  3144.8 104.3 reduce-scatter.33
  3253.5 61.2 reduce-scatter.31
where the time goes:
time: 3340 us; the launch traced here: 3320 us
  waiting for transfers between devices  1440 us (43%)
  matrix products  1100 us (33%)
  other arithmetic  325 us (10%)
  local copies, waits for them, and re-layouts  266 us (8%)
  blocking collectives  164 us (5%)
    reduce_scatter x4, waiting for transfers between devices, summed_part(): lax.psum_scatter(product_rows, 'cols', scatter_dimension=1, tiled=True)  578 us
    all_gather x4, waiting for transfers between devices, full_features(): return lax.all_gather(part_rows, 'cols', axis=1, tiled=True)  323 us
    dot_general x12, matrix products, block_logits(): jnp.einsum('qhd,khd->hqk', query_block, key_window, preferred_element_typ...  194 us
    dynamic_update_slice x12, local copies, waits for them, and re-layouts, attention_forward(): lax.map(one_block, jnp.arange(row_count // ABLK, dtype=jnp.int32))  144 us
    dot_general x4, matrix products, match_table(): jnp.dot(matched.astype(jnp.float32), member_float, precision=lax.Precisio...  140 us
    convert_element_type x6, other arithmetic, one_block(): logit_grad = (weights * (flow - inner)).astype(jnp.bfloat16)  128 us
    reduce_scatter x1, waiting for transfers between devices, on_device(): lax.psum_scatter(w_up_grad, 'rows', scatter_dimension=0, tiled=True)  109 us
    reduce_scatter x1, waiting for transfers between devices, on_device(): lax.psum_scatter(w_down_grad, 'rows', scatter_dimension=1, tiled=True)  108 us
  transfers between devices with their start and end apart: 19, of which 18 were waited for; matrix products, arithmetic and copies ran while one was open for 4% of the time, Pallas kernels for 0%

commit v1 on v0

v1 whole, which is shorter than its diff:
```python
import functools
import math

import jax
import jax.numpy as jnp
from jax import lax
from jax.experimental import pallas as pl
from jax.experimental.pallas import tpu as pltpu
from jax.sharding import PartitionSpec as P

DH = 64
QLEN = 32
ROW_LEN = 1024
F32 = jnp.float32
BF16 = jnp.bfloat16
VMEM_LIMIT = 56 * 1024 * 1024
NT = (((1,), (1,)), ((), ()))
NN = (((1,), (0,)), ((), ()))
TN = (((0,), (0,)), ((), ()))


def mm(left, right, dims=NN):
    return lax.dot_general(left, right, dims, preferred_element_type=F32)


def swap_halves(block):
    lane = lax.broadcasted_iota(jnp.int32, block.shape, 1)
    return jnp.where((lane & 32) == 0, pltpu.roll(block, 96, 1), pltpu.roll(block, 32, 1))


def half_lanes(block, head):
    lane = lax.broadcasted_iota(jnp.int32, block.shape, 1)
    return jnp.where((lane >= 64) == (head == 1), block, jnp.zeros_like(block))


def scaled(block):
    return (block.astype(F32) * DH**-0.5).astype(BF16)


def query_mask(size):
    down = lax.broadcasted_iota(jnp.int32, (size, size), 0) // QLEN
    across = lax.broadcasted_iota(jnp.int32, (size, size), 1) // QLEN
    return down == across


def attend_tile(keys, values_t, query_tile, mask):
    outs, masses = [], []
    for head in range(2):
        logits = mm(keys, half_lanes(query_tile, head), NT)
        logits = jnp.where(mask, logits, -1e30)
        top = jnp.max(logits, axis=0, keepdims=True)
        weights = jnp.exp(logits - top)
        mass = jnp.sum(weights, axis=0, keepdims=True)
        probs = (weights * (1.0 / mass)).astype(BF16)
        outs.append(mm(values_t[head * DH : (head + 1) * DH], probs))
        masses.append(top + jnp.log(mass))
    return jnp.concatenate(outs, axis=0).T.astype(BF16), masses


def attention_forward_kernel(
    q_ref, k_ref, v_ref, cos_ref, sin_ref, segc_ref, segr_ref,
    qo_ref, ko_ref, out_ref, qlse_ref, dlse_ref, *, q_rows, q_tile, d_tile,
):
    rows = q_ref.shape[0]
    d_rows = rows - q_rows

    @pl.loop(0, rows // q_tile)
    def _(step):
        at = pl.ds(pl.multiple_of(step * q_tile, q_tile), q_tile)
        for src, dst in ((q_ref, qo_ref), (k_ref, ko_ref)):
            block = src[at, :]
            dst[at, :] = (block * cos_ref[at, :] + swap_halves(block) * sin_ref[at, :]).astype(BF16)

    @pl.loop(0, q_rows // q_tile)
    def _(step):
        at = pl.ds(pl.multiple_of(step * q_tile, q_tile), q_tile)
        values_t = v_ref[at, :].astype(F32).T.astype(BF16)
        out, masses = attend_tile(ko_ref[at, :], values_t, scaled(qo_ref[at, :]), query_mask(q_tile))
        out_ref[at, :] = out
        for head in range(2):
            qlse_ref[0, step, head : head + 1, :] = masses[head]

    keys = ko_ref[q_rows:, :]
    values_t = v_ref[q_rows:, :].astype(F32).T.astype(BF16)
    seg_keys = segc_ref[...]

    @pl.loop(0, d_rows // d_tile)
    def _(step):
        at = pl.ds(pl.multiple_of(q_rows + step * d_tile, q_tile), d_tile)
        mask = seg_keys == segr_ref[step]
        out, masses = attend_tile(keys, values_t, scaled(qo_ref[at, :]), mask)
        out_ref[at, :] = out
        for head in range(2):
            dlse_ref[0, step, head : head + 1, :] = masses[head]


def grad_tile(keys, keys_t, values, query_tile, grad_out, mask, masses):
    probs, flows, query_heads, grad_heads, dq = [], [], [], [], []
    for head in range(2):
        query_head = half_lanes(query_tile, head)
        grad_head = half_lanes(grad_out, head)
        logits = jnp.where(mask, mm(keys, query_head, NT), -1e30)
        weights = jnp.exp(logits - masses[head])
        flow = mm(values, grad_head, NT)
        inner = jnp.sum(weights * flow, axis=0, keepdims=True)
        slope = (weights * (flow - inner)).astype(BF16)
        dq.append(mm(keys_t[head * DH : (head + 1) * DH], slope))
        probs.append(weights.astype(BF16))
        flows.append(slope)
        query_heads.append(query_head)
        grad_heads.append(grad_head)
    dv = mm(jnp.concatenate(probs, axis=1), jnp.concatenate(grad_heads, axis=0))
    dk = mm(jnp.concatenate(flows, axis=1), jnp.concatenate(query_heads, axis=0))
    return jnp.concatenate(dq, axis=0).T, dk, dv


def attention_backward_kernel(
    q_ref, k_ref, v_ref, g_ref, cos_ref, sin_ref, segc_ref, segr_ref, qlse_ref, dlse_ref,
    out_ref, sum_ref, dq_ref, dk_ref, dv_ref, *, q_rows, q_tile, d_tile,
):
    rows = q_ref.shape[0]
    d_rows = rows - q_rows

    @pl.loop(0, q_rows // q_tile)
    def _(step):
        at = pl.ds(pl.multiple_of(step * q_tile, q_tile), q_tile)
        keys = k_ref[at, :]
        keys_t = scaled(keys).astype(F32).T.astype(BF16)
        masses = [qlse_ref[0, step, head : head + 1, :] for head in range(2)]
        dq, dk, dv = grad_tile(
            keys, keys_t, v_ref[at, :], scaled(q_ref[at, :]), g_ref[at, :],
            query_mask(q_tile), masses,
        )
        dq_ref[at, :] = dq
        dk_ref[at, :] = dk
        dv_ref[at, :] = dv

    keys = k_ref[q_rows:, :]
    keys_t = scaled(keys).astype(F32).T.astype(BF16)
    values = v_ref[q_rows:, :]
    seg_keys = segc_ref[...]
    dk_ref[q_rows:, :] = jnp.zeros((d_rows, 128), F32)
    dv_ref[q_rows:, :] = jnp.zeros((d_rows, 128), F32)

    @pl.loop(0, d_rows // d_tile)
    def _(step):
        at = pl.ds(pl.multiple_of(q_rows + step * d_tile, q_tile), d_tile)
        mask = seg_keys == segr_ref[step]
        masses = [dlse_ref[0, step, head : head + 1, :] for head in range(2)]
        dq, dk, dv = grad_tile(
            keys, keys_t, values, scaled(q_ref[at, :]), g_ref[at, :], mask, masses
        )
        dq_ref[at, :] = dq
        dk_ref[q_rows:, :] += dk
        dv_ref[q_rows:, :] += dv

    def finish(step, sums):
        at = pl.ds(pl.multiple_of(step * q_tile, q_tile), q_tile)
        cosine, sine = cos_ref[at, :], sin_ref[at, :]
        added = []
        for which, src in enumerate((dq_ref, dk_ref, dv_ref)):
            block = src[at, :]
            if which < 2:
                block = block * cosine - swap_halves(block) * sine
            low = block.astype(BF16)
            out_ref[which, at, :] = low
            added.append(sums[which] + jnp.sum(low.astype(F32), axis=0, keepdims=True))
        return tuple(added)

    zero = jnp.zeros((1, 128), F32)
    sums = lax.fori_loop(0, rows // q_tile, finish, (zero, zero, zero))
    sum_ref[0] = jnp.concatenate(sums + (jnp.zeros((5, 128), F32),), axis=0)


def attention_sizes(rows, q_rows):
    q_tile = min(128, q_rows)
    return dict(q_rows=q_rows, q_tile=q_tile, d_tile=min(256, rows - q_rows))


def attention_forward(q_mixed, k_mixed, values, cosine, sine, seg_col, seg_row, q_rows):
    rows, width = q_mixed.shape
    sizes = attention_sizes(rows, q_rows)
    pairs = width // 128
    q_steps, d_steps = q_rows // sizes["q_tile"], (rows - q_rows) // sizes["d_tile"]
    wide = pl.BlockSpec((rows, 128), lambda i: (0, i))
    fixed = pl.BlockSpec((rows, 128), lambda i: (0, 0))
    q_mass = pl.BlockSpec((1, q_steps, 2, sizes["q_tile"]), lambda i: (i, 0, 0, 0))
    d_mass = pl.BlockSpec((1, d_steps, 2, sizes["d_tile"]), lambda i: (i, 0, 0, 0))
    low = jax.ShapeDtypeStruct((rows, width), BF16)
    return pl.pallas_call(
        functools.partial(attention_forward_kernel, **sizes),
        grid=(pairs,),
        in_specs=[
            wide, wide, wide, fixed, fixed,
            pl.BlockSpec(seg_col.shape, lambda i: (0, 0)),
            pl.BlockSpec(seg_row.shape, lambda i: (0, 0, 0)),
        ],
        out_specs=[wide, wide, wide, q_mass, d_mass],
        out_shape=[
            low, low, low,
            jax.ShapeDtypeStruct((pairs, q_steps, 2, sizes["q_tile"]), F32),
            jax.ShapeDtypeStruct((pairs, d_steps, 2, sizes["d_tile"]), F32),
        ],
        compiler_params=pltpu.CompilerParams(vmem_limit_bytes=VMEM_LIMIT),
        cost_estimate=pl.CostEstimate(
            flops=20_000_000_000, bytes_accessed=30_000_000, transcendentals=0
        ),
        name="attention_forward",
    )(q_mixed, k_mixed, values, cosine, sine, seg_col, seg_row)


def attention_backward(queries, keys, values, grads, cosine, sine, seg_col, seg_row, masses, q_rows):
    rows, width = queries.shape
    sizes = attention_sizes(rows, q_rows)
    pairs = width // 128
    q_steps, d_steps = q_rows // sizes["q_tile"], (rows - q_rows) // sizes["d_tile"]
    wide = pl.BlockSpec((rows, 128), lambda i: (0, i))
    fixed = pl.BlockSpec((rows, 128), lambda i: (0, 0))
    q_mass = pl.BlockSpec((1, q_steps, 2, sizes["q_tile"]), lambda i: (i, 0, 0, 0))
    d_mass = pl.BlockSpec((1, d_steps, 2, sizes["d_tile"]), lambda i: (i, 0, 0, 0))
    return pl.pallas_call(
        functools.partial(attention_backward_kernel, **sizes),
        grid=(pairs,),
        in_specs=[
            wide, wide, wide, wide, fixed, fixed,
            pl.BlockSpec(seg_col.shape, lambda i: (0, 0)),
            pl.BlockSpec(seg_row.shape, lambda i: (0, 0, 0)),
            q_mass, d_mass,
        ],
        out_specs=[
            pl.BlockSpec((3, rows, 128), lambda i: (0, 0, i)),
            pl.BlockSpec((1, 8, 128), lambda i: (i, 0, 0)),
        ],
        out_shape=[
            jax.ShapeDtypeStruct((3, rows, width), BF16),
            jax.ShapeDtypeStruct((pairs, 8, 128), F32),
        ],
        scratch_shapes=[pltpu.VMEM((rows, 128), F32)] * 3,
        compiler_params=pltpu.CompilerParams(vmem_limit_bytes=VMEM_LIMIT),
        cost_estimate=pl.CostEstimate(
            flops=60_000_000_000, bytes_accessed=30_000_000, transcendentals=0
        ),
        name="attention_backward",
    )(queries, keys, values, grads, cosine, sine, seg_col, seg_row, *masses)


STRIP = 32


def score_kernel(begin_ref, size_ref, doc_ref, query_ref, pick_ref, out_ref, sim_ref):
    group = pl.program_id(0)
    docs, width = pick_ref.shape[1:]
    chunk = min(256, doc_ref.shape[0])

    @pl.loop(0, doc_ref.shape[0] // chunk)
    def _(step):
        at = pl.ds(pl.multiple_of(step * chunk, chunk), chunk)
        sim_ref[at, :] = mm(doc_ref[at, :], query_ref[...], NT)

    for doc in range(docs):
        begin = begin_ref[group * docs + doc]
        end = begin + size_ref[group * docs + doc]
        pick = pick_ref[0, doc : doc + 1, :]

        def strip(step, total):
            first = pl.multiple_of(step * STRIP, STRIP)
            row = lax.broadcasted_iota(jnp.int32, (STRIP, width), 0) + first
            held = jnp.where(row == pick, sim_ref[pl.ds(first, STRIP), :], 0.0)
            return total + jnp.sum(held.reshape(STRIP // 8, 8, width), axis=0)

        total = lax.fori_loop(
            begin // STRIP, (end + STRIP - 1) // STRIP, strip, jnp.zeros((8, width), F32)
        )
        out_ref[0, doc : doc + 1, :] = jnp.sum(total, axis=0, keepdims=True)


def score_grad_kernel(
    begin_ref, size_ref, doc_ref, query_ref, pick_ref, weight_ref, doc_out, query_out, sparse_ref
):
    group = pl.program_id(0)
    docs, width = pick_ref.shape[1:]
    doc_rows = doc_ref.shape[0]

    @pl.loop(0, doc_rows // STRIP)
    def _(step):
        first = pl.multiple_of(step * STRIP, STRIP)
        row = lax.broadcasted_iota(jnp.int32, (STRIP, width), 0) + first
        low = jnp.int32(0)
        high = jnp.int32(0)
        for doc in range(docs):
            begin = begin_ref[group * docs + doc]
            end = begin + size_ref[group * docs + doc]
            low += (end <= first).astype(jnp.int32)
            high += (begin < first + STRIP).astype(jnp.int32)

        def one_doc(doc, held):
            pick = pick_ref[0, pl.ds(doc, 1), :]
            return jnp.where(row == pick, weight_ref[0, pl.ds(doc, 1), :], held)

        held = lax.fori_loop(low, high, one_doc, jnp.zeros((STRIP, width), F32))
        sparse_ref[pl.ds(first, STRIP), :] = held.astype(BF16)

    docs_t = doc_ref[...].astype(F32).T.astype(BF16)
    doc_out[...] = mm(sparse_ref[...], query_ref[...])

    @pl.when(group == 0)
    def _():
        query_out[...] = jnp.zeros_like(query_out)

    query_out[...] += mm(docs_t, sparse_ref[...])


def score_specs(doc_tile, query_tile, picks):
    groups, docs, width = picks.shape
    doc_rows = doc_tile.shape[0] // groups
    return (
        pl.BlockSpec((doc_rows, 128), lambda i, *_: (i, 0)),
        pl.BlockSpec(query_tile.shape, lambda i, *_: (0, 0)),
        pl.BlockSpec((1, docs, width), lambda i, *_: (i, 0, 0)),
    )


def score_forward(begins, sizes, doc_tile, query_tile, picks):
    groups, docs, width = picks.shape
    doc_spec, query_spec, pick_spec = score_specs(doc_tile, query_tile, picks)
    return pl.pallas_call(
        score_kernel,
        grid_spec=pltpu.PrefetchScalarGridSpec(
            num_scalar_prefetch=2,
            grid=(groups,),
            in_specs=[doc_spec, query_spec, pick_spec],
            out_specs=pick_spec,
            scratch_shapes=[pltpu.VMEM((doc_tile.shape[0] // groups, width), F32)],
        ),
        out_shape=jax.ShapeDtypeStruct((groups, docs, width), F32),
        compiler_params=pltpu.CompilerParams(vmem_limit_bytes=VMEM_LIMIT),
        name="score_forward",
    )(begins, sizes, doc_tile, query_tile, picks)


def score_backward(begins, sizes, doc_tile, query_tile, picks, weights):
    groups, docs, width = picks.shape
    doc_spec, query_spec, pick_spec = score_specs(doc_tile, query_tile, picks)
    return pl.pallas_call(
        score_grad_kernel,
        grid_spec=pltpu.PrefetchScalarGridSpec(
            num_scalar_prefetch=2,
            grid=(groups,),
            in_specs=[doc_spec, query_spec, pick_spec, pick_spec],
            out_specs=[doc_spec, pl.BlockSpec((128, width), lambda i, *_: (0, 0))],
            scratch_shapes=[pltpu.VMEM((doc_tile.shape[0] // groups, width), BF16)],
        ),
        out_shape=[
            jax.ShapeDtypeStruct(doc_tile.shape, F32),
            jax.ShapeDtypeStruct((128, width), F32),
        ],
        compiler_params=pltpu.CompilerParams(vmem_limit_bytes=VMEM_LIMIT),
        name="score_backward",
    )(begins, sizes, doc_tile, query_tile, picks, weights)


def rotary_tables(position):
    half_size = DH // 2
    frequency = jnp.exp(
        jnp.arange(half_size, dtype=F32) * (-2.0 * math.log(10000.0) / DH)
    )
    angles = position.astype(F32)[:, None] * frequency[None, :]
    cosine, sine = jnp.cos(angles), jnp.sin(angles)
    return (
        jnp.concatenate([cosine] * 4, axis=1),
        jnp.concatenate([-sine, sine, -sine, sine], axis=1),
    )


def norm_forward(residual, gain, bias):
    mean = jnp.mean(residual, axis=1, keepdims=True)
    centred = residual - mean
    inverse = lax.rsqrt(jnp.mean(centred * centred, axis=1, keepdims=True) + 1e-05)
    normed = centred * inverse
    return normed * gain + bias, normed, inverse


def norm_backward(grad_rows, normed, inverse, gain):
    spread = grad_rows * gain
    grad = inverse * (
        spread
        - jnp.mean(spread, axis=1, keepdims=True)
        - normed * jnp.mean(spread * normed, axis=1, keepdims=True)
    )
    return grad, jnp.sum(grad_rows * normed, axis=0), jnp.sum(grad_rows, axis=0)


def on_device(
    tokens,
    doc_lengths,
    match_picks,
    labels,
    w_qkv,
    b_qkv,
    w_out,
    b_out,
    ln1_gain,
    ln1_bias,
    w_up,
    b_up,
    w_down,
    b_down,
    ln2_gain,
    ln2_bias,
    w_proj,
    log_scale,
):
    C = lax.axis_size("cols")
    R = lax.axis_size("rows")
    c = lax.axis_index("cols")
    r = lax.axis_index("rows")
    width = tokens.shape[1]
    D = width * C
    Q = ROW_LEN // C
    DS = (tokens.shape[0] - ROW_LEN) // C
    n = Q + DS

    def shift_cols(value, k):
        return lax.ppermute(value, "cols", [(i, (i + k) % C) for i in range(C)])

    def swap_rows(value, bit):
        return lax.ppermute(value, "rows", [(i, i ^ bit) for i in range(R)])

    def in_order(slots):
        if len(slots) == 1:
            return slots
        if len(slots) == 2:
            return [lax.select(c == 0, slots[0], slots[1]), lax.select(c == 0, slots[1], slots[0])]
        stacked = jnp.stack(slots)
        return [
            lax.dynamic_index_in_dim(stacked, (c - j) % C, 0, keepdims=False) for j in range(C)
        ]

    parts = jnp.concatenate(
        [tokens[:ROW_LEN].reshape(C, Q, width), tokens[ROW_LEN:].reshape(C, DS, width)], axis=1
    )

    def part(k):
        return lax.dynamic_index_in_dim(parts, (c + k) % C, 0, keepdims=False)

    slots = [part(0)] + [shift_cols(part(k), k) for k in range(1, C)]
    x = jnp.concatenate(in_order(slots), axis=1)

    def gather_slots(shard):
        flat = shard.reshape(-1, shard.shape[-1])
        piece = lax.dynamic_index_in_dim(
            flat.reshape(R, flat.shape[0] // R, flat.shape[1]), r, 0, keepdims=False
        )
        others = [
            lax.all_gather(shift_cols(piece, k), "rows", axis=0, tiled=True).reshape(shard.shape)
            for k in range(1, C)
        ]
        return [shard] + others

    wqkv_slots = gather_slots(w_qkv)
    wout_slots = gather_slots(w_out)
    wup_slots = gather_slots(w_up)
    wdown_slots = gather_slots(w_down)
    wproj = lax.all_gather(w_proj, "cols", axis=0, tiled=True)

    vectors = [b_qkv.reshape(-1), b_up, b_out, ln1_gain, ln1_bias, b_down, ln2_gain, ln2_bias]
    spread = lax.all_gather(jnp.concatenate(vectors), "cols", axis=0)
    ends = [0]
    for vector in vectors:
        ends.append(ends[-1] + vector.shape[0])

    def of_slot(which, k):
        row = lax.dynamic_index_in_dim(spread, (c - k) % C, 0, keepdims=False)
        return row[ends[which] : ends[which + 1]]

    def whole(which):
        return spread[:, ends[which] : ends[which + 1]].reshape(-1)

    bqkv_slots = [of_slot(0, k).reshape(b_qkv.shape) for k in range(C)]
    bup_slots = [of_slot(1, k) for k in range(C)]
    bout, gain1, bias1, bdown, gain2, bias2 = [whole(which) for which in range(2, 8)]

    own_sizes = lax.dynamic_index_in_dim(
        lax.dynamic_index_in_dim(doc_lengths, r, 0, keepdims=False), c, 0, keepdims=False
    )
    own_ends = jnp.cumsum(own_sizes)
    places = jnp.arange(DS, dtype=jnp.int32)
    passed = places[:, None] >= own_ends[None, :]
    slot_id = jnp.sum(passed.astype(jnp.int32), axis=1)
    slot_begin = jnp.sum(jnp.where(passed, own_sizes[None, :], 0), axis=1)
    position = jnp.concatenate([jnp.arange(Q, dtype=jnp.int32) % QLEN, places - slot_begin])
    cosine, sine = rotary_tables(position)
    d_tile = attention_sizes(n, Q)["d_tile"]
    seg_col = slot_id[:, None]
    seg_row = slot_id.reshape(DS // d_tile, 1, d_tile)

    def project(which):
        return jnp.concatenate(
            [mm(x, wqkv_slots[k][which]) + bqkv_slots[k][which] for k in range(C)], axis=1
        )

    values = project(2).astype(BF16)
    queries, keys, attended, *masses = attention_forward(
        project(0), project(1), values, cosine, sine, seg_col, seg_row, Q
    )

    def slot_of(array, k):
        size = array.shape[1] // C
        return array[:, k * size : (k + 1) * size]

    resid_one = x.astype(F32) + bout
    for k in range(C):
        resid_one = resid_one + mm(slot_of(attended, k), wout_slots[k])
    hidden, normed_one, inverse_one = norm_forward(resid_one, gain1, bias1)
    hidden_low = hidden.astype(BF16)
    pre = [mm(hidden_low, wup_slots[k]) + bup_slots[k] for k in range(C)]
    active = [jax.nn.gelu(p, approximate=False).astype(BF16) for p in pre]
    resid_two = hidden + bdown
    for k in range(C):
        resid_two = resid_two + mm(active[k], wdown_slots[k])
    normed_out, normed_two, inverse_two = norm_forward(resid_two, gain2, bias2)
    output_low = normed_out.astype(BF16)
    embedding = mm(output_low, wproj)
    inverse_unit = lax.rsqrt(jnp.sum(embedding * embedding, axis=1, keepdims=True) + 1e-06)
    unit = embedding * inverse_unit
    unit_low = unit.astype(BF16)

    doc_tile = lax.all_gather(unit_low[Q:], "rows", axis=0, tiled=True)
    query_tile = lax.all_gather(unit_low[:Q], "cols", axis=0, tiled=True)
    queries_here, tile_docs, _ = match_picks.shape
    docs = own_sizes.shape[0]
    sizes = lax.dynamic_index_in_dim(doc_lengths, c, 1, keepdims=False)
    begins = jnp.cumsum(sizes, axis=1) - sizes
    sizes_flat, begins_flat = sizes.reshape(-1), begins.reshape(-1)
    picks = jnp.transpose(match_picks, (1, 0, 2)).reshape(tile_docs, queries_here * QLEN)
    picks = begins_flat[:, None] + picks % sizes_flat[:, None]
    picks = picks.reshape(R, docs, queries_here * QLEN)
    sims = score_forward(begins_flat, sizes_flat, doc_tile, query_tile, picks)
    scores = jnp.sum(sims.reshape(tile_docs, queries_here, QLEN), axis=2).T

    scale = jnp.exp(log_scale[0])
    z = scale * scores
    row_top = jnp.max(z, axis=1)
    row_mass = jnp.sum(jnp.exp(z - row_top[:, None]), axis=1)
    is_label = (
        jnp.arange(tile_docs, dtype=jnp.int32)[None, :] == (labels - c * tile_docs)[:, None]
    )
    chosen = jnp.sum(jnp.where(is_label, z, 0.0), axis=1)
    stats = lax.all_gather(jnp.stack([row_top, row_mass, chosen]), "cols", axis=0)
    top_all = jnp.max(stats[:, 0], axis=0)
    mass_all = jnp.sum(stats[:, 1] * jnp.exp(stats[:, 0] - top_all), axis=0)
    log_total = top_all + jnp.log(mass_all)
    loss = log_total - jnp.sum(stats[:, 2], axis=0)
    dz = (jnp.exp(z - log_total[:, None]) - is_label.astype(F32)) / (queries_here * R)
    scale_sum = lax.psum(jnp.sum(dz * z), ("rows", "cols"))
    dscores = (scale * dz).astype(BF16).astype(F32)
    weights = jnp.broadcast_to(
        dscores.T[:, :, None], (tile_docs, queries_here, QLEN)
    ).reshape(R, docs, queries_here * QLEN)
    doc_grad, query_grad_t = score_backward(
        begins_flat, sizes_flat, doc_tile, query_tile, picks, weights
    )
    query_grad = lax.psum_scatter(query_grad_t.T, "cols", scatter_dimension=0, tiled=True)

    def halve(total, bit):
        size = total.shape[0] // 2
        pairs = total.reshape((size, 2) + total.shape[1:])
        mine = (r // bit) % 2
        send = lax.dynamic_index_in_dim(pairs, 1 - mine, 1, keepdims=False).astype(BF16)
        keep = lax.dynamic_index_in_dim(pairs, mine, 1, keepdims=False)
        return keep + swap_rows(send, bit).astype(F32)

    doc_sum = doc_grad.reshape(R, DS, 128)
    bit = 1
    while bit < R:
        doc_sum = halve(doc_sum, bit)
        bit *= 2
    unit_grad = jnp.concatenate([query_grad, doc_sum[0]], axis=0)
    embed_grad = (
        inverse_unit * (unit_grad - unit * jnp.sum(unit_grad * unit, axis=1, keepdims=True))
    ).astype(BF16)

    def weight_grad(left, right_slots):
        share = left.shape[1] // R
        split = left.reshape(n, R // 2, 2, share)
        own = lax.dynamic_index_in_dim(split, r % 2, 2, keepdims=False).reshape(n, -1)
        other = lax.dynamic_index_in_dim(split, 1 - r % 2, 2, keepdims=False).reshape(n, -1)
        arrived = [swap_rows(mm(other, right, TN).astype(BF16), 1) for right in right_slots]
        sums = [
            mm(own, right, TN) + came.astype(F32) for right, came in zip(right_slots, arrived)
        ]
        total = sums[0]
        for k in range(1, C):
            total = total + shift_cols(sums[k].astype(BF16), C - k).astype(F32)
        total = total.reshape(R // 2, share, -1)
        bit = 2
        while bit < R:
            total = halve(total, bit)
            bit *= 2
        return total[0]

    proj_grad = mm(output_low, embed_grad, TN)
    proj_grad = proj_grad.reshape(C, width, R, -1).transpose(0, 2, 1, 3).reshape(C * R, -1)
    proj_grad = lax.psum_scatter(proj_grad, ("cols", "rows"), scatter_dimension=0, tiled=True)
    output_grad = mm(embed_grad, wproj, NT)
    resid_two_grad, gain2_grad, bias2_grad = norm_backward(
        output_grad, normed_two, inverse_two, gain2
    )
    bdown_grad = jnp.sum(resid_two_grad, axis=0)
    branch = resid_two_grad.astype(BF16)
    down_grad = weight_grad(branch, active)
    pre_grad = []
    for k in range(C):
        _, pull = jax.vjp(functools.partial(jax.nn.gelu, approximate=False), pre[k])
        pre_grad.append(pull(mm(branch, wdown_slots[k], NT))[0].astype(BF16))
    bup_grad = [jnp.sum(g.astype(F32), axis=0) for g in pre_grad]
    up_grad = weight_grad(hidden_low, pre_grad)
    hidden_grad = resid_two_grad
    for k in range(C):
        hidden_grad = hidden_grad + mm(pre_grad[k], wup_slots[k], NT)
    resid_one_grad, gain1_grad, bias1_grad = norm_backward(
        hidden_grad, normed_one, inverse_one, gain1
    )
    bout_grad = jnp.sum(resid_one_grad, axis=0)
    branch_one = resid_one_grad.astype(BF16)
    out_grad = weight_grad(branch_one, [slot_of(attended, k) for k in range(C)])
    attended_grad = jnp.concatenate(
        [mm(branch_one, wout_slots[k], NT).astype(BF16) for k in range(C)], axis=1
    )
    mixed_grad, mixed_sums = attention_backward(
        queries, keys, values, attended_grad, cosine, sine, seg_col, seg_row, masses, Q
    )
    tokens_part = resid_one_grad
    for k in range(C):
        for which in range(3):
            tokens_part = tokens_part + mm(
                slot_of(mixed_grad[which], k), wqkv_slots[k][which], NT
            )
    blocks = tokens_part.reshape(n, C, width)

    def block(k):
        return lax.dynamic_index_in_dim(blocks, (c + k) % C, 1, keepdims=False)

    slots = [block(0)] + [
        shift_cols(block(k).astype(BF16), k).astype(F32) for k in range(1, C)
    ]
    ordered = in_order(slots)
    tokens_grad = jnp.concatenate([s[:Q] for s in ordered] + [s[Q:] for s in ordered], axis=0)
    qkv_grad = jnp.stack(
        [
            weight_grad(x, [slot_of(mixed_grad[which], k) for k in range(C)])
            for which in range(3)
        ]
    )

    def canonical(slot_list):
        return jnp.concatenate(in_order(slot_list), axis=-1)

    bqkv_sums = mixed_sums[:, :3].transpose(1, 0, 2).reshape(3, D)
    bqkv_grad = canonical([slot_of(bqkv_sums, k) for k in range(C)])
    small = jnp.concatenate(
        [g.reshape(C * R, -1) for g in bqkv_grad]
        + [
            g.reshape(C * R, -1)
            for g in (
                canonical(bup_grad), bout_grad, gain1_grad, bias1_grad,
                bdown_grad, gain2_grad, bias2_grad,
            )
        ],
        axis=1,
    )
    small = lax.psum_scatter(small, ("cols", "rows"), scatter_dimension=0, tiled=True)[0]
    one = D // (C * R)
    up_part = bup_grad[0].shape[0] // R
    bounds = [3 * one, 3 * one + up_part]
    for _ in range(6):
        bounds.append(bounds[-1] + one)
    pieces = [small[: bounds[0]].reshape(3, one)] + [
        small[a:b] for a, b in zip(bounds[:-1], bounds[1:])
    ]
    (bqkv_out, bup_out, bout_out, gain1_out, bias1_out, bdown_out, gain2_out, bias2_out) = pieces
    return (
        scores,
        loss,
        tokens_grad,
        qkv_grad,
        bqkv_out,
        out_grad.T,
        bout_out,
        gain1_out,
        bias1_out,
        up_grad,
        bup_out,
        down_grad.T,
        bdown_out,
        gain2_out,
        bias2_out,
        proj_grad.reshape(width, -1),
        scale_sum.reshape(1),
    )


def solution(mesh):
    in_specs = (
        P("rows", "cols"),
        P(),
        P("rows", "cols", None),
        P("rows"),
        P(None, None, "cols"),
        P(None, "cols"),
        P("cols", None),
        P("cols"),
        P("cols"),
        P("cols"),
        P(None, "cols"),
        P("cols"),
        P("cols", None),
        P("cols"),
        P("cols"),
        P("cols"),
        P("cols", None),
        P(),
    )
    out_specs = (
        P("rows", "cols"),
        P("rows"),
        P("rows", "cols"),
        P(None, "rows", "cols"),
        P(None, ("cols", "rows")),
        P("cols", "rows"),
        P(("cols", "rows")),
        P(("cols", "rows")),
        P(("cols", "rows")),
        P("rows", "cols"),
        P(("cols", "rows")),
        P("cols", "rows"),
        P(("cols", "rows")),
        P(("cols", "rows")),
        P(("cols", "rows")),
        P("cols", "rows"),
        P(),
    )
    return jax.shard_map(
        on_device, mesh=mesh, in_specs=in_specs, out_specs=out_specs, check_vma=False
    )
```

time: 3340 us -> 1270 us (0.38)
  waiting for transfers between devices: 1440 us -> 286 us
  matrix products: 1100 us -> 325 us
  Pallas kernels: 0 us -> 290 us
  other arithmetic: 325 us -> 67.6 us
  local copies, waits for them, and re-layouts: 266 us -> 94.9 us
  starting transfers between devices: 1 us -> 49.7 us
  blocking collectives: 164 us -> 129 us
    reduce_scatter x12 -> x1, waiting for transfers between devices: 1050 us -> 0.02 us  [on_device(): lax.psum_scatter(query_grad_t.T, 'cols', scatter_dimension=0, tiled=True)]
    dot_general x71 -> x51, matrix products: 1100 us -> 325 us  [mm(): return lax.dot_general(left, right, dims, preferred_element_type=F32)]
    all_gather x5, waiting for transfers between devices: 367 us -> 34 us  [the longest x1 34 us: on_device(): doc_tile = lax.all_gather(unit_low[Q:], 'rows', axis=0, tiled=True)]
    pallas_call x0 -> x4, Pallas kernels: none -> 290 us  [the longest x1 106 us: attention_backward(): pl.pallas_call(functools.partial(attention_backward_kernel, **sizes), gri...]
    ppermute x0 -> x46, waiting for transfers between devices: none -> 219 us  [the longest x12 118 us: shift_cols(): return lax.ppermute(value, 'cols', [(i, (i + k) % C) for i in range(C)])]
    dynamic_update_slice x14 -> x0, local copies, waits for them, and re-layouts: 144 us -> none  [the longest x12 144 us: attention_forward(): lax.map(one_block, jnp.arange(row_count // ABLK, dtype=jnp.int32))]
    convert_element_type x15 -> x8, other arithmetic: 147 us -> 5.07 us  [the longest x1 1.42 us: on_device(): embed_grad = (inverse_unit * (unit_grad - unit * jnp.sum(unit_grad * unit...]
    reduce_sum x19 -> x10, other arithmetic: 121 us -> 9.38 us  [the longest x1 2.97 us: on_device(): bdown_grad = jnp.sum(resid_two_grad, axis=0)]
  transfers between devices with their start and end apart: 19 -> 53, of which waited for: 18 -> 27; matrix products, arithmetic and copies ran while one was open for 4% -> 22% of each run, Pallas kernels for 0% -> 8%
where the time goes in v1:
time: 1270 us; the launch traced here: 1260 us
  matrix products  325 us (26%)
  Pallas kernels  290 us (23%)
  waiting for transfers between devices  286 us (23%)
  blocking collectives  129 us (10%)
  local copies, waits for them, and re-layouts  94.9 us (7%)
  other arithmetic  67.6 us (5%)
  starting transfers between devices  49.7 us (4%)
  between operations  17 us (1%)
    dot_general x51, matrix products, mm(): return lax.dot_general(left, right, dims, preferred_element_type=F32)  325 us
    ppermute x12, waiting for transfers between devices, shift_cols(): return lax.ppermute(value, 'cols', [(i, (i + k) % C) for i in range(C)])  118 us
    pallas_call x1, Pallas kernels, attention_backward(): pl.pallas_call(functools.partial(attention_backward_kernel, **sizes), gri...  106 us
    ppermute x34, waiting for transfers between devices, swap_rows(): return lax.ppermute(value, 'rows', [(i, i ^ bit) for i in range(R)])  101 us
    pallas_call x1, Pallas kernels, attention_forward(): pl.pallas_call(functools.partial(attention_forward_kernel, **sizes), grid...  99.7 us
    pallas_call x1, Pallas kernels, score_backward(): pl.pallas_call(score_grad_kernel, grid_spec=pltpu.PrefetchScalarGridSpec(...  52.6 us
    unnamed x1, blocking collectives  41.6 us
    psum x1, blocking collectives, on_device(): scale_sum = lax.psum(jnp.sum(dz * z), ('rows', 'cols'))  38.7 us
  transfers between devices with their start and end apart: 53, of which 27 were waited for; matrix products, arithmetic and copies ran while one was open for 22% of the time, Pallas kernels for 8%

profile of v1, /device:TPU:0, one launch (start us, length us, event | category | flops | bytes accessed | tf_op | source)
XLA Modules:
  0.0 1259.0 jit_solution(17020910795452900226)
XLA Ops:
  11.4 4.9 collective-permute-done.1
  24.9 4.6 collective-permute-done.3
  43.7 32.6 %all-gather.2 = f32[2,1,6656]{2,1,0:T(1,128)S(1)} all-gather(f32[1,1,6656]{2,1,0:T(1,128)S(1)} %reshape.501), channel_id=2, replica_groups=mesh['rows'=16,'cols'=2] {'cols'}, dimensions={0}, use_global_device_ids=true | all-gather | bytes 79872 | tf_op jit(solution)/shard_map/all_gather | solution.py:467
  80.0 6.1 all_gather.39
  104.9 4.1 fusion.14
  123.9 99.7 %attention_forward.1 = (bf16[1536,1024]{1,0:T(8,128)(2,1)}, bf16[1536,1024]{1,0:T(8,128)(2,1)}, bf16[1536,1024]{1,0:T(8,128)(2,1)}, f32[8,4,2,128]{3,2,1,0:T(2,128)}, f32[8,4,2,256]{3,2,1,0:T(2,128)}) custom-call(f32[1536,1024]{1,0:T(8,128)} %pad_maximum_fusion.q_ref, f32[1536,1024]{1,0:T(8,128)} %pad_maximum_fusion.1.k_ref, ...), custom_call_target="tpu_custom_call" | custom-call | flops 20000000000 | bytes 30000000 | tf_op jit(solution)/shard_map/attention_forward/pallas_call | solution.py:190
  223.7 6.0 fusion.60
  229.7 6.6 fusion.110
  241.8 35.6 %multiply_convert_fusion.1 = (bf16[1536,2048]{1,0:T(8,128)(2,1)S(1)}, f32[1536,2048]{1,0:T(8,128)}, f32[1536,2048]{1,0:T(8,128)}) fusion(f32[2048]{0:T(1024)S(1)} %bitcast.432, bf16[1536,1024]{0,1:T(8,128)(2,1)S(1)} %fusion.12, bf16[1024,2048]{1,0:T(8,128)(2,1)S(1)} %copy-done.75), kind=kOutput, calls=%fused_computation.21 | convolution fusion | flops 6650068992 | bytes 38805504 | tf_op jit(solution)/shard_map/dot_general | solution.py:23
  280.0 8.9 fusion.112
  289.0 36.9 %multiply_convert_fusion = (bf16[1536,2048]{1,0:T(8,128)(2,1)}, f32[1536,2048]{1,0:T(8,128)}, f32[1536,2048]{1,0:T(8,128)}) fusion(f32[2048]{0:T(1024)S(1)} %bitcast.430, bf16[1536,1024]{0,1:T(8,128)(2,1)} %copy-done.17, bf16[1024,2048]{1,0:T(8,128)(2,1)} %all-gather.14.cloned.1.call-done), kind=kOutput, calls=%fused_computation.8 | convolution fusion | flops 6650068992 | bytes 38805504 | tf_op jit(solution)/shard_map/dot_general | solution.py:23
  325.9 15.5 %fusion.111 = (f32[1536]{0:T(1024)S(1)}, f32[1536,1024]{0,1:T(8,128)S(1)}) fusion(bf16[1536,2048]{1,0:T(8,128)(2,1)} %get-tuple-element.166, bf16[2048,1024]{1,0:T(8,128)(2,1)} %all-gather.16.cloned.1.call-done, f32[1536,1024]{0,1:T(8,128)} %fusion.112, f32[1024]{0:T(1024)S(1)} %bitcast.435, f32[1024]{0:T(1024)S(1)} %bitcast.425, f32[1024]{0:T(1024)S(1)} %bitcast.413, ...), kind=kOutput, calls=%fused_computation.336 | convolution fusion | flops 6455032320 | bytes 29390848 | tf_op jit(solution)/shard_map/dot_general | solution.py:23
  352.2 6.8 fusion.86.pick_ref
  359.1 5.8 all_gather.41.query_ref
  364.8 34.0 %all-gather.18.cloned.1.call-done.doc_ref = bf16[16384,128]{1,0:T(8,128)(2,1)} async-done(((bf16[1024,128]{1,0:T(8,128)(2,1)}), bf16[16384,128]{1,0:T(8,128)(2,1)}) %all-gather.18.cloned.1.call-update) | async-done | bytes 4194320 | tf_op jit(solution)/shard_map/all_gather | solution.py:528
  398.8 31.9 %score_forward.1 = f32[16,4,1024]{2,1,0:T(4,128)} custom-call(s32[64]{0:T(128)} %sub.169.begin_ref, s32[64]{0:T(128)} %copy-done.86, bf16[16384,128]{1,0:T(8,128)(2,1)} %all-gather.18.cloned.1.call-done.doc_ref, bf16[1024,128]{1,0:T(8,128)(2,1)} %all_gather.41.query_ref, s32[16,4,1024]{2,1,0:T(4,128)} %fusion.86.pick_ref), custom_call_target="tpu_custom_call" | custom-call | tf_op jit(solution)/shard_map/score_forward/pallas_call | solution.py:326
  432.5 4.3 all-gather.3
  438.9 52.6 %score_backward.1 = (f32[16384,128]{1,0:T(8,128)}, f32[128,1024]{1,0:T(8,128)}) custom-call(s32[64]{0:T(128)} %sub.169.begin_ref, s32[64]{0:T(128)} %copy-done.86, bf16[16384,128]{1,0:T(8,128)(2,1)} %all-gather.18.cloned.1.call-done.doc_ref, bf16[1024,128]{1,0:T(8,128)(2,1)} %all_gather.41.query_ref, s32[16,4,1024]{2,1,0:T(4,128)} %fusion.86.pick_ref, ...), custom_call_target="tpu_custom_call" | custom-call | tf_op jit(solution)/shard_map/score_backward/pallas_call | solution.py:344
  491.5 3.8 fusion.15
  495.4 4.5 collective-permute-done.5
  507.3 24.4 %collective-permute-done.6 = bf16[4,1024,128]{2,1,0:T(8,128)(2,1)} collective-permute-done((bf16[4,1024,128]{2,1,0:T(8,128)(2,1)}, bf16[4,1024,128]{2,1,0:T(8,128)(2,1)}, u32[]{:S(2)}, u32[]{:S(2)}) %collective-permute-start.6) | collective-permute-done | bytes 1048608 | tf_op jit(solution)/shard_map/ppermute | solution.py:427
  539.9 8.8 collective-permute-done.7
  554.6 38.7 %psum.7 = f32[1]{0:T(128)} all-reduce(f32[1]{0:T(128)} %bitcast.121), channel_id=1, replica_groups=mesh['rows'=16,'cols'=2] {'rows','cols'}, use_global_device_ids=true, to_apply=%region_33.34 | all-reduce | flops 1 | bytes 8 | tf_op jit(solution)/shard_map/psum | solution.py:555
  600.1 5.5 multiply_reduce_fusion
  612.6 4.7 convolution_convert_fusion
  617.3 4.6 convolution_convert_fusion.1
  622.0 18.5 %convert_reduce_fusion.1 = (f32[2048]{0:T(1024)}, bf16[1536,2048]{1,0:T(8,128)(2,1)}) fusion(f32[1536,2048]{1,0:T(8,128)} %get-tuple-element.169, f32[1536,2048]{1,0:T(8,128)} %get-tuple-element.220, f32[2048]{0:T(1024)S(1)} %bitcast.433, bf16[1536,1024]{0,1:T(8,128)(2,1)S(1)} %convert_element_type.401, bf16[2048,1024]{1,0:T(8,128)(2,1)} %param.30), kind=kOutput, calls=%fused_computation.5 | convolution fusion | flops 6495926272 | bytes 38813696 | tf_op jit(solution)/shard_map/dot_general | solution.py:23
  640.5 12.4 fusion.113
  652.8 4.8 convolution_convert_fusion.3
  657.6 18.5 %convert_reduce_fusion = (f32[2048]{0:T(1024)}, bf16[1536,2048]{1,0:T(8,128)(2,1)}) fusion(f32[1536,2048]{1,0:T(8,128)} %get-tuple-element.167, f32[1536,2048]{1,0:T(8,128)} %get-tuple-element.221, f32[2048]{0:T(1024)S(1)} %bitcast.431, bf16[1536,1024]{0,1:T(8,128)(2,1)S(1)} %convert_element_type.401, bf16[2048,1024]{1,0:T(8,128)(2,1)} %all-gather.16.cloned.1.call-done), kind=kOutput, calls=%fused_computation.4 | convolution fusion | flops 6495926272 | bytes 38813696 | tf_op jit(solution)/shard_map/dot_general | solution.py:23
  676.1 7.5 convolution_convert_fusion.2
  683.6 16.8 %multiply_reduce_fusion.1 = (f32[1024]{0:T(1024)S(1)}, f32[1536]{0:T(1024)S(1)}, f32[1536]{0:T(1024)S(1)}, f32[1024]{0:T(1024)S(1)}, f32[1536,1024]{0,1:T(8,128)S(1)}) fusion(f32[1536,1024]{0,1:T(8,128)} %copy-done.1, f32[1536]{0:T(1024)S(1)} %copy-done.63, f32[1536]{0:T(1024)S(1)} %copy-done.60, f32[1024]{0:T(1024)S(1)} %bitcast.414, ...), kind=kOutput, calls=%fused_computation.40 | convolution fusion | flops 6459747328 | bytes 35688448 | tf_op jit(solution)/shard_map/dot_general | solution.py:23
  711.3 105.9 %attention_backward.1 = (bf16[3,1536,1024]{2,1,0:T(8,128)(2,1)}, f32[8,8,128]{2,1,0:T(8,128)}) custom-call(bf16[1536,1024]{1,0:T(8,128)(2,1)} %get-tuple-element.29.q_ref, bf16[1536,1024]{1,0:T(8,128)(2,1)} %get-tuple-element.30.k_ref, bf16[1536,1024]{1,0:T(8,128)(2,1)} %pad_maximum_fusion.4.v_ref, bf16[1536,1024]{1,0:T(8,128)(2,1)} %pad_maximum_fusion.5.g_ref, ...), custom_call_target="tpu_custom_call" | custom-call | flops 60000002048 | bytes 30000000 | tf_op jit(solution)/shard_map/attention_backward/pallas_call | solution.py:221
  817.2 4.6 slice_bitcast_fusion
  839.1 4.4 fusion.41
  843.6 4.5 fusion.46
  848.1 4.5 fusion.51
  853.0 4.5 copy.226
  857.5 5.9 reshape.496
  863.7 7.8 fusion.115
  871.5 7.9 fusion.114
  880.1 41.6 %all-reduce = f32[32,416]{1,0:T(8,128)S(1)} all-reduce(f32[32,416]{1,0:T(8,128)S(1)} %concatenate.65), channel_id=5, replica_groups=mesh['rows'=16,'cols'=2] {'cols','rows'}, use_global_device_ids=true, to_apply=%region_30.31.clone | all-reduce | flops 13312 | bytes 106496
  930.8 4.5 fusion.31
  935.3 4.5 fusion.36
  939.8 16.4 %add_add_fusion = f32[1536,1024]{0,1:T(8,128)} fusion(f32[1536,1024]{0,1:T(8,128)} %fusion.31, f32[1536,1024]{0,1:T(8,128)} %fusion.36, f32[1536,1024]{0,1:T(8,128)} %fusion.41, f32[1536,1024]{0,1:T(8,128)} %fusion.46, f32[1536,1024]{0,1:T(8,128)} %copy-done.3, f32[1536,1024]{0,1:T(8,128)} %fusion.51, bf16[1536,1024]{1,0:T(8,128)(2,1)S(1)} %copy-done.21, ...), kind=kOutput, calls=%fused_computation.41 | convolution fusion | flops 1620049920 | bytes 46661632 | tf_op jit(solution)/shard_map/dot_general | solution.py:23
  965.6 32.8 %all-reduce.4.cloned.1.call-done = f32[32,4096]{0,1:T(8,128)} async-done(((f32[32,4096]{0,1:T(8,128)}), f32[32,4096]{0,1:T(8,128)}) %all-reduce.4.cloned.1.call-update) | async-done | bytes 524304
  1014.3 9.1 collective-permute-done.24
  1025.2 9.5 collective-permute-done.12
  1036.6 9.4 collective-permute-done.18
  1047.8 8.6 collective-permute-done.30
  1058.8 6.7 collective-permute-done.13
  1067.1 4.1 collective-permute-done.19
  1081.4 4.4 collective-permute-done.14
  1087.2 4.7 collective-permute-done.20
  1093.4 3.9 collective-permute-done.32
  1098.8 4.4 collective-permute-done.27
  1104.0 4.8 collective-permute-done.15
  1117.1 6.0 add_convert_fusion.4
  1126.9 37.4 %collective-permute-done.42 = bf16[512,2048]{1,0:T(8,128)(2,1)S(1)} collective-permute-done((bf16[512,2048]{1,0:T(8,128)(2,1)S(1)}, bf16[512,2048]{1,0:T(8,128)(2,1)S(1)}, u32[]{:S(2)}, u32[]{:S(2)}) %collective-permute-start.42) | collective-permute-done | bytes 2097184 | tf_op jit(solution)/shard_map/ppermute | solution.py:424
  1166.9 31.8 %collective-permute-done.36 = bf16[512,2048]{1,0:T(8,128)(2,1)} collective-permute-done((bf16[512,2048]{1,0:T(8,128)(2,1)}, bf16[512,2048]{1,0:T(8,128)(2,1)}, u32[]{:S(2)}, u32[]{:S(2)}) %collective-permute-start.36) | collective-permute-done | bytes 2097184 | tf_op jit(solution)/shard_map/ppermute | solution.py:424
  1208.3 6.6 copy.228
  1223.6 7.4 collective-permute-done.44
  1232.6 8.9 collective-permute-done.38
  1242.9 8.2 collective-permute-done.39
  (550 shorter events, 245.9 us)
Async XLA Ops:
  7.2 97.6 %all-gather.10.cloned.1.call-start = ((), (), s32[]{:S(2)}) async-start(), calls=%async_computation.1 | async-start | bytes 3342336 | tf_op jit(solution)/shard_map/all_gather | solution.py:455
  8.4 7.9 collective-permute-start.1
  17.0 212.7 %all-gather.12.cloned.1.call-start = ((), (), s32[]{:S(2)}) async-start(), calls=%async_computation.2 | async-start | bytes 1114112 | tf_op jit(solution)/shard_map/all_gather | solution.py:455
  17.1 4.3 collective-permute-start.2
  22.1 266.9 %all-gather.14.cloned.1.call-start = ((), (), s32[]{:S(2)}) async-start(), calls=%async_computation.3 | async-start | bytes 4456448 | tf_op jit(solution)/shard_map/all_gather | solution.py:455
  23.1 6.4 collective-permute-start.3
  30.2 295.6 %all-gather.16.cloned.1.call-start = ((), (), s32[]{:S(2)}) async-start(), calls=%async_computation.4 | async-start | bytes 4456448 | tf_op jit(solution)/shard_map/all_gather | solution.py:455
  31.3 60.0 %collective-permute-start.4 = (bf16[128,1024]{1,0:T(8,128)(2,1)S(1)}, bf16[128,1024]{1,0:T(8,128)(2,1)}, u32[]{:S(2)}, u32[]{:S(2)}) collective-permute-start(bf16[128,1024]{1,0:T(8,128)(2,1)S(1)} %dynamic-slice_bitcast_fusion), channel_id=1, source_target_pairs={{0,1},{1,0},{2,3},{3,2},{4,5},{5,4},{6,7},{7,6},{8,9},{9,8},{10,11... | collective-permute-start | bytes 786440 | tf_op jit(solution)/shard_map/ppermute | solution.py:424
  42.9 49.0 %collective-permute-start = (bf16[1536,512]{0,1:T(8,128)(2,1)}, bf16[1536,512]{0,1:T(8,128)(2,1)}, u32[]{:S(2)}, u32[]{:S(2)}) collective-permute-start(bf16[1536,512]{0,1:T(8,128)(2,1)} %fusion.18), channel_id=1, source_target_pairs={{0,1},{1,0},{2,3},{3,2},{4,5},{5,4},{6,7},{7,6},{8,9},{9,8},{10,11... | collective-permute-start | bytes 4718600 | tf_op jit(solution)/shard_map/ppermute | solution.py:424
  77.6 159.4 %copy-start.72 = (f32[1,4,2,128]{3,1,2,0:T(4,128)}, f32[1,4,2,128]{3,1,2,0:T(4,128)S(1)}, u32[]{:S(2)}) copy-start(f32[1,4,2,128]{3,1,2,0:T(4,128)S(1)} %copy.254) | copy-start | bytes 12292
  77.6 159.4 %copy-start.65 = (f32[1,4,2,128]{3,1,2,0:T(4,128)}, f32[1,4,2,128]{3,1,2,0:T(4,128)S(1)}, u32[]{:S(2)}) copy-start(f32[1,4,2,128]{3,1,2,0:T(4,128)S(1)} %copy.253) | copy-start | bytes 12292
  78.2 160.9 %copy-start.82 = (f32[1,2048]{1,0:T(1,128)}, f32[1,2048]{1,0:T(1,128)S(1)}, u32[]{:S(2)}) copy-start(f32[1,2048]{1,0:T(1,128)S(1)} %slice.299) | copy-start | bytes 24580
  91.3 307.5 %all-gather.18.cloned.1.call-start = ((), (), s32[]{:S(2)}) async-start(), calls=%async_computation.5 | async-start | bytes 4456448 | tf_op jit(solution)/shard_map/all_gather | solution.py:528
  239.1 38.4 %copy-start.17 = (bf16[1536,1024]{0,1:T(8,128)(2,1)}, bf16[1536,1024]{0,1:T(8,128)(2,1)S(1)}, u32[]{:S(2)}) copy-start(bf16[1536,1024]{0,1:T(8,128)(2,1)S(1)} %fusion.12) | copy-start | bytes 9437188
  241.8 38.2 %copy-start.74 = (bf16[2048,1024]{1,0:T(8,128)(2,1)S(1)}, bf16[2048,1024]{1,0:T(8,128)(2,1)}, u32[]{:S(2)}) copy-start(bf16[2048,1024]{1,0:T(8,128)(2,1)} %param.30) | copy-start | bytes 12582916
  288.9 36.9 %copy-start.59 = (f32[1536]{0:T(1024)S(1)}, f32[1536]{0:T(1024)}, u32[]{:S(2)}) copy-start(f32[1536]{0:T(1024)} %copy-done.58) | copy-start | bytes 18436
  288.9 36.9 %copy-start.62 = (f32[1536]{0:T(1024)S(1)}, f32[1536]{0:T(1024)}, u32[]{:S(2)}) copy-start(f32[1536]{0:T(1024)} %copy-done.61) | copy-start | bytes 18436
  346.9 248.1 %reduce-scatter.3.cloned.1.call-start = ((), (), s32[]{:S(2)}) async-start(), calls=%async_computation.6 | async-start | bytes 786432 | tf_op jit(solution)/shard_map/reduce_scatter | solution.py:563
  348.4 50.4 %copy-start.86 = (s32[64]{0:T(128)}, s32[64]{0:T(128)S(1)}, u32[]{:S(2)}) copy-start(s32[64]{0:T(128)S(1)} %squeeze.213.size_ref) | copy-start | bytes 772
  495.4 4.5 collective-permute-start.5
  506.1 25.5 %collective-permute-start.6 = (bf16[4,1024,128]{2,1,0:T(8,128)(2,1)}, bf16[4,1024,128]{2,1,0:T(8,128)(2,1)}, u32[]{:S(2)}, u32[]{:S(2)}) collective-permute-start(bf16[4,1024,128]{2,1,0:T(8,128)(2,1)} %fusion.62), channel_id=1, source_target_pairs={{0,4},{2,6},{4,0},{6,2},{8,12},{10,14},{12,8},{14,10},{16,20},{18,... | collective-permute-start | bytes 3145736 | tf_op jit(solution)/shard_map/ppermute | solution.py:427
  535.2 13.5 %collective-permute-start.7 = (bf16[2,1024,128]{2,1,0:T(8,128)(2,1)}, bf16[2,1024,128]{2,1,0:T(8,128)(2,1)}, u32[]{:S(2)}, u32[]{:S(2)}) collective-permute-start(bf16[2,1024,128]{2,1,0:T(8,128)(2,1)} %fusion.85), channel_id=1, source_target_pairs={{0,8},{2,10},{4,12},{6,14},{8,0},{10,2},{12,4},{14,6},{16,24},{18,... | collective-permute-start | bytes 1572872 | tf_op jit(solution)/shard_map/ppermute | solution.py:427
  539.8 458.6 %all-reduce.4.cloned.1.call-start = ((), (), s32[]{:S(2)}) async-start(), calls=%async_computation.7 | async-start | bytes 4194304
  550.2 43.8 %collective-permute-start.8 = (bf16[1,1024,128]{2,1,0:T(8,128)(2,1)S(1)}, bf16[1,1024,128]{2,1,0:T(8,128)(2,1)}, u32[]{:S(2)}, u32[]{:S(2)}) collective-permute-start(bf16[1,1024,128]{2,1,0:T(8,128)(2,1)S(1)} %dynamic-slice_convert_fusion.6), channel_id=1, source_target_pairs={{0,16},{2,18},{4,20},{6,22},{8,24},{10,26},{12,28},{14,30},{16,0},... | collective-permute-start | bytes 786440 | tf_op jit(solution)/shard_map/ppermute | solution.py:427
  871.5 244.1 %collective-permute-start.35 = (bf16[512,2048]{1,0:T(8,128)(2,1)}, bf16[512,2048]{1,0:T(8,128)(2,1)}, u32[]{:S(2)}, u32[]{:S(2)}) collective-permute-start(bf16[512,2048]{1,0:T(8,128)(2,1)} %convolution_convert_fusion.2), channel_id=1, source_target_pairs={{0,2},{2,0},{4,6},{6,4},{8,10},{10,8},{12,14},{14,12},{16,18},{18,... | collective-permute-start | bytes 6291464 | tf_op jit(solution)/shard_map/ppermute | solution.py:427
  923.0 79.7 %collective-permute-start.11 = (bf16[512,512]{1,0:T(8,128)(2,1)}, bf16[512,512]{1,0:T(8,128)(2,1)}, u32[]{:S(2)}, u32[]{:S(2)}) collective-permute-start(bf16[512,512]{1,0:T(8,128)(2,1)} %convolution_convert_fusion.12), channel_id=1, source_target_pairs={{0,2},{2,0},{4,6},{6,4},{8,10},{10,8},{12,14},{14,12},{16,18},{18,... | collective-permute-start | bytes 1572872 | tf_op jit(solution)/shard_map/ppermute | solution.py:427
  923.0 100.7 %collective-permute-start.10 = (bf16[512,512]{1,0:T(8,128)(2,1)}, bf16[512,512]{1,0:T(8,128)(2,1)S(1)}, u32[]{:S(2)}, u32[]{:S(2)}) collective-permute-start(bf16[512,512]{1,0:T(8,128)(2,1)} %convolution_convert_fusion.13), channel_id=1, source_target_pairs={{0,2},{2,0},{4,6},{6,4},{8,10},{10,8},{12,14},{14,12},{16,18},{18,... | collective-permute-start | bytes 1572872 | tf_op jit(solution)/shard_map/ppermute | solution.py:427
  923.5 85.1 %collective-permute-start.17 = (bf16[512,512]{1,0:T(8,128)(2,1)}, bf16[512,512]{1,0:T(8,128)(2,1)}, u32[]{:S(2)}, u32[]{:S(2)}) collective-permute-start(bf16[512,512]{1,0:T(8,128)(2,1)} %convolution_convert_fusion.10), channel_id=1, source_target_pairs={{0,2},{2,0},{4,6},{6,4},{8,10},{10,8},{12,14},{14,12},{16,18},{18,... | collective-permute-start | bytes 1572872 | tf_op jit(solution)/shard_map/ppermute | solution.py:427
  923.5 82.4 %collective-permute-start.23 = (bf16[512,512]{1,0:T(8,128)(2,1)}, bf16[512,512]{1,0:T(8,128)(2,1)}, u32[]{:S(2)}, u32[]{:S(2)}) collective-permute-start(bf16[512,512]{1,0:T(8,128)(2,1)} %convolution_convert_fusion.8), channel_id=1, source_target_pairs={{0,2},{2,0},{4,6},{6,4},{8,10},{10,8},{12,14},{14,12},{16,18},{18,... | collective-permute-start | bytes 1572872 | tf_op jit(solution)/shard_map/ppermute | solution.py:427
  1002.7 11.5 collective-permute-start.22
  1005.9 6.3 collective-permute-start.29
  1008.6 14.8 %collective-permute-start.24 = (bf16[512,512]{1,0:T(8,128)(2,1)S(1)}, bf16[512,512]{1,0:T(8,128)(2,1)S(1)}, u32[]{:S(2)}, u32[]{:S(2)}) collective-permute-start(bf16[512,512]{1,0:T(8,128)(2,1)S(1)} %add_convert_fusion.6), channel_id=1, source_target_pairs={{0,1},{1,0},{2,3},{3,2},{4,5},{5,4},{6,7},{7,6},{8,9},{9,8},{10,11... | collective-permute-start | bytes 1572872 | tf_op jit(solution)/shard_map/ppermute | solution.py:424
  1012.2 22.5 %collective-permute-start.12 = (bf16[512,512]{1,0:T(8,128)(2,1)S(1)}, bf16[512,512]{1,0:T(8,128)(2,1)S(1)}, u32[]{:S(2)}, u32[]{:S(2)}) collective-permute-start(bf16[512,512]{1,0:T(8,128)(2,1)S(1)} %add_convert_fusion.8), channel_id=1, source_target_pairs={{0,1},{1,0},{2,3},{3,2},{4,5},{5,4},{6,7},{7,6},{8,9},{9,8},{10,11... | collective-permute-start | bytes 1572872 | tf_op jit(solution)/shard_map/ppermute | solution.py:424
  1014.3 22.2 %collective-permute-start.16 = (bf16[512,512]{1,0:T(8,128)(2,1)S(1)}, bf16[512,512]{1,0:T(8,128)(2,1)S(1)}, u32[]{:S(2)}, u32[]{:S(2)}) collective-permute-start(bf16[512,512]{1,0:T(8,128)(2,1)S(1)} %copy-done.100), channel_id=1, source_target_pairs={{0,2},{2,0},{4,6},{6,4},{8,10},{10,8},{12,14},{14,12},{16,18},{18,... | collective-permute-start | bytes 1572872 | tf_op jit(solution)/shard_map/ppermute | solution.py:427
  1023.5 22.8 %collective-permute-start.28 = (bf16[512,512]{1,0:T(8,128)(2,1)S(1)}, bf16[512,512]{1,0:T(8,128)(2,1)S(1)}, u32[]{:S(2)}, u32[]{:S(2)}) collective-permute-start(bf16[512,512]{1,0:T(8,128)(2,1)S(1)} %copy-done.101), channel_id=1, source_target_pairs={{0,2},{2,0},{4,6},{6,4},{8,10},{10,8},{12,14},{14,12},{16,18},{18,... | collective-permute-start | bytes 1572872 | tf_op jit(solution)/shard_map/ppermute | solution.py:427
  1023.7 22.2 %collective-permute-start.18 = (bf16[512,512]{1,0:T(8,128)(2,1)S(1)}, bf16[512,512]{1,0:T(8,128)(2,1)S(1)}, u32[]{:S(2)}, u32[]{:S(2)}) collective-permute-start(bf16[512,512]{1,0:T(8,128)(2,1)S(1)} %add_convert_fusion.7), channel_id=1, source_target_pairs={{0,1},{1,0},{2,3},{3,2},{4,5},{5,4},{6,7},{7,6},{8,9},{9,8},{10,11... | collective-permute-start | bytes 1572872 | tf_op jit(solution)/shard_map/ppermute | solution.py:424
  1034.7 21.6 %collective-permute-start.30 = (bf16[512,512]{1,0:T(8,128)(2,1)S(1)}, bf16[512,512]{1,0:T(8,128)(2,1)S(1)}, u32[]{:S(2)}, u32[]{:S(2)}) collective-permute-start(bf16[512,512]{1,0:T(8,128)(2,1)S(1)} %add_convert_fusion.5), channel_id=1, source_target_pairs={{0,1},{1,0},{2,3},{3,2},{4,5},{5,4},{6,7},{7,6},{8,9},{9,8},{10,11... | collective-permute-start | bytes 1572872 | tf_op jit(solution)/shard_map/ppermute | solution.py:424
  1036.5 90.3 %collective-permute-start.40 = (bf16[512,2048]{1,0:T(8,128)(2,1)S(1)}, bf16[512,2048]{1,0:T(8,128)(2,1)S(1)}, u32[]{:S(2)}, u32[]{:S(2)}) collective-permute-start(bf16[512,2048]{1,0:T(8,128)(2,1)S(1)} %copy-done.98), channel_id=1, source_target_pairs={{0,2},{2,0},{4,6},{6,4},{8,10},{10,8},{12,14},{14,12},{16,18},{18,... | collective-permute-start | bytes 6291464 | tf_op jit(solution)/shard_map/ppermute | solution.py:427
  1045.9 63.2 %collective-permute-start.41 = (bf16[512,2048]{1,0:T(8,128)(2,1)S(1)}, bf16[512,2048]{1,0:T(8,128)(2,1)S(1)}, u32[]{:S(2)}, u32[]{:S(2)}) collective-permute-start(bf16[512,2048]{1,0:T(8,128)(2,1)S(1)} %copy-done.99), channel_id=1, source_target_pairs={{0,2},{2,0},{4,6},{6,4},{8,10},{10,8},{12,14},{14,12},{16,18},{18,... | collective-permute-start | bytes 6291464 | tf_op jit(solution)/shard_map/ppermute | solution.py:427
  1046.0 65.9 %slice-start.11 = ((s8[6291456]{0:T(1024)(128)(4,1)}), s8[4194304]{0:T(1024)(128)(4,1)S(1)}, s32[]{:S(2)}) async-start(s8[6291456]{0:T(1024)(128)(4,1)} %bitcast.452), calls=%async_computation.19 | async-start | bytes 8388608
  1046.2 11.8 collective-permute-start.25
  1056.3 9.2 collective-permute-start.13
  1058.1 13.1 %collective-permute-start.19 = (bf16[4,64,512]{2,1,0:T(8,128)(2,1)S(1)}, bf16[4,64,512]{2,1,0:T(8,128)(2,1)S(1)}, u32[]{:S(2)}, u32[]{:S(2)}) collective-permute-start(bf16[4,64,512]{2,1,0:T(8,128)(2,1)S(1)} %fusion.87), channel_id=1, source_target_pairs={{0,4},{2,6},{4,0},{6,2},{8,12},{10,14},{12,8},{14,10},{16,20},{18,... | collective-permute-start | bytes 786440 | tf_op jit(solution)/shard_map/ppermute | solution.py:427
  1058.8 53.0 %slice-start.12 = ((s8[6291456]{0:T(1024)(128)(4,1)}), s8[2097152]{0:T(1024)(128)(4,1)S(1)}, s32[]{:S(2)}) async-start(s8[6291456]{0:T(1024)(128)(4,1)} %bitcast.452), calls=%async_computation.20 | async-start | bytes 4194304
  1065.6 9.5 collective-permute-start.31
  1071.2 54.2 %collective-permute-start.9 = (bf16[1536,512]{0,1:T(8,128)(2,1)}, bf16[1536,512]{0,1:T(8,128)(2,1)S(1)}, u32[]{:S(2)}, u32[]{:S(2)}) collective-permute-start(bf16[1536,512]{0,1:T(8,128)(2,1)} %fusion.16), channel_id=1, source_target_pairs={{0,1},{1,0},{2,3},{3,2},{4,5},{5,4},{6,7},{7,6},{8,9},{9,8},{10,11... | collective-permute-start | bytes 4718600 | tf_op jit(solution)/shard_map/ppermute | solution.py:424
  1075.0 5.0 collective-permute-start.26
  1080.0 5.8 collective-permute-start.14
  1085.8 6.1 collective-permute-start.20
  1091.9 5.4 collective-permute-start.32
  1097.3 5.9 collective-permute-start.27
  1103.2 5.6 collective-permute-start.15
  1108.8 14.4 %collective-permute-start.21 = (bf16[1,64,512]{2,1,0:T(8,128)(2,1)S(1)}, bf16[1,64,512]{2,1,0:T(8,128)(2,1)S(1)}, u32[]{:S(2)}, u32[]{:S(2)}) collective-permute-start(bf16[1,64,512]{2,1,0:T(8,128)(2,1)S(1)} %dynamic-slice_convert_fusion.11), channel_id=1, source_target_pairs={{0,16},{2,18},{4,20},{6,22},{8,24},{10,26},{12,28},{14,30},{16,0},... | collective-permute-start | bytes 196616 | tf_op jit(solution)/shard_map/ppermute | solution.py:427
  1109.2 14.1 %collective-permute-start.33 = (bf16[1,64,512]{2,1,0:T(8,128)(2,1)S(1)}, bf16[1,64,512]{2,1,0:T(8,128)(2,1)S(1)}, u32[]{:S(2)}, u32[]{:S(2)}) collective-permute-start(bf16[1,64,512]{2,1,0:T(8,128)(2,1)S(1)} %dynamic-slice_convert_fusion.9), channel_id=1, source_target_pairs={{0,16},{2,18},{4,20},{6,22},{8,24},{10,26},{12,28},{14,30},{16,0},... | collective-permute-start | bytes 196616 | tf_op jit(solution)/shard_map/ppermute | solution.py:427
  1115.6 48.6 %collective-permute-start.42 = (bf16[512,2048]{1,0:T(8,128)(2,1)S(1)}, bf16[512,2048]{1,0:T(8,128)(2,1)S(1)}, u32[]{:S(2)}, u32[]{:S(2)}) collective-permute-start(bf16[512,2048]{1,0:T(8,128)(2,1)S(1)} %add_convert_fusion.3), channel_id=1, source_target_pairs={{0,1},{1,0},{2,3},{3,2},{4,5},{5,4},{6,7},{7,6},{8,9},{9,8},{10,11... | collective-permute-start | bytes 6291464 | tf_op jit(solution)/shard_map/ppermute | solution.py:424
  1123.2 43.8 %collective-permute-start.34 = (bf16[512,2048]{1,0:T(8,128)(2,1)}, bf16[512,2048]{1,0:T(8,128)(2,1)S(1)}, u32[]{:S(2)}, u32[]{:S(2)}) collective-permute-start(bf16[512,2048]{1,0:T(8,128)(2,1)} %convolution_convert_fusion.3), channel_id=1, source_target_pairs={{0,2},{2,0},{4,6},{6,4},{8,10},{10,8},{12,14},{14,12},{16,18},{18,... | collective-permute-start | bytes 6291464 | tf_op jit(solution)/shard_map/ppermute | solution.py:427
  1123.3 75.5 %collective-permute-start.36 = (bf16[512,2048]{1,0:T(8,128)(2,1)}, bf16[512,2048]{1,0:T(8,128)(2,1)}, u32[]{:S(2)}, u32[]{:S(2)}) collective-permute-start(bf16[512,2048]{1,0:T(8,128)(2,1)} %add_convert_fusion.4), channel_id=1, source_target_pairs={{0,1},{1,0},{2,3},{3,2},{4,5},{5,4},{6,7},{7,6},{8,9},{9,8},{10,11... | collective-permute-start | bytes 6291464 | tf_op jit(solution)/shard_map/ppermute | solution.py:424
  1126.6 37.7 %copy-start.25 = (f32[512,2048]{1,0:T(8,128)S(1)}, f32[512,2048]{1,0:T(8,128)}, u32[]{:S(2)}) copy-start(f32[512,2048]{1,0:T(8,128)} %fusion.115) | copy-start | bytes 12582916
  1165.4 49.4 %collective-permute-start.43 = (bf16[4,64,2048]{2,1,0:T(8,128)(2,1)S(1)}, bf16[4,64,2048]{2,1,0:T(8,128)(2,1)}, u32[]{:S(2)}, u32[]{:S(2)}) collective-permute-start(bf16[4,64,2048]{2,1,0:T(8,128)(2,1)S(1)} %fusion.64), channel_id=1, source_target_pairs={{0,4},{2,6},{4,0},{6,2},{8,12},{10,14},{12,8},{14,10},{16,20},{18,... | collective-permute-start | bytes 3145736 | tf_op jit(solution)/shard_map/ppermute | solution.py:427
  1203.4 15.5 %collective-permute-start.37 = (bf16[4,64,2048]{2,1,0:T(8,128)(2,1)S(1)}, bf16[4,64,2048]{2,1,0:T(8,128)(2,1)}, u32[]{:S(2)}, u32[]{:S(2)}) collective-permute-start(bf16[4,64,2048]{2,1,0:T(8,128)(2,1)S(1)} %fusion.63), channel_id=1, source_target_pairs={{0,4},{2,6},{4,0},{6,2},{8,12},{10,14},{12,8},{14,10},{16,20},{18,... | collective-permute-start | bytes 3145736 | tf_op jit(solution)/shard_map/ppermute | solution.py:427
  1217.2 13.8 %collective-permute-start.44 = (bf16[2,64,2048]{2,1,0:T(8,128)(2,1)S(1)}, bf16[2,64,2048]{2,1,0:T(8,128)(2,1)S(1)}, u32[]{:S(2)}, u32[]{:S(2)}) collective-permute-start(bf16[2,64,2048]{2,1,0:T(8,128)(2,1)S(1)} %fusion.84), channel_id=1, source_target_pairs={{0,8},{2,10},{4,12},{6,14},{8,0},{10,2},{12,4},{14,6},{16,24},{18,... | collective-permute-start | bytes 1572872 | tf_op jit(solution)/shard_map/ppermute | solution.py:427
  1220.6 20.9 %collective-permute-start.38 = (bf16[2,64,2048]{2,1,0:T(8,128)(2,1)S(1)}, bf16[2,64,2048]{2,1,0:T(8,128)(2,1)S(1)}, u32[]{:S(2)}, u32[]{:S(2)}) collective-permute-start(bf16[2,64,2048]{2,1,0:T(8,128)(2,1)S(1)} %fusion.83), channel_id=1, source_target_pairs={{0,8},{2,10},{4,12},{6,14},{8,0},{10,2},{12,4},{14,6},{16,24},{18,... | collective-permute-start | bytes 1572872 | tf_op jit(solution)/shard_map/ppermute | solution.py:427
  1231.2 10.9 collective-permute-start.45
  1241.7 9.4 collective-permute-start.39
  (111 other events, 1013.0 us)
Sparse Core Ops, SparseCore 0:
  17.1 47.0 all-gather.9
  67.0 36.3 all-gather.11
  106.1 49.4 all-gather.13
  157.7 49.4 all-gather.15
  347.0 51.6 all-gather.17
  539.9 13.0 reduce-scatter.2
  863.6 134.8 all-reduce.3

commit v2 on v1

v2 whole, which is shorter than its diff:
```python
import functools
import math

import jax
import jax.numpy as jnp
from jax import lax
from jax.experimental import pallas as pl
from jax.experimental.pallas import tpu as pltpu
from jax.sharding import PartitionSpec as P

DH = 64
QLEN = 32
ROW_LEN = 1024
F32 = jnp.float32
BF16 = jnp.bfloat16
VMEM_LIMIT = 56 * 1024 * 1024
NT = (((1,), (1,)), ((), ()))
NN = (((1,), (0,)), ((), ()))
TN = (((0,), (0,)), ((), ()))


def mm(left, right, dims=NN):
    return lax.dot_general(left, right, dims, preferred_element_type=F32)


def row_step(rows):
    return 512 if rows % 512 == 0 else 128


def held(shape):
    return pl.BlockSpec(shape, lambda *_: (0,) * len(shape), pipeline_mode=pl.Buffered(1))


def shaped(dtype, *shape):
    return jax.ShapeDtypeStruct(shape, dtype)


def call(body, name, grid, in_specs, out_specs, out_shape, operands, flops, scratch=(), prefetch=0):
    size = sum(math.prod(o.shape) * o.dtype.itemsize for o in list(operands) + list(out_shape))
    return pl.pallas_call(
        body,
        grid_spec=pltpu.PrefetchScalarGridSpec(
            num_scalar_prefetch=prefetch,
            grid=grid,
            in_specs=in_specs,
            out_specs=out_specs,
            scratch_shapes=list(scratch),
        ),
        out_shape=out_shape,
        compiler_params=pltpu.CompilerParams(vmem_limit_bytes=VMEM_LIMIT),
        cost_estimate=pl.CostEstimate(flops=flops, bytes_accessed=size, transcendentals=0),
        name=name,
    )(*operands)


def row_spec(step, width):
    return pl.BlockSpec((step, width), lambda i, *_: (i, 0))


def column_spec(width, step):
    return pl.BlockSpec((width, step), lambda i, *_: (0, i))


def swap_halves(block):
    lane = lax.broadcasted_iota(jnp.int32, block.shape, 1)
    width = block.shape[1]
    return jnp.where((lane & 32) == 0, pltpu.roll(block, width - 32, 1), pltpu.roll(block, 32, 1))


def wide_table(table, width):
    return jnp.concatenate([table] * (width // 128), axis=1)


def qkv_kernel(x_ref, w_ref, b_ref, cos_ref, sin_ref, out_ref):
    which = pl.program_id(0)
    mixed = mm(x_ref[...], w_ref[0]) + b_ref[pl.ds(which, 1), :]
    width = mixed.shape[1]

    @pl.when(which < 2)
    def _():
        turned = mixed * wide_table(cos_ref[...], width)
        turned = turned + swap_halves(mixed) * wide_table(sin_ref[...], width)
        out_ref[0] = turned.astype(BF16)

    @pl.when(which == 2)
    def _():
        out_ref[0] = mixed.astype(BF16)


def project_qkv(x, weight, bias, cosine, sine):
    n, D = x.shape
    width = weight.shape[2]
    step = row_step(n)
    return call(
        qkv_kernel, "project_qkv", (3, n // step),
        [
            pl.BlockSpec((step, D), lambda j, i: (i, 0)),
            pl.BlockSpec((1, D, width), lambda j, i: (j, 0, 0)),
            held(bias.shape),
            pl.BlockSpec((step, 128), lambda j, i: (i, 0)),
            pl.BlockSpec((step, 128), lambda j, i: (i, 0)),
        ],
        [pl.BlockSpec((1, step, width), lambda j, i: (j, i, 0))],
        [shaped(BF16, 3, n, width)],
        (x, weight, bias, cosine, sine), 6 * n * D * width,
    )[0]


def normed_rows(residual):
    mean = jnp.mean(residual, axis=1, keepdims=True)
    centred = residual - mean
    inverse = lax.rsqrt(jnp.mean(centred * centred, axis=1, keepdims=True) + 1e-05)
    return centred * inverse, inverse


def norm_pull(grad_rows, normed, inverse, gain):
    spread = grad_rows * gain
    return inverse * (
        spread
        - jnp.mean(spread, axis=1, keepdims=True)
        - normed * jnp.mean(spread * normed, axis=1, keepdims=True)
    )


def column_sums(*arrays):
    rows = [jnp.sum(array, axis=0, keepdims=True) for array in arrays]
    rows.append(jnp.zeros((8 - len(rows), rows[0].shape[1]), F32))
    return jnp.concatenate(rows, axis=0)


def add_over_steps(ref, value):
    first = pl.program_id(0) == 0

    @pl.when(first)
    def _():
        ref[...] = value

    @pl.when(jnp.logical_not(first))
    def _():
        ref[...] += value


def out_norm_kernel(slots, *refs):
    x_ref, vec_ref = refs[:2]
    att_refs, w_refs = refs[2 : 2 + slots], refs[2 + slots : 2 + 2 * slots]
    normed_ref, inverse_ref, low_ref, turned_ref = refs[2 + 2 * slots :]
    residual = x_ref[...].astype(F32) + vec_ref[0:1, :]
    for att_ref, w_ref in zip(att_refs, w_refs):
        residual = residual + mm(att_ref[...], w_ref[...])
    normed, inverse = normed_rows(residual)
    hidden = normed * vec_ref[1:2, :] + vec_ref[2:3, :]
    normed_ref[...] = normed
    inverse_ref[...] = inverse
    low_ref[...] = hidden.astype(BF16)
    turned_ref[...] = hidden.T.astype(BF16)


def out_and_norm(x, vectors, attended, weights):
    n, D = x.shape
    step = row_step(n)
    slots = len(attended)
    width = attended[0].shape[1]
    return call(
        functools.partial(out_norm_kernel, slots), "out_and_norm", (n // step,),
        [row_spec(step, D), held(vectors.shape)]
        + [row_spec(step, width)] * slots + [held((width, D))] * slots,
        [row_spec(step, D), row_spec(step, 1), row_spec(step, D), column_spec(D, step)],
        [shaped(F32, n, D), shaped(F32, n, 1), shaped(BF16, n, D), shaped(BF16, D, n)],
        (x, vectors, *attended, *weights), 2 * n * D * D,
    )


GELU_TERMS = (
    0.23532527933595032, 0.09138803439798156, 0.6495603483388861,
    -0.6354014529895687, 0.8866650885491606, -0.22753729931242958,
)


def gelu_parts(values):
    size = jnp.abs(values)
    part = pl.reciprocal(1.0 + (0.39 / math.sqrt(2.0)) * size)
    bell = jnp.exp(-0.5 * (values * values))
    series = 0.5 * GELU_TERMS[-1]
    for term in GELU_TERMS[-2::-1]:
        series = series * part + 0.5 * term
    tail = series * part * bell
    below = jnp.where(values >= 0.0, 1.0 - tail, tail)
    return values * below, below + values * bell * (1.0 / math.sqrt(2.0 * math.pi))


def up_kernel(x_ref, w_ref, b_ref, active_ref, slope_ref):
    width = w_ref.shape[1]
    chunk = min(512, width)
    for first in range(0, width, chunk):
        at = slice(first, first + chunk)
        active, slope = gelu_parts(mm(x_ref[...], w_ref[:, at]) + b_ref[:, at])
        active_ref[:, at] = active.astype(BF16)
        slope_ref[:, at] = slope


def up_and_gelu(x, weight, bias):
    n, D = x.shape
    width = weight.shape[1]
    step = row_step(n)
    return call(
        up_kernel, "up_and_gelu", (n // step,),
        [row_spec(step, D), held(weight.shape), held(bias.shape)],
        [row_spec(step, width)] * 2,
        [shaped(BF16, n, width), shaped(F32, n, width)],
        (x, weight, bias), 5 * n * D * width,
    )


def down_norm_kernel(slots, *refs):
    normed_ref, vec_ref, proj_ref = refs[:3]
    act_refs, w_refs = refs[3 : 3 + slots], refs[3 + slots : 3 + 2 * slots]
    normed_out, inverse_ref, low_ref, unit_ref, unit_low_ref, unit_inverse_ref = refs[3 + 2 * slots :]
    residual = normed_ref[...] * vec_ref[1:2, :] + vec_ref[2:3, :] + vec_ref[3:4, :]
    for act_ref, w_ref in zip(act_refs, w_refs):
        residual = residual + mm(act_ref[...], w_ref[...])
    normed, inverse = normed_rows(residual)
    normed_out[...] = normed
    inverse_ref[...] = inverse
    low = (normed * vec_ref[4:5, :] + vec_ref[5:6, :]).astype(BF16)
    low_ref[...] = low
    embedding = mm(low, proj_ref[...])
    unit_inverse = lax.rsqrt(jnp.sum(embedding * embedding, axis=1, keepdims=True) + 1e-06)
    unit = embedding * unit_inverse
    unit_ref[...] = unit
    unit_low_ref[...] = unit.astype(BF16)
    unit_inverse_ref[...] = unit_inverse


def down_and_norm(normed, vectors, proj, active, weights):
    n, D = normed.shape
    step = row_step(n)
    slots = len(active)
    width = active[0].shape[1]
    return call(
        functools.partial(down_norm_kernel, slots), "down_and_norm", (n // step,),
        [row_spec(step, D), held(vectors.shape), held(proj.shape)]
        + [row_spec(step, width)] * slots + [held((width, D))] * slots,
        [
            row_spec(step, D), row_spec(step, 1), row_spec(step, D),
            row_spec(step, 128), row_spec(step, 128), row_spec(step, 1),
        ],
        [
            shaped(F32, n, D), shaped(F32, n, 1), shaped(BF16, n, D),
            shaped(F32, n, 128), shaped(BF16, n, 128), shaped(F32, n, 1),
        ],
        (normed, vectors, proj, *active, *weights), 2 * n * D * width * slots,
    )


def head_pull_kernel(
    grad_ref, unit_ref, unit_inverse_ref, proj_ref, normed_ref, inverse_ref, vec_ref,
    embed_ref, residual_ref, low_ref, turned_ref, sum_ref,
):
    grad, unit = grad_ref[...], unit_ref[...]
    embed = unit_inverse_ref[...] * (grad - unit * jnp.sum(grad * unit, axis=1, keepdims=True))
    embed = embed.astype(BF16)
    embed_ref[...] = embed
    output_grad = mm(embed, proj_ref[...], NT)
    normed = normed_ref[...]
    residual = norm_pull(output_grad, normed, inverse_ref[...], vec_ref[4:5, :])
    residual_ref[...] = residual
    low_ref[...] = residual.astype(BF16)
    turned_ref[...] = residual.T.astype(BF16)
    add_over_steps(sum_ref, column_sums(residual, output_grad * normed, output_grad))


def head_pull(unit_grad, unit, unit_inverse, proj, normed, inverse, vectors):
    n, D = normed.shape
    step = row_step(n)
    return call(
        head_pull_kernel, "head_pull", (n // step,),
        [
            row_spec(step, 128), row_spec(step, 128), row_spec(step, 1), held(proj.shape),
            row_spec(step, D), row_spec(step, 1), held(vectors.shape),
        ],
        [
            row_spec(step, 128), row_spec(step, D), row_spec(step, D),
            column_spec(D, step), pl.BlockSpec((8, D), lambda i: (0, 0)),
        ],
        [
            shaped(BF16, n, 128), shaped(F32, n, D), shaped(BF16, n, D),
            shaped(BF16, D, n), shaped(F32, 8, D),
        ],
        (unit_grad, unit, unit_inverse, proj, normed, inverse, vectors), 4 * n * D * 128,
    )


def up_pull_kernel(branch_ref, w_ref, slope_ref, out_ref, sum_ref):
    width = w_ref.shape[0]
    chunk = min(512, width)
    sums = []
    for first in range(0, width, chunk):
        at = slice(first, first + chunk)
        low = (mm(branch_ref[...], w_ref[at, :], NT) * slope_ref[:, at]).astype(BF16)
        out_ref[:, at] = low
        sums.append(column_sums(low.astype(F32)))
    add_over_steps(sum_ref, jnp.concatenate(sums, axis=1))


def up_pull(branch, weight, slope):
    n, D = branch.shape
    width = weight.shape[0]
    step = row_step(n)
    return call(
        up_pull_kernel, "up_pull", (n // step,),
        [row_spec(step, D), held(weight.shape), row_spec(step, width)],
        [row_spec(step, width), pl.BlockSpec((8, width), lambda i: (0, 0))],
        [shaped(BF16, n, width), shaped(F32, 8, width)],
        (branch, weight, slope), 2 * n * D * width,
    )


def hidden_pull_kernel(slots, *refs):
    residual_ref, normed_ref, inverse_ref, vec_ref = refs[:4]
    pre_refs, up_refs, out_refs = (refs[4 + j * slots : 4 + (j + 1) * slots] for j in range(3))
    rest = refs[4 + 3 * slots :]
    grad_ref, turned_ref, sum_ref = rest[:3]
    att_refs = rest[3:]
    hidden_grad = residual_ref[...]
    for pre_ref, up_ref in zip(pre_refs, up_refs):
        hidden_grad = hidden_grad + mm(pre_ref[...], up_ref[...], NT)
    normed = normed_ref[...]
    residual = norm_pull(hidden_grad, normed, inverse_ref[...], vec_ref[1:2, :])
    grad_ref[...] = residual
    low = residual.astype(BF16)
    turned_ref[...] = residual.T.astype(BF16)
    add_over_steps(sum_ref, column_sums(residual, hidden_grad * normed, hidden_grad))
    for att_ref, out_ref in zip(att_refs, out_refs):
        att_ref[...] = mm(low, out_ref[...], NT).astype(BF16)


def hidden_pull(residual, normed, inverse, vectors, pre_grads, ups, outs):
    n, D = residual.shape
    step = row_step(n)
    slots = len(ups)
    wide, width = ups[0].shape[1], outs[0].shape[0]
    return call(
        functools.partial(hidden_pull_kernel, slots), "hidden_pull", (n // step,),
        [row_spec(step, D), row_spec(step, D), row_spec(step, 1), held(vectors.shape)]
        + [row_spec(step, wide)] * slots + [held((D, wide))] * slots
        + [held((width, D))] * slots,
        [row_spec(step, D), column_spec(D, step), pl.BlockSpec((8, D), lambda i: (0, 0))]
        + [row_spec(step, width)] * slots,
        [shaped(F32, n, D), shaped(BF16, D, n), shaped(F32, 8, D)]
        + [shaped(BF16, n, width)] * slots,
        (residual, normed, inverse, vectors, *pre_grads, *ups, *outs),
        2 * n * D * (wide + width) * slots,
    )


def token_pull_kernel(slots, place_ref, *refs):
    residual_ref = refs[0]
    mixed_refs, w_refs = refs[1 : 1 + slots], refs[1 + slots : 1 + 2 * slots]
    out_ref = refs[-1]
    width = out_ref.shape[1]
    at = pl.ds(pl.multiple_of(place_ref[0] * width, width), width)
    total = residual_ref[...]
    for mixed_ref, w_ref in zip(mixed_refs, w_refs):
        for which in range(3):
            total = total + mm(mixed_ref[which], w_ref[which, at, :], NT)
    out_ref[...] = total.astype(out_ref.dtype)


def token_pull(place, residual, mixed_grads, weights, dtype):
    n, D = residual.shape
    step = row_step(n)
    slots = len(weights)
    width = weights[0].shape[2]
    return call(
        functools.partial(token_pull_kernel, slots), "token_pull", (n // step,),
        [pl.BlockSpec((step, width), lambda i, p: (i, p[0]))]
        + [pl.BlockSpec((3, step, width), lambda i, p: (0, i, 0))] * slots
        + [held((3, D, width))] * slots,
        [row_spec(step, width)],
        [shaped(dtype, n, width)],
        (place.reshape(1), residual, *mixed_grads, *weights), 6 * n * D * width, prefetch=1,
    )[0]


def weight_pull_kernel(place_ref, left_ref, right_ref, *refs):
    out_ref = refs[-1]
    total = mm(left_ref[:, 0].reshape(-1, left_ref.shape[-1]), right_ref[0])
    if len(refs) > 1:
        total = total + refs[0][0].astype(F32)
    out_ref[0] = total.astype(out_ref.dtype)


def weight_pull(place, left, right, arrived, dtype):
    pairs, _, share, n = left.shape
    count, _, m = right.shape
    rows = pairs * share
    chunk = min(512, m)
    spec = pl.BlockSpec((1, rows, chunk), lambda j, i, p: (j, 0, i))
    return call(
        weight_pull_kernel, "weight_pull", (count, m // chunk),
        [
            pl.BlockSpec((pairs, 1, share, n), lambda j, i, p: (0, p[0], 0, 0)),
            pl.BlockSpec((1, n, chunk), lambda j, i, p: (j, 0, i)),
        ] + ([] if arrived is None else [spec]),
        [spec],
        [shaped(dtype, count, rows, m)],
        (place.reshape(1), left, right) + (() if arrived is None else (arrived,)),
        2 * count * rows * n * m, prefetch=1,
    )[0]


def row_step(rows):
    return 512 if rows % 512 == 0 else 128


def held(shape):
    return pl.BlockSpec(shape, lambda *_: (0,) * len(shape), pipeline_mode=pl.Buffered(1))


def shaped(dtype, *shape):
    return jax.ShapeDtypeStruct(shape, dtype)


def call(body, name, grid, in_specs, out_specs, out_shape, operands, flops, scratch=(), prefetch=0):
    size = sum(math.prod(o.shape) * o.dtype.itemsize for o in list(operands) + list(out_shape))
    return pl.pallas_call(
        body,
        grid_spec=pltpu.PrefetchScalarGridSpec(
            num_scalar_prefetch=prefetch,
            grid=grid,
            in_specs=in_specs,
            out_specs=out_specs,
            scratch_shapes=list(scratch),
        ),
        out_shape=out_shape,
        compiler_params=pltpu.CompilerParams(vmem_limit_bytes=VMEM_LIMIT),
        cost_estimate=pl.CostEstimate(flops=flops, bytes_accessed=size, transcendentals=0),
        name=name,
    )(*operands)


def row_spec(step, width):
    return pl.BlockSpec((step, width), lambda i, *_: (i, 0))


def column_spec(width, step):
    return pl.BlockSpec((width, step), lambda i, *_: (0, i))


def swap_halves(block):
    lane = lax.broadcasted_iota(jnp.int32, block.shape, 1)
    width = block.shape[1]
    return jnp.where((lane & 32) == 0, pltpu.roll(block, width - 32, 1), pltpu.roll(block, 32, 1))


def wide_table(table, width):
    return jnp.concatenate([table] * (width // 128), axis=1)


def qkv_kernel(x_ref, w_ref, b_ref, cos_ref, sin_ref, out_ref):
    which = pl.program_id(0)
    mixed = mm(x_ref[...], w_ref[0]) + b_ref[pl.ds(which, 1), :]
    width = mixed.shape[1]

    @pl.when(which < 2)
    def _():
        turned = mixed * wide_table(cos_ref[...], width)
        turned = turned + swap_halves(mixed) * wide_table(sin_ref[...], width)
        out_ref[0] = turned.astype(BF16)

    @pl.when(which == 2)
    def _():
        out_ref[0] = mixed.astype(BF16)


def project_qkv(x, weight, bias, cosine, sine):
    n, D = x.shape
    width = weight.shape[2]
    step = row_step(n)
    return call(
        qkv_kernel, "project_qkv", (3, n // step),
        [
            pl.BlockSpec((step, D), lambda j, i: (i, 0)),
            pl.BlockSpec((1, D, width), lambda j, i: (j, 0, 0)),
            held(bias.shape),
            pl.BlockSpec((step, 128), lambda j, i: (i, 0)),
            pl.BlockSpec((step, 128), lambda j, i: (i, 0)),
        ],
        [pl.BlockSpec((1, step, width), lambda j, i: (j, i, 0))],
        [shaped(BF16, 3, n, width)],
        (x, weight, bias, cosine, sine), 6 * n * D * width,
    )[0]


def normed_rows(residual):
    mean = jnp.mean(residual, axis=1, keepdims=True)
    centred = residual - mean
    inverse = lax.rsqrt(jnp.mean(centred * centred, axis=1, keepdims=True) + 1e-05)
    return centred * inverse, inverse


def norm_pull(grad_rows, normed, inverse, gain):
    spread = grad_rows * gain
    return inverse * (
        spread
        - jnp.mean(spread, axis=1, keepdims=True)
        - normed * jnp.mean(spread * normed, axis=1, keepdims=True)
    )


def column_sums(*arrays):
    rows = [jnp.sum(array, axis=0, keepdims=True) for array in arrays]
    rows.append(jnp.zeros((8 - len(rows), rows[0].shape[1]), F32))
    return jnp.concatenate(rows, axis=0)


def add_over_steps(ref, value):
    first = pl.program_id(0) == 0

    @pl.when(first)
    def _():
        ref[...] = value

    @pl.when(jnp.logical_not(first))
    def _():
        ref[...] += value


def out_norm_kernel(slots, *refs):
    x_ref, vec_ref = refs[:2]
    att_refs, w_refs = refs[2 : 2 + slots], refs[2 + slots : 2 + 2 * slots]
    normed_ref, inverse_ref, low_ref, turned_ref = refs[2 + 2 * slots :]
    residual = x_ref[...].astype(F32) + vec_ref[0:1, :]
    for att_ref, w_ref in zip(att_refs, w_refs):
        residual = residual + mm(att_ref[...], w_ref[...])
    normed, inverse = normed_rows(residual)
    hidden = normed * vec_ref[1:2, :] + vec_ref[2:3, :]
    normed_ref[...] = normed
    inverse_ref[...] = inverse
    low_ref[...] = hidden.astype(BF16)
    turned_ref[...] = hidden.T.astype(BF16)


def out_and_norm(x, vectors, attended, weights):
    n, D = x.shape
    step = row_step(n)
    slots = len(attended)
    width = attended[0].shape[1]
    return call(
        functools.partial(out_norm_kernel, slots), "out_and_norm", (n // step,),
        [row_spec(step, D), held(vectors.shape)]
        + [row_spec(step, width)] * slots + [held((width, D))] * slots,
        [row_spec(step, D), row_spec(step, 1), row_spec(step, D), column_spec(D, step)],
        [shaped(F32, n, D), shaped(F32, n, 1), shaped(BF16, n, D), shaped(BF16, D, n)],
        (x, vectors, *attended, *weights), 2 * n * D * D,
    )


GELU_TERMS = (
    0.23532527933595032, 0.09138803439798156, 0.6495603483388861,
    -0.6354014529895687, 0.8866650885491606, -0.22753729931242958,
)


def gelu_parts(values):
    size = jnp.abs(values)
    part = pl.reciprocal(1.0 + (0.39 / math.sqrt(2.0)) * size)
    bell = jnp.exp(-0.5 * (values * values))
    series = 0.5 * GELU_TERMS[-1]
    for term in GELU_TERMS[-2::-1]:
        series = series * part + 0.5 * term
    tail = series * part * bell
    below = jnp.where(values >= 0.0, 1.0 - tail, tail)
    return values * below, below + values * bell * (1.0 / math.sqrt(2.0 * math.pi))


def up_kernel(x_ref, w_ref, b_ref, active_ref, slope_ref):
    width = w_ref.shape[1]
    chunk = min(512, width)
    for first in range(0, width, chunk):
        at = slice(first, first + chunk)
        active, slope = gelu_parts(mm(x_ref[...], w_ref[:, at]) + b_ref[:, at])
        active_ref[:, at] = active.astype(BF16)
        slope_ref[:, at] = slope


def up_and_gelu(x, weight, bias):
    n, D = x.shape
    width = weight.shape[1]
    step = row_step(n)
    return call(
        up_kernel, "up_and_gelu", (n // step,),
        [row_spec(step, D), held(weight.shape), held(bias.shape)],
        [row_spec(step, width)] * 2,
        [shaped(BF16, n, width), shaped(F32, n, width)],
        (x, weight, bias), 5 * n * D * width,
    )


def down_norm_kernel(slots, *refs):
    normed_ref, vec_ref, proj_ref = refs[:3]
    act_refs, w_refs = refs[3 : 3 + slots], refs[3 + slots : 3 + 2 * slots]
    normed_out, inverse_ref, low_ref, unit_ref, unit_low_ref, unit_inverse_ref = refs[3 + 2 * slots :]
    residual = normed_ref[...] * vec_ref[1:2, :] + vec_ref[2:3, :] + vec_ref[3:4, :]
    for act_ref, w_ref in zip(act_refs, w_refs):
        residual = residual + mm(act_ref[...], w_ref[...])
    normed, inverse = normed_rows(residual)
    normed_out[...] = normed
    inverse_ref[...] = inverse
    low = (normed * vec_ref[4:5, :] + vec_ref[5:6, :]).astype(BF16)
    low_ref[...] = low
    embedding = mm(low, proj_ref[...])
    unit_inverse = lax.rsqrt(jnp.sum(embedding * embedding, axis=1, keepdims=True) + 1e-06)
    unit = embedding * unit_inverse
    unit_ref[...] = unit
    unit_low_ref[...] = unit.astype(BF16)
    unit_inverse_ref[...] = unit_inverse


def down_and_norm(normed, vectors, proj, active, weights):
    n, D = normed.shape
    step = row_step(n)
    slots = len(active)
    width = active[0].shape[1]
    return call(
        functools.partial(down_norm_kernel, slots), "down_and_norm", (n // step,),
        [row_spec(step, D), held(vectors.shape), held(proj.shape)]
        + [row_spec(step, width)] * slots + [held((width, D))] * slots,
        [
            row_spec(step, D), row_spec(step, 1), row_spec(step, D),
            row_spec(step, 128), row_spec(step, 128), row_spec(step, 1),
        ],
        [
            shaped(F32, n, D), shaped(F32, n, 1), shaped(BF16, n, D),
            shaped(F32, n, 128), shaped(BF16, n, 128), shaped(F32, n, 1),
        ],
        (normed, vectors, proj, *active, *weights), 2 * n * D * width * slots,
    )


def head_pull_kernel(
    grad_ref, unit_ref, unit_inverse_ref, proj_ref, normed_ref, inverse_ref, vec_ref,
    embed_ref, residual_ref, low_ref, turned_ref, sum_ref,
):
    grad, unit = grad_ref[...], unit_ref[...]
    embed = unit_inverse_ref[...] * (grad - unit * jnp.sum(grad * unit, axis=1, keepdims=True))
    embed = embed.astype(BF16)
    embed_ref[...] = embed
    output_grad = mm(embed, proj_ref[...], NT)
    normed = normed_ref[...]
    residual = norm_pull(output_grad, normed, inverse_ref[...], vec_ref[4:5, :])
    residual_ref[...] = residual
    low_ref[...] = residual.astype(BF16)
    turned_ref[...] = residual.T.astype(BF16)
    add_over_steps(sum_ref, column_sums(residual, output_grad * normed, output_grad))


def head_pull(unit_grad, unit, unit_inverse, proj, normed, inverse, vectors):
    n, D = normed.shape
    step = row_step(n)
    return call(
        head_pull_kernel, "head_pull", (n // step,),
        [
            row_spec(step, 128), row_spec(step, 128), row_spec(step, 1), held(proj.shape),
            row_spec(step, D), row_spec(step, 1), held(vectors.shape),
        ],
        [
            row_spec(step, 128), row_spec(step, D), row_spec(step, D),
            column_spec(D, step), pl.BlockSpec((8, D), lambda i: (0, 0)),
        ],
        [
            shaped(BF16, n, 128), shaped(F32, n, D), shaped(BF16, n, D),
            shaped(BF16, D, n), shaped(F32, 8, D),
        ],
        (unit_grad, unit, unit_inverse, proj, normed, inverse, vectors), 4 * n * D * 128,
    )


def up_pull_kernel(branch_ref, w_ref, slope_ref, out_ref, sum_ref):
    width = w_ref.shape[0]
    chunk = min(512, width)
    sums = []
    for first in range(0, width, chunk):
        at = slice(first, first + chunk)
        low = (mm(branch_ref[...], w_ref[at, :], NT) * slope_ref[:, at]).astype(BF16)
        out_ref[:, at] = low
        sums.append(column_sums(low.astype(F32)))
    add_over_steps(sum_ref, jnp.concatenate(sums, axis=1))


def up_pull(branch, weight, slope):
    n, D = branch.shape
    width = weight.shape[0]
    step = row_step(n)
    return call(
        up_pull_kernel, "up_pull", (n // step,),
        [row_spec(step, D), held(weight.shape), row_spec(step, width)],
        [row_spec(step, width), pl.BlockSpec((8, width), lambda i: (0, 0))],
        [shaped(BF16, n, width), shaped(F32, 8, width)],
        (branch, weight, slope), 2 * n * D * width,
    )


def hidden_pull_kernel(slots, *refs):
    residual_ref, normed_ref, inverse_ref, vec_ref = refs[:4]
    pre_refs, up_refs, out_refs = (refs[4 + j * slots : 4 + (j + 1) * slots] for j in range(3))
    rest = refs[4 + 3 * slots :]
    grad_ref, turned_ref, sum_ref = rest[:3]
    att_refs = rest[3:]
    hidden_grad = residual_ref[...]
    for pre_ref, up_ref in zip(pre_refs, up_refs):
        hidden_grad = hidden_grad + mm(pre_ref[...], up_ref[...], NT)
    normed = normed_ref[...]
    residual = norm_pull(hidden_grad, normed, inverse_ref[...], vec_ref[1:2, :])
    grad_ref[...] = residual
    low = residual.astype(BF16)
    turned_ref[...] = residual.T.astype(BF16)
    add_over_steps(sum_ref, column_sums(residual, hidden_grad * normed, hidden_grad))
    for att_ref, out_ref in zip(att_refs, out_refs):
        att_ref[...] = mm(low, out_ref[...], NT).astype(BF16)


def hidden_pull(residual, normed, inverse, vectors, pre_grads, ups, outs):
    n, D = residual.shape
    step = row_step(n)
    slots = len(ups)
    wide, width = ups[0].shape[1], outs[0].shape[0]
    return call(
        functools.partial(hidden_pull_kernel, slots), "hidden_pull", (n // step,),
        [row_spec(step, D), row_spec(step, D), row_spec(step, 1), held(vectors.shape)]
        + [row_spec(step, wide)] * slots + [held((D, wide))] * slots
        + [held((width, D))] * slots,
        [row_spec(step, D), column_spec(D, step), pl.BlockSpec((8, D), lambda i: (0, 0))]
        + [row_spec(step, width)] * slots,
        [shaped(F32, n, D), shaped(BF16, D, n), shaped(F32, 8, D)]
        + [shaped(BF16, n, width)] * slots,
        (residual, normed, inverse, vectors, *pre_grads, *ups, *outs),
        2 * n * D * (wide + width) * slots,
    )


def token_pull_kernel(slots, place_ref, *refs):
    residual_ref = refs[0]
    mixed_refs, w_refs = refs[1 : 1 + slots], refs[1 + slots : 1 + 2 * slots]
    out_ref = refs[-1]
    width = out_ref.shape[1]
    at = pl.ds(pl.multiple_of(place_ref[0] * width, width), width)
    total = residual_ref[...]
    for mixed_ref, w_ref in zip(mixed_refs, w_refs):
        for which in range(3):
            total = total + mm(mixed_ref[which], w_ref[which, at, :], NT)
    out_ref[...] = total.astype(out_ref.dtype)


def token_pull(place, residual, mixed_grads, weights, dtype):
    n, D = residual.shape
    step = row_step(n)
    slots = len(weights)
    width = weights[0].shape[2]
    return call(
        functools.partial(token_pull_kernel, slots), "token_pull", (n // step,),
        [pl.BlockSpec((step, width), lambda i, p: (i, p[0]))]
        + [pl.BlockSpec((3, step, width), lambda i, p: (0, i, 0))] * slots
        + [held((3, D, width))] * slots,
        [row_spec(step, width)],
        [shaped(dtype, n, width)],
        (place.reshape(1), residual, *mixed_grads, *weights), 6 * n * D * width, prefetch=1,
    )[0]


def weight_pull_kernel(place_ref, left_ref, right_ref, *refs):
    out_ref = refs[-1]
    total = mm(left_ref[:, 0].reshape(-1, left_ref.shape[-1]), right_ref[0])
    if len(refs) > 1:
        total = total + refs[0][0].astype(F32)
    out_ref[0] = total.astype(out_ref.dtype)


def weight_pull(place, left, right, arrived, dtype):
    pairs, _, share, n = left.shape
    count, _, m = right.shape
    rows = pairs * share
    chunk = min(512, m)
    spec = pl.BlockSpec((1, rows, chunk), lambda j, i, p: (j, 0, i))
    return call(
        weight_pull_kernel, "weight_pull", (count, m // chunk),
        [
            pl.BlockSpec((pairs, 1, share, n), lambda j, i, p: (0, p[0], 0, 0)),
            pl.BlockSpec((1, n, chunk), lambda j, i, p: (j, 0, i)),
        ] + ([] if arrived is None else [spec]),
        [spec],
        [shaped(dtype, count, rows, m)],
        (place.reshape(1), left, right) + (() if arrived is None else (arrived,)),
        2 * count * rows * n * m, prefetch=1,
    )[0]


def row_step(rows):
    return 512 if rows % 512 == 0 else 128


def held(shape):
    return pl.BlockSpec(shape, lambda *_: (0,) * len(shape), pipeline_mode=pl.Buffered(1))


def shaped(dtype, *shape):
    return jax.ShapeDtypeStruct(shape, dtype)


def call(body, name, grid, in_specs, out_specs, out_shape, operands, flops, scratch=(), prefetch=0):
    size = sum(math.prod(o.shape) * o.dtype.itemsize for o in list(operands) + list(out_shape))
    return pl.pallas_call(
        body,
        grid_spec=pltpu.PrefetchScalarGridSpec(
            num_scalar_prefetch=prefetch,
            grid=grid,
            in_specs=in_specs,
            out_specs=out_specs,
            scratch_shapes=list(scratch),
        ),
        out_shape=out_shape,
        compiler_params=pltpu.CompilerParams(vmem_limit_bytes=VMEM_LIMIT),
        cost_estimate=pl.CostEstimate(flops=flops, bytes_accessed=size, transcendentals=0),
        name=name,
    )(*operands)


def row_spec(step, width):
    return pl.BlockSpec((step, width), lambda i, *_: (i, 0))


def column_spec(width, step):
    return pl.BlockSpec((width, step), lambda i, *_: (0, i))


def swap_halves(block):
    lane = lax.broadcasted_iota(jnp.int32, block.shape, 1)
    width = block.shape[1]
    return jnp.where((lane & 32) == 0, pltpu.roll(block, width - 32, 1), pltpu.roll(block, 32, 1))


def wide_table(table, width):
    return jnp.concatenate([table] * (width // 128), axis=1)


def qkv_kernel(x_ref, w_ref, b_ref, cos_ref, sin_ref, out_ref):
    which = pl.program_id(0)
    mixed = mm(x_ref[...], w_ref[0]) + b_ref[pl.ds(which, 1), :]
    width = mixed.shape[1]

    @pl.when(which < 2)
    def _():
        turned = mixed * wide_table(cos_ref[...], width)
        turned = turned + swap_halves(mixed) * wide_table(sin_ref[...], width)
        out_ref[0] = turned.astype(BF16)

    @pl.when(which == 2)
    def _():
        out_ref[0] = mixed.astype(BF16)


def project_qkv(x, weight, bias, cosine, sine):
    n, D = x.shape
    width = weight.shape[2]
    step = row_step(n)
    return call(
        qkv_kernel, "project_qkv", (3, n // step),
        [
            pl.BlockSpec((step, D), lambda j, i: (i, 0)),
            pl.BlockSpec((1, D, width), lambda j, i: (j, 0, 0)),
            held(bias.shape),
            pl.BlockSpec((step, 128), lambda j, i: (i, 0)),
            pl.BlockSpec((step, 128), lambda j, i: (i, 0)),
        ],
        [pl.BlockSpec((1, step, width), lambda j, i: (j, i, 0))],
        [shaped(BF16, 3, n, width)],
        (x, weight, bias, cosine, sine), 6 * n * D * width,
    )[0]


def normed_rows(residual):
    mean = jnp.mean(residual, axis=1, keepdims=True)
    centred = residual - mean
    inverse = lax.rsqrt(jnp.mean(centred * centred, axis=1, keepdims=True) + 1e-05)
    return centred * inverse, inverse


def norm_pull(grad_rows, normed, inverse, gain):
    spread = grad_rows * gain
    return inverse * (
        spread
        - jnp.mean(spread, axis=1, keepdims=True)
        - normed * jnp.mean(spread * normed, axis=1, keepdims=True)
    )


def column_sums(*arrays):
    rows = [jnp.sum(array, axis=0, keepdims=True) for array in arrays]
    rows.append(jnp.zeros((8 - len(rows), rows[0].shape[1]), F32))
    return jnp.concatenate(rows, axis=0)


def add_over_steps(ref, value):
    first = pl.program_id(0) == 0

    @pl.when(first)
    def _():
        ref[...] = value

    @pl.when(jnp.logical_not(first))
    def _():
        ref[...] += value


def out_norm_kernel(slots, *refs):
    x_ref, vec_ref = refs[:2]
    att_refs, w_refs = refs[2 : 2 + slots], refs[2 + slots : 2 + 2 * slots]
    normed_ref, inverse_ref, low_ref, turned_ref = refs[2 + 2 * slots :]
    residual = x_ref[...].astype(F32) + vec_ref[0:1, :]
    for att_ref, w_ref in zip(att_refs, w_refs):
        residual = residual + mm(att_ref[...], w_ref[...])
    normed, inverse = normed_rows(residual)
    hidden = normed * vec_ref[1:2, :] + vec_ref[2:3, :]
    normed_ref[...] = normed
    inverse_ref[...] = inverse
    low_ref[...] = hidden.astype(BF16)
    turned_ref[...] = hidden.T.astype(BF16)


def out_and_norm(x, vectors, attended, weights):
    n, D = x.shape
    step = row_step(n)
    slots = len(attended)
    width = attended[0].shape[1]
    return call(
        functools.partial(out_norm_kernel, slots), "out_and_norm", (n // step,),
        [row_spec(step, D), held(vectors.shape)]
        + [row_spec(step, width)] * slots + [held((width, D))] * slots,
        [row_spec(step, D), row_spec(step, 1), row_spec(step, D), column_spec(D, step)],
        [shaped(F32, n, D), shaped(F32, n, 1), shaped(BF16, n, D), shaped(BF16, D, n)],
        (x, vectors, *attended, *weights), 2 * n * D * D,
    )


GELU_TERMS = (
    0.23532527933595032, 0.09138803439798156, 0.6495603483388861,
    -0.6354014529895687, 0.8866650885491606, -0.22753729931242958,
)


def gelu_parts(values):
    size = jnp.abs(values)
    part = pl.reciprocal(1.0 + (0.39 / math.sqrt(2.0)) * size)
    bell = jnp.exp(-0.5 * (values * values))
    series = 0.5 * GELU_TERMS[-1]
    for term in GELU_TERMS[-2::-1]:
        series = series * part + 0.5 * term
    tail = series * part * bell
    below = jnp.where(values >= 0.0, 1.0 - tail, tail)
    return values * below, below + values * bell * (1.0 / math.sqrt(2.0 * math.pi))


def up_kernel(x_ref, w_ref, b_ref, active_ref, slope_ref):
    width = w_ref.shape[1]
    chunk = min(512, width)
    for first in range(0, width, chunk):
        at = slice(first, first + chunk)
        active, slope = gelu_parts(mm(x_ref[...], w_ref[:, at]) + b_ref[:, at])
        active_ref[:, at] = active.astype(BF16)
        slope_ref[:, at] = slope


def up_and_gelu(x, weight, bias):
    n, D = x.shape
    width = weight.shape[1]
    step = row_step(n)
    return call(
        up_kernel, "up_and_gelu", (n // step,),
        [row_spec(step, D), held(weight.shape), held(bias.shape)],
        [row_spec(step, width)] * 2,
        [shaped(BF16, n, width), shaped(F32, n, width)],
        (x, weight, bias), 5 * n * D * width,
    )


def down_norm_kernel(slots, *refs):
    normed_ref, vec_ref, proj_ref = refs[:3]
    act_refs, w_refs = refs[3 : 3 + slots], refs[3 + slots : 3 + 2 * slots]
    normed_out, inverse_ref, low_ref, unit_ref, unit_low_ref, unit_inverse_ref = refs[3 + 2 * slots :]
    residual = normed_ref[...] * vec_ref[1:2, :] + vec_ref[2:3, :] + vec_ref[3:4, :]
    for act_ref, w_ref in zip(act_refs, w_refs):
        residual = residual + mm(act_ref[...], w_ref[...])
    normed, inverse = normed_rows(residual)
    normed_out[...] = normed
    inverse_ref[...] = inverse
    low = (normed * vec_ref[4:5, :] + vec_ref[5:6, :]).astype(BF16)
    low_ref[...] = low
    embedding = mm(low, proj_ref[...])
    unit_inverse = lax.rsqrt(jnp.sum(embedding * embedding, axis=1, keepdims=True) + 1e-06)
    unit = embedding * unit_inverse
    unit_ref[...] = unit
    unit_low_ref[...] = unit.astype(BF16)
    unit_inverse_ref[...] = unit_inverse


def down_and_norm(normed, vectors, proj, active, weights):
    n, D = normed.shape
    step = row_step(n)
    slots = len(active)
    width = active[0].shape[1]
    return call(
        functools.partial(down_norm_kernel, slots), "down_and_norm", (n // step,),
        [row_spec(step, D), held(vectors.shape), held(proj.shape)]
        + [row_spec(step, width)] * slots + [held((width, D))] * slots,
        [
            row_spec(step, D), row_spec(step, 1), row_spec(step, D),
            row_spec(step, 128), row_spec(step, 128), row_spec(step, 1),
        ],
        [
            shaped(F32, n, D), shaped(F32, n, 1), shaped(BF16, n, D),
            shaped(F32, n, 128), shaped(BF16, n, 128), shaped(F32, n, 1),
        ],
        (normed, vectors, proj, *active, *weights), 2 * n * D * width * slots,
    )


def head_pull_kernel(
    grad_ref, unit_ref, unit_inverse_ref, proj_ref, normed_ref, inverse_ref, vec_ref,
    embed_ref, residual_ref, low_ref, turned_ref, sum_ref,
):
    grad, unit = grad_ref[...], unit_ref[...]
    embed = unit_inverse_ref[...] * (grad - unit * jnp.sum(grad * unit, axis=1, keepdims=True))
    embed = embed.astype(BF16)
    embed_ref[...] = embed
    output_grad = mm(embed, proj_ref[...], NT)
    normed = normed_ref[...]
    residual = norm_pull(output_grad, normed, inverse_ref[...], vec_ref[4:5, :])
    residual_ref[...] = residual
    low_ref[...] = residual.astype(BF16)
    turned_ref[...] = residual.T.astype(BF16)
    add_over_steps(sum_ref, column_sums(residual, output_grad * normed, output_grad))


def head_pull(unit_grad, unit, unit_inverse, proj, normed, inverse, vectors):
    n, D = normed.shape
    step = row_step(n)
    return call(
        head_pull_kernel, "head_pull", (n // step,),
        [
            row_spec(step, 128), row_spec(step, 128), row_spec(step, 1), held(proj.shape),
            row_spec(step, D), row_spec(step, 1), held(vectors.shape),
        ],
        [
            row_spec(step, 128), row_spec(step, D), row_spec(step, D),
            column_spec(D, step), pl.BlockSpec((8, D), lambda i: (0, 0)),
        ],
        [
            shaped(BF16, n, 128), shaped(F32, n, D), shaped(BF16, n, D),
            shaped(BF16, D, n), shaped(F32, 8, D),
        ],
        (unit_grad, unit, unit_inverse, proj, normed, inverse, vectors), 4 * n * D * 128,
    )


def up_pull_kernel(branch_ref, w_ref, slope_ref, out_ref, sum_ref):
    width = w_ref.shape[0]
    chunk = min(512, width)
    sums = []
    for first in range(0, width, chunk):
        at = slice(first, first + chunk)
        low = (mm(branch_ref[...], w_ref[at, :], NT) * slope_ref[:, at]).astype(BF16)
        out_ref[:, at] = low
        sums.append(column_sums(low.astype(F32)))
    add_over_steps(sum_ref, jnp.concatenate(sums, axis=1))


def up_pull(branch, weight, slope):
    n, D = branch.shape
    width = weight.shape[0]
    step = row_step(n)
    return call(
        up_pull_kernel, "up_pull", (n // step,),
        [row_spec(step, D), held(weight.shape), row_spec(step, width)],
        [row_spec(step, width), pl.BlockSpec((8, width), lambda i: (0, 0))],
        [shaped(BF16, n, width), shaped(F32, 8, width)],
        (branch, weight, slope), 2 * n * D * width,
    )


def hidden_pull_kernel(slots, *refs):
    residual_ref, normed_ref, inverse_ref, vec_ref = refs[:4]
    pre_refs, up_refs, out_refs = (refs[4 + j * slots : 4 + (j + 1) * slots] for j in range(3))
    rest = refs[4 + 3 * slots :]
    grad_ref, turned_ref, sum_ref = rest[:3]
    att_refs = rest[3:]
    hidden_grad = residual_ref[...]
    for pre_ref, up_ref in zip(pre_refs, up_refs):
        hidden_grad = hidden_grad + mm(pre_ref[...], up_ref[...], NT)
    normed = normed_ref[...]
    residual = norm_pull(hidden_grad, normed, inverse_ref[...], vec_ref[1:2, :])
    grad_ref[...] = residual
    low = residual.astype(BF16)
    turned_ref[...] = residual.T.astype(BF16)
    add_over_steps(sum_ref, column_sums(residual, hidden_grad * normed, hidden_grad))
    for att_ref, out_ref in zip(att_refs, out_refs):
        att_ref[...] = mm(low, out_ref[...], NT).astype(BF16)


def hidden_pull(residual, normed, inverse, vectors, pre_grads, ups, outs):
    n, D = residual.shape
    step = row_step(n)
    slots = len(ups)
    wide, width = ups[0].shape[1], outs[0].shape[0]
    return call(
        functools.partial(hidden_pull_kernel, slots), "hidden_pull", (n // step,),
        [row_spec(step, D), row_spec(step, D), row_spec(step, 1), held(vectors.shape)]
        + [row_spec(step, wide)] * slots + [held((D, wide))] * slots
        + [held((width, D))] * slots,
        [row_spec(step, D), column_spec(D, step), pl.BlockSpec((8, D), lambda i: (0, 0))]
        + [row_spec(step, width)] * slots,
        [shaped(F32, n, D), shaped(BF16, D, n), shaped(F32, 8, D)]
        + [shaped(BF16, n, width)] * slots,
        (residual, normed, inverse, vectors, *pre_grads, *ups, *outs),
        2 * n * D * (wide + width) * slots,
    )


def token_pull_kernel(slots, place_ref, *refs):
    residual_ref = refs[0]
    mixed_refs, w_refs = refs[1 : 1 + slots], refs[1 + slots : 1 + 2 * slots]
    out_ref = refs[-1]
    width = out_ref.shape[1]
    at = pl.ds(pl.multiple_of(place_ref[0] * width, width), width)
    total = residual_ref[...]
    for mixed_ref, w_ref in zip(mixed_refs, w_refs):
        for which in range(3):
            total = total + mm(mixed_ref[which], w_ref[which, at, :], NT)
    out_ref[...] = total.astype(out_ref.dtype)


def token_pull(place, residual, mixed_grads, weights, dtype):
    n, D = residual.shape
    step = row_step(n)
    slots = len(weights)
    width = weights[0].shape[2]
    return call(
        functools.partial(token_pull_kernel, slots), "token_pull", (n // step,),
        [pl.BlockSpec((step, width), lambda i, p: (i, p[0]))]
        + [pl.BlockSpec((3, step, width), lambda i, p: (0, i, 0))] * slots
        + [held((3, D, width))] * slots,
        [row_spec(step, width)],
        [shaped(dtype, n, width)],
        (place.reshape(1), residual, *mixed_grads, *weights), 6 * n * D * width, prefetch=1,
    )[0]


def weight_pull_kernel(place_ref, left_ref, right_ref, *refs):
    out_ref = refs[-1]
    total = mm(left_ref[:, 0].reshape(-1, left_ref.shape[-1]), right_ref[0])
    if len(refs) > 1:
        total = total + refs[0][0].astype(F32)
    out_ref[0] = total.astype(out_ref.dtype)


def weight_pull(place, left, right, arrived, dtype):
    pairs, _, share, n = left.shape
    count, _, m = right.shape
    rows = pairs * share
    chunk = min(512, m)
    spec = pl.BlockSpec((1, rows, chunk), lambda j, i, p: (j, 0, i))
    return call(
        weight_pull_kernel, "weight_pull", (count, m // chunk),
        [
            pl.BlockSpec((pairs, 1, share, n), lambda j, i, p: (0, p[0], 0, 0)),
            pl.BlockSpec((1, n, chunk), lambda j, i, p: (j, 0, i)),
        ] + ([] if arrived is None else [spec]),
        [spec],
        [shaped(dtype, count, rows, m)],
        (place.reshape(1), left, right) + (() if arrived is None else (arrived,)),
        2 * count * rows * n * m, prefetch=1,
    )[0]


SEGMENTS = 8


def half_lanes(block, head, other):
    lane = lax.broadcasted_iota(jnp.int32, block.shape, 1)
    return jnp.where((lane >= DH) == (head == 1), block, other)


def scaled(block):
    return (block.astype(F32) * DH**-0.5).astype(BF16)


def three_terms(value):
    high = value.astype(BF16).astype(F32)
    middle = (value - high).astype(BF16).astype(F32)
    return high, middle, value - high - middle


def attention_forward_kernel(
    span_ref, qkv_ref, ext_k_ref, ext_q_ref, out_ref, rest_ref, ext_ref,
    keys_ref, queries_ref, values_ref, logits_ref, *, tile,
):
    n = ext_k_ref.shape[0]
    tiles = n // tile
    for head in range(2):
        keys_ref[head] = half_lanes(qkv_ref[1], head, ext_k_ref[...])
        queries_ref[head] = half_lanes(scaled(qkv_ref[0]), head, ext_q_ref[...])
    for step in range(tiles):
        block = qkv_ref[2, step * tile : (step + 1) * tile, :]
        values_ref[step] = block.astype(F32).T.astype(BF16)

    def rows(step):
        return pl.ds(pl.multiple_of(step * tile, tile), tile)

    def by_eight(block):
        return block.reshape(tile // 8, 8, tile)

    @pl.loop(0, tiles)
    def _(step):
        low, high = span_ref[step], span_ref[tiles + step]
        queries = [queries_ref[head, rows(step), :] for head in range(2)]

        def find_top(block, tops):
            found = []
            for head in range(2):
                logits = mm(keys_ref[head, rows(block), :], queries[head], NT)
                logits_ref[head, block] = logits
                found.append(jnp.maximum(tops[head], jnp.max(by_eight(logits), axis=0)))
            return tuple(found)

        start = jnp.full((8, tile), -3e38, F32)
        tops = lax.fori_loop(low, high, find_top, (start, start))
        tops = [jnp.max(top, axis=0, keepdims=True) for top in tops]

        def add_mass(block, masses):
            after = []
            for head in range(2):
                weights = jnp.exp(logits_ref[head, block] - tops[head])
                logits_ref[head, block] = weights
                after.append(masses[head] + jnp.sum(by_eight(weights), axis=0))
            return tuple(after)

        start = jnp.zeros((8, tile), F32)
        masses = lax.fori_loop(low, high, add_mass, (start, start))
        masses = [jnp.sum(mass, axis=0, keepdims=True) for mass in masses]
        shares = [1.0 / mass for mass in masses]

        def add_values(block, totals):
            after = []
            for head in range(2):
                probs = (logits_ref[head, block] * shares[head]).astype(BF16)
                values = values_ref[block, head * DH : (head + 1) * DH, :]
                after.append(totals[head] + mm(values, probs))
            return tuple(after)

        zero = jnp.zeros((DH, tile), F32)
        outs = lax.fori_loop(low, high, add_values, (zero, zero))
        extras = []
        for head in range(2):
            terms = three_terms(-(tops[head] + jnp.log(masses[head])))
            extras.append(
                jnp.concatenate(
                    [jnp.zeros((8, tile), F32), *terms, jnp.zeros((DH - 11, tile), F32)], axis=0
                )
            )
        out = jnp.concatenate(outs, axis=0).T
        out_ref[rows(step), :] = out.astype(BF16)
        rest_ref[rows(step), :] = (out - out.astype(BF16).astype(F32)).astype(BF16)
        extra = jnp.concatenate(extras[::-1], axis=0).T
        ext_ref[rows(step), :] = (extra + ext_q_ref[rows(step), :].astype(F32)).astype(BF16)


def attention_forward(spans, qkv, ext_k, ext_q, tile):
    _, n, width = qkv.shape
    wide = pl.BlockSpec((n, 128), lambda i, *_: (0, i))
    tiles = n // tile
    return call(
        functools.partial(attention_forward_kernel, tile=tile), "attention_forward",
        (width // 128,),
        [pl.BlockSpec((3, n, 128), lambda i, *_: (0, 0, i)), held((n, 128)), held((n, 128))],
        [wide, wide, wide],
        [shaped(BF16, n, width)] * 3,
        (spans, qkv, ext_k, ext_q), 6_000_000_000, prefetch=1,
        scratch=[
            pltpu.VMEM((2, n, 128), BF16), pltpu.VMEM((2, n, 128), BF16),
            pltpu.VMEM((tiles, 128, tile), BF16), pltpu.VMEM((2, tiles, tile, tile), F32),
        ],
    )


def attention_backward_kernel(
    span_ref, qkv_ref, ext_ref, att_ref, rest_ref, grad_ref, ext_k_ref, cos_ref, sin_ref,
    out_ref, sum_ref,
    keys_ref, turned_ref, values_ref, queries_ref, plain_ref, grads_ref, plain_grads_ref,
    dq_ref, dk_ref, dv_ref, *, tile,
):
    n = ext_k_ref.shape[0]
    tiles = n // tile
    zeros = jnp.zeros((n, 128), BF16)
    lane = lax.broadcasted_iota(jnp.int32, (n, 128), 1)
    product = grad_ref[...].astype(F32) * (att_ref[...].astype(F32) + rest_ref[...].astype(F32))
    query = scaled(qkv_ref[0])
    for head in range(2):
        keys_ref[head] = half_lanes(qkv_ref[1], head, ext_k_ref[...])
        values_ref[head] = half_lanes(qkv_ref[2], head, ext_k_ref[...])
        queries_ref[head] = half_lanes(query, head, ext_ref[...])
        plain_ref[head] = half_lanes(query, head, zeros)
        plain_grads_ref[head] = half_lanes(grad_ref[...], head, zeros)
        inner = jnp.sum(half_lanes(product, head, 0.0), axis=1, keepdims=True)
        extra = jnp.zeros((n, 128), F32)
        for place, term in enumerate(three_terms(-inner)):
            extra = jnp.where((lane & (DH - 1)) == SEGMENTS + place, term, extra)
        grads_ref[head] = half_lanes(grad_ref[...], head, extra.astype(BF16))
    for step in range(tiles):
        block = scaled(qkv_ref[1, step * tile : (step + 1) * tile, :])
        turned_ref[step] = block.astype(F32).T.astype(BF16)
    dk_ref[...] = jnp.zeros((n, 128), F32)
    dv_ref[...] = jnp.zeros((n, 128), F32)

    def rows(step):
        return pl.ds(pl.multiple_of(step * tile, tile), tile)

    @pl.loop(0, tiles)
    def _(step):
        queries = [queries_ref[head, rows(step), :] for head in range(2)]
        grads = [grads_ref[head, rows(step), :] for head in range(2)]
        plain = jnp.concatenate([plain_ref[head, rows(step), :] for head in range(2)], axis=0)
        plain_grads = jnp.concatenate(
            [plain_grads_ref[head, rows(step), :] for head in range(2)], axis=0
        )

        def one_block(block, totals):
            probs, slopes, after = [], [], []
            for head in range(2):
                weights = jnp.exp(mm(keys_ref[head, rows(block), :], queries[head], NT))
                flow = mm(values_ref[head, rows(block), :], grads[head], NT)
                slope = (weights * flow).astype(BF16)
                probs.append(weights.astype(BF16))
                slopes.append(slope)
                turned = turned_ref[block, head * DH : (head + 1) * DH, :]
                after.append(totals[head] + mm(turned, slope))
            dv_ref[rows(block), :] += mm(jnp.concatenate(probs, axis=1), plain_grads)
            dk_ref[rows(block), :] += mm(jnp.concatenate(slopes, axis=1), plain)
            return tuple(after)

        zero = jnp.zeros((DH, tile), F32)
        totals = lax.fori_loop(span_ref[step], span_ref[tiles + step], one_block, (zero, zero))
        dq_ref[rows(step), :] = jnp.concatenate(totals, axis=0).T

    def finish(step, sums):
        cosine, sine = cos_ref[rows(step), :], sin_ref[rows(step), :]
        added = []
        for which, src in enumerate((dq_ref, dk_ref, dv_ref)):
            block = src[rows(step), :]
            if which < 2:
                block = block * cosine - swap_halves(block) * sine
            low = block.astype(BF16)
            out_ref[which, rows(step), :] = low
            added.append(sums[which] + jnp.sum(low.astype(F32), axis=0, keepdims=True))
        return tuple(added)

    zero = jnp.zeros((1, 128), F32)
    sums = lax.fori_loop(0, tiles, finish, (zero, zero, zero))
    sum_ref[...] = jnp.concatenate(sums + (jnp.zeros((5, 128), F32),), axis=0)


def attention_backward(spans, qkv, ext, attended, rest, grads, ext_k, cosine, sine, tile):
    _, n, width = qkv.shape
    wide = pl.BlockSpec((n, 128), lambda i, *_: (0, i))
    three = pl.BlockSpec((3, n, 128), lambda i, *_: (0, 0, i))
    tiles = n // tile
    two = pltpu.VMEM((2, n, 128), BF16)
    return call(
        functools.partial(attention_backward_kernel, tile=tile), "attention_backward",
        (width // 128,),
        [three, wide, wide, wide, wide, held((n, 128)), held((n, 128)), held((n, 128))],
        [three, pl.BlockSpec((8, 128), lambda i, *_: (0, i))],
        [shaped(BF16, 3, n, width), shaped(F32, 8, width)],
        (spans, qkv, ext, attended, rest, grads, ext_k, cosine, sine), 15_000_000_000, prefetch=1,
        scratch=[two, pltpu.VMEM((tiles, 128, tile), BF16)] + [two] * 5
        + [pltpu.VMEM((n, 128), F32)] * 3,
    )


STRIP = 32


def score_kernel(begin_ref, size_ref, doc_ref, query_ref, pick_ref, out_ref, sim_ref):
    group = pl.program_id(0)
    docs, width = pick_ref.shape[1:]
    chunk = min(256, doc_ref.shape[0])

    @pl.loop(0, doc_ref.shape[0] // chunk)
    def _(step):
        at = pl.ds(pl.multiple_of(step * chunk, chunk), chunk)
        sim_ref[at, :] = mm(doc_ref[at, :], query_ref[...], NT)

    for doc in range(docs):
        begin = begin_ref[group * docs + doc]
        end = begin + size_ref[group * docs + doc]
        pick = pick_ref[0, doc : doc + 1, :]

        def strip(step, total):
            first = pl.multiple_of(step * STRIP, STRIP)
            row = lax.broadcasted_iota(jnp.int32, (STRIP, width), 0) + first
            held = jnp.where(row == pick, sim_ref[pl.ds(first, STRIP), :], 0.0)
            return total + jnp.sum(held.reshape(STRIP // 8, 8, width), axis=0)

        total = lax.fori_loop(
            begin // STRIP, (end + STRIP - 1) // STRIP, strip, jnp.zeros((8, width), F32)
        )
        out_ref[0, doc : doc + 1, :] = jnp.sum(total, axis=0, keepdims=True)


def score_grad_kernel(
    begin_ref, size_ref, doc_ref, query_ref, pick_ref, weight_ref, doc_out, query_out, sparse_ref
):
    group = pl.program_id(0)
    docs, width = pick_ref.shape[1:]
    doc_rows = doc_ref.shape[0]

    @pl.loop(0, doc_rows // STRIP)
    def _(step):
        first = pl.multiple_of(step * STRIP, STRIP)
        row = lax.broadcasted_iota(jnp.int32, (STRIP, width), 0) + first
        low = jnp.int32(0)
        high = jnp.int32(0)
        for doc in range(docs):
            begin = begin_ref[group * docs + doc]
            end = begin + size_ref[group * docs + doc]
            low += (end <= first).astype(jnp.int32)
            high += (begin < first + STRIP).astype(jnp.int32)

        def one_doc(doc, held):
            pick = pick_ref[0, pl.ds(doc, 1), :]
            return jnp.where(row == pick, weight_ref[0, pl.ds(doc, 1), :], held)

        held = lax.fori_loop(low, high, one_doc, jnp.zeros((STRIP, width), F32))
        sparse_ref[pl.ds(first, STRIP), :] = held.astype(BF16)

    docs_t = doc_ref[...].astype(F32).T.astype(BF16)
    doc_out[...] = mm(sparse_ref[...], query_ref[...])

    @pl.when(group == 0)
    def _():
        query_out[...] = jnp.zeros_like(query_out)

    query_out[...] += mm(docs_t, sparse_ref[...])


def score_specs(doc_tile, query_tile, picks):
    groups, docs, width = picks.shape
    doc_rows = doc_tile.shape[0] // groups
    return (
        pl.BlockSpec((doc_rows, 128), lambda i, *_: (i, 0)),
        pl.BlockSpec(query_tile.shape, lambda i, *_: (0, 0)),
        pl.BlockSpec((1, docs, width), lambda i, *_: (i, 0, 0)),
    )


def score_forward(begins, sizes, doc_tile, query_tile, picks):
    groups, docs, width = picks.shape
    doc_spec, query_spec, pick_spec = score_specs(doc_tile, query_tile, picks)
    return pl.pallas_call(
        score_kernel,
        grid_spec=pltpu.PrefetchScalarGridSpec(
            num_scalar_prefetch=2,
            grid=(groups,),
            in_specs=[doc_spec, query_spec, pick_spec],
            out_specs=pick_spec,
            scratch_shapes=[pltpu.VMEM((doc_tile.shape[0] // groups, width), F32)],
        ),
        out_shape=jax.ShapeDtypeStruct((groups, docs, width), F32),
        compiler_params=pltpu.CompilerParams(vmem_limit_bytes=VMEM_LIMIT),
        name="score_forward",
    )(begins, sizes, doc_tile, query_tile, picks)


def score_backward(begins, sizes, doc_tile, query_tile, picks, weights):
    groups, docs, width = picks.shape
    doc_spec, query_spec, pick_spec = score_specs(doc_tile, query_tile, picks)
    return pl.pallas_call(
        score_grad_kernel,
        grid_spec=pltpu.PrefetchScalarGridSpec(
            num_scalar_prefetch=2,
            grid=(groups,),
            in_specs=[doc_spec, query_spec, pick_spec, pick_spec],
            out_specs=[doc_spec, pl.BlockSpec((128, width), lambda i, *_: (0, 0))],
            scratch_shapes=[pltpu.VMEM((doc_tile.shape[0] // groups, width), BF16)],
        ),
        out_shape=[
            jax.ShapeDtypeStruct(doc_tile.shape, F32),
            jax.ShapeDtypeStruct((128, width), F32),
        ],
        compiler_params=pltpu.CompilerParams(vmem_limit_bytes=VMEM_LIMIT),
        name="score_backward",
    )(begins, sizes, doc_tile, query_tile, picks, weights)


def rotary_tables(position):
    half_size = DH // 2
    frequency = jnp.exp(
        jnp.arange(half_size, dtype=F32) * (-2.0 * math.log(10000.0) / DH)
    )
    angles = position.astype(F32)[:, None] * frequency[None, :]
    cosine, sine = jnp.cos(angles), jnp.sin(angles)
    return (
        jnp.concatenate([cosine] * 4, axis=1),
        jnp.concatenate([-sine, sine, -sine, sine], axis=1),
    )


def on_device(
    tokens,
    doc_lengths,
    match_picks,
    labels,
    w_qkv,
    b_qkv,
    w_out,
    b_out,
    ln1_gain,
    ln1_bias,
    w_up,
    b_up,
    w_down,
    b_down,
    ln2_gain,
    ln2_bias,
    w_proj,
    log_scale,
):
    C = lax.axis_size("cols")
    R = lax.axis_size("rows")
    c = lax.axis_index("cols")
    r = lax.axis_index("rows")
    width = tokens.shape[1]
    D = width * C
    Q = ROW_LEN // C
    DS = (tokens.shape[0] - ROW_LEN) // C
    n = Q + DS
    tile = math.gcd(256, math.gcd(Q, DS))

    def shift_cols(value, k):
        return lax.ppermute(value, "cols", [(i, (i + k) % C) for i in range(C)])

    def swap_rows(value, bit):
        return lax.ppermute(value, "rows", [(i, i ^ bit) for i in range(R)])

    def in_order(slots):
        if len(slots) == 1:
            return slots
        if len(slots) == 2:
            return [lax.select(c == 0, slots[0], slots[1]), lax.select(c == 0, slots[1], slots[0])]
        stacked = jnp.stack(slots)
        return [
            lax.dynamic_index_in_dim(stacked, (c - j) % C, 0, keepdims=False) for j in range(C)
        ]

    parts = jnp.concatenate(
        [tokens[:ROW_LEN].reshape(C, Q, width), tokens[ROW_LEN:].reshape(C, DS, width)], axis=1
    )

    def part(k):
        return lax.dynamic_index_in_dim(parts, (c + k) % C, 0, keepdims=False)

    slots = [part(0)] + [shift_cols(part(k), k) for k in range(1, C)]
    x = jnp.concatenate(in_order(slots), axis=1)

    def gather_slots(shard):
        flat = shard.reshape(-1, shard.shape[-1])
        piece = lax.dynamic_index_in_dim(
            flat.reshape(R, flat.shape[0] // R, flat.shape[1]), r, 0, keepdims=False
        )
        others = [
            lax.all_gather(shift_cols(piece, k), "rows", axis=0, tiled=True).reshape(shard.shape)
            for k in range(1, C)
        ]
        return [shard] + others

    wqkv_slots = gather_slots(w_qkv)
    wout_slots = gather_slots(w_out)
    wup_slots = gather_slots(w_up)
    wdown_slots = gather_slots(w_down)
    wproj = jnp.concatenate(
        in_order([w_proj] + [shift_cols(w_proj, k) for k in range(1, C)]), axis=0
    )

    pack = [b_qkv.reshape(-1), b_up, b_out, ln1_gain, ln1_bias, b_down, ln2_gain, ln2_bias]
    ends = [0]
    for vector in pack:
        ends.append(ends[-1] + vector.shape[0])
    packed = jnp.concatenate(pack)
    packs = [packed] + [shift_cols(packed, k) for k in range(1, C)]
    ordered_packs = in_order(packs)

    def of_slot(which, k):
        return packs[k][ends[which] : ends[which + 1]]

    def whole(which):
        return jnp.concatenate([p[ends[which] : ends[which + 1]] for p in ordered_packs])

    bqkv_slots = [of_slot(0, k).reshape(b_qkv.shape) for k in range(C)]
    bup_slots = [of_slot(1, k)[None, :] for k in range(C)]
    bout, gain1, bias1, bdown, gain2, bias2 = [whole(which) for which in range(2, 8)]
    zero_row = jnp.zeros_like(bout)
    vectors = jnp.stack([bout, gain1, bias1, bdown, gain2, bias2, zero_row, zero_row])

    own_sizes = lax.dynamic_index_in_dim(
        lax.dynamic_index_in_dim(doc_lengths, r, 0, keepdims=False), c, 0, keepdims=False
    )
    own_ends = jnp.cumsum(own_sizes)
    places = jnp.arange(DS, dtype=jnp.int32)
    passed = places[:, None] >= own_ends[None, :]
    slot_id = jnp.sum(passed.astype(jnp.int32), axis=1)
    slot_begin = jnp.sum(jnp.where(passed, own_sizes[None, :], 0), axis=1)
    query_places = jnp.arange(Q, dtype=jnp.int32)
    position = jnp.concatenate([query_places % QLEN, places - slot_begin])
    cosine, sine = rotary_tables(position)
    segment = jnp.concatenate([(query_places // QLEN) % SEGMENTS, slot_id])
    lane = jnp.arange(128, dtype=jnp.int32)[None, :] % DH
    same = segment[:, None] == lane
    ext_k = (same | ((lane >= SEGMENTS) & (lane < SEGMENTS + 3))).astype(BF16)
    ext_q = jnp.where((lane < SEGMENTS) & ~same, -1e30, 0.0).astype(BF16)
    q_tiles, d_tiles = Q // tile, DS // tile
    steps = jnp.arange(q_tiles, dtype=jnp.int32)
    first_rows = jnp.arange(d_tiles, dtype=jnp.int32) * tile
    is_passed = first_rows[:, None] >= own_ends[None, :]
    low_rows = jnp.sum(jnp.where(is_passed, own_sizes[None, :], 0), axis=1)
    last_passed = (first_rows + tile - 1)[:, None] >= own_ends[None, :]
    high_rows = jnp.min(jnp.where(last_passed, DS, own_ends[None, :]), axis=1)
    spans = jnp.concatenate(
        [steps, q_tiles + low_rows // tile, steps + 1, q_tiles + (high_rows + tile - 1) // tile]
    ).astype(jnp.int32)

    qkv, attended, rests, exts = [], [], [], []
    for k in range(C):
        qkv.append(project_qkv(x, wqkv_slots[k], bqkv_slots[k], cosine, sine))
        out, rest, ext = attention_forward(spans, qkv[k], ext_k, ext_q, tile)
        attended.append(out)
        rests.append(rest)
        exts.append(ext)
    normed_one, inverse_one, hidden_low, hidden_t = out_and_norm(x, vectors, attended, wout_slots)
    active, slopes = zip(*[up_and_gelu(hidden_low, wup_slots[k], bup_slots[k]) for k in range(C)])
    normed_two, inverse_two, output_low, unit, unit_low, unit_inverse = down_and_norm(
        normed_one, vectors, wproj, active, wdown_slots
    )

    doc_tile = lax.all_gather(unit_low[Q:], "rows", axis=0, tiled=True)
    query_tile = jnp.concatenate(
        in_order([unit_low[:Q]] + [shift_cols(unit_low[:Q], k) for k in range(1, C)]), axis=0
    )
    queries_here, tile_docs, _ = match_picks.shape
    docs = own_sizes.shape[0]
    sizes = lax.dynamic_index_in_dim(doc_lengths, c, 1, keepdims=False)
    begins = jnp.cumsum(sizes, axis=1) - sizes
    sizes_flat, begins_flat = sizes.reshape(-1), begins.reshape(-1)
    picks = jnp.transpose(match_picks, (1, 0, 2)).reshape(tile_docs, queries_here * QLEN)
    picks = begins_flat[:, None] + picks % sizes_flat[:, None]
    picks = picks.reshape(R, docs, queries_here * QLEN)
    sims = score_forward(begins_flat, sizes_flat, doc_tile, query_tile, picks)
    scores = jnp.sum(sims.reshape(tile_docs, queries_here, QLEN), axis=2).T

    scale = jnp.exp(log_scale[0])
    z = scale * scores
    row_top = jnp.max(z, axis=1)
    row_mass = jnp.sum(jnp.exp(z - row_top[:, None]), axis=1)
    is_label = (
        jnp.arange(tile_docs, dtype=jnp.int32)[None, :] == (labels - c * tile_docs)[:, None]
    )
    chosen = jnp.sum(jnp.where(is_label, z, 0.0), axis=1)
    own_stats = jnp.stack([row_top, row_mass, chosen])
    stats = jnp.stack([own_stats] + [shift_cols(own_stats, k) for k in range(1, C)])
    top_all = jnp.max(stats[:, 0], axis=0)
    mass_all = jnp.sum(stats[:, 1] * jnp.exp(stats[:, 0] - top_all), axis=0)
    log_total = top_all + jnp.log(mass_all)
    loss = log_total - jnp.sum(stats[:, 2], axis=0)
    dz = (jnp.exp(z - log_total[:, None]) - is_label.astype(F32)) / (queries_here * R)
    scale_part = jnp.sum(dz * z)
    dscores = (scale * dz).astype(BF16).astype(F32)
    weights = jnp.broadcast_to(
        dscores.T[:, :, None], (tile_docs, queries_here, QLEN)
    ).reshape(R, docs, queries_here * QLEN)
    doc_grad, query_grad_t = score_backward(
        begins_flat, sizes_flat, doc_tile, query_tile, picks, weights
    )
    query_parts = query_grad_t.T.reshape(C, Q, 128)

    def query_part(k):
        return lax.dynamic_index_in_dim(query_parts, (c + k) % C, 0, keepdims=False)

    query_grad = query_part(0)
    for k in range(1, C):
        query_grad = query_grad + shift_cols(query_part(k), k)

    def halve(total, bit, wire):
        size = total.shape[0] // 2
        pairs = total.reshape((size, 2) + total.shape[1:])
        mine = (r // bit) % 2
        send = lax.dynamic_index_in_dim(pairs, 1 - mine, 1, keepdims=False).astype(wire)
        keep = lax.dynamic_index_in_dim(pairs, mine, 1, keepdims=False)
        return keep + swap_rows(send, bit).astype(F32)

    doc_sum = doc_grad.reshape(R, DS, 128)
    bit = 1
    while bit < R:
        doc_sum = halve(doc_sum, bit, BF16)
        bit *= 2
    unit_grad = jnp.concatenate([query_grad, doc_sum[0]], axis=0)

    core = r % 2

    def weight_grad(left_t, right_slots):
        left = left_t.reshape(R // 2, 2, -1, n)
        arrived = [
            swap_rows(weight_pull(1 - core, left, right, None, BF16), 1)
            for right in right_slots[::-1]
        ][::-1]
        total = None
        for k in range(C - 1, 0, -1):
            part = weight_pull(core, left, right_slots[k], arrived[k], BF16)
            part = shift_cols(part, C - k).astype(F32)
            total = part if total is None else total + part
        own = weight_pull(core, left, right_slots[0], arrived[0], F32)
        total = own if total is None else own + total
        total = jnp.moveaxis(total.reshape(total.shape[0], R // 2, -1, total.shape[2]), 1, 0)
        bit = 2
        while bit < R:
            total = halve(total, bit, BF16)
            bit *= 2
        return total[0]

    embed_grad, resid_two_grad, branch, branch_t, head_sums = head_pull(
        unit_grad, unit, unit_inverse, wproj, normed_two, inverse_two, vectors
    )
    down_grad = weight_grad(branch_t, [a[None] for a in active])
    pre_grads, up_sums = zip(
        *[up_pull(branch, wdown_slots[k], slopes[k]) for k in range(C)]
    )
    up_grad = weight_grad(hidden_t, [g[None] for g in pre_grads])
    resid_one_grad, branch_one_t, hidden_sums, *attended_grads = hidden_pull(
        resid_two_grad, normed_one, inverse_one, vectors, pre_grads, wup_slots, wout_slots
    )
    out_grad = weight_grad(branch_one_t, [a[None] for a in attended])
    output_slots = [
        lax.dynamic_slice_in_dim(output_low, ((c - k) % C) * width, width, 1)[None]
        for k in range(C)
    ]
    proj_grad = weight_grad(embed_grad.T, output_slots)
    mixed_grads, mixed_sums = [None] * C, [None] * C
    for k in range(C - 1, -1, -1):
        mixed_grads[k], mixed_sums[k] = attention_backward(
            spans, qkv[k], exts[k], attended[k], rests[k], attended_grads[k], ext_k, cosine, sine,
            tile,
        )
    sent = [
        shift_cols(token_pull((c + k) % C, resid_one_grad, mixed_grads, wqkv_slots, BF16), k)
        for k in range(1, C)
    ]
    kept = token_pull(c, resid_one_grad, mixed_grads, wqkv_slots, F32)
    ordered = in_order([kept] + [s.astype(F32) for s in sent])
    tokens_grad = jnp.concatenate([s[:Q] for s in ordered] + [s[Q:] for s in ordered], axis=0)
    qkv_grad = weight_grad(x.T, mixed_grads)

    def cut(values, slot_rows):
        return values.reshape(slot_rows, R, -1)

    own_order = [(c - k) % C for k in range(C)]
    canonical = jnp.stack(
        [hidden_sums[0], hidden_sums[1], hidden_sums[2], head_sums[0], head_sums[1], head_sums[2]]
    ).reshape(6, C, R, -1)
    slots_small = []
    for k in range(C):
        rows = [mixed_sums[k][j].reshape(R, -1) for j in range(3)]
        rows.append(up_sums[k][0].reshape(R, -1))
        rows += [
            lax.dynamic_index_in_dim(canonical[j], own_order[k], 0, keepdims=False)
            for j in range(6)
        ]
        rows.append(jnp.broadcast_to(scale_part, (R, 1)))
        slots_small.append(jnp.concatenate(rows, axis=1))
    small = halve(jnp.stack(slots_small, axis=1), 1, F32)
    own_small = small[:, 0]
    for k in range(1, C):
        own_small = own_small + shift_cols(small[:, k], C - k)
    bit = 2
    while bit < R:
        own_small = halve(own_small, bit, F32)
        bit *= 2
    small = own_small[0]
    one = D // (C * R)
    up_part = bup_slots[0].shape[1] // R
    bounds = [3 * one, 3 * one + up_part]
    for _ in range(6):
        bounds.append(bounds[-1] + one)
    pieces = [small[a:b] for a, b in zip(bounds[:-1], bounds[1:])]
    bup_out, bout_out, gain1_out, bias1_out, bdown_out, gain2_out, bias2_out = pieces
    return (
        scores,
        loss,
        tokens_grad,
        qkv_grad,
        small[: bounds[0]].reshape(3, one),
        out_grad[0].T,
        bout_out,
        gain1_out,
        bias1_out,
        up_grad[0],
        bup_out,
        down_grad[0].T,
        bdown_out,
        gain2_out,
        bias2_out,
        proj_grad[0].T,
        small[-1:],
    )


def solution(mesh):
    in_specs = (
        P("rows", "cols"),
        P(),
        P("rows", "cols", None),
        P("rows"),
        P(None, None, "cols"),
        P(None, "cols"),
        P("cols", None),
        P("cols"),
        P("cols"),
        P("cols"),
        P(None, "cols"),
        P("cols"),
        P("cols", None),
        P("cols"),
        P("cols"),
        P("cols"),
        P("cols", None),
        P(),
    )
    out_specs = (
        P("rows", "cols"),
        P("rows"),
        P("rows", "cols"),
        P(None, "rows", "cols"),
        P(None, ("cols", "rows")),
        P("cols", "rows"),
        P(("cols", "rows")),
        P(("cols", "rows")),
        P(("cols", "rows")),
        P("rows", "cols"),
        P(("cols", "rows")),
        P("cols", "rows"),
        P(("cols", "rows")),
        P(("cols", "rows")),
        P(("cols", "rows")),
        P("cols", "rows"),
        P(),
    )
    return jax.shard_map(
        on_device, mesh=mesh, in_specs=in_specs, out_specs=out_specs, check_vma=False
    )
```

time: 1270 us -> 1060 us (0.83)
  matrix products: 325 us -> 0 us
  Pallas kernels: 290 us -> 563 us
  blocking collectives: 129 us -> 0 us
  starting transfers between devices: 49.7 us -> 86.6 us
  waiting for transfers between devices: 286 us -> 258 us
  local copies, waits for them, and re-layouts: 94.9 us -> 71.3 us
    dot_general x51 -> x0, matrix products: 325 us -> none  [mm(): return lax.dot_general(left, right, dims, preferred_element_type=F32)]
    pallas_call x2 -> x36, Pallas kernels: 206 us -> 479 us  [call(): pl.pallas_call(body, grid_spec=pltpu.PrefetchScalarGridSpec(num_scalar_pr...]
    all_gather x4 -> x0, blocking collectives: 48.8 us -> none  [the longest x1 32.6 us: on_device(): spread = lax.all_gather(jnp.concatenate(vectors), 'cols', axis=0)]
    ppermute x12 -> x17, starting transfers between devices: 17.7 us -> 62.2 us  [shift_cols(): return lax.ppermute(value, 'cols', [(i, (i + k) % C) for i in range(C)])]
    unnamed x1 -> x0, blocking collectives: 41.6 us -> none
    psum x1 -> x0, blocking collectives: 38.7 us -> none  [on_device(): scale_sum = lax.psum(jnp.sum(dz * z), ('rows', 'cols'))]
    unnamed x8 -> x5, waiting for transfers between devices: 33 us -> 0.08 us
    unnamed x263 -> x61, local copies, waits for them, and re-layouts: 36.1 us -> 17.7 us
  transfers between devices with their start and end apart: 53 -> 55, of which waited for: 27 -> 24; matrix products, arithmetic and copies ran while one was open for 22% -> 9% of each run, Pallas kernels for 8% -> 27%
where the time goes in v2:
time: 1060 us; the launch traced here: 1050 us
  Pallas kernels  563 us (53%)
  waiting for transfers between devices  258 us (24%)
  starting transfers between devices  86.6 us (8%)
  local copies, waits for them, and re-layouts  71.3 us (7%)
  other arithmetic  57.1 us (5%)
  between operations  15.8 us (1%)
    pallas_call x36, Pallas kernels, call(): pl.pallas_call(body, grid_spec=pltpu.PrefetchScalarGridSpec(num_scalar_pr...  479 us
    ppermute x17, waiting for transfers between devices, shift_cols(): return lax.ppermute(value, 'cols', [(i, (i + k) % C) for i in range(C)])  135 us
    ppermute x33, waiting for transfers between devices, swap_rows(): return lax.ppermute(value, 'rows', [(i, i ^ bit) for i in range(R)])  90.3 us
    ppermute x17, starting transfers between devices, shift_cols(): return lax.ppermute(value, 'cols', [(i, (i + k) % C) for i in range(C)])  62.2 us
    pallas_call x1, Pallas kernels, score_backward(): pl.pallas_call(score_grad_kernel, grid_spec=pltpu.PrefetchScalarGridSpec(...  52.6 us
    all_gather x1, waiting for transfers between devices, on_device(): doc_tile = lax.all_gather(unit_low[Q:], 'rows', axis=0, tiled=True)  32.6 us
    pallas_call x1, Pallas kernels, score_forward(): pl.pallas_call(score_kernel, grid_spec=pltpu.PrefetchScalarGridSpec(num_s...  31.9 us
    ppermute x33, starting transfers between devices, swap_rows(): return lax.ppermute(value, 'rows', [(i, i ^ bit) for i in range(R)])  24.2 us
  transfers between devices with their start and end apart: 55, of which 24 were waited for; matrix products, arithmetic and copies ran while one was open for 9% of the time, Pallas kernels for 27%

profile of v2, /device:TPU:0, one launch (start us, length us, event | category | flops | bytes accessed | tf_op | source)
XLA Modules:
  0.0 1051.7 jit_solution(2054789858642948434)
XLA Ops:
  8.2 3.0 collective-permute-start.2
  11.2 4.9 collective-permute-done.2
  25.5 4.6 collective-permute-done.5
  52.2 2.8 fusion.17
  66.8 18.8 %collective-permute-done = bf16[1536,512]{1,0:T(8,128)(2,1)} collective-permute-done((bf16[1536,512]{1,0:T(8,128)(2,1)}, bf16[1536,512]{1,0:T(8,128)(2,1)}, u32[]{:S(2)}, u32[]{:S(2)}) %collective-permute-start) | collective-permute-done | bytes 1572896 | tf_op jit(solution)/shard_map/ppermute | solution.py:1548
  90.1 16.1 %project_qkv.2.qkv_ref = bf16[3,1536,512]{2,1,0:T(8,128)(2,1)} custom-call(bf16[1536,1024]{1,0:T(8,128)(2,1)} %get-tuple-element.179.x_ref.refs_0_, bf16[3,1024,512]{2,1,0:T(8,128)(2,1)} %refs_3_.3, f32[3,512]{1,0:T(4,128)} %b_ref.1, f32[1536,128]{1,0:T(8,128)} %pad_maximum_fusion.2.cos_ref, f32[1536,128]{1,0:T(8,128)} %pad_maximum_fusion.3.sin_ref), custom_call_target="tpu_custom_call" | custom-call | flops 4831838208 | bytes 12589056 | tf_op jit(solution)/shard_map/project_qkv/pallas_call | solution.py:812
  106.2 29.9 %attention_forward.2 = (bf16[1536,512]{1,0:T(8,128)(2,1)}, bf16[1536,512]{1,0:T(8,128)(2,1)}, bf16[1536,512]{1,0:T(8,128)(2,1)}) custom-call(s32[12]{0:T(128)} %pad_add_fusion.1.span_ref, bf16[3,1536,512]{2,1,0:T(8,128)(2,1)} %project_qkv.2.qkv_ref, bf16[1536,128]{1,0:T(8,128)(2,1)} %fusion.9.ext_k_ref, bf16[1536,128]{1,0:T(8,128)(2,1)} %select_convert_fusion.ext_q_ref), custom_call_target="tpu_custom_call" | custom-call | flops 6000000000 | bytes 10223664 | tf_op jit(solution)/shard_map/attention_forward/pallas_call | solution.py:812
  136.2 15.7 %project_qkv.3.qkv_ref = bf16[3,1536,512]{2,1,0:T(8,128)(2,1)} custom-call(bf16[1536,1024]{1,0:T(8,128)(2,1)} %get-tuple-element.179.x_ref.refs_0_, bf16[3,1024,512]{2,1,0:T(8,128)(2,1)} %bitcast.261, f32[3,512]{1,0:T(4,128)} %slice.234.b_ref, f32[1536,128]{1,0:T(8,128)} %pad_maximum_fusion.2.cos_ref, f32[1536,128]{1,0:T(8,128)} %pad_maximum_fusion.3.sin_ref), custom_call_target="tpu_custom_call" | custom-call | flops 4831838208 | bytes 12589056 | tf_op jit(solution)/shard_map/project_qkv/pallas_call | solution.py:812
  151.8 30.0 %attention_forward.3 = (bf16[1536,512]{1,0:T(8,128)(2,1)}, bf16[1536,512]{1,0:T(8,128)(2,1)}, bf16[1536,512]{1,0:T(8,128)(2,1)}) custom-call(s32[12]{0:T(128)} %pad_add_fusion.1.span_ref, bf16[3,1536,512]{2,1,0:T(8,128)(2,1)} %project_qkv.3.qkv_ref, bf16[1536,128]{1,0:T(8,128)(2,1)} %fusion.9.ext_k_ref, bf16[1536,128]{1,0:T(8,128)(2,1)} %select_convert_fusion.ext_q_ref), custom_call_target="tpu_custom_call" | custom-call | flops 6000000000 | bytes 10223664 | tf_op jit(solution)/shard_map/attention_forward/pallas_call | solution.py:812
  181.8 12.1 %out_and_norm.1 = (f32[1536,1024]{1,0:T(8,128)}, f32[1536,1]{1,0:T(8,128)}, bf16[1536,1024]{1,0:T(8,128)(2,1)}, bf16[1024,1536]{1,0:T(8,128)(2,1)}) custom-call(bf16[1536,1024]{1,0:T(8,128)(2,1)} %get-tuple-element.179.x_ref.refs_0_, f32[8,1024]{1,0:T(8,128)} %stack.59.refs_1_.vec_ref.refs_3_, bf16[1536,512]{1,0:T(8,128)(2,1)} %get-tuple-element.57.refs_2_.att_ref, ...), custom_call_target="tpu_custom_call" | custom-call | flops 3221225472 | bytes 21010432 | tf_op jit(solution)/shard_map/out_and_norm/pallas_call | solution.py:812
  193.9 22.7 %up_and_gelu.2 = (bf16[1536,2048]{1,0:T(8,128)(2,1)}, f32[1536,2048]{1,0:T(8,128)}) custom-call(bf16[1536,1024]{1,0:T(8,128)(2,1)} %get-tuple-element.60.x_ref, bf16[1024,2048]{1,0:T(8,128)(2,1)} %refs_6_.1, f32[1,2048]{1,0:T(1,128)} %bitcast.340), custom_call_target="tpu_custom_call" | custom-call | flops 16106127360 | bytes 26222592 | tf_op jit(solution)/shard_map/up_and_gelu/pallas_call | solution.py:812
  216.6 22.7 %up_and_gelu.3 = (bf16[1536,2048]{1,0:T(8,128)(2,1)}, f32[1536,2048]{1,0:T(8,128)}) custom-call(bf16[1536,1024]{1,0:T(8,128)(2,1)} %get-tuple-element.60.x_ref, bf16[1024,2048]{1,0:T(8,128)(2,1)} %all-gather.10.cloned.1.call-done.w_ref.refs_7_, f32[1,2048]{1,0:T(1,128)} %bitcast.341), custom_call_target="tpu_custom_call" | custom-call | flops 16106127360 | bytes 26222592 | tf_op jit(solution)/shard_map/up_and_gelu/pallas_call | solution.py:812
  239.4 25.3 %down_and_norm.1 = (f32[1536,1024]{1,0:T(8,128)}, f32[1536,1]{1,0:T(8,128)}, bf16[1536,1024]{1,0:T(8,128)(2,1)}, f32[1536,128]{1,0:T(8,128)}, bf16[1536,128]{1,0:T(8,128)(2,1)}, /*index=5*/f32[1536,1]{1,0:T(8,128)}) custom-call(f32[1536,1024]{1,0:T(8,128)} %get-tuple-element.59.refs_0_.refs_1_, f32[8,1024]{1,0:T(8,128)} %stack.59.refs_1_.vec_ref.refs_3_, ...), custom_call_target="tpu_custom_call" | custom-call | flops 12884901888 | bytes 38187008 | tf_op jit(solution)/shard_map/down_and_norm/pallas_call | solution.py:812
  267.8 2.8 copy.120
  272.9 5.9 fusion.15.pick_ref
  279.7 16.8 %collective-permute-start.7 = (bf16[512,128]{1,0:T(8,128)(2,1)S(1)}, bf16[512,128]{1,0:T(8,128)(2,1)S(1)}, u32[]{:S(2)}, u32[]{:S(2)}) collective-permute-start(bf16[512,128]{1,0:T(8,128)(2,1)S(1)} %slice.237), channel_id=1, source_target_pairs={{0,1},{1,0},{2,3},{3,2},{4,5},{5,4},{6,7},{7,6},{8,9},{9,8},{10,11... | collective-permute-start | bytes 393224 | tf_op jit(solution)/shard_map/ppermute | solution.py:1548
  296.5 2.9 collective-permute-done.7
  301.1 32.6 %all-gather.14.cloned.1.call-done.doc_ref = bf16[16384,128]{1,0:T(8,128)(2,1)} async-done(((bf16[1024,128]{1,0:T(8,128)(2,1)}), bf16[16384,128]{1,0:T(8,128)(2,1)}) %all-gather.14.cloned.1.call-update) | async-done | bytes 4194320 | tf_op jit(solution)/shard_map/all_gather | solution.py:1652
  333.7 31.9 %score_forward.1 = f32[16,4,1024]{2,1,0:T(4,128)} custom-call(s32[64]{0:T(128)} %sub.153.begin_ref, s32[64]{0:T(128)} %copy-done.22, bf16[16384,128]{1,0:T(8,128)(2,1)} %all-gather.14.cloned.1.call-done.doc_ref, bf16[1024,128]{1,0:T(8,128)(2,1)} %pad_maximum_fusion.6.query_ref, s32[16,4,1024]{2,1,0:T(4,128)} %fusion.15.pick_ref), custom_call_target="tpu_custom_call" | custom-call | tf_op jit(solution)/shard_map/score_forward/pallas_call | solution.py:1467
  377.5 52.6 %score_backward.1 = (f32[16384,128]{1,0:T(8,128)}, f32[128,1024]{1,0:T(8,128)}) custom-call(s32[64]{0:T(128)} %sub.153.begin_ref, s32[64]{0:T(128)} %copy-done.22, bf16[16384,128]{1,0:T(8,128)(2,1)} %all-gather.14.cloned.1.call-done.doc_ref, bf16[1024,128]{1,0:T(8,128)(2,1)} %pad_maximum_fusion.6.query_ref, s32[16,4,1024]{2,1,0:T(4,128)} %fusion.15.pick_ref, ...), custom_call_target="tpu_custom_call" | custom-call | tf_op jit(solution)/shard_map/score_backward/pallas_call | solution.py:1485
  430.1 3.9 fusion
  433.9 4.5 collective-permute-done.10
  438.4 3.2 bitcast_add_fusion
  445.2 25.0 %collective-permute-done.11 = bf16[4,1024,128]{2,1,0:T(8,128)(2,1)} collective-permute-done((bf16[4,1024,128]{2,1,0:T(8,128)(2,1)}, bf16[4,1024,128]{2,1,0:T(8,128)(2,1)}, u32[]{:S(2)}, u32[]{:S(2)}) %collective-permute-start.11) | collective-permute-done | bytes 1048608 | tf_op jit(solution)/shard_map/ppermute | solution.py:1551
  476.0 3.3 copy.127
  479.3 3.9 dynamic-slice_bitcast_fusion
  491.6 10.7 %collective-permute-done.13 = bf16[1,1024,128]{2,1,0:T(8,128)(2,1)S(1)} collective-permute-done((bf16[1,1024,128]{2,1,0:T(8,128)(2,1)S(1)}, bf16[1,1024,128]{2,1,0:T(8,128)(2,1)S(1)}, u32[]{:S(2)}, u32[]{:S(2)}) %collective-permute-start.13) | collective-permute-done | bytes 262176 | tf_op jit(solution)/shard_map/ppermute | solution.py:1551
  503.3 12.1 %head_pull.1 = (bf16[1536,128]{1,0:T(8,128)(2,1)}, f32[1536,1024]{1,0:T(8,128)}, bf16[1536,1024]{1,0:T(8,128)(2,1)}, bf16[1024,1536]{1,0:T(8,128)(2,1)}, f32[8,1024]{1,0:T(8,128)}) custom-call(f32[1536,128]{1,0:T(8,128)} %pad_maximum_fusion.4.grad_ref, f32[1536,128]{1,0:T(8,128)} %get-tuple-element.66.unit_ref, ...), custom_call_target="tpu_custom_call" | custom-call | flops 805306368 | bytes 21180416 | tf_op jit(solution)/shard_map/head_pull/pallas_call | solution.py:812
  515.4 13.6 %up_pull.2 = (bf16[1536,2048]{1,0:T(8,128)(2,1)}, f32[8,2048]{1,0:T(8,128)}) custom-call(bf16[1536,1024]{1,0:T(8,128)(2,1)} %get-tuple-element.72.branch_ref, bf16[2048,1024]{1,0:T(8,128)(2,1)} %w_ref.5, f32[1536,2048]{1,0:T(8,128)} %get-tuple-element.73.slope_ref), custom_call_target="tpu_custom_call" | custom-call | flops 6442450944 | bytes 26279936 | tf_op jit(solution)/shard_map/up_pull/pallas_call | solution.py:812
  529.8 13.6 %up_pull.3 = (bf16[1536,2048]{1,0:T(8,128)(2,1)}, f32[8,2048]{1,0:T(8,128)}) custom-call(bf16[1536,1024]{1,0:T(8,128)(2,1)} %get-tuple-element.72.branch_ref, bf16[2048,1024]{1,0:T(8,128)(2,1)} %all-gather.12.cloned.1.call-done.refs_6_.w_ref, f32[1536,2048]{1,0:T(8,128)} %get-tuple-element.75.slope_ref), custom_call_target="tpu_custom_call" | custom-call | flops 6442450944 | bytes 26279936 | tf_op jit(solution)/shard_map/up_pull/pallas_call | solution.py:812
  544.2 29.6 %hidden_pull.1 = (f32[1536,1024]{1,0:T(8,128)}, bf16[1024,1536]{1,0:T(8,128)(2,1)}, f32[8,1024]{1,0:T(8,128)}, bf16[1536,512]{1,0:T(8,128)(2,1)}, bf16[1536,512]{1,0:T(8,128)(2,1)}) custom-call(f32[1536,1024]{1,0:T(8,128)} %get-tuple-element.70.refs_0_, f32[1536,1024]{1,0:T(8,128)} %get-tuple-element.59.refs_0_.refs_1_, ...), custom_call_target="tpu_custom_call" | custom-call | flops 16106127360 | bytes 48306176 | tf_op jit(solution)/shard_map/hidden_pull/pallas_call | solution.py:812
  573.8 49.8 %attention_backward.2 = (bf16[3,1536,512]{2,1,0:T(8,128)(2,1)}, f32[8,512]{1,0:T(8,128)}) custom-call(s32[12]{0:T(128)} %pad_add_fusion.1.span_ref, bf16[3,1536,512]{2,1,0:T(8,128)(2,1)} %project_qkv.2.qkv_ref, bf16[1536,512]{1,0:T(8,128)(2,1)} %get-tuple-element.78.ext_ref, bf16[1536,512]{1,0:T(8,128)(2,1)} %get-tuple-element.57.refs_2_.att_ref, ...), custom_call_target="tpu_custom_call" | custom-call | flops 15000000512 | bytes 17711152 | tf_op jit(solution)/shard_map/attention_backward/pallas_call | solution.py:812
  624.5 50.2 %attention_backward.3 = (bf16[3,1536,512]{2,1,0:T(8,128)(2,1)}, f32[8,512]{1,0:T(8,128)}) custom-call(s32[12]{0:T(128)} %pad_add_fusion.1.span_ref, bf16[3,1536,512]{2,1,0:T(8,128)(2,1)} %project_qkv.3.qkv_ref, bf16[1536,512]{1,0:T(8,128)(2,1)} %get-tuple-element.82.ext_ref, bf16[1536,512]{1,0:T(8,128)(2,1)} %get-tuple-element.58.refs_3_.att_ref, ...), custom_call_target="tpu_custom_call" | custom-call | flops 15000000512 | bytes 17711152 | tf_op jit(solution)/shard_map/attention_backward/pallas_call | solution.py:812
  686.1 3.7 weight_pull.26
  689.8 3.7 weight_pull.24
  693.9 6.3 weight_pull.22
  700.2 6.3 weight_pull.20
  706.5 10.9 %token_pull.3 = bf16[1536,512]{1,0:T(8,128)(2,1)} custom-call(s32[1]{0:T(128)} %bitcast.48.place_ref, f32[1536,1024]{1,0:T(8,128)} %get-tuple-element.77.refs_0_, bf16[3,1536,512]{2,1,0:T(8,128)(2,1)} %get-tuple-element.81.refs_1_.right_ref, bf16[3,1536,512]{2,1,0:T(8,128)(2,1)} %get-tuple-element.85.refs_2_.right_ref, bf16[3,1024,512]{2,1,0:T(8,128)(2,1)} %refs_3_.3, ...), custom_call_target="tpu_custom_call" | custom-call | flops 4831838208 | bytes 23592964 | tf_op jit(solution)/shard_map/token_pull/pallas_call | solution.py:812
  717.4 11.3 %token_pull.2 = f32[1536,512]{1,0:T(8,128)} custom-call(s32[1]{0:T(128)} %bitcast.33.place_ref, f32[1536,1024]{1,0:T(8,128)} %get-tuple-element.77.refs_0_, bf16[3,1536,512]{2,1,0:T(8,128)(2,1)} %get-tuple-element.81.refs_1_.right_ref, bf16[3,1536,512]{2,1,0:T(8,128)(2,1)} %get-tuple-element.85.refs_2_.right_ref, bf16[3,1024,512]{2,1,0:T(8,128)(2,1)} %refs_3_.3, ...), custom_call_target="tpu_custom_call" | custom-call | flops 4831838208 | bytes 25165828 | tf_op jit(solution)/shard_map/token_pull/pallas_call | solution.py:812
  728.7 25.4 %collective-permute-start.22 = (f32[8,417]{1,0:T(8,128)S(1)}, f32[8,417]{1,0:T(8,128)S(1)}, u32[]{:S(2)}, u32[]{:S(2)}) collective-permute-start(f32[8,417]{1,0:T(8,128)S(1)} %slice_bitcast_fusion), channel_id=1, source_target_pairs={{0,1},{1,0},{2,3},{3,2},{4,5},{5,4},{6,7},{7,6},{8,9},{9,8},{10,11... | collective-permute-start | bytes 40040 | tf_op jit(solution)/shard_map/ppermute | solution.py:1548
  754.1 7.4 weight_pull.34
  762.2 7.4 weight_pull.32
  769.8 7.5 weight_pull.30
  779.7 7.6 weight_pull.28
  797.5 3.8 weight_pull.27
  804.4 4.0 weight_pull.25
  808.4 6.6 collective-permute-done.28
  820.5 4.6 collective-permute-done.29
  829.1 6.5 weight_pull.23
  837.9 5.1 collective-permute-done.31
  843.8 7.2 weight_pull.21
  852.3 7.8 weight_pull.31
  862.0 7.7 weight_pull.35
  869.8 3.5 collective-permute-done.17
  877.2 29.8 %collective-permute-done.14 = bf16[1536,512]{1,0:T(8,128)(2,1)} collective-permute-done((bf16[1536,512]{1,0:T(8,128)(2,1)}, bf16[1536,512]{1,0:T(8,128)(2,1)}, u32[]{:S(2)}, u32[]{:S(2)}) %collective-permute-start.14) | collective-permute-done | bytes 1572896 | tf_op jit(solution)/shard_map/ppermute | solution.py:1548
  912.4 8.1 weight_pull.29
  920.5 8.2 weight_pull.33
  930.4 21.5 %collective-permute-done.34 = bf16[1,512,2048]{2,1,0:T(8,128)(2,1)} collective-permute-done((bf16[1,512,2048]{2,1,0:T(8,128)(2,1)}, bf16[1,512,2048]{2,1,0:T(8,128)(2,1)}, u32[]{:S(2)}, u32[]{:S(2)}) %collective-permute-start.34) | collective-permute-done | bytes 2097184 | tf_op jit(solution)/shard_map/ppermute | solution.py:1548
  955.3 36.4 %collective-permute-done.40 = bf16[1,512,2048]{2,1,0:T(8,128)(2,1)} collective-permute-done((bf16[1,512,2048]{2,1,0:T(8,128)(2,1)}, bf16[1,512,2048]{2,1,0:T(8,128)(2,1)}, u32[]{:S(2)}, u32[]{:S(2)}) %collective-permute-start.40) | collective-permute-done | bytes 2097184 | tf_op jit(solution)/shard_map/ppermute | solution.py:1548
  997.0 3.1 pad_maximum_fusion
  1000.1 4.0 collective-permute-done.20
  1005.3 9.3 collective-permute-done.41
  1019.2 12.1 %collective-permute-done.42 = bf16[2,1,64,2048]{3,2,0,1:T(8,128)(2,1)S(1)} collective-permute-done((bf16[2,1,64,2048]{3,2,0,1:T(8,128)(2,1)S(1)}, bf16[2,1,64,2048]{3,2,0,1:T(8,128)(2,1)S(1)}, u32[]{:S(2)}, u32[]{:S(2)}) %collective-permute-start.42) | collective-permute-done | bytes 524320 | tf_op jit(solution)/shard_map/ppermute | solution.py:1551
  1032.5 11.4 %collective-permute-done.43 = bf16[1,1,64,2048]{3,2,0,1:T(8,128)(2,1)S(1)} collective-permute-done((bf16[1,1,64,2048]{3,2,0,1:T(8,128)(2,1)S(1)}, bf16[1,1,64,2048]{3,2,0,1:T(8,128)(2,1)S(1)}, u32[]{:S(2)}, u32[]{:S(2)}) %collective-permute-start.43) | collective-permute-done | bytes 262176 | tf_op jit(solution)/shard_map/ppermute | solution.py:1551
  (332 shorter events, 160.2 us)
Async XLA Ops:
  7.2 129.0 %all-gather.6.cloned.1.call-start = ((), (), s32[]{:S(2)}) async-start(), calls=%async_computation | async-start | bytes 3342336 | tf_op jit(solution)/shard_map/all_gather | solution.py:1579
  8.2 7.9 collective-permute-start.2
  16.8 165.0 %all-gather.8.cloned.1.call-start = ((), (), s32[]{:S(2)}) async-start(), calls=%async_computation.1 | async-start | bytes 1114112 | tf_op jit(solution)/shard_map/all_gather | solution.py:1579
  17.7 4.3 collective-permute-start.3
  22.6 194.0 %all-gather.10.cloned.1.call-start = ((), (), s32[]{:S(2)}) async-start(), calls=%async_computation.2 | async-start | bytes 4456448 | tf_op jit(solution)/shard_map/all_gather | solution.py:1579
  23.7 6.4 collective-permute-start.5
  30.8 208.5 %all-gather.12.cloned.1.call-start = ((), (), s32[]{:S(2)}) async-start(), calls=%async_computation.3 | async-start | bytes 4456448 | tf_op jit(solution)/shard_map/all_gather | solution.py:1579
  42.0 19.0 %collective-permute-start.1 = (f32[6656]{0:T(1024)}, f32[6656]{0:T(1024)}, u32[]{:S(2)}, u32[]{:S(2)}) collective-permute-start(f32[6656]{0:T(1024)} %constant_dynamic-update-slice_fusion), channel_id=1, source_target_pairs={{0,1},{1,0},{2,3},{3,2},{4,5},{5,4},{6,7},{7,6},{8,9},{9,8},{10,11... | collective-permute-start | bytes 79880 | tf_op jit(solution)/shard_map/ppermute | solution.py:1548
  43.7 21.4 %collective-permute-start.4 = (bf16[512,128]{1,0:T(8,128)(2,1)}, bf16[512,128]{1,0:T(8,128)(2,1)}, u32[]{:S(2)}, u32[]{:S(2)}) collective-permute-start(bf16[512,128]{1,0:T(8,128)(2,1)} %param.34), channel_id=1, source_target_pairs={{0,1},{1,0},{2,3},{3,2},{4,5},{5,4},{6,7},{7,6},{8,9},{9,8},{10,11... | collective-permute-start | bytes 393224 | tf_op jit(solution)/shard_map/ppermute | solution.py:1548
  45.0 15.8 %collective-permute-start.6 = (bf16[128,1024]{1,0:T(8,128)(2,1)S(1)}, bf16[128,1024]{1,0:T(8,128)(2,1)}, u32[]{:S(2)}, u32[]{:S(2)}) collective-permute-start(bf16[128,1024]{1,0:T(8,128)(2,1)S(1)} %dynamic-slice_bitcast_fusion.3), channel_id=1, source_target_pairs={{0,1},{1,0},{2,3},{3,2},{4,5},{5,4},{6,7},{7,6},{8,9},{9,8},{10,11... | collective-permute-start | bytes 786440 | tf_op jit(solution)/shard_map/ppermute | solution.py:1548
  51.2 34.4 %collective-permute-start = (bf16[1536,512]{1,0:T(8,128)(2,1)}, bf16[1536,512]{1,0:T(8,128)(2,1)}, u32[]{:S(2)}, u32[]{:S(2)}) collective-permute-start(bf16[1536,512]{1,0:T(8,128)(2,1)} %fusion.2), channel_id=1, source_target_pairs={{0,1},{1,0},{2,3},{3,2},{4,5},{5,4},{6,7},{7,6},{8,9},{9,8},{10,11... | collective-permute-start | bytes 4718600 | tf_op jit(solution)/shard_map/ppermute | solution.py:1548
  55.0 10.1 copy-start.18
  60.9 272.8 %all-gather.14.cloned.1.call-start = ((), (), s32[]{:S(2)}) async-start(), calls=%async_computation.4 | async-start | bytes 4456448 | tf_op jit(solution)/shard_map/all_gather | solution.py:1652
  264.7 31.8 %copy-start.24 = (s32[32]{0:T(128)S(1)}, s32[32]{0:T(128)}, u32[]{:S(2)}) copy-start(s32[32]{0:T(128)} %param.21) | copy-start | bytes 388
  267.6 66.1 %copy-start.22 = (s32[64]{0:T(128)}, s32[64]{0:T(128)S(1)}, u32[]{:S(2)}) copy-start(s32[64]{0:T(128)S(1)} %squeeze.220.size_ref) | copy-start | bytes 772
  279.7 19.8 %collective-permute-start.7 = (bf16[512,128]{1,0:T(8,128)(2,1)S(1)}, bf16[512,128]{1,0:T(8,128)(2,1)S(1)}, u32[]{:S(2)}, u32[]{:S(2)}) collective-permute-start(bf16[512,128]{1,0:T(8,128)(2,1)S(1)} %slice.237), channel_id=1, source_target_pairs={{0,1},{1,0},{2,3},{3,2},{4,5},{5,4},{6,7},{7,6},{8,9},{9,8},{10,11... | collective-permute-start | bytes 393224 | tf_op jit(solution)/shard_map/ppermute | solution.py:1548
  369.5 3.6 collective-permute-start.8
  433.9 4.5 collective-permute-start.10
  444.7 25.5 %collective-permute-start.11 = (bf16[4,1024,128]{2,1,0:T(8,128)(2,1)}, bf16[4,1024,128]{2,1,0:T(8,128)(2,1)}, u32[]{:S(2)}, u32[]{:S(2)}) collective-permute-start(bf16[4,1024,128]{2,1,0:T(8,128)(2,1)} %fusion.5), channel_id=1, source_target_pairs={{0,4},{2,6},{4,0},{6,2},{8,12},{10,14},{12,8},{14,10},{16,20},{18,... | collective-permute-start | bytes 3145736 | tf_op jit(solution)/shard_map/ppermute | solution.py:1551
  474.5 13.5 %collective-permute-start.12 = (bf16[2,1024,128]{2,1,0:T(8,128)(2,1)}, bf16[2,1024,128]{2,1,0:T(8,128)(2,1)}, u32[]{:S(2)}, u32[]{:S(2)}) collective-permute-start(bf16[2,1024,128]{2,1,0:T(8,128)(2,1)} %fusion.13), channel_id=1, source_target_pairs={{0,8},{2,10},{4,12},{6,14},{8,0},{10,2},{12,4},{14,6},{16,24},{18,... | collective-permute-start | bytes 1572872 | tf_op jit(solution)/shard_map/ppermute | solution.py:1551
  479.3 8.6 copy-start.6
  484.1 7.5 collective-permute-start.9
  489.1 13.2 %collective-permute-start.13 = (bf16[1,1024,128]{2,1,0:T(8,128)(2,1)S(1)}, bf16[1,1024,128]{2,1,0:T(8,128)(2,1)S(1)}, u32[]{:S(2)}, u32[]{:S(2)}) collective-permute-start(bf16[1,1024,128]{2,1,0:T(8,128)(2,1)S(1)} %dynamic-slice_convert_fusion.7), channel_id=1, source_target_pairs={{0,16},{2,18},{4,20},{6,22},{8,24},{10,26},{12,28},{14,30},{16,0},... | collective-permute-start | bytes 786440 | tf_op jit(solution)/shard_map/ppermute | solution.py:1551
  624.5 55.1 %copy-start.15 = (bf16[1536,128]{1,0:T(8,128)(2,1)S(1)}, bf16[1536,128]{1,0:T(8,128)(2,1)}, u32[]{:S(2)}) copy-start(bf16[1536,128]{1,0:T(8,128)(2,1)} %get-tuple-element.95) | copy-start | bytes 1179652
  679.5 49.2 %collective-permute-start.21 = (f32[8,2,417]{2,0,1:T(8,128)S(1)}, f32[8,2,417]{2,0,1:T(8,128)S(1)}, u32[]{:S(2)}, u32[]{:S(2)}) collective-permute-start(f32[8,2,417]{2,0,1:T(8,128)S(1)} %bitcast.316), channel_id=1, source_target_pairs={{0,2},{2,0},{4,6},{6,4},{8,10},{10,8},{12,14},{14,12},{16,18},{18,... | collective-permute-start | bytes 80072 | tf_op jit(solution)/shard_map/ppermute | solution.py:1551
  685.6 106.0 %collective-permute-start.44 = (bf16[1,64,512]{2,1,0:T(8,128)(2,1)}, bf16[1,64,512]{2,1,0:T(8,128)(2,1)S(1)}, u32[]{:S(2)}, u32[]{:S(2)}) collective-permute-start(bf16[1,64,512]{2,1,0:T(8,128)(2,1)} %weight_pull.36), channel_id=1, source_target_pairs={{0,2},{2,0},{4,6},{6,4},{8,10},{10,8},{12,14},{14,12},{16,18},{18,... | collective-permute-start | bytes 196616 | tf_op jit(solution)/shard_map/ppermute | solution.py:1551
  686.1 101.9 %collective-permute-start.45 = (bf16[1,64,512]{2,1,0:T(8,128)(2,1)}, bf16[1,64,512]{2,1,0:T(8,128)(2,1)S(1)}, u32[]{:S(2)}, u32[]{:S(2)}) collective-permute-start(bf16[1,64,512]{2,1,0:T(8,128)(2,1)} %weight_pull.38), channel_id=1, source_target_pairs={{0,2},{2,0},{4,6},{6,4},{8,10},{10,8},{12,14},{14,12},{16,18},{18,... | collective-permute-start | bytes 196616 | tf_op jit(solution)/shard_map/ppermute | solution.py:1551
  693.4 110.2 %collective-permute-start.26 = (bf16[1,512,512]{2,1,0:T(8,128)(2,1)}, bf16[1,512,512]{2,1,0:T(8,128)(2,1)S(1)}, u32[]{:S(2)}, u32[]{:S(2)}) collective-permute-start(bf16[1,512,512]{2,1,0:T(8,128)(2,1)} %weight_pull.24), channel_id=1, source_target_pairs={{0,2},{2,0},{4,6},{6,4},{8,10},{10,8},{12,14},{14,12},{16,18},{18,... | collective-permute-start | bytes 1572872 | tf_op jit(solution)/shard_map/ppermute | solution.py:1551
  693.9 102.9 %collective-permute-start.27 = (bf16[1,512,512]{2,1,0:T(8,128)(2,1)}, bf16[1,512,512]{2,1,0:T(8,128)(2,1)S(1)}, u32[]{:S(2)}, u32[]{:S(2)}) collective-permute-start(bf16[1,512,512]{2,1,0:T(8,128)(2,1)} %weight_pull.26), channel_id=1, source_target_pairs={{0,2},{2,0},{4,6},{6,4},{8,10},{10,8},{12,14},{14,12},{16,18},{18,... | collective-permute-start | bytes 1572872 | tf_op jit(solution)/shard_map/ppermute | solution.py:1551
  728.7 32.8 %collective-permute-start.22 = (f32[8,417]{1,0:T(8,128)S(1)}, f32[8,417]{1,0:T(8,128)S(1)}, u32[]{:S(2)}, u32[]{:S(2)}) collective-permute-start(f32[8,417]{1,0:T(8,128)S(1)} %slice_bitcast_fusion), channel_id=1, source_target_pairs={{0,1},{1,0},{2,3},{3,2},{4,5},{5,4},{6,7},{7,6},{8,9},{9,8},{10,11... | collective-permute-start | bytes 40040 | tf_op jit(solution)/shard_map/ppermute | solution.py:1548
  761.6 8.1 collective-permute-start.23
  769.7 7.6 collective-permute-start.24
  777.3 10.0 collective-permute-start.25
  787.3 56.5 %collective-permute-start.15 = (bf16[3,512,512]{2,1,0:T(8,128)(2,1)S(1)}, bf16[3,512,512]{2,1,0:T(8,128)(2,1)}, u32[]{:S(2)}, u32[]{:S(2)}) collective-permute-start(bf16[3,512,512]{2,1,0:T(8,128)(2,1)S(1)} %copy-done.11), channel_id=1, source_target_pairs={{0,2},{2,0},{4,6},{6,4},{8,10},{10,8},{12,14},{14,12},{16,18},{18,... | collective-permute-start | bytes 4718600 | tf_op jit(solution)/shard_map/ppermute | solution.py:1551
  791.0 4.7 collective-permute-start.46
  791.6 35.4 %collective-permute-start.16 = (bf16[3,512,512]{2,1,0:T(8,128)(2,1)}, bf16[3,512,512]{2,1,0:T(8,128)(2,1)}, u32[]{:S(2)}, u32[]{:S(2)}) collective-permute-start(bf16[3,512,512]{2,1,0:T(8,128)(2,1)} %weight_pull.22), channel_id=1, source_target_pairs={{0,2},{2,0},{4,6},{6,4},{8,10},{10,8},{12,14},{14,12},{16,18},{18,... | collective-permute-start | bytes 4718600 | tf_op jit(solution)/shard_map/ppermute | solution.py:1551
  796.6 6.9 collective-permute-start.47
  801.3 13.7 %collective-permute-start.28 = (bf16[1,512,512]{2,1,0:T(8,128)(2,1)}, bf16[1,512,512]{2,1,0:T(8,128)(2,1)S(1)}, u32[]{:S(2)}, u32[]{:S(2)}) collective-permute-start(bf16[1,512,512]{2,1,0:T(8,128)(2,1)} %weight_pull.27), channel_id=1, source_target_pairs={{0,1},{1,0},{2,3},{3,2},{4,5},{5,4},{6,7},{7,6},{8,9},{9,8},{10,11... | collective-permute-start | bytes 1572872 | tf_op jit(solution)/shard_map/ppermute | solution.py:1548
  803.6 47.4 %collective-permute-start.33 = (bf16[1,512,2048]{2,1,0:T(8,128)(2,1)}, bf16[1,512,2048]{2,1,0:T(8,128)(2,1)S(1)}, u32[]{:S(2)}, u32[]{:S(2)}) collective-permute-start(bf16[1,512,2048]{2,1,0:T(8,128)(2,1)} %weight_pull.30), channel_id=1, source_target_pairs={{0,2},{2,0},{4,6},{6,4},{8,10},{10,8},{12,14},{14,12},{16,18},{18,... | collective-permute-start | bytes 6291464 | tf_op jit(solution)/shard_map/ppermute | solution.py:1551
  803.6 56.4 %collective-permute-start.39 = (bf16[1,512,2048]{2,1,0:T(8,128)(2,1)}, bf16[1,512,2048]{2,1,0:T(8,128)(2,1)S(1)}, u32[]{:S(2)}, u32[]{:S(2)}) collective-permute-start(bf16[1,512,2048]{2,1,0:T(8,128)(2,1)} %weight_pull.34), channel_id=1, source_target_pairs={{0,2},{2,0},{4,6},{6,4},{8,10},{10,8},{12,14},{14,12},{16,18},{18,... | collective-permute-start | bytes 6291464 | tf_op jit(solution)/shard_map/ppermute | solution.py:1551
  815.1 3.7 collective-permute-start.48
  818.8 6.4 collective-permute-start.29
  825.2 12.0 %collective-permute-start.49 = (bf16[1,1,8,512]{3,2,0,1:T(8,128)(2,1)S(1)}, bf16[1,1,8,512]{3,2,0,1:T(8,128)(2,1)S(1)}, u32[]{:S(2)}, u32[]{:S(2)}) collective-permute-start(bf16[1,1,8,512]{3,2,0,1:T(8,128)(2,1)S(1)} %fusion.24), channel_id=1, source_target_pairs={{0,16},{2,18},{4,20},{6,22},{8,24},{10,26},{12,28},{14,30},{16,0},... | collective-permute-start | bytes 24584 | tf_op jit(solution)/shard_map/ppermute | solution.py:1551
  827.0 8.6 collective-permute-start.30
  835.6 37.6 %collective-permute-start.17 = (bf16[3,512,512]{2,1,0:T(8,128)(2,1)}, bf16[3,512,512]{2,1,0:T(8,128)(2,1)}, u32[]{:S(2)}, u32[]{:S(2)}) collective-permute-start(bf16[3,512,512]{2,1,0:T(8,128)(2,1)} %weight_pull.23), channel_id=1, source_target_pairs={{0,1},{1,0},{2,3},{3,2},{4,5},{5,4},{6,7},{7,6},{8,9},{9,8},{10,11... | collective-permute-start | bytes 4718600 | tf_op jit(solution)/shard_map/ppermute | solution.py:1548
  837.2 5.8 collective-permute-start.31
  843.0 64.0 %collective-permute-start.14 = (bf16[1536,512]{1,0:T(8,128)(2,1)}, bf16[1536,512]{1,0:T(8,128)(2,1)}, u32[]{:S(2)}, u32[]{:S(2)}) collective-permute-start(bf16[1536,512]{1,0:T(8,128)(2,1)} %token_pull.3), channel_id=1, source_target_pairs={{0,1},{1,0},{2,3},{3,2},{4,5},{5,4},{6,7},{7,6},{8,9},{9,8},{10,11... | collective-permute-start | bytes 4718600 | tf_op jit(solution)/shard_map/ppermute | solution.py:1548
  843.8 68.6 %collective-permute-start.32 = (bf16[1,512,2048]{2,1,0:T(8,128)(2,1)}, bf16[1,512,2048]{2,1,0:T(8,128)(2,1)}, u32[]{:S(2)}, u32[]{:S(2)}) collective-permute-start(bf16[1,512,2048]{2,1,0:T(8,128)(2,1)} %weight_pull.28), channel_id=1, source_target_pairs={{0,2},{2,0},{4,6},{6,4},{8,10},{10,8},{12,14},{14,12},{16,18},{18,... | collective-permute-start | bytes 6291464 | tf_op jit(solution)/shard_map/ppermute | solution.py:1551
  851.0 69.5 %collective-permute-start.38 = (bf16[1,512,2048]{2,1,0:T(8,128)(2,1)}, bf16[1,512,2048]{2,1,0:T(8,128)(2,1)}, u32[]{:S(2)}, u32[]{:S(2)}) collective-permute-start(bf16[1,512,2048]{2,1,0:T(8,128)(2,1)} %weight_pull.32), channel_id=1, source_target_pairs={{0,2},{2,0},{4,6},{6,4},{8,10},{10,8},{12,14},{14,12},{16,18},{18,... | collective-permute-start | bytes 6291464 | tf_op jit(solution)/shard_map/ppermute | solution.py:1551
  860.1 14.7 %copy-start.3 = (f32[3,512,512]{2,1,0:T(8,128)S(1)}, f32[3,512,512]{2,1,0:T(8,128)}, u32[]{:S(2)}) copy-start(f32[3,512,512]{2,1,0:T(8,128)} %weight_pull.21) | copy-start | bytes 9437188
  860.1 91.8 %collective-permute-start.34 = (bf16[1,512,2048]{2,1,0:T(8,128)(2,1)}, bf16[1,512,2048]{2,1,0:T(8,128)(2,1)}, u32[]{:S(2)}, u32[]{:S(2)}) collective-permute-start(bf16[1,512,2048]{2,1,0:T(8,128)(2,1)} %weight_pull.31), channel_id=1, source_target_pairs={{0,1},{1,0},{2,3},{3,2},{4,5},{5,4},{6,7},{7,6},{8,9},{9,8},{10,11... | collective-permute-start | bytes 6291464 | tf_op jit(solution)/shard_map/ppermute | solution.py:1548
  873.3 118.5 %collective-permute-start.40 = (bf16[1,512,2048]{2,1,0:T(8,128)(2,1)}, bf16[1,512,2048]{2,1,0:T(8,128)(2,1)}, u32[]{:S(2)}, u32[]{:S(2)}) collective-permute-start(bf16[1,512,2048]{2,1,0:T(8,128)(2,1)} %weight_pull.35), channel_id=1, source_target_pairs={{0,1},{1,0},{2,3},{3,2},{4,5},{5,4},{6,7},{7,6},{8,9},{9,8},{10,11... | collective-permute-start | bytes 6291464 | tf_op jit(solution)/shard_map/ppermute | solution.py:1548
  876.7 30.8 %copy-start.4 = (f32[1536,512]{1,0:T(8,128)S(1)}, f32[1536,512]{1,0:T(8,128)}, u32[]{:S(2)}) copy-start(f32[1536,512]{1,0:T(8,128)} %token_pull.2) | copy-start | bytes 9437188
  907.0 21.7 %collective-permute-start.18 = (bf16[4,3,64,512]{3,2,1,0:T(8,128)(2,1)S(1)}, bf16[4,3,64,512]{3,2,1,0:T(8,128)(2,1)}, u32[]{:S(2)}, u32[]{:S(2)}) collective-permute-start(bf16[4,3,64,512]{3,2,1,0:T(8,128)(2,1)S(1)} %fusion.8), channel_id=1, source_target_pairs={{0,4},{2,6},{4,0},{6,2},{8,12},{10,14},{12,8},{14,10},{16,20},{18,... | collective-permute-start | bytes 2359304 | tf_op jit(solution)/shard_map/ppermute | solution.py:1551
  928.7 23.3 %copy-start.1 = (f32[1,512,2048]{2,1,0:T(8,128)S(1)}, f32[1,512,2048]{2,1,0:T(8,128)}, u32[]{:S(2)}) copy-start(f32[1,512,2048]{2,1,0:T(8,128)} %weight_pull.29) | copy-start | bytes 12582916
  930.3 64.8 %collective-permute-start.19 = (bf16[2,3,64,512]{3,2,1,0:T(8,128)(2,1)S(1)}, bf16[2,3,64,512]{3,2,1,0:T(8,128)(2,1)S(1)}, u32[]{:S(2)}, u32[]{:S(2)}) collective-permute-start(bf16[2,3,64,512]{3,2,1,0:T(8,128)(2,1)S(1)} %fusion.14), channel_id=1, source_target_pairs={{0,8},{2,10},{4,12},{6,14},{8,0},{10,2},{12,4},{14,6},{16,24},{18,... | collective-permute-start | bytes 1179656 | tf_op jit(solution)/shard_map/ppermute | solution.py:1551
  951.9 39.9 %copy-start = (f32[1,512,2048]{2,1,0:T(8,128)S(1)}, f32[1,512,2048]{2,1,0:T(8,128)}, u32[]{:S(2)}) copy-start(f32[1,512,2048]{2,1,0:T(8,128)} %weight_pull.33) | copy-start | bytes 12582916
  954.7 50.2 %collective-permute-start.35 = (bf16[4,1,64,2048]{3,2,0,1:T(8,128)(2,1)S(1)}, bf16[4,1,64,2048]{3,2,0,1:T(8,128)(2,1)S(1)}, u32[]{:S(2)}, u32[]{:S(2)}) collective-permute-start(bf16[4,1,64,2048]{3,2,0,1:T(8,128)(2,1)S(1)} %fusion.6), channel_id=1, source_target_pairs={{0,4},{2,6},{4,0},{6,2},{8,12},{10,14},{12,8},{14,10},{16,20},{18,... | collective-permute-start | bytes 3145736 | tf_op jit(solution)/shard_map/ppermute | solution.py:1551
  994.4 20.2 %collective-permute-start.41 = (bf16[4,1,64,2048]{3,2,0,1:T(8,128)(2,1)S(1)}, bf16[4,1,64,2048]{3,2,0,1:T(8,128)(2,1)S(1)}, u32[]{:S(2)}, u32[]{:S(2)}) collective-permute-start(bf16[4,1,64,2048]{3,2,0,1:T(8,128)(2,1)S(1)} %fusion.7), channel_id=1, source_target_pairs={{0,4},{2,6},{4,0},{6,2},{8,12},{10,14},{12,8},{14,10},{16,20},{18,... | collective-permute-start | bytes 3145736 | tf_op jit(solution)/shard_map/ppermute | solution.py:1551
  995.2 8.8 collective-permute-start.20
  1005.2 12.3 %collective-permute-start.36 = (bf16[2,1,64,2048]{3,2,0,1:T(8,128)(2,1)S(1)}, bf16[2,1,64,2048]{3,2,0,1:T(8,128)(2,1)S(1)}, u32[]{:S(2)}, u32[]{:S(2)}) collective-permute-start(bf16[2,1,64,2048]{3,2,0,1:T(8,128)(2,1)S(1)} %fusion.11), channel_id=1, source_target_pairs={{0,8},{2,10},{4,12},{6,14},{8,0},{10,2},{12,4},{14,6},{16,24},{18,... | collective-permute-start | bytes 1572872 | tf_op jit(solution)/shard_map/ppermute | solution.py:1551
  1014.9 16.4 %collective-permute-start.42 = (bf16[2,1,64,2048]{3,2,0,1:T(8,128)(2,1)S(1)}, bf16[2,1,64,2048]{3,2,0,1:T(8,128)(2,1)S(1)}, u32[]{:S(2)}, u32[]{:S(2)}) collective-permute-start(bf16[2,1,64,2048]{3,2,0,1:T(8,128)(2,1)S(1)} %fusion.12), channel_id=1, source_target_pairs={{0,8},{2,10},{4,12},{6,14},{8,0},{10,2},{12,4},{14,6},{16,24},{18,... | collective-permute-start | bytes 1572872 | tf_op jit(solution)/shard_map/ppermute | solution.py:1551
  1017.7 13.9 %collective-permute-start.37 = (bf16[1,1,64,2048]{3,2,0,1:T(8,128)(2,1)S(1)}, bf16[1,1,64,2048]{3,2,0,1:T(8,128)(2,1)S(1)}, u32[]{:S(2)}, u32[]{:S(2)}) collective-permute-start(bf16[1,1,64,2048]{3,2,0,1:T(8,128)(2,1)S(1)} %dynamic-slice_convert_fusion.6), channel_id=1, source_target_pairs={{0,16},{2,18},{4,20},{6,22},{8,24},{10,26},{12,28},{14,30},{16,0},... | collective-permute-start | bytes 786440 | tf_op jit(solution)/shard_map/ppermute | solution.py:1551
  1031.5 12.3 %collective-permute-start.43 = (bf16[1,1,64,2048]{3,2,0,1:T(8,128)(2,1)S(1)}, bf16[1,1,64,2048]{3,2,0,1:T(8,128)(2,1)S(1)}, u32[]{:S(2)}, u32[]{:S(2)}) collective-permute-start(bf16[1,1,64,2048]{3,2,0,1:T(8,128)(2,1)S(1)} %dynamic-slice_convert_fusion.5), channel_id=1, source_target_pairs={{0,16},{2,18},{4,20},{6,22},{8,24},{10,26},{12,28},{14,30},{16,0},... | collective-permute-start | bytes 786440 | tf_op jit(solution)/shard_map/ppermute | solution.py:1551
  (16 other events, 30.4 us)
Sparse Core Ops, SparseCore 0:
  16.9 46.8 all-gather.5
  66.6 36.7 all-gather.7
  106.1 49.7 all-gather.9
  157.9 49.2 all-gather.11
  266.6 67.1 all-gather.13

commit v3 on v1

v3 whole, which is shorter than its diff:
```python
import functools
import math

import jax
import jax.numpy as jnp
from jax import lax
from jax.experimental import pallas as pl
from jax.experimental.pallas import tpu as pltpu
from jax.sharding import PartitionSpec as P

DH = 64
QLEN = 32
ROW_LEN = 1024
F32 = jnp.float32
BF16 = jnp.bfloat16
VMEM_LIMIT = 56 * 1024 * 1024
NT = (((1,), (1,)), ((), ()))
NN = (((1,), (0,)), ((), ()))
TN = (((0,), (0,)), ((), ()))


def mm(left, right, dims=NN):
    return lax.dot_general(left, right, dims, preferred_element_type=F32)


def row_step(rows):
    return 512 if rows % 512 == 0 else 128


def parts_of(step):
    size = min(step, 256)
    return [slice(first, first + size) for first in range(0, step, size)]


def held(shape):
    return pl.BlockSpec(shape, lambda *_: (0,) * len(shape), pipeline_mode=pl.Buffered(1))


def shaped(dtype, *shape):
    return jax.ShapeDtypeStruct(shape, dtype)


class Order:
    last = ()


def call(
    body, name, grid, in_specs, out_specs, out_shape, operands, flops, scratch=(), prefetch=0, after=()
):
    count = len(operands)
    after = tuple(after) + Order.last

    def wrapped(*refs):
        body(*refs[:count], *refs[count + len(after) :])

    size = sum(math.prod(o.shape) * o.dtype.itemsize for o in list(operands) + list(out_shape))
    if flops == 0:
        size = 1024
    outs = pl.pallas_call(
        wrapped,
        grid_spec=pltpu.PrefetchScalarGridSpec(
            num_scalar_prefetch=prefetch,
            grid=grid,
            in_specs=list(in_specs) + [pl.BlockSpec(memory_space=pl.ANY)] * len(after),
            out_specs=out_specs,
            scratch_shapes=list(scratch),
        ),
        out_shape=out_shape,
        compiler_params=pltpu.CompilerParams(vmem_limit_bytes=VMEM_LIMIT),
        cost_estimate=pl.CostEstimate(flops=flops, bytes_accessed=size, transcendentals=0),
        name=name,
    )(*operands, *after)
    Order.last = (min(outs, key=lambda out: out.size * out.dtype.itemsize),)
    return outs


def row_spec(step, width):
    return pl.BlockSpec((step, width), lambda i, *_: (i, 0))


def column_spec(width, step):
    return pl.BlockSpec((width, step), lambda i, *_: (0, i))


def swap_halves(block):
    lane = lax.broadcasted_iota(jnp.int32, block.shape, 1)
    return jnp.where((lane & 32) == 0, pltpu.roll(block, 96, 1), pltpu.roll(block, 32, 1))


def qkv_kernel(x_ref, w_ref, b_ref, cos_ref, sin_ref, out_ref):
    which = pl.program_id(0)
    bias = b_ref[pl.ds(which, 1), :]

    @pl.when(which < 2)
    def _():
        for at in parts_of(x_ref.shape[0]):
            mixed = mm(x_ref[at, :], w_ref[0]) + bias
            for first in range(0, mixed.shape[1], 128):
                block = mixed[:, first : first + 128]
                turned = block * cos_ref[at, :] + swap_halves(block) * sin_ref[at, :]
                out_ref[0, at, first : first + 128] = turned.astype(BF16)

    @pl.when(which == 2)
    def _():
        for at in parts_of(x_ref.shape[0]):
            out_ref[0, at, :] = (mm(x_ref[at, :], w_ref[0]) + bias).astype(BF16)


def project_qkv(x, weight, bias, cosine, sine, after=()):
    n, D = x.shape
    width = weight.shape[2]
    step = row_step(n)
    return call(
        qkv_kernel, "project_qkv", (3, n // step),
        [
            pl.BlockSpec((step, D), lambda j, i: (i, 0)),
            pl.BlockSpec((1, D, width), lambda j, i: (j, 0, 0)),
            held(bias.shape),
            pl.BlockSpec((step, 128), lambda j, i: (i, 0)),
            pl.BlockSpec((step, 128), lambda j, i: (i, 0)),
        ],
        [pl.BlockSpec((1, step, width), lambda j, i: (j, i, 0))],
        [shaped(BF16, 3, n, width)],
        (x, weight, bias, cosine, sine), 6 * n * D * width, after=after,
    )[0]


def normed_rows(residual):
    mean = jnp.mean(residual, axis=1, keepdims=True)
    centred = residual - mean
    inverse = lax.rsqrt(jnp.mean(centred * centred, axis=1, keepdims=True) + 1e-05)
    return centred * inverse, inverse


def norm_pull(grad_rows, normed, inverse, gain):
    spread = grad_rows * gain
    return inverse * (
        spread
        - jnp.mean(spread, axis=1, keepdims=True)
        - normed * jnp.mean(spread * normed, axis=1, keepdims=True)
    )


def column_sums(*arrays):
    rows = [jnp.sum(array, axis=0, keepdims=True) for array in arrays]
    rows.append(jnp.zeros((8 - len(rows), rows[0].shape[1]), F32))
    return jnp.concatenate(rows, axis=0)


def add_over_steps(ref, value):
    first = pl.program_id(0) == 0

    @pl.when(first)
    def _():
        ref[...] = value

    @pl.when(jnp.logical_not(first))
    def _():
        ref[...] += value


def out_norm_kernel(slots, *refs):
    x_ref, vec_ref = refs[:2]
    att_refs, w_refs = refs[2 : 2 + slots], refs[2 + slots : 2 + 2 * slots]
    normed_ref, inverse_ref, low_ref, turned_ref = refs[2 + 2 * slots :]
    for at in parts_of(x_ref.shape[0]):
        residual = x_ref[at, :].astype(F32) + vec_ref[0:1, :]
        for att_ref, w_ref in zip(att_refs, w_refs):
            residual = residual + mm(att_ref[at, :], w_ref[...])
        normed, inverse = normed_rows(residual)
        hidden = normed * vec_ref[1:2, :] + vec_ref[2:3, :]
        normed_ref[at, :] = normed
        inverse_ref[at, :] = inverse
        low_ref[at, :] = hidden.astype(BF16)
        turned_ref[:, at] = hidden.T.astype(BF16)


def out_and_norm(x, vectors, attended, weights):
    n, D = x.shape
    step = row_step(n)
    slots = len(attended)
    width = attended[0].shape[1]
    return call(
        functools.partial(out_norm_kernel, slots), "out_and_norm", (n // step,),
        [row_spec(step, D), held(vectors.shape)]
        + [row_spec(step, width)] * slots + [held((width, D))] * slots,
        [row_spec(step, D), row_spec(step, 1), row_spec(step, D), column_spec(D, step)],
        [shaped(F32, n, D), shaped(F32, n, 1), shaped(BF16, n, D), shaped(BF16, D, n)],
        (x, vectors, *attended, *weights), 2 * n * D * D,
    )


GELU_TERMS = (
    0.23532527933595032, 0.09138803439798156, 0.6495603483388861,
    -0.6354014529895687, 0.8866650885491606, -0.22753729931242958,
)


def gelu_parts(values):
    size = jnp.abs(values)
    part = pl.reciprocal(1.0 + (0.39 / math.sqrt(2.0)) * size)
    bell = jnp.exp(-0.5 * (values * values))
    series = 0.5 * GELU_TERMS[-1]
    for term in GELU_TERMS[-2::-1]:
        series = series * part + 0.5 * term
    tail = series * part * bell
    below = jnp.where(values >= 0.0, 1.0 - tail, tail)
    return values * below, below + values * bell * (1.0 / math.sqrt(2.0 * math.pi))


def up_kernel(x_ref, w_ref, b_ref, active_ref, slope_ref):
    width = w_ref.shape[1]
    chunk = min(256, width)
    for first in range(0, width, chunk):
        at = slice(first, first + chunk)
        active, slope = gelu_parts(mm(x_ref[...], w_ref[:, at]) + b_ref[:, at])
        active_ref[:, at] = active.astype(BF16)
        slope_ref[:, at] = slope


def up_and_gelu(x, weight, bias):
    n, D = x.shape
    width = weight.shape[1]
    step = row_step(n)
    return call(
        up_kernel, "up_and_gelu", (n // step,),
        [row_spec(step, D), held(weight.shape), held(bias.shape)],
        [row_spec(step, width)] * 2,
        [shaped(BF16, n, width), shaped(F32, n, width)],
        (x, weight, bias), 5 * n * D * width,
    )


def down_norm_kernel(slots, *refs):
    normed_ref, vec_ref, proj_ref = refs[:3]
    act_refs, w_refs = refs[3 : 3 + slots], refs[3 + slots : 3 + 2 * slots]
    normed_out, inverse_ref, low_ref, unit_ref, unit_low_ref, unit_inverse_ref = refs[3 + 2 * slots :]
    for at in parts_of(normed_ref.shape[0]):
        residual = normed_ref[at, :] * vec_ref[1:2, :] + vec_ref[2:3, :] + vec_ref[3:4, :]
        for act_ref, w_ref in zip(act_refs, w_refs):
            residual = residual + mm(act_ref[at, :], w_ref[...])
        normed, inverse = normed_rows(residual)
        normed_out[at, :] = normed
        inverse_ref[at, :] = inverse
        low = (normed * vec_ref[4:5, :] + vec_ref[5:6, :]).astype(BF16)
        low_ref[at, :] = low
        embedding = mm(low, proj_ref[...])
        unit_inverse = lax.rsqrt(jnp.sum(embedding * embedding, axis=1, keepdims=True) + 1e-06)
        unit = embedding * unit_inverse
        unit_ref[at, :] = unit
        unit_low_ref[at, :] = unit.astype(BF16)
        unit_inverse_ref[at, :] = unit_inverse


def down_and_norm(normed, vectors, proj, active, weights):
    n, D = normed.shape
    step = row_step(n)
    slots = len(active)
    width = active[0].shape[1]
    return call(
        functools.partial(down_norm_kernel, slots), "down_and_norm", (n // step,),
        [row_spec(step, D), held(vectors.shape), held(proj.shape)]
        + [row_spec(step, width)] * slots + [held((width, D))] * slots,
        [
            row_spec(step, D), row_spec(step, 1), row_spec(step, D),
            row_spec(step, 128), row_spec(step, 128), row_spec(step, 1),
        ],
        [
            shaped(F32, n, D), shaped(F32, n, 1), shaped(BF16, n, D),
            shaped(F32, n, 128), shaped(BF16, n, 128), shaped(F32, n, 1),
        ],
        (normed, vectors, proj, *active, *weights), 2 * n * D * width * slots,
    )


def head_pull_kernel(
    grad_ref, unit_ref, unit_inverse_ref, proj_ref, normed_ref, inverse_ref, vec_ref,
    embed_ref, residual_ref, low_ref, turned_ref, sum_ref,
):
    sums = []
    for at in parts_of(grad_ref.shape[0]):
        grad, unit = grad_ref[at, :], unit_ref[at, :]
        embed = grad - unit * jnp.sum(grad * unit, axis=1, keepdims=True)
        embed = (unit_inverse_ref[at, :] * embed).astype(BF16)
        embed_ref[at, :] = embed
        output_grad = mm(embed, proj_ref[...], NT)
        normed = normed_ref[at, :]
        residual = norm_pull(output_grad, normed, inverse_ref[at, :], vec_ref[4:5, :])
        residual_ref[at, :] = residual
        low_ref[at, :] = residual.astype(BF16)
        turned_ref[:, at] = residual.T.astype(BF16)
        sums.append(column_sums(residual, output_grad * normed, output_grad))
    add_over_steps(sum_ref, sum(sums))


def head_pull(unit_grad, unit, unit_inverse, proj, normed, inverse, vectors):
    n, D = normed.shape
    step = row_step(n)
    return call(
        head_pull_kernel, "head_pull", (n // step,),
        [
            row_spec(step, 128), row_spec(step, 128), row_spec(step, 1), held(proj.shape),
            row_spec(step, D), row_spec(step, 1), held(vectors.shape),
        ],
        [
            row_spec(step, 128), row_spec(step, D), row_spec(step, D),
            column_spec(D, step), pl.BlockSpec((8, D), lambda i: (0, 0)),
        ],
        [
            shaped(BF16, n, 128), shaped(F32, n, D), shaped(BF16, n, D),
            shaped(BF16, D, n), shaped(F32, 8, D),
        ],
        (unit_grad, unit, unit_inverse, proj, normed, inverse, vectors), 4 * n * D * 128,
    )


def up_pull_kernel(branch_ref, w_ref, slope_ref, out_ref, sum_ref):
    width = w_ref.shape[0]
    chunk = min(512, width)
    sums = []
    for first in range(0, width, chunk):
        at = slice(first, first + chunk)
        low = (mm(branch_ref[...], w_ref[at, :], NT) * slope_ref[:, at]).astype(BF16)
        out_ref[:, at] = low
        sums.append(column_sums(low.astype(F32)))
    add_over_steps(sum_ref, jnp.concatenate(sums, axis=1))


def up_pull(branch, weight, slope):
    n, D = branch.shape
    width = weight.shape[0]
    step = row_step(n)
    return call(
        up_pull_kernel, "up_pull", (n // step,),
        [row_spec(step, D), held(weight.shape), row_spec(step, width)],
        [row_spec(step, width), pl.BlockSpec((8, width), lambda i: (0, 0))],
        [shaped(BF16, n, width), shaped(F32, 8, width)],
        (branch, weight, slope), 2 * n * D * width,
    )


def hidden_pull_kernel(slots, *refs):
    residual_ref, normed_ref, inverse_ref, vec_ref = refs[:4]
    pre_refs, up_refs, out_refs = (refs[4 + j * slots : 4 + (j + 1) * slots] for j in range(3))
    rest = refs[4 + 3 * slots :]
    grad_ref, turned_ref, sum_ref = rest[:3]
    att_refs = rest[3:]
    sums = []
    for at in parts_of(residual_ref.shape[0]):
        hidden_grad = residual_ref[at, :]
        for pre_ref, up_ref in zip(pre_refs, up_refs):
            hidden_grad = hidden_grad + mm(pre_ref[at, :], up_ref[...], NT)
        normed = normed_ref[at, :]
        residual = norm_pull(hidden_grad, normed, inverse_ref[at, :], vec_ref[1:2, :])
        grad_ref[at, :] = residual
        low = residual.astype(BF16)
        turned_ref[:, at] = residual.T.astype(BF16)
        sums.append(column_sums(residual, hidden_grad * normed, hidden_grad))
        for att_ref, out_ref in zip(att_refs, out_refs):
            att_ref[at, :] = mm(low, out_ref[...], NT).astype(BF16)
    add_over_steps(sum_ref, sum(sums))


def hidden_pull(residual, normed, inverse, vectors, pre_grads, ups, outs):
    n, D = residual.shape
    step = row_step(n)
    slots = len(ups)
    wide, width = ups[0].shape[1], outs[0].shape[0]
    return call(
        functools.partial(hidden_pull_kernel, slots), "hidden_pull", (n // step,),
        [row_spec(step, D), row_spec(step, D), row_spec(step, 1), held(vectors.shape)]
        + [row_spec(step, wide)] * slots + [held((D, wide))] * slots
        + [held((width, D))] * slots,
        [row_spec(step, D), column_spec(D, step), pl.BlockSpec((8, D), lambda i: (0, 0))]
        + [row_spec(step, width)] * slots,
        [shaped(F32, n, D), shaped(BF16, D, n), shaped(F32, 8, D)]
        + [shaped(BF16, n, width)] * slots,
        (residual, normed, inverse, vectors, *pre_grads, *ups, *outs),
        0,
    )


def token_pull_kernel(slots, place_ref, *refs):
    residual_ref = refs[0]
    mixed_refs, w_refs = refs[1 : 1 + slots], refs[1 + slots : 1 + 2 * slots]
    out_ref = refs[-1]
    width = out_ref.shape[1]
    at = pl.ds(pl.multiple_of(place_ref[0] * width, width), width)
    total = residual_ref[...]
    for mixed_ref, w_ref in zip(mixed_refs, w_refs):
        for which in range(3):
            total = total + mm(mixed_ref[which], w_ref[which, at, :], NT)
    out_ref[...] = total.astype(out_ref.dtype)


def token_pull(place, residual, mixed_grads, weights, dtype):
    n, D = residual.shape
    step = row_step(n)
    slots = len(weights)
    width = weights[0].shape[2]
    return call(
        functools.partial(token_pull_kernel, slots), "token_pull", (n // step,),
        [pl.BlockSpec((step, width), lambda i, p: (i, p[0]))]
        + [pl.BlockSpec((3, step, width), lambda i, p: (0, i, 0))] * slots
        + [held((3, D, width))] * slots,
        [row_spec(step, width)],
        [shaped(dtype, n, width)],
        (place.reshape(1), residual, *mixed_grads, *weights), 6 * n * D * width, prefetch=1,
    )[0]


def put_halves(total, inner, side, refs):
    pairs = total.reshape(-1, 2, inner, total.shape[1])
    keep = jnp.where(side == 0, pairs[:, 0], pairs[:, 1]).reshape(-1, total.shape[1])
    send = jnp.where(side == 0, pairs[:, 1], pairs[:, 0]).reshape(-1, total.shape[1])
    refs[0][0] = send.astype(BF16)
    refs[1][0] = keep


def grouped_index(starts, place, count):
    def index(j, i, *_):
        inside = (j >= starts[place]) & (j < starts[place + 1])
        row = jnp.clip(j - starts[place], 0, starts[place + 1] - starts[place] - 1)
        rest = jnp.where(j < starts[place], 0, count - 1)
        return row, 0, jnp.where(inside, i, rest)

    return index


def for_group(starts, body):
    for place in range(len(starts) - 1):

        @pl.when((pl.program_id(0) >= starts[place]) & (pl.program_id(0) < starts[place + 1]))
        def _(place=place):
            body(place)


def weight_pull_kernel(starts, added, inner, place_ref, *refs):
    groups = len(starts) - 1
    lefts, rights, refs = refs[:groups], refs[groups : 2 * groups], refs[2 * groups :]

    def one_group(place):
        left = lefts[place]
        total = mm(left[:, 0].reshape(-1, left.shape[-1]), rights[place][0])
        outs = refs
        if added:
            total = total + refs[0][0].astype(F32)
            outs = refs[1:]
        if inner:
            put_halves(total, inner, place_ref[1], outs)
        else:
            outs[0][0] = total.astype(outs[0].dtype)

    for_group(starts, one_group)


def weight_pull(places, lefts, rights, arrived=None, dtype=BF16, inner=0):
    pairs, _, share, n = lefts[0].shape
    m = rights[0].shape[2]
    rows = pairs * share
    chunk = min(512, m)
    starts = [0]
    for right in rights:
        starts.append(starts[-1] + right.shape[0])

    def spec(size):
        return pl.BlockSpec((1, size, chunk), lambda j, i, p: (j, 0, i))

    half = rows // 2
    outs = [(BF16, half), (F32, half)] if inner else [(dtype, rows)]
    return call(
        functools.partial(weight_pull_kernel, starts, arrived is not None, inner), "weight_pull",
        (starts[-1], m // chunk),
        [pl.BlockSpec((pairs, 1, share, n), lambda j, i, p: (0, p[0], 0, 0)) for _ in lefts]
        + [
            pl.BlockSpec((1, n, chunk), grouped_index(starts, place, m // chunk))
            for place in range(len(rights))
        ] + ([] if arrived is None else [spec(rows)]),
        [spec(size) for _, size in outs],
        [shaped(kind, starts[-1], size, m) for kind, size in outs],
        (places, *lefts, *rights) + (() if arrived is None else (arrived,)),
        2 * starts[-1] * rows * n * m, prefetch=1,
    )


def fold_kernel(starts, inner, place_ref, *refs):
    groups = len(starts) - 1

    def one_group(place):
        total = refs[place][0] + refs[groups + place][0].astype(F32)
        put_halves(total, inner, place_ref[0], refs[2 * groups :])

    for_group(starts, one_group)


def fold(side, owns, arrived, inner):
    _, rows, m = owns[0].shape
    chunk = min(1024, m)
    starts = [0]
    for own in owns:
        starts.append(starts[-1] + own.shape[0])

    def spec(size):
        return pl.BlockSpec((1, size, chunk), lambda j, i, p: (j, 0, i))

    half = rows // 2
    specs = [
        pl.BlockSpec((1, rows, chunk), grouped_index(starts, place, m // chunk))
        for place in range(len(owns))
    ]
    return call(
        functools.partial(fold_kernel, starts, inner), "fold", (starts[-1], m // chunk),
        specs + specs, [spec(half), spec(half)],
        [shaped(BF16, starts[-1], half, m), shaped(F32, starts[-1], half, m)],
        (side.reshape(1), *owns, *arrived), 0, prefetch=1,
    )


SEGMENTS = 8
ATTENTION_LANES = 256


def half_lanes(block, head, other):
    lane = lax.broadcasted_iota(jnp.int32, block.shape, 1)
    return jnp.where((lane >= DH) == (head == 1), block, other)


def scaled(block):
    return (block.astype(F32) * DH**-0.5).astype(BF16)


def three_terms(value):
    high = value.astype(BF16).astype(F32)
    middle = (value - high).astype(BF16).astype(F32)
    return high, middle, value - high - middle


def attention_forward_kernel(
    span_ref, qkv_ref, ext_k_ref, ext_q_ref, out_ref, rest_ref, ext_ref,
    keys_ref, queries_ref, values_ref, logits_ref, *, tile,
):
    n = ext_k_ref.shape[0]
    tiles = n // tile
    pairs = qkv_ref.shape[2] // 128
    heads = range(2 * pairs)

    def lanes(head):
        return slice(head // 2 * 128, head // 2 * 128 + 128)

    def own_rows(head):
        return slice(head % 2 * DH, head % 2 * DH + DH)

    for head in heads:
        keys_ref[head] = half_lanes(qkv_ref[1, :, lanes(head)], head % 2, ext_k_ref[...])
        queries_ref[head] = half_lanes(
            scaled(qkv_ref[0, :, lanes(head)]), head % 2, ext_q_ref[...]
        )
    for pair in range(pairs):
        for step in range(tiles):
            block = qkv_ref[2, step * tile : (step + 1) * tile, lanes(2 * pair)]
            values_ref[pair, step] = block.astype(F32).T.astype(BF16)

    def rows(step):
        return pl.ds(pl.multiple_of(step * tile, tile), tile)

    def by_eight(block):
        return block.reshape(tile // 8, 8, tile)

    @pl.loop(0, tiles)
    def _(step):
        low, high = span_ref[step], span_ref[tiles + step]

        def find_top(block, tops):
            found = []
            for head in heads:
                logits = mm(
                    keys_ref[head, rows(block), :], queries_ref[head, rows(step), :], NT
                )
                logits_ref[head, block] = logits
                found.append(jnp.maximum(tops[head], jnp.max(by_eight(logits), axis=0)))
            return tuple(found)

        start = jnp.full((8, tile), -3e38, F32)
        tops = lax.fori_loop(low, high, find_top, tuple(start for _ in heads))
        tops = [jnp.max(top, axis=0, keepdims=True) for top in tops]

        def add_mass(block, masses):
            after = []
            for head in heads:
                weights = jnp.exp(logits_ref[head, block] - tops[head])
                logits_ref[head, block] = weights
                after.append(masses[head] + jnp.sum(by_eight(weights), axis=0))
            return tuple(after)

        start = jnp.zeros((8, tile), F32)
        masses = lax.fori_loop(low, high, add_mass, tuple(start for _ in heads))
        masses = [jnp.sum(mass, axis=0, keepdims=True) for mass in masses]
        shares = [1.0 / mass for mass in masses]

        def add_values(block, totals):
            after = []
            for head in heads:
                probs = (logits_ref[head, block] * shares[head]).astype(BF16)
                after.append(totals[head] + mm(values_ref[head // 2, block, own_rows(head), :], probs))
            return tuple(after)

        zero = jnp.zeros((DH, tile), F32)
        outs = lax.fori_loop(low, high, add_values, tuple(zero for _ in heads))
        for pair in range(pairs):
            extras = []
            for head in (2 * pair + 1, 2 * pair):
                terms = three_terms(-(tops[head] + jnp.log(masses[head])))
                extras += [
                    jnp.zeros((8, tile), F32), *terms, jnp.zeros((DH - 11, tile), F32)
                ]
            at = lanes(2 * pair)
            out = jnp.concatenate(outs[2 * pair : 2 * pair + 2], axis=0).T
            out_ref[rows(step), at] = out.astype(BF16)
            rest_ref[rows(step), at] = (out - out.astype(BF16).astype(F32)).astype(BF16)
            extra = jnp.concatenate(extras, axis=0).T
            ext_ref[rows(step), at] = (extra + ext_q_ref[rows(step), :].astype(F32)).astype(BF16)


def attention_forward(spans, qkv, ext_k, ext_q, tile):
    _, n, width = qkv.shape
    span = min(width, ATTENTION_LANES)
    wide = pl.BlockSpec((n, span), lambda i, *_: (0, i))
    tiles, pairs = n // tile, span // 128
    return call(
        functools.partial(attention_forward_kernel, tile=tile), "attention_forward",
        (width // span,),
        [pl.BlockSpec((3, n, span), lambda i, *_: (0, 0, i)), held((n, 128)), held((n, 128))],
        [wide, wide, wide],
        [shaped(BF16, n, width)] * 3,
        (spans, qkv, ext_k, ext_q), 0, prefetch=1,
        scratch=[
            pltpu.VMEM((2 * pairs, n, 128), BF16), pltpu.VMEM((2 * pairs, n, 128), BF16),
            pltpu.VMEM((pairs, tiles, 128, tile), BF16),
            pltpu.VMEM((2 * pairs, tiles, tile, tile), F32),
        ],
    )


def attention_backward_kernel(
    span_ref, qkv_ref, ext_ref, att_ref, rest_ref, grad_ref, ext_k_ref, cos_ref, sin_ref,
    out_ref, sum_ref,
    keys_ref, turned_ref, values_ref, queries_ref, plain_ref, grads_ref, plain_grads_ref,
    dq_ref, dk_ref, dv_ref, *, tile,
):
    n = ext_k_ref.shape[0]
    tiles = n // tile
    pairs = qkv_ref.shape[2] // 128
    heads = range(2 * pairs)

    def lanes(head):
        return slice(head // 2 * 128, head // 2 * 128 + 128)

    def own_rows(head):
        return slice(head % 2 * DH, head % 2 * DH + DH)

    def rows(step):
        return pl.ds(pl.multiple_of(step * tile, tile), tile)

    @pl.loop(0, tiles)
    def _(step):
        at = rows(step)
        zeros = jnp.zeros((tile, 128), BF16)
        lane = lax.broadcasted_iota(jnp.int32, (tile, 128), 1)
        ext_k = ext_k_ref[at, :]
        for pair in range(pairs):
            cut = lanes(2 * pair)
            grad = grad_ref[at, cut]
            out = att_ref[at, cut].astype(F32) + rest_ref[at, cut].astype(F32)
            product = grad.astype(F32) * out
            query = scaled(qkv_ref[0, at, cut])
            turned_ref[pair, step] = scaled(qkv_ref[1, at, cut]).astype(F32).T.astype(BF16)
            for half in range(2):
                head = 2 * pair + half
                keys_ref[head, at, :] = half_lanes(qkv_ref[1, at, cut], half, ext_k)
                values_ref[head, at, :] = half_lanes(qkv_ref[2, at, cut], half, ext_k)
                queries_ref[head, at, :] = half_lanes(query, half, ext_ref[at, cut])
                plain_ref[head, at, :] = half_lanes(query, half, zeros)
                plain_grads_ref[head, at, :] = half_lanes(grad, half, zeros)
                inner = jnp.sum(half_lanes(product, half, 0.0), axis=1, keepdims=True)
                extra = jnp.zeros((tile, 128), F32)
                for place, term in enumerate(three_terms(-inner)):
                    extra = jnp.where((lane & (DH - 1)) == SEGMENTS + place, term, extra)
                grads_ref[head, at, :] = half_lanes(grad, half, extra.astype(BF16))

    dk_ref[...] = jnp.zeros(dk_ref.shape, F32)
    dv_ref[...] = jnp.zeros(dv_ref.shape, F32)

    @pl.loop(0, tiles)
    def _(step):
        def one_block(block, totals):
            after = []
            for pair in range(pairs):
                probs, slopes = [], []
                for head in (2 * pair, 2 * pair + 1):
                    weights = jnp.exp(
                        mm(keys_ref[head, rows(block), :], queries_ref[head, rows(step), :], NT)
                    )
                    flow = mm(values_ref[head, rows(block), :], grads_ref[head, rows(step), :], NT)
                    slope = (weights * flow).astype(BF16)
                    probs.append(weights.astype(BF16))
                    slopes.append(slope)
                    after.append(totals[head] + mm(turned_ref[pair, block, own_rows(head), :], slope))
                both = range(2 * pair, 2 * pair + 2)
                plain = jnp.concatenate([plain_ref[h, rows(step), :] for h in both], axis=0)
                grads = jnp.concatenate([plain_grads_ref[h, rows(step), :] for h in both], axis=0)
                at = lanes(2 * pair)
                dv_ref[rows(block), at] += mm(jnp.concatenate(probs, axis=1), grads)
                dk_ref[rows(block), at] += mm(jnp.concatenate(slopes, axis=1), plain)
            return tuple(after)

        zero = jnp.zeros((DH, tile), F32)
        totals = lax.fori_loop(
            span_ref[step], span_ref[tiles + step], one_block, tuple(zero for _ in heads)
        )
        for pair in range(pairs):
            both = jnp.concatenate(totals[2 * pair : 2 * pair + 2], axis=0)
            dq_ref[rows(step), lanes(2 * pair)] = both.T

    def finish(step, sums):
        cosine, sine = cos_ref[rows(step), :], sin_ref[rows(step), :]
        added = []
        for which, src in enumerate((dq_ref, dk_ref, dv_ref)):
            for pair in range(pairs):
                at = lanes(2 * pair)
                block = src[rows(step), at]
                if which < 2:
                    block = block * cosine - swap_halves(block) * sine
                low = block.astype(BF16)
                out_ref[which, rows(step), at] = low
                total = jnp.sum(low.astype(F32), axis=0, keepdims=True)
                added.append(sums[which * pairs + pair] + total)
        return tuple(added)

    zero = jnp.zeros((1, 128), F32)
    sums = lax.fori_loop(0, tiles, finish, (zero,) * (3 * pairs))
    sums = [jnp.concatenate(sums[w * pairs : (w + 1) * pairs], axis=1) for w in range(3)]
    sum_ref[...] = jnp.concatenate(sums + [jnp.zeros((5, pairs * 128), F32)], axis=0)


def attention_backward(
    spans, qkv, ext, attended, rest, grads, ext_k, cosine, sine, tile
):
    _, n, width = qkv.shape
    span = min(width, ATTENTION_LANES)
    wide = pl.BlockSpec((n, span), lambda i, *_: (0, i))
    three = pl.BlockSpec((3, n, span), lambda i, *_: (0, 0, i))
    tiles, pairs = n // tile, span // 128
    heads = pltpu.VMEM((2 * pairs, n, 128), BF16)
    return call(
        functools.partial(attention_backward_kernel, tile=tile), "attention_backward",
        (width // span,),
        [three, wide, wide, wide, wide, held((n, 128)), held((n, 128)), held((n, 128))],
        [three, pl.BlockSpec((8, span), lambda i, *_: (0, i))],
        [shaped(BF16, 3, n, width), shaped(F32, 8, width)],
        (spans, qkv, ext, attended, rest, grads, ext_k, cosine, sine), 0,
        prefetch=1,
        scratch=[heads, pltpu.VMEM((pairs, tiles, 128, tile), BF16)] + [heads] * 5
        + [pltpu.VMEM((n, span), F32)] * 3,
    )


STRIP = 32


def token_sums(width, queries):
    token = lax.broadcasted_iota(jnp.int32, (width, queries), 0) // QLEN
    return token == lax.broadcasted_iota(jnp.int32, (width, queries), 1)


def score_kernel(low_ref, high_ref, doc_ref, query_ref, pick_ref, out_ref, sum_ref):
    group = pl.program_id(0)
    docs, width = pick_ref.shape[1:]
    doc_rows = doc_ref.shape[0]
    strips = doc_rows // STRIP
    chunk = min(256, doc_rows)
    row = lax.broadcasted_iota(jnp.int32, (STRIP, width), 0)
    sum_ref[...] = jnp.zeros(sum_ref.shape, F32)

    def add_strip(sim, first, doc, pick):
        kept = jnp.where(row == pick - first, sim, 0.0)
        sum_ref[pl.ds(doc, 1)] += jnp.sum(kept.reshape(1, STRIP // 8, 8, width), axis=1)

    for start in range(0, doc_rows, chunk):
        sims = mm(doc_ref[start : start + chunk, :], query_ref[...], NT)
        for first in range(0, chunk, STRIP):
            place = group * strips + (start + first) // STRIP
            low, high = low_ref[place], high_ref[place]
            sim = sims[first : first + STRIP]
            add_strip(sim, start + first, low, pick_ref[0, pl.ds(low, 1), :])
            pick = jnp.where(high > low, pick_ref[0, pl.ds(high, 1), :], -1)
            add_strip(sim, start + first, high, pick)

    @pl.loop(0, strips)
    def _(strip):
        low, high = low_ref[group * strips + strip], high_ref[group * strips + strip]

        @pl.when(high > low + 1)
        def _():
            first = pl.multiple_of(strip * STRIP, STRIP)
            sim = mm(doc_ref[pl.ds(first, STRIP), :], query_ref[...], NT)

            @pl.loop(low + 1, high)
            def _(doc):
                add_strip(sim, first, doc, pick_ref[0, pl.ds(doc, 1), :])

    totals = jnp.sum(sum_ref[...], axis=1)
    totals = jnp.concatenate([totals, jnp.zeros((8 - docs, width), F32)], axis=0)
    spread = token_sums(width, out_ref.shape[2]).astype(F32)
    out_ref[0] = lax.dot_general(
        totals, spread, NN, precision=lax.Precision.HIGHEST, preferred_element_type=F32
    )[:docs]


def score_grad_kernel(
    low_ref, high_ref, doc_ref, query_ref, pick_ref, weight_ref, doc_out, query_out,
    sparse_ref, token_ref,
):
    group = pl.program_id(0)
    docs, width = pick_ref.shape[1:]
    doc_rows = doc_ref.shape[0]
    strips = doc_rows // STRIP
    chunk = min(256, doc_rows)
    row = lax.broadcasted_iota(jnp.int32, (STRIP, width), 0)
    spread = token_sums(width, weight_ref.shape[2]).astype(F32).astype(BF16)
    weights = jnp.concatenate(
        [weight_ref[0], jnp.zeros((16 - docs, weight_ref.shape[2]), F32)], axis=0
    )
    token_ref[...] = mm(weights.astype(BF16), spread, NT)

    def fill(held, first, doc, pick):
        return jnp.where(row == pick - first, token_ref[pl.ds(doc, 1), :], held)

    @pl.when(group == 0)
    def _():
        query_out[...] = jnp.zeros_like(query_out)

    total = None
    for start in range(0, doc_rows, chunk):
        for first in range(start, start + chunk, STRIP):
            place = group * strips + first // STRIP
            low, high = low_ref[place], high_ref[place]
            held = fill(jnp.zeros((STRIP, width), F32), first, low, pick_ref[0, pl.ds(low, 1), :])
            pick = jnp.where(high > low, pick_ref[0, pl.ds(high, 1), :], -1)
            sparse_ref[first : first + STRIP, :] = fill(held, first, high, pick).astype(BF16)
        sparse = sparse_ref[start : start + chunk, :]
        doc_out[start : start + chunk, :] = mm(sparse, query_ref[...])
        turned = doc_ref[start : start + chunk, :].astype(F32).T.astype(BF16)
        part = mm(turned, sparse)
        total = part if total is None else total + part
    query_out[...] += total

    @pl.loop(0, strips)
    def _(strip):
        low, high = low_ref[group * strips + strip], high_ref[group * strips + strip]

        @pl.when(high > low + 1)
        def _():
            first = pl.multiple_of(strip * STRIP, STRIP)
            held = lax.fori_loop(
                low + 1,
                high,
                lambda doc, held: fill(held, first, doc, pick_ref[0, pl.ds(doc, 1), :]),
                jnp.zeros((STRIP, width), F32),
            ).astype(BF16)
            doc_out[pl.ds(first, STRIP), :] += mm(held, query_ref[...])
            turned = doc_ref[pl.ds(first, STRIP), :].astype(F32).T.astype(BF16)
            query_out[...] += mm(turned, held)


def score_specs(doc_tile, query_tile, picks, queries):
    groups, docs, width = picks.shape
    doc_rows = doc_tile.shape[0] // groups
    return (
        pl.BlockSpec((doc_rows, 128), lambda i, *_: (i, 0)),
        held(query_tile.shape),
        pl.BlockSpec((1, docs, width), lambda i, *_: (i, 0, 0)),
        pl.BlockSpec((1, docs, queries), lambda i, *_: (i, 0, 0)),
    )


def score_forward(lows, highs, doc_tile, query_tile, picks):
    groups, docs, width = picks.shape
    queries = width // QLEN
    doc_spec, query_spec, pick_spec, out_spec = score_specs(doc_tile, query_tile, picks, queries)
    return call(
        score_kernel, "score_forward", (groups,),
        [doc_spec, query_spec, pick_spec], [out_spec],
        [shaped(F32, groups, docs, queries)],
        (lows, highs, doc_tile, query_tile, picks), 2 * doc_tile.shape[0] * width * 128,
        prefetch=2, scratch=[pltpu.VMEM((docs, 8, width), F32)],
    )[0]


def score_backward(lows, highs, doc_tile, query_tile, picks, weights):
    groups, docs, width = picks.shape
    doc_spec, query_spec, pick_spec, weight_spec = score_specs(
        doc_tile, query_tile, picks, weights.shape[2]
    )
    return call(
        score_grad_kernel, "score_backward", (groups,),
        [doc_spec, query_spec, pick_spec, weight_spec],
        [doc_spec, pl.BlockSpec((128, width), lambda i, *_: (0, 0))],
        [shaped(F32, *doc_tile.shape), shaped(F32, 128, width)],
        (lows, highs, doc_tile, query_tile, picks, weights), 4 * doc_tile.shape[0] * width * 128,
        prefetch=2,
        scratch=[
            pltpu.VMEM((doc_tile.shape[0] // groups, width), BF16), pltpu.VMEM((16, width), F32)
        ],
    )


def rotary_tables(position):
    half_size = DH // 2
    frequency = jnp.exp(
        jnp.arange(half_size, dtype=F32) * (-2.0 * math.log(10000.0) / DH)
    )
    angles = position.astype(F32)[:, None] * frequency[None, :]
    cosine, sine = jnp.cos(angles), jnp.sin(angles)
    return (
        jnp.concatenate([cosine] * 4, axis=1),
        jnp.concatenate([-sine, sine, -sine, sine], axis=1),
    )


def on_device(
    tokens,
    doc_lengths,
    match_picks,
    labels,
    w_qkv,
    b_qkv,
    w_out,
    b_out,
    ln1_gain,
    ln1_bias,
    w_up,
    b_up,
    w_down,
    b_down,
    ln2_gain,
    ln2_bias,
    w_proj,
    log_scale,
):
    Order.last = ()
    C = lax.axis_size("cols")
    R = lax.axis_size("rows")
    c = lax.axis_index("cols")
    r = lax.axis_index("rows")
    width = tokens.shape[1]
    D = width * C
    Q = ROW_LEN // C
    DS = (tokens.shape[0] - ROW_LEN) // C
    n = Q + DS
    tile = math.gcd(256, math.gcd(Q, DS))

    def shift_cols(value, k):
        return lax.ppermute(value, "cols", [(i, (i + k) % C) for i in range(C)])

    def swap_rows(value, bit):
        return lax.ppermute(value, "rows", [(i, i ^ bit) for i in range(R)])

    def in_order(slots):
        if len(slots) == 1:
            return slots
        if len(slots) == 2:
            return [lax.select(c == 0, slots[0], slots[1]), lax.select(c == 0, slots[1], slots[0])]
        stacked = jnp.stack(slots)
        return [
            lax.dynamic_index_in_dim(stacked, (c - j) % C, 0, keepdims=False) for j in range(C)
        ]

    parts = jnp.concatenate(
        [tokens[:ROW_LEN].reshape(C, Q, width), tokens[ROW_LEN:].reshape(C, DS, width)], axis=1
    )

    def part(k):
        return lax.dynamic_index_in_dim(parts, (c + k) % C, 0, keepdims=False)

    arrived = [shift_cols(part(k), k) for k in range(1, C)]
    x = jnp.concatenate(in_order([part(0)] + arrived), axis=1)

    def gather_slots(shard, behind):
        flat = shard.reshape(-1, shard.shape[-1])
        piece = lax.dynamic_index_in_dim(
            flat.reshape(R, flat.shape[0] // R, flat.shape[1]), r, 0, keepdims=False
        )
        if behind:
            piece, _ = lax.optimization_barrier((piece, arrived))
        others = [
            lax.all_gather(shift_cols(piece, k), "rows", axis=0, tiled=True).reshape(shard.shape)
            for k in range(1, C)
        ]
        return [shard] + others

    wqkv_slots = gather_slots(w_qkv, False)
    wout_slots = gather_slots(w_out, True)
    wup_slots = gather_slots(w_up, True)
    wdown_slots = gather_slots(w_down, True)
    own_proj, _ = lax.optimization_barrier((w_proj, arrived))
    wproj = jnp.concatenate(
        in_order([own_proj] + [shift_cols(own_proj, k) for k in range(1, C)]), axis=0
    )

    pack = [b_qkv.reshape(-1), b_up, b_out, ln1_gain, ln1_bias, b_down, ln2_gain, ln2_bias]
    ends = [0]
    for vector in pack:
        ends.append(ends[-1] + vector.shape[0])
    packed, _ = lax.optimization_barrier((jnp.concatenate(pack), arrived))
    packs = [packed] + [shift_cols(packed, k) for k in range(1, C)]
    ordered_packs = in_order(packs)

    def of_slot(which, k):
        return packs[k][ends[which] : ends[which + 1]]

    def whole(which):
        return jnp.concatenate([p[ends[which] : ends[which + 1]] for p in ordered_packs])

    bqkv_slots = [of_slot(0, k).reshape(b_qkv.shape) for k in range(C)]
    bup_slots = [of_slot(1, k)[None, :] for k in range(C)]
    bout, gain1, bias1, bdown, gain2, bias2 = [whole(which) for which in range(2, 8)]
    zero_row = jnp.zeros_like(bout)
    vectors = jnp.stack([bout, gain1, bias1, bdown, gain2, bias2, zero_row, zero_row])

    own_sizes = lax.dynamic_index_in_dim(
        lax.dynamic_index_in_dim(doc_lengths, r, 0, keepdims=False), c, 0, keepdims=False
    )
    own_ends = jnp.cumsum(own_sizes)
    places = jnp.arange(DS, dtype=jnp.int32)
    passed = places[:, None] >= own_ends[None, :]
    slot_id = jnp.sum(passed.astype(jnp.int32), axis=1)
    slot_begin = jnp.sum(jnp.where(passed, own_sizes[None, :], 0), axis=1)
    query_places = jnp.arange(Q, dtype=jnp.int32)
    position = jnp.concatenate([query_places % QLEN, places - slot_begin])
    cosine, sine = rotary_tables(position)
    segment = jnp.concatenate([(query_places // QLEN) % SEGMENTS, slot_id])
    lane = jnp.arange(128, dtype=jnp.int32)[None, :] % DH
    same = segment[:, None] == lane
    ext_k = (same | ((lane >= SEGMENTS) & (lane < SEGMENTS + 3))).astype(BF16)
    ext_q = jnp.where((lane < SEGMENTS) & ~same, -1e30, 0.0).astype(BF16)
    q_tiles, d_tiles = Q // tile, DS // tile
    steps = jnp.arange(q_tiles, dtype=jnp.int32)
    first_rows = jnp.arange(d_tiles, dtype=jnp.int32) * tile
    is_passed = first_rows[:, None] >= own_ends[None, :]
    low_rows = jnp.sum(jnp.where(is_passed, own_sizes[None, :], 0), axis=1)
    last_passed = (first_rows + tile - 1)[:, None] >= own_ends[None, :]
    high_rows = jnp.min(jnp.where(last_passed, DS, own_ends[None, :]), axis=1)
    spans = jnp.concatenate(
        [steps, q_tiles + low_rows // tile, steps + 1, q_tiles + (high_rows + tile - 1) // tile]
    ).astype(jnp.int32)

    queries_here, tile_docs, _ = match_picks.shape
    docs = own_sizes.shape[0]
    sizes = lax.dynamic_index_in_dim(doc_lengths, c, 1, keepdims=False)
    doc_ends = jnp.cumsum(sizes, axis=1)
    begins = doc_ends - sizes
    picks = jnp.transpose(match_picks, (1, 0, 2)).reshape(tile_docs, queries_here * QLEN)
    picks = begins.reshape(-1)[:, None] + picks % sizes.reshape(-1)[:, None]
    picks = picks.reshape(R, docs, queries_here * QLEN)
    strip_rows = (jnp.arange(DS // STRIP, dtype=jnp.int32) * STRIP)[None, :, None]
    lows = jnp.sum(doc_ends[:, None, :] <= strip_rows, axis=2).astype(jnp.int32).reshape(-1)
    highs = jnp.sum(begins[:, None, :] < strip_rows + STRIP, axis=2).astype(jnp.int32) - 1
    highs = highs.reshape(-1)

    qkv, attended, rests, exts = [], [], [], []
    for k in range(C):
        first = (picks, lows, highs) if k == 0 else ()
        qkv.append(project_qkv(x, wqkv_slots[k], bqkv_slots[k], cosine, sine, first))
        out, rest, ext = attention_forward(spans, qkv[k], ext_k, ext_q, tile)
        attended.append(out)
        rests.append(rest)
        exts.append(ext)
    normed_one, inverse_one, hidden_low, hidden_t = out_and_norm(x, vectors, attended, wout_slots)
    active, slopes = zip(*[up_and_gelu(hidden_low, wup_slots[k], bup_slots[k]) for k in range(C)])
    normed_two, inverse_two, output_low, unit, unit_low, unit_inverse = down_and_norm(
        normed_one, vectors, wproj, active, wdown_slots
    )

    doc_tile = lax.all_gather(unit_low[Q:], "rows", axis=0, tiled=True)
    query_tile = jnp.concatenate(
        in_order([unit_low[:Q]] + [shift_cols(unit_low[:Q], k) for k in range(1, C)]), axis=0
    )
    sims = score_forward(lows, highs, doc_tile, query_tile, picks)
    scores = sims.reshape(tile_docs, queries_here).T

    scale = jnp.exp(log_scale[0])
    z = scale * scores
    row_top = jnp.max(z, axis=1)
    row_mass = jnp.sum(jnp.exp(z - row_top[:, None]), axis=1)
    is_label = (
        jnp.arange(tile_docs, dtype=jnp.int32)[None, :] == (labels - c * tile_docs)[:, None]
    )
    chosen = jnp.sum(jnp.where(is_label, z, 0.0), axis=1)
    own_stats = jnp.stack([row_top, row_mass, chosen])
    stats = jnp.stack([own_stats] + [shift_cols(own_stats, k) for k in range(1, C)])
    top_all = jnp.max(stats[:, 0], axis=0)
    mass_all = jnp.sum(stats[:, 1] * jnp.exp(stats[:, 0] - top_all), axis=0)
    log_total = top_all + jnp.log(mass_all)
    loss = log_total - jnp.sum(stats[:, 2], axis=0)
    dz = (jnp.exp(z - log_total[:, None]) - is_label.astype(F32)) / (queries_here * R)
    scale_part = jnp.sum(dz * z)
    dscores = (scale * dz).T.reshape(R, docs, queries_here)
    doc_grad, query_grad_t = score_backward(lows, highs, doc_tile, query_tile, picks, dscores)
    query_parts = query_grad_t.T.reshape(C, Q, 128)

    def query_part(k):
        return lax.dynamic_index_in_dim(query_parts, (c + k) % C, 0, keepdims=False)

    query_grad = query_part(0)
    for k in range(1, C):
        query_grad = query_grad + shift_cols(query_part(k), k)

    def halve(total, bit, wire):
        size = total.shape[0] // 2
        pairs = total.reshape((size, 2) + total.shape[1:])
        mine = (r // bit) % 2
        send = lax.dynamic_index_in_dim(pairs, 1 - mine, 1, keepdims=False).astype(wire)
        keep = lax.dynamic_index_in_dim(pairs, mine, 1, keepdims=False)
        return keep + swap_rows(send, bit).astype(F32)

    doc_sum = doc_grad.reshape(R, DS, 128)
    bit = 1
    while bit < R:
        doc_sum = halve(doc_sum, bit, BF16)
        bit *= 2
    unit_grad = jnp.concatenate([query_grad, doc_sum[0]], axis=0)

    core = r % 2
    slots_back = range(C - 1, -1, -1)
    share = D // R
    x_bit, *z_bits = [1 << b for b in range(1, R.bit_length() - 1)]

    def side_of(bit):
        return ((r // bit) % 2).astype(jnp.int32)

    keep_places = jnp.stack([core, side_of(z_bits[0])]).astype(jnp.int32)
    send_places = jnp.stack([1 - core, 0 * core]).astype(jnp.int32)

    def halves_of(left_t):
        return left_t.reshape(R // 2, 2, share, n)

    def send_half(lefts, rights):
        return swap_rows(weight_pull(send_places, lefts, rights)[0], 1)

    def keep_half(left, right, arrived, k):
        kept = weight_pull(keep_places, [left], [right], arrived, F32 if k == 0 else BF16)[0]
        return kept if k == 0 else shift_cols(kept, C - k)

    def next_fold(states, bit, inner):
        send, keep = fold(side_of(bit), [s[0] for s in states], [s[1] for s in states], inner)
        return keep, swap_rows(send, bit)

    def close(state):
        return state[0] + state[1].astype(F32)

    def cols_state(kept):
        rest = kept[1]
        for other in kept[2:]:
            rest = rest.astype(F32) + other.astype(F32)
        return kept[0], rest

    embed_grad, resid_two_grad, branch, branch_t, head_sums = head_pull(
        unit_grad, unit, unit_inverse, wproj, normed_two, inverse_two, vectors
    )
    down_left, down_right = halves_of(branch_t), [a[None] for a in active]
    pre_grads, up_sums, down_kept = [None] * C, [None] * C, [None] * C
    down_arrived = [None] * C
    for k in slots_back:
        down_arrived[k] = send_half([down_left], [down_right[k]])
    for k in slots_back:
        pre_grads[k], up_sums[k] = up_pull(branch, wdown_slots[k], slopes[k])
        if k > 0:
            down_kept[k] = keep_half(down_left, down_right[k], down_arrived[k], k)
    up_left, up_right = halves_of(hidden_t), [g[None] for g in pre_grads]
    up_arrived, up_kept = [None] * C, [None] * C
    for k in slots_back:
        up_arrived[k] = send_half([up_left], [up_right[k]])
    down_kept[0] = keep_half(down_left, down_right[0], down_arrived[0], 0)
    for k in slots_back[:-1]:
        up_kept[k] = keep_half(up_left, up_right[k], up_arrived[k], k)
    resid_one_grad, branch_one_t, hidden_sums, *attended_grads = hidden_pull(
        resid_two_grad, normed_one, inverse_one, vectors, pre_grads, wup_slots, wout_slots
    )
    up_kept[0] = keep_half(up_left, up_right[0], up_arrived[0], 0)
    mixed_grads, mixed_sums = [None] * C, [None] * C
    late_lefts, late_state, late_arrived = [halves_of(x.T), halves_of(branch_one_t)], [None] * C, [None] * C

    def late_rights(k):
        return [mixed_grads[k], attended[k][None]]

    def pull_attention(k):
        mixed_grads[k], mixed_sums[k] = attention_backward(
            spans, qkv[k], exts[k], attended[k], rests[k], attended_grads[k], ext_k, cosine, sine,
            tile,
        )
        late_arrived[k] = send_half(late_lefts, late_rights(k))

    def keep_late(k):
        send, keep = weight_pull(
            keep_places, late_lefts, late_rights(k), late_arrived[k], inner=2 * share
        )
        late_state[k] = (keep, swap_rows(send, z_bits[0]))

    for k in slots_back[:-1]:
        pull_attention(k)
    wide_state = next_fold([cols_state(down_kept), cols_state(up_kept)], x_bit, share)
    pull_attention(0)
    for k in slots_back[:-1]:
        keep_late(k)
    sent = [
        shift_cols(token_pull((c + k) % C, resid_one_grad, mixed_grads, wqkv_slots, BF16), k)
        for k in range(1, C)
    ]
    keep_late(0)
    for k in slots_back[:-1]:
        late_state[k] = next_fold([late_state[k]], (z_bits + [x_bit])[1], 2 * share)
    own_tokens = token_pull(c, resid_one_grad, mixed_grads, wqkv_slots, F32)
    wide_state = next_fold([wide_state], z_bits[0], share)
    for bit in z_bits[2:] + [x_bit]:
        for k in slots_back[:-1]:
            late_state[k] = next_fold([late_state[k]], bit, share if bit == x_bit else 2 * share)
    for bit in z_bits[1:] + [x_bit]:
        late_state[0] = next_fold([late_state[0]], bit, share if bit == x_bit else 2 * share)
        if bit != x_bit:
            wide_state = next_fold([wide_state], bit, share)
    late_grad = close(late_state[0])
    for k in slots_back[:-1]:
        late_grad = late_grad + shift_cols(close(late_state[k]).astype(BF16), C - k).astype(F32)
    qkv_grad, out_grad = late_grad[:3], late_grad[3]
    down_grad, up_grad = close(wide_state)
    ordered = in_order([own_tokens] + [s.astype(F32) for s in sent])
    tokens_grad = jnp.concatenate([s[:Q] for s in ordered] + [s[Q:] for s in ordered], axis=0)
    proj_grad = mm(embed_grad, output_low, TN).reshape(R, -1, C, width)

    def cut(values, slot_rows):
        return values.reshape(slot_rows, R, -1)

    own_order = [(c - k) % C for k in range(C)]
    canonical = jnp.stack(
        [hidden_sums[0], hidden_sums[1], hidden_sums[2], head_sums[0], head_sums[1], head_sums[2]]
    ).reshape(6, C, R, -1)
    slots_small = []
    for k in range(C):
        rows = [mixed_sums[k][j].reshape(R, -1) for j in range(3)]
        rows.append(up_sums[k][0].reshape(R, -1))
        rows += [
            lax.dynamic_index_in_dim(canonical[j], own_order[k], 0, keepdims=False)
            for j in range(6)
        ]
        own_proj_grad = lax.dynamic_index_in_dim(proj_grad, own_order[k], 2, keepdims=False)
        rows.append(own_proj_grad.reshape(R, -1))
        rows.append(jnp.broadcast_to(scale_part, (R, 1)))
        slots_small.append(jnp.concatenate(rows, axis=1))
    small = jnp.stack(in_order(slots_small)).reshape(C * R, -1)
    small = lax.psum_scatter(small, ("cols", "rows"), scatter_dimension=0, tiled=True)[0]
    one = D // (C * R)
    up_part = bup_slots[0].shape[1] // R
    bounds = [3 * one, 3 * one + up_part]
    for _ in range(6):
        bounds.append(bounds[-1] + one)
    pieces = [small[a:b] for a, b in zip(bounds[:-1], bounds[1:])]
    bup_out, bout_out, gain1_out, bias1_out, bdown_out, gain2_out, bias2_out = pieces
    return (
        scores,
        loss,
        tokens_grad,
        qkv_grad,
        small[: bounds[0]].reshape(3, one),
        out_grad.T,
        bout_out,
        gain1_out,
        bias1_out,
        up_grad,
        bup_out,
        down_grad.T,
        bdown_out,
        gain2_out,
        bias2_out,
        small[bounds[-1] : -1].reshape(-1, width).T,
        small[-1:],
    )


def solution(mesh):
    in_specs = (
        P("rows", "cols"),
        P(),
        P("rows", "cols", None),
        P("rows"),
        P(None, None, "cols"),
        P(None, "cols"),
        P("cols", None),
        P("cols"),
        P("cols"),
        P("cols"),
        P(None, "cols"),
        P("cols"),
        P("cols", None),
        P("cols"),
        P("cols"),
        P("cols"),
        P("cols", None),
        P(),
    )
    out_specs = (
        P("rows", "cols"),
        P("rows"),
        P("rows", "cols"),
        P(None, "rows", "cols"),
        P(None, ("cols", "rows")),
        P("cols", "rows"),
        P(("cols", "rows")),
        P(("cols", "rows")),
        P(("cols", "rows")),
        P("rows", "cols"),
        P(("cols", "rows")),
        P("cols", "rows"),
        P(("cols", "rows")),
        P(("cols", "rows")),
        P(("cols", "rows")),
        P("cols", "rows"),
        P(),
    )
    return jax.shard_map(
        on_device, mesh=mesh, in_specs=in_specs, out_specs=out_specs, check_vma=False
    )
```

time: 1270 us -> 1070 us (0.84)
  matrix products: 325 us -> 0.6 us
  Pallas kernels: 290 us -> 594 us
  blocking collectives: 129 us -> 0 us
  local copies, waits for them, and re-layouts: 94.9 us -> 72.3 us
  other arithmetic: 67.6 us -> 50.1 us
  starting transfers between devices: 49.7 us -> 35.8 us
    dot_general x51 -> x1, matrix products: 325 us -> 0.6 us  [mm(): return lax.dot_general(left, right, dims, preferred_element_type=F32)]
    pallas_call x4 -> x37, Pallas kernels: 290 us -> 594 us  [call(): pl.pallas_call(wrapped, grid_spec=pltpu.PrefetchScalarGridSpec(num_scalar...]
    ppermute x12 -> x14, waiting for transfers between devices: 118 us -> 53.5 us  [shift_cols(): return lax.ppermute(value, 'cols', [(i, (i + k) % C) for i in range(C)])]
    unnamed x8 -> x7, waiting for transfers between devices: 33 us -> 94.3 us
    all_gather x4 -> x0, blocking collectives: 48.8 us -> none  [the longest x1 32.6 us: on_device(): spread = lax.all_gather(jnp.concatenate(vectors), 'cols', axis=0)]
    unnamed x1 -> x0, blocking collectives: 41.6 us -> none
    psum x1 -> x0, blocking collectives: 38.7 us -> none  [on_device(): scale_sum = lax.psum(jnp.sum(dz * z), ('rows', 'cols'))]
    unnamed x263 -> x76, local copies, waits for them, and re-layouts: 36.1 us -> 12.3 us
  transfers between devices with their start and end apart: 53 -> 39, of which waited for: 27 -> 17; matrix products, arithmetic and copies ran while one was open for 22% -> 9% of each run, Pallas kernels for 8% -> 45%
where the time goes in v3:
time: 1070 us; the launch traced here: 1060 us
  Pallas kernels  594 us (56%)
  waiting for transfers between devices  290 us (27%)
  local copies, waits for them, and re-layouts  72.3 us (7%)
  other arithmetic  50.1 us (5%)
  starting transfers between devices  35.8 us (3%)
  between operations  16 us (1%)
    pallas_call x37, Pallas kernels, call(): pl.pallas_call(wrapped, grid_spec=pltpu.PrefetchScalarGridSpec(num_scalar...  594 us
    ppermute x19, waiting for transfers between devices, swap_rows(): return lax.ppermute(value, 'rows', [(i, i ^ bit) for i in range(R)])  98.4 us
    unnamed x7, waiting for transfers between devices  94.3 us
    ppermute x14, waiting for transfers between devices, shift_cols(): return lax.ppermute(value, 'cols', [(i, (i + k) % C) for i in range(C)])  53.5 us
    all_gather x1, waiting for transfers between devices, on_device(): doc_tile = lax.all_gather(unit_low[Q:], 'rows', axis=0, tiled=True)  44.2 us
  transfers between devices with their start and end apart: 39, of which 17 were waited for; matrix products, arithmetic and copies ran while one was open for 9% of the time, Pallas kernels for 45%

profile of v3, /device:TPU:0, one launch (start us, length us, event | category | flops | bytes accessed | tf_op | source)
XLA Modules:
  0.0 1058.7 jit_solution(14332408255723336728)
XLA Ops:
  8.2 3.0 collective-permute-start.2
  11.2 4.9 collective-permute-done.2
  22.8 33.0 %collective-permute-done = bf16[1536,512]{1,0:T(8,128)(2,1)S(1)} collective-permute-done((bf16[1536,512]{1,0:T(8,128)(2,1)S(1)}, bf16[1536,512]{1,0:T(8,128)(2,1)S(1)}, u32[]{:S(2)}, u32[]{:S(2)}) %collective-permute-start) | collective-permute-done | bytes 1572896 | tf_op jit(solution)/shard_map/ppermute | solution.py:963
  58.4 2.8 collective-permute-done.3
  64.4 4.9 collective-permute-done.5
  70.6 2.8 copy.95
  80.3 5.9 fusion.9.refs_5_.refs_4_
  86.2 2.8 fusion.10
  94.2 2.9 collective-permute-done.6
  111.4 2.5 fusion.24
  113.9 13.7 %project_qkv.2.refs_1_.refs_4_ = bf16[3,1536,512]{2,1,0:T(8,128)(2,1)} custom-call(bf16[1536,1024]{1,0:T(8,128)(2,1)} %get-tuple-element.172.refs_0_, bf16[3,1024,512]{2,1,0:T(8,128)(2,1)} %refs_4_.5, f32[3,512]{1,0:T(4,128)} %slice.254.refs_2_, f32[1536,128]{1,0:T(8,128)} %pad_maximum_fusion.2.refs_3_.refs_7_, ...), custom_call_target="tpu_custom_call" | custom-call | flops 4831838208 | bytes 12589056 | tf_op jit(solution)/shard_map/project_qkv/pallas_call | solution.py:59
  127.6 29.1 %attention_forward.2 = (bf16[1536,512]{1,0:T(8,128)(2,1)}, bf16[1536,512]{1,0:T(8,128)(2,1)}, bf16[1536,512]{1,0:T(8,128)(2,1)}) custom-call(s32[12]{0:T(128)} %pad_add_fusion.1.refs_0_, bf16[3,1536,512]{2,1,0:T(8,128)(2,1)} %project_qkv.2.refs_1_.refs_4_, bf16[1536,128]{1,0:T(8,128)(2,1)} %fusion.6.refs_2_.refs_6_, ...), custom_call_target="tpu_custom_call" | custom-call | bytes 1024 | tf_op jit(solution)/shard_map/attention_forward/pallas_call | solution.py:59
  159.5 13.8 %project_qkv.3.refs_1_.refs_4_ = bf16[3,1536,512]{2,1,0:T(8,128)(2,1)} custom-call(bf16[1536,1024]{1,0:T(8,128)(2,1)} %get-tuple-element.172.refs_0_, bf16[3,1024,512]{2,1,0:T(8,128)(2,1)} %bitcast.179, f32[3,512]{1,0:T(4,128)} %slice.256.refs_2_, f32[1536,128]{1,0:T(8,128)} %pad_maximum_fusion.2.refs_3_.refs_7_, ...), custom_call_target="tpu_custom_call" | custom-call | flops 4831838208 | bytes 12589056 | tf_op jit(solution)/shard_map/project_qkv/pallas_call | solution.py:59
  173.3 28.9 %attention_forward.3 = (bf16[1536,512]{1,0:T(8,128)(2,1)}, bf16[1536,512]{1,0:T(8,128)(2,1)}, bf16[1536,512]{1,0:T(8,128)(2,1)}) custom-call(s32[12]{0:T(128)} %pad_add_fusion.1.refs_0_, bf16[3,1536,512]{2,1,0:T(8,128)(2,1)} %project_qkv.3.refs_1_.refs_4_, bf16[1536,128]{1,0:T(8,128)(2,1)} %fusion.6.refs_2_.refs_6_, ...), custom_call_target="tpu_custom_call" | custom-call | bytes 1024 | tf_op jit(solution)/shard_map/attention_forward/pallas_call | solution.py:59
  202.2 11.4 %out_and_norm.1 = (f32[1536,1024]{1,0:T(8,128)}, f32[1536,1]{1,0:T(8,128)}, bf16[1536,1024]{1,0:T(8,128)(2,1)}, bf16[1024,1536]{1,0:T(8,128)(2,1)}) custom-call(bf16[1536,1024]{1,0:T(8,128)(2,1)} %get-tuple-element.172.refs_0_, f32[8,1024]{1,0:T(8,128)} %stack.74.refs_1_.refs_6_.refs_3_, bf16[1536,512]{1,0:T(8,128)(2,1)} %get-tuple-element.81.refs_5_.refs_2_.refs_3_, ...), custom_call_target="tpu_custom_call" | custom-call | flops 3221225472 | bytes 21010432 | tf_op jit(solution)/shard_map/out_and_norm/pallas_call | solution.py:59
  213.6 32.9 %up_and_gelu.2 = (bf16[1536,2048]{1,0:T(8,128)(2,1)}, f32[1536,2048]{1,0:T(8,128)}) custom-call(bf16[1536,1024]{1,0:T(8,128)(2,1)} %get-tuple-element.86.refs_0_, bf16[1024,2048]{1,0:T(8,128)(2,1)} %refs_6_.1, f32[1,2048]{1,0:T(1,128)} %bitcast.210, f32[1536,1]{1,0:T(8,128)} %get-tuple-element.87.refs_3_.refs_2_), custom_call_target="tpu_custom_call" | custom-call | flops 16106127360 | bytes 26222592 | tf_op jit(solution)/shard_map/up_and_gelu/pallas_call | solution.py:59
  246.5 22.5 %up_and_gelu.3 = (bf16[1536,2048]{1,0:T(8,128)(2,1)}, f32[1536,2048]{1,0:T(8,128)}) custom-call(bf16[1536,1024]{1,0:T(8,128)(2,1)} %get-tuple-element.86.refs_0_, bf16[1024,2048]{1,0:T(8,128)(2,1)} %all-gather.10.cloned.1.call-done.refs_1_.refs_7_, f32[1,2048]{1,0:T(1,128)} %bitcast.211, bf16[1536,2048]{1,0:T(8,128)(2,1)} %get-tuple-element.88.refs_3_), custom_call_target="tpu_custom_call" | custom-call | flops 16106127360 | bytes 26222592 | tf_op jit(solution)/shard_map/up_and_gelu/pallas_call | solution.py:59
  269.0 24.6 %down_and_norm.1 = (f32[1536,1024]{1,0:T(8,128)}, f32[1536,1]{1,0:T(8,128)}, bf16[1536,1024]{1,0:T(8,128)(2,1)}, f32[1536,128]{1,0:T(8,128)}, bf16[1536,128]{1,0:T(8,128)(2,1)}, /*index=5*/f32[1536,1]{1,0:T(8,128)}) custom-call(f32[1536,1024]{1,0:T(8,128)} %get-tuple-element.84.refs_0_.refs_1_, f32[8,1024]{1,0:T(8,128)} %stack.74.refs_1_.refs_6_.refs_3_, ...), custom_call_target="tpu_custom_call" | custom-call | flops 12884901888 | bytes 38187008 | tf_op jit(solution)/shard_map/down_and_norm/pallas_call | solution.py:59
  298.5 2.8 collective-permute-done.7
  303.0 44.2 %all-gather.14.cloned.1.call-done.refs_2_ = bf16[16384,128]{1,0:T(8,128)(2,1)} async-done(((bf16[1024,128]{1,0:T(8,128)(2,1)}), bf16[16384,128]{1,0:T(8,128)(2,1)}) %all-gather.14.cloned.1.call-update) | async-done | bytes 4194320 | tf_op jit(solution)/shard_map/all_gather | solution.py:1084
  347.1 39.6 %score_forward.1.refs_6_ = f32[16,4,32]{2,1,0:T(4,128)} custom-call(s32[512]{0:T(512)} %reshape.924.refs_6_.refs_0_, s32[512]{0:T(512)} %sub.123.refs_7_.refs_1_, bf16[16384,128]{1,0:T(8,128)(2,1)} %all-gather.14.cloned.1.call-done.refs_2_, bf16[1024,128]{1,0:T(8,128)(2,1)} %pad_maximum_fusion.7.refs_3_, s32[16,4,1024]{2,1,0:T(4,128)} %fusion.9.refs_5_.refs_4_, ...), custom_call_target="tpu_custom_call" | custom-call | flops 4294967296 | bytes 4730880 | tf_op jit(solution)/shard_map/score_forward/pallas_call | solution.py:59
  393.6 37.2 %score_backward.1 = (f32[16384,128]{1,0:T(8,128)}, f32[128,1024]{1,0:T(8,128)}) custom-call(s32[512]{0:T(512)} %reshape.924.refs_6_.refs_0_, s32[512]{0:T(512)} %sub.123.refs_7_.refs_1_, bf16[16384,128]{1,0:T(8,128)(2,1)} %all-gather.14.cloned.1.call-done.refs_2_, bf16[1024,128]{1,0:T(8,128)(2,1)} %pad_maximum_fusion.7.refs_3_, ...), custom_call_target="tpu_custom_call" | custom-call | flops 8589934592 | bytes 13643776 | tf_op jit(solution)/shard_map/score_backward/pallas_call | solution.py:59
  430.7 3.8 fusion
  434.6 4.5 collective-permute-done.10
  439.1 3.2 bitcast_add_fusion
  445.9 25.0 %collective-permute-done.11 = bf16[4,1024,128]{2,1,0:T(8,128)(2,1)} collective-permute-done((bf16[4,1024,128]{2,1,0:T(8,128)(2,1)}, bf16[4,1024,128]{2,1,0:T(8,128)(2,1)}, u32[]{:S(2)}, u32[]{:S(2)}) %collective-permute-start.11) | collective-permute-done | bytes 1048608 | tf_op jit(solution)/shard_map/ppermute | solution.py:966
  481.8 6.8 collective-permute-done.12
  495.2 9.9 collective-permute-done.13
  507.2 12.1 %head_pull.1 = (bf16[1536,128]{1,0:T(8,128)(2,1)}, f32[1536,1024]{1,0:T(8,128)}, bf16[1536,1024]{1,0:T(8,128)(2,1)}, bf16[1024,1536]{1,0:T(8,128)(2,1)}, f32[8,1024]{1,0:T(8,128)}) custom-call(f32[1536,128]{1,0:T(8,128)} %pad_maximum_fusion.4.refs_0_, f32[1536,128]{1,0:T(8,128)} %get-tuple-element.96.refs_1_, f32[1536,1]{1,0:T(8,128)} %get-tuple-element.97.refs_2_, ...), custom_call_target="tpu_custom_call" | custom-call | flops 805306368 | bytes 21180416 | tf_op jit(solution)/shard_map/head_pull/pallas_call | solution.py:59
  519.3 8.1 weight_pull.12.refs_3_
  528.0 8.1 weight_pull.13.refs_3_
  536.6 13.6 %up_pull.2 = (bf16[1536,2048]{1,0:T(8,128)(2,1)}, f32[8,2048]{1,0:T(8,128)}) custom-call(bf16[1536,1024]{1,0:T(8,128)(2,1)} %get-tuple-element.100.refs_0_, bf16[2048,1024]{1,0:T(8,128)(2,1)} %all-gather.12.cloned.1.call-done.refs_6_.refs_1_, f32[1536,2048]{1,0:T(8,128)} %get-tuple-element.104.refs_2_, bf16[1,512,2048]{2,1,0:T(8,128)(2,1)} %weight_pull.13.refs_3_), custom_call_target="tpu_custom_call" | custom-call | flops 6442450944 | bytes 26279936 | tf_op jit(solution)/shard_map/up_pull/pallas_call | solution.py:59
  551.5 8.5 weight_pull.14.refs_3_
  560.0 13.7 %up_pull.3 = (bf16[1536,2048]{1,0:T(8,128)(2,1)}, f32[8,2048]{1,0:T(8,128)}) custom-call(bf16[1536,1024]{1,0:T(8,128)(2,1)} %get-tuple-element.100.refs_0_, bf16[2048,1024]{1,0:T(8,128)(2,1)} %refs_1_.5, f32[1536,2048]{1,0:T(8,128)} %get-tuple-element.101.refs_2_, bf16[1,512,2048]{2,1,0:T(8,128)(2,1)} %weight_pull.14.refs_3_), custom_call_target="tpu_custom_call" | custom-call | flops 6442450944 | bytes 26279936 | tf_op jit(solution)/shard_map/up_pull/pallas_call | solution.py:59
  573.7 8.1 weight_pull.15.refs_3_
  581.9 8.1 weight_pull.16.refs_4_
  590.5 2.9 copy.103
  594.9 8.9 weight_pull.17.refs_4_.refs_1_
  603.8 8.4 weight_pull.18.refs_10_
  612.8 29.3 %hidden_pull.1 = (f32[1536,1024]{1,0:T(8,128)}, bf16[1024,1536]{1,0:T(8,128)(2,1)}, f32[8,1024]{1,0:T(8,128)}, bf16[1536,512]{1,0:T(8,128)(2,1)}, bf16[1536,512]{1,0:T(8,128)(2,1)}) custom-call(f32[1536,1024]{1,0:T(8,128)} %get-tuple-element.99.refs_0_, f32[1536,1024]{1,0:T(8,128)} %get-tuple-element.84.refs_0_.refs_1_, ...), custom_call_target="tpu_custom_call" | custom-call | bytes 1024 | tf_op jit(solution)/shard_map/hidden_pull/pallas_call | solution.py:59
  642.1 8.9 weight_pull.19.refs_9_.refs_2_
  651.0 55.9 %attention_backward.2 = (bf16[3,1536,512]{2,1,0:T(8,128)(2,1)}, f32[8,512]{1,0:T(8,128)}) custom-call(s32[12]{0:T(128)} %pad_add_fusion.1.refs_0_, bf16[3,1536,512]{2,1,0:T(8,128)(2,1)} %project_qkv.3.refs_1_.refs_4_, bf16[1536,512]{1,0:T(8,128)(2,1)} %get-tuple-element.116.refs_2_, bf16[1536,512]{1,0:T(8,128)(2,1)} %get-tuple-element.82.refs_3_.refs_6_, ...), custom_call_target="tpu_custom_call" | custom-call | bytes 1024 | tf_op jit(solution)/shard_map/attention_backward/pallas_call | solution.py:59
  706.9 9.3 weight_pull.20.refs_5_
  729.5 8.6 fold.7
  738.0 55.7 %attention_backward.3 = (bf16[3,1536,512]{2,1,0:T(8,128)(2,1)}, f32[8,512]{1,0:T(8,128)}) custom-call(s32[12]{0:T(128)} %pad_add_fusion.1.refs_0_, bf16[3,1536,512]{2,1,0:T(8,128)(2,1)} %project_qkv.2.refs_1_.refs_4_, bf16[1536,512]{1,0:T(8,128)(2,1)} %get-tuple-element.111.refs_2_, bf16[1536,512]{1,0:T(8,128)(2,1)} %get-tuple-element.81.refs_5_.refs_2_.refs_3_, ...), custom_call_target="tpu_custom_call" | custom-call | bytes 1024 | tf_op jit(solution)/shard_map/attention_backward/pallas_call | solution.py:59
  793.7 8.9 weight_pull.21.refs_6_
  803.2 9.5 weight_pull.22
  812.7 11.0 %token_pull.2.refs_6_ = bf16[1536,512]{1,0:T(8,128)(2,1)} custom-call(s32[1]{0:T(128)} %bitcast.66.refs_0_, f32[1536,1024]{1,0:T(8,128)} %get-tuple-element.110.refs_1_, bf16[3,1536,512]{2,1,0:T(8,128)(2,1)} %get-tuple-element.122.refs_3_.refs_2_, bf16[3,1536,512]{2,1,0:T(8,128)(2,1)} %get-tuple-element.119.refs_3_, bf16[3,1024,512]{2,1,0:T(8,128)(2,1)} %refs_4_.5, ...), custom_call_target="tpu_custom_call" | custom-call | flops 4831838208 | bytes 23592964 | tf_op jit(solution)/shard_map/token_pull/pallas_call | solution.py:59
  827.4 9.8 weight_pull.23
  839.2 3.9 fold.8
  843.1 11.4 %token_pull.3.refs_3_ = f32[1536,512]{1,0:T(8,128)} custom-call(s32[1]{0:T(128)} %bitcast.36.refs_0_, f32[1536,1024]{1,0:T(8,128)} %get-tuple-element.110.refs_1_, bf16[3,1536,512]{2,1,0:T(8,128)(2,1)} %get-tuple-element.122.refs_3_.refs_2_, bf16[3,1536,512]{2,1,0:T(8,128)(2,1)} %get-tuple-element.119.refs_3_, bf16[3,1024,512]{2,1,0:T(8,128)(2,1)} %refs_4_.5, ...), custom_call_target="tpu_custom_call" | custom-call | flops 4831838208 | bytes 25165828 | tf_op jit(solution)/shard_map/token_pull/pallas_call | solution.py:59
  855.8 5.3 fold.9
  861.8 94.2 %all-reduce.3.cloned.1.call-done = f32[32,4513]{1,0:T(8,128)} async-done(((f32[32,4513]{1,0:T(8,128)}), f32[32,4513]{1,0:T(8,128)}) %all-reduce.3.cloned.1.call-update) | async-done | bytes 577680
  966.3 2.7 collective-permute-start.25
  969.0 2.3 convert_select_fusion.1
  971.8 20.7 %collective-permute-done.25.refs_2_ = bf16[4,128,512]{2,1,0:T(8,128)(2,1)} collective-permute-done((bf16[4,128,512]{2,1,0:T(8,128)(2,1)}, bf16[4,128,512]{2,1,0:T(8,128)(2,1)}, u32[]{:S(2)}, u32[]{:S(2)}) %collective-permute-start.25) | collective-permute-done | bytes 524320 | tf_op jit(solution)/shard_map/ppermute | solution.py:966
  992.5 3.4 fold.10
  997.4 3.9 fold.11
  1001.3 4.0 fold.12
  1005.3 2.9 collective-permute-start.32
  1008.2 3.1 pad_maximum_fusion
  1012.4 24.9 %collective-permute-done.27.refs_2_ = bf16[4,128,512]{2,1,0:T(8,128)(2,1)S(1)} collective-permute-done((bf16[4,128,512]{2,1,0:T(8,128)(2,1)}, bf16[4,128,512]{2,1,0:T(8,128)(2,1)S(1)}, u32[]{:S(2)}, u32[]{:S(2)}) %collective-permute-start.27) | collective-permute-done | bytes 524320 | tf_op jit(solution)/shard_map/ppermute | solution.py:966
  1038.1 3.4 fold.13
  1042.1 6.3 collective-permute-done.32
  (285 shorter events, 123.3 us)
Async XLA Ops:
  7.2 152.3 %all-gather.6.cloned.1.call-start = ((), (), s32[]{:S(2)}) async-start(), calls=%async_computation | async-start | bytes 3342336 | tf_op jit(solution)/shard_map/all_gather | solution.py:996
  8.2 7.9 collective-permute-start.2
  16.8 185.4 %all-gather.8.cloned.1.call-start = ((), (), s32[]{:S(2)}) async-start(), calls=%async_computation.1 | async-start | bytes 1114112 | tf_op jit(solution)/shard_map/all_gather | solution.py:996
  19.9 50.2 %copy-start.21 = (s32[16,2,4]{0,2,1:T(4,128)S(1)}, s32[16,2,4]{0,2,1:T(4,128)}, u32[]{:S(2)}) copy-start(s32[16,2,4]{0,2,1:T(4,128)} %param.19) | copy-start | bytes 1540
  19.9 50.3 %copy-start.22 = (f32[3,512]{1,0:T(4,128)S(1)}, f32[3,512]{1,0:T(4,128)}, u32[]{:S(2)}) copy-start(f32[3,512]{1,0:T(4,128)} %param.23) | copy-start | bytes 18436
  20.1 56.9 %copy-start.23 = (f32[2048]{0:T(1024)S(1)}, f32[2048]{0:T(1024)}, u32[]{:S(2)}) copy-start(f32[2048]{0:T(1024)} %param.29) | copy-start | bytes 24580
  20.1 56.9 %copy-start.26 = (f32[512]{0:T(512)S(1)}, f32[512]{0:T(512)}, u32[]{:S(2)}) copy-start(f32[512]{0:T(512)} %param.25) | copy-start | bytes 6148
  20.1 56.9 %copy-start.27 = (f32[512]{0:T(512)S(1)}, f32[512]{0:T(512)}, u32[]{:S(2)}) copy-start(f32[512]{0:T(512)} %param.26) | copy-start | bytes 6148
  20.1 57.0 %copy-start.28 = (f32[512]{0:T(512)S(1)}, f32[512]{0:T(512)}, u32[]{:S(2)}) copy-start(f32[512]{0:T(512)} %param.27) | copy-start | bytes 6148
  20.1 57.0 %copy-start.29 = (f32[512]{0:T(512)S(1)}, f32[512]{0:T(512)}, u32[]{:S(2)}) copy-start(f32[512]{0:T(512)} %param.31) | copy-start | bytes 6148
  20.1 57.0 %copy-start.30 = (f32[512]{0:T(512)S(1)}, f32[512]{0:T(512)}, u32[]{:S(2)}) copy-start(f32[512]{0:T(512)} %param.32) | copy-start | bytes 6148
  20.1 57.0 %copy-start.31 = (f32[512]{0:T(512)S(1)}, f32[512]{0:T(512)}, u32[]{:S(2)}) copy-start(f32[512]{0:T(512)} %param.33) | copy-start | bytes 6148
  20.2 35.6 %collective-permute-start = (bf16[1536,512]{1,0:T(8,128)(2,1)S(1)}, bf16[1536,512]{1,0:T(8,128)(2,1)S(1)}, u32[]{:S(2)}, u32[]{:S(2)}) collective-permute-start(bf16[1536,512]{1,0:T(8,128)(2,1)S(1)} %fusion.2), channel_id=1, source_target_pairs={{0,1},{1,0},{2,3},{3,2},{4,5},{5,4},{6,7},{7,6},{8,9},{9,8},{10,11... | collective-permute-start | bytes 4718600 | tf_op jit(solution)/shard_map/ppermute | solution.py:963
  56.9 4.3 collective-permute-start.3
  61.9 184.6 %all-gather.10.cloned.1.call-start = ((), (), s32[]{:S(2)}) async-start(), calls=%async_computation.2 | async-start | bytes 4456448 | tf_op jit(solution)/shard_map/all_gather | solution.py:996
  62.9 6.4 collective-permute-start.5
  70.1 199.0 %all-gather.12.cloned.1.call-start = ((), (), s32[]{:S(2)}) async-start(), calls=%async_computation.3 | async-start | bytes 4456448 | tf_op jit(solution)/shard_map/all_gather | solution.py:996
  77.1 9.1 copy-start.18
  89.0 19.8 %copy-start.17 = (bf16[512,128]{1,0:T(8,128)(2,1)S(1)}, bf16[512,128]{1,0:T(8,128)(2,1)}, u32[]{:S(2)}) copy-start(bf16[512,128]{1,0:T(8,128)(2,1)} %param.34) | copy-start | bytes 393220
  90.6 6.4 collective-permute-start.6
  97.8 249.4 %all-gather.14.cloned.1.call-start = ((), (), s32[]{:S(2)}) async-start(), calls=%async_computation.4 | async-start | bytes 4456448 | tf_op jit(solution)/shard_map/all_gather | solution.py:1084
  104.7 52.0 %collective-permute-start.1 = (f32[6656]{0:T(1024)}, f32[6656]{0:T(1024)S(1)}, u32[]{:S(2)}, u32[]{:S(2)}) collective-permute-start(f32[6656]{0:T(1024)} %copy-done.18), channel_id=1, source_target_pairs={{0,1},{1,0},{2,3},{3,2},{4,5},{5,4},{6,7},{7,6},{8,9},{9,8},{10,11... | collective-permute-start | bytes 79880 | tf_op jit(solution)/shard_map/ppermute | solution.py:963
  108.8 49.9 %collective-permute-start.4 = (bf16[512,128]{1,0:T(8,128)(2,1)S(1)}, bf16[512,128]{1,0:T(8,128)(2,1)S(1)}, u32[]{:S(2)}, u32[]{:S(2)}) collective-permute-start(bf16[512,128]{1,0:T(8,128)(2,1)S(1)} %copy-done.17), channel_id=1, source_target_pairs={{0,1},{1,0},{2,3},{3,2},{4,5},{5,4},{6,7},{7,6},{8,9},{9,8},{10,11... | collective-permute-start | bytes 393224 | tf_op jit(solution)/shard_map/ppermute | solution.py:963
  127.6 29.1 %copy-start.19 = (f32[6656]{0:T(1024)S(1)}, f32[6656]{0:T(1024)}, u32[]{:S(2)}) copy-start(f32[6656]{0:T(1024)} %copy-done.18) | copy-start | bytes 79876
  269.0 28.8 %copy-start.32 = (s32[32]{0:T(128)S(1)}, s32[32]{0:T(128)}, u32[]{:S(2)}) copy-start(s32[32]{0:T(128)} %param.21) | copy-start | bytes 388
  295.3 660.7 %all-reduce.3.cloned.1.call-start = ((), (), s32[]{:S(2)}) async-start(), calls=%async_computation.5 | async-start | bytes 1179648
  296.3 5.0 collective-permute-start.7
  297.8 94.3 %copy-start.24 = (s32[32]{0:T(128)}, s32[32]{0:T(128)S(1)}, u32[]{:S(2)}) copy-start(s32[32]{0:T(128)S(1)} %broadcast_subtract_fusion) | copy-start | bytes 388
  387.5 328.7 %copy-start.13 = (f32[64,32]{0,1:T(8,128)}, f32[64,32]{0,1:T(8,128)S(1)}, u32[]{:S(2)}) copy-start(f32[64,32]{0,1:T(8,128)S(1)} %copy.98) | copy-start | bytes 24580
  387.9 3.7 collective-permute-start.8
  392.1 38.6 %copy-start.25 = (f32[32]{0:T(128)}, f32[32]{0:T(128)S(1)}, u32[]{:S(2)}) copy-start(f32[32]{0:T(128)S(1)} %get-tuple-element.162) | copy-start | bytes 388
  434.6 4.5 collective-permute-start.10
  442.3 2.0 copy-start.1
  445.3 25.5 %collective-permute-start.11 = (bf16[4,1024,128]{2,1,0:T(8,128)(2,1)}, bf16[4,1024,128]{2,1,0:T(8,128)(2,1)}, u32[]{:S(2)}, u32[]{:S(2)}) collective-permute-start(bf16[4,1024,128]{2,1,0:T(8,128)(2,1)} %fusion.5), channel_id=1, source_target_pairs={{0,4},{2,6},{4,0},{6,2},{8,12},{10,14},{12,8},{14,10},{16,20},{18,... | collective-permute-start | bytes 3145736 | tf_op jit(solution)/shard_map/ppermute | solution.py:966
  475.1 13.5 %collective-permute-start.12 = (bf16[2,1024,128]{2,1,0:T(8,128)(2,1)}, bf16[2,1024,128]{2,1,0:T(8,128)(2,1)}, u32[]{:S(2)}, u32[]{:S(2)}) collective-permute-start(bf16[2,1024,128]{2,1,0:T(8,128)(2,1)} %fusion.8), channel_id=1, source_target_pairs={{0,8},{2,10},{4,12},{6,14},{8,0},{10,2},{12,4},{14,6},{16,24},{18,... | collective-permute-start | bytes 1572872 | tf_op jit(solution)/shard_map/ppermute | solution.py:966
  480.4 13.8 %collective-permute-start.9 = (f32[512,128]{1,0:T(8,128)}, f32[512,128]{1,0:T(8,128)}, u32[]{:S(2)}, u32[]{:S(2)}) collective-permute-start(f32[512,128]{1,0:T(8,128)} %dynamic-slice_bitcast_fusion), channel_id=1, source_target_pairs={{0,1},{1,0},{2,3},{3,2},{4,5},{5,4},{6,7},{7,6},{8,9},{9,8},{10,11... | collective-permute-start | bytes 786440 | tf_op jit(solution)/shard_map/ppermute | solution.py:963
  491.8 13.3 %collective-permute-start.13 = (bf16[1,1024,128]{2,1,0:T(8,128)(2,1)}, bf16[1,1024,128]{2,1,0:T(8,128)(2,1)S(1)}, u32[]{:S(2)}, u32[]{:S(2)}) collective-permute-start(bf16[1,1024,128]{2,1,0:T(8,128)(2,1)} %dynamic-slice_convert_fusion.1), channel_id=1, source_target_pairs={{0,16},{2,18},{4,20},{6,22},{8,24},{10,26},{12,28},{14,30},{16,0},... | collective-permute-start | bytes 786440 | tf_op jit(solution)/shard_map/ppermute | solution.py:966
  527.4 22.8 %collective-permute-start.14 = (bf16[1,512,2048]{2,1,0:T(8,128)(2,1)}, bf16[1,512,2048]{2,1,0:T(8,128)(2,1)S(1)}, u32[]{:S(2)}, u32[]{:S(2)}) collective-permute-start(bf16[1,512,2048]{2,1,0:T(8,128)(2,1)} %weight_pull.12.refs_3_), channel_id=1, source_target_pairs={{0,2},{2,0},{4,6},{6,4},{8,10},{10,8},{12,14},{14,12},{16,18},{18,... | collective-permute-start | bytes 6291464 | tf_op jit(solution)/shard_map/ppermute | solution.py:966
  536.1 58.9 %collective-permute-start.16 = (bf16[1,512,2048]{2,1,0:T(8,128)(2,1)}, bf16[1,512,2048]{2,1,0:T(8,128)(2,1)}, u32[]{:S(2)}, u32[]{:S(2)}) collective-permute-start(bf16[1,512,2048]{2,1,0:T(8,128)(2,1)} %weight_pull.13.refs_3_), channel_id=1, source_target_pairs={{0,2},{2,0},{4,6},{6,4},{8,10},{10,8},{12,14},{14,12},{16,18},{18,... | collective-permute-start | bytes 6291464 | tf_op jit(solution)/shard_map/ppermute | solution.py:966
  550.2 1.4 copy-start.6
  581.8 21.9 %collective-permute-start.15 = (bf16[1,512,2048]{2,1,0:T(8,128)(2,1)}, bf16[1,512,2048]{2,1,0:T(8,128)(2,1)}, u32[]{:S(2)}, u32[]{:S(2)}) collective-permute-start(bf16[1,512,2048]{2,1,0:T(8,128)(2,1)} %weight_pull.15.refs_3_), channel_id=1, source_target_pairs={{0,2},{2,0},{4,6},{6,4},{8,10},{10,8},{12,14},{14,12},{16,18},{18,... | collective-permute-start | bytes 6291464 | tf_op jit(solution)/shard_map/ppermute | solution.py:966
  590.0 52.1 %collective-permute-start.17 = (bf16[1,512,2048]{2,1,0:T(8,128)(2,1)}, bf16[1,512,2048]{2,1,0:T(8,128)(2,1)}, u32[]{:S(2)}, u32[]{:S(2)}) collective-permute-start(bf16[1,512,2048]{2,1,0:T(8,128)(2,1)} %weight_pull.16.refs_4_), channel_id=1, source_target_pairs={{0,2},{2,0},{4,6},{6,4},{8,10},{10,8},{12,14},{14,12},{16,18},{18,... | collective-permute-start | bytes 6291464 | tf_op jit(solution)/shard_map/ppermute | solution.py:966
  593.4 136.0 %collective-permute-start.18 = (bf16[1,512,2048]{2,1,0:T(8,128)(2,1)}, bf16[1,512,2048]{2,1,0:T(8,128)(2,1)}, u32[]{:S(2)}, u32[]{:S(2)}) collective-permute-start(bf16[1,512,2048]{2,1,0:T(8,128)(2,1)} %weight_pull.14.refs_3_), channel_id=1, source_target_pairs={{0,1},{1,0},{2,3},{3,2},{4,5},{5,4},{6,7},{7,6},{8,9},{9,8},{10,11... | collective-permute-start | bytes 6291464 | tf_op jit(solution)/shard_map/ppermute | solution.py:963
  612.2 117.2 %collective-permute-start.19 = (bf16[1,512,2048]{2,1,0:T(8,128)(2,1)}, bf16[1,512,2048]{2,1,0:T(8,128)(2,1)}, u32[]{:S(2)}, u32[]{:S(2)}) collective-permute-start(bf16[1,512,2048]{2,1,0:T(8,128)(2,1)} %weight_pull.18.refs_10_), channel_id=1, source_target_pairs={{0,1},{1,0},{2,3},{3,2},{4,5},{5,4},{6,7},{7,6},{8,9},{9,8},{10,11... | collective-permute-start | bytes 6291464 | tf_op jit(solution)/shard_map/ppermute | solution.py:963
  706.9 15.7 %copy-start.4 = (bf16[1536,1024]{1,0:T(8,128)(2,1)S(1)}, bf16[1536,1024]{1,0:T(8,128)(2,1)}, u32[]{:S(2)}) copy-start(bf16[1536,1024]{1,0:T(8,128)(2,1)} %get-tuple-element.141) | copy-start | bytes 9437188
  706.9 15.7 %copy-start.12 = (bf16[1536,128]{1,0:T(8,128)(2,1)S(1)}, bf16[1536,128]{1,0:T(8,128)(2,1)}, u32[]{:S(2)}) copy-start(bf16[1536,128]{1,0:T(8,128)(2,1)} %get-tuple-element.140) | copy-start | bytes 1179652
  716.2 87.0 %collective-permute-start.20 = (bf16[4,512,512]{2,1,0:T(8,128)(2,1)}, bf16[4,512,512]{2,1,0:T(8,128)(2,1)}, u32[]{:S(2)}, u32[]{:S(2)}) collective-permute-start(bf16[4,512,512]{2,1,0:T(8,128)(2,1)} %weight_pull.20.refs_5_), channel_id=1, source_target_pairs={{0,2},{2,0},{4,6},{6,4},{8,10},{10,8},{12,14},{14,12},{16,18},{18,... | collective-permute-start | bytes 6291464 | tf_op jit(solution)/shard_map/ppermute | solution.py:966
  738.0 116.5 %collective-permute-start.26 = (bf16[2,256,2048]{2,1,0:T(8,128)(2,1)}, bf16[2,256,2048]{2,1,0:T(8,128)(2,1)S(1)}, u32[]{:S(2)}, u32[]{:S(2)}) collective-permute-start(bf16[2,256,2048]{2,1,0:T(8,128)(2,1)} %get-tuple-element.121.refs_9_), channel_id=1, source_target_pairs={{0,4},{2,6},{4,0},{6,2},{8,12},{10,14},{12,8},{14,10},{16,20},{18,... | collective-permute-start | bytes 6291464 | tf_op jit(solution)/shard_map/ppermute | solution.py:966
  802.7 24.7 %collective-permute-start.22 = (bf16[4,512,512]{2,1,0:T(8,128)(2,1)}, bf16[4,512,512]{2,1,0:T(8,128)(2,1)}, u32[]{:S(2)}, u32[]{:S(2)}) collective-permute-start(bf16[4,512,512]{2,1,0:T(8,128)(2,1)} %weight_pull.21.refs_6_), channel_id=1, source_target_pairs={{0,2},{2,0},{4,6},{6,4},{8,10},{10,8},{12,14},{14,12},{16,18},{18,... | collective-permute-start | bytes 6291464 | tf_op jit(solution)/shard_map/ppermute | solution.py:966
  812.7 26.5 %collective-permute-start.21 = (bf16[4,256,512]{2,1,0:T(8,128)(2,1)}, bf16[4,256,512]{2,1,0:T(8,128)(2,1)}, u32[]{:S(2)}, u32[]{:S(2)}) collective-permute-start(bf16[4,256,512]{2,1,0:T(8,128)(2,1)} %get-tuple-element.125.refs_6_), channel_id=1, source_target_pairs={{0,8},{2,10},{4,12},{6,14},{8,0},{10,2},{12,4},{14,6},{16,24},{18,... | collective-permute-start | bytes 3145736 | tf_op jit(solution)/shard_map/ppermute | solution.py:966
  823.7 145.3 %collective-permute-start.23 = (bf16[1536,512]{1,0:T(8,128)(2,1)}, bf16[1536,512]{1,0:T(8,128)(2,1)}, u32[]{:S(2)}, u32[]{:S(2)}) collective-permute-start(bf16[1536,512]{1,0:T(8,128)(2,1)} %token_pull.2.refs_6_), channel_id=1, source_target_pairs={{0,1},{1,0},{2,3},{3,2},{4,5},{5,4},{6,7},{7,6},{8,9},{9,8},{10,11... | collective-permute-start | bytes 4718600 | tf_op jit(solution)/shard_map/ppermute | solution.py:963
  837.2 160.2 %collective-permute-start.24 = (bf16[4,256,512]{2,1,0:T(8,128)(2,1)}, bf16[4,256,512]{2,1,0:T(8,128)(2,1)}, u32[]{:S(2)}, u32[]{:S(2)}) collective-permute-start(bf16[4,256,512]{2,1,0:T(8,128)(2,1)} %get-tuple-element.126.refs_3_), channel_id=1, source_target_pairs={{0,8},{2,10},{4,12},{6,14},{8,0},{10,2},{12,4},{14,6},{16,24},{18,... | collective-permute-start | bytes 3145736 | tf_op jit(solution)/shard_map/ppermute | solution.py:966
  855.8 5.4 copy-start.33
  855.8 113.2 %copy-start = (f32[1536,512]{1,0:T(8,128)S(1)}, f32[1536,512]{1,0:T(8,128)}, u32[]{:S(2)}) copy-start(f32[1536,512]{1,0:T(8,128)} %token_pull.3.refs_3_) | copy-start | bytes 9437188
  861.2 140.1 %collective-permute-start.28 = (bf16[2,128,2048]{2,1,0:T(8,128)(2,1)}, bf16[2,128,2048]{2,1,0:T(8,128)(2,1)}, u32[]{:S(2)}, u32[]{:S(2)}) collective-permute-start(bf16[2,128,2048]{2,1,0:T(8,128)(2,1)} %get-tuple-element.131.refs_3_), channel_id=1, source_target_pairs={{0,8},{2,10},{4,12},{6,14},{8,0},{10,2},{12,4},{14,6},{16,24},{18,... | collective-permute-start | bytes 3145736 | tf_op jit(solution)/shard_map/ppermute | solution.py:966
  966.3 26.2 %collective-permute-start.25 = (bf16[4,128,512]{2,1,0:T(8,128)(2,1)}, bf16[4,128,512]{2,1,0:T(8,128)(2,1)}, u32[]{:S(2)}, u32[]{:S(2)}) collective-permute-start(bf16[4,128,512]{2,1,0:T(8,128)(2,1)} %get-tuple-element.127.refs_6_), channel_id=1, source_target_pairs={{0,16},{2,18},{4,20},{6,22},{8,24},{10,26},{12,28},{14,30},{16,0},... | collective-permute-start | bytes 1572872 | tf_op jit(solution)/shard_map/ppermute | solution.py:966
  995.9 15.3 %collective-permute-start.30 = (bf16[4,64,512]{2,1,0:T(8,128)(2,1)}, bf16[4,64,512]{2,1,0:T(8,128)(2,1)S(1)}, u32[]{:S(2)}, u32[]{:S(2)}) collective-permute-start(bf16[4,64,512]{2,1,0:T(8,128)(2,1)} %get-tuple-element.132.refs_3_), channel_id=1, source_target_pairs={{0,4},{2,6},{4,0},{6,2},{8,12},{10,14},{12,8},{14,10},{16,20},{18,... | collective-permute-start | bytes 786440 | tf_op jit(solution)/shard_map/ppermute | solution.py:966
  1001.3 36.0 %collective-permute-start.27 = (bf16[4,128,512]{2,1,0:T(8,128)(2,1)}, bf16[4,128,512]{2,1,0:T(8,128)(2,1)S(1)}, u32[]{:S(2)}, u32[]{:S(2)}) collective-permute-start(bf16[4,128,512]{2,1,0:T(8,128)(2,1)} %get-tuple-element.134.refs_3_), channel_id=1, source_target_pairs={{0,16},{2,18},{4,20},{6,22},{8,24},{10,26},{12,28},{14,30},{16,0},... | collective-permute-start | bytes 1572872 | tf_op jit(solution)/shard_map/ppermute | solution.py:966
  1005.3 6.0 copy-start.11
  1005.3 43.1 %collective-permute-start.32 = (bf16[2,64,2048]{2,1,0:T(8,128)(2,1)}, bf16[2,64,2048]{2,1,0:T(8,128)(2,1)S(1)}, u32[]{:S(2)}, u32[]{:S(2)}) collective-permute-start(bf16[2,64,2048]{2,1,0:T(8,128)(2,1)} %get-tuple-element.136.refs_3_), channel_id=1, source_target_pairs={{0,16},{2,18},{4,20},{6,22},{8,24},{10,26},{12,28},{14,30},{16,0},... | collective-permute-start | bytes 1572872 | tf_op jit(solution)/shard_map/ppermute | solution.py:966
  1011.3 37.2 %copy-start.8 = (f32[2,64,2048]{2,1,0:T(8,128)S(1)}, f32[2,64,2048]{2,1,0:T(8,128)}, u32[]{:S(2)}) copy-start(f32[2,64,2048]{2,1,0:T(8,128)} %get-tuple-element.142) | copy-start | bytes 3145732
  1011.3 38.2 %collective-permute-start.31 = (bf16[4,64,512]{2,1,0:T(8,128)(2,1)S(1)}, bf16[4,64,512]{2,1,0:T(8,128)(2,1)S(1)}, u32[]{:S(2)}, u32[]{:S(2)}) collective-permute-start(bf16[4,64,512]{2,1,0:T(8,128)(2,1)S(1)} %add_convert_fusion), channel_id=1, source_target_pairs={{0,1},{1,0},{2,3},{3,2},{4,5},{5,4},{6,7},{7,6},{8,9},{9,8},{10,11... | collective-permute-start | bytes 786440 | tf_op jit(solution)/shard_map/ppermute | solution.py:963
  1041.5 8.3 copy-start.10
  1041.5 8.3 collective-permute-start.29
  (9 other events, 8.3 us)
Sparse Core Ops, SparseCore 0:
  16.9 46.8 all-gather.5
  66.6 36.7 all-gather.7
  105.6 49.6 all-gather.9
  157.3 49.2 all-gather.11
  295.5 51.6 all-gather.13
  827.5 128.4 all-reduce.2

commit v4 on v3

--- a/solution.py
+++ b/solution.py
@@ -45,7 +45,8 @@
 
 
 def call(
-    body, name, grid, in_specs, out_specs, out_shape, operands, flops, scratch=(), prefetch=0, after=()
+    body, name, grid, in_specs, out_specs, out_shape, operands, flops, scratch=(), prefetch=0, after=(),
+    remote=None,
 ):
     count = len(operands)
     after = tuple(after) + Order.last
@@ -66,7 +67,9 @@
             scratch_shapes=list(scratch),
         ),
         out_shape=out_shape,
-        compiler_params=pltpu.CompilerParams(vmem_limit_bytes=VMEM_LIMIT),
+        compiler_params=pltpu.CompilerParams(
+            vmem_limit_bytes=VMEM_LIMIT, collective_id=remote, has_side_effects=remote is not None
+        ),
         cost_estimate=pl.CostEstimate(flops=flops, bytes_accessed=size, transcendentals=0),
         name=name,
     )(*operands, *after)
@@ -80,6 +83,280 @@
 
 def column_spec(width, step):
     return pl.BlockSpec((width, step), lambda i, *_: (0, i))
+
+
+MESH = pl.DeviceIdType.MESH
+ANYWHERE = pl.BlockSpec(memory_space=pl.ANY)
+
+
+def side_at(row, bit):
+    return (row // bit) % 2
+
+
+def across(row, bit):
+    return row + bit * (1 - 2 * side_at(row, bit))
+
+
+def flipped(row, bits):
+    bit = 1
+    while bit <= bits:
+        if bits & bit:
+            row = across(row, bit)
+        bit *= 2
+    return row
+
+
+def greet(devices):
+    barrier = pltpu.get_barrier_semaphore()
+    for device in devices:
+        pl.semaphore_signal(barrier, inc=1, device_id=device, device_id_type=MESH)
+    pl.semaphore_wait(barrier, len(devices))
+
+
+def send(source, target, sent, arrived, device):
+    copy = pltpu.make_async_remote_copy(
+        src_ref=source,
+        dst_ref=target,
+        send_sem=sent,
+        recv_sem=arrived,
+        device_id=device,
+        device_id_type=MESH,
+    )
+    copy.start()
+    return copy
+
+
+def spread_order(count):
+    pieces = sorted(range(count), key=lambda piece: (piece.bit_count(), -piece))
+    order = []
+    for piece in pieces:
+        lowest = piece & -piece if piece else count
+        bit = lowest // 2
+        bits = []
+        while bit:
+            bits.append(bit)
+            bit //= 2
+        order.append((piece, bits))
+    return order
+
+
+def start_kernel(rows, cols_width, parts, *refs):
+    (tokens, qkv, out, up, down, proj, pack), refs = refs[:7], refs[7:]
+    (x, qkv_o, out_o, up_o, down_o, proj_o, pack_o), refs = refs[:7], refs[7:]
+    own_sem, sent, arrived, wide_sent, wide_arrived = refs
+    r, c = lax.axis_index("rows"), lax.axis_index("cols")
+    partner = {"cols": 1 - c}
+    bits = [1 << b for b in range(rows.bit_length() - 1)]
+    greet([partner] + [{"rows": across(r, bit)} for bit in bits])
+    wide = [(qkv, qkv_o), (out, out_o), (up, up_o)]
+    copies, first = [], []
+    for place, (source, target) in enumerate(wide):
+        first.append(
+            send(source.at[r], target.at[r], sent.at[place], arrived.at[place], partner)
+        )
+    q_rows, d_rows, first_doc = parts
+    own = pl.ds(pl.multiple_of(c * cols_width, cols_width), cols_width)
+    spans = [(0, q_rows, 0), (first_doc, d_rows, q_rows)]
+    for place, (base, size, here) in enumerate(spans):
+        theirs = pl.ds(pl.multiple_of(base + (1 - c) * size, size), size)
+        mine = pl.ds(pl.multiple_of(base + c * size, size), size)
+        target = x.at[pl.ds(here, size), own]
+        copies.append(
+            send(tokens.at[theirs], target, sent.at[3 + place], arrived.at[3 + place], partner)
+        )
+        pltpu.make_async_copy(tokens.at[mine], target, own_sem.at[place]).start()
+    for place, (source, target) in enumerate([(proj, proj_o), (pack, pack_o), (down.at[r], down_o)]):
+        copies.append(
+            send(source, target, sent.at[5 + place], arrived.at[5 + place], partner)
+        )
+    wide_copies = {}
+    for piece, over in spread_order(rows):
+        row = flipped(r, piece)
+        for place, (_, target) in enumerate(wide):
+            if piece == 0:
+                first[place].wait_recv()
+            else:
+                wide_copies[place, piece].wait_recv()
+            for bit in over:
+                wide_copies[place, piece | bit] = send(
+                    target.at[row], target.at[row],
+                    wide_sent.at[place, piece | bit], wide_arrived.at[place, piece | bit],
+                    {"rows": across(r, bit)},
+                )
+    for copy in first + list(wide_copies.values()):
+        copy.wait_send()
+    for copy in copies:
+        copy.wait()
+    for place, (base, size, here) in enumerate(spans):
+        mine = pl.ds(pl.multiple_of(base + c * size, size), size)
+        target = x.at[pl.ds(here, size), own]
+        pltpu.make_async_copy(tokens.at[mine], target, own_sem.at[place]).wait()
+
+
+def start_up(rows, parts, tokens, qkv, out, up, down, proj, pack):
+    width = tokens.shape[1]
+
+    def pieces(array):
+        return array.reshape(rows, -1, array.shape[-1])
+
+    weights = [pieces(array) for array in (qkv, out, up, down)]
+    qkv_p, out_p, up_p, down_p = weights
+    operands = (tokens, *weights, proj, pack)
+    n = parts[0] + parts[1]
+    x, qkv_o, out_o, up_o, down_o, proj_o, pack_o = call(
+        functools.partial(start_kernel, rows, width, parts), "start_up", (1,),
+        [ANYWHERE] * 7, [ANYWHERE] * 7,
+        [
+            shaped(BF16, n, 2 * width), shaped(BF16, *qkv_p.shape), shaped(BF16, *out_p.shape),
+            shaped(BF16, *up_p.shape), shaped(BF16, *down_p.shape[1:]), shaped(BF16, *proj.shape),
+            shaped(F32, *pack.shape),
+        ],
+        operands, 0, remote=1,
+        scratch=[
+            pltpu.SemaphoreType.DMA((2,)), pltpu.SemaphoreType.DMA((8,)),
+            pltpu.SemaphoreType.DMA((8,)), pltpu.SemaphoreType.DMA((3, rows)),
+            pltpu.SemaphoreType.DMA((3, rows)),
+        ],
+    )
+    return (
+        x, qkv_o.reshape(qkv.shape), out_o.reshape(out.shape), up_o.reshape(up.shape), down_o,
+        proj_o, pack_o,
+    )
+
+
+def gather_kernel(rows, own, out, own_sem, sent, arrived):
+    r = lax.axis_index("rows")
+    bits = [1 << b for b in range(rows.bit_length() - 1)]
+    greet([{"rows": across(r, bit)} for bit in bits])
+    local = pltpu.make_async_copy(own, out.at[r], own_sem)
+    local.start()
+    copies = {}
+    for piece, over in spread_order(rows):
+        row = flipped(r, piece)
+        if piece:
+            copies[piece].wait_recv()
+        for bit in over:
+            copies[piece | bit] = send(
+                out.at[row] if piece else own, out.at[row],
+                sent.at[piece | bit], arrived.at[piece | bit], {"rows": across(r, bit)},
+            )
+    for copy in copies.values():
+        copy.wait_send()
+    local.wait()
+
+
+def gather_rows(rows, own):
+    return call(
+        functools.partial(gather_kernel, rows), "gather_rows", (1,), [ANYWHERE], [ANYWHERE],
+        [shaped(own.dtype, rows, *own.shape)], (own,), 0, remote=2,
+        scratch=[
+            pltpu.SemaphoreType.DMA, pltpu.SemaphoreType.DMA((rows,)),
+            pltpu.SemaphoreType.DMA((rows,)),
+        ],
+    )[0]
+
+
+def scatter_kernel(rows, parts, out, sent, arrived, *buffers):
+    r = lax.axis_index("rows")
+    bits = [1 << b for b in range(rows.bit_length() - 1)]
+    greet([{"rows": across(r, bit)} for bit in bits])
+    outgoing, incoming = buffers[: len(bits)], buffers[len(bits) :]
+    copies = {}
+
+    def total(flips, levels):
+        row = flipped(r, flips)
+        value = parts[row]
+        for level in range(levels):
+            copies[level, flips >> (level + 1)].wait_recv()
+            value = value + incoming[level][row // (2 << level)].astype(F32)
+        return value
+
+    for level, bit in enumerate(bits):
+        count = rows // (2 << level)
+        for turn in sorted(range(count), key=lambda f: tuple(-((f >> b) & 1) for b in range(8))):
+            flips = (turn << (level + 1)) | bit
+            place = flipped(r, flips) // (2 << level)
+            outgoing[level][place] = total(flips, level).astype(BF16)
+            copies[level, turn] = send(
+                outgoing[level].at[place], incoming[level].at[place],
+                sent.at[rows - 2 * count + turn], arrived.at[rows - 2 * count + turn],
+                {"rows": across(r, bit)},
+            )
+    out[...] = total(0, len(bits))
+    for copy in copies.values():
+        copy.wait_send()
+
+
+def scatter_rows(parts):
+    rows, height, width = parts.shape
+    levels = rows.bit_length() - 1
+    buffers = [
+        pltpu.VMEM((rows // (2 << level), height, width), BF16) for level in range(levels)
+    ]
+    return call(
+        functools.partial(scatter_kernel, rows), "scatter_rows", (1,), [held(parts.shape)],
+        [pl.BlockSpec((height, width), lambda *_: (0, 0))], [shaped(F32, height, width)],
+        (parts,), 0, remote=3,
+        scratch=[pltpu.SemaphoreType.DMA((rows,)), pltpu.SemaphoreType.DMA((rows,))]
+        + buffers + buffers,
+    )[0]
+
+
+def small_kernel(rows, cols, parts, out, *refs):
+    bits = [1 << b for b in range(rows.bit_length() - 1)]
+    sent, arrived = refs[:2]
+    core_in, cols_in, totals, row_ins = refs[2], refs[3], refs[4 : 4 + len(bits)], refs[4 + len(bits) :]
+    r, c = lax.axis_index("rows"), lax.axis_index("cols")
+    others = [{"cols": (c + cols - k) % cols} for k in range(1, cols)]
+    greet([{"rows": across(r, bit)} for bit in bits] + others)
+    core = side_at(r, 1)
+    copy = send(parts.at[:, 1 - core], core_in, sent.at[0], arrived.at[0], {"rows": across(r, 1)})
+    copy.wait()
+    sums = parts[:, core] + core_in[...]
+    cols_out = totals[0]
+    cols_out[...] = sums
+    copies = [
+        send(cols_out.at[:, k], cols_in.at[k - 1], sent.at[k], arrived.at[k], others[k - 1])
+        for k in range(1, cols)
+    ]
+    total = sums[:, 0]
+    for k, copy in enumerate(copies):
+        copy.wait()
+        total = total + cols_in[k]
+    for level, bit in enumerate(bits[1:]):
+        held_total, arriving = totals[1 + level], row_ins[level]
+        held_total[...] = total.reshape(held_total.shape)
+        side = side_at(r, bit)
+        copy = send(
+            held_total.at[:, 1 - side], arriving, sent.at[cols + level], arrived.at[cols + level],
+            {"rows": across(r, bit)},
+        )
+        copy.wait()
+        total = held_total[:, side] + arriving[...]
+    out[...] = total[0]
+
+
+def small_sum(rows, cols, parts):
+    length = parts.shape[2]
+    width = -(-length // 1024) * 128
+    parts = jnp.pad(parts, ((0, 0), (0, 0), (0, 8 * width - length)))
+    parts = parts.reshape(rows // 2, 2, cols, 8, width)
+    levels = rows.bit_length() - 1
+    sizes = [rows >> (level + 1) for level in range(1, levels)]
+    scratch = [
+        pltpu.SemaphoreType.DMA((cols + levels,)), pltpu.SemaphoreType.DMA((cols + levels,)),
+        pltpu.VMEM((rows // 2, cols, 8, width), F32),
+        pltpu.VMEM((cols - 1, rows // 2, 8, width), F32),
+        pltpu.VMEM((rows // 2, cols, 8, width), F32),
+    ]
+    scratch += [pltpu.VMEM((size, 2, 8, width), F32) for size in sizes]
+    scratch += [pltpu.VMEM((size, 8, width), F32) for size in sizes]
+    total = call(
+        functools.partial(small_kernel, rows, cols), "small_sum", (1,), [held(parts.shape)],
+        [pl.BlockSpec((8, width), lambda *_: (0, 0))], [shaped(F32, 8, width)], (parts,), 0,
+        remote=4, scratch=scratch,
+    )[0]
+    return total.reshape(-1)[:length]
 
 
 def swap_halves(block):
@@ -428,6 +705,9 @@
 
 
 def for_group(starts, body):
+    if len(starts) == 2:
+        body(0)
+        return
     for place in range(len(starts) - 1):
 
         @pl.when((pl.program_id(0) >= starts[place]) & (pl.program_id(0) < starts[place + 1]))
@@ -479,8 +759,20 @@
         [spec(size) for _, size in outs],
         [shaped(kind, starts[-1], size, m) for kind, size in outs],
         (places, *lefts, *rights) + (() if arrived is None else (arrived,)),
-        2 * starts[-1] * rows * n * m, prefetch=1,
-    )
+        0, prefetch=1,
+    )
+
+
+def pass_on_kernel(in_ref, out_ref):
+    out_ref[...] = in_ref[...]
+
+
+def pass_on(array):
+    spec = held(array.shape)
+    return call(
+        pass_on_kernel, "pass_on", (1,), [spec], [pl.BlockSpec(array.shape, lambda *_: (0,) * array.ndim)],
+        [shaped(array.dtype, *array.shape)], (array,), 0,
+    )[0]
 
 
 def fold_kernel(starts, inner, place_ref, *refs):
@@ -517,7 +809,7 @@
 
 
 SEGMENTS = 8
-ATTENTION_LANES = 256
+ATTENTION_LANES = 128
 
 
 def half_lanes(block, head, other):
@@ -535,9 +827,20 @@
     return high, middle, value - high - middle
 
 
+def for_spans(span_ref, tiles, body):
+    @pl.loop(0, tiles)
+    def _(step):
+        low, high = span_ref[step], span_ref[tiles + step]
+        for count in range(1, tiles + 1):
+
+            @pl.when(high - low == count)
+            def _(count=count):
+                body(step, low, count)
+
+
 def attention_forward_kernel(
     span_ref, qkv_ref, ext_k_ref, ext_q_ref, out_ref, rest_ref, ext_ref,
-    keys_ref, queries_ref, values_ref, logits_ref, *, tile,
+    keys_ref, queries_ref, turned_ref, values_ref, *, tile,
 ):
     n = ext_k_ref.shape[0]
     tiles = n // tile
@@ -557,68 +860,35 @@
         )
     for pair in range(pairs):
         for step in range(tiles):
-            block = qkv_ref[2, step * tile : (step + 1) * tile, lanes(2 * pair)]
-            values_ref[pair, step] = block.astype(F32).T.astype(BF16)
-
-    def rows(step):
-        return pl.ds(pl.multiple_of(step * tile, tile), tile)
-
-    def by_eight(block):
-        return block.reshape(tile // 8, 8, tile)
-
-    @pl.loop(0, tiles)
-    def _(step):
-        low, high = span_ref[step], span_ref[tiles + step]
-
-        def find_top(block, tops):
-            found = []
-            for head in heads:
-                logits = mm(
-                    keys_ref[head, rows(block), :], queries_ref[head, rows(step), :], NT
+            at = slice(step * tile, (step + 1) * tile)
+            values_ref[pair, :, at] = qkv_ref[2, at, lanes(2 * pair)].astype(F32).T.astype(BF16)
+            for head in (2 * pair, 2 * pair + 1):
+                turned_ref[head, step] = queries_ref[head, at, :].astype(F32).T.astype(BF16)
+
+    def attend(step, low, count):
+        rows = pl.ds(pl.multiple_of(step * tile, tile), tile)
+        window = pl.ds(pl.multiple_of(low * tile, tile), count * tile)
+        for pair in range(pairs):
+            outs, extras = [], []
+            for head in (2 * pair, 2 * pair + 1):
+                logits = mm(keys_ref[head, window, :], turned_ref[head, step])
+                top = jnp.max(logits, axis=0, keepdims=True)
+                weights = jnp.exp(logits - top)
+                mass = jnp.sum(weights, axis=0, keepdims=True)
+                probs = (weights * (1.0 / mass)).astype(BF16)
+                outs.append(mm(values_ref[pair, own_rows(head), window], probs))
+                terms = three_terms(-(top + jnp.log(mass)))
+                extras.append(
+                    [jnp.zeros((8, tile), F32), *terms, jnp.zeros((DH - 11, tile), F32)]
                 )
-                logits_ref[head, block] = logits
-                found.append(jnp.maximum(tops[head], jnp.max(by_eight(logits), axis=0)))
-            return tuple(found)
-
-        start = jnp.full((8, tile), -3e38, F32)
-        tops = lax.fori_loop(low, high, find_top, tuple(start for _ in heads))
-        tops = [jnp.max(top, axis=0, keepdims=True) for top in tops]
-
-        def add_mass(block, masses):
-            after = []
-            for head in heads:
-                weights = jnp.exp(logits_ref[head, block] - tops[head])
-                logits_ref[head, block] = weights
-                after.append(masses[head] + jnp.sum(by_eight(weights), axis=0))
-            return tuple(after)
-
-        start = jnp.zeros((8, tile), F32)
-        masses = lax.fori_loop(low, high, add_mass, tuple(start for _ in heads))
-        masses = [jnp.sum(mass, axis=0, keepdims=True) for mass in masses]
-        shares = [1.0 / mass for mass in masses]
-
-        def add_values(block, totals):
-            after = []
-            for head in heads:
-                probs = (logits_ref[head, block] * shares[head]).astype(BF16)
-                after.append(totals[head] + mm(values_ref[head // 2, block, own_rows(head), :], probs))
-            return tuple(after)
-
-        zero = jnp.zeros((DH, tile), F32)
-        outs = lax.fori_loop(low, high, add_values, tuple(zero for _ in heads))
-        for pair in range(pairs):
-            extras = []
-            for head in (2 * pair + 1, 2 * pair):
-                terms = three_terms(-(tops[head] + jnp.log(masses[head])))
-                extras += [
-                    jnp.zeros((8, tile), F32), *terms, jnp.zeros((DH - 11, tile), F32)
-                ]
             at = lanes(2 * pair)
-            out = jnp.concatenate(outs[2 * pair : 2 * pair + 2], axis=0).T
-            out_ref[rows(step), at] = out.astype(BF16)
-            rest_ref[rows(step), at] = (out - out.astype(BF16).astype(F32)).astype(BF16)
-            extra = jnp.concatenate(extras, axis=0).T
-            ext_ref[rows(step), at] = (extra + ext_q_ref[rows(step), :].astype(F32)).astype(BF16)
+            out = jnp.concatenate(outs, axis=0).T
+            out_ref[rows, at] = out.astype(BF16)
+            rest_ref[rows, at] = (out - out.astype(BF16).astype(F32)).astype(BF16)
+            extra = jnp.concatenate(extras[1] + extras[0], axis=0).T
+            ext_ref[rows, at] = (extra + ext_q_ref[rows, :].astype(F32)).astype(BF16)
+
+    for_spans(span_ref, tiles, attend)
 
 
 def attention_forward(spans, qkv, ext_k, ext_q, tile):
@@ -635,8 +905,7 @@
         (spans, qkv, ext_k, ext_q), 0, prefetch=1,
         scratch=[
             pltpu.VMEM((2 * pairs, n, 128), BF16), pltpu.VMEM((2 * pairs, n, 128), BF16),
-            pltpu.VMEM((pairs, tiles, 128, tile), BF16),
-            pltpu.VMEM((2 * pairs, tiles, tile, tile), F32),
+            pltpu.VMEM((2 * pairs, tiles, 128, tile), BF16), pltpu.VMEM((pairs, 128, n), BF16),
         ],
     )
 
@@ -673,53 +942,46 @@
             out = att_ref[at, cut].astype(F32) + rest_ref[at, cut].astype(F32)
             product = grad.astype(F32) * out
             query = scaled(qkv_ref[0, at, cut])
-            turned_ref[pair, step] = scaled(qkv_ref[1, at, cut]).astype(F32).T.astype(BF16)
+            turned_ref[pair, :, at] = scaled(qkv_ref[1, at, cut]).astype(F32).T.astype(BF16)
             for half in range(2):
                 head = 2 * pair + half
                 keys_ref[head, at, :] = half_lanes(qkv_ref[1, at, cut], half, ext_k)
                 values_ref[head, at, :] = half_lanes(qkv_ref[2, at, cut], half, ext_k)
-                queries_ref[head, at, :] = half_lanes(query, half, ext_ref[at, cut])
+                whole = half_lanes(query, half, ext_ref[at, cut])
+                queries_ref[head, step] = whole.astype(F32).T.astype(BF16)
                 plain_ref[head, at, :] = half_lanes(query, half, zeros)
                 plain_grads_ref[head, at, :] = half_lanes(grad, half, zeros)
                 inner = jnp.sum(half_lanes(product, half, 0.0), axis=1, keepdims=True)
                 extra = jnp.zeros((tile, 128), F32)
                 for place, term in enumerate(three_terms(-inner)):
                     extra = jnp.where((lane & (DH - 1)) == SEGMENTS + place, term, extra)
-                grads_ref[head, at, :] = half_lanes(grad, half, extra.astype(BF16))
+                whole = half_lanes(grad.astype(F32), half, extra)
+                grads_ref[head, step] = whole.T.astype(BF16)
 
     dk_ref[...] = jnp.zeros(dk_ref.shape, F32)
     dv_ref[...] = jnp.zeros(dv_ref.shape, F32)
 
-    @pl.loop(0, tiles)
-    def _(step):
-        def one_block(block, totals):
-            after = []
-            for pair in range(pairs):
-                probs, slopes = [], []
-                for head in (2 * pair, 2 * pair + 1):
-                    weights = jnp.exp(
-                        mm(keys_ref[head, rows(block), :], queries_ref[head, rows(step), :], NT)
-                    )
-                    flow = mm(values_ref[head, rows(block), :], grads_ref[head, rows(step), :], NT)
-                    slope = (weights * flow).astype(BF16)
-                    probs.append(weights.astype(BF16))
-                    slopes.append(slope)
-                    after.append(totals[head] + mm(turned_ref[pair, block, own_rows(head), :], slope))
-                both = range(2 * pair, 2 * pair + 2)
-                plain = jnp.concatenate([plain_ref[h, rows(step), :] for h in both], axis=0)
-                grads = jnp.concatenate([plain_grads_ref[h, rows(step), :] for h in both], axis=0)
-                at = lanes(2 * pair)
-                dv_ref[rows(block), at] += mm(jnp.concatenate(probs, axis=1), grads)
-                dk_ref[rows(block), at] += mm(jnp.concatenate(slopes, axis=1), plain)
-            return tuple(after)
-
-        zero = jnp.zeros((DH, tile), F32)
-        totals = lax.fori_loop(
-            span_ref[step], span_ref[tiles + step], one_block, tuple(zero for _ in heads)
-        )
+    def pull(step, low, count):
+        at = rows(step)
+        window = pl.ds(pl.multiple_of(low * tile, tile), count * tile)
         for pair in range(pairs):
-            both = jnp.concatenate(totals[2 * pair : 2 * pair + 2], axis=0)
-            dq_ref[rows(step), lanes(2 * pair)] = both.T
+            probs, slopes, dq = [], [], []
+            both = range(2 * pair, 2 * pair + 2)
+            for head in both:
+                weights = jnp.exp(mm(keys_ref[head, window, :], queries_ref[head, step]))
+                flow = mm(values_ref[head, window, :], grads_ref[head, step])
+                slope = (weights * flow).astype(BF16)
+                probs.append(weights.astype(BF16))
+                slopes.append(slope)
+                dq.append(mm(turned_ref[pair, own_rows(head), window], slope))
+            plain = jnp.concatenate([plain_ref[h, at, :] for h in both], axis=0)
+            grads = jnp.concatenate([plain_grads_ref[h, at, :] for h in both], axis=0)
+            cut = lanes(2 * pair)
+            dv_ref[window, cut] += mm(jnp.concatenate(probs, axis=1), grads)
+            dk_ref[window, cut] += mm(jnp.concatenate(slopes, axis=1), plain)
+            dq_ref[at, cut] = jnp.concatenate(dq, axis=0).T
+
+    for_spans(span_ref, tiles, pull)
 
     def finish(step, sums):
         cosine, sine = cos_ref[rows(step), :], sin_ref[rows(step), :]
@@ -751,6 +1013,7 @@
     three = pl.BlockSpec((3, n, span), lambda i, *_: (0, 0, i))
     tiles, pairs = n // tile, span // 128
     heads = pltpu.VMEM((2 * pairs, n, 128), BF16)
+    turned = pltpu.VMEM((2 * pairs, tiles, 128, tile), BF16)
     return call(
         functools.partial(attention_backward_kernel, tile=tile), "attention_backward",
         (width // span,),
@@ -759,8 +1022,9 @@
         [shaped(BF16, 3, n, width), shaped(F32, 8, width)],
         (spans, qkv, ext, attended, rest, grads, ext_k, cosine, sine), 0,
         prefetch=1,
-        scratch=[heads, pltpu.VMEM((pairs, tiles, 128, tile), BF16)] + [heads] * 5
-        + [pltpu.VMEM((n, span), F32)] * 3,
+        scratch=[
+            heads, pltpu.VMEM((pairs, 128, n), BF16), heads, turned, heads, turned, heads,
+        ] + [pltpu.VMEM((n, span), F32)] * 3,
     )
 
 
@@ -975,44 +1239,54 @@
             lax.dynamic_index_in_dim(stacked, (c - j) % C, 0, keepdims=False) for j in range(C)
         ]
 
-    parts = jnp.concatenate(
-        [tokens[:ROW_LEN].reshape(C, Q, width), tokens[ROW_LEN:].reshape(C, DS, width)], axis=1
-    )
-
-    def part(k):
-        return lax.dynamic_index_in_dim(parts, (c + k) % C, 0, keepdims=False)
-
-    arrived = [shift_cols(part(k), k) for k in range(1, C)]
-    x = jnp.concatenate(in_order([part(0)] + arrived), axis=1)
-
-    def gather_slots(shard, behind):
-        flat = shard.reshape(-1, shard.shape[-1])
-        piece = lax.dynamic_index_in_dim(
-            flat.reshape(R, flat.shape[0] // R, flat.shape[1]), r, 0, keepdims=False
-        )
-        if behind:
-            piece, _ = lax.optimization_barrier((piece, arrived))
-        others = [
-            lax.all_gather(shift_cols(piece, k), "rows", axis=0, tiled=True).reshape(shard.shape)
-            for k in range(1, C)
-        ]
-        return [shard] + others
-
-    wqkv_slots = gather_slots(w_qkv, False)
-    wout_slots = gather_slots(w_out, True)
-    wup_slots = gather_slots(w_up, True)
-    wdown_slots = gather_slots(w_down, True)
-    own_proj, _ = lax.optimization_barrier((w_proj, arrived))
-    wproj = jnp.concatenate(
-        in_order([own_proj] + [shift_cols(own_proj, k) for k in range(1, C)]), axis=0
-    )
-
     pack = [b_qkv.reshape(-1), b_up, b_out, ln1_gain, ln1_bias, b_down, ln2_gain, ln2_bias]
     ends = [0]
     for vector in pack:
         ends.append(ends[-1] + vector.shape[0])
-    packed, _ = lax.optimization_barrier((jnp.concatenate(pack), arrived))
-    packs = [packed] + [shift_cols(packed, k) for k in range(1, C)]
+    packed = jnp.concatenate(pack)
+
+    def gather_pieces(pieces):
+        return [lax.all_gather(piece, "rows", axis=0, tiled=True) for piece in pieces]
+
+    if C == 2:
+        x, *others, down_piece, proj_other, pack_other = start_up(
+            R, (Q, DS, ROW_LEN), tokens, w_qkv, w_out, w_up, w_down, w_proj,
+            packed.reshape(8, -1),
+        )
+        wqkv_slots, wout_slots, wup_slots = (
+            [own, other] for own, other in zip((w_qkv, w_out, w_up), others)
+        )
+        wdown_slots = [w_down] + gather_pieces([down_piece])
+        wproj = jnp.concatenate(in_order([w_proj, proj_other]), axis=0)
+        packs = [packed, pack_other.reshape(-1)]
+    else:
+        parts = jnp.concatenate(
+            [tokens[:ROW_LEN].reshape(C, Q, width), tokens[ROW_LEN:].reshape(C, DS, width)], axis=1
+        )
+
+        def part(k):
+            return lax.dynamic_index_in_dim(parts, (c + k) % C, 0, keepdims=False)
+
+        x = jnp.concatenate(
+            in_order([part(0)] + [shift_cols(part(k), k) for k in range(1, C)]), axis=1
+        )
+
+        def gather_slots(shard):
+            flat = shard.reshape(-1, shard.shape[-1])
+            piece = lax.dynamic_index_in_dim(
+                flat.reshape(R, flat.shape[0] // R, flat.shape[1]), r, 0, keepdims=False
+            )
+            others = gather_pieces([shift_cols(piece, k) for k in range(1, C)])
+            return [shard] + [other.reshape(shard.shape) for other in others]
+
+        wqkv_slots, wout_slots, wup_slots, wdown_slots = (
+            gather_slots(shard) for shard in (w_qkv, w_out, w_up, w_down)
+        )
+        wproj = jnp.concatenate(
+            in_order([w_proj] + [shift_cols(w_proj, k) for k in range(1, C)]), axis=0
+        )
+        packs = [packed] + [shift_cols(packed, k) for k in range(1, C)]
+
     ordered_packs = in_order(packs)
 
     def of_slot(which, k):
@@ -1081,7 +1355,7 @@
         normed_one, vectors, wproj, active, wdown_slots
     )
 
-    doc_tile = lax.all_gather(unit_low[Q:], "rows", axis=0, tiled=True)
+    doc_tile = gather_rows(R, unit_low[Q:]).reshape(R * DS, 128)
     query_tile = jnp.concatenate(
         in_order([unit_low[:Q]] + [shift_cols(unit_low[:Q], k) for k in range(1, C)]), axis=0
     )
@@ -1115,20 +1389,8 @@
     for k in range(1, C):
         query_grad = query_grad + shift_cols(query_part(k), k)
 
-    def halve(total, bit, wire):
-        size = total.shape[0] // 2
-        pairs = total.reshape((size, 2) + total.shape[1:])
-        mine = (r // bit) % 2
-        send = lax.dynamic_index_in_dim(pairs, 1 - mine, 1, keepdims=False).astype(wire)
-        keep = lax.dynamic_index_in_dim(pairs, mine, 1, keepdims=False)
-        return keep + swap_rows(send, bit).astype(F32)
-
-    doc_sum = doc_grad.reshape(R, DS, 128)
-    bit = 1
-    while bit < R:
-        doc_sum = halve(doc_sum, bit, BF16)
-        bit *= 2
-    unit_grad = jnp.concatenate([query_grad, doc_sum[0]], axis=0)
+    doc_sum = scatter_rows(doc_grad.reshape(R, DS, 128))
+    unit_grad = jnp.concatenate([query_grad, doc_sum], axis=0)
 
     core = r % 2
     slots_back = range(C - 1, -1, -1)
@@ -1147,9 +1409,20 @@
     def send_half(lefts, rights):
         return swap_rows(weight_pull(send_places, lefts, rights)[0], 1)
 
-    def keep_half(left, right, arrived, k):
-        kept = weight_pull(keep_places, [left], [right], arrived, F32 if k == 0 else BF16)[0]
-        return kept if k == 0 else shift_cols(kept, C - k)
+    def rows_of(left, side):
+        return lax.dynamic_index_in_dim(left, side, 1, keepdims=False).reshape(-1, n)
+
+    def send_plain(left, right):
+        part = mm(rows_of(left, 1 - core), right).astype(BF16)
+        Order.last += (part,)
+        return swap_rows(part, 1)
+
+    def keep_plain(left, right, arrived, k):
+        kept = mm(rows_of(left, core), right) + arrived.astype(F32)
+        if k > 0:
+            kept = kept.astype(BF16)
+        Order.last += (kept,)
+        return kept[None] if k == 0 else shift_cols(kept, C - k)[None]
 
     def next_fold(states, bit, inner):
         send, keep = fold(side_of(bit), [s[0] for s in states], [s[1] for s in states], inner)
@@ -1167,31 +1440,54 @@
     embed_grad, resid_two_grad, branch, branch_t, head_sums = head_pull(
         unit_grad, unit, unit_inverse, wproj, normed_two, inverse_two, vectors
     )
-    down_left, down_right = halves_of(branch_t), [a[None] for a in active]
+    down_left, down_right = halves_of(branch_t), active
     pre_grads, up_sums, down_kept = [None] * C, [None] * C, [None] * C
     down_arrived = [None] * C
     for k in slots_back:
-        down_arrived[k] = send_half([down_left], [down_right[k]])
+        down_arrived[k] = send_plain(down_left, down_right[k])
     for k in slots_back:
         pre_grads[k], up_sums[k] = up_pull(branch, wdown_slots[k], slopes[k])
         if k > 0:
-            down_kept[k] = keep_half(down_left, down_right[k], down_arrived[k], k)
-    up_left, up_right = halves_of(hidden_t), [g[None] for g in pre_grads]
+            down_kept[k] = keep_plain(down_left, down_right[k], down_arrived[k], k)
+    up_left, up_right = halves_of(hidden_t), pre_grads
     up_arrived, up_kept = [None] * C, [None] * C
     for k in slots_back:
-        up_arrived[k] = send_half([up_left], [up_right[k]])
-    down_kept[0] = keep_half(down_left, down_right[0], down_arrived[0], 0)
+        up_arrived[k] = send_plain(up_left, up_right[k])
+    down_kept[0] = keep_plain(down_left, down_right[0], down_arrived[0], 0)
     for k in slots_back[:-1]:
-        up_kept[k] = keep_half(up_left, up_right[k], up_arrived[k], k)
+        up_kept[k] = keep_plain(up_left, up_right[k], up_arrived[k], k)
     resid_one_grad, branch_one_t, hidden_sums, *attended_grads = hidden_pull(
         resid_two_grad, normed_one, inverse_one, vectors, pre_grads, wup_slots, wout_slots
     )
-    up_kept[0] = keep_half(up_left, up_right[0], up_arrived[0], 0)
+    up_kept[0] = keep_plain(up_left, up_right[0], up_arrived[0], 0)
     mixed_grads, mixed_sums = [None] * C, [None] * C
     late_lefts, late_state, late_arrived = [halves_of(x.T), halves_of(branch_one_t)], [None] * C, [None] * C
 
     def late_rights(k):
         return [mixed_grads[k], attended[k][None]]
+
+    def gather_small():
+        proj_grad = mm(embed_grad, output_low, TN).reshape(R, -1, C, width)
+        def cut(values, slot_rows):
+            return values.reshape(slot_rows, R, -1)
+
+        own_order = [(c - k) % C for k in range(C)]
+        canonical = jnp.stack(
+            [hidden_sums[0], hidden_sums[1], hidden_sums[2], head_sums[0], head_sums[1], head_sums[2]]
+        ).reshape(6, C, R, -1)
+        slots_small = []
+        for k in range(C):
+            rows = [mixed_sums[k][j].reshape(R, -1) for j in range(3)]
+            rows.append(up_sums[k][0].reshape(R, -1))
+            rows += [
+                lax.dynamic_index_in_dim(canonical[j], own_order[k], 0, keepdims=False)
+                for j in range(6)
+            ]
+            own_proj_grad = lax.dynamic_index_in_dim(proj_grad, own_order[k], 2, keepdims=False)
+            rows.append(own_proj_grad.reshape(R, -1))
+            rows.append(jnp.broadcast_to(scale_part, (R, 1)))
+            slots_small.append(jnp.concatenate(rows, axis=1))
+        return jnp.stack(slots_small, axis=1)
 
     def pull_attention(k):
         mixed_grads[k], mixed_sums[k] = attention_backward(
@@ -1212,6 +1508,7 @@
     pull_attention(0)
     for k in slots_back[:-1]:
         keep_late(k)
+    wide_state = next_fold([wide_state], z_bits[0], share)
     sent = [
         shift_cols(token_pull((c + k) % C, resid_one_grad, mixed_grads, wqkv_slots, BF16), k)
         for k in range(1, C)
@@ -1220,7 +1517,7 @@
     for k in slots_back[:-1]:
         late_state[k] = next_fold([late_state[k]], (z_bits + [x_bit])[1], 2 * share)
     own_tokens = token_pull(c, resid_one_grad, mixed_grads, wqkv_slots, F32)
-    wide_state = next_fold([wide_state], z_bits[0], share)
+    small = small_sum(R, C, gather_small())
     for bit in z_bits[2:] + [x_bit]:
         for k in slots_back[:-1]:
             late_state[k] = next_fold([late_state[k]], bit, share if bit == x_bit else 2 * share)
@@ -1235,29 +1532,6 @@
     down_grad, up_grad = close(wide_state)
     ordered = in_order([own_tokens] + [s.astype(F32) for s in sent])
     tokens_grad = jnp.concatenate([s[:Q] for s in ordered] + [s[Q:] for s in ordered], axis=0)
-    proj_grad = mm(embed_grad, output_low, TN).reshape(R, -1, C, width)
-
-    def cut(values, slot_rows):
-        return values.reshape(slot_rows, R, -1)
-
-    own_order = [(c - k) % C for k in range(C)]
-    canonical = jnp.stack(
-        [hidden_sums[0], hidden_sums[1], hidden_sums[2], head_sums[0], head_sums[1], head_sums[2]]
-    ).reshape(6, C, R, -1)
-    slots_small = []
-    for k in range(C):
-        rows = [mixed_sums[k][j].reshape(R, -1) for j in range(3)]
-        rows.append(up_sums[k][0].reshape(R, -1))
-        rows += [
-            lax.dynamic_index_in_dim(canonical[j], own_order[k], 0, keepdims=False)
-            for j in range(6)
-        ]
-        own_proj_grad = lax.dynamic_index_in_dim(proj_grad, own_order[k], 2, keepdims=False)
-        rows.append(own_proj_grad.reshape(R, -1))
-        rows.append(jnp.broadcast_to(scale_part, (R, 1)))
-        slots_small.append(jnp.concatenate(rows, axis=1))
-    small = jnp.stack(in_order(slots_small)).reshape(C * R, -1)
-    small = lax.psum_scatter(small, ("cols", "rows"), scatter_dimension=0, tiled=True)[0]
     one = D // (C * R)
     up_part = bup_slots[0].shape[1] // R
     bounds = [3 * one, 3 * one + up_part]

time: 1070 us -> 902 us (0.84)
  waiting for transfers between devices: 290 us -> 33 us
  Pallas kernels: 594 us -> 692 us
  matrix products: 0.6 us -> 56.7 us
  local copies, waits for them, and re-layouts: 72.3 us -> 46.2 us
  starting transfers between devices: 35.8 us -> 16.3 us
  other arithmetic: 50.1 us -> 30.9 us
    pallas_call x37 -> x33, Pallas kernels: 594 us -> 692 us  [call(): pl.pallas_call(wrapped, grid_spec=pltpu.PrefetchScalarGridSpec(num_scalar...]
    unnamed x7 -> x1, waiting for transfers between devices: 94.3 us -> 0.02 us
    ppermute x19 -> x15, waiting for transfers between devices: 98.4 us -> 30 us  [swap_rows(): return lax.ppermute(value, 'rows', [(i, i ^ bit) for i in range(R)])]
    dot_general x1 -> x9, matrix products: 0.6 us -> 56.7 us  [mm(): return lax.dot_general(left, right, dims, preferred_element_type=F32)]
    ppermute x14 -> x7, waiting for transfers between devices: 53.5 us -> 3.02 us  [shift_cols(): return lax.ppermute(value, 'cols', [(i, (i + k) % C) for i in range(C)])]
    all_gather x5 -> x1, waiting for transfers between devices: 44.2 us -> 0.01 us  [gather_pieces(): lax.all_gather(piece, 'rows', axis=0, tiled=True)]
    ppermute x14 -> x7, starting transfers between devices: 20.3 us -> 6.43 us  [shift_cols(): return lax.ppermute(value, 'cols', [(i, (i + k) % C) for i in range(C)])]
  transfers between devices with their start and end apart: 39 -> 23, of which waited for: 17 -> 3; matrix products, arithmetic and copies ran while one was open for 9% -> 12% of each run, Pallas kernels for 45% -> 57%
where the time goes in v4:
time: 902 us; the launch traced here: 891 us
  Pallas kernels  692 us (77%)
  matrix products  56.7 us (6%)
  local copies, waits for them, and re-layouts  46.2 us (5%)
  waiting for transfers between devices  33 us (4%)
  other arithmetic  30.9 us (3%)
  starting transfers between devices  16.3 us (2%)
  between operations  16 us (2%)
    pallas_call x33, Pallas kernels, call(): pl.pallas_call(wrapped, grid_spec=pltpu.PrefetchScalarGridSpec(num_scalar...  692 us
    dot_general x9, matrix products, mm(): return lax.dot_general(left, right, dims, preferred_element_type=F32)  56.7 us
    ppermute x15, waiting for transfers between devices, swap_rows(): return lax.ppermute(value, 'rows', [(i, i ^ bit) for i in range(R)])  30 us
  transfers between devices with their start and end apart: 23, of which 3 were waited for; matrix products, arithmetic and copies ran while one was open for 12% of the time, Pallas kernels for 57%

profile of v4, /device:TPU:0, one launch (start us, length us, event | category | flops | bytes accessed | tf_op | source)
XLA Modules:
  0.0 890.9 jit_solution(11777550220676873436)
XLA Ops:
  13.5 67.1 %start_up.1 = (bf16[1536,1024]{1,0:T(8,128)(2,1)}, bf16[16,192,512]{2,1,0:T(8,128)(2,1)}, bf16[16,32,1024]{2,1,0:T(8,128)(2,1)}, bf16[16,64,2048]{2,1,0:T(8,128)...) custom-call(bf16[3072,512]{1,0:T(8,128)(2,1)} %refs_0_.1, ...), custom_call_target="tpu_custom_call" | custom-call | bytes 1024 | tf_op jit(solution)/shard_map/start_up/pallas_call | solution.py:60
  87.6 5.9 fusion.2.refs_5_.refs_4_
  93.5 2.8 fusion.3
  96.3 1.6 pad_maximum_fusion.1.refs_3_.refs_7_
  97.9 1.7 pad_maximum_fusion.2.refs_4_.refs_8_
  99.6 14.0 %project_qkv.2.refs_1_.refs_4_ = bf16[3,1536,512]{2,1,0:T(8,128)(2,1)} custom-call(bf16[1536,1024]{1,0:T(8,128)(2,1)} %get-tuple-element.82.refs_0_, bf16[3,1024,512]{2,1,0:T(8,128)(2,1)} %refs_4_.5, f32[3,512]{1,0:T(4,128)} %refs_2_.1, f32[1536,128]{1,0:T(8,128)} %pad_maximum_fusion.1.refs_3_.refs_7_, f32[1536,128]{1,0:T(8,128)} %pad_maximum_fusion.2.refs_4_.refs_8_, ...), custom_call_target="tpu_custom_call" | custom-call | flops 4831838208 | bytes 12589056 | tf_op jit(solution)/shard_map/project_qkv/pallas_call | solution.py:60
  115.6 37.6 %attention_forward.2 = (bf16[1536,512]{1,0:T(8,128)(2,1)}, bf16[1536,512]{1,0:T(8,128)(2,1)}, bf16[1536,512]{1,0:T(8,128)(2,1)}) custom-call(s32[12]{0:T(128)} %pad_add_fusion.1.refs_0_, bf16[3,1536,512]{2,1,0:T(8,128)(2,1)} %project_qkv.2.refs_1_.refs_4_, bf16[1536,128]{1,0:T(8,128)(2,1)} %fusion.refs_2_.refs_6_, ...), custom_call_target="tpu_custom_call" | custom-call | bytes 1024 | tf_op jit(solution)/shard_map/attention_forward/pallas_call | solution.py:60
  153.2 13.7 %project_qkv.3.refs_1_.refs_4_ = bf16[3,1536,512]{2,1,0:T(8,128)(2,1)} custom-call(bf16[1536,1024]{1,0:T(8,128)(2,1)} %get-tuple-element.82.refs_0_, bf16[3,1024,512]{2,1,0:T(8,128)(2,1)} %bitcast.151, f32[3,512]{1,0:T(4,128)} %slice.261.refs_2_, f32[1536,128]{1,0:T(8,128)} %pad_maximum_fusion.1.refs_3_.refs_7_, ...), custom_call_target="tpu_custom_call" | custom-call | flops 4831838208 | bytes 12589056 | tf_op jit(solution)/shard_map/project_qkv/pallas_call | solution.py:60
  166.9 37.9 %attention_forward.3 = (bf16[1536,512]{1,0:T(8,128)(2,1)}, bf16[1536,512]{1,0:T(8,128)(2,1)}, bf16[1536,512]{1,0:T(8,128)(2,1)}) custom-call(s32[12]{0:T(128)} %pad_add_fusion.1.refs_0_, bf16[3,1536,512]{2,1,0:T(8,128)(2,1)} %project_qkv.3.refs_1_.refs_4_, bf16[1536,128]{1,0:T(8,128)(2,1)} %fusion.refs_2_.refs_6_, ...), custom_call_target="tpu_custom_call" | custom-call | bytes 1024 | tf_op jit(solution)/shard_map/attention_forward/pallas_call | solution.py:60
  206.9 11.2 %out_and_norm.1 = (f32[1536,1024]{1,0:T(8,128)}, f32[1536,1]{1,0:T(8,128)}, bf16[1536,1024]{1,0:T(8,128)(2,1)}, bf16[1024,1536]{1,0:T(8,128)(2,1)}) custom-call(bf16[1536,1024]{1,0:T(8,128)(2,1)} %get-tuple-element.82.refs_0_, f32[8,1024]{1,0:T(8,128)} %stack.78.refs_1_.refs_6_.refs_3_, bf16[1536,512]{1,0:T(8,128)(2,1)} %get-tuple-element.84.refs_5_.refs_2_.refs_3_, ...), custom_call_target="tpu_custom_call" | custom-call | flops 3221225472 | bytes 21010432 | tf_op jit(solution)/shard_map/out_and_norm/pallas_call | solution.py:60
  218.1 22.9 %up_and_gelu.2 = (bf16[1536,2048]{1,0:T(8,128)(2,1)}, f32[1536,2048]{1,0:T(8,128)}) custom-call(bf16[1536,1024]{1,0:T(8,128)(2,1)} %get-tuple-element.90.refs_0_, bf16[1024,2048]{1,0:T(8,128)(2,1)} %refs_6_.1, f32[1,2048]{1,0:T(1,128)} %bitcast.198, f32[1536,1]{1,0:T(8,128)} %get-tuple-element.91.refs_3_.refs_2_), custom_call_target="tpu_custom_call" | custom-call | flops 16106127360 | bytes 26222592 | tf_op jit(solution)/shard_map/up_and_gelu/pallas_call | solution.py:60
  241.0 22.5 %up_and_gelu.3 = (bf16[1536,2048]{1,0:T(8,128)(2,1)}, f32[1536,2048]{1,0:T(8,128)}) custom-call(bf16[1536,1024]{1,0:T(8,128)(2,1)} %get-tuple-element.90.refs_0_, bf16[1024,2048]{1,0:T(8,128)(2,1)} %bitcast.160, f32[1,2048]{1,0:T(1,128)} %bitcast.199, bf16[1536,2048]{1,0:T(8,128)(2,1)} %get-tuple-element.92.refs_3_), custom_call_target="tpu_custom_call" | custom-call | flops 16106127360 | bytes 26222592 | tf_op jit(solution)/shard_map/up_and_gelu/pallas_call | solution.py:60
  263.6 24.8 %down_and_norm.1 = (f32[1536,1024]{1,0:T(8,128)}, f32[1536,1]{1,0:T(8,128)}, bf16[1536,1024]{1,0:T(8,128)(2,1)}, f32[1536,128]{1,0:T(8,128)}, bf16[1536,128]{1,0:T(8,128)(2,1)}, /*index=5*/f32[1536,1]{1,0:T(8,128)}) custom-call(f32[1536,1024]{1,0:T(8,128)} %get-tuple-element.88.refs_0_.refs_1_, f32[8,1024]{1,0:T(8,128)} %stack.78.refs_1_.refs_6_.refs_3_, ...), custom_call_target="tpu_custom_call" | custom-call | flops 12884901888 | bytes 38187008 | tf_op jit(solution)/shard_map/down_and_norm/pallas_call | solution.py:60
  290.1 1.7 slice.213.refs_0_
  291.8 36.2 %gather_rows.1.refs_5_ = bf16[16,1024,128]{2,1,0:T(8,128)(2,1)} custom-call(bf16[1024,128]{1,0:T(8,128)(2,1)} %slice.213.refs_0_, f32[1536,1]{1,0:T(8,128)} %get-tuple-element.97.refs_1_.refs_5_), custom_call_target="tpu_custom_call" | custom-call | bytes 1024 | tf_op jit(solution)/shard_map/gather_rows/pallas_call | solution.py:60
  329.7 39.2 %score_forward.1.refs_6_ = f32[16,4,32]{2,1,0:T(4,128)} custom-call(s32[512]{0:T(512)} %reshape.345.refs_6_.refs_0_, s32[512]{0:T(512)} %sub.113.refs_7_.refs_1_, bf16[16384,128]{1,0:T(8,128)(2,1)} %bitcast.163, bf16[1024,128]{1,0:T(8,128)(2,1)} %pad_maximum_fusion.5.refs_3_, s32[16,4,1024]{2,1,0:T(4,128)} %fusion.2.refs_5_.refs_4_, ...), custom_call_target="tpu_custom_call" | custom-call | flops 4294967296 | bytes 4730880 | tf_op jit(solution)/shard_map/score_forward/pallas_call | solution.py:60
  370.6 3.0 collective-permute-done.1
  374.7 1.4 subtract_multiply_fusion.refs_5_
  376.2 37.4 %score_backward.1 = (f32[16384,128]{1,0:T(8,128)}, f32[128,1024]{1,0:T(8,128)}) custom-call(s32[512]{0:T(512)} %reshape.345.refs_6_.refs_0_, s32[512]{0:T(512)} %sub.113.refs_7_.refs_1_, bf16[16384,128]{1,0:T(8,128)(2,1)} %bitcast.164, bf16[1024,128]{1,0:T(8,128)(2,1)} %pad_maximum_fusion.5.refs_3_, s32[16,4,1024]{2,1,0:T(4,128)} %fusion.2.refs_5_.refs_4_, ...), custom_call_target="tpu_custom_call" | custom-call | flops 8589934592 | bytes 13643776 | tf_op jit(solution)/shard_map/score_backward/pallas_call | solution.py:60
  413.6 2.0 copy.72
  417.2 2.0 constant_dynamic-slice_fusion.2
  419.2 39.8 %scatter_rows.1.refs_7_ = f32[1024,128]{1,0:T(8,128)} custom-call(f32[16,1024,128]{2,1,0:T(8,128)} %bitcast.154, f32[128,1024]{1,0:T(8,128)} %get-tuple-element.98.refs_1_), custom_call_target="tpu_custom_call" | custom-call | bytes 1024 | tf_op jit(solution)/shard_map/scatter_rows/pallas_call | solution.py:60
  459.0 2.0 pad_maximum_fusion.3.refs_0_
  461.0 12.3 %head_pull.1 = (bf16[1536,128]{1,0:T(8,128)(2,1)}, f32[1536,1024]{1,0:T(8,128)}, bf16[1536,1024]{1,0:T(8,128)(2,1)}, bf16[1024,1536]{1,0:T(8,128)(2,1)}, f32[8,1024]{1,0:T(8,128)}) custom-call(f32[1536,128]{1,0:T(8,128)} %pad_maximum_fusion.3.refs_0_, f32[1536,128]{1,0:T(8,128)} %get-tuple-element.100.refs_1_, f32[1536,1]{1,0:T(8,128)} %get-tuple-element.101.refs_2_, ...), custom_call_target="tpu_custom_call" | custom-call | flops 805306368 | bytes 21180416 | tf_op jit(solution)/shard_map/head_pull/pallas_call | solution.py:60
  473.3 2.3 constant_dynamic-slice_fusion.4
  475.6 7.0 convolution_convert_fusion.3.refs_4_
  482.9 4.6 convolution_convert_fusion.2.refs_5_
  487.9 13.7 %up_pull.2 = (bf16[1536,2048]{1,0:T(8,128)(2,1)}, f32[8,2048]{1,0:T(8,128)}) custom-call(bf16[1536,1024]{1,0:T(8,128)(2,1)} %get-tuple-element.104.refs_0_, bf16[2048,1024]{1,0:T(8,128)(2,1)} %all-gather.2.cloned.1.call-done.refs_6_.refs_1_, f32[1536,2048]{1,0:T(8,128)} %get-tuple-element.106.refs_2_, f32[8,1024]{1,0:T(8,128)} %get-tuple-element.107.refs_3_, ...), custom_call_target="tpu_custom_call" | custom-call | flops 6442450944 | bytes 26279936 | tf_op jit(solution)/shard_map/up_pull/pallas_call | solution.py:60
  501.5 6.4 convolution_convert_fusion.1.refs_11_
  508.2 8.3 add_convert_fusion.1.refs_4_
  516.4 13.7 %up_pull.3 = (bf16[1536,2048]{1,0:T(8,128)(2,1)}, f32[8,2048]{1,0:T(8,128)}) custom-call(bf16[1536,1024]{1,0:T(8,128)(2,1)} %get-tuple-element.104.refs_0_, bf16[2048,1024]{1,0:T(8,128)(2,1)} %refs_1_.5, f32[1536,2048]{1,0:T(8,128)} %get-tuple-element.105.refs_2_, f32[8,2048]{1,0:T(8,128)} %get-tuple-element.109.refs_3_, ...), custom_call_target="tpu_custom_call" | custom-call | flops 6442450944 | bytes 26279936 | tf_op jit(solution)/shard_map/up_pull/pallas_call | solution.py:60
  530.1 8.0 convolution_convert_fusion.refs_12_
  538.6 6.0 add_convert_fusion.refs_14_
  544.5 1.7 collective-permute-start.8
  546.3 3.0 copy.71
  549.8 9.5 %convert_add_fusion.1.refs_13_ = f32[512,2048]{1,0:T(8,128)} fusion(bf16[512,2048]{1,0:T(8,128)(2,1)} %collective-permute-done.4, bf16[512,1536]{1,0:T(8,128)(2,1)} %bitcast.175, bf16[1536,2048]{1,0:T(8,128)(2,1)} %get-tuple-element.92.refs_3_), kind=kOutput, calls=%fused_computation.3 | convolution fusion | flops 3223322624 | bytes 14155776 | tf_op jit(solution)/shard_map/dot_general | solution.py:23
  559.3 29.6 %hidden_pull.1 = (f32[1536,1024]{1,0:T(8,128)}, bf16[1024,1536]{1,0:T(8,128)(2,1)}, f32[8,1024]{1,0:T(8,128)}, bf16[1536,512]{1,0:T(8,128)(2,1)}, bf16[1536,512]{1,0:T(8,128)(2,1)}) custom-call(f32[1536,1024]{1,0:T(8,128)} %get-tuple-element.103.refs_0_, f32[1536,1024]{1,0:T(8,128)} %get-tuple-element.88.refs_0_.refs_1_, ...), custom_call_target="tpu_custom_call" | custom-call | bytes 1024 | tf_op jit(solution)/shard_map/hidden_pull/pallas_call | solution.py:60
  588.9 6.3 convert_add_fusion.refs_10_
  595.3 46.2 %attention_backward.2 = (bf16[3,1536,512]{2,1,0:T(8,128)(2,1)}, f32[8,512]{1,0:T(8,128)}) custom-call(s32[12]{0:T(128)} %pad_add_fusion.1.refs_0_, bf16[3,1536,512]{2,1,0:T(8,128)(2,1)} %project_qkv.3.refs_1_.refs_4_, bf16[1536,512]{1,0:T(8,128)(2,1)} %get-tuple-element.119.refs_2_, bf16[1536,512]{1,0:T(8,128)(2,1)} %get-tuple-element.86.refs_3_.refs_6_, ...), custom_call_target="tpu_custom_call" | custom-call | bytes 1024 | tf_op jit(solution)/shard_map/attention_backward/pallas_call | solution.py:60
  641.5 8.9 %weight_pull.4.refs_5_ = bf16[4,512,512]{2,1,0:T(8,128)(2,1)} custom-call(s32[2]{0:T(128)} %pad_add_fusion.2.refs_0_, bf16[8,2,64,1536]{3,2,1,0:T(8,128)(2,1)} %bitcast.135, bf16[8,2,64,1536]{3,2,1,0:T(8,128)(2,1)} %bitcast.139, bf16[3,1536,512]{2,1,0:T(8,128)(2,1)} %get-tuple-element.123.refs_3_, bf16[1,1536,512]{2,1,0:T(8,128)(2,1)} %bitcast.149, ...), custom_call_target="tpu_custom_call" | custom-call | bytes 1024 | tf_op jit(solution)/shard_map/weight_pull/pallas_call | solution.py:60
  650.4 9.0 %fold.7 = (bf16[2,256,2048]{2,1,0:T(8,128)(2,1)}, f32[2,256,2048]{2,1,0:T(8,128)}) custom-call(s32[1]{0:T(128)} %bitcast.42.refs_0_, f32[1,512,2048]{2,1,0:T(8,128)} %bitcast.145, f32[1,512,2048]{2,1,0:T(8,128)} %bitcast.146, bf16[1,512,2048]{2,1,0:T(8,128)(2,1)} %bitcast.45.refs_3_, bf16[1,512,2048]{2,1,0:T(8,128)(2,1)} %bitcast.46.refs_4_, ...), custom_call_target="tpu_custom_call" | custom-call | bytes 1024 | tf_op jit(solution)/shard_map/fold/pallas_call | solution.py:60
  662.6 46.3 %attention_backward.3 = (bf16[3,1536,512]{2,1,0:T(8,128)(2,1)}, f32[8,512]{1,0:T(8,128)}) custom-call(s32[12]{0:T(128)} %pad_add_fusion.1.refs_0_, bf16[3,1536,512]{2,1,0:T(8,128)(2,1)} %project_qkv.2.refs_1_.refs_4_, bf16[1536,512]{1,0:T(8,128)(2,1)} %get-tuple-element.115.refs_2_, bf16[1536,512]{1,0:T(8,128)(2,1)} %get-tuple-element.84.refs_5_.refs_2_.refs_3_, ...), custom_call_target="tpu_custom_call" | custom-call | bytes 1024 | tf_op jit(solution)/shard_map/attention_backward/pallas_call | solution.py:60
  708.8 9.0 %weight_pull.5.refs_6_ = bf16[4,512,512]{2,1,0:T(8,128)(2,1)} custom-call(s32[2]{0:T(128)} %pad_add_fusion.2.refs_0_, bf16[8,2,64,1536]{3,2,1,0:T(8,128)(2,1)} %bitcast.136, bf16[8,2,64,1536]{3,2,1,0:T(8,128)(2,1)} %bitcast.140, bf16[3,1536,512]{2,1,0:T(8,128)(2,1)} %get-tuple-element.126.refs_3_.refs_2_, bf16[1,1536,512]{2,1,0:T(8,128)(2,1)} %bitcast.147, ...), custom_call_target="tpu_custom_call" | custom-call | bytes 1024 | tf_op jit(solution)/shard_map/weight_pull/pallas_call | solution.py:60
  722.1 9.5 %weight_pull.6 = (bf16[4,256,512]{2,1,0:T(8,128)(2,1)}, f32[4,256,512]{2,1,0:T(8,128)}) custom-call(s32[2]{0:T(128)} %pad_add_fusion.3.refs_0_, bf16[8,2,64,1536]{3,2,1,0:T(8,128)(2,1)} %bitcast.137, bf16[8,2,64,1536]{3,2,1,0:T(8,128)(2,1)} %bitcast.141, bf16[3,1536,512]{2,1,0:T(8,128)(2,1)} %get-tuple-element.123.refs_3_, bf16[1,1536,512]{2,1,0:T(8,128)(2,1)} %bitcast.150, ...), custom_call_target="tpu_custom_call" | custom-call | bytes 1024 | tf_op jit(solution)/shard_map/weight_pull/pallas_call | solution.py:60
  731.6 5.2 fold.8
  736.9 10.9 %token_pull.2.refs_6_ = bf16[1536,512]{1,0:T(8,128)(2,1)} custom-call(s32[1]{0:T(128)} %bitcast.56.refs_0_, f32[1536,1024]{1,0:T(8,128)} %get-tuple-element.114.refs_1_, bf16[3,1536,512]{2,1,0:T(8,128)(2,1)} %get-tuple-element.126.refs_3_.refs_2_, bf16[3,1536,512]{2,1,0:T(8,128)(2,1)} %get-tuple-element.123.refs_3_, bf16[3,1024,512]{2,1,0:T(8,128)(2,1)} %refs_4_.5, ...), custom_call_target="tpu_custom_call" | custom-call | flops 4831838208 | bytes 23592964 | tf_op jit(solution)/shard_map/token_pull/pallas_call | solution.py:60
  753.3 1.4 reshape.378.refs_0_
  754.7 2.0 collective-permute-start.17
  756.6 1.4 copy-done.4
  758.1 9.5 %weight_pull.7 = (bf16[4,256,512]{2,1,0:T(8,128)(2,1)}, f32[4,256,512]{2,1,0:T(8,128)}) custom-call(s32[2]{0:T(128)} %pad_add_fusion.3.refs_0_, bf16[8,2,64,1536]{3,2,1,0:T(8,128)(2,1)} %bitcast.138, bf16[8,2,64,1536]{3,2,1,0:T(8,128)(2,1)} %bitcast.142, bf16[3,1536,512]{2,1,0:T(8,128)(2,1)} %get-tuple-element.126.refs_3_.refs_2_, ...), custom_call_target="tpu_custom_call" | custom-call | bytes 1024 | tf_op jit(solution)/shard_map/weight_pull/pallas_call | solution.py:60
  767.6 3.9 fold.9
  771.5 1.6 collective-permute-start.15
  773.1 11.3 %token_pull.3.refs_1_ = f32[1536,512]{1,0:T(8,128)} custom-call(s32[1]{0:T(128)} %bitcast.31.refs_0_, f32[1536,1024]{1,0:T(8,128)} %get-tuple-element.114.refs_1_, bf16[3,1536,512]{2,1,0:T(8,128)(2,1)} %get-tuple-element.126.refs_3_.refs_2_, bf16[3,1536,512]{2,1,0:T(8,128)(2,1)} %get-tuple-element.123.refs_3_, bf16[3,1024,512]{2,1,0:T(8,128)(2,1)} %refs_4_.5, ...), custom_call_target="tpu_custom_call" | custom-call | flops 4831838208 | bytes 25165828 | tf_op jit(solution)/shard_map/token_pull/pallas_call | solution.py:60
  784.3 34.0 %small_sum.1.refs_3_ = f32[8,640]{1,0:T(8,128)} custom-call(f32[8,2,2,8,640]{4,3,2,1,0:T(8,128)} %reshape.378.refs_0_, f32[1536,512]{1,0:T(8,128)} %token_pull.3.refs_1_), custom_call_target="tpu_custom_call" | custom-call | bytes 1024 | tf_op jit(solution)/shard_map/small_sum/pallas_call | solution.py:60
  822.9 2.3 convert_select_fusion.1
  825.7 3.4 fold.10
  830.5 3.9 fold.11
  834.4 1.8 collective-permute-start.16
  836.1 3.9 fold.12
  841.2 3.1 pad_maximum_fusion
  844.4 1.8 collective-permute-start.20
  846.2 24.7 %collective-permute-done.16.refs_2_ = bf16[4,128,512]{2,1,0:T(8,128)(2,1)S(1)} collective-permute-done((bf16[4,128,512]{2,1,0:T(8,128)(2,1)}, bf16[4,128,512]{2,1,0:T(8,128)(2,1)S(1)}, u32[]{:S(2)}, u32[]{:S(2)}) %collective-permute-start.16) | collective-permute-done | bytes 524320 | tf_op jit(solution)/shard_map/ppermute | solution.py:1230
  871.8 3.4 fold.13
  875.7 5.2 collective-permute-done.21
  (234 shorter events, 50.8 us)
Async XLA Ops:
  7.2 256.4 %all-gather.2.cloned.1.call-start = ((), (), s32[]{:S(2)}) async-start(), calls=%async_computation | async-start | bytes 4456448 | tf_op jit(solution)/shard_map/all_gather | solution.py:1249
  13.5 67.2 %copy-start.21 = (s32[16,2,4]{0,2,1:T(4,128)S(1)}, s32[16,2,4]{0,2,1:T(4,128)}, u32[]{:S(2)}) copy-start(s32[16,2,4]{0,2,1:T(4,128)} %param.19) | copy-start | bytes 1540
  13.5 70.9 %copy-start.14 = (s32[32,64,32]{1,2,0:T(8,128)S(1)}, s32[32,64,32]{1,2,0:T(8,128)}, u32[]{:S(2)}) copy-start(s32[32,64,32]{1,2,0:T(8,128)} %param.20) | copy-start | bytes 786436
  166.9 39.2 %copy-start.13 = (bf16[512,128]{1,0:T(8,128)(2,1)S(1)}, bf16[512,128]{1,0:T(8,128)(2,1)}, u32[]{:S(2)}) copy-start(bf16[512,128]{1,0:T(8,128)(2,1)} %refs_5_.2) | copy-start | bytes 393220
  166.9 39.2 %copy-start.20 = (bf16[512,128]{1,0:T(8,128)(2,1)S(1)}, bf16[512,128]{1,0:T(8,128)(2,1)}, u32[]{:S(2)}) copy-start(bf16[512,128]{1,0:T(8,128)(2,1)} %get-tuple-element.89) | copy-start | bytes 393220
  263.6 25.8 %copy-start.24 = (s32[32]{0:T(128)S(1)}, s32[32]{0:T(128)}, u32[]{:S(2)}) copy-start(s32[32]{0:T(128)} %param.21) | copy-start | bytes 388
  289.3 38.8 %collective-permute-start = (bf16[512,128]{1,0:T(8,128)(2,1)S(1)}, bf16[512,128]{1,0:T(8,128)(2,1)S(1)}, u32[]{:S(2)}, u32[]{:S(2)}) collective-permute-start(bf16[512,128]{1,0:T(8,128)(2,1)S(1)} %slice.214), channel_id=1, source_target_pairs={{0,1},{1,0},{2,3},{3,2},{4,5},{5,4},{6,7},{7,6},{8,9},{9,8},{10,11... | collective-permute-start | bytes 393224 | tf_op jit(solution)/shard_map/ppermute | solution.py:1227
  289.4 84.9 %copy-start.22 = (s32[32]{0:T(128)}, s32[32]{0:T(128)S(1)}, u32[]{:S(2)}) copy-start(s32[32]{0:T(128)S(1)} %broadcast_subtract_fusion) | copy-start | bytes 388
  369.7 290.9 %copy-start.19 = (f32[64,32]{0,1:T(8,128)}, f32[64,32]{0,1:T(8,128)S(1)}, u32[]{:S(2)}) copy-start(f32[64,32]{0,1:T(8,128)S(1)} %copy.68) | copy-start | bytes 24580
  370.0 3.7 collective-permute-start.1
  374.2 0.5 copy-start.23
  376.2 41.0 %copy-start.3 = (bf16[1024,1536]{1,0:T(8,128)(2,1)S(1)}, bf16[1024,1536]{1,0:T(8,128)(2,1)}, u32[]{:S(2)}) copy-start(bf16[1024,1536]{1,0:T(8,128)(2,1)} %get-tuple-element.113) | copy-start | bytes 9437188
  416.6 42.4 %collective-permute-start.2 = (f32[512,128]{1,0:T(8,128)S(1)}, f32[512,128]{1,0:T(8,128)S(1)}, u32[]{:S(2)}, u32[]{:S(2)}) collective-permute-start(f32[512,128]{1,0:T(8,128)S(1)} %dynamic-slice_bitcast_fusion), channel_id=1, source_target_pairs={{0,1},{1,0},{2,3},{3,2},{4,5},{5,4},{6,7},{7,6},{8,9},{9,8},{10,11... | collective-permute-start | bytes 786440 | tf_op jit(solution)/shard_map/ppermute | solution.py:1227
  419.2 39.8 %copy-start.7 = (f32[1024,128]{1,0:T(8,128)S(1)}, f32[1024,128]{1,0:T(8,128)}, u32[]{:S(2)}) copy-start(f32[1024,128]{1,0:T(8,128)} %copy.72) | copy-start | bytes 1572868
  473.3 9.6 %slice-start.4 = ((s8[6291456]{0:T(1024)(128)(4,1)}), s8[4194304]{0:T(1024)(128)(4,1)S(1)}, s32[]{:S(2)}) async-start(s8[6291456]{0:T(1024)(128)(4,1)} %bitcast.209), calls=%async_computation.5 | async-start | bytes 8388608
  475.6 32.5 %copy-start.10 = (bf16[8,1,64,1536]{3,2,1,0:T(8,128)(2,1)}, bf16[8,1,64,1536]{3,2,1,0:T(8,128)(2,1)S(1)}, u32[]{:S(2)}) copy-start(bf16[8,1,64,1536]{3,2,1,0:T(8,128)(2,1)S(1)} %get-tuple-element.175) | copy-start | bytes 4718596
  475.6 7.2 slice-start.5
  482.7 4.8 copy-start.6
  482.7 25.5 %collective-permute-start.3 = (bf16[512,2048]{1,0:T(8,128)(2,1)S(1)}, bf16[512,2048]{1,0:T(8,128)(2,1)}, u32[]{:S(2)}, u32[]{:S(2)}) collective-permute-start(bf16[512,2048]{1,0:T(8,128)(2,1)S(1)} %convolution_convert_fusion.3.refs_4_), channel_id=1, source_target_pairs={{0,2},{2,0},{4,6},{6,4},{8,10},{10,8},{12,14},{14,12},{16,18},{18,... | collective-permute-start | bytes 6291464 | tf_op jit(solution)/shard_map/ppermute | solution.py:1230
  487.5 62.3 %collective-permute-start.4 = (bf16[512,2048]{1,0:T(8,128)(2,1)}, bf16[512,2048]{1,0:T(8,128)(2,1)}, u32[]{:S(2)}, u32[]{:S(2)}) collective-permute-start(bf16[512,2048]{1,0:T(8,128)(2,1)} %convolution_convert_fusion.2.refs_5_), channel_id=1, source_target_pairs={{0,2},{2,0},{4,6},{6,4},{8,10},{10,8},{12,14},{14,12},{16,18},{18,... | collective-permute-start | bytes 6291464 | tf_op jit(solution)/shard_map/ppermute | solution.py:1230
  487.9 13.7 %copy-start.11 = (bf16[8,1,64,1536]{3,2,1,0:T(8,128)(2,1)S(1)}, bf16[8,1,64,1536]{3,2,1,0:T(8,128)(2,1)}, u32[]{:S(2)}) copy-start(bf16[8,1,64,1536]{3,2,1,0:T(8,128)(2,1)} %get-tuple-element.174) | copy-start | bytes 4718596
  508.0 8.5 copy-start.5
  508.0 30.6 %collective-permute-start.5 = (bf16[512,2048]{1,0:T(8,128)(2,1)S(1)}, bf16[512,2048]{1,0:T(8,128)(2,1)}, u32[]{:S(2)}, u32[]{:S(2)}) collective-permute-start(bf16[512,2048]{1,0:T(8,128)(2,1)S(1)} %convolution_convert_fusion.1.refs_11_), channel_id=1, source_target_pairs={{0,2},{2,0},{4,6},{6,4},{8,10},{10,8},{12,14},{14,12},{16,18},{18,... | collective-permute-start | bytes 6291464 | tf_op jit(solution)/shard_map/ppermute | solution.py:1230
  516.4 22.1 %slice-start = ((s8[6291456]{0:T(1024)(128)(4,1)}), s8[2097152]{0:T(1024)(128)(4,1)S(1)}, s32[]{:S(2)}) async-start(s8[6291456]{0:T(1024)(128)(4,1)} %bitcast.155), calls=%async_computation.1 | async-start | bytes 4194304
  530.1 8.4 slice-start.1
  530.1 8.4 copy-start.8
  538.1 50.8 %collective-permute-start.6 = (bf16[512,2048]{1,0:T(8,128)(2,1)}, bf16[512,2048]{1,0:T(8,128)(2,1)}, u32[]{:S(2)}, u32[]{:S(2)}) collective-permute-start(bf16[512,2048]{1,0:T(8,128)(2,1)} %convolution_convert_fusion.refs_12_), channel_id=1, source_target_pairs={{0,2},{2,0},{4,6},{6,4},{8,10},{10,8},{12,14},{14,12},{16,18},{18,... | collective-permute-start | bytes 6291464 | tf_op jit(solution)/shard_map/ppermute | solution.py:1230
  538.2 112.2 %collective-permute-start.7 = (bf16[512,2048]{1,0:T(8,128)(2,1)}, bf16[512,2048]{1,0:T(8,128)(2,1)}, u32[]{:S(2)}, u32[]{:S(2)}) collective-permute-start(bf16[512,2048]{1,0:T(8,128)(2,1)} %add_convert_fusion.1.refs_4_), channel_id=1, source_target_pairs={{0,1},{1,0},{2,3},{3,2},{4,5},{5,4},{6,7},{7,6},{8,9},{9,8},{10,11... | collective-permute-start | bytes 6291464 | tf_op jit(solution)/shard_map/ppermute | solution.py:1227
  538.6 7.7 copy-start.1
  544.5 105.9 %collective-permute-start.8 = (bf16[512,2048]{1,0:T(8,128)(2,1)}, bf16[512,2048]{1,0:T(8,128)(2,1)}, u32[]{:S(2)}, u32[]{:S(2)}) collective-permute-start(bf16[512,2048]{1,0:T(8,128)(2,1)} %add_convert_fusion.refs_14_), channel_id=1, source_target_pairs={{0,1},{1,0},{2,3},{3,2},{4,5},{5,4},{6,7},{7,6},{8,9},{9,8},{10,11... | collective-permute-start | bytes 6291464 | tf_op jit(solution)/shard_map/ppermute | solution.py:1227
  549.8 39.1 %slice-start.2 = ((s8[6291456]{0:T(1024)(128)(4,1)}), s8[4194304]{0:T(1024)(128)(4,1)S(1)}, s32[]{:S(2)}) async-start(s8[6291456]{0:T(1024)(128)(4,1)} %bitcast.157), calls=%async_computation.3 | async-start | bytes 8388608
  559.3 29.6 %slice-start.3 = ((s8[6291456]{0:T(1024)(128)(4,1)}), s8[2097152]{0:T(1024)(128)(4,1)S(1)}, s32[]{:S(2)}) async-start(s8[6291456]{0:T(1024)(128)(4,1)} %bitcast.157), calls=%async_computation.4 | async-start | bytes 4194304
  559.3 29.6 %copy-start.9 = (bf16[8,1,64,1536]{3,2,1,0:T(8,128)(2,1)S(1)}, bf16[8,1,64,1536]{3,2,1,0:T(8,128)(2,1)}, u32[]{:S(2)}) copy-start(bf16[8,1,64,1536]{3,2,1,0:T(8,128)(2,1)} %get-tuple-element.173) | copy-start | bytes 4718596
  650.4 71.7 %collective-permute-start.9 = (bf16[4,512,512]{2,1,0:T(8,128)(2,1)}, bf16[4,512,512]{2,1,0:T(8,128)(2,1)}, u32[]{:S(2)}, u32[]{:S(2)}) collective-permute-start(bf16[4,512,512]{2,1,0:T(8,128)(2,1)} %weight_pull.4.refs_5_), channel_id=1, source_target_pairs={{0,2},{2,0},{4,6},{6,4},{8,10},{10,8},{12,14},{14,12},{16,18},{18,... | collective-permute-start | bytes 6291464 | tf_op jit(solution)/shard_map/ppermute | solution.py:1230
  650.4 11.5 %copy-start.2 = (bf16[1536,1024]{1,0:T(8,128)(2,1)S(1)}, bf16[1536,1024]{1,0:T(8,128)(2,1)}, u32[]{:S(2)}) copy-start(bf16[1536,1024]{1,0:T(8,128)(2,1)} %get-tuple-element.137) | copy-start | bytes 9437188
  650.4 11.5 %copy-start.18 = (bf16[1536,128]{1,0:T(8,128)(2,1)S(1)}, bf16[1536,128]{1,0:T(8,128)(2,1)}, u32[]{:S(2)}) copy-start(bf16[1536,128]{1,0:T(8,128)(2,1)} %get-tuple-element.136) | copy-start | bytes 1179652
  659.4 72.2 %collective-permute-start.12 = (bf16[2,256,2048]{2,1,0:T(8,128)(2,1)}, bf16[2,256,2048]{2,1,0:T(8,128)(2,1)}, u32[]{:S(2)}, u32[]{:S(2)}) collective-permute-start(bf16[2,256,2048]{2,1,0:T(8,128)(2,1)} %get-tuple-element.125.refs_9_), channel_id=1, source_target_pairs={{0,4},{2,6},{4,0},{6,2},{8,12},{10,14},{12,8},{14,10},{16,20},{18,... | collective-permute-start | bytes 6291464 | tf_op jit(solution)/shard_map/ppermute | solution.py:1230
  717.8 38.8 %collective-permute-start.11 = (bf16[4,512,512]{2,1,0:T(8,128)(2,1)}, bf16[4,512,512]{2,1,0:T(8,128)(2,1)S(1)}, u32[]{:S(2)}, u32[]{:S(2)}) collective-permute-start(bf16[4,512,512]{2,1,0:T(8,128)(2,1)} %weight_pull.5.refs_6_), channel_id=1, source_target_pairs={{0,2},{2,0},{4,6},{6,4},{8,10},{10,8},{12,14},{14,12},{16,18},{18,... | collective-permute-start | bytes 6291464 | tf_op jit(solution)/shard_map/ppermute | solution.py:1230
  731.6 36.0 %collective-permute-start.10 = (bf16[4,256,512]{2,1,0:T(8,128)(2,1)}, bf16[4,256,512]{2,1,0:T(8,128)(2,1)}, u32[]{:S(2)}, u32[]{:S(2)}) collective-permute-start(bf16[4,256,512]{2,1,0:T(8,128)(2,1)} %get-tuple-element.129.refs_3_), channel_id=1, source_target_pairs={{0,8},{2,10},{4,12},{6,14},{8,0},{10,2},{12,4},{14,6},{16,24},{18,... | collective-permute-start | bytes 3145736 | tf_op jit(solution)/shard_map/ppermute | solution.py:1230
  747.8 75.1 %collective-permute-start.13 = (bf16[1536,512]{1,0:T(8,128)(2,1)}, bf16[1536,512]{1,0:T(8,128)(2,1)}, u32[]{:S(2)}, u32[]{:S(2)}) collective-permute-start(bf16[1536,512]{1,0:T(8,128)(2,1)} %token_pull.2.refs_6_), channel_id=1, source_target_pairs={{0,1},{1,0},{2,3},{3,2},{4,5},{5,4},{6,7},{7,6},{8,9},{9,8},{10,11... | collective-permute-start | bytes 4718600 | tf_op jit(solution)/shard_map/ppermute | solution.py:1227
  754.7 81.5 %collective-permute-start.17 = (bf16[2,128,2048]{2,1,0:T(8,128)(2,1)}, bf16[2,128,2048]{2,1,0:T(8,128)(2,1)}, u32[]{:S(2)}, u32[]{:S(2)}) collective-permute-start(bf16[2,128,2048]{2,1,0:T(8,128)(2,1)} %get-tuple-element.131.refs_6_), channel_id=1, source_target_pairs={{0,8},{2,10},{4,12},{6,14},{8,0},{10,2},{12,4},{14,6},{16,24},{18,... | collective-permute-start | bytes 3145736 | tf_op jit(solution)/shard_map/ppermute | solution.py:1230
  756.6 1.4 copy-start.4
  767.6 62.9 %collective-permute-start.14 = (bf16[4,256,512]{2,1,0:T(8,128)(2,1)}, bf16[4,256,512]{2,1,0:T(8,128)(2,1)}, u32[]{:S(2)}, u32[]{:S(2)}) collective-permute-start(bf16[4,256,512]{2,1,0:T(8,128)(2,1)} %get-tuple-element.132.refs_3_), channel_id=1, source_target_pairs={{0,8},{2,10},{4,12},{6,14},{8,0},{10,2},{12,4},{14,6},{16,24},{18,... | collective-permute-start | bytes 3145736 | tf_op jit(solution)/shard_map/ppermute | solution.py:1230
  771.5 54.2 %collective-permute-start.15 = (bf16[4,128,512]{2,1,0:T(8,128)(2,1)}, bf16[4,128,512]{2,1,0:T(8,128)(2,1)}, u32[]{:S(2)}, u32[]{:S(2)}) collective-permute-start(bf16[4,128,512]{2,1,0:T(8,128)(2,1)} %get-tuple-element.133.refs_6_), channel_id=1, source_target_pairs={{0,16},{2,18},{4,20},{6,22},{8,24},{10,26},{12,28},{14,30},{16,0},... | collective-permute-start | bytes 1572872 | tf_op jit(solution)/shard_map/ppermute | solution.py:1230
  784.3 38.5 %copy-start = (f32[1536,512]{1,0:T(8,128)S(1)}, f32[1536,512]{1,0:T(8,128)}, u32[]{:S(2)}) copy-start(f32[1536,512]{1,0:T(8,128)} %token_pull.3.refs_1_) | copy-start | bytes 9437188
  829.1 15.2 %collective-permute-start.19 = (bf16[4,64,512]{2,1,0:T(8,128)(2,1)}, bf16[4,64,512]{2,1,0:T(8,128)(2,1)S(1)}, u32[]{:S(2)}, u32[]{:S(2)}) collective-permute-start(bf16[4,64,512]{2,1,0:T(8,128)(2,1)} %get-tuple-element.138.refs_3_), channel_id=1, source_target_pairs={{0,4},{2,6},{4,0},{6,2},{8,12},{10,14},{12,8},{14,10},{16,20},{18,... | collective-permute-start | bytes 786440 | tf_op jit(solution)/shard_map/ppermute | solution.py:1230
  834.4 36.6 %collective-permute-start.16 = (bf16[4,128,512]{2,1,0:T(8,128)(2,1)}, bf16[4,128,512]{2,1,0:T(8,128)(2,1)S(1)}, u32[]{:S(2)}, u32[]{:S(2)}) collective-permute-start(bf16[4,128,512]{2,1,0:T(8,128)(2,1)} %get-tuple-element.140.refs_3_), channel_id=1, source_target_pairs={{0,16},{2,18},{4,20},{6,22},{8,24},{10,26},{12,28},{14,30},{16,0},... | collective-permute-start | bytes 1572872 | tf_op jit(solution)/shard_map/ppermute | solution.py:1230
  840.1 4.3 copy-start.17
  840.1 40.8 %collective-permute-start.21 = (bf16[2,64,2048]{2,1,0:T(8,128)(2,1)}, bf16[2,64,2048]{2,1,0:T(8,128)(2,1)S(1)}, u32[]{:S(2)}, u32[]{:S(2)}) collective-permute-start(bf16[2,64,2048]{2,1,0:T(8,128)(2,1)} %get-tuple-element.142.refs_3_), channel_id=1, source_target_pairs={{0,16},{2,18},{4,20},{6,22},{8,24},{10,26},{12,28},{14,30},{16,0},... | collective-permute-start | bytes 1572872 | tf_op jit(solution)/shard_map/ppermute | solution.py:1230
  844.3 36.6 %copy-start.12 = (f32[2,64,2048]{2,1,0:T(8,128)S(1)}, f32[2,64,2048]{2,1,0:T(8,128)}, u32[]{:S(2)}) copy-start(f32[2,64,2048]{2,1,0:T(8,128)} %get-tuple-element.146) | copy-start | bytes 3145732
  844.4 37.6 %collective-permute-start.20 = (bf16[4,64,512]{2,1,0:T(8,128)(2,1)S(1)}, bf16[4,64,512]{2,1,0:T(8,128)(2,1)S(1)}, u32[]{:S(2)}, u32[]{:S(2)}) collective-permute-start(bf16[4,64,512]{2,1,0:T(8,128)(2,1)S(1)} %add_convert_fusion.2), channel_id=1, source_target_pairs={{0,1},{1,0},{2,3},{3,2},{4,5},{5,4},{6,7},{7,6},{8,9},{9,8},{10,11... | collective-permute-start | bytes 786440 | tf_op jit(solution)/shard_map/ppermute | solution.py:1227
  871.0 0.8 copy-start.15
  875.2 6.9 copy-start.16
  875.2 6.9 collective-permute-start.18
Sparse Core Ops, SparseCore 0:
  80.7 48.8 all-gather.1

commit v5 on v4

--- a/solution.py
+++ b/solution.py
@@ -81,8 +81,16 @@
     return pl.BlockSpec((step, width), lambda i, *_: (i, 0))
 
 
-def column_spec(width, step):
-    return pl.BlockSpec((width, step), lambda i, *_: (0, i))
+def by_core(block, paired):
+    if not paired:
+        return block
+    firsts, seconds = [], []
+    for at in range(0, block.shape[1], 256):
+        one, two = block[:, at : at + 128], block[:, at + 128 : at + 256]
+        low = lax.broadcasted_iota(jnp.int32, one.shape, 1) < 64
+        firsts.append(jnp.where(low, one, pltpu.roll(two, 64, 1)))
+        seconds.append(jnp.where(low, pltpu.roll(one, 64, 1), two))
+    return jnp.concatenate(firsts + seconds, axis=1)
 
 
 MESH = pl.DeviceIdType.MESH
@@ -148,7 +156,7 @@
     partner = {"cols": 1 - c}
     bits = [1 << b for b in range(rows.bit_length() - 1)]
     greet([partner] + [{"rows": across(r, bit)} for bit in bits])
-    wide = [(qkv, qkv_o), (out, out_o), (up, up_o)]
+    wide = [(qkv, qkv_o)]
     copies, first = [], []
     for place, (source, target) in enumerate(wide):
         first.append(
@@ -165,7 +173,8 @@
             send(tokens.at[theirs], target, sent.at[3 + place], arrived.at[3 + place], partner)
         )
         pltpu.make_async_copy(tokens.at[mine], target, own_sem.at[place]).start()
-    for place, (source, target) in enumerate([(proj, proj_o), (pack, pack_o), (down.at[r], down_o)]):
+    narrow = [(proj, proj_o), (pack, pack_o), (out.at[r], out_o), (up.at[r], up_o), (down.at[r], down_o)]
+    for place, (source, target) in enumerate(narrow):
         copies.append(
             send(source, target, sent.at[5 + place], arrived.at[5 + place], partner)
         )
@@ -207,21 +216,18 @@
         functools.partial(start_kernel, rows, width, parts), "start_up", (1,),
         [ANYWHERE] * 7, [ANYWHERE] * 7,
         [
-            shaped(BF16, n, 2 * width), shaped(BF16, *qkv_p.shape), shaped(BF16, *out_p.shape),
-            shaped(BF16, *up_p.shape), shaped(BF16, *down_p.shape[1:]), shaped(BF16, *proj.shape),
-            shaped(F32, *pack.shape),
+            shaped(BF16, n, 2 * width), shaped(BF16, *qkv_p.shape), shaped(BF16, *out_p.shape[1:]),
+            shaped(BF16, *up_p.shape[1:]), shaped(BF16, *down_p.shape[1:]),
+            shaped(BF16, *proj.shape), shaped(F32, *pack.shape),
         ],
         operands, 0, remote=1,
         scratch=[
-            pltpu.SemaphoreType.DMA((2,)), pltpu.SemaphoreType.DMA((8,)),
-            pltpu.SemaphoreType.DMA((8,)), pltpu.SemaphoreType.DMA((3, rows)),
-            pltpu.SemaphoreType.DMA((3, rows)),
+            pltpu.SemaphoreType.DMA((2,)), pltpu.SemaphoreType.DMA((10,)),
+            pltpu.SemaphoreType.DMA((10,)), pltpu.SemaphoreType.DMA((1, rows)),
+            pltpu.SemaphoreType.DMA((1, rows)),
         ],
     )
-    return (
-        x, qkv_o.reshape(qkv.shape), out_o.reshape(out.shape), up_o.reshape(up.shape), down_o,
-        proj_o, pack_o,
-    )
+    return x, qkv_o.reshape(qkv.shape), out_o, up_o, down_o, proj_o, pack_o
 
 
 def gather_kernel(rows, own, out, own_sem, sent, arrived):
@@ -436,7 +442,7 @@
         ref[...] += value
 
 
-def out_norm_kernel(slots, *refs):
+def out_norm_kernel(slots, paired, *refs):
     x_ref, vec_ref = refs[:2]
     att_refs, w_refs = refs[2 : 2 + slots], refs[2 + slots : 2 + 2 * slots]
     normed_ref, inverse_ref, low_ref, turned_ref = refs[2 + 2 * slots :]
@@ -449,20 +455,20 @@
         normed_ref[at, :] = normed
         inverse_ref[at, :] = inverse
         low_ref[at, :] = hidden.astype(BF16)
-        turned_ref[:, at] = hidden.T.astype(BF16)
-
-
-def out_and_norm(x, vectors, attended, weights):
+        turned_ref[at, :] = by_core(hidden, paired).astype(BF16)
+
+
+def out_and_norm(x, vectors, attended, weights, paired):
     n, D = x.shape
     step = row_step(n)
     slots = len(attended)
     width = attended[0].shape[1]
     return call(
-        functools.partial(out_norm_kernel, slots), "out_and_norm", (n // step,),
+        functools.partial(out_norm_kernel, slots, paired), "out_and_norm", (n // step,),
         [row_spec(step, D), held(vectors.shape)]
         + [row_spec(step, width)] * slots + [held((width, D))] * slots,
-        [row_spec(step, D), row_spec(step, 1), row_spec(step, D), column_spec(D, step)],
-        [shaped(F32, n, D), shaped(F32, n, 1), shaped(BF16, n, D), shaped(BF16, D, n)],
+        [row_spec(step, D), row_spec(step, 1), row_spec(step, D), row_spec(step, D)],
+        [shaped(F32, n, D), shaped(F32, n, 1), shaped(BF16, n, D), shaped(BF16, n, D)],
         (x, vectors, *attended, *weights), 2 * n * D * D,
     )
 
@@ -551,7 +557,7 @@
 
 
 def head_pull_kernel(
-    grad_ref, unit_ref, unit_inverse_ref, proj_ref, normed_ref, inverse_ref, vec_ref,
+    paired, grad_ref, unit_ref, unit_inverse_ref, proj_ref, normed_ref, inverse_ref, vec_ref,
     embed_ref, residual_ref, low_ref, turned_ref, sum_ref,
 ):
     sums = []
@@ -565,27 +571,27 @@
         residual = norm_pull(output_grad, normed, inverse_ref[at, :], vec_ref[4:5, :])
         residual_ref[at, :] = residual
         low_ref[at, :] = residual.astype(BF16)
-        turned_ref[:, at] = residual.T.astype(BF16)
+        turned_ref[at, :] = by_core(residual, paired).astype(BF16)
         sums.append(column_sums(residual, output_grad * normed, output_grad))
     add_over_steps(sum_ref, sum(sums))
 
 
-def head_pull(unit_grad, unit, unit_inverse, proj, normed, inverse, vectors):
+def head_pull(unit_grad, unit, unit_inverse, proj, normed, inverse, vectors, paired):
     n, D = normed.shape
     step = row_step(n)
     return call(
-        head_pull_kernel, "head_pull", (n // step,),
+        functools.partial(head_pull_kernel, paired), "head_pull", (n // step,),
         [
             row_spec(step, 128), row_spec(step, 128), row_spec(step, 1), held(proj.shape),
             row_spec(step, D), row_spec(step, 1), held(vectors.shape),
         ],
         [
             row_spec(step, 128), row_spec(step, D), row_spec(step, D),
-            column_spec(D, step), pl.BlockSpec((8, D), lambda i: (0, 0)),
+            row_spec(step, D), pl.BlockSpec((8, D), lambda i: (0, 0)),
         ],
         [
             shaped(BF16, n, 128), shaped(F32, n, D), shaped(BF16, n, D),
-            shaped(BF16, D, n), shaped(F32, 8, D),
+            shaped(BF16, n, D), shaped(F32, 8, D),
         ],
         (unit_grad, unit, unit_inverse, proj, normed, inverse, vectors), 4 * n * D * 128,
     )
@@ -616,7 +622,7 @@
     )
 
 
-def hidden_pull_kernel(slots, *refs):
+def hidden_pull_kernel(slots, paired, *refs):
     residual_ref, normed_ref, inverse_ref, vec_ref = refs[:4]
     pre_refs, up_refs, out_refs = (refs[4 + j * slots : 4 + (j + 1) * slots] for j in range(3))
     rest = refs[4 + 3 * slots :]
@@ -631,33 +637,33 @@
         residual = norm_pull(hidden_grad, normed, inverse_ref[at, :], vec_ref[1:2, :])
         grad_ref[at, :] = residual
         low = residual.astype(BF16)
-        turned_ref[:, at] = residual.T.astype(BF16)
+        turned_ref[at, :] = by_core(residual, paired).astype(BF16)
         sums.append(column_sums(residual, hidden_grad * normed, hidden_grad))
         for att_ref, out_ref in zip(att_refs, out_refs):
             att_ref[at, :] = mm(low, out_ref[...], NT).astype(BF16)
     add_over_steps(sum_ref, sum(sums))
 
 
-def hidden_pull(residual, normed, inverse, vectors, pre_grads, ups, outs):
+def hidden_pull(residual, normed, inverse, vectors, pre_grads, ups, outs, paired):
     n, D = residual.shape
     step = row_step(n)
     slots = len(ups)
     wide, width = ups[0].shape[1], outs[0].shape[0]
     return call(
-        functools.partial(hidden_pull_kernel, slots), "hidden_pull", (n // step,),
+        functools.partial(hidden_pull_kernel, slots, paired), "hidden_pull", (n // step,),
         [row_spec(step, D), row_spec(step, D), row_spec(step, 1), held(vectors.shape)]
         + [row_spec(step, wide)] * slots + [held((D, wide))] * slots
         + [held((width, D))] * slots,
-        [row_spec(step, D), column_spec(D, step), pl.BlockSpec((8, D), lambda i: (0, 0))]
+        [row_spec(step, D), row_spec(step, D), pl.BlockSpec((8, D), lambda i: (0, 0))]
         + [row_spec(step, width)] * slots,
-        [shaped(F32, n, D), shaped(BF16, D, n), shaped(F32, 8, D)]
+        [shaped(F32, n, D), shaped(BF16, n, D), shaped(F32, 8, D)]
         + [shaped(BF16, n, width)] * slots,
         (residual, normed, inverse, vectors, *pre_grads, *ups, *outs),
         0,
     )
 
 
-def token_pull_kernel(slots, place_ref, *refs):
+def token_pull_kernel(slots, span, place_ref, *refs):
     residual_ref = refs[0]
     mixed_refs, w_refs = refs[1 : 1 + slots], refs[1 + slots : 1 + 2 * slots]
     out_ref = refs[-1]
@@ -665,8 +671,11 @@
     at = pl.ds(pl.multiple_of(place_ref[0] * width, width), width)
     total = residual_ref[...]
     for mixed_ref, w_ref in zip(mixed_refs, w_refs):
-        for which in range(3):
-            total = total + mm(mixed_ref[which], w_ref[which, at, :], NT)
+        for first in range(0, width, span):
+            for which in range(3):
+                start = 4 * first + which * span
+                mixed = mixed_ref[:, start : start + span]
+                total = total + mm(mixed, w_ref[which, at, first : first + span], NT)
     out_ref[...] = total.astype(out_ref.dtype)
 
 
@@ -676,9 +685,9 @@
     slots = len(weights)
     width = weights[0].shape[2]
     return call(
-        functools.partial(token_pull_kernel, slots), "token_pull", (n // step,),
+        functools.partial(token_pull_kernel, slots, min(width, ATTENTION_LANES)), "token_pull", (n // step,),
         [pl.BlockSpec((step, width), lambda i, p: (i, p[0]))]
-        + [pl.BlockSpec((3, step, width), lambda i, p: (0, i, 0))] * slots
+        + [row_spec(step, 4 * width)] * slots
         + [held((3, D, width))] * slots,
         [row_spec(step, width)],
         [shaped(dtype, n, width)],
@@ -713,66 +722,6 @@
         @pl.when((pl.program_id(0) >= starts[place]) & (pl.program_id(0) < starts[place + 1]))
         def _(place=place):
             body(place)
-
-
-def weight_pull_kernel(starts, added, inner, place_ref, *refs):
-    groups = len(starts) - 1
-    lefts, rights, refs = refs[:groups], refs[groups : 2 * groups], refs[2 * groups :]
-
-    def one_group(place):
-        left = lefts[place]
-        total = mm(left[:, 0].reshape(-1, left.shape[-1]), rights[place][0])
-        outs = refs
-        if added:
-            total = total + refs[0][0].astype(F32)
-            outs = refs[1:]
-        if inner:
-            put_halves(total, inner, place_ref[1], outs)
-        else:
-            outs[0][0] = total.astype(outs[0].dtype)
-
-    for_group(starts, one_group)
-
-
-def weight_pull(places, lefts, rights, arrived=None, dtype=BF16, inner=0):
-    pairs, _, share, n = lefts[0].shape
-    m = rights[0].shape[2]
-    rows = pairs * share
-    chunk = min(512, m)
-    starts = [0]
-    for right in rights:
-        starts.append(starts[-1] + right.shape[0])
-
-    def spec(size):
-        return pl.BlockSpec((1, size, chunk), lambda j, i, p: (j, 0, i))
-
-    half = rows // 2
-    outs = [(BF16, half), (F32, half)] if inner else [(dtype, rows)]
-    return call(
-        functools.partial(weight_pull_kernel, starts, arrived is not None, inner), "weight_pull",
-        (starts[-1], m // chunk),
-        [pl.BlockSpec((pairs, 1, share, n), lambda j, i, p: (0, p[0], 0, 0)) for _ in lefts]
-        + [
-            pl.BlockSpec((1, n, chunk), grouped_index(starts, place, m // chunk))
-            for place in range(len(rights))
-        ] + ([] if arrived is None else [spec(rows)]),
-        [spec(size) for _, size in outs],
-        [shaped(kind, starts[-1], size, m) for kind, size in outs],
-        (places, *lefts, *rights) + (() if arrived is None else (arrived,)),
-        0, prefetch=1,
-    )
-
-
-def pass_on_kernel(in_ref, out_ref):
-    out_ref[...] = in_ref[...]
-
-
-def pass_on(array):
-    spec = held(array.shape)
-    return call(
-        pass_on_kernel, "pass_on", (1,), [spec], [pl.BlockSpec(array.shape, lambda *_: (0,) * array.ndim)],
-        [shaped(array.dtype, *array.shape)], (array,), 0,
-    )[0]
 
 
 def fold_kernel(starts, inner, place_ref, *refs):
@@ -809,7 +758,7 @@
 
 
 SEGMENTS = 8
-ATTENTION_LANES = 128
+ATTENTION_LANES = 256
 
 
 def half_lanes(block, head, other):
@@ -840,53 +789,43 @@
 
 def attention_forward_kernel(
     span_ref, qkv_ref, ext_k_ref, ext_q_ref, out_ref, rest_ref, ext_ref,
-    keys_ref, queries_ref, turned_ref, values_ref, *, tile,
+    keys_ref, queries_ref, *, tile,
 ):
     n = ext_k_ref.shape[0]
     tiles = n // tile
     pairs = qkv_ref.shape[2] // 128
-    heads = range(2 * pairs)
-
-    def lanes(head):
-        return slice(head // 2 * 128, head // 2 * 128 + 128)
-
-    def own_rows(head):
-        return slice(head % 2 * DH, head % 2 * DH + DH)
-
-    for head in heads:
-        keys_ref[head] = half_lanes(qkv_ref[1, :, lanes(head)], head % 2, ext_k_ref[...])
-        queries_ref[head] = half_lanes(
-            scaled(qkv_ref[0, :, lanes(head)]), head % 2, ext_q_ref[...]
-        )
+
+    def lanes(pair):
+        return slice(pair * 128, pair * 128 + 128)
+
     for pair in range(pairs):
-        for step in range(tiles):
-            at = slice(step * tile, (step + 1) * tile)
-            values_ref[pair, :, at] = qkv_ref[2, at, lanes(2 * pair)].astype(F32).T.astype(BF16)
-            for head in (2 * pair, 2 * pair + 1):
-                turned_ref[head, step] = queries_ref[head, at, :].astype(F32).T.astype(BF16)
+        query = scaled(qkv_ref[0, :, lanes(pair)])
+        for half in range(2):
+            keys_ref[2 * pair + half] = half_lanes(qkv_ref[1, :, lanes(pair)], half, ext_k_ref[...])
+            queries_ref[2 * pair + half] = half_lanes(query, half, ext_q_ref[...])
 
     def attend(step, low, count):
         rows = pl.ds(pl.multiple_of(step * tile, tile), tile)
         window = pl.ds(pl.multiple_of(low * tile, tile), count * tile)
+        lane = lax.broadcasted_iota(jnp.int32, (tile, 128), 1)
         for pair in range(pairs):
-            outs, extras = [], []
-            for head in (2 * pair, 2 * pair + 1):
-                logits = mm(keys_ref[head, window, :], turned_ref[head, step])
-                top = jnp.max(logits, axis=0, keepdims=True)
+            at = lanes(pair)
+            outs, extra = [], ext_q_ref[rows, :].astype(F32)
+            for half in range(2):
+                head = 2 * pair + half
+                logits = mm(queries_ref[head, rows, :], keys_ref[head, window, :], NT)
+                top = jnp.max(logits, axis=1, keepdims=True)
                 weights = jnp.exp(logits - top)
-                mass = jnp.sum(weights, axis=0, keepdims=True)
+                mass = jnp.sum(weights, axis=1, keepdims=True)
                 probs = (weights * (1.0 / mass)).astype(BF16)
-                outs.append(mm(values_ref[pair, own_rows(head), window], probs))
-                terms = three_terms(-(top + jnp.log(mass)))
-                extras.append(
-                    [jnp.zeros((8, tile), F32), *terms, jnp.zeros((DH - 11, tile), F32)]
-                )
-            at = lanes(2 * pair)
-            out = jnp.concatenate(outs, axis=0).T
+                outs.append(mm(probs, qkv_ref[2, window, at]))
+                first = SEGMENTS + DH * (1 - half)
+                for place, term in enumerate(three_terms(-(top + jnp.log(mass)))):
+                    extra = jnp.where(lane == first + place, term, extra)
+            out = jnp.where(lane < DH, outs[0], outs[1])
             out_ref[rows, at] = out.astype(BF16)
             rest_ref[rows, at] = (out - out.astype(BF16).astype(F32)).astype(BF16)
-            extra = jnp.concatenate(extras[1] + extras[0], axis=0).T
-            ext_ref[rows, at] = (extra + ext_q_ref[rows, :].astype(F32)).astype(BF16)
+            ext_ref[rows, at] = extra.astype(BF16)
 
     for_spans(span_ref, tiles, attend)
 
@@ -895,18 +834,14 @@
     _, n, width = qkv.shape
     span = min(width, ATTENTION_LANES)
     wide = pl.BlockSpec((n, span), lambda i, *_: (0, i))
-    tiles, pairs = n // tile, span // 128
+    heads = pltpu.VMEM((span // DH, n, 128), BF16)
     return call(
         functools.partial(attention_forward_kernel, tile=tile), "attention_forward",
         (width // span,),
         [pl.BlockSpec((3, n, span), lambda i, *_: (0, 0, i)), held((n, 128)), held((n, 128))],
         [wide, wide, wide],
         [shaped(BF16, n, width)] * 3,
-        (spans, qkv, ext_k, ext_q), 0, prefetch=1,
-        scratch=[
-            pltpu.VMEM((2 * pairs, n, 128), BF16), pltpu.VMEM((2 * pairs, n, 128), BF16),
-            pltpu.VMEM((2 * pairs, tiles, 128, tile), BF16), pltpu.VMEM((pairs, 128, n), BF16),
-        ],
+        (spans, qkv, ext_k, ext_q), 0, prefetch=1, scratch=[heads, heads],
     )
 
 
@@ -947,16 +882,14 @@
                 head = 2 * pair + half
                 keys_ref[head, at, :] = half_lanes(qkv_ref[1, at, cut], half, ext_k)
                 values_ref[head, at, :] = half_lanes(qkv_ref[2, at, cut], half, ext_k)
-                whole = half_lanes(query, half, ext_ref[at, cut])
-                queries_ref[head, step] = whole.astype(F32).T.astype(BF16)
+                queries_ref[head, at, :] = half_lanes(query, half, ext_ref[at, cut])
                 plain_ref[head, at, :] = half_lanes(query, half, zeros)
                 plain_grads_ref[head, at, :] = half_lanes(grad, half, zeros)
                 inner = jnp.sum(half_lanes(product, half, 0.0), axis=1, keepdims=True)
                 extra = jnp.zeros((tile, 128), F32)
                 for place, term in enumerate(three_terms(-inner)):
                     extra = jnp.where((lane & (DH - 1)) == SEGMENTS + place, term, extra)
-                whole = half_lanes(grad.astype(F32), half, extra)
-                grads_ref[head, step] = whole.T.astype(BF16)
+                grads_ref[head, at, :] = half_lanes(grad, half, extra.astype(BF16))
 
     dk_ref[...] = jnp.zeros(dk_ref.shape, F32)
     dv_ref[...] = jnp.zeros(dv_ref.shape, F32)
@@ -968,8 +901,8 @@
             probs, slopes, dq = [], [], []
             both = range(2 * pair, 2 * pair + 2)
             for head in both:
-                weights = jnp.exp(mm(keys_ref[head, window, :], queries_ref[head, step]))
-                flow = mm(values_ref[head, window, :], grads_ref[head, step])
+                weights = jnp.exp(mm(keys_ref[head, window, :], queries_ref[head, at, :], NT))
+                flow = mm(values_ref[head, window, :], grads_ref[head, at, :], NT)
                 slope = (weights * flow).astype(BF16)
                 probs.append(weights.astype(BF16))
                 slopes.append(slope)
@@ -986,6 +919,7 @@
     def finish(step, sums):
         cosine, sine = cos_ref[rows(step), :], sin_ref[rows(step), :]
         added = []
+        out_ref[rows(step), 3 * pairs * 128 :] = att_ref[rows(step), :]
         for which, src in enumerate((dq_ref, dk_ref, dv_ref)):
             for pair in range(pairs):
                 at = lanes(2 * pair)
@@ -993,7 +927,8 @@
                 if which < 2:
                     block = block * cosine - swap_halves(block) * sine
                 low = block.astype(BF16)
-                out_ref[which, rows(step), at] = low
+                first = (which * pairs + pair) * 128
+                out_ref[rows(step), first : first + 128] = low
                 total = jnp.sum(low.astype(F32), axis=0, keepdims=True)
                 added.append(sums[which * pairs + pair] + total)
         return tuple(added)
@@ -1011,19 +946,21 @@
     span = min(width, ATTENTION_LANES)
     wide = pl.BlockSpec((n, span), lambda i, *_: (0, i))
     three = pl.BlockSpec((3, n, span), lambda i, *_: (0, 0, i))
-    tiles, pairs = n // tile, span // 128
+    pairs = span // 128
     heads = pltpu.VMEM((2 * pairs, n, 128), BF16)
-    turned = pltpu.VMEM((2 * pairs, tiles, 128, tile), BF16)
     return call(
         functools.partial(attention_backward_kernel, tile=tile), "attention_backward",
         (width // span,),
         [three, wide, wide, wide, wide, held((n, 128)), held((n, 128)), held((n, 128))],
-        [three, pl.BlockSpec((8, span), lambda i, *_: (0, i))],
-        [shaped(BF16, 3, n, width), shaped(F32, 8, width)],
+        [
+            pl.BlockSpec((n, 4 * span), lambda i, *_: (0, i)),
+            pl.BlockSpec((8, span), lambda i, *_: (0, i)),
+        ],
+        [shaped(BF16, n, 4 * width), shaped(F32, 8, width)],
         (spans, qkv, ext, attended, rest, grads, ext_k, cosine, sine), 0,
         prefetch=1,
         scratch=[
-            heads, pltpu.VMEM((pairs, 128, n), BF16), heads, turned, heads, turned, heads,
+            heads, pltpu.VMEM((pairs, 128, n), BF16), heads, heads, heads, heads, heads,
         ] + [pltpu.VMEM((n, span), F32)] * 3,
     )
 
@@ -1036,7 +973,7 @@
     return token == lax.broadcasted_iota(jnp.int32, (width, queries), 1)
 
 
-def score_kernel(low_ref, high_ref, doc_ref, query_ref, pick_ref, out_ref, sum_ref):
+def score_kernel(low_ref, high_ref, doc_ref, query_ref, pick_ref, out_ref, sum_ref, total_ref):
     group = pl.program_id(0)
     docs, width = pick_ref.shape[1:]
     doc_rows = doc_ref.shape[0]
@@ -1072,12 +1009,13 @@
             def _(doc):
                 add_strip(sim, first, doc, pick_ref[0, pl.ds(doc, 1), :])
 
-    totals = jnp.sum(sum_ref[...], axis=1)
-    totals = jnp.concatenate([totals, jnp.zeros((8 - docs, width), F32)], axis=0)
-    spread = token_sums(width, out_ref.shape[2]).astype(F32)
-    out_ref[0] = lax.dot_general(
-        totals, spread, NN, precision=lax.Precision.HIGHEST, preferred_element_type=F32
-    )[:docs]
+    total_ref[group] = jnp.sum(sum_ref[...], axis=1)
+
+    @pl.when(group == pl.num_programs(0) - 1)
+    def _():
+        spread = token_sums(width, out_ref.shape[1]).astype(F32).astype(BF16)
+        total = jnp.concatenate([total_ref[g] for g in range(total_ref.shape[0])], axis=0)
+        out_ref[...] = sum(mm(term.astype(BF16), spread) for term in three_terms(total))
 
 
 def score_grad_kernel(
@@ -1090,18 +1028,17 @@
     strips = doc_rows // STRIP
     chunk = min(256, doc_rows)
     row = lax.broadcasted_iota(jnp.int32, (STRIP, width), 0)
-    spread = token_sums(width, weight_ref.shape[2]).astype(F32).astype(BF16)
-    weights = jnp.concatenate(
-        [weight_ref[0], jnp.zeros((16 - docs, weight_ref.shape[2]), F32)], axis=0
-    )
-    token_ref[...] = mm(weights.astype(BF16), spread, NT)
 
     def fill(held, first, doc, pick):
-        return jnp.where(row == pick - first, token_ref[pl.ds(doc, 1), :], held)
+        return jnp.where(row == pick - first, token_ref[group, pl.ds(doc, 1), :], held)
 
     @pl.when(group == 0)
     def _():
         query_out[...] = jnp.zeros_like(query_out)
+        spread = token_sums(width, weight_ref.shape[1]).astype(F32).astype(BF16)
+        weights = mm(weight_ref[...].astype(BF16), spread, NT)
+        for g in range(token_ref.shape[0]):
+            token_ref[g] = weights[g * docs : (g + 1) * docs]
 
     total = None
     for start in range(0, doc_rows, chunk):
@@ -1136,44 +1073,44 @@
             query_out[...] += mm(turned, held)
 
 
-def score_specs(doc_tile, query_tile, picks, queries):
+def score_specs(doc_tile, query_tile, picks):
     groups, docs, width = picks.shape
     doc_rows = doc_tile.shape[0] // groups
     return (
         pl.BlockSpec((doc_rows, 128), lambda i, *_: (i, 0)),
         held(query_tile.shape),
         pl.BlockSpec((1, docs, width), lambda i, *_: (i, 0, 0)),
-        pl.BlockSpec((1, docs, queries), lambda i, *_: (i, 0, 0)),
     )
 
 
 def score_forward(lows, highs, doc_tile, query_tile, picks):
     groups, docs, width = picks.shape
     queries = width // QLEN
-    doc_spec, query_spec, pick_spec, out_spec = score_specs(doc_tile, query_tile, picks, queries)
+    doc_spec, query_spec, pick_spec = score_specs(doc_tile, query_tile, picks)
     return call(
         score_kernel, "score_forward", (groups,),
-        [doc_spec, query_spec, pick_spec], [out_spec],
-        [shaped(F32, groups, docs, queries)],
+        [doc_spec, query_spec, pick_spec],
+        [pl.BlockSpec((groups * docs, queries), lambda i, *_: (0, 0))],
+        [shaped(F32, groups * docs, queries)],
         (lows, highs, doc_tile, query_tile, picks), 2 * doc_tile.shape[0] * width * 128,
-        prefetch=2, scratch=[pltpu.VMEM((docs, 8, width), F32)],
+        prefetch=2,
+        scratch=[pltpu.VMEM((docs, 8, width), F32), pltpu.VMEM((groups, docs, width), F32)],
     )[0]
 
 
 def score_backward(lows, highs, doc_tile, query_tile, picks, weights):
     groups, docs, width = picks.shape
-    doc_spec, query_spec, pick_spec, weight_spec = score_specs(
-        doc_tile, query_tile, picks, weights.shape[2]
-    )
+    doc_spec, query_spec, pick_spec = score_specs(doc_tile, query_tile, picks)
     return call(
         score_grad_kernel, "score_backward", (groups,),
-        [doc_spec, query_spec, pick_spec, weight_spec],
+        [doc_spec, query_spec, pick_spec, held(weights.shape)],
         [doc_spec, pl.BlockSpec((128, width), lambda i, *_: (0, 0))],
         [shaped(F32, *doc_tile.shape), shaped(F32, 128, width)],
         (lows, highs, doc_tile, query_tile, picks, weights), 4 * doc_tile.shape[0] * width * 128,
         prefetch=2,
         scratch=[
-            pltpu.VMEM((doc_tile.shape[0] // groups, width), BF16), pltpu.VMEM((16, width), F32)
+            pltpu.VMEM((doc_tile.shape[0] // groups, width), BF16),
+            pltpu.VMEM((groups, docs, width), F32),
         ],
     )
 
@@ -1249,14 +1186,14 @@
         return [lax.all_gather(piece, "rows", axis=0, tiled=True) for piece in pieces]
 
     if C == 2:
-        x, *others, down_piece, proj_other, pack_other = start_up(
+        x, qkv_other, *pieces, proj_other, pack_other = start_up(
             R, (Q, DS, ROW_LEN), tokens, w_qkv, w_out, w_up, w_down, w_proj,
             packed.reshape(8, -1),
         )
-        wqkv_slots, wout_slots, wup_slots = (
-            [own, other] for own, other in zip((w_qkv, w_out, w_up), others)
+        wqkv_slots = [w_qkv, qkv_other]
+        wout_slots, wup_slots, wdown_slots = (
+            [own, other] for own, other in zip((w_out, w_up, w_down), gather_pieces(pieces))
         )
-        wdown_slots = [w_down] + gather_pieces([down_piece])
         wproj = jnp.concatenate(in_order([w_proj, proj_other]), axis=0)
         packs = [packed, pack_other.reshape(-1)]
     else:
@@ -1312,6 +1249,8 @@
     query_places = jnp.arange(Q, dtype=jnp.int32)
     position = jnp.concatenate([query_places % QLEN, places - slot_begin])
     cosine, sine = rotary_tables(position)
+    share = D // R
+    paired = share == 64
     segment = jnp.concatenate([(query_places // QLEN) % SEGMENTS, slot_id])
     lane = jnp.arange(128, dtype=jnp.int32)[None, :] % DH
     same = segment[:, None] == lane
@@ -1349,7 +1288,9 @@
         attended.append(out)
         rests.append(rest)
         exts.append(ext)
-    normed_one, inverse_one, hidden_low, hidden_t = out_and_norm(x, vectors, attended, wout_slots)
+    normed_one, inverse_one, hidden_low, hidden_left = out_and_norm(
+        x, vectors, attended, wout_slots, paired
+    )
     active, slopes = zip(*[up_and_gelu(hidden_low, wup_slots[k], bup_slots[k]) for k in range(C)])
     normed_two, inverse_two, output_low, unit, unit_low, unit_inverse = down_and_norm(
         normed_one, vectors, wproj, active, wdown_slots
@@ -1360,7 +1301,7 @@
         in_order([unit_low[:Q]] + [shift_cols(unit_low[:Q], k) for k in range(1, C)]), axis=0
     )
     sims = score_forward(lows, highs, doc_tile, query_tile, picks)
-    scores = sims.reshape(tile_docs, queries_here).T
+    scores = sims.T
 
     scale = jnp.exp(log_scale[0])
     z = scale * scores
@@ -1378,7 +1319,7 @@
     loss = log_total - jnp.sum(stats[:, 2], axis=0)
     dz = (jnp.exp(z - log_total[:, None]) - is_label.astype(F32)) / (queries_here * R)
     scale_part = jnp.sum(dz * z)
-    dscores = (scale * dz).T.reshape(R, docs, queries_here)
+    dscores = (scale * dz).T
     doc_grad, query_grad_t = score_backward(lows, highs, doc_tile, query_tile, picks, dscores)
     query_parts = query_grad_t.T.reshape(C, Q, 128)
 
@@ -1394,31 +1335,27 @@
 
     core = r % 2
     slots_back = range(C - 1, -1, -1)
-    share = D // R
     x_bit, *z_bits = [1 << b for b in range(1, R.bit_length() - 1)]
+    half = D // 2
 
     def side_of(bit):
         return ((r // bit) % 2).astype(jnp.int32)
 
-    keep_places = jnp.stack([core, side_of(z_bits[0])]).astype(jnp.int32)
-    send_places = jnp.stack([1 - core, 0 * core]).astype(jnp.int32)
-
-    def halves_of(left_t):
-        return left_t.reshape(R // 2, 2, share, n)
-
-    def send_half(lefts, rights):
-        return swap_rows(weight_pull(send_places, lefts, rights)[0], 1)
-
-    def rows_of(left, side):
-        return lax.dynamic_index_in_dim(left, side, 1, keepdims=False).reshape(-1, n)
+    def core_order(left):
+        if paired:
+            return left
+        return left.reshape(n, R // 2, 2, share).transpose(0, 2, 1, 3).reshape(n, D)
+
+    def columns_of(left, side):
+        return lax.dynamic_slice_in_dim(left, side * half, half, 1)
 
     def send_plain(left, right):
-        part = mm(rows_of(left, 1 - core), right).astype(BF16)
+        part = mm(columns_of(left, 1 - core), right, TN).astype(BF16)
         Order.last += (part,)
         return swap_rows(part, 1)
 
     def keep_plain(left, right, arrived, k):
-        kept = mm(rows_of(left, core), right) + arrived.astype(F32)
+        kept = mm(columns_of(left, core), right, TN) + arrived.astype(F32)
         if k > 0:
             kept = kept.astype(BF16)
         Order.last += (kept,)
@@ -1437,10 +1374,10 @@
             rest = rest.astype(F32) + other.astype(F32)
         return kept[0], rest
 
-    embed_grad, resid_two_grad, branch, branch_t, head_sums = head_pull(
-        unit_grad, unit, unit_inverse, wproj, normed_two, inverse_two, vectors
-    )
-    down_left, down_right = halves_of(branch_t), active
+    embed_grad, resid_two_grad, branch, branch_left, head_sums = head_pull(
+        unit_grad, unit, unit_inverse, wproj, normed_two, inverse_two, vectors, paired
+    )
+    down_left, down_right = core_order(branch_left), active
     pre_grads, up_sums, down_kept = [None] * C, [None] * C, [None] * C
     down_arrived = [None] * C
     for k in slots_back:
@@ -1449,22 +1386,22 @@
         pre_grads[k], up_sums[k] = up_pull(branch, wdown_slots[k], slopes[k])
         if k > 0:
             down_kept[k] = keep_plain(down_left, down_right[k], down_arrived[k], k)
-    up_left, up_right = halves_of(hidden_t), pre_grads
+    up_left, up_right = core_order(hidden_left), pre_grads
     up_arrived, up_kept = [None] * C, [None] * C
     for k in slots_back:
         up_arrived[k] = send_plain(up_left, up_right[k])
     down_kept[0] = keep_plain(down_left, down_right[0], down_arrived[0], 0)
     for k in slots_back[:-1]:
         up_kept[k] = keep_plain(up_left, up_right[k], up_arrived[k], k)
-    resid_one_grad, branch_one_t, hidden_sums, *attended_grads = hidden_pull(
-        resid_two_grad, normed_one, inverse_one, vectors, pre_grads, wup_slots, wout_slots
+    resid_one_grad, branch_one_left, hidden_sums, *attended_grads = hidden_pull(
+        resid_two_grad, normed_one, inverse_one, vectors, pre_grads, wup_slots, wout_slots, paired
     )
     up_kept[0] = keep_plain(up_left, up_right[0], up_arrived[0], 0)
     mixed_grads, mixed_sums = [None] * C, [None] * C
-    late_lefts, late_state, late_arrived = [halves_of(x.T), halves_of(branch_one_t)], [None] * C, [None] * C
-
-    def late_rights(k):
-        return [mixed_grads[k], attended[k][None]]
+    x_left = x.reshape(n, R // 2, 2, share).transpose(0, 2, 1, 3).reshape(n, D)
+    late_lefts = [x_left, core_order(branch_one_left)]
+    span = min(width, ATTENTION_LANES)
+    late_state, late_arrived = [None] * C, [None] * C
 
     def gather_small():
         proj_grad = mm(embed_grad, output_low, TN).reshape(R, -1, C, width)
@@ -1494,40 +1431,66 @@
             spans, qkv[k], exts[k], attended[k], rests[k], attended_grads[k], ext_k, cosine, sine,
             tile,
         )
-        late_arrived[k] = send_half(late_lefts, late_rights(k))
+
+    def late_product(columns, k):
+        right = mixed_grads[k]
+        parts = []
+        for first in range(0, width, span):
+            at = 4 * first
+            parts.append(mm(columns[0], right[:, at : at + 3 * span], TN))
+            parts.append(mm(columns[1], right[:, at + 3 * span : at + 4 * span], TN))
+        return jnp.concatenate(parts, axis=1)
+
+    def send_late(k):
+        part = late_product([columns_of(left, 1 - core) for left in late_lefts], k).astype(BF16)
+        Order.last += (part,)
+        late_arrived[k] = swap_rows(part, 1)
 
     def keep_late(k):
-        send, keep = weight_pull(
-            keep_places, late_lefts, late_rights(k), late_arrived[k], inner=2 * share
-        )
-        late_state[k] = (keep, swap_rows(send, z_bits[0]))
+        total = late_product([columns_of(left, core) for left in late_lefts], k)
+        total = (total + late_arrived[k].astype(F32)).reshape(-1, 2, 2 * share, 4 * width)
+        side = side_of(z_bits[0])
+        part = lax.dynamic_index_in_dim(total, 1 - side, 1, keepdims=False).astype(BF16)
+        kept = lax.dynamic_index_in_dim(total, side, 1, keepdims=False)
+        part, kept = (v.reshape(1, half // 2, 4 * width) for v in (part, kept))
+        Order.last += (part, kept)
+        late_state[k] = (kept, swap_rows(part, z_bits[0]))
 
     for k in slots_back[:-1]:
         pull_attention(k)
+        send_late(k)
     wide_state = next_fold([cols_state(down_kept), cols_state(up_kept)], x_bit, share)
     pull_attention(0)
+    wide_state = next_fold([wide_state], z_bits[0], share)
+    send_late(0)
     for k in slots_back[:-1]:
         keep_late(k)
-    wide_state = next_fold([wide_state], z_bits[0], share)
     sent = [
         shift_cols(token_pull((c + k) % C, resid_one_grad, mixed_grads, wqkv_slots, BF16), k)
         for k in range(1, C)
     ]
     keep_late(0)
+    late_bits = z_bits[1:] + [x_bit]
+
+    def fold_late(k, bit):
+        late_state[k] = next_fold([late_state[k]], bit, share if bit == x_bit else 2 * share)
+
     for k in slots_back[:-1]:
-        late_state[k] = next_fold([late_state[k]], (z_bits + [x_bit])[1], 2 * share)
+        fold_late(k, late_bits[0])
     own_tokens = token_pull(c, resid_one_grad, mixed_grads, wqkv_slots, F32)
+    for place, bit in enumerate(late_bits):
+        fold_late(0, bit)
+        if place < len(z_bits) - 1:
+            wide_state = next_fold([wide_state], z_bits[place + 1], share)
+        for k in slots_back[:-1]:
+            if place + 1 < len(late_bits):
+                fold_late(k, late_bits[place + 1])
     small = small_sum(R, C, gather_small())
-    for bit in z_bits[2:] + [x_bit]:
-        for k in slots_back[:-1]:
-            late_state[k] = next_fold([late_state[k]], bit, share if bit == x_bit else 2 * share)
-    for bit in z_bits[1:] + [x_bit]:
-        late_state[0] = next_fold([late_state[0]], bit, share if bit == x_bit else 2 * share)
-        if bit != x_bit:
-            wide_state = next_fold([wide_state], bit, share)
     late_grad = close(late_state[0])
     for k in slots_back[:-1]:
         late_grad = late_grad + shift_cols(close(late_state[k]).astype(BF16), C - k).astype(F32)
+    late_grad = late_grad[0].reshape(share, width // span, 4, span).transpose(2, 0, 1, 3)
+    late_grad = late_grad.reshape(4, share, width)
     qkv_grad, out_grad = late_grad[:3], late_grad[3]
     down_grad, up_grad = close(wide_state)
     ordered = in_order([own_tokens] + [s.astype(F32) for s in sent])

time: 902 us -> 938 us (1.040)
  Pallas kernels: 692 us -> 605 us
  starting transfers between devices: 16.3 us -> 72.5 us
  matrix products: 56.7 us -> 92.8 us
  waiting for transfers between devices: 33 us -> 46.6 us
  other arithmetic: 30.9 us -> 41.7 us
    pallas_call x33 -> x29, Pallas kernels: 692 us -> 605 us  [call(): pl.pallas_call(wrapped, grid_spec=pltpu.PrefetchScalarGridSpec(num_scalar...]
    ppermute x15, starting transfers between devices: 9.85 us -> 50.3 us  [swap_rows(): return lax.ppermute(value, 'rows', [(i, i ^ bit) for i in range(R)])]
    dot_general x9 -> x25, matrix products: 56.7 us -> 92.8 us  [mm(): return lax.dot_general(left, right, dims, preferred_element_type=F32)]
    ppermute x7, starting transfers between devices: 6.43 us -> 22.1 us  [shift_cols(): return lax.ppermute(value, 'cols', [(i, (i + k) % C) for i in range(C)])]
    ppermute x15, waiting for transfers between devices: 30 us -> 41.6 us  [swap_rows(): return lax.ppermute(value, 'rows', [(i, i ^ bit) for i in range(R)])]
  transfers between devices with their start and end apart: 23 -> 25, of which waited for: 3 -> 4; matrix products, arithmetic and copies ran while one was open for 12% -> 15% of each run, Pallas kernels for 57% -> 42%
where the time goes in v5:
time: 938 us; the launch traced here: 926 us
  Pallas kernels  605 us (64%)
  matrix products  92.8 us (10%)
  starting transfers between devices  72.5 us (8%)
  local copies, waits for them, and re-layouts  51.9 us (6%)
  waiting for transfers between devices  46.6 us (5%)
  other arithmetic  41.7 us (4%)
  between operations  15.9 us (2%)
    pallas_call x29, Pallas kernels, call(): pl.pallas_call(wrapped, grid_spec=pltpu.PrefetchScalarGridSpec(num_scalar...  605 us
    dot_general x25, matrix products, mm(): return lax.dot_general(left, right, dims, preferred_element_type=F32)  92.8 us
    ppermute x15, starting transfers between devices, swap_rows(): return lax.ppermute(value, 'rows', [(i, i ^ bit) for i in range(R)])  50.3 us
    ppermute x15, waiting for transfers between devices, swap_rows(): return lax.ppermute(value, 'rows', [(i, i ^ bit) for i in range(R)])  41.6 us
    ppermute x7, starting transfers between devices, shift_cols(): return lax.ppermute(value, 'cols', [(i, (i + k) % C) for i in range(C)])  22.1 us
  transfers between devices with their start and end apart: 25, of which 4 were waited for; matrix products, arithmetic and copies ran while one was open for 15% of the time, Pallas kernels for 42%

profile of v5, /device:TPU:0, one launch (start us, length us, event | category | flops | bytes accessed | tf_op | source)
XLA Modules:
  0.0 926.4 jit_solution(10688990249742224809)
XLA Ops:
  13.5 60.7 %start_up.1 = (bf16[1536,1024]{1,0:T(8,128)(2,1)}, bf16[16,192,512]{2,1,0:T(8,128)(2,1)}, bf16[32,1024]{1,0:T(8,128)(2,1)}, bf16[64,2048]{1,0:T(8,128)(2,1)}, bf...) custom-call(bf16[3072,512]{1,0:T(8,128)(2,1)} %refs_0_.1, bf16[16,192,512]{2,1,0:T(8,128)(2,1)} %bitcast.134, ...), custom_call_target="tpu_custom_call" | custom-call | bytes 1024 | tf_op jit(solution)/shard_map/start_up/pallas_call | solution.py:60
  84.0 5.9 fusion.78.refs_5_.refs_4_
  89.9 2.8 fusion.79
  95.9 13.8 %project_qkv.2.refs_1_.refs_4_ = bf16[3,1536,512]{2,1,0:T(8,128)(2,1)} custom-call(bf16[1536,1024]{1,0:T(8,128)(2,1)} %get-tuple-element.78.refs_0_, bf16[3,1024,512]{2,1,0:T(8,128)(2,1)} %refs_4_.5, f32[3,512]{1,0:T(4,128)} %refs_2_.1, f32[1536,128]{1,0:T(8,128)} %pad_maximum_fusion.3.refs_3_.refs_7_, f32[1536,128]{1,0:T(8,128)} %pad_maximum_fusion.4.refs_4_.refs_8_, ...), custom_call_target="tpu_custom_call" | custom-call | flops 4831838208 | bytes 12589056 | tf_op jit(solution)/shard_map/project_qkv/pallas_call | solution.py:60
  111.7 36.3 %attention_forward.2 = (bf16[1536,512]{1,0:T(8,128)(2,1)}, bf16[1536,512]{1,0:T(8,128)(2,1)}, bf16[1536,512]{1,0:T(8,128)(2,1)}) custom-call(s32[12]{0:T(128)} %pad_add_fusion.1.refs_0_, bf16[3,1536,512]{2,1,0:T(8,128)(2,1)} %project_qkv.2.refs_1_.refs_4_, bf16[1536,128]{1,0:T(8,128)(2,1)} %fusion.68.refs_2_.refs_6_, ...), custom_call_target="tpu_custom_call" | custom-call | bytes 1024 | tf_op jit(solution)/shard_map/attention_forward/pallas_call | solution.py:60
  148.0 13.8 %project_qkv.3.refs_1_.refs_4_ = bf16[3,1536,512]{2,1,0:T(8,128)(2,1)} custom-call(bf16[1536,1024]{1,0:T(8,128)(2,1)} %get-tuple-element.78.refs_0_, bf16[3,1024,512]{2,1,0:T(8,128)(2,1)} %bitcast.149, f32[3,512]{1,0:T(4,128)} %slice.306.refs_2_, f32[1536,128]{1,0:T(8,128)} %pad_maximum_fusion.3.refs_3_.refs_7_, ...), custom_call_target="tpu_custom_call" | custom-call | flops 4831838208 | bytes 12589056 | tf_op jit(solution)/shard_map/project_qkv/pallas_call | solution.py:60
  161.8 26.5 %attention_forward.3 = (bf16[1536,512]{1,0:T(8,128)(2,1)}, bf16[1536,512]{1,0:T(8,128)(2,1)}, bf16[1536,512]{1,0:T(8,128)(2,1)}) custom-call(s32[12]{0:T(128)} %pad_add_fusion.1.refs_0_, bf16[3,1536,512]{2,1,0:T(8,128)(2,1)} %project_qkv.3.refs_1_.refs_4_, bf16[1536,128]{1,0:T(8,128)(2,1)} %fusion.68.refs_2_.refs_6_, ...), custom_call_target="tpu_custom_call" | custom-call | bytes 1024 | tf_op jit(solution)/shard_map/attention_forward/pallas_call | solution.py:60
  189.9 11.9 %out_and_norm.1 = (f32[1536,1024]{1,0:T(8,128)}, f32[1536,1]{1,0:T(8,128)}, bf16[1536,1024]{1,0:T(8,128)(2,1)}, bf16[1536,1024]{1,0:T(8,128)(2,1)}) custom-call(bf16[1536,1024]{1,0:T(8,128)(2,1)} %get-tuple-element.78.refs_0_, f32[8,1024]{1,0:T(8,128)} %stack.63.refs_1_.refs_6_.refs_3_, bf16[1536,512]{1,0:T(8,128)(2,1)} %get-tuple-element.80.refs_5_.refs_2_.refs_3_, ...), custom_call_target="tpu_custom_call" | custom-call | flops 3221225472 | bytes 21010432 | tf_op jit(solution)/shard_map/out_and_norm/pallas_call | solution.py:60
  201.8 22.5 %up_and_gelu.2 = (bf16[1536,2048]{1,0:T(8,128)(2,1)}, f32[1536,2048]{1,0:T(8,128)}) custom-call(bf16[1536,1024]{1,0:T(8,128)(2,1)} %get-tuple-element.86.refs_0_, bf16[1024,2048]{1,0:T(8,128)(2,1)} %refs_6_.1, f32[1,2048]{1,0:T(1,128)} %bitcast.199, f32[1536,1]{1,0:T(8,128)} %get-tuple-element.87.refs_3_.refs_2_), custom_call_target="tpu_custom_call" | custom-call | flops 16106127360 | bytes 26222592 | tf_op jit(solution)/shard_map/up_and_gelu/pallas_call | solution.py:60
  224.3 22.7 %up_and_gelu.3 = (bf16[1536,2048]{1,0:T(8,128)(2,1)}, f32[1536,2048]{1,0:T(8,128)}) custom-call(bf16[1536,1024]{1,0:T(8,128)(2,1)} %get-tuple-element.86.refs_0_, bf16[1024,2048]{1,0:T(8,128)(2,1)} %all-gather.6.cloned.1.call-done.refs_1_.refs_7_, f32[1,2048]{1,0:T(1,128)} %bitcast.200, bf16[1536,2048]{1,0:T(8,128)(2,1)} %get-tuple-element.88.refs_3_), custom_call_target="tpu_custom_call" | custom-call | flops 16106127360 | bytes 26222592 | tf_op jit(solution)/shard_map/up_and_gelu/pallas_call | solution.py:60
  247.0 24.7 %down_and_norm.1 = (f32[1536,1024]{1,0:T(8,128)}, f32[1536,1]{1,0:T(8,128)}, bf16[1536,1024]{1,0:T(8,128)(2,1)}, f32[1536,128]{1,0:T(8,128)}, bf16[1536,128]{1,0:T(8,128)(2,1)}, /*index=5*/f32[1536,1]{1,0:T(8,128)}) custom-call(f32[1536,1024]{1,0:T(8,128)} %get-tuple-element.84.refs_0_.refs_1_, f32[8,1024]{1,0:T(8,128)} %stack.63.refs_1_.refs_6_.refs_3_, ...), custom_call_target="tpu_custom_call" | custom-call | flops 12884901888 | bytes 38187008 | tf_op jit(solution)/shard_map/down_and_norm/pallas_call | solution.py:60
  274.4 42.4 %gather_rows.1.refs_5_ = bf16[16,1024,128]{2,1,0:T(8,128)(2,1)} custom-call(bf16[1024,128]{1,0:T(8,128)(2,1)} %slice.249.refs_0_, f32[1536,1]{1,0:T(8,128)} %get-tuple-element.93.refs_1_.refs_5_), custom_call_target="tpu_custom_call" | custom-call | bytes 1024 | tf_op jit(solution)/shard_map/gather_rows/pallas_call | solution.py:60
  318.5 34.3 %score_forward.1.refs_6_ = f32[64,32]{1,0:T(8,128)} custom-call(s32[512]{0:T(512)} %reshape.336.refs_6_.refs_0_, s32[512]{0:T(512)} %sub.119.refs_7_.refs_1_, bf16[16384,128]{1,0:T(8,128)(2,1)} %bitcast.165, bf16[1024,128]{1,0:T(8,128)(2,1)} %pad_maximum_fusion.7.refs_3_, s32[16,4,1024]{2,1,0:T(4,128)} %fusion.78.refs_5_.refs_4_, ...), custom_call_target="tpu_custom_call" | custom-call | flops 4294967296 | bytes 4730880 | tf_op jit(solution)/shard_map/score_forward/pallas_call | solution.py:60
  354.4 3.6 collective-permute-done.1
  360.0 34.9 %score_backward.1 = (f32[16384,128]{1,0:T(8,128)}, f32[128,1024]{1,0:T(8,128)}) custom-call(s32[512]{0:T(512)} %reshape.336.refs_6_.refs_0_, s32[512]{0:T(512)} %sub.119.refs_7_.refs_1_, bf16[16384,128]{1,0:T(8,128)(2,1)} %bitcast.166, bf16[1024,128]{1,0:T(8,128)(2,1)} %pad_maximum_fusion.7.refs_3_, s32[16,4,1024]{2,1,0:T(4,128)} %fusion.78.refs_5_.refs_4_, ...), custom_call_target="tpu_custom_call" | custom-call | flops 8589934592 | bytes 13643776 | tf_op jit(solution)/shard_map/score_backward/pallas_call | solution.py:60
  396.9 3.2 copy.110
  402.7 38.7 %scatter_rows.1.refs_7_ = f32[1024,128]{1,0:T(8,128)} custom-call(f32[16,1024,128]{2,1,0:T(8,128)} %bitcast.152, f32[128,1024]{1,0:T(8,128)} %get-tuple-element.94.refs_1_), custom_call_target="tpu_custom_call" | custom-call | bytes 1024 | tf_op jit(solution)/shard_map/scatter_rows/pallas_call | solution.py:60
  443.2 2.2 pad_maximum_fusion.5.refs_0_
  445.4 12.8 %head_pull.1 = (bf16[1536,128]{1,0:T(8,128)(2,1)}, f32[1536,1024]{1,0:T(8,128)}, bf16[1536,1024]{1,0:T(8,128)(2,1)}, bf16[1536,1024]{1,0:T(8,128)(2,1)}, f32[8,1024]{1,0:T(8,128)}) custom-call(f32[1536,128]{1,0:T(8,128)} %pad_maximum_fusion.5.refs_0_, f32[1536,128]{1,0:T(8,128)} %get-tuple-element.96.refs_1_, f32[1536,1]{1,0:T(8,128)} %get-tuple-element.97.refs_2_, ...), custom_call_target="tpu_custom_call" | custom-call | flops 805306368 | bytes 21180416 | tf_op jit(solution)/shard_map/head_pull/pallas_call | solution.py:60
  458.3 6.3 convolution_convert_fusion.2.refs_5_
  464.5 6.7 convolution_convert_fusion.3.refs_4_
  473.9 13.7 %up_pull.2 = (bf16[1536,2048]{1,0:T(8,128)(2,1)}, f32[8,2048]{1,0:T(8,128)}) custom-call(bf16[1536,1024]{1,0:T(8,128)(2,1)} %get-tuple-element.100.refs_0_, bf16[2048,1024]{1,0:T(8,128)(2,1)} %all-gather.8.cloned.1.call-done.refs_6_.refs_1_, f32[1536,2048]{1,0:T(8,128)} %get-tuple-element.102.refs_2_, f32[8,1024]{1,0:T(8,128)} %get-tuple-element.103.refs_3_, ...), custom_call_target="tpu_custom_call" | custom-call | flops 6442450944 | bytes 26279936 | tf_op jit(solution)/shard_map/up_pull/pallas_call | solution.py:60
  488.5 7.9 convolution_convert_fusion.1.refs_11_
  496.4 7.9 add_convert_fusion.1.refs_4_
  505.1 13.7 %up_pull.3 = (bf16[1536,2048]{1,0:T(8,128)(2,1)}, f32[8,2048]{1,0:T(8,128)}) custom-call(bf16[1536,1024]{1,0:T(8,128)(2,1)} %get-tuple-element.100.refs_0_, bf16[2048,1024]{1,0:T(8,128)(2,1)} %refs_1_.5, f32[1536,2048]{1,0:T(8,128)} %get-tuple-element.101.refs_2_, f32[8,2048]{1,0:T(8,128)} %get-tuple-element.105.refs_3_, ...), custom_call_target="tpu_custom_call" | custom-call | flops 6442450944 | bytes 26279936 | tf_op jit(solution)/shard_map/up_pull/pallas_call | solution.py:60
  518.8 8.2 convolution_convert_fusion.refs_12_
  527.2 6.1 add_convert_fusion.refs_14_
  535.5 6.2 convert_add_fusion.1.refs_13_
  541.8 30.3 %hidden_pull.1 = (f32[1536,1024]{1,0:T(8,128)}, bf16[1536,1024]{1,0:T(8,128)(2,1)}, f32[8,1024]{1,0:T(8,128)}, bf16[1536,512]{1,0:T(8,128)(2,1)}, bf16[1536,512]{1,0:T(8,128)(2,1)}) custom-call(f32[1536,1024]{1,0:T(8,128)} %get-tuple-element.99.refs_0_, f32[1536,1024]{1,0:T(8,128)} %get-tuple-element.84.refs_0_.refs_1_, ...), custom_call_target="tpu_custom_call" | custom-call | bytes 1024 | tf_op jit(solution)/shard_map/hidden_pull/pallas_call | solution.py:60
  573.2 9.3 %convert_add_fusion.refs_10_ = f32[512,2048]{1,0:T(8,128)} fusion(bf16[512,2048]{1,0:T(8,128)(2,1)} %collective-permute-done.6, bf16[1536,2048]{1,0:T(8,128)(2,1)} %get-tuple-element.106.refs_4_, bf16[1536,1024]{1,0:T(8,128)(2,1)} %get-tuple-element.109, s32[]{:T(128)S(6)} %select_n.285), kind=kOutput, calls=%fused_computation.3 | convolution fusion | flops 3223322624 | bytes 14155780 | tf_op jit(solution)/shard_map/dot_general | solution.py:23
  582.6 39.3 %attention_backward.2 = (bf16[1536,2048]{1,0:T(8,128)(2,1)}, f32[8,512]{1,0:T(8,128)}) custom-call(s32[12]{0:T(128)} %pad_add_fusion.1.refs_0_, bf16[3,1536,512]{2,1,0:T(8,128)(2,1)} %project_qkv.3.refs_1_.refs_4_, bf16[1536,512]{1,0:T(8,128)(2,1)} %get-tuple-element.114.refs_2_, bf16[1536,512]{1,0:T(8,128)(2,1)} %get-tuple-element.82.refs_3_.refs_6_, ...), custom_call_target="tpu_custom_call" | custom-call | bytes 1024 | tf_op jit(solution)/shard_map/attention_backward/pallas_call | solution.py:60
  636.4 8.5 fold.7
  644.9 39.2 %attention_backward.3 = (bf16[1536,2048]{1,0:T(8,128)(2,1)}, f32[8,512]{1,0:T(8,128)}) custom-call(s32[12]{0:T(128)} %pad_add_fusion.1.refs_0_, bf16[3,1536,512]{2,1,0:T(8,128)(2,1)} %project_qkv.2.refs_1_.refs_4_, bf16[1536,512]{1,0:T(8,128)(2,1)} %get-tuple-element.111.refs_2_, bf16[1536,512]{1,0:T(8,128)(2,1)} %get-tuple-element.80.refs_5_.refs_2_.refs_3_, ...), custom_call_target="tpu_custom_call" | custom-call | bytes 1024 | tf_op jit(solution)/shard_map/attention_backward/pallas_call | solution.py:60
  686.1 2.6 convolution_convert_fusion.5
  688.7 2.3 fusion.25
  691.0 2.3 fusion.22
  694.8 7.6 collective-permute-start.9
  703.7 3.2 pad_maximum_fusion.2.refs_7_
  708.5 2.4 fusion.50
  710.9 4.5 fusion.4
  715.4 2.6 fusion
  718.1 2.6 fusion.12
  723.6 10.6 %collective-permute-done.11.refs_2_ = bf16[2,256,2048]{2,1,0:T(8,128)(2,1)} collective-permute-done((bf16[2,256,2048]{2,1,0:T(8,128)(2,1)}, bf16[2,256,2048]{2,1,0:T(8,128)(2,1)}, u32[]{:S(2)}, u32[]{:S(2)}) %collective-permute-start.11) | collective-permute-done | bytes 2097184 | tf_op jit(solution)/shard_map/ppermute | solution.py:1167
  734.2 5.1 fold.8
  739.4 2.2 maximum_add_fusion
  745.3 12.4 %token_pull.2.refs_3_ = bf16[1536,512]{1,0:T(8,128)(2,1)} custom-call(s32[1]{0:T(128)} %bitcast.45.refs_0_, f32[1536,1024]{1,0:T(8,128)} %get-tuple-element.110.refs_1_, bf16[1536,2048]{1,0:T(8,128)(2,1)} %get-tuple-element.122.refs_2_, bf16[1536,2048]{1,0:T(8,128)(2,1)} %get-tuple-element.119.refs_3_, bf16[3,1024,512]{2,1,0:T(8,128)(2,1)} %refs_4_.5, ...), custom_call_target="tpu_custom_call" | custom-call | flops 4831838208 | bytes 26738692 | tf_op jit(solution)/shard_map/token_pull/pallas_call | solution.py:60
  757.8 17.1 %collective-permute-start.13 = (bf16[1536,512]{1,0:T(8,128)(2,1)}, bf16[1536,512]{1,0:T(8,128)(2,1)}, u32[]{:S(2)}, u32[]{:S(2)}) collective-permute-start(bf16[1536,512]{1,0:T(8,128)(2,1)} %token_pull.2.refs_3_), channel_id=1, source_target_pairs={{0,1},{1,0},{2,3},{3,2},{4,5},{5,4},{6,7},{7,6},{8,9},{9,8},{10,11... | collective-permute-start | bytes 4718600 | tf_op jit(solution)/shard_map/ppermute | solution.py:1164
  774.9 2.2 maximum_add_fusion.1
  777.2 2.1 copy-done.3
  781.6 3.2 constant_dynamic-slice_fusion.2
  784.8 2.8 fold.9
  787.6 20.6 %collective-permute-start.16 = (bf16[1,128,2048]{2,1,0:T(8,128)(2,1)}, bf16[1,128,2048]{2,1,0:T(8,128)(2,1)S(1)}, u32[]{:S(2)}, u32[]{:S(2)}) collective-permute-start(bf16[1,128,2048]{2,1,0:T(8,128)(2,1)} %get-tuple-element.126.refs_6_), channel_id=1, source_target_pairs={{0,16},{2,18},{4,20},{6,22},{8,24},{10,26},{12,28},{14,30},{16,0},... | collective-permute-start | bytes 1572872 | tf_op jit(solution)/shard_map/ppermute | solution.py:1167
  808.3 12.7 %token_pull.3.refs_3_ = f32[1536,512]{1,0:T(8,128)} custom-call(s32[1]{0:T(128)} %bitcast.28.refs_0_, f32[1536,1024]{1,0:T(8,128)} %get-tuple-element.110.refs_1_, bf16[1536,2048]{1,0:T(8,128)(2,1)} %get-tuple-element.122.refs_2_, bf16[1536,2048]{1,0:T(8,128)(2,1)} %get-tuple-element.119.refs_3_, bf16[3,1024,512]{2,1,0:T(8,128)(2,1)} %refs_4_.5, ...), custom_call_target="tpu_custom_call" | custom-call | flops 4831838208 | bytes 28311556 | tf_op jit(solution)/shard_map/token_pull/pallas_call | solution.py:60
  821.0 2.8 fold.10
  823.8 15.8 %collective-permute-start.15 = (bf16[1,128,2048]{2,1,0:T(8,128)(2,1)}, bf16[1,128,2048]{2,1,0:T(8,128)(2,1)}, u32[]{:S(2)}, u32[]{:S(2)}) collective-permute-start(bf16[1,128,2048]{2,1,0:T(8,128)(2,1)} %get-tuple-element.128.refs_3_), channel_id=1, source_target_pairs={{0,16},{2,18},{4,20},{6,22},{8,24},{10,26},{12,28},{14,30},{16,0},... | collective-permute-start | bytes 1572872 | tf_op jit(solution)/shard_map/ppermute | solution.py:1167
  839.6 3.9 fold.11
  843.7 2.3 convert_select_fusion.1
  847.3 2.2 fold.12
  850.1 24.9 %collective-permute-done.15.refs_2_ = bf16[1,128,2048]{2,1,0:T(8,128)(2,1)} collective-permute-done((bf16[1,128,2048]{2,1,0:T(8,128)(2,1)}, bf16[1,128,2048]{2,1,0:T(8,128)(2,1)}, u32[]{:S(2)}, u32[]{:S(2)}) %collective-permute-start.15) | collective-permute-done | bytes 524320 | tf_op jit(solution)/shard_map/ppermute | solution.py:1167
  875.0 2.2 fold.13
  878.0 6.1 collective-permute-done.21
  885.3 3.1 pad_maximum_fusion
  888.4 2.7 collective-permute-start.20
  892.2 20.1 %small_sum.1 = f32[8,640]{1,0:T(8,128)} custom-call(f32[8,2,2,8,640]{4,3,2,1,0:T(8,128)} %reshape.365.refs_0_, bf16[1,64,2048]{2,1,0:T(8,128)(2,1)} %get-tuple-element.134.refs_1_), custom_call_target="tpu_custom_call" | custom-call | bytes 1024 | tf_op jit(solution)/shard_map/small_sum/pallas_call | solution.py:60
  (298 shorter events, 86.1 us)
Async XLA Ops:
  7.2 182.7 %all-gather.4.cloned.1.call-start = ((), (), s32[]{:S(2)}) async-start(), calls=%async_computation | async-start | bytes 1114112 | tf_op jit(solution)/shard_map/all_gather | solution.py:1186
  13.5 62.4 %copy-start.33 = (s32[16,2,4]{0,2,1:T(4,128)S(1)}, s32[16,2,4]{0,2,1:T(4,128)}, u32[]{:S(2)}) copy-start(s32[16,2,4]{0,2,1:T(4,128)} %param.19) | copy-start | bytes 1540
  13.5 67.1 %copy-start.24 = (s32[32,64,32]{1,2,0:T(8,128)S(1)}, s32[32,64,32]{1,2,0:T(8,128)}, u32[]{:S(2)}) copy-start(s32[32,64,32]{1,2,0:T(8,128)} %param.20) | copy-start | bytes 786436
  74.2 150.1 %all-gather.6.cloned.1.call-start = ((), (), s32[]{:S(2)}) async-start(), calls=%async_computation.1 | async-start | bytes 4456448 | tf_op jit(solution)/shard_map/all_gather | solution.py:1186
  75.0 172.0 %all-gather.8.cloned.1.call-start = ((), (), s32[]{:S(2)}) async-start(), calls=%async_computation.2 | async-start | bytes 4456448 | tf_op jit(solution)/shard_map/all_gather | solution.py:1186
  161.8 27.3 %copy-start.23 = (bf16[512,128]{1,0:T(8,128)(2,1)S(1)}, bf16[512,128]{1,0:T(8,128)(2,1)}, u32[]{:S(2)}) copy-start(bf16[512,128]{1,0:T(8,128)(2,1)} %refs_5_.2) | copy-start | bytes 393220
  161.8 27.3 %copy-start.32 = (bf16[512,128]{1,0:T(8,128)(2,1)S(1)}, bf16[512,128]{1,0:T(8,128)(2,1)}, u32[]{:S(2)}) copy-start(bf16[512,128]{1,0:T(8,128)(2,1)} %get-tuple-element.85) | copy-start | bytes 393220
  247.0 25.7 %copy-start.38 = (s32[32]{0:T(128)S(1)}, s32[32]{0:T(128)}, u32[]{:S(2)}) copy-start(s32[32]{0:T(128)} %param.21) | copy-start | bytes 388
  272.6 44.2 %collective-permute-start = (bf16[512,128]{1,0:T(8,128)(2,1)S(1)}, bf16[512,128]{1,0:T(8,128)(2,1)S(1)}, u32[]{:S(2)}, u32[]{:S(2)}) collective-permute-start(bf16[512,128]{1,0:T(8,128)(2,1)S(1)} %slice.250), channel_id=1, source_target_pairs={{0,1},{1,0},{2,3},{3,2},{4,5},{5,4},{6,7},{7,6},{8,9},{9,8},{10,11... | collective-permute-start | bytes 393224 | tf_op jit(solution)/shard_map/ppermute | solution.py:1164
  354.4 3.7 collective-permute-start.1
  396.2 45.9 %collective-permute-start.2 = (f32[512,128]{1,0:T(8,128)S(1)}, f32[512,128]{1,0:T(8,128)}, u32[]{:S(2)}, u32[]{:S(2)}) collective-permute-start(f32[512,128]{1,0:T(8,128)S(1)} %dynamic-slice_bitcast_fusion), channel_id=1, source_target_pairs={{0,1},{1,0},{2,3},{3,2},{4,5},{5,4},{6,7},{7,6},{8,9},{9,8},{10,11... | collective-permute-start | bytes 786440 | tf_op jit(solution)/shard_map/ppermute | solution.py:1164
  402.7 39.4 %copy-start.12 = (f32[1024,128]{1,0:T(8,128)S(1)}, f32[1024,128]{1,0:T(8,128)}, u32[]{:S(2)}) copy-start(f32[1024,128]{1,0:T(8,128)} %copy-done.11) | copy-start | bytes 1572868
  442.1 16.1 %slice-start.6 = ((s8[6291456]{0:T(1024)(128)(4,1)}), s8[4194304]{0:T(1024)(128)(4,1)S(1)}, s32[]{:S(2)}) async-start(s8[6291456]{0:T(1024)(128)(4,1)} %bitcast.155), calls=%async_computation.9 | async-start | bytes 8388608
  445.4 12.8 %slice-start.7 = ((s8[6291456]{0:T(1024)(128)(4,1)}), s8[2097152]{0:T(1024)(128)(4,1)S(1)}, s32[]{:S(2)}) async-start(s8[6291456]{0:T(1024)(128)(4,1)} %bitcast.155), calls=%async_computation.10 | async-start | bytes 4194304
  458.3 6.3 copy-start.20
  464.5 6.8 copy-start.8
  464.5 6.8 copy-start.31
  471.2 2.7 copy-start.10
  471.2 25.2 %collective-permute-start.3 = (bf16[512,2048]{1,0:T(8,128)(2,1)S(1)}, bf16[512,2048]{1,0:T(8,128)(2,1)}, u32[]{:S(2)}, u32[]{:S(2)}) collective-permute-start(bf16[512,2048]{1,0:T(8,128)(2,1)S(1)} %convolution_convert_fusion.3.refs_4_), channel_id=1, source_target_pairs={{0,2},{2,0},{4,6},{6,4},{8,10},{10,8},{12,14},{14,12},{16,18},{18,... | collective-permute-start | bytes 6291464 | tf_op jit(solution)/shard_map/ppermute | solution.py:1167
  473.5 62.0 %collective-permute-start.4 = (bf16[512,2048]{1,0:T(8,128)(2,1)}, bf16[512,2048]{1,0:T(8,128)(2,1)}, u32[]{:S(2)}, u32[]{:S(2)}) collective-permute-start(bf16[512,2048]{1,0:T(8,128)(2,1)} %convolution_convert_fusion.2.refs_5_), channel_id=1, source_target_pairs={{0,2},{2,0},{4,6},{6,4},{8,10},{10,8},{12,14},{14,12},{16,18},{18,... | collective-permute-start | bytes 6291464 | tf_op jit(solution)/shard_map/ppermute | solution.py:1167
  473.9 14.6 %copy-start.18 = (bf16[1536,1024]{1,0:T(8,128)(2,1)S(1)}, bf16[1536,1024]{1,0:T(8,128)(2,1)}, u32[]{:S(2)}) copy-start(bf16[1536,1024]{1,0:T(8,128)(2,1)} %get-tuple-element.109) | copy-start | bytes 9437188
  488.5 7.9 copy-start.21
  496.4 30.8 %collective-permute-start.5 = (bf16[512,2048]{1,0:T(8,128)(2,1)}, bf16[512,2048]{1,0:T(8,128)(2,1)}, u32[]{:S(2)}, u32[]{:S(2)}) collective-permute-start(bf16[512,2048]{1,0:T(8,128)(2,1)} %convolution_convert_fusion.1.refs_11_), channel_id=1, source_target_pairs={{0,2},{2,0},{4,6},{6,4},{8,10},{10,8},{12,14},{14,12},{16,18},{18,... | collective-permute-start | bytes 6291464 | tf_op jit(solution)/shard_map/ppermute | solution.py:1167
  496.4 30.8 %slice-start.4 = ((s8[6291456]{0:T(1024)(128)(4,1)}), s8[4194304]{0:T(1024)(128)(4,1)S(1)}, s32[]{:S(2)}) async-start(s8[6291456]{0:T(1024)(128)(4,1)} %bitcast.153), calls=%async_computation.7 | async-start | bytes 8388608
  504.4 130.7 %collective-permute-start.7 = (bf16[512,2048]{1,0:T(8,128)(2,1)}, bf16[512,2048]{1,0:T(8,128)(2,1)}, u32[]{:S(2)}, u32[]{:S(2)}) collective-permute-start(bf16[512,2048]{1,0:T(8,128)(2,1)} %add_convert_fusion.1.refs_4_), channel_id=1, source_target_pairs={{0,1},{1,0},{2,3},{3,2},{4,5},{5,4},{6,7},{7,6},{8,9},{9,8},{10,11... | collective-permute-start | bytes 6291464 | tf_op jit(solution)/shard_map/ppermute | solution.py:1164
  505.1 22.1 %slice-start.5 = ((s8[6291456]{0:T(1024)(128)(4,1)}), s8[2097152]{0:T(1024)(128)(4,1)S(1)}, s32[]{:S(2)}) async-start(s8[6291456]{0:T(1024)(128)(4,1)} %bitcast.153), calls=%async_computation.8 | async-start | bytes 4194304
  518.7 16.7 %slice-start.8 = ((s8[6291456]{0:T(1024)(128)(4,1)}), s8[4194304]{0:T(1024)(128)(4,1)S(1)}, s32[]{:S(2)}) async-start(s8[6291456]{0:T(1024)(128)(4,1)} %bitcast.157), calls=%async_computation.11 | async-start | bytes 8388608
  518.7 8.5 copy-start.19
  518.7 16.7 %slice-start.9 = ((s8[6291456]{0:T(1024)(128)(4,1)}), s8[2097152]{0:T(1024)(128)(4,1)S(1)}, s32[]{:S(2)}) async-start(s8[6291456]{0:T(1024)(128)(4,1)} %bitcast.157), calls=%async_computation.12 | async-start | bytes 4194304
  527.0 8.5 copy-start.22
  527.0 46.3 %collective-permute-start.6 = (bf16[512,2048]{1,0:T(8,128)(2,1)}, bf16[512,2048]{1,0:T(8,128)(2,1)}, u32[]{:S(2)}, u32[]{:S(2)}) collective-permute-start(bf16[512,2048]{1,0:T(8,128)(2,1)} %convolution_convert_fusion.refs_12_), channel_id=1, source_target_pairs={{0,2},{2,0},{4,6},{6,4},{8,10},{10,8},{12,14},{14,12},{16,18},{18,... | collective-permute-start | bytes 6291464 | tf_op jit(solution)/shard_map/ppermute | solution.py:1167
  533.3 101.8 %collective-permute-start.8 = (bf16[512,2048]{1,0:T(8,128)(2,1)}, bf16[512,2048]{1,0:T(8,128)(2,1)S(1)}, u32[]{:S(2)}, u32[]{:S(2)}) collective-permute-start(bf16[512,2048]{1,0:T(8,128)(2,1)} %add_convert_fusion.refs_14_), channel_id=1, source_target_pairs={{0,1},{1,0},{2,3},{3,2},{4,5},{5,4},{6,7},{7,6},{8,9},{9,8},{10,11... | collective-permute-start | bytes 6291464 | tf_op jit(solution)/shard_map/ppermute | solution.py:1164
  582.6 40.1 %copy-start.34 = (bf16[1536,1024]{1,0:T(8,128)(2,1)S(1)}, bf16[1536,1024]{1,0:T(8,128)(2,1)}, u32[]{:S(2)}) copy-start(bf16[1536,1024]{1,0:T(8,128)(2,1)} %get-tuple-element.120) | copy-start | bytes 9437188
  622.7 3.8 copy-start.1
  644.9 39.2 %copy-start.36 = (bf16[1536,1024]{1,0:T(8,128)(2,1)S(1)}, bf16[1536,1024]{1,0:T(8,128)(2,1)}, u32[]{:S(2)}) copy-start(bf16[1536,1024]{1,0:T(8,128)(2,1)} %get-tuple-element.120) | copy-start | bytes 9437188
  684.1 4.5 copy-start.2
  693.3 40.9 %collective-permute-start.11 = (bf16[2,256,2048]{2,1,0:T(8,128)(2,1)}, bf16[2,256,2048]{2,1,0:T(8,128)(2,1)}, u32[]{:S(2)}, u32[]{:S(2)}) collective-permute-start(bf16[2,256,2048]{2,1,0:T(8,128)(2,1)} %get-tuple-element.121.refs_9_), channel_id=1, source_target_pairs={{0,4},{2,6},{4,0},{6,2},{8,12},{10,14},{12,8},{14,10},{16,20},{18,... | collective-permute-start | bytes 6291464 | tf_op jit(solution)/shard_map/ppermute | solution.py:1167
  694.8 44.5 %collective-permute-start.9 = (bf16[512,2048]{1,0:T(8,128)(2,1)}, bf16[512,2048]{1,0:T(8,128)(2,1)}, u32[]{:S(2)}, u32[]{:S(2)}) collective-permute-start(bf16[512,2048]{1,0:T(8,128)(2,1)} %pad_maximum_fusion.1.refs_6_), channel_id=1, source_target_pairs={{0,2},{2,0},{4,6},{6,4},{8,10},{10,8},{12,14},{14,12},{16,18},{18,... | collective-permute-start | bytes 6291464 | tf_op jit(solution)/shard_map/ppermute | solution.py:1167
  703.7 11.7 %slice-start.2 = ((s8[6291456]{0:T(1024)(128)(4,1)}), s8[2097152]{0:T(1024)(128)(4,1)S(1)}, s32[]{:S(2)}) async-start(s8[6291456]{0:T(1024)(128)(4,1)} %bitcast.137), calls=%async_computation.5 | async-start | bytes 4194304
  708.4 7.0 slice-start.3
  708.4 66.5 %collective-permute-start.12 = (bf16[512,2048]{1,0:T(8,128)(2,1)}, bf16[512,2048]{1,0:T(8,128)(2,1)}, u32[]{:S(2)}, u32[]{:S(2)}) collective-permute-start(bf16[512,2048]{1,0:T(8,128)(2,1)} %pad_maximum_fusion.2.refs_7_), channel_id=1, source_target_pairs={{0,2},{2,0},{4,6},{6,4},{8,10},{10,8},{12,14},{14,12},{16,18},{18,... | collective-permute-start | bytes 6291464 | tf_op jit(solution)/shard_map/ppermute | solution.py:1167
  710.9 7.2 slice-start
  734.2 5.2 copy-start.15
  734.2 5.2 copy-start.25
  734.2 5.2 copy-start.26
  739.3 100.3 %collective-permute-start.17 = (bf16[2,128,2048]{2,1,0:T(8,128)(2,1)}, bf16[2,128,2048]{2,1,0:T(8,128)(2,1)}, u32[]{:S(2)}, u32[]{:S(2)}) collective-permute-start(bf16[2,128,2048]{2,1,0:T(8,128)(2,1)} %get-tuple-element.125.refs_6_), channel_id=1, source_target_pairs={{0,8},{2,10},{4,12},{6,14},{8,0},{10,2},{12,4},{14,6},{16,24},{18,... | collective-permute-start | bytes 3145736 | tf_op jit(solution)/shard_map/ppermute | solution.py:1167
  741.7 3.6 copy-start.4
  741.7 43.1 %collective-permute-start.10 = (bf16[1,256,2048]{2,1,0:T(8,128)(2,1)S(1)}, bf16[1,256,2048]{2,1,0:T(8,128)(2,1)}, u32[]{:S(2)}, u32[]{:S(2)}) collective-permute-start(bf16[1,256,2048]{2,1,0:T(8,128)(2,1)S(1)} %bitcast.161), channel_id=1, source_target_pairs={{0,8},{2,10},{4,12},{6,14},{8,0},{10,2},{12,4},{14,6},{16,24},{18,... | collective-permute-start | bytes 3145736 | tf_op jit(solution)/shard_map/ppermute | solution.py:1167
  745.3 29.6 %copy-start.13 = (f32[512,768]{1,0:T(8,128)S(1)}, f32[512,768]{1,0:T(8,128)}, u32[]{:S(2)}) copy-start(f32[512,768]{1,0:T(8,128)} %fusion.4) | copy-start | bytes 4718596
  745.3 29.6 %copy-start.14 = (f32[512,768]{1,0:T(8,128)S(1)}, f32[512,768]{1,0:T(8,128)}, u32[]{:S(2)}) copy-start(f32[512,768]{1,0:T(8,128)} %fusion) | copy-start | bytes 4718596
  745.3 29.6 %copy-start.29 = (f32[512,256]{1,0:T(8,128)S(1)}, f32[512,256]{1,0:T(8,128)}, u32[]{:S(2)}) copy-start(f32[512,256]{1,0:T(8,128)} %fusion.48) | copy-start | bytes 1572868
  757.8 86.0 %collective-permute-start.13 = (bf16[1536,512]{1,0:T(8,128)(2,1)}, bf16[1536,512]{1,0:T(8,128)(2,1)}, u32[]{:S(2)}, u32[]{:S(2)}) collective-permute-start(bf16[1536,512]{1,0:T(8,128)(2,1)} %token_pull.2.refs_3_), channel_id=1, source_target_pairs={{0,1},{1,0},{2,3},{3,2},{4,5},{5,4},{6,7},{7,6},{8,9},{9,8},{10,11... | collective-permute-start | bytes 4718600 | tf_op jit(solution)/shard_map/ppermute | solution.py:1164
  779.4 5.4 copy-start.5
  779.4 41.6 %collective-permute-start.14 = (bf16[1,256,2048]{2,1,0:T(8,128)(2,1)S(1)}, bf16[1,256,2048]{2,1,0:T(8,128)(2,1)}, u32[]{:S(2)}, u32[]{:S(2)}) collective-permute-start(bf16[1,256,2048]{2,1,0:T(8,128)(2,1)S(1)} %bitcast.163), channel_id=1, source_target_pairs={{0,8},{2,10},{4,12},{6,14},{8,0},{10,2},{12,4},{14,6},{16,24},{18,... | collective-permute-start | bytes 3145736 | tf_op jit(solution)/shard_map/ppermute | solution.py:1167
  787.6 58.9 %collective-permute-start.16 = (bf16[1,128,2048]{2,1,0:T(8,128)(2,1)}, bf16[1,128,2048]{2,1,0:T(8,128)(2,1)S(1)}, u32[]{:S(2)}, u32[]{:S(2)}) collective-permute-start(bf16[1,128,2048]{2,1,0:T(8,128)(2,1)} %get-tuple-element.126.refs_6_), channel_id=1, source_target_pairs={{0,16},{2,18},{4,20},{6,22},{8,24},{10,26},{12,28},{14,30},{16,0},... | collective-permute-start | bytes 1572872 | tf_op jit(solution)/shard_map/ppermute | solution.py:1167
  823.8 19.9 %copy-start = (f32[1536,512]{1,0:T(8,128)S(1)}, f32[1536,512]{1,0:T(8,128)}, u32[]{:S(2)}) copy-start(f32[1536,512]{1,0:T(8,128)} %token_pull.3.refs_3_) | copy-start | bytes 9437188
  823.8 51.2 %collective-permute-start.15 = (bf16[1,128,2048]{2,1,0:T(8,128)(2,1)}, bf16[1,128,2048]{2,1,0:T(8,128)(2,1)}, u32[]{:S(2)}, u32[]{:S(2)}) collective-permute-start(bf16[1,128,2048]{2,1,0:T(8,128)(2,1)} %get-tuple-element.128.refs_3_), channel_id=1, source_target_pairs={{0,16},{2,18},{4,20},{6,22},{8,24},{10,26},{12,28},{14,30},{16,0},... | collective-permute-start | bytes 1572872 | tf_op jit(solution)/shard_map/ppermute | solution.py:1167
  843.5 40.6 %collective-permute-start.21 = (bf16[2,64,2048]{2,1,0:T(8,128)(2,1)}, bf16[2,64,2048]{2,1,0:T(8,128)(2,1)}, u32[]{:S(2)}, u32[]{:S(2)}) collective-permute-start(bf16[2,64,2048]{2,1,0:T(8,128)(2,1)} %get-tuple-element.131.refs_3_), channel_id=1, source_target_pairs={{0,16},{2,18},{4,20},{6,22},{8,24},{10,26},{12,28},{14,30},{16,0},... | collective-permute-start | bytes 1572872 | tf_op jit(solution)/shard_map/ppermute | solution.py:1167
  846.3 37.8 %copy-start.16 = (f32[2,64,2048]{2,1,0:T(8,128)S(1)}, f32[2,64,2048]{2,1,0:T(8,128)}, u32[]{:S(2)}) copy-start(f32[2,64,2048]{2,1,0:T(8,128)} %get-tuple-element.138) | copy-start | bytes 3145732
  849.5 38.9 %collective-permute-start.19 = (bf16[1,64,2048]{2,1,0:T(8,128)(2,1)}, bf16[1,64,2048]{2,1,0:T(8,128)(2,1)S(1)}, u32[]{:S(2)}, u32[]{:S(2)}) collective-permute-start(bf16[1,64,2048]{2,1,0:T(8,128)(2,1)} %get-tuple-element.132.refs_3_), channel_id=1, source_target_pairs={{0,4},{2,6},{4,0},{6,2},{8,12},{10,14},{12,8},{14,10},{16,20},{18,... | collective-permute-start | bytes 786440 | tf_op jit(solution)/shard_map/ppermute | solution.py:1167
  877.2 39.6 %collective-permute-start.18 = (bf16[1,64,2048]{2,1,0:T(8,128)(2,1)}, bf16[1,64,2048]{2,1,0:T(8,128)(2,1)S(1)}, u32[]{:S(2)}, u32[]{:S(2)}) collective-permute-start(bf16[1,64,2048]{2,1,0:T(8,128)(2,1)} %get-tuple-element.134.refs_1_), channel_id=1, source_target_pairs={{0,4},{2,6},{4,0},{6,2},{8,12},{10,14},{12,8},{14,10},{16,20},{18,... | collective-permute-start | bytes 786440 | tf_op jit(solution)/shard_map/ppermute | solution.py:1167
  885.2 3.1 copy-start.30
  888.4 28.5 %copy-start.27 = (f32[1,64,2048]{2,1,0:T(8,128)S(1)}, f32[1,64,2048]{2,1,0:T(8,128)}, u32[]{:S(2)}) copy-start(f32[1,64,2048]{2,1,0:T(8,128)} %get-tuple-element.133) | copy-start | bytes 1572868
  888.4 28.4 %collective-permute-start.20 = (bf16[1,64,2048]{2,1,0:T(8,128)(2,1)S(1)}, bf16[1,64,2048]{2,1,0:T(8,128)(2,1)S(1)}, u32[]{:S(2)}, u32[]{:S(2)}) collective-permute-start(bf16[1,64,2048]{2,1,0:T(8,128)(2,1)S(1)} %add_convert_fusion.2), channel_id=1, source_target_pairs={{0,1},{1,0},{2,3},{3,2},{4,5},{5,4},{6,7},{7,6},{8,9},{9,8},{10,11... | collective-permute-start | bytes 786440 | tf_op jit(solution)/shard_map/ppermute | solution.py:1164
  (10 other events, 19.1 us)
Sparse Core Ops, SparseCore 0:
  74.4 37.1 all-gather.3
  113.7 49.1 all-gather.5
  165.1 49.5 all-gather.7

commit v6 on v5

--- a/solution.py
+++ b/solution.py
@@ -24,7 +24,7 @@
 
 
 def row_step(rows):
-    return 512 if rows % 512 == 0 else 128
+    return 256 if rows % 256 == 0 else 128
 
 
 def parts_of(step):
@@ -81,16 +81,8 @@
     return pl.BlockSpec((step, width), lambda i, *_: (i, 0))
 
 
-def by_core(block, paired):
-    if not paired:
-        return block
-    firsts, seconds = [], []
-    for at in range(0, block.shape[1], 256):
-        one, two = block[:, at : at + 128], block[:, at + 128 : at + 256]
-        low = lax.broadcasted_iota(jnp.int32, one.shape, 1) < 64
-        firsts.append(jnp.where(low, one, pltpu.roll(two, 64, 1)))
-        seconds.append(jnp.where(low, pltpu.roll(one, 64, 1), two))
-    return jnp.concatenate(firsts + seconds, axis=1)
+def column_spec(width, step):
+    return pl.BlockSpec((width, step), lambda i, *_: (0, i))
 
 
 MESH = pl.DeviceIdType.MESH
@@ -149,8 +141,8 @@
 
 
 def start_kernel(rows, cols_width, parts, *refs):
-    (tokens, qkv, out, up, down, proj, pack), refs = refs[:7], refs[7:]
-    (x, qkv_o, out_o, up_o, down_o, proj_o, pack_o), refs = refs[:7], refs[7:]
+    (tokens, qkv, proj, pack), refs = refs[:4], refs[4:]
+    (x, qkv_o, proj_o, pack_o), refs = refs[:4], refs[4:]
     own_sem, sent, arrived, wide_sent, wide_arrived = refs
     r, c = lax.axis_index("rows"), lax.axis_index("cols")
     partner = {"cols": 1 - c}
@@ -173,8 +165,7 @@
             send(tokens.at[theirs], target, sent.at[3 + place], arrived.at[3 + place], partner)
         )
         pltpu.make_async_copy(tokens.at[mine], target, own_sem.at[place]).start()
-    narrow = [(proj, proj_o), (pack, pack_o), (out.at[r], out_o), (up.at[r], up_o), (down.at[r], down_o)]
-    for place, (source, target) in enumerate(narrow):
+    for place, (source, target) in enumerate([(proj, proj_o), (pack, pack_o)]):
         copies.append(
             send(source, target, sent.at[5 + place], arrived.at[5 + place], partner)
         )
@@ -202,32 +193,24 @@
         pltpu.make_async_copy(tokens.at[mine], target, own_sem.at[place]).wait()
 
 
-def start_up(rows, parts, tokens, qkv, out, up, down, proj, pack):
+def start_up(rows, parts, tokens, qkv, proj, pack):
     width = tokens.shape[1]
-
-    def pieces(array):
-        return array.reshape(rows, -1, array.shape[-1])
-
-    weights = [pieces(array) for array in (qkv, out, up, down)]
-    qkv_p, out_p, up_p, down_p = weights
-    operands = (tokens, *weights, proj, pack)
-    n = parts[0] + parts[1]
-    x, qkv_o, out_o, up_o, down_o, proj_o, pack_o = call(
+    pieces = qkv.reshape(rows, -1, width)
+    x, qkv_o, proj_o, pack_o = call(
         functools.partial(start_kernel, rows, width, parts), "start_up", (1,),
-        [ANYWHERE] * 7, [ANYWHERE] * 7,
+        [ANYWHERE] * 4, [ANYWHERE] * 4,
         [
-            shaped(BF16, n, 2 * width), shaped(BF16, *qkv_p.shape), shaped(BF16, *out_p.shape[1:]),
-            shaped(BF16, *up_p.shape[1:]), shaped(BF16, *down_p.shape[1:]),
+            shaped(BF16, parts[0] + parts[1], 2 * width), shaped(BF16, *pieces.shape),
             shaped(BF16, *proj.shape), shaped(F32, *pack.shape),
         ],
-        operands, 0, remote=1,
+        (tokens, pieces, proj, pack), 0, remote=1,
         scratch=[
-            pltpu.SemaphoreType.DMA((2,)), pltpu.SemaphoreType.DMA((10,)),
-            pltpu.SemaphoreType.DMA((10,)), pltpu.SemaphoreType.DMA((1, rows)),
+            pltpu.SemaphoreType.DMA((2,)), pltpu.SemaphoreType.DMA((7,)),
+            pltpu.SemaphoreType.DMA((7,)), pltpu.SemaphoreType.DMA((1, rows)),
             pltpu.SemaphoreType.DMA((1, rows)),
         ],
     )
-    return x, qkv_o.reshape(qkv.shape), out_o, up_o, down_o, proj_o, pack_o
+    return x, qkv_o.reshape(qkv.shape), proj_o, pack_o
 
 
 def gather_kernel(rows, own, out, own_sem, sent, arrived):
@@ -237,18 +220,25 @@
     local = pltpu.make_async_copy(own, out.at[r], own_sem)
     local.start()
     copies = {}
+    size = own.shape[0] // PARTS
     for piece, over in spread_order(rows):
         row = flipped(r, piece)
-        if piece:
-            copies[piece].wait_recv()
-        for bit in over:
-            copies[piece | bit] = send(
-                out.at[row] if piece else own, out.at[row],
-                sent.at[piece | bit], arrived.at[piece | bit], {"rows": across(r, bit)},
-            )
+        for part in range(PARTS):
+            at = pl.ds(part * size, size)
+            if piece:
+                copies[piece, part].wait_recv()
+            for bit in over:
+                copies[piece | bit, part] = send(
+                    out.at[row, at] if piece else own.at[at], out.at[row, at],
+                    sent.at[piece | bit, part], arrived.at[piece | bit, part],
+                    {"rows": across(r, bit)},
+                )
     for copy in copies.values():
         copy.wait_send()
     local.wait()
+
+
+PARTS = 2
 
 
 def gather_rows(rows, own):
@@ -256,8 +246,8 @@
         functools.partial(gather_kernel, rows), "gather_rows", (1,), [ANYWHERE], [ANYWHERE],
         [shaped(own.dtype, rows, *own.shape)], (own,), 0, remote=2,
         scratch=[
-            pltpu.SemaphoreType.DMA, pltpu.SemaphoreType.DMA((rows,)),
-            pltpu.SemaphoreType.DMA((rows,)),
+            pltpu.SemaphoreType.DMA, pltpu.SemaphoreType.DMA((rows, PARTS)),
+            pltpu.SemaphoreType.DMA((rows, PARTS)),
         ],
     )[0]
 
@@ -267,14 +257,15 @@
     bits = [1 << b for b in range(rows.bit_length() - 1)]
     greet([{"rows": across(r, bit)} for bit in bits])
     outgoing, incoming = buffers[: len(bits)], buffers[len(bits) :]
+    size = parts.shape[1] // PARTS
     copies = {}
 
-    def total(flips, levels):
-        row = flipped(r, flips)
-        value = parts[row]
+    def total(flips, levels, part):
+        row, at = flipped(r, flips), pl.ds(part * size, size)
+        value = parts[row, at]
         for level in range(levels):
-            copies[level, flips >> (level + 1)].wait_recv()
-            value = value + incoming[level][row // (2 << level)].astype(F32)
+            copies[level, flips >> (level + 1), part].wait_recv()
+            value = value + incoming[level][row // (2 << level), at].astype(F32)
         return value
 
     for level, bit in enumerate(bits):
@@ -282,13 +273,16 @@
         for turn in sorted(range(count), key=lambda f: tuple(-((f >> b) & 1) for b in range(8))):
             flips = (turn << (level + 1)) | bit
             place = flipped(r, flips) // (2 << level)
-            outgoing[level][place] = total(flips, level).astype(BF16)
-            copies[level, turn] = send(
-                outgoing[level].at[place], incoming[level].at[place],
-                sent.at[rows - 2 * count + turn], arrived.at[rows - 2 * count + turn],
-                {"rows": across(r, bit)},
-            )
-    out[...] = total(0, len(bits))
+            for part in range(PARTS):
+                at = pl.ds(part * size, size)
+                outgoing[level][place, at] = total(flips, level, part).astype(BF16)
+                name = rows - 2 * count + turn
+                copies[level, turn, part] = send(
+                    outgoing[level].at[place, at], incoming[level].at[place, at],
+                    sent.at[name, part], arrived.at[name, part], {"rows": across(r, bit)},
+                )
+    for part in range(PARTS):
+        out[part * size : (part + 1) * size, :] = total(0, len(bits), part)
     for copy in copies.values():
         copy.wait_send()
 
@@ -303,9 +297,172 @@
         functools.partial(scatter_kernel, rows), "scatter_rows", (1,), [held(parts.shape)],
         [pl.BlockSpec((height, width), lambda *_: (0, 0))], [shaped(F32, height, width)],
         (parts,), 0, remote=3,
-        scratch=[pltpu.SemaphoreType.DMA((rows,)), pltpu.SemaphoreType.DMA((rows,))]
-        + buffers + buffers,
+        scratch=[
+            pltpu.SemaphoreType.DMA((rows, PARTS)), pltpu.SemaphoreType.DMA((rows, PARTS)),
+        ] + buffers + buffers,
     )[0]
+
+
+def late_kernel(rows, cols, *refs):
+    tokens_t, branch_t = refs[:2]
+    rights, attended, refs = refs[2 : 2 + cols], refs[2 + cols : 2 + 2 * cols], refs[2 + 2 * cols :]
+    (du_own, du_in, out, du_out), refs = refs[:4], refs[4:]
+    (core_out, core_in, x_out, x_in, kept, cols_out, cols_in), refs = refs[:7], refs[7:]
+    r, c = lax.axis_index("rows"), lax.axis_index("cols")
+    x_bit, *z_bits = [1 << b for b in range(1, rows.bit_length() - 1)]
+    levels = len(z_bits)
+    z_out, z_in, z_kept = refs[:levels], refs[levels : 2 * levels], refs[2 * levels : 3 * levels]
+    refs = refs[3 * levels :]
+    du_z_out, du_z_in, du_kept = refs[:levels], refs[levels : 2 * levels], refs[2 * levels : 3 * levels]
+    (core_sem, x_sem, cols_sem, z_sem, du_sem) = refs[3 * levels :]
+    share = out.shape[1]
+    others = [{"cols": (c + cols - k) % cols} for k in range(1, cols)]
+    core, x_side = side_at(r, 1), side_at(r, x_bit)
+    greet([{"rows": across(r, bit)} for bit in [1, x_bit] + z_bits] + others)
+    chunks = range(4)
+    slots = range(cols - 1, -1, -1)
+    copies = {}
+
+    def halves(total, side):
+        pairs = total.reshape(-1, 2, share, total.shape[1])
+        near = jnp.where(side == 0, pairs[:, 0], pairs[:, 1]).reshape(-1, total.shape[1])
+        far = jnp.where(side == 0, pairs[:, 1], pairs[:, 0]).reshape(-1, total.shape[1])
+        return near, far
+
+    def product(side, slot, chunk):
+        left = (tokens_t if chunk < 3 else branch_t)[:, side]
+        right = rights[slot][chunk] if chunk < 3 else attended[slot][...]
+        return mm(left.reshape(-1, left.shape[-1]), right)
+
+    def begin(chunk):
+        for slot in slots:
+            core_out[slot, chunk] = product(1 - core, slot, chunk).astype(BF16)
+            copies["core", slot, chunk] = send(
+                core_out.at[slot, chunk], core_in.at[slot, chunk],
+                core_sem.at[0, slot, chunk], core_sem.at[1, slot, chunk],
+                {"rows": across(r, 1)},
+            )
+
+    def after_core(chunk):
+        for slot in slots:
+            total = product(core, slot, chunk)
+            copies["core", slot, chunk].wait_recv()
+            near, far = halves(total + core_in[slot, chunk].astype(F32), x_side)
+            x_out[slot, chunk] = far.astype(BF16)
+            kept[slot, chunk] = near
+            copies["x", slot, chunk] = send(
+                x_out.at[slot, chunk], x_in.at[slot, chunk], x_sem.at[0, slot, chunk],
+                x_sem.at[1, slot, chunk], {"rows": across(r, x_bit)},
+            )
+
+    def after_x(chunk):
+        for slot in slots:
+            copies["x", slot, chunk].wait_recv()
+            total = kept[slot, chunk] + x_in[slot, chunk].astype(F32)
+            if slot == 0:
+                kept[0, chunk] = total
+            else:
+                cols_out[slot - 1, chunk] = total.astype(BF16)
+                copies["cols", slot, chunk] = send(
+                    cols_out.at[slot - 1, chunk], cols_in.at[slot - 1, chunk],
+                    cols_sem.at[0, slot - 1, chunk], cols_sem.at[1, slot - 1, chunk],
+                    others[slot - 1],
+                )
+
+    def after_cols(chunk):
+        total = kept[0, chunk]
+        for slot in slots[:-1]:
+            copies["cols", slot, chunk].wait_recv()
+            total = total + cols_in[slot - 1, chunk].astype(F32)
+        pass_z(chunk, 0, total)
+
+    def pass_z(chunk, level, total):
+        if level == levels:
+            out[chunk] = total
+            return
+        bit = z_bits[level]
+        near, far = halves(total, side_at(r, bit))
+        z_out[level][chunk] = far.astype(BF16)
+        z_kept[level][chunk] = near
+        copies["z", level, chunk] = send(
+            z_out[level].at[chunk], z_in[level].at[chunk], z_sem.at[0, level, chunk],
+            z_sem.at[1, level, chunk], {"rows": across(r, bit)},
+        )
+
+    def after_z(chunk, level):
+        copies["z", level, chunk].wait_recv()
+        pass_z(chunk, level + 1, z_kept[level][chunk] + z_in[level][chunk].astype(F32))
+
+    def pass_du(place, level, total):
+        if level == levels:
+            du_out[place] = total
+            return
+        bit = z_bits[level]
+        near, far = halves(total, side_at(r, bit))
+        du_z_out[level][place] = far.astype(BF16)
+        du_kept[level][place] = near
+        copies["du", level, place] = send(
+            du_z_out[level].at[place], du_z_in[level].at[place], du_sem.at[0, level, place],
+            du_sem.at[1, level, place], {"rows": across(r, bit)},
+        )
+
+    def after_du(place, level):
+        copies["du", level, place].wait_recv()
+        pass_du(place, level + 1, du_kept[level][place] + du_z_in[level][place].astype(F32))
+
+    for place in range(2):
+        pass_du(place, 0, du_own[place] + du_in[place].astype(F32))
+    stages = [(0, begin), (1, after_core), (3, after_x), (4, after_cols)]
+    stages += [(5 + level, functools.partial(after_z, level=level)) for level in range(levels)]
+    for turn in range(len(chunks) + stages[-1][0]):
+        for delay, stage in stages[::-1]:
+            if 0 <= turn - delay < len(chunks):
+                stage(turn - delay)
+        if 3 <= turn < 3 + levels:
+            for place in range(2):
+                after_du(place, turn - 3)
+    for copy in copies.values():
+        copy.wait_send()
+
+
+def late_sums(rows, cols, tokens_t, branch_t, rights, attended, du_own, du_in):
+    share, n = tokens_t.shape[2:]
+    width = attended[0].shape[1]
+    wide = du_own.shape[2]
+    half, quarter = rows // 2 * share, rows // 4 * share
+    levels = rows.bit_length() - 3
+    heights = [quarter >> (level + 1) for level in range(levels)]
+
+    def vmem(dtype, *shape):
+        return pltpu.VMEM(shape, dtype)
+
+    def pair_of(*shape):
+        return pltpu.SemaphoreType.DMA((2,) + shape)
+
+    operands = (tokens_t, branch_t, *rights, *attended, du_own, du_in)
+    scratch = [
+        vmem(BF16, cols, 4, half, width), vmem(BF16, cols, 4, half, width),
+        vmem(BF16, cols, 4, quarter, width), vmem(BF16, cols, 4, quarter, width),
+        vmem(F32, cols, 4, quarter, width),
+        vmem(BF16, cols - 1, 4, quarter, width), vmem(BF16, cols - 1, 4, quarter, width),
+    ]
+    for count, size in ((4, width), (2, wide)):
+        for dtype in (BF16, BF16, F32):
+            scratch += [vmem(dtype, count, height, size) for height in heights]
+    scratch += [
+        pair_of(cols, 4), pair_of(cols, 4), pair_of(cols - 1, 4), pair_of(levels, 4),
+        pair_of(levels, 2),
+    ]
+    return call(
+        functools.partial(late_kernel, rows, cols), "late_sums", (1,),
+        [held(o.shape) for o in operands],
+        [
+            pl.BlockSpec((4, share, width), lambda *_: (0, 0, 0)),
+            pl.BlockSpec((2, share, wide), lambda *_: (0, 0, 0)),
+        ],
+        [shaped(F32, 4, share, width), shaped(F32, 2, share, wide)],
+        operands, 100_000_000_000, remote=5, scratch=scratch,
+    )
 
 
 def small_kernel(rows, cols, parts, out, *refs):
@@ -442,7 +599,7 @@
         ref[...] += value
 
 
-def out_norm_kernel(slots, paired, *refs):
+def out_norm_kernel(slots, *refs):
     x_ref, vec_ref = refs[:2]
     att_refs, w_refs = refs[2 : 2 + slots], refs[2 + slots : 2 + 2 * slots]
     normed_ref, inverse_ref, low_ref, turned_ref = refs[2 + 2 * slots :]
@@ -455,20 +612,20 @@
         normed_ref[at, :] = normed
         inverse_ref[at, :] = inverse
         low_ref[at, :] = hidden.astype(BF16)
-        turned_ref[at, :] = by_core(hidden, paired).astype(BF16)
-
-
-def out_and_norm(x, vectors, attended, weights, paired):
+        turned_ref[:, at] = hidden.T.astype(BF16)
+
+
+def out_and_norm(x, vectors, attended, weights):
     n, D = x.shape
     step = row_step(n)
     slots = len(attended)
     width = attended[0].shape[1]
     return call(
-        functools.partial(out_norm_kernel, slots, paired), "out_and_norm", (n // step,),
+        functools.partial(out_norm_kernel, slots), "out_and_norm", (n // step,),
         [row_spec(step, D), held(vectors.shape)]
         + [row_spec(step, width)] * slots + [held((width, D))] * slots,
-        [row_spec(step, D), row_spec(step, 1), row_spec(step, D), row_spec(step, D)],
-        [shaped(F32, n, D), shaped(F32, n, 1), shaped(BF16, n, D), shaped(BF16, n, D)],
+        [row_spec(step, D), row_spec(step, 1), row_spec(step, D), column_spec(D, step)],
+        [shaped(F32, n, D), shaped(F32, n, 1), shaped(BF16, n, D), shaped(BF16, D, n)],
         (x, vectors, *attended, *weights), 2 * n * D * D,
     )
 
@@ -557,7 +714,7 @@
 
 
 def head_pull_kernel(
-    paired, grad_ref, unit_ref, unit_inverse_ref, proj_ref, normed_ref, inverse_ref, vec_ref,
+    grad_ref, unit_ref, unit_inverse_ref, proj_ref, normed_ref, inverse_ref, vec_ref,
     embed_ref, residual_ref, low_ref, turned_ref, sum_ref,
 ):
     sums = []
@@ -571,27 +728,27 @@
         residual = norm_pull(output_grad, normed, inverse_ref[at, :], vec_ref[4:5, :])
         residual_ref[at, :] = residual
         low_ref[at, :] = residual.astype(BF16)
-        turned_ref[at, :] = by_core(residual, paired).astype(BF16)
+        turned_ref[:, at] = residual.T.astype(BF16)
         sums.append(column_sums(residual, output_grad * normed, output_grad))
     add_over_steps(sum_ref, sum(sums))
 
 
-def head_pull(unit_grad, unit, unit_inverse, proj, normed, inverse, vectors, paired):
+def head_pull(unit_grad, unit, unit_inverse, proj, normed, inverse, vectors):
     n, D = normed.shape
     step = row_step(n)
     return call(
-        functools.partial(head_pull_kernel, paired), "head_pull", (n // step,),
+        head_pull_kernel, "head_pull", (n // step,),
         [
             row_spec(step, 128), row_spec(step, 128), row_spec(step, 1), held(proj.shape),
             row_spec(step, D), row_spec(step, 1), held(vectors.shape),
         ],
         [
             row_spec(step, 128), row_spec(step, D), row_spec(step, D),
-            row_spec(step, D), pl.BlockSpec((8, D), lambda i: (0, 0)),
+            column_spec(D, step), pl.BlockSpec((8, D), lambda i: (0, 0)),
         ],
         [
             shaped(BF16, n, 128), shaped(F32, n, D), shaped(BF16, n, D),
-            shaped(BF16, n, D), shaped(F32, 8, D),
+            shaped(BF16, D, n), shaped(F32, 8, D),
         ],
         (unit_grad, unit, unit_inverse, proj, normed, inverse, vectors), 4 * n * D * 128,
     )
@@ -622,7 +779,7 @@
     )
 
 
-def hidden_pull_kernel(slots, paired, *refs):
+def hidden_pull_kernel(slots, *refs):
     residual_ref, normed_ref, inverse_ref, vec_ref = refs[:4]
     pre_refs, up_refs, out_refs = (refs[4 + j * slots : 4 + (j + 1) * slots] for j in range(3))
     rest = refs[4 + 3 * slots :]
@@ -637,33 +794,33 @@
         residual = norm_pull(hidden_grad, normed, inverse_ref[at, :], vec_ref[1:2, :])
         grad_ref[at, :] = residual
         low = residual.astype(BF16)
-        turned_ref[at, :] = by_core(residual, paired).astype(BF16)
+        turned_ref[:, at] = residual.T.astype(BF16)
         sums.append(column_sums(residual, hidden_grad * normed, hidden_grad))
         for att_ref, out_ref in zip(att_refs, out_refs):
             att_ref[at, :] = mm(low, out_ref[...], NT).astype(BF16)
     add_over_steps(sum_ref, sum(sums))
 
 
-def hidden_pull(residual, normed, inverse, vectors, pre_grads, ups, outs, paired):
+def hidden_pull(residual, normed, inverse, vectors, pre_grads, ups, outs):
     n, D = residual.shape
     step = row_step(n)
     slots = len(ups)
     wide, width = ups[0].shape[1], outs[0].shape[0]
     return call(
-        functools.partial(hidden_pull_kernel, slots, paired), "hidden_pull", (n // step,),
+        functools.partial(hidden_pull_kernel, slots), "hidden_pull", (n // step,),
         [row_spec(step, D), row_spec(step, D), row_spec(step, 1), held(vectors.shape)]
         + [row_spec(step, wide)] * slots + [held((D, wide))] * slots
         + [held((width, D))] * slots,
-        [row_spec(step, D), row_spec(step, D), pl.BlockSpec((8, D), lambda i: (0, 0))]
+        [row_spec(step, D), column_spec(D, step), pl.BlockSpec((8, D), lambda i: (0, 0))]
         + [row_spec(step, width)] * slots,
-        [shaped(F32, n, D), shaped(BF16, n, D), shaped(F32, 8, D)]
+        [shaped(F32, n, D), shaped(BF16, D, n), shaped(F32, 8, D)]
         + [shaped(BF16, n, width)] * slots,
         (residual, normed, inverse, vectors, *pre_grads, *ups, *outs),
         0,
     )
 
 
-def token_pull_kernel(slots, span, place_ref, *refs):
+def token_pull_kernel(slots, place_ref, *refs):
     residual_ref = refs[0]
     mixed_refs, w_refs = refs[1 : 1 + slots], refs[1 + slots : 1 + 2 * slots]
     out_ref = refs[-1]
@@ -671,11 +828,8 @@
     at = pl.ds(pl.multiple_of(place_ref[0] * width, width), width)
     total = residual_ref[...]
     for mixed_ref, w_ref in zip(mixed_refs, w_refs):
-        for first in range(0, width, span):
-            for which in range(3):
-                start = 4 * first + which * span
-                mixed = mixed_ref[:, start : start + span]
-                total = total + mm(mixed, w_ref[which, at, first : first + span], NT)
+        for which in range(3):
+            total = total + mm(mixed_ref[which], w_ref[which, at, :], NT)
     out_ref[...] = total.astype(out_ref.dtype)
 
 
@@ -685,13 +839,13 @@
     slots = len(weights)
     width = weights[0].shape[2]
     return call(
-        functools.partial(token_pull_kernel, slots, min(width, ATTENTION_LANES)), "token_pull", (n // step,),
+        functools.partial(token_pull_kernel, slots), "token_pull", (n // step,),
         [pl.BlockSpec((step, width), lambda i, p: (i, p[0]))]
-        + [row_spec(step, 4 * width)] * slots
+        + [pl.BlockSpec((3, step, width), lambda i, p: (0, i, 0))] * slots
         + [held((3, D, width))] * slots,
         [row_spec(step, width)],
         [shaped(dtype, n, width)],
-        (place.reshape(1), residual, *mixed_grads, *weights), 6 * n * D * width, prefetch=1,
+        (place.reshape(1), residual, *mixed_grads, *weights), 0, prefetch=1,
     )[0]
 
 
@@ -722,6 +876,52 @@
         @pl.when((pl.program_id(0) >= starts[place]) & (pl.program_id(0) < starts[place + 1]))
         def _(place=place):
             body(place)
+
+
+def assemble_kernel(place_ref, *refs):
+    out_ref = refs[-1]
+    slot = place_ref[1 + pl.program_id(0)]
+    for k, ref in enumerate(refs[:-1]):
+
+        @pl.when(slot == k)
+        def _(ref=ref):
+            out_ref[...] = ref[...].astype(F32)
+
+
+def assemble(c, q_rows, slots):
+    n, width = slots[0].shape
+    count = len(slots)
+    step = math.gcd(256, q_rows)
+    q_steps, d_steps = q_rows // step, (n - q_rows) // step
+    turns, owners = [], []
+    for base, steps in ((0, q_steps), (q_steps, d_steps)):
+        for owner in range(count):
+            turns += [base + turn for turn in range(steps)]
+            owners += [owner] * steps
+    places = jnp.concatenate([c.reshape(1), (c - jnp.array(owners)) % count]).astype(jnp.int32)
+
+    def turn_of(j, p):
+        turn = jnp.where(j < count * q_steps, j % q_steps, q_steps + (j - count * q_steps) % d_steps)
+        return turn, 0
+
+    return call(
+        assemble_kernel, "assemble", (len(turns),),
+        [pl.BlockSpec((step, width), turn_of)] * count,
+        [pl.BlockSpec((step, width), lambda j, p: (j, 0))],
+        [shaped(F32, n * count, width)], (places, *slots), 0, prefetch=1,
+    )[0]
+
+
+def pass_on_kernel(in_ref, out_ref):
+    out_ref[...] = in_ref[...]
+
+
+def pass_on(array):
+    spec = held(array.shape)
+    return call(
+        pass_on_kernel, "pass_on", (1,), [spec], [pl.BlockSpec(array.shape, lambda *_: (0,) * array.ndim)],
+        [shaped(array.dtype, *array.shape)], (array,), 0,
+    )[0]
 
 
 def fold_kernel(starts, inner, place_ref, *refs):
@@ -758,7 +958,7 @@
 
 
 SEGMENTS = 8
-ATTENTION_LANES = 256
+ATTENTION_LANES = 128
 
 
 def half_lanes(block, head, other):
@@ -882,14 +1082,16 @@
                 head = 2 * pair + half
                 keys_ref[head, at, :] = half_lanes(qkv_ref[1, at, cut], half, ext_k)
                 values_ref[head, at, :] = half_lanes(qkv_ref[2, at, cut], half, ext_k)
-                queries_ref[head, at, :] = half_lanes(query, half, ext_ref[at, cut])
+                whole = half_lanes(query, half, ext_ref[at, cut])
+                queries_ref[head, step] = whole.astype(F32).T.astype(BF16)
                 plain_ref[head, at, :] = half_lanes(query, half, zeros)
                 plain_grads_ref[head, at, :] = half_lanes(grad, half, zeros)
                 inner = jnp.sum(half_lanes(product, half, 0.0), axis=1, keepdims=True)
                 extra = jnp.zeros((tile, 128), F32)
                 for place, term in enumerate(three_terms(-inner)):
                     extra = jnp.where((lane & (DH - 1)) == SEGMENTS + place, term, extra)
-                grads_ref[head, at, :] = half_lanes(grad, half, extra.astype(BF16))
+                whole = half_lanes(grad.astype(F32), half, extra)
+                grads_ref[head, step] = whole.T.astype(BF16)
 
     dk_ref[...] = jnp.zeros(dk_ref.shape, F32)
     dv_ref[...] = jnp.zeros(dv_ref.shape, F32)
@@ -901,8 +1103,8 @@
             probs, slopes, dq = [], [], []
             both = range(2 * pair, 2 * pair + 2)
             for head in both:
-                weights = jnp.exp(mm(keys_ref[head, window, :], queries_ref[head, at, :], NT))
-                flow = mm(values_ref[head, window, :], grads_ref[head, at, :], NT)
+                weights = jnp.exp(mm(keys_ref[head, window, :], queries_ref[head, step]))
+                flow = mm(values_ref[head, window, :], grads_ref[head, step])
                 slope = (weights * flow).astype(BF16)
                 probs.append(weights.astype(BF16))
                 slopes.append(slope)
@@ -919,7 +1121,6 @@
     def finish(step, sums):
         cosine, sine = cos_ref[rows(step), :], sin_ref[rows(step), :]
         added = []
-        out_ref[rows(step), 3 * pairs * 128 :] = att_ref[rows(step), :]
         for which, src in enumerate((dq_ref, dk_ref, dv_ref)):
             for pair in range(pairs):
                 at = lanes(2 * pair)
@@ -927,8 +1128,7 @@
                 if which < 2:
                     block = block * cosine - swap_halves(block) * sine
                 low = block.astype(BF16)
-                first = (which * pairs + pair) * 128
-                out_ref[rows(step), first : first + 128] = low
+                out_ref[which, rows(step), at] = low
                 total = jnp.sum(low.astype(F32), axis=0, keepdims=True)
                 added.append(sums[which * pairs + pair] + total)
         return tuple(added)
@@ -946,21 +1146,19 @@
     span = min(width, ATTENTION_LANES)
     wide = pl.BlockSpec((n, span), lambda i, *_: (0, i))
     three = pl.BlockSpec((3, n, span), lambda i, *_: (0, 0, i))
-    pairs = span // 128
+    tiles, pairs = n // tile, span // 128
     heads = pltpu.VMEM((2 * pairs, n, 128), BF16)
+    turned = pltpu.VMEM((2 * pairs, tiles, 128, tile), BF16)
     return call(
         functools.partial(attention_backward_kernel, tile=tile), "attention_backward",
         (width // span,),
         [three, wide, wide, wide, wide, held((n, 128)), held((n, 128)), held((n, 128))],
-        [
-            pl.BlockSpec((n, 4 * span), lambda i, *_: (0, i)),
-            pl.BlockSpec((8, span), lambda i, *_: (0, i)),
-        ],
-        [shaped(BF16, n, 4 * width), shaped(F32, 8, width)],
+        [three, pl.BlockSpec((8, span), lambda i, *_: (0, i))],
+        [shaped(BF16, 3, n, width), shaped(F32, 8, width)],
         (spans, qkv, ext, attended, rest, grads, ext_k, cosine, sine), 0,
         prefetch=1,
         scratch=[
-            heads, pltpu.VMEM((pairs, 128, n), BF16), heads, heads, heads, heads, heads,
+            heads, pltpu.VMEM((pairs, 128, n), BF16), heads, turned, heads, turned, heads,
         ] + [pltpu.VMEM((n, span), F32)] * 3,
     )
 
@@ -1185,15 +1383,16 @@
     def gather_pieces(pieces):
         return [lax.all_gather(piece, "rows", axis=0, tiled=True) for piece in pieces]
 
+    late_weights = (w_out, w_up, w_down)
+    late_pieces = [
+        lax.dynamic_index_in_dim(w.reshape(R, -1, w.shape[1]), r, 0, keepdims=False)
+        for w in late_weights
+    ]
     if C == 2:
-        x, qkv_other, *pieces, proj_other, pack_other = start_up(
-            R, (Q, DS, ROW_LEN), tokens, w_qkv, w_out, w_up, w_down, w_proj,
-            packed.reshape(8, -1),
+        x, qkv_other, proj_other, pack_other = start_up(
+            R, (Q, DS, ROW_LEN), tokens, w_qkv, w_proj, packed.reshape(8, -1)
         )
         wqkv_slots = [w_qkv, qkv_other]
-        wout_slots, wup_slots, wdown_slots = (
-            [own, other] for own, other in zip((w_out, w_up, w_down), gather_pieces(pieces))
-        )
         wproj = jnp.concatenate(in_order([w_proj, proj_other]), axis=0)
         packs = [packed, pack_other.reshape(-1)]
     else:
@@ -1216,9 +1415,7 @@
             others = gather_pieces([shift_cols(piece, k) for k in range(1, C)])
             return [shard] + [other.reshape(shard.shape) for other in others]
 
-        wqkv_slots, wout_slots, wup_slots, wdown_slots = (
-            gather_slots(shard) for shard in (w_qkv, w_out, w_up, w_down)
-        )
+        wqkv_slots = gather_slots(w_qkv)
         wproj = jnp.concatenate(
             in_order([w_proj] + [shift_cols(w_proj, k) for k in range(1, C)]), axis=0
         )
@@ -1249,8 +1446,6 @@
     query_places = jnp.arange(Q, dtype=jnp.int32)
     position = jnp.concatenate([query_places % QLEN, places - slot_begin])
     cosine, sine = rotary_tables(position)
-    share = D // R
-    paired = share == 64
     segment = jnp.concatenate([(query_places // QLEN) % SEGMENTS, slot_id])
     lane = jnp.arange(128, dtype=jnp.int32)[None, :] % DH
     same = segment[:, None] == lane
@@ -1284,13 +1479,29 @@
     for k in range(C):
         first = (picks, lows, highs) if k == 0 else ()
         qkv.append(project_qkv(x, wqkv_slots[k], bqkv_slots[k], cosine, sine, first))
+        if k == 0:
+            flat = jnp.concatenate([piece.reshape(-1, D) for piece in late_pieces])
+            flat, _ = lax.optimization_barrier((flat, x))
+            arrived = [shift_cols(flat, j) for j in range(1, C)]
+            arrived = [pass_on(a) for a in arrived]
+            ends_of = [0]
+            for piece in late_pieces:
+                ends_of.append(ends_of[-1] + piece.size // D)
+            wout_slots, wup_slots, wdown_slots = (
+                [own] + gather_pieces([
+                    a[ends_of[j] : ends_of[j + 1]].reshape(late_pieces[j].shape) for a in arrived
+                ])
+                for j, own in enumerate(late_weights)
+            )
+            wout_slots, wup_slots, wdown_slots = (
+                [slot.reshape(own.shape) for slot in slots_of]
+                for slots_of, own in zip((wout_slots, wup_slots, wdown_slots), late_weights)
+            )
         out, rest, ext = attention_forward(spans, qkv[k], ext_k, ext_q, tile)
         attended.append(out)
         rests.append(rest)
         exts.append(ext)
-    normed_one, inverse_one, hidden_low, hidden_left = out_and_norm(
-        x, vectors, attended, wout_slots, paired
-    )
+    normed_one, inverse_one, hidden_low, hidden_t = out_and_norm(x, vectors, attended, wout_slots)
     active, slopes = zip(*[up_and_gelu(hidden_low, wup_slots[k], bup_slots[k]) for k in range(C)])
     normed_two, inverse_two, output_low, unit, unit_low, unit_inverse = down_and_norm(
         normed_one, vectors, wproj, active, wdown_slots
@@ -1335,27 +1546,25 @@
 
     core = r % 2
     slots_back = range(C - 1, -1, -1)
+    share = D // R
     x_bit, *z_bits = [1 << b for b in range(1, R.bit_length() - 1)]
-    half = D // 2
 
     def side_of(bit):
         return ((r // bit) % 2).astype(jnp.int32)
 
-    def core_order(left):
-        if paired:
-            return left
-        return left.reshape(n, R // 2, 2, share).transpose(0, 2, 1, 3).reshape(n, D)
-
-    def columns_of(left, side):
-        return lax.dynamic_slice_in_dim(left, side * half, half, 1)
+    def halves_of(left_t):
+        return left_t.reshape(R // 2, 2, share, n)
+
+    def rows_of(left, side):
+        return lax.dynamic_index_in_dim(left, side, 1, keepdims=False).reshape(-1, n)
 
     def send_plain(left, right):
-        part = mm(columns_of(left, 1 - core), right, TN).astype(BF16)
+        part = mm(rows_of(left, 1 - core), right).astype(BF16)
         Order.last += (part,)
         return swap_rows(part, 1)
 
     def keep_plain(left, right, arrived, k):
-        kept = mm(columns_of(left, core), right, TN) + arrived.astype(F32)
+        kept = mm(rows_of(left, core), right) + arrived.astype(F32)
         if k > 0:
             kept = kept.astype(BF16)
         Order.last += (kept,)
@@ -1364,9 +1573,6 @@
     def next_fold(states, bit, inner):
         send, keep = fold(side_of(bit), [s[0] for s in states], [s[1] for s in states], inner)
         return keep, swap_rows(send, bit)
-
-    def close(state):
-        return state[0] + state[1].astype(F32)
 
     def cols_state(kept):
         rest = kept[1]
@@ -1374,10 +1580,10 @@
             rest = rest.astype(F32) + other.astype(F32)
         return kept[0], rest
 
-    embed_grad, resid_two_grad, branch, branch_left, head_sums = head_pull(
-        unit_grad, unit, unit_inverse, wproj, normed_two, inverse_two, vectors, paired
-    )
-    down_left, down_right = core_order(branch_left), active
+    embed_grad, resid_two_grad, branch, branch_t, head_sums = head_pull(
+        unit_grad, unit, unit_inverse, wproj, normed_two, inverse_two, vectors
+    )
+    down_left, down_right = halves_of(branch_t), active
     pre_grads, up_sums, down_kept = [None] * C, [None] * C, [None] * C
     down_arrived = [None] * C
     for k in slots_back:
@@ -1386,23 +1592,18 @@
         pre_grads[k], up_sums[k] = up_pull(branch, wdown_slots[k], slopes[k])
         if k > 0:
             down_kept[k] = keep_plain(down_left, down_right[k], down_arrived[k], k)
-    up_left, up_right = core_order(hidden_left), pre_grads
+    up_left, up_right = halves_of(hidden_t), pre_grads
     up_arrived, up_kept = [None] * C, [None] * C
     for k in slots_back:
         up_arrived[k] = send_plain(up_left, up_right[k])
     down_kept[0] = keep_plain(down_left, down_right[0], down_arrived[0], 0)
     for k in slots_back[:-1]:
         up_kept[k] = keep_plain(up_left, up_right[k], up_arrived[k], k)
-    resid_one_grad, branch_one_left, hidden_sums, *attended_grads = hidden_pull(
-        resid_two_grad, normed_one, inverse_one, vectors, pre_grads, wup_slots, wout_slots, paired
+    resid_one_grad, branch_one_t, hidden_sums, *attended_grads = hidden_pull(
+        resid_two_grad, normed_one, inverse_one, vectors, pre_grads, wup_slots, wout_slots
     )
     up_kept[0] = keep_plain(up_left, up_right[0], up_arrived[0], 0)
     mixed_grads, mixed_sums = [None] * C, [None] * C
-    x_left = x.reshape(n, R // 2, 2, share).transpose(0, 2, 1, 3).reshape(n, D)
-    late_lefts = [x_left, core_order(branch_one_left)]
-    span = min(width, ATTENTION_LANES)
-    late_state, late_arrived = [None] * C, [None] * C
-
     def gather_small():
         proj_grad = mm(embed_grad, output_low, TN).reshape(R, -1, C, width)
         def cut(values, slot_rows):
@@ -1432,69 +1633,22 @@
             tile,
         )
 
-    def late_product(columns, k):
-        right = mixed_grads[k]
-        parts = []
-        for first in range(0, width, span):
-            at = 4 * first
-            parts.append(mm(columns[0], right[:, at : at + 3 * span], TN))
-            parts.append(mm(columns[1], right[:, at + 3 * span : at + 4 * span], TN))
-        return jnp.concatenate(parts, axis=1)
-
-    def send_late(k):
-        part = late_product([columns_of(left, 1 - core) for left in late_lefts], k).astype(BF16)
-        Order.last += (part,)
-        late_arrived[k] = swap_rows(part, 1)
-
-    def keep_late(k):
-        total = late_product([columns_of(left, core) for left in late_lefts], k)
-        total = (total + late_arrived[k].astype(F32)).reshape(-1, 2, 2 * share, 4 * width)
-        side = side_of(z_bits[0])
-        part = lax.dynamic_index_in_dim(total, 1 - side, 1, keepdims=False).astype(BF16)
-        kept = lax.dynamic_index_in_dim(total, side, 1, keepdims=False)
-        part, kept = (v.reshape(1, half // 2, 4 * width) for v in (part, kept))
-        Order.last += (part, kept)
-        late_state[k] = (kept, swap_rows(part, z_bits[0]))
-
     for k in slots_back[:-1]:
         pull_attention(k)
-        send_late(k)
     wide_state = next_fold([cols_state(down_kept), cols_state(up_kept)], x_bit, share)
     pull_attention(0)
-    wide_state = next_fold([wide_state], z_bits[0], share)
-    send_late(0)
-    for k in slots_back[:-1]:
-        keep_late(k)
     sent = [
         shift_cols(token_pull((c + k) % C, resid_one_grad, mixed_grads, wqkv_slots, BF16), k)
         for k in range(1, C)
     ]
-    keep_late(0)
-    late_bits = z_bits[1:] + [x_bit]
-
-    def fold_late(k, bit):
-        late_state[k] = next_fold([late_state[k]], bit, share if bit == x_bit else 2 * share)
-
-    for k in slots_back[:-1]:
-        fold_late(k, late_bits[0])
     own_tokens = token_pull(c, resid_one_grad, mixed_grads, wqkv_slots, F32)
-    for place, bit in enumerate(late_bits):
-        fold_late(0, bit)
-        if place < len(z_bits) - 1:
-            wide_state = next_fold([wide_state], z_bits[place + 1], share)
-        for k in slots_back[:-1]:
-            if place + 1 < len(late_bits):
-                fold_late(k, late_bits[place + 1])
+    late_grad, wide_grad = late_sums(
+        R, C, halves_of(x.T), halves_of(branch_one_t), mixed_grads, attended, *wide_state
+    )
     small = small_sum(R, C, gather_small())
-    late_grad = close(late_state[0])
-    for k in slots_back[:-1]:
-        late_grad = late_grad + shift_cols(close(late_state[k]).astype(BF16), C - k).astype(F32)
-    late_grad = late_grad[0].reshape(share, width // span, 4, span).transpose(2, 0, 1, 3)
-    late_grad = late_grad.reshape(4, share, width)
+    tokens_grad = assemble(c, Q, [own_tokens] + sent)
     qkv_grad, out_grad = late_grad[:3], late_grad[3]
-    down_grad, up_grad = close(wide_state)
-    ordered = in_order([own_tokens] + [s.astype(F32) for s in sent])
-    tokens_grad = jnp.concatenate([s[:Q] for s in ordered] + [s[Q:] for s in ordered], axis=0)
+    down_grad, up_grad = wide_grad
     one = D // (C * R)
     up_part = bup_slots[0].shape[1] // R
     bounds = [3 * one, 3 * one + up_part]

time: 938 us -> 857 us (0.914)
  Pallas kernels: 605 us -> 684 us
  starting transfers between devices: 72.5 us -> 9.4 us
  waiting for transfers between devices: 46.6 us -> 2.31 us
  matrix products: 92.8 us -> 56.2 us
  other arithmetic: 41.7 us -> 25.1 us
    pallas_call x29 -> x26, Pallas kernels: 605 us -> 684 us  [call(): pl.pallas_call(wrapped, grid_spec=pltpu.PrefetchScalarGridSpec(num_scalar...]
    ppermute x15 -> x5, starting transfers between devices: 50.3 us -> 0.76 us  [swap_rows(): return lax.ppermute(value, 'rows', [(i, i ^ bit) for i in range(R)])]
    ppermute x15 -> x5, waiting for transfers between devices: 41.6 us -> 0.01 us  [swap_rows(): return lax.ppermute(value, 'rows', [(i, i ^ bit) for i in range(R)])]
    dot_general x25 -> x9, matrix products: 92.8 us -> 56.2 us  [mm(): return lax.dot_general(left, right, dims, preferred_element_type=F32)]
    ppermute x7, starting transfers between devices: 22.1 us -> 8.52 us  [shift_cols(): return lax.ppermute(value, 'cols', [(i, (i + k) % C) for i in range(C)])]
  transfers between devices with their start and end apart: 25 -> 15, of which waited for: 4 -> 1; matrix products, arithmetic and copies ran while one was open for 15% -> 12% of each run, Pallas kernels for 42% -> 60%
where the time goes in v6:
time: 857 us; the launch traced here: 845 us
  Pallas kernels  684 us (80%)
  matrix products  56.2 us (7%)
  local copies, waits for them, and re-layouts  51.4 us (6%)
  other arithmetic  25.1 us (3%)
  between operations  15.8 us (2%)
  starting transfers between devices  9.4 us (1%)
    pallas_call x26, Pallas kernels, call(): pl.pallas_call(wrapped, grid_spec=pltpu.PrefetchScalarGridSpec(num_scalar...  684 us
    dot_general x9, matrix products, mm(): return lax.dot_general(left, right, dims, preferred_element_type=F32)  56.2 us
  transfers between devices with their start and end apart: 15, of which 1 were waited for; matrix products, arithmetic and copies ran while one was open for 12% of the time, Pallas kernels for 60%

profile of v6, /device:TPU:0, one launch (start us, length us, event | category | flops | bytes accessed | tf_op | source)
XLA Modules:
  0.0 844.7 jit_solution(4805796717134821727)
XLA Ops:
  14.3 1.0 dynamic-slice_bitcast_fusion.1
  15.3 1.0 constant_dynamic-slice_fusion.6
  16.4 53.3 %start_up.1 = (bf16[1536,1024]{1,0:T(8,128)(2,1)}, bf16[16,192,512]{2,1,0:T(8,128)(2,1)}, bf16[512,128]{1,0:T(8,128)(2,1)}, f32[8,832]{1,0:T(8,128)}) custom-call(bf16[3072,512]{1,0:T(8,128)(2,1)} %refs_0_.1, bf16[16,192,512]{2,1,0:T(8,128)(2,1)} %bitcast.131, bf16[512,128]{1,0:T(8,128)(2,1)} %refs_2_.2, f32[8,832]{1,0:T(8,128)} %reshape.321.refs_3_), custom_call_target="tpu_custom_call" | custom-call | bytes 1024 | tf_op jit(solution)/shard_map/start_up/pallas_call | solution.py:60
  69.7 1.6 collective-permute-start
  73.6 0.9 copy.66
  75.1 2.8 fusion.3
  77.9 1.6 pad_maximum_fusion.refs_3_.refs_7_
  79.5 1.6 pad_maximum_fusion.1.refs_4_.refs_8_
  81.0 5.9 fusion.2.refs_5_.refs_4_
  86.9 19.2 %project_qkv.2.refs_1_ = bf16[3,1536,512]{2,1,0:T(8,128)(2,1)} custom-call(bf16[1536,1024]{1,0:T(8,128)(2,1)} %get-tuple-element.66.refs_0_, bf16[3,1024,512]{2,1,0:T(8,128)(2,1)} %refs_4_.5, f32[3,512]{1,0:T(4,128)} %refs_2_.3, f32[1536,128]{1,0:T(8,128)} %pad_maximum_fusion.refs_3_.refs_7_, f32[1536,128]{1,0:T(8,128)} %pad_maximum_fusion.1.refs_4_.refs_8_, ...), custom_call_target="tpu_custom_call" | custom-call | flops 4831838208 | bytes 12589056 | tf_op jit(solution)/shard_map/project_qkv/pallas_call | solution.py:60
  106.9 2.0 pass_on.1.refs_4_
  108.9 1.5 slice.258
  110.5 1.8 fusion.21
  118.3 1.0 fusion.refs_2_.refs_6_
  119.4 1.0 select_convert_fusion.refs_3_
  120.4 32.8 %attention_forward.2 = (bf16[1536,512]{1,0:T(8,128)(2,1)}, bf16[1536,512]{1,0:T(8,128)(2,1)}, bf16[1536,512]{1,0:T(8,128)(2,1)}) custom-call(s32[12]{0:T(128)} %pad_add_fusion.1.refs_0_, bf16[3,1536,512]{2,1,0:T(8,128)(2,1)} %project_qkv.2.refs_1_, bf16[1536,128]{1,0:T(8,128)(2,1)} %fusion.refs_2_.refs_6_, bf16[1536,128]{1,0:T(8,128)(2,1)} %select_convert_fusion.refs_3_, ...), custom_call_target="tpu_custom_call" | custom-call | bytes 1024 | tf_op jit(solution)/shard_map/attention_forward/pallas_call | solution.py:60
  153.2 19.0 %project_qkv.3.refs_1_.refs_4_ = bf16[3,1536,512]{2,1,0:T(8,128)(2,1)} custom-call(bf16[1536,1024]{1,0:T(8,128)(2,1)} %get-tuple-element.66.refs_0_, bf16[3,1024,512]{2,1,0:T(8,128)(2,1)} %bitcast.134, f32[3,512]{1,0:T(4,128)} %slice.257.refs_2_, f32[1536,128]{1,0:T(8,128)} %pad_maximum_fusion.refs_3_.refs_7_, ...), custom_call_target="tpu_custom_call" | custom-call | flops 4831838208 | bytes 12589056 | tf_op jit(solution)/shard_map/project_qkv/pallas_call | solution.py:60
  172.3 33.2 %attention_forward.3 = (bf16[1536,512]{1,0:T(8,128)(2,1)}, bf16[1536,512]{1,0:T(8,128)(2,1)}, bf16[1536,512]{1,0:T(8,128)(2,1)}) custom-call(s32[12]{0:T(128)} %pad_add_fusion.1.refs_0_, bf16[3,1536,512]{2,1,0:T(8,128)(2,1)} %project_qkv.3.refs_1_.refs_4_, bf16[1536,128]{1,0:T(8,128)(2,1)} %fusion.refs_2_.refs_6_, ...), custom_call_target="tpu_custom_call" | custom-call | bytes 1024 | tf_op jit(solution)/shard_map/attention_forward/pallas_call | solution.py:60
  205.4 11.8 %out_and_norm.1 = (f32[1536,1024]{1,0:T(8,128)}, f32[1536,1]{1,0:T(8,128)}, bf16[1536,1024]{1,0:T(8,128)(2,1)}, bf16[1024,1536]{1,0:T(8,128)(2,1)}) custom-call(bf16[1536,1024]{1,0:T(8,128)(2,1)} %get-tuple-element.66.refs_0_, f32[8,1024]{1,0:T(8,128)} %stack.63.refs_1_.refs_6_.refs_3_, bf16[1536,512]{1,0:T(8,128)(2,1)} %get-tuple-element.69.refs_5_.refs_2_.refs_3_.refs_4_, ...), custom_call_target="tpu_custom_call" | custom-call | flops 3221225472 | bytes 21010432 | tf_op jit(solution)/shard_map/out_and_norm/pallas_call | solution.py:60
  217.2 22.4 %up_and_gelu.2 = (bf16[1536,2048]{1,0:T(8,128)(2,1)}, f32[1536,2048]{1,0:T(8,128)}) custom-call(bf16[1536,1024]{1,0:T(8,128)(2,1)} %get-tuple-element.74.refs_0_, bf16[1024,2048]{1,0:T(8,128)(2,1)} %refs_6_.1, f32[1,2048]{1,0:T(1,128)} %bitcast.178, f32[1536,1]{1,0:T(8,128)} %get-tuple-element.75.refs_3_.refs_2_), custom_call_target="tpu_custom_call" | custom-call | flops 16106127360 | bytes 26222592 | tf_op jit(solution)/shard_map/up_and_gelu/pallas_call | solution.py:60
  239.6 22.6 %up_and_gelu.3 = (bf16[1536,2048]{1,0:T(8,128)(2,1)}, f32[1536,2048]{1,0:T(8,128)}) custom-call(bf16[1536,1024]{1,0:T(8,128)(2,1)} %get-tuple-element.74.refs_0_, bf16[1024,2048]{1,0:T(8,128)(2,1)} %all-gather.6.cloned.1.call-done.refs_1_.refs_7_, f32[1,2048]{1,0:T(1,128)} %bitcast.179, bf16[1536,2048]{1,0:T(8,128)(2,1)} %get-tuple-element.76.refs_3_), custom_call_target="tpu_custom_call" | custom-call | flops 16106127360 | bytes 26222592 | tf_op jit(solution)/shard_map/up_and_gelu/pallas_call | solution.py:60
  262.2 23.6 %down_and_norm.1 = (f32[1536,1024]{1,0:T(8,128)}, f32[1536,1]{1,0:T(8,128)}, bf16[1536,1024]{1,0:T(8,128)(2,1)}, f32[1536,128]{1,0:T(8,128)}, bf16[1536,128]{1,0:T(8,128)(2,1)}, /*index=5*/f32[1536,1]{1,0:T(8,128)}) custom-call(f32[1536,1024]{1,0:T(8,128)} %get-tuple-element.72.refs_0_.refs_1_, f32[8,1024]{1,0:T(8,128)} %stack.63.refs_1_.refs_6_.refs_3_, ...), custom_call_target="tpu_custom_call" | custom-call | flops 12884901888 | bytes 38187008 | tf_op jit(solution)/shard_map/down_and_norm/pallas_call | solution.py:60
  285.9 0.9 slice.214
  286.9 1.7 slice.213.refs_0_
  288.6 32.2 %gather_rows.1.refs_5_ = bf16[16,1024,128]{2,1,0:T(8,128)(2,1)} custom-call(bf16[1024,128]{1,0:T(8,128)(2,1)} %slice.213.refs_0_, f32[1536,1]{1,0:T(8,128)} %get-tuple-element.79.refs_1_.refs_5_), custom_call_target="tpu_custom_call" | custom-call | bytes 1024 | tf_op jit(solution)/shard_map/gather_rows/pallas_call | solution.py:60
  320.7 0.9 broadcast_select_fusion.1
  322.4 34.3 %score_forward.1.refs_6_ = f32[64,32]{1,0:T(8,128)} custom-call(s32[512]{0:T(512)} %reshape.318.refs_6_.refs_0_, s32[512]{0:T(512)} %sub.105.refs_7_.refs_1_, bf16[16384,128]{1,0:T(8,128)(2,1)} %bitcast.143, bf16[1024,128]{1,0:T(8,128)(2,1)} %pad_maximum_fusion.5.refs_3_, s32[16,4,1024]{2,1,0:T(4,128)} %fusion.2.refs_5_.refs_4_, ...), custom_call_target="tpu_custom_call" | custom-call | flops 4294967296 | bytes 4730880 | tf_op jit(solution)/shard_map/score_forward/pallas_call | solution.py:60
  358.3 2.7 collective-permute-start.2
  361.0 1.6 collective-permute-done.2
  363.1 1.4 subtract_multiply_fusion.refs_5_
  364.5 34.7 %score_backward.1 = (f32[16384,128]{1,0:T(8,128)}, f32[128,1024]{1,0:T(8,128)}) custom-call(s32[512]{0:T(512)} %reshape.318.refs_6_.refs_0_, s32[512]{0:T(512)} %sub.105.refs_7_.refs_1_, bf16[16384,128]{1,0:T(8,128)(2,1)} %bitcast.144, bf16[1024,128]{1,0:T(8,128)(2,1)} %pad_maximum_fusion.5.refs_3_, s32[16,4,1024]{2,1,0:T(4,128)} %fusion.2.refs_5_.refs_4_, ...), custom_call_target="tpu_custom_call" | custom-call | flops 8589934592 | bytes 13643776 | tf_op jit(solution)/shard_map/score_backward/pallas_call | solution.py:60
  399.2 2.0 copy.73
  401.2 1.0 dynamic-slice_bitcast_fusion
  402.2 2.1 collective-permute-start.3
  404.3 2.0 constant_dynamic-slice_fusion.2
  406.2 36.6 %scatter_rows.1.refs_7_ = f32[1024,128]{1,0:T(8,128)} custom-call(f32[16,1024,128]{2,1,0:T(8,128)} %bitcast.137, f32[128,1024]{1,0:T(8,128)} %get-tuple-element.80.refs_1_), custom_call_target="tpu_custom_call" | custom-call | bytes 1024 | tf_op jit(solution)/shard_map/scatter_rows/pallas_call | solution.py:60
  442.9 2.0 pad_maximum_fusion.2.refs_0_
  444.9 12.5 %head_pull.1 = (bf16[1536,128]{1,0:T(8,128)(2,1)}, f32[1536,1024]{1,0:T(8,128)}, bf16[1536,1024]{1,0:T(8,128)(2,1)}, bf16[1024,1536]{1,0:T(8,128)(2,1)}, f32[8,1024]{1,0:T(8,128)}) custom-call(f32[1536,128]{1,0:T(8,128)} %pad_maximum_fusion.2.refs_0_, f32[1536,128]{1,0:T(8,128)} %get-tuple-element.82.refs_1_, f32[1536,1]{1,0:T(8,128)} %get-tuple-element.83.refs_2_, ...), custom_call_target="tpu_custom_call" | custom-call | flops 805306368 | bytes 21180416 | tf_op jit(solution)/shard_map/head_pull/pallas_call | solution.py:60
  457.4 2.3 constant_dynamic-slice_fusion.4
  459.8 7.0 convolution_convert_fusion.3.refs_4_
  467.0 4.6 convolution_convert_fusion.2.refs_5_
  472.0 14.2 %up_pull.2 = (bf16[1536,2048]{1,0:T(8,128)(2,1)}, f32[8,2048]{1,0:T(8,128)}) custom-call(bf16[1536,1024]{1,0:T(8,128)(2,1)} %get-tuple-element.86.refs_0_, bf16[2048,1024]{1,0:T(8,128)(2,1)} %all-gather.8.cloned.1.call-done.refs_6_.refs_1_, f32[1536,2048]{1,0:T(8,128)} %get-tuple-element.88.refs_2_, f32[8,1024]{1,0:T(8,128)} %get-tuple-element.89.refs_3_, ...), custom_call_target="tpu_custom_call" | custom-call | flops 6442450944 | bytes 26279936 | tf_op jit(solution)/shard_map/up_pull/pallas_call | solution.py:60
  486.3 6.4 convolution_convert_fusion.1.refs_11_
  492.9 8.3 add_convert_fusion.1.refs_4_
  501.5 14.2 %up_pull.3 = (bf16[1536,2048]{1,0:T(8,128)(2,1)}, f32[8,2048]{1,0:T(8,128)}) custom-call(bf16[1536,1024]{1,0:T(8,128)(2,1)} %get-tuple-element.86.refs_0_, bf16[2048,1024]{1,0:T(8,128)(2,1)} %refs_1_.5, f32[1536,2048]{1,0:T(8,128)} %get-tuple-element.87.refs_2_, f32[8,2048]{1,0:T(8,128)} %get-tuple-element.91.refs_3_, ...), custom_call_target="tpu_custom_call" | custom-call | flops 6442450944 | bytes 26279936 | tf_op jit(solution)/shard_map/up_pull/pallas_call | solution.py:60
  515.7 7.5 convolution_convert_fusion.refs_12_
  523.3 6.0 add_convert_fusion.refs_14_
  529.4 1.7 collective-permute-start.9
  531.7 3.4 copy.71
  537.3 9.5 %convert_add_fusion.1.refs_13_ = f32[512,2048]{1,0:T(8,128)} fusion(bf16[512,2048]{1,0:T(8,128)(2,1)} %collective-permute-done.5, bf16[512,1536]{1,0:T(8,128)(2,1)} %bitcast.156, bf16[1536,2048]{1,0:T(8,128)(2,1)} %get-tuple-element.76.refs_3_), kind=kOutput, calls=%fused_computation.2 | convolution fusion | flops 3223322624 | bytes 14155776 | tf_op jit(solution)/shard_map/dot_general | solution.py:23
  546.8 28.0 %hidden_pull.1 = (f32[1536,1024]{1,0:T(8,128)}, bf16[1024,1536]{1,0:T(8,128)(2,1)}, f32[8,1024]{1,0:T(8,128)}, bf16[1536,512]{1,0:T(8,128)(2,1)}, bf16[1536,512]{1,0:T(8,128)(2,1)}) custom-call(f32[1536,1024]{1,0:T(8,128)} %get-tuple-element.85.refs_0_, f32[1536,1024]{1,0:T(8,128)} %get-tuple-element.72.refs_0_.refs_1_, ...), custom_call_target="tpu_custom_call" | custom-call | bytes 1024 | tf_op jit(solution)/shard_map/hidden_pull/pallas_call | solution.py:60
  574.8 6.2 convert_add_fusion.refs_10_
  581.1 46.4 %attention_backward.2 = (bf16[3,1536,512]{2,1,0:T(8,128)(2,1)}, f32[8,512]{1,0:T(8,128)}) custom-call(s32[12]{0:T(128)} %pad_add_fusion.1.refs_0_, bf16[3,1536,512]{2,1,0:T(8,128)(2,1)} %project_qkv.3.refs_1_.refs_4_, bf16[1536,512]{1,0:T(8,128)(2,1)} %get-tuple-element.100.refs_2_, bf16[1536,512]{1,0:T(8,128)(2,1)} %get-tuple-element.71.refs_3_.refs_6_.refs_5_, ...), custom_call_target="tpu_custom_call" | custom-call | bytes 1024 | tf_op jit(solution)/shard_map/attention_backward/pallas_call | solution.py:60
  627.5 8.9 %fold.1 = (bf16[2,256,2048]{2,1,0:T(8,128)(2,1)}, f32[2,256,2048]{2,1,0:T(8,128)}) custom-call(s32[1]{0:T(128)} %bitcast.41.refs_0_, f32[1,512,2048]{2,1,0:T(8,128)} %bitcast.132, f32[1,512,2048]{2,1,0:T(8,128)} %bitcast.133, bf16[1,512,2048]{2,1,0:T(8,128)(2,1)} %bitcast.44.refs_3_, bf16[1,512,2048]{2,1,0:T(8,128)(2,1)} %bitcast.45.refs_4_, ...), custom_call_target="tpu_custom_call" | custom-call | bytes 1024 | tf_op jit(solution)/shard_map/fold/pallas_call | solution.py:60
  640.5 46.5 %attention_backward.3 = (bf16[3,1536,512]{2,1,0:T(8,128)(2,1)}, f32[8,512]{1,0:T(8,128)}) custom-call(s32[12]{0:T(128)} %pad_add_fusion.1.refs_0_, bf16[3,1536,512]{2,1,0:T(8,128)(2,1)} %project_qkv.2.refs_1_, bf16[1536,512]{1,0:T(8,128)(2,1)} %get-tuple-element.97.refs_2_, bf16[1536,512]{1,0:T(8,128)(2,1)} %get-tuple-element.69.refs_5_.refs_2_.refs_3_.refs_4_, ...), custom_call_target="tpu_custom_call" | custom-call | bytes 1024 | tf_op jit(solution)/shard_map/attention_backward/pallas_call | solution.py:60
  687.0 11.8 %token_pull.2.refs_6_ = bf16[1536,512]{1,0:T(8,128)(2,1)} custom-call(s32[1]{0:T(128)} %bitcast.46.refs_0_, f32[1536,1024]{1,0:T(8,128)} %get-tuple-element.96.refs_1_, bf16[3,1536,512]{2,1,0:T(8,128)(2,1)} %get-tuple-element.106.refs_2_, bf16[3,1536,512]{2,1,0:T(8,128)(2,1)} %get-tuple-element.107.refs_3_, bf16[3,1024,512]{2,1,0:T(8,128)(2,1)} %refs_4_.5, ...), custom_call_target="tpu_custom_call" | custom-call | bytes 1024 | tf_op jit(solution)/shard_map/token_pull/pallas_call | solution.py:60
  698.8 12.5 %token_pull.3.refs_8_.refs_1_ = f32[1536,512]{1,0:T(8,128)} custom-call(s32[1]{0:T(128)} %bitcast.30.refs_0_, f32[1536,1024]{1,0:T(8,128)} %get-tuple-element.96.refs_1_, bf16[3,1536,512]{2,1,0:T(8,128)(2,1)} %get-tuple-element.106.refs_2_, bf16[3,1536,512]{2,1,0:T(8,128)(2,1)} %get-tuple-element.107.refs_3_, bf16[3,1024,512]{2,1,0:T(8,128)(2,1)} %refs_4_.5, ...), custom_call_target="tpu_custom_call" | custom-call | bytes 1024 | tf_op jit(solution)/shard_map/token_pull/pallas_call | solution.py:60
  715.7 1.4 reshape.347.refs_0_
  717.0 81.7 %late_sums.1 = (f32[4,64,512]{2,1,0:T(8,128)}, f32[2,64,2048]{2,1,0:T(8,128)}) custom-call(bf16[8,2,64,1536]{3,2,1,0:T(8,128)(2,1)} %bitcast.146, bf16[8,2,64,1536]{3,2,1,0:T(8,128)(2,1)} %bitcast.189, bf16[3,1536,512]{2,1,0:T(8,128)(2,1)} %get-tuple-element.106.refs_2_, bf16[3,1536,512]{2,1,0:T(8,128)(2,1)} %get-tuple-element.107.refs_3_, ...), custom_call_target="tpu_custom_call" | custom-call | flops 99999997952 | bytes 26738688 | tf_op jit(solution)/shard_map/late_sums/pallas_call | solution.py:60
  798.8 19.4 %small_sum.1.refs_3_ = f32[8,640]{1,0:T(8,128)} custom-call(f32[8,2,2,8,640]{4,3,2,1,0:T(8,128)} %reshape.347.refs_0_, f32[4,64,512]{2,1,0:T(8,128)} %get-tuple-element.113.refs_1_), custom_call_target="tpu_custom_call" | custom-call | bytes 1024 | tf_op jit(solution)/shard_map/small_sum/pallas_call | solution.py:60
  821.0 1.8 slice.232
  824.6 1.6 slice_bitcast_fusion.2
  826.1 1.0 slice_bitcast_fusion
  827.2 10.5 %assemble.1 = f32[3072,512]{1,0:T(8,128)} custom-call(s32[13]{0:T(128)} %pad_add_fusion.2.refs_0_, f32[1536,512]{1,0:T(8,128)} %token_pull.3.refs_8_.refs_1_, bf16[1536,512]{1,0:T(8,128)(2,1)} %collective-permute-done.10.refs_2_, f32[8,640]{1,0:T(8,128)} %small_sum.1.refs_3_), custom_call_target="tpu_custom_call" | custom-call | bytes 1024 | tf_op jit(solution)/shard_map/assemble/pallas_call | solution.py:60
  (206 shorter events, 36.0 us)
Async XLA Ops:
  7.2 198.2 %all-gather.4.cloned.1.call-start = ((), (), s32[]{:S(2)}) async-start(), calls=%async_computation | async-start | bytes 1114112 | tf_op jit(solution)/shard_map/all_gather | solution.py:1384
  16.4 54.9 %copy-start.19 = (s32[16,2,4]{0,2,1:T(4,128)S(1)}, s32[16,2,4]{0,2,1:T(4,128)}, u32[]{:S(2)}) copy-start(s32[16,2,4]{0,2,1:T(4,128)} %param.20) | copy-start | bytes 1540
  16.4 57.2 %copy-start.14 = (s32[32,64,32]{1,2,0:T(8,128)S(1)}, s32[32,64,32]{1,2,0:T(8,128)}, u32[]{:S(2)}) copy-start(s32[32,64,32]{1,2,0:T(8,128)} %param.21) | copy-start | bytes 786436
  69.7 36.3 %collective-permute-start = (bf16[288,1024]{1,0:T(8,128)(2,1)S(1)}, bf16[288,1024]{1,0:T(8,128)(2,1)S(1)}, u32[]{:S(2)}, u32[]{:S(2)}) collective-permute-start(bf16[288,1024]{1,0:T(8,128)(2,1)S(1)} %pad_maximum_fusion.3), channel_id=1, source_target_pairs={{0,1},{1,0},{2,3},{3,2},{4,5},{5,4},{6,7},{7,6},{8,9},{9,8},{10,11... | collective-permute-start | bytes 1769480 | tf_op jit(solution)/shard_map/ppermute | solution.py:1362
  106.1 7.8 copy-start.18
  106.1 11.5 %copy-start.15 = (bf16[512,128]{1,0:T(8,128)(2,1)S(1)}, bf16[512,128]{1,0:T(8,128)(2,1)}, u32[]{:S(2)}) copy-start(bf16[512,128]{1,0:T(8,128)(2,1)} %refs_2_.2) | copy-start | bytes 393220
  106.1 11.5 %copy-start.17 = (bf16[512,128]{1,0:T(8,128)(2,1)S(1)}, bf16[512,128]{1,0:T(8,128)(2,1)}, u32[]{:S(2)}) copy-start(bf16[512,128]{1,0:T(8,128)(2,1)} %get-tuple-element.73) | copy-start | bytes 393220
  106.1 0.8 copy-start.13
  108.9 9.4 %copy-start.21 = (s32[12]{0:T(128)S(1)}, s32[12]{0:T(128)}, u32[]{:S(2)}) copy-start(s32[12]{0:T(128)} %constant.286) | copy-start | bytes 148
  110.4 129.2 %all-gather.6.cloned.1.call-start = ((), (), s32[]{:S(2)}) async-start(), calls=%async_computation.1 | async-start | bytes 4456448 | tf_op jit(solution)/shard_map/all_gather | solution.py:1384
  113.1 149.2 %all-gather.8.cloned.1.call-start = ((), (), s32[]{:S(2)}) async-start(), calls=%async_computation.2 | async-start | bytes 4456448 | tf_op jit(solution)/shard_map/all_gather | solution.py:1384
  262.2 24.6 %copy-start.20 = (s32[32]{0:T(128)S(1)}, s32[32]{0:T(128)}, u32[]{:S(2)}) copy-start(s32[32]{0:T(128)} %param.22) | copy-start | bytes 388
  286.8 34.0 %collective-permute-start.1 = (bf16[512,128]{1,0:T(8,128)(2,1)S(1)}, bf16[512,128]{1,0:T(8,128)(2,1)S(1)}, u32[]{:S(2)}, u32[]{:S(2)}) collective-permute-start(bf16[512,128]{1,0:T(8,128)(2,1)S(1)} %slice.214), channel_id=1, source_target_pairs={{0,1},{1,0},{2,3},{3,2},{4,5},{5,4},{6,7},{7,6},{8,9},{9,8},{10,11... | collective-permute-start | bytes 393224 | tf_op jit(solution)/shard_map/ppermute | solution.py:1362
  358.3 4.2 collective-permute-start.2
  364.5 39.8 %copy-start.3 = (bf16[1024,1536]{1,0:T(8,128)(2,1)S(1)}, bf16[1024,1536]{1,0:T(8,128)(2,1)}, u32[]{:S(2)}) copy-start(bf16[1024,1536]{1,0:T(8,128)(2,1)} %get-tuple-element.95) | copy-start | bytes 9437188
  402.2 40.7 %collective-permute-start.3 = (f32[512,128]{1,0:T(8,128)S(1)}, f32[512,128]{1,0:T(8,128)S(1)}, u32[]{:S(2)}, u32[]{:S(2)}) collective-permute-start(f32[512,128]{1,0:T(8,128)S(1)} %dynamic-slice_bitcast_fusion), channel_id=1, source_target_pairs={{0,1},{1,0},{2,3},{3,2},{4,5},{5,4},{6,7},{7,6},{8,9},{9,8},{10,11... | collective-permute-start | bytes 786440 | tf_op jit(solution)/shard_map/ppermute | solution.py:1362
  406.2 36.6 %copy-start.6 = (f32[1024,128]{1,0:T(8,128)S(1)}, f32[1024,128]{1,0:T(8,128)}, u32[]{:S(2)}) copy-start(f32[1024,128]{1,0:T(8,128)} %copy.73) | copy-start | bytes 1572868
  457.4 9.6 %slice-start.4 = ((s8[6291456]{0:T(1024)(128)(4,1)}), s8[4194304]{0:T(1024)(128)(4,1)S(1)}, s32[]{:S(2)}) async-start(s8[6291456]{0:T(1024)(128)(4,1)} %bitcast.190), calls=%async_computation.7 | async-start | bytes 8388608
  459.8 33.1 %copy-start.9 = (bf16[8,1,64,1536]{3,2,1,0:T(8,128)(2,1)}, bf16[8,1,64,1536]{3,2,1,0:T(8,128)(2,1)S(1)}, u32[]{:S(2)}) copy-start(bf16[8,1,64,1536]{3,2,1,0:T(8,128)(2,1)S(1)} %get-tuple-element.209) | copy-start | bytes 4718596
  459.8 7.2 slice-start.5
  466.8 4.8 copy-start.5
  466.8 26.0 %collective-permute-start.4 = (bf16[512,2048]{1,0:T(8,128)(2,1)S(1)}, bf16[512,2048]{1,0:T(8,128)(2,1)}, u32[]{:S(2)}, u32[]{:S(2)}) collective-permute-start(bf16[512,2048]{1,0:T(8,128)(2,1)S(1)} %convolution_convert_fusion.3.refs_4_), channel_id=1, source_target_pairs={{0,2},{2,0},{4,6},{6,4},{8,10},{10,8},{12,14},{14,12},{16,18},{18,... | collective-permute-start | bytes 6291464 | tf_op jit(solution)/shard_map/ppermute | solution.py:1365
  471.6 65.6 %collective-permute-start.5 = (bf16[512,2048]{1,0:T(8,128)(2,1)}, bf16[512,2048]{1,0:T(8,128)(2,1)}, u32[]{:S(2)}, u32[]{:S(2)}) collective-permute-start(bf16[512,2048]{1,0:T(8,128)(2,1)} %convolution_convert_fusion.2.refs_5_), channel_id=1, source_target_pairs={{0,2},{2,0},{4,6},{6,4},{8,10},{10,8},{12,14},{14,12},{16,18},{18,... | collective-permute-start | bytes 6291464 | tf_op jit(solution)/shard_map/ppermute | solution.py:1365
  472.0 14.2 %copy-start.10 = (bf16[8,1,64,1536]{3,2,1,0:T(8,128)(2,1)S(1)}, bf16[8,1,64,1536]{3,2,1,0:T(8,128)(2,1)}, u32[]{:S(2)}) copy-start(bf16[8,1,64,1536]{3,2,1,0:T(8,128)(2,1)} %get-tuple-element.208) | copy-start | bytes 4718596
  492.7 8.5 %copy-start.4 = (bf16[512,2048]{1,0:T(8,128)(2,1)}, bf16[512,2048]{1,0:T(8,128)(2,1)S(1)}, u32[]{:S(2)}) copy-start(bf16[512,2048]{1,0:T(8,128)(2,1)S(1)} %convolution_convert_fusion.1.refs_11_) | copy-start | bytes 6291460
  492.7 30.6 %collective-permute-start.6 = (bf16[512,2048]{1,0:T(8,128)(2,1)S(1)}, bf16[512,2048]{1,0:T(8,128)(2,1)}, u32[]{:S(2)}, u32[]{:S(2)}) collective-permute-start(bf16[512,2048]{1,0:T(8,128)(2,1)S(1)} %convolution_convert_fusion.1.refs_11_), channel_id=1, source_target_pairs={{0,2},{2,0},{4,6},{6,4},{8,10},{10,8},{12,14},{14,12},{16,18},{18,... | collective-permute-start | bytes 6291464 | tf_op jit(solution)/shard_map/ppermute | solution.py:1365
  501.1 126.3 %collective-permute-start.8 = (bf16[512,2048]{1,0:T(8,128)(2,1)}, bf16[512,2048]{1,0:T(8,128)(2,1)}, u32[]{:S(2)}, u32[]{:S(2)}) collective-permute-start(bf16[512,2048]{1,0:T(8,128)(2,1)} %add_convert_fusion.1.refs_4_), channel_id=1, source_target_pairs={{0,1},{1,0},{2,3},{3,2},{4,5},{5,4},{6,7},{7,6},{8,9},{9,8},{10,11... | collective-permute-start | bytes 6291464 | tf_op jit(solution)/shard_map/ppermute | solution.py:1362
  501.5 21.8 %slice-start = ((s8[6291456]{0:T(1024)(128)(4,1)}), s8[2097152]{0:T(1024)(128)(4,1)S(1)}, s32[]{:S(2)}) async-start(s8[6291456]{0:T(1024)(128)(4,1)} %bitcast.138), calls=%async_computation.3 | async-start | bytes 4194304
  515.7 7.6 slice-start.1
  515.7 7.6 copy-start.7
  523.3 51.5 %collective-permute-start.7 = (bf16[512,2048]{1,0:T(8,128)(2,1)}, bf16[512,2048]{1,0:T(8,128)(2,1)}, u32[]{:S(2)}, u32[]{:S(2)}) collective-permute-start(bf16[512,2048]{1,0:T(8,128)(2,1)} %convolution_convert_fusion.refs_12_), channel_id=1, source_target_pairs={{0,2},{2,0},{4,6},{6,4},{8,10},{10,8},{12,14},{14,12},{16,18},{18,... | collective-permute-start | bytes 6291464 | tf_op jit(solution)/shard_map/ppermute | solution.py:1365
  523.3 8.4 copy-start.1
  529.4 98.1 %collective-permute-start.9 = (bf16[512,2048]{1,0:T(8,128)(2,1)}, bf16[512,2048]{1,0:T(8,128)(2,1)}, u32[]{:S(2)}, u32[]{:S(2)}) collective-permute-start(bf16[512,2048]{1,0:T(8,128)(2,1)} %add_convert_fusion.refs_14_), channel_id=1, source_target_pairs={{0,1},{1,0},{2,3},{3,2},{4,5},{5,4},{6,7},{7,6},{8,9},{9,8},{10,11... | collective-permute-start | bytes 6291464 | tf_op jit(solution)/shard_map/ppermute | solution.py:1362
  531.7 3.4 copy-start.12
  537.3 37.5 %slice-start.2 = ((s8[6291456]{0:T(1024)(128)(4,1)}), s8[4194304]{0:T(1024)(128)(4,1)S(1)}, s32[]{:S(2)}) async-start(s8[6291456]{0:T(1024)(128)(4,1)} %bitcast.140), calls=%async_computation.5 | async-start | bytes 8388608
  546.8 28.0 %slice-start.3 = ((s8[6291456]{0:T(1024)(128)(4,1)}), s8[2097152]{0:T(1024)(128)(4,1)S(1)}, s32[]{:S(2)}) async-start(s8[6291456]{0:T(1024)(128)(4,1)} %bitcast.140), calls=%async_computation.6 | async-start | bytes 4194304
  546.8 28.0 %copy-start.8 = (bf16[8,1,64,1536]{3,2,1,0:T(8,128)(2,1)S(1)}, bf16[8,1,64,1536]{3,2,1,0:T(8,128)(2,1)}, u32[]{:S(2)}) copy-start(bf16[8,1,64,1536]{3,2,1,0:T(8,128)(2,1)} %get-tuple-element.207) | copy-start | bytes 4718596
  627.5 8.9 %copy-start.2 = (bf16[1536,1024]{1,0:T(8,128)(2,1)S(1)}, bf16[1536,1024]{1,0:T(8,128)(2,1)}, u32[]{:S(2)}) copy-start(bf16[1536,1024]{1,0:T(8,128)(2,1)} %get-tuple-element.110) | copy-start | bytes 9437188
  627.5 8.9 %copy-start.16 = (bf16[1536,128]{1,0:T(8,128)(2,1)S(1)}, bf16[1536,128]{1,0:T(8,128)(2,1)}, u32[]{:S(2)}) copy-start(bf16[1536,128]{1,0:T(8,128)(2,1)} %get-tuple-element.109) | copy-start | bytes 1179652
  636.4 80.6 %collective-permute-start.11 = (bf16[2,256,2048]{2,1,0:T(8,128)(2,1)}, bf16[2,256,2048]{2,1,0:T(8,128)(2,1)}, u32[]{:S(2)}, u32[]{:S(2)}) collective-permute-start(bf16[2,256,2048]{2,1,0:T(8,128)(2,1)} %get-tuple-element.105.refs_9_), channel_id=1, source_target_pairs={{0,4},{2,6},{4,0},{6,2},{8,12},{10,14},{12,8},{14,10},{16,20},{18,... | collective-permute-start | bytes 6291464 | tf_op jit(solution)/shard_map/ppermute | solution.py:1365
  698.8 12.5 %copy-start = (bf16[1536,512]{1,0:T(8,128)(2,1)S(1)}, bf16[1536,512]{1,0:T(8,128)(2,1)}, u32[]{:S(2)}) copy-start(bf16[1536,512]{1,0:T(8,128)(2,1)} %token_pull.2.refs_6_) | copy-start | bytes 4718596
  711.4 115.8 %collective-permute-start.10 = (bf16[1536,512]{1,0:T(8,128)(2,1)S(1)}, bf16[1536,512]{1,0:T(8,128)(2,1)}, u32[]{:S(2)}, u32[]{:S(2)}) collective-permute-start(bf16[1536,512]{1,0:T(8,128)(2,1)S(1)} %copy-done), channel_id=1, source_target_pairs={{0,1},{1,0},{2,3},{3,2},{4,5},{5,4},{6,7},{7,6},{8,9},{9,8},{10,11... | collective-permute-start | bytes 4718600 | tf_op jit(solution)/shard_map/ppermute | solution.py:1362
  798.8 27.4 %copy-start.11 = (f32[2,64,2048]{2,1,0:T(8,128)S(1)}, f32[2,64,2048]{2,1,0:T(8,128)}, u32[]{:S(2)}) copy-start(f32[2,64,2048]{2,1,0:T(8,128)} %get-tuple-element.114) | copy-start | bytes 3145732
Sparse Core Ops, SparseCore 0:
  110.5 37.0 all-gather.3
  149.8 49.5 all-gather.5
  201.7 49.2 all-gather.7

commit v7 on v6

--- a/solution.py
+++ b/solution.py
@@ -24,11 +24,11 @@
 
 
 def row_step(rows):
-    return 256 if rows % 256 == 0 else 128
+    return 512 if rows % 512 == 0 else 128
 
 
 def parts_of(step):
-    size = min(step, 256)
+    size = 256 if step % 256 == 0 else 128
     return [slice(first, first + size) for first in range(0, step, size)]
 
 
@@ -140,77 +140,45 @@
     return order
 
 
-def start_kernel(rows, cols_width, parts, *refs):
-    (tokens, qkv, proj, pack), refs = refs[:4], refs[4:]
-    (x, qkv_o, proj_o, pack_o), refs = refs[:4], refs[4:]
-    own_sem, sent, arrived, wide_sent, wide_arrived = refs
+def weights_kernel(rows, *refs):
+    (qkv, proj, pack, qkv_o, proj_o, pack_o), (sent, arrived, wide_sent, wide_arrived) = refs[:6], refs[6:]
     r, c = lax.axis_index("rows"), lax.axis_index("cols")
     partner = {"cols": 1 - c}
     bits = [1 << b for b in range(rows.bit_length() - 1)]
     greet([partner] + [{"rows": across(r, bit)} for bit in bits])
-    wide = [(qkv, qkv_o)]
-    copies, first = [], []
-    for place, (source, target) in enumerate(wide):
-        first.append(
-            send(source.at[r], target.at[r], sent.at[place], arrived.at[place], partner)
-        )
-    q_rows, d_rows, first_doc = parts
-    own = pl.ds(pl.multiple_of(c * cols_width, cols_width), cols_width)
-    spans = [(0, q_rows, 0), (first_doc, d_rows, q_rows)]
-    for place, (base, size, here) in enumerate(spans):
-        theirs = pl.ds(pl.multiple_of(base + (1 - c) * size, size), size)
-        mine = pl.ds(pl.multiple_of(base + c * size, size), size)
-        target = x.at[pl.ds(here, size), own]
-        copies.append(
-            send(tokens.at[theirs], target, sent.at[3 + place], arrived.at[3 + place], partner)
-        )
-        pltpu.make_async_copy(tokens.at[mine], target, own_sem.at[place]).start()
-    for place, (source, target) in enumerate([(proj, proj_o), (pack, pack_o)]):
-        copies.append(
-            send(source, target, sent.at[5 + place], arrived.at[5 + place], partner)
-        )
-    wide_copies = {}
+    pairs = [(qkv.at[r], qkv_o.at[r]), (proj, proj_o), (pack, pack_o)]
+    copies = [
+        send(source, target, sent.at[place], arrived.at[place], partner)
+        for place, (source, target) in enumerate(pairs)
+    ]
+    round_copies = {0: copies[0]}
     for piece, over in spread_order(rows):
         row = flipped(r, piece)
-        for place, (_, target) in enumerate(wide):
-            if piece == 0:
-                first[place].wait_recv()
-            else:
-                wide_copies[place, piece].wait_recv()
-            for bit in over:
-                wide_copies[place, piece | bit] = send(
-                    target.at[row], target.at[row],
-                    wide_sent.at[place, piece | bit], wide_arrived.at[place, piece | bit],
-                    {"rows": across(r, bit)},
-                )
-    for copy in first + list(wide_copies.values()):
+        round_copies[piece].wait_recv()
+        for bit in over:
+            round_copies[piece | bit] = send(
+                qkv_o.at[row], qkv_o.at[row], wide_sent.at[piece | bit], wide_arrived.at[piece | bit],
+                {"rows": across(r, bit)},
+            )
+    for copy in round_copies.values():
         copy.wait_send()
-    for copy in copies:
+    for copy in copies[1:]:
         copy.wait()
-    for place, (base, size, here) in enumerate(spans):
-        mine = pl.ds(pl.multiple_of(base + c * size, size), size)
-        target = x.at[pl.ds(here, size), own]
-        pltpu.make_async_copy(tokens.at[mine], target, own_sem.at[place]).wait()
-
-
-def start_up(rows, parts, tokens, qkv, proj, pack):
-    width = tokens.shape[1]
-    pieces = qkv.reshape(rows, -1, width)
-    x, qkv_o, proj_o, pack_o = call(
-        functools.partial(start_kernel, rows, width, parts), "start_up", (1,),
-        [ANYWHERE] * 4, [ANYWHERE] * 4,
-        [
-            shaped(BF16, parts[0] + parts[1], 2 * width), shaped(BF16, *pieces.shape),
-            shaped(BF16, *proj.shape), shaped(F32, *pack.shape),
+
+
+def gather_weights(rows, qkv, proj, pack):
+    pieces = qkv.reshape(rows, -1, qkv.shape[-1])
+    operands = (pieces, proj, pack)
+    qkv_o, proj_o, pack_o = call(
+        functools.partial(weights_kernel, rows), "gather_weights", (1,),
+        [ANYWHERE] * 3, [ANYWHERE] * 3, [shaped(o.dtype, *o.shape) for o in operands],
+        operands, 0, remote=1,
+        scratch=[
+            pltpu.SemaphoreType.DMA((3,)), pltpu.SemaphoreType.DMA((3,)),
+            pltpu.SemaphoreType.DMA((rows,)), pltpu.SemaphoreType.DMA((rows,)),
         ],
-        (tokens, pieces, proj, pack), 0, remote=1,
-        scratch=[
-            pltpu.SemaphoreType.DMA((2,)), pltpu.SemaphoreType.DMA((7,)),
-            pltpu.SemaphoreType.DMA((7,)), pltpu.SemaphoreType.DMA((1, rows)),
-            pltpu.SemaphoreType.DMA((1, rows)),
-        ],
-    )
-    return x, qkv_o.reshape(qkv.shape), proj_o, pack_o
+    )
+    return qkv_o.reshape(qkv.shape), proj_o, pack_o
 
 
 def gather_kernel(rows, own, out, own_sem, sent, arrived):
@@ -303,10 +271,80 @@
     )[0]
 
 
+def small_sums(rows, cols, parts, out, *refs):
+    bits = [1 << b for b in range(rows.bit_length() - 1)]
+    sent, arrived = refs[:2]
+    core_in, cols_in, totals = refs[2], refs[3], refs[4 : 4 + len(bits)]
+    row_ins = refs[4 + len(bits) :]
+    r, c = lax.axis_index("rows"), lax.axis_index("cols")
+    others = [{"cols": (c + cols - k) % cols} for k in range(1, cols)]
+    core = side_at(r, 1)
+    copies = {}
+
+    def first():
+        copies["core"] = send(
+            parts.at[:, 1 - core], core_in, sent.at[0], arrived.at[0], {"rows": across(r, 1)}
+        )
+
+    def second():
+        copies["core"].wait()
+        totals[0][...] = parts[:, core] + core_in[...]
+        for k in range(1, cols):
+            copies["cols", k] = send(
+                totals[0].at[:, k], cols_in.at[k - 1], sent.at[k], arrived.at[k], others[k - 1]
+            )
+
+    def third():
+        total = totals[0][:, 0]
+        for k in range(1, cols):
+            copies["cols", k].wait()
+            total = total + cols_in[k - 1]
+        pass_on(0, total)
+
+    def pass_on(level, total):
+        if level == len(bits) - 1:
+            out[...] = total[0]
+            return
+        whole = totals[1 + level]
+        whole[...] = total.reshape(whole.shape)
+        copies["row", level] = send(
+            whole.at[:, 1 - side_at(r, bits[1 + level])], row_ins[level],
+            sent.at[cols + level], arrived.at[cols + level],
+            {"rows": across(r, bits[1 + level])},
+        )
+
+    def later(level):
+        copies["row", level].wait()
+        pass_on(level + 1, totals[1 + level][:, side_at(r, bits[1 + level])] + row_ins[level][...])
+
+    return [first, second, third] + [
+        functools.partial(later, level) for level in range(len(bits) - 1)
+    ]
+
+
+def small_blocks(rows, cols, parts):
+    length = parts.shape[2]
+    width = -(-length // 1024) * 128
+    parts = jnp.pad(parts, ((0, 0), (0, 0), (0, 8 * width - length)))
+    parts = parts.reshape(rows // 2, 2, cols, 8, width)
+    levels = rows.bit_length() - 1
+    heights = [rows >> (level + 1) for level in range(1, levels)]
+    scratch = [
+        pltpu.SemaphoreType.DMA((cols + levels,)), pltpu.SemaphoreType.DMA((cols + levels,)),
+        pltpu.VMEM((rows // 2, cols, 8, width), F32),
+        pltpu.VMEM((cols - 1, rows // 2, 8, width), F32),
+        pltpu.VMEM((rows // 2, cols, 8, width), F32),
+    ]
+    scratch += [pltpu.VMEM((height, 2, 8, width), F32) for height in heights]
+    scratch += [pltpu.VMEM((height, 8, width), F32) for height in heights]
+    return parts, scratch
+
+
 def late_kernel(rows, cols, *refs):
     tokens_t, branch_t = refs[:2]
-    rights, attended, refs = refs[2 : 2 + cols], refs[2 + cols : 2 + 2 * cols], refs[2 + 2 * cols :]
-    (du_own, du_in, out, du_out), refs = refs[:4], refs[4:]
+    far_rights, far_attended, refs = refs[2 : 2 + cols], refs[2 + cols : 2 + 2 * cols], refs[2 + 2 * cols :]
+    (du_own, du_in, small, out, du_out, small_out), refs = refs[:6], refs[6:]
+    (rights, right_sem), refs = refs[:2], refs[2:]
     (core_out, core_in, x_out, x_in, kept, cols_out, cols_in), refs = refs[:7], refs[7:]
     r, c = lax.axis_index("rows"), lax.axis_index("cols")
     x_bit, *z_bits = [1 << b for b in range(1, rows.bit_length() - 1)]
@@ -314,31 +352,44 @@
     z_out, z_in, z_kept = refs[:levels], refs[levels : 2 * levels], refs[2 * levels : 3 * levels]
     refs = refs[3 * levels :]
     du_z_out, du_z_in, du_kept = refs[:levels], refs[levels : 2 * levels], refs[2 * levels : 3 * levels]
-    (core_sem, x_sem, cols_sem, z_sem, du_sem) = refs[3 * levels :]
+    refs = refs[3 * levels :]
+    (core_sem, x_sem, cols_sem, z_sem, du_sem), refs = refs[:5], refs[5:]
+    small_steps = small_sums(rows, cols, small, small_out, *refs)
     share = out.shape[1]
     others = [{"cols": (c + cols - k) % cols} for k in range(1, cols)]
     core, x_side = side_at(r, 1), side_at(r, x_bit)
     greet([{"rows": across(r, bit)} for bit in [1, x_bit] + z_bits] + others)
+    du_bits = z_bits[1:] + [x_bit]
     chunks = range(4)
     slots = range(cols - 1, -1, -1)
     copies = {}
 
-    def halves(total, side):
-        pairs = total.reshape(-1, 2, share, total.shape[1])
+    def halves(total, side, inner):
+        pairs = total.reshape(-1, 2, inner, total.shape[1])
         near = jnp.where(side == 0, pairs[:, 0], pairs[:, 1]).reshape(-1, total.shape[1])
         far = jnp.where(side == 0, pairs[:, 1], pairs[:, 0]).reshape(-1, total.shape[1])
         return near, far
 
     def product(side, slot, chunk):
         left = (tokens_t if chunk < 3 else branch_t)[:, side]
-        right = rights[slot][chunk] if chunk < 3 else attended[slot][...]
-        return mm(left.reshape(-1, left.shape[-1]), right)
+        return mm(left.reshape(-1, left.shape[-1]), rights[slot, chunk])
+
+    def load(slot, chunk):
+        source = far_rights[slot].at[chunk] if chunk < 3 else far_attended[slot]
+        return pltpu.make_async_copy(source, rights.at[slot, chunk], right_sem.at[slot, chunk])
+
+    for chunk in chunks:
+        for slot in slots:
+            load(slot, chunk).start()
 
     def begin(chunk):
         for slot in slots:
-            core_out[slot, chunk] = product(1 - core, slot, chunk).astype(BF16)
+            load(slot, chunk).wait()
+            if chunk >= 2:
+                copies["core", slot, chunk - 2].wait_send()
+            core_out[slot, chunk % 2] = product(1 - core, slot, chunk).astype(BF16)
             copies["core", slot, chunk] = send(
-                core_out.at[slot, chunk], core_in.at[slot, chunk],
+                core_out.at[slot, chunk % 2], core_in.at[slot, chunk],
                 core_sem.at[0, slot, chunk], core_sem.at[1, slot, chunk],
                 {"rows": across(r, 1)},
             )
@@ -347,7 +398,7 @@
         for slot in slots:
             total = product(core, slot, chunk)
             copies["core", slot, chunk].wait_recv()
-            near, far = halves(total + core_in[slot, chunk].astype(F32), x_side)
+            near, far = halves(total + core_in[slot, chunk].astype(F32), x_side, share)
             x_out[slot, chunk] = far.astype(BF16)
             kept[slot, chunk] = near
             copies["x", slot, chunk] = send(
@@ -381,7 +432,7 @@
             out[chunk] = total
             return
         bit = z_bits[level]
-        near, far = halves(total, side_at(r, bit))
+        near, far = halves(total, side_at(r, bit), share)
         z_out[level][chunk] = far.astype(BF16)
         z_kept[level][chunk] = near
         copies["z", level, chunk] = send(
@@ -397,8 +448,8 @@
         if level == levels:
             du_out[place] = total
             return
-        bit = z_bits[level]
-        near, far = halves(total, side_at(r, bit))
+        bit = du_bits[level]
+        near, far = halves(total, side_at(r, bit), share if bit == x_bit else 2 * share)
         du_z_out[level][place] = far.astype(BF16)
         du_kept[level][place] = near
         copies["du", level, place] = send(
@@ -421,11 +472,16 @@
         if 3 <= turn < 3 + levels:
             for place in range(2):
                 after_du(place, turn - 3)
-    for copy in copies.values():
-        copy.wait_send()
-
-
-def late_sums(rows, cols, tokens_t, branch_t, rights, attended, du_own, du_in):
+        if turn >= 1 and small_steps:
+            small_steps.pop(0)()
+    for step in small_steps:
+        step()
+    for name, copy in copies.items():
+        if name[0] != "core" or name[2] >= 2:
+            copy.wait_send()
+
+
+def late_sums(rows, cols, tokens_t, branch_t, rights, attended, du_own, du_in, small):
     share, n = tokens_t.shape[2:]
     width = attended[0].shape[1]
     wide = du_own.shape[2]
@@ -439,9 +495,12 @@
     def pair_of(*shape):
         return pltpu.SemaphoreType.DMA((2,) + shape)
 
-    operands = (tokens_t, branch_t, *rights, *attended, du_own, du_in)
+    length = small.shape[2]
+    small, small_scratch = small_blocks(rows, cols, small)
+    operands = (tokens_t, branch_t, *rights, *attended, du_own, du_in, small)
     scratch = [
-        vmem(BF16, cols, 4, half, width), vmem(BF16, cols, 4, half, width),
+        vmem(BF16, cols, 4, n, width), pltpu.SemaphoreType.DMA((cols, 4)),
+        vmem(BF16, cols, 2, half, width), vmem(BF16, cols, 4, half, width),
         vmem(BF16, cols, 4, quarter, width), vmem(BF16, cols, 4, quarter, width),
         vmem(F32, cols, 4, quarter, width),
         vmem(BF16, cols - 1, 4, quarter, width), vmem(BF16, cols - 1, 4, quarter, width),
@@ -453,73 +512,20 @@
         pair_of(cols, 4), pair_of(cols, 4), pair_of(cols - 1, 4), pair_of(levels, 4),
         pair_of(levels, 2),
     ]
-    return call(
+    def whole(*shape):
+        return pl.BlockSpec(shape, lambda *_: (0,) * len(shape))
+
+    late, wide_sum, small_sum = call(
         functools.partial(late_kernel, rows, cols), "late_sums", (1,),
-        [held(o.shape) for o in operands],
+        [held(tokens_t.shape), held(branch_t.shape)] + [ANYWHERE] * (2 * cols)
+        + [held(du_own.shape), held(du_in.shape), held(small.shape)],
+        [whole(4, share, width), whole(2, share, wide), whole(*small.shape[3:])],
         [
-            pl.BlockSpec((4, share, width), lambda *_: (0, 0, 0)),
-            pl.BlockSpec((2, share, wide), lambda *_: (0, 0, 0)),
+            shaped(F32, 4, share, width), shaped(F32, 2, share, wide), shaped(F32, *small.shape[3:])
         ],
-        [shaped(F32, 4, share, width), shaped(F32, 2, share, wide)],
-        operands, 100_000_000_000, remote=5, scratch=scratch,
-    )
-
-
-def small_kernel(rows, cols, parts, out, *refs):
-    bits = [1 << b for b in range(rows.bit_length() - 1)]
-    sent, arrived = refs[:2]
-    core_in, cols_in, totals, row_ins = refs[2], refs[3], refs[4 : 4 + len(bits)], refs[4 + len(bits) :]
-    r, c = lax.axis_index("rows"), lax.axis_index("cols")
-    others = [{"cols": (c + cols - k) % cols} for k in range(1, cols)]
-    greet([{"rows": across(r, bit)} for bit in bits] + others)
-    core = side_at(r, 1)
-    copy = send(parts.at[:, 1 - core], core_in, sent.at[0], arrived.at[0], {"rows": across(r, 1)})
-    copy.wait()
-    sums = parts[:, core] + core_in[...]
-    cols_out = totals[0]
-    cols_out[...] = sums
-    copies = [
-        send(cols_out.at[:, k], cols_in.at[k - 1], sent.at[k], arrived.at[k], others[k - 1])
-        for k in range(1, cols)
-    ]
-    total = sums[:, 0]
-    for k, copy in enumerate(copies):
-        copy.wait()
-        total = total + cols_in[k]
-    for level, bit in enumerate(bits[1:]):
-        held_total, arriving = totals[1 + level], row_ins[level]
-        held_total[...] = total.reshape(held_total.shape)
-        side = side_at(r, bit)
-        copy = send(
-            held_total.at[:, 1 - side], arriving, sent.at[cols + level], arrived.at[cols + level],
-            {"rows": across(r, bit)},
-        )
-        copy.wait()
-        total = held_total[:, side] + arriving[...]
-    out[...] = total[0]
-
-
-def small_sum(rows, cols, parts):
-    length = parts.shape[2]
-    width = -(-length // 1024) * 128
-    parts = jnp.pad(parts, ((0, 0), (0, 0), (0, 8 * width - length)))
-    parts = parts.reshape(rows // 2, 2, cols, 8, width)
-    levels = rows.bit_length() - 1
-    sizes = [rows >> (level + 1) for level in range(1, levels)]
-    scratch = [
-        pltpu.SemaphoreType.DMA((cols + levels,)), pltpu.SemaphoreType.DMA((cols + levels,)),
-        pltpu.VMEM((rows // 2, cols, 8, width), F32),
-        pltpu.VMEM((cols - 1, rows // 2, 8, width), F32),
-        pltpu.VMEM((rows // 2, cols, 8, width), F32),
-    ]
-    scratch += [pltpu.VMEM((size, 2, 8, width), F32) for size in sizes]
-    scratch += [pltpu.VMEM((size, 8, width), F32) for size in sizes]
-    total = call(
-        functools.partial(small_kernel, rows, cols), "small_sum", (1,), [held(parts.shape)],
-        [pl.BlockSpec((8, width), lambda *_: (0, 0))], [shaped(F32, 8, width)], (parts,), 0,
-        remote=4, scratch=scratch,
-    )[0]
-    return total.reshape(-1)[:length]
+        operands, 100_000_000_000, remote=5, scratch=scratch + small_scratch,
+    )
+    return late, wide_sum, small_sum.reshape(-1)[:length]
 
 
 def swap_halves(block):
@@ -549,20 +555,75 @@
 def project_qkv(x, weight, bias, cosine, sine, after=()):
     n, D = x.shape
     width = weight.shape[2]
-    step = row_step(n)
-    return call(
-        qkv_kernel, "project_qkv", (3, n // step),
+    return call(
+        qkv_kernel, "project_qkv", (3,),
         [
-            pl.BlockSpec((step, D), lambda j, i: (i, 0)),
-            pl.BlockSpec((1, D, width), lambda j, i: (j, 0, 0)),
-            held(bias.shape),
-            pl.BlockSpec((step, 128), lambda j, i: (i, 0)),
-            pl.BlockSpec((step, 128), lambda j, i: (i, 0)),
+            held((n, D)), pl.BlockSpec((1, D, width), lambda j: (j, 0, 0)), held(bias.shape),
+            held((n, 128)), held((n, 128)),
         ],
-        [pl.BlockSpec((1, step, width), lambda j, i: (j, i, 0))],
+        [pl.BlockSpec((1, n, width), lambda j: (j, 0, 0))],
         [shaped(BF16, 3, n, width)],
         (x, weight, bias, cosine, sine), 6 * n * D * width, after=after,
     )[0]
+
+
+def prepare_kernel(
+    q_rows, sizes_ref, picks_ref, docs_ref, cos_ref, sin_ref, ext_k_ref, ext_q_ref, out_ref
+):
+    n = cos_ref.shape[0]
+    size = math.gcd(256, math.gcd(q_rows, n))
+    lane = lax.broadcasted_iota(jnp.int32, (size, 128), 1)
+    frequency = jnp.exp((lane & (DH // 2 - 1)).astype(F32) * (-2.0 * math.log(10000.0) / DH))
+    place_lane = lane & (DH - 1)
+    for first in range(0, n, size):
+        at = slice(first, first + size)
+        row = lax.broadcasted_iota(jnp.int32, (size, 128), 0) + first
+        if first < q_rows:
+            position, segment = row & (QLEN - 1), (row // QLEN) & (SEGMENTS - 1)
+        else:
+            place = row - q_rows
+            begin, segment, end = jnp.zeros_like(row), jnp.zeros_like(row), 0
+            for doc in range(sizes_ref.shape[0]):
+                end = end + sizes_ref[doc]
+                passed = place >= end
+                begin = jnp.where(passed, end, begin)
+                segment = segment + passed.astype(jnp.int32)
+            position = place - begin
+        angles = position.astype(F32) * frequency
+        sine = jnp.sin(angles)
+        cos_ref[at, :] = jnp.cos(angles)
+        sin_ref[at, :] = jnp.where((lane & (DH // 2)) == 0, -sine, sine)
+        same = segment == place_lane
+        ones = (place_lane >= SEGMENTS) & (place_lane < SEGMENTS + 3)
+        ext_k_ref[at, :] = (same | ones).astype(F32).astype(BF16)
+        apart = (place_lane < SEGMENTS) & jnp.logical_not(same)
+        ext_q_ref[at, :] = jnp.where(apart, -1e30, 0.0).astype(BF16)
+    queries = picks_ref.shape[0]
+    begins, sizes = docs_ref[:, 0:1], docs_ref[:, 1:2]
+    groups, docs = out_ref.shape[:2]
+    for first in range(0, queries, 4):
+        lanes = jnp.concatenate([picks_ref[first + j] for j in range(4)], axis=1)
+        rows = begins + lax.rem(lanes, jnp.broadcast_to(sizes, lanes.shape))
+        at = slice(first * QLEN, (first + 4) * QLEN)
+        for group in range(groups):
+            out_ref[group, :, at] = rows[group * docs : (group + 1) * docs]
+
+
+def prepare(n, q_rows, own_sizes, match_picks, begins, sizes):
+    groups, docs = sizes.shape
+    width = match_picks.shape[0] * QLEN
+    table = jnp.stack([begins.reshape(-1), sizes.reshape(-1)], axis=1)
+    return call(
+        functools.partial(prepare_kernel, q_rows), "prepare", (1,),
+        [held(match_picks.shape), held(table.shape)],
+        [pl.BlockSpec((n, 128), lambda *_: (0, 0))] * 4
+        + [pl.BlockSpec((groups, docs, width), lambda *_: (0, 0, 0))],
+        [
+            shaped(F32, n, 128), shaped(F32, n, 128), shaped(BF16, n, 128), shaped(BF16, n, 128),
+            shaped(jnp.int32, groups, docs, width),
+        ],
+        (own_sizes, match_picks, table), 0, prefetch=1,
+    )
 
 
 def normed_rows(residual):
@@ -878,6 +939,27 @@
             body(place)
 
 
+def join_kernel(slots, place_ref, *refs):
+    out_ref, turned_ref = refs[-2:]
+    width = refs[0].shape[1]
+    for k in range(slots):
+        at = pl.ds(pl.multiple_of((place_ref[0] + slots - k) % slots * width, width), width)
+        out_ref[:, at] = refs[k][...]
+        turned_ref[at, :] = refs[k][...].astype(F32).T.astype(BF16)
+
+
+def join(c, slots):
+    n, width = slots[0].shape
+    D = width * len(slots)
+    step = row_step(n)
+    return call(
+        functools.partial(join_kernel, len(slots)), "join", (n // step,),
+        [row_spec(step, width)] * len(slots),
+        [row_spec(step, D), pl.BlockSpec((D, step), lambda i, *_: (0, i))],
+        [shaped(BF16, n, D), shaped(BF16, D, n)], (c.reshape(1), *slots), 0, prefetch=1,
+    )
+
+
 def assemble_kernel(place_ref, *refs):
     out_ref = refs[-1]
     slot = place_ref[1 + pl.program_id(0)]
@@ -891,7 +973,7 @@
 def assemble(c, q_rows, slots):
     n, width = slots[0].shape
     count = len(slots)
-    step = math.gcd(256, q_rows)
+    step = math.gcd(512, math.gcd(q_rows, n))
     q_steps, d_steps = q_rows // step, (n - q_rows) // step
     turns, owners = [], []
     for base, steps in ((0, q_steps), (q_steps, d_steps)):
@@ -1310,19 +1392,6 @@
             pltpu.VMEM((doc_tile.shape[0] // groups, width), BF16),
             pltpu.VMEM((groups, docs, width), F32),
         ],
-    )
-
-
-def rotary_tables(position):
-    half_size = DH // 2
-    frequency = jnp.exp(
-        jnp.arange(half_size, dtype=F32) * (-2.0 * math.log(10000.0) / DH)
-    )
-    angles = position.astype(F32)[:, None] * frequency[None, :]
-    cosine, sine = jnp.cos(angles), jnp.sin(angles)
-    return (
-        jnp.concatenate([cosine] * 4, axis=1),
-        jnp.concatenate([-sine, sine, -sine, sine], axis=1),
     )
 
 
@@ -1388,24 +1457,27 @@
         lax.dynamic_index_in_dim(w.reshape(R, -1, w.shape[1]), r, 0, keepdims=False)
         for w in late_weights
     ]
+    parts = jnp.concatenate(
+        [tokens[:ROW_LEN].reshape(C, Q, width), tokens[ROW_LEN:].reshape(C, DS, width)], axis=1
+    )
+
+    def part(k):
+        return lax.dynamic_index_in_dim(parts, (c + k) % C, 0, keepdims=False)
+
+    token_slots = [part(0)] + [shift_cols(part(k), k) for k in range(1, C)]
+    own_sizes = lax.dynamic_index_in_dim(
+        lax.dynamic_index_in_dim(doc_lengths, r, 0, keepdims=False), c, 0, keepdims=False
+    )
+    sizes = lax.dynamic_index_in_dim(doc_lengths, c, 1, keepdims=False)
+    doc_ends = jnp.cumsum(sizes, axis=1)
+    begins = doc_ends - sizes
+    cosine, sine, ext_k, ext_q, picks = prepare(n, Q, own_sizes, match_picks, begins, sizes)
     if C == 2:
-        x, qkv_other, proj_other, pack_other = start_up(
-            R, (Q, DS, ROW_LEN), tokens, w_qkv, w_proj, packed.reshape(8, -1)
-        )
+        qkv_other, proj_other, pack_other = gather_weights(R, w_qkv, w_proj, packed.reshape(8, -1))
         wqkv_slots = [w_qkv, qkv_other]
         wproj = jnp.concatenate(in_order([w_proj, proj_other]), axis=0)
         packs = [packed, pack_other.reshape(-1)]
     else:
-        parts = jnp.concatenate(
-            [tokens[:ROW_LEN].reshape(C, Q, width), tokens[ROW_LEN:].reshape(C, DS, width)], axis=1
-        )
-
-        def part(k):
-            return lax.dynamic_index_in_dim(parts, (c + k) % C, 0, keepdims=False)
-
-        x = jnp.concatenate(
-            in_order([part(0)] + [shift_cols(part(k), k) for k in range(1, C)]), axis=1
-        )
 
         def gather_slots(shard):
             flat = shard.reshape(-1, shard.shape[-1])
@@ -1420,6 +1492,7 @@
             in_order([w_proj] + [shift_cols(w_proj, k) for k in range(1, C)]), axis=0
         )
         packs = [packed] + [shift_cols(packed, k) for k in range(1, C)]
+    x, x_t = join(c, token_slots)
 
     ordered_packs = in_order(packs)
 
@@ -1435,22 +1508,8 @@
     zero_row = jnp.zeros_like(bout)
     vectors = jnp.stack([bout, gain1, bias1, bdown, gain2, bias2, zero_row, zero_row])
 
-    own_sizes = lax.dynamic_index_in_dim(
-        lax.dynamic_index_in_dim(doc_lengths, r, 0, keepdims=False), c, 0, keepdims=False
-    )
     own_ends = jnp.cumsum(own_sizes)
-    places = jnp.arange(DS, dtype=jnp.int32)
-    passed = places[:, None] >= own_ends[None, :]
-    slot_id = jnp.sum(passed.astype(jnp.int32), axis=1)
-    slot_begin = jnp.sum(jnp.where(passed, own_sizes[None, :], 0), axis=1)
-    query_places = jnp.arange(Q, dtype=jnp.int32)
-    position = jnp.concatenate([query_places % QLEN, places - slot_begin])
-    cosine, sine = rotary_tables(position)
-    segment = jnp.concatenate([(query_places // QLEN) % SEGMENTS, slot_id])
-    lane = jnp.arange(128, dtype=jnp.int32)[None, :] % DH
-    same = segment[:, None] == lane
-    ext_k = (same | ((lane >= SEGMENTS) & (lane < SEGMENTS + 3))).astype(BF16)
-    ext_q = jnp.where((lane < SEGMENTS) & ~same, -1e30, 0.0).astype(BF16)
+    share = D // R
     q_tiles, d_tiles = Q // tile, DS // tile
     steps = jnp.arange(q_tiles, dtype=jnp.int32)
     first_rows = jnp.arange(d_tiles, dtype=jnp.int32) * tile
@@ -1463,13 +1522,6 @@
     ).astype(jnp.int32)
 
     queries_here, tile_docs, _ = match_picks.shape
-    docs = own_sizes.shape[0]
-    sizes = lax.dynamic_index_in_dim(doc_lengths, c, 1, keepdims=False)
-    doc_ends = jnp.cumsum(sizes, axis=1)
-    begins = doc_ends - sizes
-    picks = jnp.transpose(match_picks, (1, 0, 2)).reshape(tile_docs, queries_here * QLEN)
-    picks = begins.reshape(-1)[:, None] + picks % sizes.reshape(-1)[:, None]
-    picks = picks.reshape(R, docs, queries_here * QLEN)
     strip_rows = (jnp.arange(DS // STRIP, dtype=jnp.int32) * STRIP)[None, :, None]
     lows = jnp.sum(doc_ends[:, None, :] <= strip_rows, axis=2).astype(jnp.int32).reshape(-1)
     highs = jnp.sum(begins[:, None, :] < strip_rows + STRIP, axis=2).astype(jnp.int32) - 1
@@ -1477,7 +1529,7 @@
 
     qkv, attended, rests, exts = [], [], [], []
     for k in range(C):
-        first = (picks, lows, highs) if k == 0 else ()
+        first = (lows, highs) if k == 0 else ()
         qkv.append(project_qkv(x, wqkv_slots[k], bqkv_slots[k], cosine, sine, first))
         if k == 0:
             flat = jnp.concatenate([piece.reshape(-1, D) for piece in late_pieces])
@@ -1635,17 +1687,17 @@
 
     for k in slots_back[:-1]:
         pull_attention(k)
-    wide_state = next_fold([cols_state(down_kept), cols_state(up_kept)], x_bit, share)
+    wide_state = next_fold([cols_state(down_kept), cols_state(up_kept)], z_bits[0], 2 * share)
     pull_attention(0)
     sent = [
         shift_cols(token_pull((c + k) % C, resid_one_grad, mixed_grads, wqkv_slots, BF16), k)
         for k in range(1, C)
     ]
     own_tokens = token_pull(c, resid_one_grad, mixed_grads, wqkv_slots, F32)
-    late_grad, wide_grad = late_sums(
-        R, C, halves_of(x.T), halves_of(branch_one_t), mixed_grads, attended, *wide_state
-    )
-    small = small_sum(R, C, gather_small())
+    late_grad, wide_grad, small = late_sums(
+        R, C, halves_of(x_t), halves_of(branch_one_t), mixed_grads, attended, *wide_state,
+        gather_small(),
+    )
     tokens_grad = assemble(c, Q, [own_tokens] + sent)
     qkv_grad, out_grad = late_grad[:3], late_grad[3]
     down_grad, up_grad = wide_grad

time: 857 us -> 832 us (0.971)
  other arithmetic: 25.1 us -> 13 us
  Pallas kernels: 684 us -> 672 us
    pallas_call x26 -> x27, Pallas kernels: 684 us -> 672 us  [call(): pl.pallas_call(wrapped, grid_spec=pltpu.PrefetchScalarGridSpec(num_scalar...]
  transfers between devices with their start and end apart: 15 -> 16, of which waited for: 1 -> 2; matrix products, arithmetic and copies ran while one was open for 12% -> 11% of each run, Pallas kernels for 60% -> 65%
where the time goes in v7:
time: 832 us; the launch traced here: 824 us
  Pallas kernels  672 us (81%)
  matrix products  55.3 us (7%)
  local copies, waits for them, and re-layouts  51.1 us (6%)
  between operations  15.5 us (2%)
  other arithmetic  13 us (2%)
  starting transfers between devices  10.4 us (1%)
    pallas_call x27, Pallas kernels, call(): pl.pallas_call(wrapped, grid_spec=pltpu.PrefetchScalarGridSpec(num_scalar...  672 us
    dot_general x9, matrix products, mm(): return lax.dot_general(left, right, dims, preferred_element_type=F32)  55.3 us
  transfers between devices with their start and end apart: 16, of which 2 were waited for; matrix products, arithmetic and copies ran while one was open for 11% of the time, Pallas kernels for 65%

profile of v7, /device:TPU:0, one launch (start us, length us, event | category | flops | bytes accessed | tf_op | source)
XLA Modules:
  0.0 823.8 jit_solution(11223274608450987033)
XLA Ops:
  7.3 1.2 slice-done
  9.2 1.9 fusion.1
  11.2 3.0 collective-permute-start
  16.1 1.0 constant_dynamic-slice_fusion.6
  17.2 2.4 copy.69.refs_1_
  20.3 9.2 %prepare.1 = (f32[1536,128]{1,0:T(8,128)}, f32[1536,128]{1,0:T(8,128)}, bf16[1536,128]{1,0:T(8,128)(2,1)}, bf16[1536,128]{1,0:T(8,128)(2,1)}, s32[16,4,1024]{2,1,0:T(4,128)}) custom-call(s32[4]{0:T(128)} %fusion.4.refs_0_, s32[32,64,32]{2,1,0:T(8,128)} %copy.69.refs_1_, s32[64,2]{1,0:T(8,128)} %copy.70.refs_2_), custom_call_target="tpu_custom_call" | custom-call | bytes 1024 | tf_op jit(solution)/shard_map/prepare/pallas_call | solution.py:60
  29.5 50.2 %gather_weights.1 = (bf16[16,192,512]{2,1,0:T(8,128)(2,1)}, bf16[512,128]{1,0:T(8,128)(2,1)}, f32[8,832]{1,0:T(8,128)}) custom-call(bf16[16,192,512]{2,1,0:T(8,128)(2,1)} %bitcast.136, bf16[512,128]{1,0:T(8,128)(2,1)} %refs_1_.5, f32[8,832]{1,0:T(8,128)} %reshape.248.refs_2_, s32[16,4,1024]{2,1,0:T(4,128)} %get-tuple-element.73.refs_3_.refs_4_), custom_call_target="tpu_custom_call" | custom-call | bytes 1024 | tf_op jit(solution)/shard_map/gather_weights/pallas_call | solution.py:60
  80.7 1.0 dynamic-slice_bitcast_fusion.1
  81.7 1.1 copy-done.7
  82.9 15.6 %join.1 = (bf16[1536,1024]{1,0:T(8,128)(2,1)}, bf16[1024,1536]{1,0:T(8,128)(2,1)}) custom-call(s32[1]{0:T(128)} %bitcast.3.refs_0_, bf16[1536,512]{1,0:T(8,128)(2,1)} %get-tuple-element.222.refs_1_, bf16[1536,512]{1,0:T(8,128)(2,1)} %copy-done.7, f32[8,832]{1,0:T(8,128)} %get-tuple-element.74.refs_3_), custom_call_target="tpu_custom_call" | custom-call | bytes 1024 | tf_op jit(solution)/shard_map/join/pallas_call | solution.py:60
  98.5 1.5 collective-permute-start.1
  101.4 9.8 %project_qkv.2.refs_1_ = bf16[3,1536,512]{2,1,0:T(8,128)(2,1)} custom-call(bf16[1536,1024]{1,0:T(8,128)(2,1)} %get-tuple-element.75.refs_0_.refs_7_, bf16[3,1024,512]{2,1,0:T(8,128)(2,1)} %refs_4_.5, f32[3,512]{1,0:T(4,128)} %refs_2_.1, f32[1536,128]{1,0:T(8,128)} %get-tuple-element.76.refs_3_.refs_7_, f32[1536,128]{1,0:T(8,128)} %get-tuple-element.77.refs_4_.refs_8_, ...), custom_call_target="tpu_custom_call" | custom-call | flops 4831838208 | bytes 12589056 | tf_op jit(solution)/shard_map/project_qkv/pallas_call | solution.py:60
  111.2 2.9 collective-permute-done.1.refs_0_
  114.9 1.9 pass_on.1.refs_4_
  116.9 1.5 slice.266
  118.4 1.8 fusion.13
  126.4 32.8 %attention_forward.2 = (bf16[1536,512]{1,0:T(8,128)(2,1)}, bf16[1536,512]{1,0:T(8,128)(2,1)}, bf16[1536,512]{1,0:T(8,128)(2,1)}) custom-call(s32[12]{0:T(128)} %pad_add_fusion.1.refs_0_, bf16[3,1536,512]{2,1,0:T(8,128)(2,1)} %project_qkv.2.refs_1_, bf16[1536,128]{1,0:T(8,128)(2,1)} %get-tuple-element.78.refs_2_.refs_6_, ...), custom_call_target="tpu_custom_call" | custom-call | bytes 1024 | tf_op jit(solution)/shard_map/attention_forward/pallas_call | solution.py:60
  159.3 9.8 %project_qkv.3.refs_1_.refs_4_ = bf16[3,1536,512]{2,1,0:T(8,128)(2,1)} custom-call(bf16[1536,1024]{1,0:T(8,128)(2,1)} %get-tuple-element.75.refs_0_.refs_7_, bf16[3,1024,512]{2,1,0:T(8,128)(2,1)} %bitcast.139, f32[3,512]{1,0:T(4,128)} %slice.265.refs_2_, f32[1536,128]{1,0:T(8,128)} %get-tuple-element.76.refs_3_.refs_7_, ...), custom_call_target="tpu_custom_call" | custom-call | flops 4831838208 | bytes 12589056 | tf_op jit(solution)/shard_map/project_qkv/pallas_call | solution.py:60
  169.0 33.0 %attention_forward.3 = (bf16[1536,512]{1,0:T(8,128)(2,1)}, bf16[1536,512]{1,0:T(8,128)(2,1)}, bf16[1536,512]{1,0:T(8,128)(2,1)}) custom-call(s32[12]{0:T(128)} %pad_add_fusion.1.refs_0_, bf16[3,1536,512]{2,1,0:T(8,128)(2,1)} %project_qkv.3.refs_1_.refs_4_, bf16[1536,128]{1,0:T(8,128)(2,1)} %get-tuple-element.78.refs_2_.refs_6_, ...), custom_call_target="tpu_custom_call" | custom-call | bytes 1024 | tf_op jit(solution)/shard_map/attention_forward/pallas_call | solution.py:60
  202.1 11.3 %out_and_norm.1 = (f32[1536,1024]{1,0:T(8,128)}, f32[1536,1]{1,0:T(8,128)}, bf16[1536,1024]{1,0:T(8,128)(2,1)}, bf16[1024,1536]{1,0:T(8,128)(2,1)}) custom-call(bf16[1536,1024]{1,0:T(8,128)(2,1)} %get-tuple-element.75.refs_0_.refs_7_, f32[8,1024]{1,0:T(8,128)} %stack.67.refs_1_.refs_6_.refs_3_, ...), custom_call_target="tpu_custom_call" | custom-call | flops 3221225472 | bytes 21010432 | tf_op jit(solution)/shard_map/out_and_norm/pallas_call | solution.py:60
  213.4 23.2 %up_and_gelu.2 = (bf16[1536,2048]{1,0:T(8,128)(2,1)}, f32[1536,2048]{1,0:T(8,128)}) custom-call(bf16[1536,1024]{1,0:T(8,128)(2,1)} %get-tuple-element.86.refs_0_, bf16[1024,2048]{1,0:T(8,128)(2,1)} %refs_6_.1, f32[1,2048]{1,0:T(1,128)} %bitcast.182, f32[1536,1]{1,0:T(8,128)} %get-tuple-element.87.refs_3_.refs_2_), custom_call_target="tpu_custom_call" | custom-call | flops 16106127360 | bytes 26222592 | tf_op jit(solution)/shard_map/up_and_gelu/pallas_call | solution.py:60
  236.6 22.6 %up_and_gelu.3 = (bf16[1536,2048]{1,0:T(8,128)(2,1)}, f32[1536,2048]{1,0:T(8,128)}) custom-call(bf16[1536,1024]{1,0:T(8,128)(2,1)} %get-tuple-element.86.refs_0_, bf16[1024,2048]{1,0:T(8,128)(2,1)} %all-gather.6.cloned.1.call-done.refs_1_.refs_7_, f32[1,2048]{1,0:T(1,128)} %bitcast.183, bf16[1536,2048]{1,0:T(8,128)(2,1)} %get-tuple-element.88.refs_3_), custom_call_target="tpu_custom_call" | custom-call | flops 16106127360 | bytes 26222592 | tf_op jit(solution)/shard_map/up_and_gelu/pallas_call | solution.py:60
  259.2 24.8 %down_and_norm.1 = (f32[1536,1024]{1,0:T(8,128)}, f32[1536,1]{1,0:T(8,128)}, bf16[1536,1024]{1,0:T(8,128)(2,1)}, f32[1536,128]{1,0:T(8,128)}, bf16[1536,128]{1,0:T(8,128)(2,1)}, /*index=5*/f32[1536,1]{1,0:T(8,128)}) custom-call(f32[1536,1024]{1,0:T(8,128)} %get-tuple-element.84.refs_0_.refs_1_, f32[8,1024]{1,0:T(8,128)} %stack.67.refs_1_.refs_6_.refs_3_, ...), custom_call_target="tpu_custom_call" | custom-call | flops 12884901888 | bytes 38187008 | tf_op jit(solution)/shard_map/down_and_norm/pallas_call | solution.py:60
  283.9 0.9 slice.222
  284.9 1.1 collective-permute-start.2
  286.0 1.7 slice.221.refs_0_
  287.6 32.4 %gather_rows.1.refs_5_ = bf16[16,1024,128]{2,1,0:T(8,128)(2,1)} custom-call(bf16[1024,128]{1,0:T(8,128)(2,1)} %slice.221.refs_0_, f32[1536,1]{1,0:T(8,128)} %get-tuple-element.91.refs_1_.refs_5_), custom_call_target="tpu_custom_call" | custom-call | bytes 1024 | tf_op jit(solution)/shard_map/gather_rows/pallas_call | solution.py:60
  320.1 0.9 broadcast_select_fusion.1
  321.8 34.3 %score_forward.1.refs_6_ = f32[64,32]{1,0:T(8,128)} custom-call(s32[512]{0:T(512)} %reshape.242.refs_5_.refs_0_, s32[512]{0:T(512)} %sub.97.refs_6_.refs_1_, bf16[16384,128]{1,0:T(8,128)(2,1)} %bitcast.150, bf16[1024,128]{1,0:T(8,128)(2,1)} %pad_maximum_fusion.3.refs_3_, s32[16,4,1024]{2,1,0:T(4,128)} %get-tuple-element.73.refs_3_.refs_4_, ...), custom_call_target="tpu_custom_call" | custom-call | flops 4294967296 | bytes 4730880 | tf_op jit(solution)/shard_map/score_forward/pallas_call | solution.py:60
  358.3 3.0 collective-permute-done.3
  361.9 1.4 subtract_multiply_fusion.refs_5_
  363.3 34.7 %score_backward.1 = (f32[16384,128]{1,0:T(8,128)}, f32[128,1024]{1,0:T(8,128)}) custom-call(s32[512]{0:T(512)} %reshape.242.refs_5_.refs_0_, s32[512]{0:T(512)} %sub.97.refs_6_.refs_1_, bf16[16384,128]{1,0:T(8,128)(2,1)} %bitcast.151, bf16[1024,128]{1,0:T(8,128)(2,1)} %pad_maximum_fusion.3.refs_3_, s32[16,4,1024]{2,1,0:T(4,128)} %get-tuple-element.73.refs_3_.refs_4_, ...), custom_call_target="tpu_custom_call" | custom-call | flops 8589934592 | bytes 13643776 | tf_op jit(solution)/shard_map/score_backward/pallas_call | solution.py:60
  398.0 2.0 copy.74
  400.0 1.0 dynamic-slice_bitcast_fusion
  401.6 1.9 constant_dynamic-slice_fusion.2
  403.5 37.3 %scatter_rows.1.refs_7_ = f32[1024,128]{1,0:T(8,128)} custom-call(f32[16,1024,128]{2,1,0:T(8,128)} %bitcast.142, f32[128,1024]{1,0:T(8,128)} %get-tuple-element.92.refs_1_), custom_call_target="tpu_custom_call" | custom-call | bytes 1024 | tf_op jit(solution)/shard_map/scatter_rows/pallas_call | solution.py:60
  440.9 2.0 pad_maximum_fusion.refs_0_
  442.9 12.3 %head_pull.1 = (bf16[1536,128]{1,0:T(8,128)(2,1)}, f32[1536,1024]{1,0:T(8,128)}, bf16[1536,1024]{1,0:T(8,128)(2,1)}, bf16[1024,1536]{1,0:T(8,128)(2,1)}, f32[8,1024]{1,0:T(8,128)}) custom-call(f32[1536,128]{1,0:T(8,128)} %pad_maximum_fusion.refs_0_, f32[1536,128]{1,0:T(8,128)} %get-tuple-element.94.refs_1_, f32[1536,1]{1,0:T(8,128)} %get-tuple-element.95.refs_2_, ...), custom_call_target="tpu_custom_call" | custom-call | flops 805306368 | bytes 21180416 | tf_op jit(solution)/shard_map/head_pull/pallas_call | solution.py:60
  455.2 3.5 constant_dynamic-slice_fusion.4
  458.6 6.5 convolution_convert_fusion.3.refs_4_
  465.4 3.6 convolution_convert_fusion.2.refs_5_
  470.4 13.6 %up_pull.2 = (bf16[1536,2048]{1,0:T(8,128)(2,1)}, f32[8,2048]{1,0:T(8,128)}) custom-call(bf16[1536,1024]{1,0:T(8,128)(2,1)} %get-tuple-element.98.refs_0_, bf16[2048,1024]{1,0:T(8,128)(2,1)} %all-gather.8.cloned.1.call-done.refs_6_.refs_1_, f32[1536,2048]{1,0:T(8,128)} %get-tuple-element.100.refs_2_, f32[8,1024]{1,0:T(8,128)} %get-tuple-element.101.refs_3_, ...), custom_call_target="tpu_custom_call" | custom-call | flops 6442450944 | bytes 26279936 | tf_op jit(solution)/shard_map/up_pull/pallas_call | solution.py:60
  483.9 6.8 convolution_convert_fusion.1.refs_11_
  491.2 8.0 add_convert_fusion.1.refs_4_
  499.2 1.0 collective-permute-start.9
  500.2 14.1 %up_pull.3 = (bf16[1536,2048]{1,0:T(8,128)(2,1)}, f32[8,2048]{1,0:T(8,128)}) custom-call(bf16[1536,1024]{1,0:T(8,128)(2,1)} %get-tuple-element.98.refs_0_, bf16[2048,1024]{1,0:T(8,128)(2,1)} %refs_1_.8, f32[1536,2048]{1,0:T(8,128)} %get-tuple-element.99.refs_2_, f32[8,2048]{1,0:T(8,128)} %get-tuple-element.103.refs_3_, ...), custom_call_target="tpu_custom_call" | custom-call | flops 6442450944 | bytes 26279936 | tf_op jit(solution)/shard_map/up_pull/pallas_call | solution.py:60
  514.3 8.2 convolution_convert_fusion.refs_12_
  522.7 5.9 add_convert_fusion.refs_14_
  528.6 1.0 collective-permute-start.10
  532.4 9.5 %convert_add_fusion.1.refs_13_ = f32[512,2048]{1,0:T(8,128)} fusion(bf16[512,2048]{1,0:T(8,128)(2,1)} %collective-permute-done.6, bf16[512,1536]{1,0:T(8,128)(2,1)} %bitcast.160, bf16[1536,2048]{1,0:T(8,128)(2,1)} %get-tuple-element.88.refs_3_), kind=kOutput, calls=%fused_computation.2 | convolution fusion | flops 3223322624 | bytes 14155776 | tf_op jit(solution)/shard_map/dot_general | solution.py:23
  541.8 29.7 %hidden_pull.1 = (f32[1536,1024]{1,0:T(8,128)}, bf16[1024,1536]{1,0:T(8,128)(2,1)}, f32[8,1024]{1,0:T(8,128)}, bf16[1536,512]{1,0:T(8,128)(2,1)}, bf16[1536,512]{1,0:T(8,128)(2,1)}) custom-call(f32[1536,1024]{1,0:T(8,128)} %get-tuple-element.97.refs_0_, f32[1536,1024]{1,0:T(8,128)} %get-tuple-element.84.refs_0_.refs_1_, ...), custom_call_target="tpu_custom_call" | custom-call | bytes 1024 | tf_op jit(solution)/shard_map/hidden_pull/pallas_call | solution.py:60
  571.6 6.2 convert_add_fusion.refs_10_
  577.8 46.5 %attention_backward.2 = (bf16[3,1536,512]{2,1,0:T(8,128)(2,1)}, f32[8,512]{1,0:T(8,128)}) custom-call(s32[12]{0:T(128)} %pad_add_fusion.1.refs_0_, bf16[3,1536,512]{2,1,0:T(8,128)(2,1)} %project_qkv.3.refs_1_.refs_4_, bf16[1536,512]{1,0:T(8,128)(2,1)} %get-tuple-element.112.refs_2_, bf16[1536,512]{1,0:T(8,128)(2,1)} %get-tuple-element.83.refs_3_.refs_6_.refs_5_, ...), custom_call_target="tpu_custom_call" | custom-call | bytes 1024 | tf_op jit(solution)/shard_map/attention_backward/pallas_call | solution.py:60
  624.3 8.9 %fold.1 = (bf16[2,256,2048]{2,1,0:T(8,128)(2,1)}, f32[2,256,2048]{2,1,0:T(8,128)}) custom-call(s32[1]{0:T(128)} %bitcast.44.refs_0_, f32[1,512,2048]{2,1,0:T(8,128)} %bitcast.137, f32[1,512,2048]{2,1,0:T(8,128)} %bitcast.138, bf16[1,512,2048]{2,1,0:T(8,128)(2,1)} %bitcast.47.refs_3_, bf16[1,512,2048]{2,1,0:T(8,128)(2,1)} %bitcast.48.refs_4_, ...), custom_call_target="tpu_custom_call" | custom-call | bytes 1024 | tf_op jit(solution)/shard_map/fold/pallas_call | solution.py:60
  634.2 0.9 slice_reduce_fusion
  637.3 46.8 %attention_backward.3 = (bf16[3,1536,512]{2,1,0:T(8,128)(2,1)}, f32[8,512]{1,0:T(8,128)}) custom-call(s32[12]{0:T(128)} %pad_add_fusion.1.refs_0_, bf16[3,1536,512]{2,1,0:T(8,128)(2,1)} %project_qkv.2.refs_1_, bf16[1536,512]{1,0:T(8,128)(2,1)} %get-tuple-element.109.refs_2_, bf16[1536,512]{1,0:T(8,128)(2,1)} %get-tuple-element.81.refs_5_.refs_2_.refs_3_.refs_4_, ...), custom_call_target="tpu_custom_call" | custom-call | bytes 1024 | tf_op jit(solution)/shard_map/attention_backward/pallas_call | solution.py:60
  684.1 10.9 %token_pull.2.refs_6_ = bf16[1536,512]{1,0:T(8,128)(2,1)} custom-call(s32[1]{0:T(128)} %bitcast.49.refs_0_, f32[1536,1024]{1,0:T(8,128)} %get-tuple-element.108.refs_1_, bf16[3,1536,512]{2,1,0:T(8,128)(2,1)} %get-tuple-element.118.refs_2_, bf16[3,1536,512]{2,1,0:T(8,128)(2,1)} %get-tuple-element.119.refs_3_, bf16[3,1024,512]{2,1,0:T(8,128)(2,1)} %refs_4_.5, ...), custom_call_target="tpu_custom_call" | custom-call | bytes 1024 | tf_op jit(solution)/shard_map/token_pull/pallas_call | solution.py:60
  695.0 11.6 %token_pull.3.refs_9_.refs_1_ = f32[1536,512]{1,0:T(8,128)} custom-call(s32[1]{0:T(128)} %bitcast.3.refs_0_, f32[1536,1024]{1,0:T(8,128)} %get-tuple-element.108.refs_1_, bf16[3,1536,512]{2,1,0:T(8,128)(2,1)} %get-tuple-element.118.refs_2_, bf16[3,1536,512]{2,1,0:T(8,128)(2,1)} %get-tuple-element.119.refs_3_, bf16[3,1024,512]{2,1,0:T(8,128)(2,1)} %refs_4_.5, ...), custom_call_target="tpu_custom_call" | custom-call | bytes 1024 | tf_op jit(solution)/shard_map/token_pull/pallas_call | solution.py:60
  711.0 1.4 reshape.274.refs_8_
  712.4 86.5 %late_sums.1 = (f32[4,64,512]{2,1,0:T(8,128)}, f32[2,64,2048]{2,1,0:T(8,128)}, f32[8,640]{1,0:T(8,128)}) custom-call(bf16[8,2,64,1536]{3,2,1,0:T(8,128)(2,1)} %bitcast.192, bf16[8,2,64,1536]{3,2,1,0:T(8,128)(2,1)} %bitcast.193, bf16[3,1536,512]{2,1,0:T(8,128)(2,1)} %get-tuple-element.118.refs_2_, bf16[3,1536,512]{2,1,0:T(8,128)(2,1)} %get-tuple-element.119.refs_3_, ...), custom_call_target="tpu_custom_call" | custom-call | flops 99999997952 | bytes 27414528 | tf_op jit(solution)/shard_map/late_sums/pallas_call | solution.py:60
  802.9 1.8 slice.240
  805.2 1.6 slice_bitcast_fusion.2
  806.8 2.3 slice_bitcast_fusion
  809.1 8.0 assemble.1
  (215 shorter events, 33.3 us)
Async XLA Ops:
  7.2 194.9 %all-gather.4.cloned.1.call-start = ((), (), s32[]{:S(2)}) async-start(), calls=%async_computation | async-start | bytes 1114112 | tf_op jit(solution)/shard_map/all_gather | solution.py:1453
  7.3 1.2 slice-start
  7.3 1.9 slice-start.1
  9.2 4.9 copy-start.17
  9.2 5.3 copy-start.18
  9.2 5.4 copy-start.19
  9.2 5.4 copy-start.21
  9.2 5.4 copy-start.22
  9.2 5.4 copy-start.23
  9.2 5.4 copy-start.24
  9.2 5.4 copy-start.25
  9.2 5.5 copy-start.26
  11.2 70.5 %collective-permute-start = (bf16[1536,512]{1,0:T(8,128)(2,1)}, bf16[1536,512]{1,0:T(8,128)(2,1)S(1)}, u32[]{:S(2)}, u32[]{:S(2)}) collective-permute-start(bf16[1536,512]{1,0:T(8,128)(2,1)} %get-tuple-element.221), channel_id=1, source_target_pairs={{0,1},{1,0},{2,3},{3,2},{4,5},{5,4},{6,7},{7,6},{8,9},{9,8},{10,11... | collective-permute-start | bytes 4718600 | tf_op jit(solution)/shard_map/ppermute | solution.py:1431
  81.7 1.1 copy-start.7
  98.5 15.7 %collective-permute-start.1 = (bf16[288,1024]{1,0:T(8,128)(2,1)S(1)}, bf16[288,1024]{1,0:T(8,128)(2,1)S(1)}, u32[]{:S(2)}, u32[]{:S(2)}) collective-permute-start(bf16[288,1024]{1,0:T(8,128)(2,1)S(1)} %pad_maximum_fusion.1), channel_id=1, source_target_pairs={{0,1},{1,0},{2,3},{3,2},{4,5},{5,4},{6,7},{7,6},{8,9},{9,8},{10,11... | collective-permute-start | bytes 1769480 | tf_op jit(solution)/shard_map/ppermute | solution.py:1431
  111.2 10.6 %copy-start.15 = (f32[8,832]{1,0:T(8,128)S(1)}, f32[8,832]{1,0:T(8,128)}, u32[]{:S(2)}) copy-start(f32[8,832]{1,0:T(8,128)} %get-tuple-element.74.refs_3_) | copy-start | bytes 79876
  111.2 11.4 %copy-start.20 = (s32[4]{0:T(128)S(1)}, s32[4]{0:T(128)}, u32[]{:S(2)}) copy-start(s32[4]{0:T(128)} %fusion.4.refs_0_) | copy-start | bytes 52
  111.2 14.5 %copy-start.13 = (bf16[512,128]{1,0:T(8,128)(2,1)S(1)}, bf16[512,128]{1,0:T(8,128)(2,1)}, u32[]{:S(2)}) copy-start(bf16[512,128]{1,0:T(8,128)(2,1)} %refs_1_.5) | copy-start | bytes 393220
  111.2 14.5 %copy-start.16 = (bf16[512,128]{1,0:T(8,128)(2,1)S(1)}, bf16[512,128]{1,0:T(8,128)(2,1)}, u32[]{:S(2)}) copy-start(bf16[512,128]{1,0:T(8,128)(2,1)} %get-tuple-element.85) | copy-start | bytes 393220
  114.1 0.8 copy-start.12
  116.9 9.5 %copy-start.28 = (s32[6]{0:T(128)S(1)}, s32[6]{0:T(128)}, u32[]{:S(2)}) copy-start(s32[6]{0:T(128)} %constant.234) | copy-start | bytes 76
  118.4 118.2 %all-gather.6.cloned.1.call-start = ((), (), s32[]{:S(2)}) async-start(), calls=%async_computation.1 | async-start | bytes 4456448 | tf_op jit(solution)/shard_map/all_gather | solution.py:1453
  121.0 138.1 %all-gather.8.cloned.1.call-start = ((), (), s32[]{:S(2)}) async-start(), calls=%async_computation.2 | async-start | bytes 4456448 | tf_op jit(solution)/shard_map/all_gather | solution.py:1453
  259.2 26.8 %copy-start.27 = (s32[32]{0:T(128)S(1)}, s32[32]{0:T(128)}, u32[]{:S(2)}) copy-start(s32[32]{0:T(128)} %param.22) | copy-start | bytes 388
  284.9 35.2 %collective-permute-start.2 = (bf16[512,128]{1,0:T(8,128)(2,1)S(1)}, bf16[512,128]{1,0:T(8,128)(2,1)S(1)}, u32[]{:S(2)}, u32[]{:S(2)}) collective-permute-start(bf16[512,128]{1,0:T(8,128)(2,1)S(1)} %slice.222), channel_id=1, source_target_pairs={{0,1},{1,0},{2,3},{3,2},{4,5},{5,4},{6,7},{7,6},{8,9},{9,8},{10,11... | collective-permute-start | bytes 393224 | tf_op jit(solution)/shard_map/ppermute | solution.py:1431
  357.7 3.6 collective-permute-start.3
  363.3 38.3 %copy-start.2 = (bf16[1024,1536]{1,0:T(8,128)(2,1)S(1)}, bf16[1024,1536]{1,0:T(8,128)(2,1)}, u32[]{:S(2)}) copy-start(bf16[1024,1536]{1,0:T(8,128)(2,1)} %get-tuple-element.107) | copy-start | bytes 9437188
  401.0 39.9 %collective-permute-start.4 = (f32[512,128]{1,0:T(8,128)S(1)}, f32[512,128]{1,0:T(8,128)S(1)}, u32[]{:S(2)}, u32[]{:S(2)}) collective-permute-start(f32[512,128]{1,0:T(8,128)S(1)} %dynamic-slice_bitcast_fusion), channel_id=1, source_target_pairs={{0,1},{1,0},{2,3},{3,2},{4,5},{5,4},{6,7},{7,6},{8,9},{9,8},{10,11... | collective-permute-start | bytes 786440 | tf_op jit(solution)/shard_map/ppermute | solution.py:1431
  403.5 37.3 %copy-start.6 = (f32[1024,128]{1,0:T(8,128)S(1)}, f32[1024,128]{1,0:T(8,128)}, u32[]{:S(2)}) copy-start(f32[1024,128]{1,0:T(8,128)} %copy.74) | copy-start | bytes 1572868
  455.2 10.2 %slice-start.6 = ((s8[6291456]{0:T(1024)(128)(4,1)}), s8[4194304]{0:T(1024)(128)(4,1)S(1)}, s32[]{:S(2)}) async-start(s8[6291456]{0:T(1024)(128)(4,1)} %bitcast.194), calls=%async_computation.9 | async-start | bytes 8388608
  458.6 6.7 slice-start.7
  465.2 3.8 copy-start.5
  465.2 26.0 %collective-permute-start.5 = (bf16[512,2048]{1,0:T(8,128)(2,1)S(1)}, bf16[512,2048]{1,0:T(8,128)(2,1)}, u32[]{:S(2)}, u32[]{:S(2)}) collective-permute-start(bf16[512,2048]{1,0:T(8,128)(2,1)S(1)} %convolution_convert_fusion.3.refs_4_), channel_id=1, source_target_pairs={{0,2},{2,0},{4,6},{6,4},{8,10},{10,8},{12,14},{14,12},{16,18},{18,... | collective-permute-start | bytes 6291464 | tf_op jit(solution)/shard_map/ppermute | solution.py:1434
  469.0 1.3 copy-start.4
  469.0 63.3 %collective-permute-start.6 = (bf16[512,2048]{1,0:T(8,128)(2,1)S(1)}, bf16[512,2048]{1,0:T(8,128)(2,1)}, u32[]{:S(2)}, u32[]{:S(2)}) collective-permute-start(bf16[512,2048]{1,0:T(8,128)(2,1)S(1)} %convolution_convert_fusion.2.refs_5_), channel_id=1, source_target_pairs={{0,2},{2,0},{4,6},{6,4},{8,10},{10,8},{12,14},{14,12},{16,18},{18,... | collective-permute-start | bytes 6291464 | tf_op jit(solution)/shard_map/ppermute | solution.py:1434
  483.9 7.3 copy-start.10
  490.7 8.4 %copy-start.3 = (bf16[512,2048]{1,0:T(8,128)(2,1)}, bf16[512,2048]{1,0:T(8,128)(2,1)S(1)}, u32[]{:S(2)}) copy-start(bf16[512,2048]{1,0:T(8,128)(2,1)S(1)} %convolution_convert_fusion.1.refs_11_) | copy-start | bytes 6291460
  490.7 31.9 %collective-permute-start.7 = (bf16[512,2048]{1,0:T(8,128)(2,1)S(1)}, bf16[512,2048]{1,0:T(8,128)(2,1)}, u32[]{:S(2)}, u32[]{:S(2)}) collective-permute-start(bf16[512,2048]{1,0:T(8,128)(2,1)S(1)} %convolution_convert_fusion.1.refs_11_), channel_id=1, source_target_pairs={{0,2},{2,0},{4,6},{6,4},{8,10},{10,8},{12,14},{14,12},{16,18},{18,... | collective-permute-start | bytes 6291464 | tf_op jit(solution)/shard_map/ppermute | solution.py:1434
  499.2 125.1 %collective-permute-start.9 = (bf16[512,2048]{1,0:T(8,128)(2,1)}, bf16[512,2048]{1,0:T(8,128)(2,1)}, u32[]{:S(2)}, u32[]{:S(2)}) collective-permute-start(bf16[512,2048]{1,0:T(8,128)(2,1)} %add_convert_fusion.1.refs_4_), channel_id=1, source_target_pairs={{0,1},{1,0},{2,3},{3,2},{4,5},{5,4},{6,7},{7,6},{8,9},{9,8},{10,11... | collective-permute-start | bytes 6291464 | tf_op jit(solution)/shard_map/ppermute | solution.py:1431
  500.2 22.5 %slice-start.2 = ((s8[6291456]{0:T(1024)(128)(4,1)}), s8[2097152]{0:T(1024)(128)(4,1)S(1)}, s32[]{:S(2)}) async-start(s8[6291456]{0:T(1024)(128)(4,1)} %bitcast.145), calls=%async_computation.5 | async-start | bytes 4194304
  514.3 8.4 %slice-start.3 = ((s8[6291456]{0:T(1024)(128)(4,1)}), s8[4194304]{0:T(1024)(128)(4,1)S(1)}, s32[]{:S(2)}) async-start(s8[6291456]{0:T(1024)(128)(4,1)} %bitcast.145), calls=%async_computation.6 | async-start | bytes 8388608
  514.3 8.4 %copy-start.8 = (bf16[8,1,64,1536]{3,2,1,0:T(8,128)(2,1)S(1)}, bf16[8,1,64,1536]{3,2,1,0:T(8,128)(2,1)}, u32[]{:S(2)}) copy-start(bf16[8,1,64,1536]{3,2,1,0:T(8,128)(2,1)} %get-tuple-element.217) | copy-start | bytes 4718596
  522.5 49.0 %collective-permute-start.8 = (bf16[512,2048]{1,0:T(8,128)(2,1)}, bf16[512,2048]{1,0:T(8,128)(2,1)}, u32[]{:S(2)}, u32[]{:S(2)}) collective-permute-start(bf16[512,2048]{1,0:T(8,128)(2,1)} %convolution_convert_fusion.refs_12_), channel_id=1, source_target_pairs={{0,2},{2,0},{4,6},{6,4},{8,10},{10,8},{12,14},{14,12},{16,18},{18,... | collective-permute-start | bytes 6291464 | tf_op jit(solution)/shard_map/ppermute | solution.py:1434
  522.7 7.5 copy-start.11
  528.6 95.7 %collective-permute-start.10 = (bf16[512,2048]{1,0:T(8,128)(2,1)}, bf16[512,2048]{1,0:T(8,128)(2,1)}, u32[]{:S(2)}, u32[]{:S(2)}) collective-permute-start(bf16[512,2048]{1,0:T(8,128)(2,1)} %add_convert_fusion.refs_14_), channel_id=1, source_target_pairs={{0,1},{1,0},{2,3},{3,2},{4,5},{5,4},{6,7},{7,6},{8,9},{9,8},{10,11... | collective-permute-start | bytes 6291464 | tf_op jit(solution)/shard_map/ppermute | solution.py:1431
  532.3 39.2 %slice-start.4 = ((s8[6291456]{0:T(1024)(128)(4,1)}), s8[4194304]{0:T(1024)(128)(4,1)S(1)}, s32[]{:S(2)}) async-start(s8[6291456]{0:T(1024)(128)(4,1)} %bitcast.147), calls=%async_computation.7 | async-start | bytes 8388608
  541.8 29.7 %slice-start.5 = ((s8[6291456]{0:T(1024)(128)(4,1)}), s8[2097152]{0:T(1024)(128)(4,1)S(1)}, s32[]{:S(2)}) async-start(s8[6291456]{0:T(1024)(128)(4,1)} %bitcast.147), calls=%async_computation.8 | async-start | bytes 4194304
  541.8 29.7 %copy-start.9 = (bf16[8,1,64,1536]{3,2,1,0:T(8,128)(2,1)S(1)}, bf16[8,1,64,1536]{3,2,1,0:T(8,128)(2,1)}, u32[]{:S(2)}) copy-start(bf16[8,1,64,1536]{3,2,1,0:T(8,128)(2,1)} %get-tuple-element.217) | copy-start | bytes 4718596
  624.3 8.9 %copy-start.1 = (bf16[1536,1024]{1,0:T(8,128)(2,1)S(1)}, bf16[1536,1024]{1,0:T(8,128)(2,1)}, u32[]{:S(2)}) copy-start(bf16[1536,1024]{1,0:T(8,128)(2,1)} %get-tuple-element.125) | copy-start | bytes 9437188
  624.3 8.9 %copy-start.14 = (bf16[1536,128]{1,0:T(8,128)(2,1)S(1)}, bf16[1536,128]{1,0:T(8,128)(2,1)}, u32[]{:S(2)}) copy-start(bf16[1536,128]{1,0:T(8,128)(2,1)} %get-tuple-element.124) | copy-start | bytes 1179652
  633.2 79.1 %collective-permute-start.12 = (bf16[2,256,2048]{2,1,0:T(8,128)(2,1)}, bf16[2,256,2048]{2,1,0:T(8,128)(2,1)}, u32[]{:S(2)}, u32[]{:S(2)}) collective-permute-start(bf16[2,256,2048]{2,1,0:T(8,128)(2,1)} %get-tuple-element.117.refs_9_), channel_id=1, source_target_pairs={{0,8},{2,10},{4,12},{6,14},{8,0},{10,2},{12,4},{14,6},{16,24},{18,... | collective-permute-start | bytes 6291464 | tf_op jit(solution)/shard_map/ppermute | solution.py:1434
  695.0 11.6 %copy-start = (bf16[1536,512]{1,0:T(8,128)(2,1)S(1)}, bf16[1536,512]{1,0:T(8,128)(2,1)}, u32[]{:S(2)}) copy-start(bf16[1536,512]{1,0:T(8,128)(2,1)} %token_pull.2.refs_6_) | copy-start | bytes 4718596
  706.6 102.4 %collective-permute-start.11 = (bf16[1536,512]{1,0:T(8,128)(2,1)S(1)}, bf16[1536,512]{1,0:T(8,128)(2,1)}, u32[]{:S(2)}, u32[]{:S(2)}) collective-permute-start(bf16[1536,512]{1,0:T(8,128)(2,1)S(1)} %copy-done), channel_id=1, source_target_pairs={{0,1},{1,0},{2,3},{3,2},{4,5},{5,4},{6,7},{7,6},{8,9},{9,8},{10,11... | collective-permute-start | bytes 4718600 | tf_op jit(solution)/shard_map/ppermute | solution.py:1431
Sparse Core Ops, SparseCore 0:
  118.5 37.0 all-gather.3
  157.8 49.4 all-gather.5
  209.5 49.2 all-gather.7

commit v8 on v7

--- a/solution.py
+++ b/solution.py
@@ -40,6 +40,9 @@
     return jax.ShapeDtypeStruct(shape, dtype)
 
 
+VMEM_SLACK = 16 * 1024 * 1024
+
+
 class Order:
     last = ()
 
@@ -57,6 +60,14 @@
     size = sum(math.prod(o.shape) * o.dtype.itemsize for o in list(operands) + list(out_shape))
     if flops == 0:
         size = 1024
+    need = VMEM_SLACK
+    for spec, array in zip(list(in_specs) + list(out_specs), list(operands)[prefetch:] + list(out_shape)):
+        if spec.block_shape is not None:
+            block = math.prod(spec.block_shape) * array.dtype.itemsize
+            need += block if spec.pipeline_mode is not None else 2 * block
+    for buffer in scratch:
+        if getattr(buffer, "memory_space", None) == pltpu.VMEM:
+            need += math.prod(buffer.shape) * jnp.dtype(buffer.dtype).itemsize
     outs = pl.pallas_call(
         wrapped,
         grid_spec=pltpu.PrefetchScalarGridSpec(
@@ -68,7 +79,7 @@
         ),
         out_shape=out_shape,
         compiler_params=pltpu.CompilerParams(
-            vmem_limit_bytes=VMEM_LIMIT, collective_id=remote, has_side_effects=remote is not None
+            vmem_limit_bytes=min(VMEM_LIMIT, need), collective_id=remote, has_side_effects=remote is not None
         ),
         cost_estimate=pl.CostEstimate(flops=flops, bytes_accessed=size, transcendentals=0),
         name=name,
@@ -138,47 +149,6 @@
             bit //= 2
         order.append((piece, bits))
     return order
-
-
-def weights_kernel(rows, *refs):
-    (qkv, proj, pack, qkv_o, proj_o, pack_o), (sent, arrived, wide_sent, wide_arrived) = refs[:6], refs[6:]
-    r, c = lax.axis_index("rows"), lax.axis_index("cols")
-    partner = {"cols": 1 - c}
-    bits = [1 << b for b in range(rows.bit_length() - 1)]
-    greet([partner] + [{"rows": across(r, bit)} for bit in bits])
-    pairs = [(qkv.at[r], qkv_o.at[r]), (proj, proj_o), (pack, pack_o)]
-    copies = [
-        send(source, target, sent.at[place], arrived.at[place], partner)
-        for place, (source, target) in enumerate(pairs)
-    ]
-    round_copies = {0: copies[0]}
-    for piece, over in spread_order(rows):
-        row = flipped(r, piece)
-        round_copies[piece].wait_recv()
-        for bit in over:
-            round_copies[piece | bit] = send(
-                qkv_o.at[row], qkv_o.at[row], wide_sent.at[piece | bit], wide_arrived.at[piece | bit],
-                {"rows": across(r, bit)},
-            )
-    for copy in round_copies.values():
-        copy.wait_send()
-    for copy in copies[1:]:
-        copy.wait()
-
-
-def gather_weights(rows, qkv, proj, pack):
-    pieces = qkv.reshape(rows, -1, qkv.shape[-1])
-    operands = (pieces, proj, pack)
-    qkv_o, proj_o, pack_o = call(
-        functools.partial(weights_kernel, rows), "gather_weights", (1,),
-        [ANYWHERE] * 3, [ANYWHERE] * 3, [shaped(o.dtype, *o.shape) for o in operands],
-        operands, 0, remote=1,
-        scratch=[
-            pltpu.SemaphoreType.DMA((3,)), pltpu.SemaphoreType.DMA((3,)),
-            pltpu.SemaphoreType.DMA((rows,)), pltpu.SemaphoreType.DMA((rows,)),
-        ],
-    )
-    return qkv_o.reshape(qkv.shape), proj_o, pack_o
 
 
 def gather_kernel(rows, own, out, own_sem, sent, arrived):
@@ -209,10 +179,10 @@
 PARTS = 2
 
 
-def gather_rows(rows, own):
+def gather_rows(rows, own, remote):
     return call(
         functools.partial(gather_kernel, rows), "gather_rows", (1,), [ANYWHERE], [ANYWHERE],
-        [shaped(own.dtype, rows, *own.shape)], (own,), 0, remote=2,
+        [shaped(own.dtype, rows, *own.shape)], (own,), 0, remote=remote,
         scratch=[
             pltpu.SemaphoreType.DMA, pltpu.SemaphoreType.DMA((rows, PARTS)),
             pltpu.SemaphoreType.DMA((rows, PARTS)),
@@ -359,7 +329,6 @@
     others = [{"cols": (c + cols - k) % cols} for k in range(1, cols)]
     core, x_side = side_at(r, 1), side_at(r, x_bit)
     greet([{"rows": across(r, bit)} for bit in [1, x_bit] + z_bits] + others)
-    du_bits = z_bits[1:] + [x_bit]
     chunks = range(4)
     slots = range(cols - 1, -1, -1)
     copies = {}
@@ -448,8 +417,8 @@
         if level == levels:
             du_out[place] = total
             return
-        bit = du_bits[level]
-        near, far = halves(total, side_at(r, bit), share if bit == x_bit else 2 * share)
+        bit = z_bits[level]
+        near, far = halves(total, side_at(r, bit), share)
         du_z_out[level][place] = far.astype(BF16)
         du_kept[level][place] = near
         copies["du", level, place] = send(
@@ -940,12 +909,11 @@
 
 
 def join_kernel(slots, place_ref, *refs):
-    out_ref, turned_ref = refs[-2:]
+    out_ref = refs[-1]
     width = refs[0].shape[1]
     for k in range(slots):
         at = pl.ds(pl.multiple_of((place_ref[0] + slots - k) % slots * width, width), width)
         out_ref[:, at] = refs[k][...]
-        turned_ref[at, :] = refs[k][...].astype(F32).T.astype(BF16)
 
 
 def join(c, slots):
@@ -955,9 +923,8 @@
     return call(
         functools.partial(join_kernel, len(slots)), "join", (n // step,),
         [row_spec(step, width)] * len(slots),
-        [row_spec(step, D), pl.BlockSpec((D, step), lambda i, *_: (0, i))],
-        [shaped(BF16, n, D), shaped(BF16, D, n)], (c.reshape(1), *slots), 0, prefetch=1,
-    )
+        [row_spec(step, D)], [shaped(BF16, n, D)], (c.reshape(1), *slots), 0, prefetch=1,
+    )[0]
 
 
 def assemble_kernel(place_ref, *refs):
@@ -1464,6 +1431,10 @@
     def part(k):
         return lax.dynamic_index_in_dim(parts, (c + k) % C, 0, keepdims=False)
 
+    qkv_piece = lax.dynamic_index_in_dim(
+        w_qkv.reshape(R, -1, w_qkv.shape[2]), r, 0, keepdims=False
+    )
+    qkv_pieces = [shift_cols(qkv_piece, k) for k in range(1, C)]
     token_slots = [part(0)] + [shift_cols(part(k), k) for k in range(1, C)]
     own_sizes = lax.dynamic_index_in_dim(
         lax.dynamic_index_in_dim(doc_lengths, r, 0, keepdims=False), c, 0, keepdims=False
@@ -1472,27 +1443,19 @@
     doc_ends = jnp.cumsum(sizes, axis=1)
     begins = doc_ends - sizes
     cosine, sine, ext_k, ext_q, picks = prepare(n, Q, own_sizes, match_picks, begins, sizes)
-    if C == 2:
-        qkv_other, proj_other, pack_other = gather_weights(R, w_qkv, w_proj, packed.reshape(8, -1))
-        wqkv_slots = [w_qkv, qkv_other]
-        wproj = jnp.concatenate(in_order([w_proj, proj_other]), axis=0)
-        packs = [packed, pack_other.reshape(-1)]
-    else:
-
-        def gather_slots(shard):
-            flat = shard.reshape(-1, shard.shape[-1])
-            piece = lax.dynamic_index_in_dim(
-                flat.reshape(R, flat.shape[0] // R, flat.shape[1]), r, 0, keepdims=False
-            )
-            others = gather_pieces([shift_cols(piece, k) for k in range(1, C)])
-            return [shard] + [other.reshape(shard.shape) for other in others]
-
-        wqkv_slots = gather_slots(w_qkv)
-        wproj = jnp.concatenate(
-            in_order([w_proj] + [shift_cols(w_proj, k) for k in range(1, C)]), axis=0
-        )
-        packs = [packed] + [shift_cols(packed, k) for k in range(1, C)]
-    x, x_t = join(c, token_slots)
+    wqkv_slots = [w_qkv]
+    for k in range(1, C):
+        if C == 2:
+            other = gather_rows(R, qkv_pieces[k - 1], 1)
+        else:
+            other = lax.all_gather(qkv_pieces[k - 1], "rows", axis=0, tiled=True)
+        wqkv_slots.append(other.reshape(w_qkv.shape))
+    x = join(c, token_slots)
+    behind, _ = lax.optimization_barrier(((w_proj, packed), x))
+    wproj = jnp.concatenate(
+        in_order([w_proj] + [shift_cols(behind[0], k) for k in range(1, C)]), axis=0
+    )
+    packs = [packed] + [shift_cols(behind[1], k) for k in range(1, C)]
 
     ordered_packs = in_order(packs)
 
@@ -1559,7 +1522,7 @@
         normed_one, vectors, wproj, active, wdown_slots
     )
 
-    doc_tile = gather_rows(R, unit_low[Q:]).reshape(R * DS, 128)
+    doc_tile = gather_rows(R, unit_low[Q:], 2).reshape(R * DS, 128)
     query_tile = jnp.concatenate(
         in_order([unit_low[:Q]] + [shift_cols(unit_low[:Q], k) for k in range(1, C)]), axis=0
     )
@@ -1687,7 +1650,7 @@
 
     for k in slots_back[:-1]:
         pull_attention(k)
-    wide_state = next_fold([cols_state(down_kept), cols_state(up_kept)], z_bits[0], 2 * share)
+    wide_state = next_fold([cols_state(down_kept), cols_state(up_kept)], x_bit, share)
     pull_attention(0)
     sent = [
         shift_cols(token_pull((c + k) % C, resid_one_grad, mixed_grads, wqkv_slots, BF16), k)
@@ -1695,7 +1658,7 @@
     ]
     own_tokens = token_pull(c, resid_one_grad, mixed_grads, wqkv_slots, F32)
     late_grad, wide_grad, small = late_sums(
-        R, C, halves_of(x_t), halves_of(branch_one_t), mixed_grads, attended, *wide_state,
+        R, C, halves_of(x.T), halves_of(branch_one_t), mixed_grads, attended, *wide_state,
         gather_small(),
     )
     tokens_grad = assemble(c, Q, [own_tokens] + sent)

time: 832 us -> 871 us (1.047)
  local copies, waits for them, and re-layouts: 51.1 us -> 195 us
  Pallas kernels: 672 us -> 561 us
    unnamed x81 -> x313, local copies, waits for them, and re-layouts: 6.39 us -> 123 us
    pallas_call x27, Pallas kernels: 672 us -> 561 us  [call(): pl.pallas_call(wrapped, grid_spec=pltpu.PrefetchScalarGridSpec(num_scalar...]
  transfers between devices with their start and end apart: 16 -> 19, of which waited for: 2 -> 2; matrix products, arithmetic and copies ran while one was open for 11% -> 16% of each run, Pallas kernels for 65% -> 52%
where the time goes in v8:
time: 871 us; the launch traced here: 862 us
  Pallas kernels  561 us (64%)
  local copies, waits for them, and re-layouts  195 us (22%)
  matrix products  49.4 us (6%)
  other arithmetic  21.5 us (2%)
  between operations  16.4 us (2%)
  starting transfers between devices  14.3 us (2%)
    pallas_call x27, Pallas kernels, call(): pl.pallas_call(wrapped, grid_spec=pltpu.PrefetchScalarGridSpec(num_scalar...  561 us
    unnamed x313, local copies, waits for them, and re-layouts  123 us
    dot_general x9, matrix products, mm(): return lax.dot_general(left, right, dims, preferred_element_type=F32)  49.4 us
  transfers between devices with their start and end apart: 19, of which 2 were waited for; matrix products, arithmetic and copies ran while one was open for 16% of the time, Pallas kernels for 52%

profile of v8, /device:TPU:0, one launch (start us, length us, event | category | flops | bytes accessed | tf_op | source)
XLA Modules:
  0.0 861.9 jit_solution(451587950184236137)
XLA Ops:
  8.2 3.0 collective-permute-start.1
  11.2 3.1 slice.209
  14.4 3.5 fusion.1
  20.1 7.0 prepare.1
  32.3 26.3 %gather_rows.2.refs_3_ = bf16[16,192,512]{2,1,0:T(8,128)(2,1)S(1)} custom-call(bf16[192,512]{1,0:T(8,128)(2,1)S(1)} %copy-done.99, s32[16,4,1024]{2,1,0:T(4,128)S(1)} %get-tuple-element.70.refs_1_.refs_4_), custom_call_target="tpu_custom_call" | custom-call | bytes 1024 | tf_op jit(solution)/shard_map/gather_rows/pallas_call | solution.py:71
  58.7 2.3 join.1.refs_0_.refs_7_
  74.2 6.0 project_qkv.2.refs_1_
  81.4 2.2 copy-done.1
  120.3 2.4 copy-done.2
  124.7 31.8 %attention_forward.2 = (bf16[1536,512]{1,0:T(8,128)(2,1)S(1)}, bf16[1536,512]{1,0:T(8,128)(2,1)S(1)}, bf16[1536,512]{1,0:T(8,128)(2,1)S(1)}) custom-call(s32[12]{0:T(128)S(1)} %pad_add_fusion.1.refs_0_, bf16[3,1536,512]{2,1,0:T(8,128)(2,1)S(1)} %copy-done.2, bf16[1536,128]{1,0:T(8,128)(2,1)S(1)} %get-tuple-element.74.refs_2_.refs_6_, ...), custom_call_target="tpu_custom_call" | custom-call | bytes 1024 | tf_op jit(solution)/shard_map/attention_forward/pallas_call | solution.py:71
  157.7 6.0 project_qkv.3.refs_1_.refs_4_
  163.8 32.0 %attention_forward.3 = (bf16[1536,512]{1,0:T(8,128)(2,1)S(1)}, bf16[1536,512]{1,0:T(8,128)(2,1)S(1)}, bf16[1536,512]{1,0:T(8,128)(2,1)S(1)}) custom-call(s32[12]{0:T(128)S(1)} %pad_add_fusion.1.refs_0_, bf16[3,1536,512]{2,1,0:T(8,128)(2,1)S(1)} %project_qkv.3.refs_1_.refs_4_, bf16[1536,128]{1,0:T(8,128)(2,1)S(1)} %get-tuple-element.74.refs_2_.refs_6_, ...), custom_call_target="tpu_custom_call" | custom-call | bytes 1024 | tf_op jit(solution)/shard_map/attention_forward/pallas_call | solution.py:71
  195.9 2.2 copy-done
  201.5 2.3 copy-done.19
  209.9 6.0 out_and_norm.1
  215.9 2.7 copy-done.24
  220.4 19.6 %up_and_gelu.2 = (bf16[1536,2048]{1,0:T(8,128)(2,1)S(1)}, f32[1536,2048]{1,0:T(8,128)}) custom-call(bf16[1536,1024]{1,0:T(8,128)(2,1)S(1)} %get-tuple-element.81.refs_0_, bf16[1024,2048]{1,0:T(8,128)(2,1)S(1)} %copy-done.32, f32[1,2048]{1,0:T(1,128)S(1)} %bitcast.160, f32[1536,1]{1,0:T(8,128)S(1)} %get-tuple-element.82.refs_3_.refs_2_), custom_call_target="tpu_custom_call" | custom-call | flops 16106127360 | bytes 26222592 | tf_op jit(solution)/shard_map/up_and_gelu/pallas_call | solution.py:71
  242.5 2.6 copy-done.125
  245.1 2.2 copy-done.33
  249.2 2.8 copy-done.126
  252.0 19.4 %up_and_gelu.3 = (bf16[1536,2048]{1,0:T(8,128)(2,1)S(1)}, f32[1536,2048]{1,0:T(8,128)}) custom-call(bf16[1536,1024]{1,0:T(8,128)(2,1)S(1)} %copy-done.124, bf16[1024,2048]{1,0:T(8,128)(2,1)S(1)} %copy-done.33, f32[1,2048]{1,0:T(1,128)S(1)} %bitcast.161, bf16[1536,2048]{1,0:T(8,128)(2,1)S(1)} %copy-done.126), custom_call_target="tpu_custom_call" | custom-call | flops 16106127360 | bytes 26222592 | tf_op jit(solution)/shard_map/up_and_gelu/pallas_call | solution.py:71
  271.4 2.7 copy-done.127
  275.8 2.2 copy-done.106
  278.0 23.7 %down_and_norm.1 = (f32[1536,1024]{1,0:T(8,128)}, f32[1536,1]{1,0:T(8,128)S(1)}, bf16[1536,1024]{1,0:T(8,128)(2,1)S(1)}, f32[1536,128]{1,0:T(8,128)S(1)}, bf16[1...) custom-call(f32[1536,1024]{1,0:T(8,128)} %copy-done.24, f32[8,1024]{1,0:T(8,128)S(1)} %copy-done.90, ...), custom_call_target="tpu_custom_call" | custom-call | flops 12884901888 | bytes 38187008 | tf_op jit(solution)/shard_map/down_and_norm/pallas_call | solution.py:71
  301.9 31.8 %gather_rows.3.refs_5_ = bf16[16,1024,128]{2,1,0:T(8,128)(2,1)S(1)} custom-call(bf16[1024,128]{1,0:T(8,128)(2,1)S(1)} %slice.228.refs_0_, f32[1536,1]{1,0:T(8,128)S(1)} %get-tuple-element.86.refs_1_.refs_5_), custom_call_target="tpu_custom_call" | custom-call | bytes 1024 | tf_op jit(solution)/shard_map/gather_rows/pallas_call | solution.py:71
  333.9 33.0 %score_forward.1.refs_6_ = f32[64,32]{1,0:T(8,128)S(1)} custom-call(s32[512]{0:T(512)S(1)} %copy-done.119, s32[512]{0:T(512)S(1)} %copy-done.117, bf16[16384,128]{1,0:T(8,128)(2,1)S(1)} %bitcast.152, bf16[1024,128]{1,0:T(8,128)(2,1)S(1)} %pad_maximum_fusion.3.refs_3_, s32[16,4,1024]{2,1,0:T(4,128)S(1)} %copy-done.94, ...), custom_call_target="tpu_custom_call" | custom-call | flops 4294967296 | bytes 4730880 | tf_op jit(solution)/shard_map/score_forward/pallas_call | solution.py:71
  369.7 2.3 collective-permute-done.6
  374.2 2.2 copy-done.35
  379.0 31.9 %score_backward.1 = (f32[16384,128]{1,0:T(8,128)S(1)}, f32[128,1024]{1,0:T(8,128)S(1)}) custom-call(s32[512]{0:T(512)S(1)} %copy-done.119, s32[512]{0:T(512)S(1)} %copy-done.117, bf16[16384,128]{1,0:T(8,128)(2,1)S(1)} %bitcast.153, bf16[1024,128]{1,0:T(8,128)(2,1)S(1)} %copy-done.97, s32[16,4,1024]{2,1,0:T(4,128)S(1)} %copy-done.95, ...), custom_call_target="tpu_custom_call" | custom-call | flops 8589934592 | bytes 13643776 | tf_op jit(solution)/shard_map/score_backward/pallas_call | solution.py:71
  410.9 3.3 copy-done.22
  419.9 3.4 constant_dynamic-slice_fusion.2
  423.4 3.9 copy-done.23
  427.3 32.9 %scatter_rows.1.refs_7_ = f32[1024,128]{1,0:T(8,128)S(1)} custom-call(f32[16,1024,128]{2,1,0:T(8,128)S(1)} %bitcast.150, f32[128,1024]{1,0:T(8,128)S(1)} %copy-done.53), custom_call_target="tpu_custom_call" | custom-call | bytes 1024 | tf_op jit(solution)/shard_map/scatter_rows/pallas_call | solution.py:71
  460.4 2.8 copy-done.28
  463.2 5.8 head_pull.1
  470.0 2.5 copy-done.25
  472.6 7.0 convolution_convert_fusion.3.refs_4_
  479.8 4.7 convolution_convert_fusion.2.refs_5_
  484.9 9.7 %up_pull.2 = (bf16[1536,2048]{1,0:T(8,128)(2,1)S(1)}, f32[8,2048]{1,0:T(8,128)S(1)}) custom-call(bf16[1536,1024]{1,0:T(8,128)(2,1)S(1)} %get-tuple-element.93.refs_0_, bf16[2048,1024]{1,0:T(8,128)(2,1)S(1)} %copy-done.36, f32[1536,2048]{1,0:T(8,128)} %get-tuple-element.95.refs_2_, f32[8,1024]{1,0:T(8,128)S(1)} %get-tuple-element.96.refs_3_, ...), custom_call_target="tpu_custom_call" | custom-call | flops 6442450944 | bytes 26279936 | tf_op jit(solution)/shard_map/up_pull/pallas_call | solution.py:71
  494.6 3.6 convolution_convert_fusion.1.refs_11_
  499.1 6.0 add_convert_fusion.1.refs_4_
  505.1 9.7 %up_pull.3 = (bf16[1536,2048]{1,0:T(8,128)(2,1)S(1)}, f32[8,2048]{1,0:T(8,128)S(1)}) custom-call(bf16[1536,1024]{1,0:T(8,128)(2,1)S(1)} %get-tuple-element.93.refs_0_, bf16[2048,1024]{1,0:T(8,128)(2,1)S(1)} %copy-done.107, f32[1536,2048]{1,0:T(8,128)} %get-tuple-element.94.refs_2_, f32[8,2048]{1,0:T(8,128)S(1)} %get-tuple-element.98.refs_3_, ...), custom_call_target="tpu_custom_call" | custom-call | flops 6442450944 | bytes 26279936 | tf_op jit(solution)/shard_map/up_pull/pallas_call | solution.py:71
  514.8 4.9 convolution_convert_fusion.refs_12_
  519.8 5.9 add_convert_fusion.refs_14_
  528.2 4.7 copy.76
  537.2 9.4 %convert_add_fusion.1.refs_13_ = f32[512,2048]{1,0:T(8,128)} fusion(bf16[512,2048]{1,0:T(8,128)(2,1)} %collective-permute-done.9, bf16[512,1536]{1,0:T(8,128)(2,1)} %bitcast.176, bf16[1536,2048]{1,0:T(8,128)(2,1)} %copy-done.125), kind=kOutput, calls=%fused_computation.2 | convolution fusion | flops 3223322624 | bytes 14155776 | tf_op jit(solution)/shard_map/dot_general | solution.py:23
  546.6 29.6 %hidden_pull.1 = (f32[1536,1024]{1,0:T(8,128)}, bf16[1024,1536]{1,0:T(8,128)(2,1)}, f32[8,1024]{1,0:T(8,128)S(1)}, bf16[1536,512]{1,0:T(8,128)(2,1)}, bf16[1536,512]{1,0:T(8,128)(2,1)}) custom-call(f32[1536,1024]{1,0:T(8,128)} %copy-done.25, f32[1536,1024]{1,0:T(8,128)} %copy-done.24, f32[1536,1]{1,0:T(8,128)S(1)} %copy-done.86, f32[8,1024]{1,0:T(8,128)S(1)} %copy-done.92, ...), custom_call_target="tpu_custom_call" | custom-call | bytes 1024 | tf_op jit(solution)/shard_map/hidden_pull/pallas_call | solution.py:71
  576.4 7.4 convert_add_fusion.refs_10_
  583.9 45.2 %attention_backward.2 = (bf16[3,1536,512]{2,1,0:T(8,128)(2,1)S(1)}, f32[8,512]{1,0:T(8,128)S(1)}) custom-call(s32[12]{0:T(128)S(1)} %copy-done.109, bf16[3,1536,512]{2,1,0:T(8,128)(2,1)S(1)} %bitcast.143, bf16[1536,512]{1,0:T(8,128)(2,1)S(1)} %copy-done.70, bf16[1536,512]{1,0:T(8,128)(2,1)S(1)} %copy-done.62, bf16[1536,512]{1,0:T(8,128)(2,1)S(1)} %copy-done.68, ...), custom_call_target="tpu_custom_call" | custom-call | bytes 1024 | tf_op jit(solution)/shard_map/attention_backward/pallas_call | solution.py:71
  629.2 2.2 copy-done.5
  631.4 2.2 copy-done.12
  633.6 5.8 fold.1
  665.2 2.3 copy-done.3
  676.0 45.2 %attention_backward.3 = (bf16[3,1536,512]{2,1,0:T(8,128)(2,1)S(1)}, f32[8,512]{1,0:T(8,128)S(1)}) custom-call(s32[12]{0:T(128)S(1)} %copy-done.110, bf16[3,1536,512]{2,1,0:T(8,128)(2,1)S(1)} %copy-done.3, bf16[1536,512]{1,0:T(8,128)(2,1)S(1)} %copy-done.66, bf16[1536,512]{1,0:T(8,128)(2,1)S(1)} %copy-done.59, bf16[1536,512]{1,0:T(8,128)(2,1)S(1)} %copy-done.64, ...), custom_call_target="tpu_custom_call" | custom-call | bytes 1024 | tf_op jit(solution)/shard_map/attention_backward/pallas_call | solution.py:71
  721.3 2.2 copy-done.7
  723.5 2.8 copy-done.4
  726.2 2.3 copy-done.6
  728.6 2.3 copy-done.8
  732.8 7.2 token_pull.2.refs_6_
  740.0 2.3 copy-done.9
  744.2 7.2 token_pull.3.refs_9_.refs_1_
  760.1 78.2 %late_sums.1 = (f32[4,64,512]{2,1,0:T(8,128)}, f32[2,64,2048]{2,1,0:T(8,128)}, f32[8,640]{1,0:T(8,128)}) custom-call(bf16[8,2,64,1536]{3,2,1,0:T(8,128)(2,1)} %bitcast.169, bf16[8,2,64,1536]{3,2,1,0:T(8,128)(2,1)} %bitcast.200, bf16[3,1536,512]{2,1,0:T(8,128)(2,1)} %copy-done.7, bf16[3,1536,512]{2,1,0:T(8,128)(2,1)} %copy-done.5, ...), custom_call_target="tpu_custom_call" | custom-call | flops 99999997952 | bytes 27414528 | tf_op jit(solution)/shard_map/late_sums/pallas_call | solution.py:71
  846.3 2.3 slice_bitcast_fusion
  848.6 6.3 assemble.1
  (453 shorter events, 157.1 us)
Async XLA Ops:
  7.2 194.4 %all-gather.4.cloned.1.call-start = ((), (), s32[]{:S(2)}) async-start(), calls=%async_computation | async-start | bytes 1114112 | tf_op jit(solution)/shard_map/all_gather | solution.py:1420
  8.2 22.5 %collective-permute-start.1 = (bf16[192,512]{1,0:T(8,128)(2,1)S(1)}, bf16[192,512]{1,0:T(8,128)(2,1)S(1)}, u32[]{:S(2)}, u32[]{:S(2)}) collective-permute-start(bf16[192,512]{1,0:T(8,128)(2,1)S(1)} %dynamic-slice_bitcast_fusion.2), channel_id=1, source_target_pairs={{0,1},{1,0},{2,3},{3,2},{4,5},{5,4},{6,7},{7,6},{8,9},{9,8},{10,11... | collective-permute-start | bytes 589832 | tf_op jit(solution)/shard_map/ppermute | solution.py:1398
  17.9 40.7 %collective-permute-start = (bf16[1536,512]{1,0:T(8,128)(2,1)}, bf16[1536,512]{1,0:T(8,128)(2,1)}, u32[]{:S(2)}, u32[]{:S(2)}) collective-permute-start(bf16[1536,512]{1,0:T(8,128)(2,1)} %get-tuple-element.215), channel_id=1, source_target_pairs={{0,1},{1,0},{2,3},{3,2},{4,5},{5,4},{6,7},{7,6},{8,9},{9,8},{10,11... | collective-permute-start | bytes 4718600 | tf_op jit(solution)/shard_map/ppermute | solution.py:1398
  20.1 38.5 %copy-start.115 = (s32[4]{0:T(128)}, s32[4]{0:T(128)S(1)}, u32[]{:S(2)}) copy-start(s32[4]{0:T(128)S(1)} %fusion.4.refs_0_) | copy-start | bytes 52
  20.1 38.6 %copy-start.29 = (bf16[1536,512]{1,0:T(8,128)(2,1)S(1)}, bf16[1536,512]{1,0:T(8,128)(2,1)}, u32[]{:S(2)}) copy-start(bf16[1536,512]{1,0:T(8,128)(2,1)} %get-tuple-element.216.refs_1_) | copy-start | bytes 4718596
  27.1 31.5 %copy-start.37 = (f32[1536,128]{1,0:T(8,128)}, f32[1536,128]{1,0:T(8,128)S(1)}, u32[]{:S(2)}) copy-start(f32[1536,128]{1,0:T(8,128)S(1)} %get-tuple-element.72.refs_3_.refs_7_) | copy-start | bytes 2359300
  27.1 31.5 %copy-start.42 = (f32[1536,128]{1,0:T(8,128)}, f32[1536,128]{1,0:T(8,128)S(1)}, u32[]{:S(2)}) copy-start(f32[1536,128]{1,0:T(8,128)S(1)} %get-tuple-element.73.refs_4_.refs_8_) | copy-start | bytes 2359300
  27.2 31.5 %copy-start.54 = (bf16[1536,128]{1,0:T(8,128)(2,1)}, bf16[1536,128]{1,0:T(8,128)(2,1)S(1)}, u32[]{:S(2)}) copy-start(bf16[1536,128]{1,0:T(8,128)(2,1)S(1)} %get-tuple-element.75.refs_3_) | copy-start | bytes 1179652
  27.2 31.5 %copy-start.93 = (s32[16,4,1024]{2,1,0:T(4,128)}, s32[16,4,1024]{2,1,0:T(4,128)S(1)}, u32[]{:S(2)}) copy-start(s32[16,4,1024]{2,1,0:T(4,128)S(1)} %get-tuple-element.70.refs_1_.refs_4_) | copy-start | bytes 786436
  62.7 17.6 %collective-permute-start.3 = (bf16[288,1024]{1,0:T(8,128)(2,1)}, bf16[288,1024]{1,0:T(8,128)(2,1)}, u32[]{:S(2)}, u32[]{:S(2)}) collective-permute-start(bf16[288,1024]{1,0:T(8,128)(2,1)} %pad_maximum_fusion.1), channel_id=1, source_target_pairs={{0,1},{1,0},{2,3},{3,2},{4,5},{5,4},{6,7},{7,6},{8,9},{9,8},{10,11... | collective-permute-start | bytes 1769480 | tf_op jit(solution)/shard_map/ppermute | solution.py:1398
  80.2 11.9 %copy-start.112 = (f32[2048]{0:T(1024)S(1)}, f32[2048]{0:T(1024)}, u32[]{:S(2)}) copy-start(f32[2048]{0:T(1024)} %param.30) | copy-start | bytes 24580
  85.0 160.1 %all-gather.6.cloned.1.call-start = ((), (), s32[]{:S(2)}) async-start(), calls=%async_computation.1 | async-start | bytes 4456448 | tf_op jit(solution)/shard_map/all_gather | solution.py:1420
  88.6 185.4 %all-gather.8.cloned.1.call-start = ((), (), s32[]{:S(2)}) async-start(), calls=%async_computation.2 | async-start | bytes 4456448 | tf_op jit(solution)/shard_map/all_gather | solution.py:1420
  103.3 4.3 collective-permute-start.2
  104.0 59.8 %copy-start.108 = (s32[12]{0:T(128)}, s32[12]{0:T(128)S(1)}, u32[]{:S(2)}) copy-start(s32[12]{0:T(128)S(1)} %pad_add_fusion.1.refs_0_) | copy-start | bytes 148
  104.7 13.9 %collective-permute-start.4 = (bf16[512,128]{1,0:T(8,128)(2,1)}, bf16[512,128]{1,0:T(8,128)(2,1)}, u32[]{:S(2)}, u32[]{:S(2)}) collective-permute-start(bf16[512,128]{1,0:T(8,128)(2,1)} %param.35), channel_id=1, source_target_pairs={{0,1},{1,0},{2,3},{3,2},{4,5},{5,4},{6,7},{7,6},{8,9},{9,8},{10,11... | collective-permute-start | bytes 393224 | tf_op jit(solution)/shard_map/ppermute | solution.py:1398
  119.5 38.1 %copy-start.114 = (f32[3,512]{1,0:T(4,128)S(1)}, f32[3,512]{1,0:T(4,128)}, u32[]{:S(2)}) copy-start(f32[3,512]{1,0:T(4,128)} %slice.223.refs_2_) | copy-start | bytes 18436
  124.7 33.0 %copy-start.18 = (bf16[1536,1024]{1,0:T(8,128)(2,1)S(1)}, bf16[1536,1024]{1,0:T(8,128)(2,1)}, u32[]{:S(2)}) copy-start(bf16[1536,1024]{1,0:T(8,128)(2,1)} %copy-done.16) | copy-start | bytes 9437188
  124.7 33.0 %copy-start.39 = (f32[1536,128]{1,0:T(8,128)S(1)}, f32[1536,128]{1,0:T(8,128)}, u32[]{:S(2)}) copy-start(f32[1536,128]{1,0:T(8,128)} %copy-done.37) | copy-start | bytes 2359300
  124.7 33.0 %copy-start.44 = (f32[1536,128]{1,0:T(8,128)S(1)}, f32[1536,128]{1,0:T(8,128)}, u32[]{:S(2)}) copy-start(f32[1536,128]{1,0:T(8,128)} %copy-done.42) | copy-start | bytes 2359300
  220.4 24.8 %copy-start.113 = (f32[2048]{0:T(1024)S(1)}, f32[2048]{0:T(1024)}, u32[]{:S(2)}) copy-start(f32[2048]{0:T(1024)} %slice.275) | copy-start | bytes 24580
  278.0 23.8 %copy-start.141 = (s32[32]{0:T(128)S(1)}, s32[32]{0:T(128)}, u32[]{:S(2)}) copy-start(s32[32]{0:T(128)} %param.22) | copy-start | bytes 388
  301.7 32.1 %copy-start.47 = (f32[1536,1]{1,0:T(8,128)}, f32[1536,1]{1,0:T(8,128)S(1)}, u32[]{:S(2)}) copy-start(f32[1536,1]{1,0:T(8,128)S(1)} %get-tuple-element.86.refs_1_.refs_5_) | copy-start | bytes 18436
  301.7 32.1 %copy-start.49 = (bf16[1536,1024]{1,0:T(8,128)(2,1)}, bf16[1536,1024]{1,0:T(8,128)(2,1)S(1)}, u32[]{:S(2)}) copy-start(bf16[1536,1024]{1,0:T(8,128)(2,1)S(1)} %get-tuple-element.119) | copy-start | bytes 9437188
  301.7 32.1 %copy-start.81 = (f32[1536,128]{1,0:T(8,128)}, f32[1536,128]{1,0:T(8,128)S(1)}, u32[]{:S(2)}) copy-start(f32[1536,128]{1,0:T(8,128)S(1)} %get-tuple-element.89.refs_1_) | copy-start | bytes 2359300
  301.7 32.1 %copy-start.83 = (f32[1536,1]{1,0:T(8,128)}, f32[1536,1]{1,0:T(8,128)S(1)}, u32[]{:S(2)}) copy-start(f32[1536,1]{1,0:T(8,128)S(1)} %get-tuple-element.90.refs_2_) | copy-start | bytes 18436
  301.7 32.0 %collective-permute-start.5 = (bf16[512,128]{1,0:T(8,128)(2,1)S(1)}, bf16[512,128]{1,0:T(8,128)(2,1)S(1)}, u32[]{:S(2)}, u32[]{:S(2)}) collective-permute-start(bf16[512,128]{1,0:T(8,128)(2,1)S(1)} %slice.229), channel_id=1, source_target_pairs={{0,1},{1,0},{2,3},{3,2},{4,5},{5,4},{6,7},{7,6},{8,9},{9,8},{10,11... | collective-permute-start | bytes 393224 | tf_op jit(solution)/shard_map/ppermute | solution.py:1398
  301.8 32.0 %copy-start.94 = (s32[16,4,1024]{2,1,0:T(4,128)S(1)}, s32[16,4,1024]{2,1,0:T(4,128)}, u32[]{:S(2)}) copy-start(s32[16,4,1024]{2,1,0:T(4,128)} %copy-done.93) | copy-start | bytes 786436
  301.9 32.0 %copy-start.117 = (s32[512]{0:T(512)S(1)}, s32[512]{0:T(512)}, u32[]{:S(2)}) copy-start(s32[512]{0:T(512)} %copy-done.116) | copy-start | bytes 6148
  301.9 32.0 %copy-start.119 = (s32[512]{0:T(512)S(1)}, s32[512]{0:T(512)}, u32[]{:S(2)}) copy-start(s32[512]{0:T(512)} %copy-done.118) | copy-start | bytes 6148
  333.7 33.2 %copy-start.34 = (bf16[16,1024,128]{2,1,0:T(8,128)(2,1)}, bf16[16,1024,128]{2,1,0:T(8,128)(2,1)S(1)}, u32[]{:S(2)}) copy-start(bf16[16,1024,128]{2,1,0:T(8,128)(2,1)S(1)} %gather_rows.3.refs_5_) | copy-start | bytes 12582916
  333.8 33.1 %copy-start.96 = (bf16[1024,128]{1,0:T(8,128)(2,1)}, bf16[1024,128]{1,0:T(8,128)(2,1)S(1)}, u32[]{:S(2)}) copy-start(bf16[1024,128]{1,0:T(8,128)(2,1)S(1)} %pad_maximum_fusion.3.refs_3_) | copy-start | bytes 786436
  368.1 3.9 collective-permute-start.6
  418.0 42.3 %collective-permute-start.7 = (f32[512,128]{1,0:T(8,128)S(1)}, f32[512,128]{1,0:T(8,128)S(1)}, u32[]{:S(2)}, u32[]{:S(2)}) collective-permute-start(f32[512,128]{1,0:T(8,128)S(1)} %dynamic-slice_bitcast_fusion), channel_id=1, source_target_pairs={{0,1},{1,0},{2,3},{3,2},{4,5},{5,4},{6,7},{7,6},{8,9},{9,8},{10,11... | collective-permute-start | bytes 786440 | tf_op jit(solution)/shard_map/ppermute | solution.py:1398
  423.3 71.2 %copy-start.132 = (bf16[8,1,64,1536]{3,2,1,0:T(8,128)(2,1)}, bf16[8,1,64,1536]{3,2,1,0:T(8,128)(2,1)S(1)}, u32[]{:S(2)}) copy-start(bf16[8,1,64,1536]{3,2,1,0:T(8,128)(2,1)S(1)} %get-tuple-element.212) | copy-start | bytes 4718596
  427.3 33.0 %copy-start.129 = (f32[1024,128]{1,0:T(8,128)S(1)}, f32[1024,128]{1,0:T(8,128)}, u32[]{:S(2)}) copy-start(f32[1024,128]{1,0:T(8,128)} %copy.78) | copy-start | bytes 1572868
  427.3 33.1 %copy-start.48 = (f32[1536,1]{1,0:T(8,128)S(1)}, f32[1536,1]{1,0:T(8,128)}, u32[]{:S(2)}) copy-start(f32[1536,1]{1,0:T(8,128)} %copy-done.47) | copy-start | bytes 18436
  427.3 33.1 %copy-start.78 = (bf16[1024,128]{1,0:T(8,128)(2,1)S(1)}, bf16[1024,128]{1,0:T(8,128)(2,1)}, u32[]{:S(2)}) copy-start(bf16[1024,128]{1,0:T(8,128)(2,1)} %pad_maximum_fusion.2.refs_2_.refs_3_) | copy-start | bytes 786436
  427.3 33.1 %copy-start.82 = (f32[1536,128]{1,0:T(8,128)S(1)}, f32[1536,128]{1,0:T(8,128)}, u32[]{:S(2)}) copy-start(f32[1536,128]{1,0:T(8,128)} %copy-done.81) | copy-start | bytes 2359300
  427.3 33.1 %copy-start.84 = (f32[1536,1]{1,0:T(8,128)S(1)}, f32[1536,1]{1,0:T(8,128)}, u32[]{:S(2)}) copy-start(f32[1536,1]{1,0:T(8,128)} %copy-done.83) | copy-start | bytes 18436
  427.3 33.1 %copy-start.91 = (f32[8,1024]{1,0:T(8,128)S(1)}, f32[8,1024]{1,0:T(8,128)}, u32[]{:S(2)}) copy-start(f32[8,1024]{1,0:T(8,128)} %stack.67.refs_1_.refs_6_.refs_3_) | copy-start | bytes 98308
  469.7 15.1 %copy-start.103 = (f32[8,1024]{1,0:T(8,128)}, f32[8,1024]{1,0:T(8,128)S(1)}, u32[]{:S(2)}) copy-start(f32[8,1024]{1,0:T(8,128)S(1)} %get-tuple-element.96.refs_3_) | copy-start | bytes 98308
  472.6 25.9 %copy-start.131 = (bf16[8,1,64,1536]{3,2,1,0:T(8,128)(2,1)}, bf16[8,1,64,1536]{3,2,1,0:T(8,128)(2,1)S(1)}, u32[]{:S(2)}) copy-start(bf16[8,1,64,1536]{3,2,1,0:T(8,128)(2,1)S(1)} %get-tuple-element.213) | copy-start | bytes 4718596
  479.6 18.8 %collective-permute-start.8 = (bf16[512,2048]{1,0:T(8,128)(2,1)S(1)}, bf16[512,2048]{1,0:T(8,128)(2,1)}, u32[]{:S(2)}, u32[]{:S(2)}) collective-permute-start(bf16[512,2048]{1,0:T(8,128)(2,1)S(1)} %convolution_convert_fusion.3.refs_4_), channel_id=1, source_target_pairs={{0,2},{2,0},{4,6},{6,4},{8,10},{10,8},{12,14},{14,12},{16,18},{18,... | collective-permute-start | bytes 6291464 | tf_op jit(solution)/shard_map/ppermute | solution.py:1401
  484.5 52.7 %collective-permute-start.9 = (bf16[512,2048]{1,0:T(8,128)(2,1)}, bf16[512,2048]{1,0:T(8,128)(2,1)}, u32[]{:S(2)}, u32[]{:S(2)}) collective-permute-start(bf16[512,2048]{1,0:T(8,128)(2,1)} %convolution_convert_fusion.2.refs_5_), channel_id=1, source_target_pairs={{0,2},{2,0},{4,6},{6,4},{8,10},{10,8},{12,14},{14,12},{16,18},{18,... | collective-permute-start | bytes 6291464 | tf_op jit(solution)/shard_map/ppermute | solution.py:1401
  484.9 13.6 %slice-start.6 = ((s8[6291456]{0:T(1024)(128)(4,1)}), s8[2097152]{0:T(1024)(128)(4,1)S(1)}, s32[]{:S(2)}) async-start(s8[6291456]{0:T(1024)(128)(4,1)} %bitcast.165), calls=%async_computation.9 | async-start | bytes 4194304
  494.6 25.2 %copy-start.26 = (bf16[1536,2048]{1,0:T(8,128)(2,1)}, bf16[1536,2048]{1,0:T(8,128)(2,1)S(1)}, u32[]{:S(2)}) copy-start(bf16[1536,2048]{1,0:T(8,128)(2,1)S(1)} %get-tuple-element.100.refs_5_) | copy-start | bytes 18874372
  498.3 21.6 %collective-permute-start.10 = (bf16[512,2048]{1,0:T(8,128)(2,1)S(1)}, bf16[512,2048]{1,0:T(8,128)(2,1)}, u32[]{:S(2)}, u32[]{:S(2)}) collective-permute-start(bf16[512,2048]{1,0:T(8,128)(2,1)S(1)} %convolution_convert_fusion.1.refs_11_), channel_id=1, source_target_pairs={{0,2},{2,0},{4,6},{6,4},{8,10},{10,8},{12,14},{14,12},{16,18},{18,... | collective-permute-start | bytes 6291464 | tf_op jit(solution)/shard_map/ppermute | solution.py:1401
  505.1 126.3 %collective-permute-start.12 = (bf16[512,2048]{1,0:T(8,128)(2,1)}, bf16[512,2048]{1,0:T(8,128)(2,1)}, u32[]{:S(2)}, u32[]{:S(2)}) collective-permute-start(bf16[512,2048]{1,0:T(8,128)(2,1)} %add_convert_fusion.1.refs_4_), channel_id=1, source_target_pairs={{0,1},{1,0},{2,3},{3,2},{4,5},{5,4},{6,7},{7,6},{8,9},{9,8},{10,11... | collective-permute-start | bytes 6291464 | tf_op jit(solution)/shard_map/ppermute | solution.py:1398
  519.7 56.7 %collective-permute-start.11 = (bf16[512,2048]{1,0:T(8,128)(2,1)}, bf16[512,2048]{1,0:T(8,128)(2,1)}, u32[]{:S(2)}, u32[]{:S(2)}) collective-permute-start(bf16[512,2048]{1,0:T(8,128)(2,1)} %convolution_convert_fusion.refs_12_), channel_id=1, source_target_pairs={{0,2},{2,0},{4,6},{6,4},{8,10},{10,8},{12,14},{14,12},{16,18},{18,... | collective-permute-start | bytes 6291464 | tf_op jit(solution)/shard_map/ppermute | solution.py:1401
  525.7 105.7 %collective-permute-start.13 = (bf16[512,2048]{1,0:T(8,128)(2,1)}, bf16[512,2048]{1,0:T(8,128)(2,1)}, u32[]{:S(2)}, u32[]{:S(2)}) collective-permute-start(bf16[512,2048]{1,0:T(8,128)(2,1)} %add_convert_fusion.refs_14_), channel_id=1, source_target_pairs={{0,1},{1,0},{2,3},{3,2},{4,5},{5,4},{6,7},{7,6},{8,9},{9,8},{10,11... | collective-permute-start | bytes 6291464 | tf_op jit(solution)/shard_map/ppermute | solution.py:1398
  546.6 37.2 %slice-start = ((s8[4718592]{0:T(1024)(128)(4,1)}), s8[4194304]{0:T(1024)(128)(4,1)S(1)}, s32[]{:S(2)}) async-start(s8[4718592]{0:T(1024)(128)(4,1)} %bitcast.142), calls=%async_computation.3 | async-start | bytes 8388608
  546.6 37.2 %slice-start.1 = ((s8[4718592]{0:T(1024)(128)(4,1)}), s8[524288]{0:T(1024)(128)(4,1)S(1)}, s32[]{:S(2)}) async-start(s8[4718592]{0:T(1024)(128)(4,1)} %bitcast.142), calls=%async_computation.4 | async-start | bytes 1048576
  583.8 45.4 %copy-start.11 = (f32[512,2048]{1,0:T(8,128)}, f32[512,2048]{1,0:T(8,128)S(1)}, u32[]{:S(2)}) copy-start(f32[512,2048]{1,0:T(8,128)S(1)} %convert_add_fusion.refs_10_) | copy-start | bytes 12582916
  583.9 47.5 %copy-start.10 = (f32[512,2048]{1,0:T(8,128)S(1)}, f32[512,2048]{1,0:T(8,128)}, u32[]{:S(2)}) copy-start(f32[512,2048]{1,0:T(8,128)} %convert_add_fusion.1.refs_13_) | copy-start | bytes 12582916
  641.3 118.8 %collective-permute-start.15 = (bf16[2,256,2048]{2,1,0:T(8,128)(2,1)}, bf16[2,256,2048]{2,1,0:T(8,128)(2,1)}, u32[]{:S(2)}, u32[]{:S(2)}) collective-permute-start(bf16[2,256,2048]{2,1,0:T(8,128)(2,1)} %get-tuple-element.112.refs_9_), channel_id=1, source_target_pairs={{0,4},{2,6},{4,0},{6,2},{8,12},{10,14},{12,8},{14,10},{16,20},{18,... | collective-permute-start | bytes 6291464 | tf_op jit(solution)/shard_map/ppermute | solution.py:1401
  676.0 63.9 %slice-start.2 = ((s8[4718592]{0:T(1024)(128)(4,1)}), s8[4194304]{0:T(1024)(128)(4,1)S(1)}, s32[]{:S(2)}) async-start(s8[4718592]{0:T(1024)(128)(4,1)} %bitcast.144), calls=%async_computation.5 | async-start | bytes 8388608
  723.4 16.5 %copy-start.105 = (f32[8,512]{1,0:T(8,128)}, f32[8,512]{1,0:T(8,128)S(1)}, u32[]{:S(2)}) copy-start(f32[8,512]{1,0:T(8,128)S(1)} %get-tuple-element.115.refs_6_) | copy-start | bytes 49156
  744.2 11.0 %copy-start.136 = (f32[1,2048]{1,0:T(1,128)S(1)}, f32[1,2048]{1,0:T(1,128)}, u32[]{:S(2)}) copy-start(f32[1,2048]{1,0:T(1,128)} %slice.236) | copy-start | bytes 24580
  744.2 12.4 %copy-start.135 = (f32[1,2048]{1,0:T(1,128)S(1)}, f32[1,2048]{1,0:T(1,128)}, u32[]{:S(2)}) copy-start(f32[1,2048]{1,0:T(1,128)} %slice.246) | copy-start | bytes 24580
  744.2 12.4 %copy-start.137 = (f32[16,32]{1,0:T(8,128)S(1)}, f32[16,32]{1,0:T(8,128)}, u32[]{:S(2)}) copy-start(f32[16,32]{1,0:T(8,128)} %get-tuple-element.248) | copy-start | bytes 6148
  744.2 12.5 %copy-start.138 = (f32[16,32]{1,0:T(8,128)S(1)}, f32[16,32]{1,0:T(8,128)}, u32[]{:S(2)}) copy-start(f32[16,32]{1,0:T(8,128)} %get-tuple-element.250) | copy-start | bytes 6148
  744.2 12.5 %copy-start.139 = (f32[16,32]{1,0:T(8,128)S(1)}, f32[16,32]{1,0:T(8,128)}, u32[]{:S(2)}) copy-start(f32[16,32]{1,0:T(8,128)} %get-tuple-element.252) | copy-start | bytes 6148
  753.2 95.4 %collective-permute-start.14 = (bf16[1536,512]{1,0:T(8,128)(2,1)}, bf16[1536,512]{1,0:T(8,128)(2,1)}, u32[]{:S(2)}, u32[]{:S(2)}) collective-permute-start(bf16[1536,512]{1,0:T(8,128)(2,1)} %token_pull.2.refs_6_), channel_id=1, source_target_pairs={{0,1},{1,0},{2,3},{3,2},{4,5},{5,4},{6,7},{7,6},{8,9},{9,8},{10,11... | collective-permute-start | bytes 4718600 | tf_op jit(solution)/shard_map/ppermute | solution.py:1398
  (107 other events, 411.8 us)
Sparse Core Ops, SparseCore 0:
  85.1 36.8 all-gather.3
  124.2 49.7 all-gather.5
  176.7 49.3 all-gather.7

commit v9 on v8

--- a/solution.py
+++ b/solution.py
@@ -40,9 +40,6 @@
     return jax.ShapeDtypeStruct(shape, dtype)
 
 
-VMEM_SLACK = 16 * 1024 * 1024
-
-
 class Order:
     last = ()
 
@@ -60,14 +57,6 @@
     size = sum(math.prod(o.shape) * o.dtype.itemsize for o in list(operands) + list(out_shape))
     if flops == 0:
         size = 1024
-    need = VMEM_SLACK
-    for spec, array in zip(list(in_specs) + list(out_specs), list(operands)[prefetch:] + list(out_shape)):
-        if spec.block_shape is not None:
-            block = math.prod(spec.block_shape) * array.dtype.itemsize
-            need += block if spec.pipeline_mode is not None else 2 * block
-    for buffer in scratch:
-        if getattr(buffer, "memory_space", None) == pltpu.VMEM:
-            need += math.prod(buffer.shape) * jnp.dtype(buffer.dtype).itemsize
     outs = pl.pallas_call(
         wrapped,
         grid_spec=pltpu.PrefetchScalarGridSpec(
@@ -79,7 +68,7 @@
         ),
         out_shape=out_shape,
         compiler_params=pltpu.CompilerParams(
-            vmem_limit_bytes=min(VMEM_LIMIT, need), collective_id=remote, has_side_effects=remote is not None
+            vmem_limit_bytes=VMEM_LIMIT, collective_id=remote, has_side_effects=remote is not None
         ),
         cost_estimate=pl.CostEstimate(flops=flops, bytes_accessed=size, transcendentals=0),
         name=name,
@@ -497,6 +486,9 @@
     return late, wide_sum, small_sum.reshape(-1)[:length]
 
 
+QKV_BIAS, UP_BIAS = 6, 9
+
+
 def swap_halves(block):
     lane = lax.broadcasted_iota(jnp.int32, block.shape, 1)
     return jnp.where((lane & 32) == 0, pltpu.roll(block, 96, 1), pltpu.roll(block, 32, 1))
@@ -504,7 +496,7 @@
 
 def qkv_kernel(x_ref, w_ref, b_ref, cos_ref, sin_ref, out_ref):
     which = pl.program_id(0)
-    bias = b_ref[pl.ds(which, 1), :]
+    bias = b_ref[pl.ds(QKV_BIAS + which, 1), :]
 
     @pl.when(which < 2)
     def _():
@@ -679,11 +671,13 @@
 
 
 def up_kernel(x_ref, w_ref, b_ref, active_ref, slope_ref):
-    width = w_ref.shape[1]
-    chunk = min(256, width)
+    width, part = w_ref.shape[1], b_ref.shape[1]
+    chunk = min(256, part)
     for first in range(0, width, chunk):
         at = slice(first, first + chunk)
-        active, slope = gelu_parts(mm(x_ref[...], w_ref[:, at]) + b_ref[:, at])
+        row, lane = UP_BIAS + first // part, first % part
+        bias = b_ref[row : row + 1, lane : lane + chunk]
+        active, slope = gelu_parts(mm(x_ref[...], w_ref[:, at]) + bias)
         active_ref[:, at] = active.astype(BF16)
         slope_ref[:, at] = slope
 
@@ -1410,11 +1404,11 @@
             lax.dynamic_index_in_dim(stacked, (c - j) % C, 0, keepdims=False) for j in range(C)
         ]
 
-    pack = [b_qkv.reshape(-1), b_up, b_out, ln1_gain, ln1_bias, b_down, ln2_gain, ln2_bias]
-    ends = [0]
-    for vector in pack:
-        ends.append(ends[-1] + vector.shape[0])
-    packed = jnp.concatenate(pack)
+    rows_in_order = [b_out, ln1_gain, ln1_bias, b_down, ln2_gain, ln2_bias]
+    packed = jnp.concatenate(
+        [jnp.stack(rows_in_order), b_qkv, b_up.reshape(-1, width)], axis=0
+    )
+    packed = jnp.pad(packed, ((0, 16 - packed.shape[0]), (0, 0)))
 
     def gather_pieces(pieces):
         return [lax.all_gather(piece, "rows", axis=0, tiled=True) for piece in pieces]
@@ -1457,19 +1451,7 @@
     )
     packs = [packed] + [shift_cols(behind[1], k) for k in range(1, C)]
 
-    ordered_packs = in_order(packs)
-
-    def of_slot(which, k):
-        return packs[k][ends[which] : ends[which + 1]]
-
-    def whole(which):
-        return jnp.concatenate([p[ends[which] : ends[which + 1]] for p in ordered_packs])
-
-    bqkv_slots = [of_slot(0, k).reshape(b_qkv.shape) for k in range(C)]
-    bup_slots = [of_slot(1, k)[None, :] for k in range(C)]
-    bout, gain1, bias1, bdown, gain2, bias2 = [whole(which) for which in range(2, 8)]
-    zero_row = jnp.zeros_like(bout)
-    vectors = jnp.stack([bout, gain1, bias1, bdown, gain2, bias2, zero_row, zero_row])
+    vectors = jnp.concatenate([p[:8] for p in in_order(packs)], axis=1)
 
     own_ends = jnp.cumsum(own_sizes)
     share = D // R
@@ -1493,7 +1475,7 @@
     qkv, attended, rests, exts = [], [], [], []
     for k in range(C):
         first = (lows, highs) if k == 0 else ()
-        qkv.append(project_qkv(x, wqkv_slots[k], bqkv_slots[k], cosine, sine, first))
+        qkv.append(project_qkv(x, wqkv_slots[k], packs[k], cosine, sine, first))
         if k == 0:
             flat = jnp.concatenate([piece.reshape(-1, D) for piece in late_pieces])
             flat, _ = lax.optimization_barrier((flat, x))
@@ -1517,7 +1499,7 @@
         rests.append(rest)
         exts.append(ext)
     normed_one, inverse_one, hidden_low, hidden_t = out_and_norm(x, vectors, attended, wout_slots)
-    active, slopes = zip(*[up_and_gelu(hidden_low, wup_slots[k], bup_slots[k]) for k in range(C)])
+    active, slopes = zip(*[up_and_gelu(hidden_low, wup_slots[k], packs[k]) for k in range(C)])
     normed_two, inverse_two, output_low, unit, unit_low, unit_inverse = down_and_norm(
         normed_one, vectors, wproj, active, wdown_slots
     )
@@ -1665,7 +1647,7 @@
     qkv_grad, out_grad = late_grad[:3], late_grad[3]
     down_grad, up_grad = wide_grad
     one = D // (C * R)
-    up_part = bup_slots[0].shape[1] // R
+    up_part = b_up.shape[0] // R
     bounds = [3 * one, 3 * one + up_part]
     for _ in range(6):
         bounds.append(bounds[-1] + one)

time: 871 us -> 806 us (0.925)
  local copies, waits for them, and re-layouts: 195 us -> 51.8 us
  Pallas kernels: 561 us -> 639 us
    unnamed x313 -> x78, local copies, waits for them, and re-layouts: 123 us -> 6.16 us
    pallas_call x27, Pallas kernels: 561 us -> 639 us  [call(): pl.pallas_call(wrapped, grid_spec=pltpu.PrefetchScalarGridSpec(num_scalar...]
  transfers between devices with their start and end apart: 19 -> 19, of which waited for: 2 -> 4; matrix products, arithmetic and copies ran while one was open for 16% -> 12% of each run, Pallas kernels for 52% -> 63%
where the time goes in v9:
time: 806 us; the launch traced here: 797 us
  Pallas kernels  639 us (79%)
  matrix products  56.9 us (7%)
  local copies, waits for them, and re-layouts  51.8 us (6%)
  between operations  15.4 us (2%)
  other arithmetic  13.5 us (2%)
  starting transfers between devices  12 us (1%)
  waiting for transfers between devices  9.2 us (1%)
    pallas_call x27, Pallas kernels, call(): pl.pallas_call(wrapped, grid_spec=pltpu.PrefetchScalarGridSpec(num_scalar...  639 us
    dot_general x9, matrix products, mm(): return lax.dot_general(left, right, dims, preferred_element_type=F32)  56.9 us
  transfers between devices with their start and end apart: 19, of which 4 were waited for; matrix products, arithmetic and copies ran while one was open for 12% of the time, Pallas kernels for 63%

profile of v9, /device:TPU:0, one launch (start us, length us, event | category | flops | bytes accessed | tf_op | source)
XLA Modules:
  0.0 797.3 jit_solution(6532650757957551023)
XLA Ops:
  8.2 3.0 collective-permute-start.1
  11.2 1.2 slice-done
  13.1 1.9 fusion.1
  16.2 1.0 constant_dynamic-slice_fusion.6
  17.3 2.4 copy.72.refs_1_
  20.4 9.2 %prepare.1 = (f32[1536,128]{1,0:T(8,128)}, f32[1536,128]{1,0:T(8,128)}, bf16[1536,128]{1,0:T(8,128)(2,1)}, bf16[1536,128]{1,0:T(8,128)(2,1)}, s32[16,4,1024]{2,1,0:T(4,128)}) custom-call(s32[4]{0:T(128)} %fusion.4.refs_0_, s32[32,64,32]{2,1,0:T(8,128)} %copy.72.refs_1_, s32[64,2]{1,0:T(8,128)} %copy.73.refs_2_), custom_call_target="tpu_custom_call" | custom-call | bytes 1024 | tf_op jit(solution)/shard_map/prepare/pallas_call | solution.py:60
  30.5 1.0 dynamic-slice_bitcast_fusion.1
  32.2 26.9 %gather_rows.2.refs_3_ = bf16[16,192,512]{2,1,0:T(8,128)(2,1)} custom-call(bf16[192,512]{1,0:T(8,128)(2,1)} %copy-done.15, s32[16,4,1024]{2,1,0:T(4,128)} %get-tuple-element.70.refs_1_.refs_4_), custom_call_target="tpu_custom_call" | custom-call | bytes 1024 | tf_op jit(solution)/shard_map/gather_rows/pallas_call | solution.py:60
  59.2 1.1 copy-done.7
  60.4 14.9 %join.1.refs_0_.refs_7_ = bf16[1536,1024]{1,0:T(8,128)(2,1)} custom-call(s32[1]{0:T(128)} %bitcast.3.refs_0_, bf16[1536,512]{1,0:T(8,128)(2,1)} %get-tuple-element.216.refs_1_, bf16[1536,512]{1,0:T(8,128)(2,1)} %copy-done.7, bf16[16,192,512]{2,1,0:T(8,128)(2,1)} %gather_rows.2.refs_3_), custom_call_target="tpu_custom_call" | custom-call | bytes 1024 | tf_op jit(solution)/shard_map/join/pallas_call | solution.py:60
  75.2 1.5 collective-permute-start.3
  79.0 9.8 %project_qkv.2.refs_1_ = bf16[3,1536,512]{2,1,0:T(8,128)(2,1)} custom-call(bf16[1536,1024]{1,0:T(8,128)(2,1)} %join.1.refs_0_.refs_7_, bf16[3,1024,512]{2,1,0:T(8,128)(2,1)} %refs_4_.5, f32[16,512]{1,0:T(8,128)} %pad.8.refs_2_, f32[1536,128]{1,0:T(8,128)} %get-tuple-element.72.refs_3_.refs_7_, f32[1536,128]{1,0:T(8,128)} %get-tuple-element.73.refs_4_.refs_8_, ...), custom_call_target="tpu_custom_call" | custom-call | flops 4831838208 | bytes 12615680 | tf_op jit(solution)/shard_map/project_qkv/pallas_call | solution.py:60
  88.8 2.0 collective-permute-done.3.refs_0_
  91.7 1.9 pass_on.1.refs_4_
  93.7 1.5 slice.203
  95.2 1.8 fusion.13
  99.0 1.6 collective-permute-start.2
  103.6 3.3 collective-permute-done.4
  107.7 32.8 %attention_forward.2 = (bf16[1536,512]{1,0:T(8,128)(2,1)}, bf16[1536,512]{1,0:T(8,128)(2,1)}, bf16[1536,512]{1,0:T(8,128)(2,1)}) custom-call(s32[12]{0:T(128)} %pad_add_fusion.1.refs_0_, bf16[3,1536,512]{2,1,0:T(8,128)(2,1)} %project_qkv.2.refs_1_, bf16[1536,128]{1,0:T(8,128)(2,1)} %get-tuple-element.74.refs_2_.refs_6_, ...), custom_call_target="tpu_custom_call" | custom-call | bytes 1024 | tf_op jit(solution)/shard_map/attention_forward/pallas_call | solution.py:60
  140.5 10.0 %project_qkv.3.refs_1_.refs_4_ = bf16[3,1536,512]{2,1,0:T(8,128)(2,1)} custom-call(bf16[1536,1024]{1,0:T(8,128)(2,1)} %join.1.refs_0_.refs_7_, bf16[3,1024,512]{2,1,0:T(8,128)(2,1)} %bitcast.137, f32[16,512]{1,0:T(8,128)} %copy-done.19, f32[1536,128]{1,0:T(8,128)} %get-tuple-element.72.refs_3_.refs_7_, f32[1536,128]{1,0:T(8,128)} %get-tuple-element.73.refs_4_.refs_8_, ...), custom_call_target="tpu_custom_call" | custom-call | flops 4831838208 | bytes 12615680 | tf_op jit(solution)/shard_map/project_qkv/pallas_call | solution.py:60
  150.5 33.0 %attention_forward.3 = (bf16[1536,512]{1,0:T(8,128)(2,1)}, bf16[1536,512]{1,0:T(8,128)(2,1)}, bf16[1536,512]{1,0:T(8,128)(2,1)}) custom-call(s32[12]{0:T(128)} %pad_add_fusion.1.refs_0_, bf16[3,1536,512]{2,1,0:T(8,128)(2,1)} %project_qkv.3.refs_1_.refs_4_, bf16[1536,128]{1,0:T(8,128)(2,1)} %get-tuple-element.74.refs_2_.refs_6_, ...), custom_call_target="tpu_custom_call" | custom-call | bytes 1024 | tf_op jit(solution)/shard_map/attention_forward/pallas_call | solution.py:60
  183.5 11.3 %out_and_norm.1 = (f32[1536,1024]{1,0:T(8,128)}, f32[1536,1]{1,0:T(8,128)}, bf16[1536,1024]{1,0:T(8,128)(2,1)}, bf16[1024,1536]{1,0:T(8,128)(2,1)}) custom-call(bf16[1536,1024]{1,0:T(8,128)(2,1)} %join.1.refs_0_.refs_7_, f32[8,1024]{1,0:T(8,128)} %pad_maximum_fusion.4.refs_1_.refs_6_.refs_3_, ...), custom_call_target="tpu_custom_call" | custom-call | flops 3221225472 | bytes 21010432 | tf_op jit(solution)/shard_map/out_and_norm/pallas_call | solution.py:60
  194.8 23.0 %up_and_gelu.2 = (bf16[1536,2048]{1,0:T(8,128)(2,1)}, f32[1536,2048]{1,0:T(8,128)}) custom-call(bf16[1536,1024]{1,0:T(8,128)(2,1)} %get-tuple-element.81.refs_0_, bf16[1024,2048]{1,0:T(8,128)(2,1)} %refs_6_.1, f32[16,512]{1,0:T(8,128)} %pad.8.refs_2_, f32[1536,1]{1,0:T(8,128)} %get-tuple-element.82.refs_3_.refs_2_), custom_call_target="tpu_custom_call" | custom-call | flops 16106127360 | bytes 26247168 | tf_op jit(solution)/shard_map/up_and_gelu/pallas_call | solution.py:60
  217.7 22.6 %up_and_gelu.3 = (bf16[1536,2048]{1,0:T(8,128)(2,1)}, f32[1536,2048]{1,0:T(8,128)}) custom-call(bf16[1536,1024]{1,0:T(8,128)(2,1)} %get-tuple-element.81.refs_0_, bf16[1024,2048]{1,0:T(8,128)(2,1)} %all-gather.6.cloned.1.call-done.refs_1_.refs_7_, f32[16,512]{1,0:T(8,128)} %copy-done.19, bf16[1536,2048]{1,0:T(8,128)(2,1)} %get-tuple-element.83.refs_3_), custom_call_target="tpu_custom_call" | custom-call | flops 16106127360 | bytes 26247168 | tf_op jit(solution)/shard_map/up_and_gelu/pallas_call | solution.py:60
  240.3 24.8 %down_and_norm.1 = (f32[1536,1024]{1,0:T(8,128)}, f32[1536,1]{1,0:T(8,128)}, bf16[1536,1024]{1,0:T(8,128)(2,1)}, f32[1536,128]{1,0:T(8,128)}, bf16[1536,128]{1,0:T(8,128)(2,1)}, /*index=5*/f32[1536,1]{1,0:T(8,128)}) custom-call(f32[1536,1024]{1,0:T(8,128)} %get-tuple-element.79.refs_0_.refs_1_, f32[8,1024]{1,0:T(8,128)} %pad_maximum_fusion.4.refs_1_.refs_6_.refs_3_, ...), custom_call_target="tpu_custom_call" | custom-call | flops 12884901888 | bytes 38187008 | tf_op jit(solution)/shard_map/down_and_norm/pallas_call | solution.py:60
  266.1 1.7 slice.169.refs_0_
  267.8 29.4 %gather_rows.3.refs_5_ = bf16[16,1024,128]{2,1,0:T(8,128)(2,1)} custom-call(bf16[1024,128]{1,0:T(8,128)(2,1)} %slice.169.refs_0_, f32[1536,1]{1,0:T(8,128)} %get-tuple-element.86.refs_1_.refs_5_), custom_call_target="tpu_custom_call" | custom-call | bytes 1024 | tf_op jit(solution)/shard_map/gather_rows/pallas_call | solution.py:60
  298.8 34.3 %score_forward.1.refs_6_ = f32[64,32]{1,0:T(8,128)} custom-call(s32[512]{0:T(512)} %reshape.233.refs_5_.refs_0_, s32[512]{0:T(512)} %sub.97.refs_6_.refs_1_, bf16[16384,128]{1,0:T(8,128)(2,1)} %bitcast.152, bf16[1024,128]{1,0:T(8,128)(2,1)} %pad_maximum_fusion.3.refs_3_, s32[16,4,1024]{2,1,0:T(4,128)} %get-tuple-element.70.refs_1_.refs_4_, ...), custom_call_target="tpu_custom_call" | custom-call | flops 4294967296 | bytes 4730880 | tf_op jit(solution)/shard_map/score_forward/pallas_call | solution.py:60
  334.7 1.1 collective-permute-start.6
  335.8 2.6 collective-permute-done.6
  338.9 1.4 subtract_multiply_fusion.refs_5_
  340.3 34.7 %score_backward.1 = (f32[16384,128]{1,0:T(8,128)}, f32[128,1024]{1,0:T(8,128)}) custom-call(s32[512]{0:T(512)} %reshape.233.refs_5_.refs_0_, s32[512]{0:T(512)} %sub.97.refs_6_.refs_1_, bf16[16384,128]{1,0:T(8,128)(2,1)} %bitcast.153, bf16[1024,128]{1,0:T(8,128)(2,1)} %pad_maximum_fusion.3.refs_3_, s32[16,4,1024]{2,1,0:T(4,128)} %get-tuple-element.70.refs_1_.refs_4_, ...), custom_call_target="tpu_custom_call" | custom-call | flops 8589934592 | bytes 13643776 | tf_op jit(solution)/shard_map/score_backward/pallas_call | solution.py:60
  375.0 2.0 copy.78
  377.0 1.0 dynamic-slice_bitcast_fusion
  378.0 1.1 collective-permute-start.7
  379.1 1.9 constant_dynamic-slice_fusion.2
  381.0 40.2 %scatter_rows.1.refs_7_ = f32[1024,128]{1,0:T(8,128)} custom-call(f32[16,1024,128]{2,1,0:T(8,128)} %bitcast.144, f32[128,1024]{1,0:T(8,128)} %get-tuple-element.87.refs_1_), custom_call_target="tpu_custom_call" | custom-call | bytes 1024 | tf_op jit(solution)/shard_map/scatter_rows/pallas_call | solution.py:60
  421.2 2.0 pad_maximum_fusion.refs_0_
  423.2 12.3 %head_pull.1 = (bf16[1536,128]{1,0:T(8,128)(2,1)}, f32[1536,1024]{1,0:T(8,128)}, bf16[1536,1024]{1,0:T(8,128)(2,1)}, bf16[1024,1536]{1,0:T(8,128)(2,1)}, f32[8,1024]{1,0:T(8,128)}) custom-call(f32[1536,128]{1,0:T(8,128)} %pad_maximum_fusion.refs_0_, f32[1536,128]{1,0:T(8,128)} %get-tuple-element.89.refs_1_, f32[1536,1]{1,0:T(8,128)} %get-tuple-element.90.refs_2_, ...), custom_call_target="tpu_custom_call" | custom-call | flops 805306368 | bytes 21180416 | tf_op jit(solution)/shard_map/head_pull/pallas_call | solution.py:60
  435.5 2.3 constant_dynamic-slice_fusion.4
  437.9 7.0 convolution_convert_fusion.3.refs_4_
  445.1 4.6 convolution_convert_fusion.2.refs_5_
  450.1 13.7 %up_pull.2 = (bf16[1536,2048]{1,0:T(8,128)(2,1)}, f32[8,2048]{1,0:T(8,128)}) custom-call(bf16[1536,1024]{1,0:T(8,128)(2,1)} %get-tuple-element.93.refs_0_, bf16[2048,1024]{1,0:T(8,128)(2,1)} %all-gather.8.cloned.1.call-done.refs_6_.refs_1_, f32[1536,2048]{1,0:T(8,128)} %get-tuple-element.95.refs_2_, f32[8,1024]{1,0:T(8,128)} %get-tuple-element.96.refs_3_, ...), custom_call_target="tpu_custom_call" | custom-call | flops 6442450944 | bytes 26279936 | tf_op jit(solution)/shard_map/up_pull/pallas_call | solution.py:60
  463.8 6.4 convolution_convert_fusion.1.refs_11_
  470.4 8.3 %add_convert_fusion.1.refs_4_ = bf16[512,2048]{1,0:T(8,128)(2,1)} fusion(bf16[512,2048]{1,0:T(8,128)(2,1)} %collective-permute-done.8, bf16[512,1536]{1,0:T(8,128)(2,1)S(1)} %bitcast.163, bf16[1536,2048]{1,0:T(8,128)(2,1)} %get-tuple-element.84.refs_4_.refs_7_), kind=kOutput, calls=%fused_computation.3 | convolution fusion | flops 3224371200 | bytes 12058624 | tf_op jit(solution)/shard_map/dot_general | solution.py:23
  479.2 13.7 %up_pull.3 = (bf16[1536,2048]{1,0:T(8,128)(2,1)}, f32[8,2048]{1,0:T(8,128)}) custom-call(bf16[1536,1024]{1,0:T(8,128)(2,1)} %get-tuple-element.93.refs_0_, bf16[2048,1024]{1,0:T(8,128)(2,1)} %refs_1_.6, f32[1536,2048]{1,0:T(8,128)} %get-tuple-element.94.refs_2_, f32[8,2048]{1,0:T(8,128)} %get-tuple-element.98.refs_3_, ...), custom_call_target="tpu_custom_call" | custom-call | flops 6442450944 | bytes 26279936 | tf_op jit(solution)/shard_map/up_pull/pallas_call | solution.py:60
  492.9 8.0 %convolution_convert_fusion.refs_12_ = bf16[512,2048]{1,0:T(8,128)(2,1)} fusion(bf16[512,1536]{1,0:T(8,128)(2,1)S(1)} %bitcast.166, bf16[1536,2048]{1,0:T(8,128)(2,1)} %get-tuple-element.99.refs_4_), kind=kOutput, calls=%fused_computation.8 | convolution fusion | flops 3222274048 | bytes 9961472 | tf_op jit(solution)/shard_map/dot_general | solution.py:23
  501.0 6.1 add_convert_fusion.refs_14_
  507.1 1.4 collective-permute-start.13
  509.1 3.0 copy.76
  514.2 9.5 %convert_add_fusion.1.refs_13_ = f32[512,2048]{1,0:T(8,128)} fusion(bf16[512,2048]{1,0:T(8,128)(2,1)} %collective-permute-done.9, bf16[512,1536]{1,0:T(8,128)(2,1)} %bitcast.164, bf16[1536,2048]{1,0:T(8,128)(2,1)} %get-tuple-element.83.refs_3_), kind=kOutput, calls=%fused_computation.2 | convolution fusion | flops 3223322624 | bytes 14155776 | tf_op jit(solution)/shard_map/dot_general | solution.py:23
  523.7 29.5 %hidden_pull.1 = (f32[1536,1024]{1,0:T(8,128)}, bf16[1024,1536]{1,0:T(8,128)(2,1)}, f32[8,1024]{1,0:T(8,128)}, bf16[1536,512]{1,0:T(8,128)(2,1)}, bf16[1536,512]{1,0:T(8,128)(2,1)}) custom-call(f32[1536,1024]{1,0:T(8,128)} %get-tuple-element.92.refs_0_, f32[1536,1024]{1,0:T(8,128)} %get-tuple-element.79.refs_0_.refs_1_, ...), custom_call_target="tpu_custom_call" | custom-call | bytes 1024 | tf_op jit(solution)/shard_map/hidden_pull/pallas_call | solution.py:60
  553.3 6.4 convert_add_fusion.refs_10_
  559.7 46.3 %attention_backward.2 = (bf16[3,1536,512]{2,1,0:T(8,128)(2,1)}, f32[8,512]{1,0:T(8,128)}) custom-call(s32[12]{0:T(128)} %pad_add_fusion.1.refs_0_, bf16[3,1536,512]{2,1,0:T(8,128)(2,1)} %project_qkv.3.refs_1_.refs_4_, bf16[1536,512]{1,0:T(8,128)(2,1)} %get-tuple-element.107.refs_2_, bf16[1536,512]{1,0:T(8,128)(2,1)} %get-tuple-element.78.refs_3_.refs_6_.refs_5_, ...), custom_call_target="tpu_custom_call" | custom-call | bytes 1024 | tf_op jit(solution)/shard_map/attention_backward/pallas_call | solution.py:60
  606.0 8.8 %fold.1 = (bf16[2,256,2048]{2,1,0:T(8,128)(2,1)}, f32[2,256,2048]{2,1,0:T(8,128)}) custom-call(s32[1]{0:T(128)} %bitcast.43.refs_0_, f32[1,512,2048]{2,1,0:T(8,128)} %bitcast.140, f32[1,512,2048]{2,1,0:T(8,128)} %bitcast.141, bf16[1,512,2048]{2,1,0:T(8,128)(2,1)} %bitcast.46.refs_3_, bf16[1,512,2048]{2,1,0:T(8,128)(2,1)} %bitcast.47.refs_4_, ...), custom_call_target="tpu_custom_call" | custom-call | bytes 1024 | tf_op jit(solution)/shard_map/fold/pallas_call | solution.py:60
  619.0 46.8 %attention_backward.3 = (bf16[3,1536,512]{2,1,0:T(8,128)(2,1)}, f32[8,512]{1,0:T(8,128)}) custom-call(s32[12]{0:T(128)} %pad_add_fusion.1.refs_0_, bf16[3,1536,512]{2,1,0:T(8,128)(2,1)} %project_qkv.2.refs_1_, bf16[1536,512]{1,0:T(8,128)(2,1)} %get-tuple-element.104.refs_2_, bf16[1536,512]{1,0:T(8,128)(2,1)} %get-tuple-element.77.refs_5_.refs_2_.refs_3_.refs_4_, ...), custom_call_target="tpu_custom_call" | custom-call | bytes 1024 | tf_op jit(solution)/shard_map/attention_backward/pallas_call | solution.py:60
  665.7 10.9 %token_pull.2.refs_6_ = bf16[1536,512]{1,0:T(8,128)(2,1)} custom-call(s32[1]{0:T(128)} %bitcast.48.refs_0_, f32[1536,1024]{1,0:T(8,128)} %get-tuple-element.103.refs_1_, bf16[3,1536,512]{2,1,0:T(8,128)(2,1)} %get-tuple-element.113.refs_2_, bf16[3,1536,512]{2,1,0:T(8,128)(2,1)} %get-tuple-element.114.refs_3_, bf16[3,1024,512]{2,1,0:T(8,128)(2,1)} %refs_4_.5, ...), custom_call_target="tpu_custom_call" | custom-call | bytes 1024 | tf_op jit(solution)/shard_map/token_pull/pallas_call | solution.py:60
  676.7 11.6 %token_pull.3.refs_9_.refs_1_ = f32[1536,512]{1,0:T(8,128)} custom-call(s32[1]{0:T(128)} %bitcast.3.refs_0_, f32[1536,1024]{1,0:T(8,128)} %get-tuple-element.103.refs_1_, bf16[3,1536,512]{2,1,0:T(8,128)(2,1)} %get-tuple-element.113.refs_2_, bf16[3,1536,512]{2,1,0:T(8,128)(2,1)} %get-tuple-element.114.refs_3_, bf16[3,1024,512]{2,1,0:T(8,128)(2,1)} %refs_4_.5, ...), custom_call_target="tpu_custom_call" | custom-call | bytes 1024 | tf_op jit(solution)/shard_map/token_pull/pallas_call | solution.py:60
  692.6 1.4 reshape.263.refs_8_
  694.0 78.4 %late_sums.1 = (f32[4,64,512]{2,1,0:T(8,128)}, f32[2,64,2048]{2,1,0:T(8,128)}, f32[8,640]{1,0:T(8,128)}) custom-call(bf16[8,2,64,1536]{3,2,1,0:T(8,128)(2,1)} %bitcast.154, bf16[8,2,64,1536]{3,2,1,0:T(8,128)(2,1)} %bitcast.193, bf16[3,1536,512]{2,1,0:T(8,128)(2,1)} %get-tuple-element.113.refs_2_, bf16[3,1536,512]{2,1,0:T(8,128)(2,1)} %get-tuple-element.114.refs_3_, ...), custom_call_target="tpu_custom_call" | custom-call | flops 99999997952 | bytes 27414528 | tf_op jit(solution)/shard_map/late_sums/pallas_call | solution.py:60
  776.4 1.8 slice.188
  778.7 1.6 slice_bitcast_fusion.2
  780.3 2.3 slice_bitcast_fusion
  782.6 8.0 assemble.1
  (207 shorter events, 35.2 us)
Async XLA Ops:
  7.2 176.3 %all-gather.4.cloned.1.call-start = ((), (), s32[]{:S(2)}) async-start(), calls=%async_computation | async-start | bytes 1114112 | tf_op jit(solution)/shard_map/all_gather | solution.py:1414
  8.2 23.4 %collective-permute-start.1 = (bf16[192,512]{1,0:T(8,128)(2,1)S(1)}, bf16[192,512]{1,0:T(8,128)(2,1)S(1)}, u32[]{:S(2)}, u32[]{:S(2)}) collective-permute-start(bf16[192,512]{1,0:T(8,128)(2,1)S(1)} %dynamic-slice_bitcast_fusion.2), channel_id=1, source_target_pairs={{0,1},{1,0},{2,3},{3,2},{4,5},{5,4},{6,7},{7,6},{8,9},{9,8},{10,11... | collective-permute-start | bytes 589832 | tf_op jit(solution)/shard_map/ppermute | solution.py:1392
  11.2 1.2 slice-start
  11.2 1.9 slice-start.1
  13.1 1.9 copy-start.18
  15.0 44.1 %collective-permute-start = (bf16[1536,512]{1,0:T(8,128)(2,1)}, bf16[1536,512]{1,0:T(8,128)(2,1)S(1)}, u32[]{:S(2)}, u32[]{:S(2)}) collective-permute-start(bf16[1536,512]{1,0:T(8,128)(2,1)} %get-tuple-element.215), channel_id=1, source_target_pairs={{0,1},{1,0},{2,3},{3,2},{4,5},{5,4},{6,7},{7,6},{8,9},{9,8},{10,11... | collective-permute-start | bytes 4718600 | tf_op jit(solution)/shard_map/ppermute | solution.py:1392
  31.6 0.7 copy-start.15
  59.2 1.1 copy-start.7
  60.3 17.8 %copy-start.21 = (f32[2048]{0:T(1024)S(1)}, f32[2048]{0:T(1024)}, u32[]{:S(2)}) copy-start(f32[2048]{0:T(1024)} %param.30) | copy-start | bytes 24580
  60.3 17.9 %copy-start.20 = (f32[3,512]{1,0:T(4,128)S(1)}, f32[3,512]{1,0:T(4,128)}, u32[]{:S(2)}) copy-start(f32[3,512]{1,0:T(4,128)} %param.24) | copy-start | bytes 18436
  60.3 17.9 %copy-start.23 = (f32[512]{0:T(512)S(1)}, f32[512]{0:T(512)}, u32[]{:S(2)}) copy-start(f32[512]{0:T(512)} %param.26) | copy-start | bytes 6148
  60.3 17.9 %copy-start.24 = (f32[512]{0:T(512)S(1)}, f32[512]{0:T(512)}, u32[]{:S(2)}) copy-start(f32[512]{0:T(512)} %param.27) | copy-start | bytes 6148
  60.3 17.9 %copy-start.25 = (f32[512]{0:T(512)S(1)}, f32[512]{0:T(512)}, u32[]{:S(2)}) copy-start(f32[512]{0:T(512)} %param.28) | copy-start | bytes 6148
  60.3 17.9 %copy-start.26 = (f32[512]{0:T(512)S(1)}, f32[512]{0:T(512)}, u32[]{:S(2)}) copy-start(f32[512]{0:T(512)} %param.32) | copy-start | bytes 6148
  60.3 17.9 %copy-start.27 = (f32[512]{0:T(512)S(1)}, f32[512]{0:T(512)}, u32[]{:S(2)}) copy-start(f32[512]{0:T(512)} %param.33) | copy-start | bytes 6148
  60.3 17.9 %copy-start.28 = (f32[512]{0:T(512)S(1)}, f32[512]{0:T(512)}, u32[]{:S(2)}) copy-start(f32[512]{0:T(512)} %param.34) | copy-start | bytes 6148
  75.2 15.7 %collective-permute-start.3 = (bf16[288,1024]{1,0:T(8,128)(2,1)S(1)}, bf16[288,1024]{1,0:T(8,128)(2,1)S(1)}, u32[]{:S(2)}, u32[]{:S(2)}) collective-permute-start(bf16[288,1024]{1,0:T(8,128)(2,1)S(1)} %pad_maximum_fusion.1), channel_id=1, source_target_pairs={{0,1},{1,0},{2,3},{3,2},{4,5},{5,4},{6,7},{7,6},{8,9},{9,8},{10,11... | collective-permute-start | bytes 1769480 | tf_op jit(solution)/shard_map/ppermute | solution.py:1392
  88.8 9.7 %copy-start.22 = (s32[4]{0:T(128)S(1)}, s32[4]{0:T(128)}, u32[]{:S(2)}) copy-start(s32[4]{0:T(128)} %fusion.4.refs_0_) | copy-start | bytes 52
  88.8 10.1 %copy-start.30 = (s32[6]{0:T(128)S(1)}, s32[6]{0:T(128)}, u32[]{:S(2)}) copy-start(s32[6]{0:T(128)} %constant.238) | copy-start | bytes 76
  88.8 10.2 %copy-start.17 = (f32[16,512]{1,0:T(8,128)S(1)}, f32[16,512]{1,0:T(8,128)}, u32[]{:S(2)}) copy-start(f32[16,512]{1,0:T(8,128)} %pad.8.refs_2_) | copy-start | bytes 98308
  88.8 13.0 %copy-start.16 = (bf16[512,128]{1,0:T(8,128)(2,1)S(1)}, bf16[512,128]{1,0:T(8,128)(2,1)}, u32[]{:S(2)}) copy-start(bf16[512,128]{1,0:T(8,128)(2,1)} %param.35) | copy-start | bytes 393220
  90.9 0.8 copy-start.13
  95.2 122.6 %all-gather.6.cloned.1.call-start = ((), (), s32[]{:S(2)}) async-start(), calls=%async_computation.1 | async-start | bytes 4456448 | tf_op jit(solution)/shard_map/all_gather | solution.py:1414
  97.8 142.5 %all-gather.8.cloned.1.call-start = ((), (), s32[]{:S(2)}) async-start(), calls=%async_computation.2 | async-start | bytes 4456448 | tf_op jit(solution)/shard_map/all_gather | solution.py:1414
  99.0 4.0 collective-permute-start.2
  101.9 5.0 collective-permute-start.4
  103.0 37.5 %copy-start.19 = (f32[16,512]{1,0:T(8,128)}, f32[16,512]{1,0:T(8,128)S(1)}, u32[]{:S(2)}) copy-start(f32[16,512]{1,0:T(8,128)S(1)} %collective-permute-done.2.refs_2_) | copy-start | bytes 98308
  240.3 25.8 %copy-start.29 = (s32[32]{0:T(128)S(1)}, s32[32]{0:T(128)}, u32[]{:S(2)}) copy-start(s32[32]{0:T(128)} %param.22) | copy-start | bytes 388
  266.0 31.1 %collective-permute-start.5 = (bf16[512,128]{1,0:T(8,128)(2,1)S(1)}, bf16[512,128]{1,0:T(8,128)(2,1)S(1)}, u32[]{:S(2)}, u32[]{:S(2)}) collective-permute-start(bf16[512,128]{1,0:T(8,128)(2,1)S(1)} %slice.170), channel_id=1, source_target_pairs={{0,1},{1,0},{2,3},{3,2},{4,5},{5,4},{6,7},{7,6},{8,9},{9,8},{10,11... | collective-permute-start | bytes 393224 | tf_op jit(solution)/shard_map/ppermute | solution.py:1392
  334.7 3.6 collective-permute-start.6
  340.3 38.8 %copy-start.3 = (bf16[1024,1536]{1,0:T(8,128)(2,1)S(1)}, bf16[1024,1536]{1,0:T(8,128)(2,1)}, u32[]{:S(2)}) copy-start(bf16[1024,1536]{1,0:T(8,128)(2,1)} %get-tuple-element.102) | copy-start | bytes 9437188
  378.0 43.2 %collective-permute-start.7 = (f32[512,128]{1,0:T(8,128)S(1)}, f32[512,128]{1,0:T(8,128)S(1)}, u32[]{:S(2)}, u32[]{:S(2)}) collective-permute-start(f32[512,128]{1,0:T(8,128)S(1)} %dynamic-slice_bitcast_fusion), channel_id=1, source_target_pairs={{0,1},{1,0},{2,3},{3,2},{4,5},{5,4},{6,7},{7,6},{8,9},{9,8},{10,11... | collective-permute-start | bytes 786440 | tf_op jit(solution)/shard_map/ppermute | solution.py:1392
  381.0 40.2 %copy-start.6 = (f32[1024,128]{1,0:T(8,128)S(1)}, f32[1024,128]{1,0:T(8,128)}, u32[]{:S(2)}) copy-start(f32[1024,128]{1,0:T(8,128)} %copy.78) | copy-start | bytes 1572868
  435.5 9.6 %slice-start.6 = ((s8[6291456]{0:T(1024)(128)(4,1)}), s8[4194304]{0:T(1024)(128)(4,1)S(1)}, s32[]{:S(2)}) async-start(s8[6291456]{0:T(1024)(128)(4,1)} %bitcast.194), calls=%async_computation.9 | async-start | bytes 8388608
  437.8 32.5 %copy-start.10 = (bf16[8,1,64,1536]{3,2,1,0:T(8,128)(2,1)}, bf16[8,1,64,1536]{3,2,1,0:T(8,128)(2,1)S(1)}, u32[]{:S(2)}) copy-start(bf16[8,1,64,1536]{3,2,1,0:T(8,128)(2,1)S(1)} %get-tuple-element.213) | copy-start | bytes 4718596
  437.9 7.2 slice-start.7
  444.9 4.8 copy-start.5
  444.9 25.5 %collective-permute-start.8 = (bf16[512,2048]{1,0:T(8,128)(2,1)S(1)}, bf16[512,2048]{1,0:T(8,128)(2,1)}, u32[]{:S(2)}, u32[]{:S(2)}) collective-permute-start(bf16[512,2048]{1,0:T(8,128)(2,1)S(1)} %convolution_convert_fusion.3.refs_4_), channel_id=1, source_target_pairs={{0,2},{2,0},{4,6},{6,4},{8,10},{10,8},{12,14},{14,12},{16,18},{18,... | collective-permute-start | bytes 6291464 | tf_op jit(solution)/shard_map/ppermute | solution.py:1395
  449.7 64.5 %collective-permute-start.9 = (bf16[512,2048]{1,0:T(8,128)(2,1)}, bf16[512,2048]{1,0:T(8,128)(2,1)}, u32[]{:S(2)}, u32[]{:S(2)}) collective-permute-start(bf16[512,2048]{1,0:T(8,128)(2,1)} %convolution_convert_fusion.2.refs_5_), channel_id=1, source_target_pairs={{0,2},{2,0},{4,6},{6,4},{8,10},{10,8},{12,14},{14,12},{16,18},{18,... | collective-permute-start | bytes 6291464 | tf_op jit(solution)/shard_map/ppermute | solution.py:1395
  450.1 13.7 %copy-start.11 = (bf16[8,1,64,1536]{3,2,1,0:T(8,128)(2,1)S(1)}, bf16[8,1,64,1536]{3,2,1,0:T(8,128)(2,1)}, u32[]{:S(2)}) copy-start(bf16[8,1,64,1536]{3,2,1,0:T(8,128)(2,1)} %get-tuple-element.212) | copy-start | bytes 4718596
  470.2 8.5 %copy-start.4 = (bf16[512,2048]{1,0:T(8,128)(2,1)}, bf16[512,2048]{1,0:T(8,128)(2,1)S(1)}, u32[]{:S(2)}) copy-start(bf16[512,2048]{1,0:T(8,128)(2,1)S(1)} %convolution_convert_fusion.1.refs_11_) | copy-start | bytes 6291460
  470.2 30.8 %collective-permute-start.10 = (bf16[512,2048]{1,0:T(8,128)(2,1)S(1)}, bf16[512,2048]{1,0:T(8,128)(2,1)}, u32[]{:S(2)}, u32[]{:S(2)}) collective-permute-start(bf16[512,2048]{1,0:T(8,128)(2,1)S(1)} %convolution_convert_fusion.1.refs_11_), channel_id=1, source_target_pairs={{0,2},{2,0},{4,6},{6,4},{8,10},{10,8},{12,14},{14,12},{16,18},{18,... | collective-permute-start | bytes 6291464 | tf_op jit(solution)/shard_map/ppermute | solution.py:1395
  478.7 127.3 %collective-permute-start.12 = (bf16[512,2048]{1,0:T(8,128)(2,1)}, bf16[512,2048]{1,0:T(8,128)(2,1)}, u32[]{:S(2)}, u32[]{:S(2)}) collective-permute-start(bf16[512,2048]{1,0:T(8,128)(2,1)} %add_convert_fusion.1.refs_4_), channel_id=1, source_target_pairs={{0,1},{1,0},{2,3},{3,2},{4,5},{5,4},{6,7},{7,6},{8,9},{9,8},{10,11... | collective-permute-start | bytes 6291464 | tf_op jit(solution)/shard_map/ppermute | solution.py:1392
  479.2 21.7 %slice-start.2 = ((s8[6291456]{0:T(1024)(128)(4,1)}), s8[2097152]{0:T(1024)(128)(4,1)S(1)}, s32[]{:S(2)}) async-start(s8[6291456]{0:T(1024)(128)(4,1)} %bitcast.147), calls=%async_computation.5 | async-start | bytes 4194304
  492.9 8.0 %slice-start.3 = ((s8[6291456]{0:T(1024)(128)(4,1)}), s8[4194304]{0:T(1024)(128)(4,1)S(1)}, s32[]{:S(2)}) async-start(s8[6291456]{0:T(1024)(128)(4,1)} %bitcast.147), calls=%async_computation.6 | async-start | bytes 8388608
  492.9 8.0 %copy-start.8 = (bf16[8,1,64,1536]{3,2,1,0:T(8,128)(2,1)S(1)}, bf16[8,1,64,1536]{3,2,1,0:T(8,128)(2,1)}, u32[]{:S(2)}) copy-start(bf16[8,1,64,1536]{3,2,1,0:T(8,128)(2,1)} %get-tuple-element.211) | copy-start | bytes 4718596
  501.0 52.3 %collective-permute-start.11 = (bf16[512,2048]{1,0:T(8,128)(2,1)}, bf16[512,2048]{1,0:T(8,128)(2,1)}, u32[]{:S(2)}, u32[]{:S(2)}) collective-permute-start(bf16[512,2048]{1,0:T(8,128)(2,1)} %convolution_convert_fusion.refs_12_), channel_id=1, source_target_pairs={{0,2},{2,0},{4,6},{6,4},{8,10},{10,8},{12,14},{14,12},{16,18},{18,... | collective-permute-start | bytes 6291464 | tf_op jit(solution)/shard_map/ppermute | solution.py:1395
  501.0 8.1 %copy-start = (bf16[1536,1024]{1,0:T(8,128)(2,1)S(1)}, bf16[1536,1024]{1,0:T(8,128)(2,1)}, u32[]{:S(2)}) copy-start(bf16[1536,1024]{1,0:T(8,128)(2,1)} %join.1.refs_0_.refs_7_) | copy-start | bytes 9437188
  507.1 98.9 %collective-permute-start.13 = (bf16[512,2048]{1,0:T(8,128)(2,1)}, bf16[512,2048]{1,0:T(8,128)(2,1)}, u32[]{:S(2)}, u32[]{:S(2)}) collective-permute-start(bf16[512,2048]{1,0:T(8,128)(2,1)} %add_convert_fusion.refs_14_), channel_id=1, source_target_pairs={{0,1},{1,0},{2,3},{3,2},{4,5},{5,4},{6,7},{7,6},{8,9},{9,8},{10,11... | collective-permute-start | bytes 6291464 | tf_op jit(solution)/shard_map/ppermute | solution.py:1392
  509.1 3.0 copy-start.12
  514.2 39.0 %slice-start.4 = ((s8[6291456]{0:T(1024)(128)(4,1)}), s8[4194304]{0:T(1024)(128)(4,1)S(1)}, s32[]{:S(2)}) async-start(s8[6291456]{0:T(1024)(128)(4,1)} %bitcast.149), calls=%async_computation.7 | async-start | bytes 8388608
  523.7 29.6 %slice-start.5 = ((s8[6291456]{0:T(1024)(128)(4,1)}), s8[2097152]{0:T(1024)(128)(4,1)S(1)}, s32[]{:S(2)}) async-start(s8[6291456]{0:T(1024)(128)(4,1)} %bitcast.149), calls=%async_computation.8 | async-start | bytes 4194304
  523.7 29.6 %copy-start.9 = (bf16[8,1,64,1536]{3,2,1,0:T(8,128)(2,1)S(1)}, bf16[8,1,64,1536]{3,2,1,0:T(8,128)(2,1)}, u32[]{:S(2)}) copy-start(bf16[8,1,64,1536]{3,2,1,0:T(8,128)(2,1)} %get-tuple-element.211) | copy-start | bytes 4718596
  606.0 8.9 %copy-start.2 = (bf16[1536,1024]{1,0:T(8,128)(2,1)S(1)}, bf16[1536,1024]{1,0:T(8,128)(2,1)}, u32[]{:S(2)}) copy-start(bf16[1536,1024]{1,0:T(8,128)(2,1)} %get-tuple-element.119) | copy-start | bytes 9437188
  606.0 8.9 %copy-start.14 = (bf16[1536,128]{1,0:T(8,128)(2,1)S(1)}, bf16[1536,128]{1,0:T(8,128)(2,1)}, u32[]{:S(2)}) copy-start(bf16[1536,128]{1,0:T(8,128)(2,1)} %get-tuple-element.118) | copy-start | bytes 1179652
  614.9 79.1 %collective-permute-start.15 = (bf16[2,256,2048]{2,1,0:T(8,128)(2,1)}, bf16[2,256,2048]{2,1,0:T(8,128)(2,1)}, u32[]{:S(2)}, u32[]{:S(2)}) collective-permute-start(bf16[2,256,2048]{2,1,0:T(8,128)(2,1)} %get-tuple-element.112.refs_9_), channel_id=1, source_target_pairs={{0,4},{2,6},{4,0},{6,2},{8,12},{10,14},{12,8},{14,10},{16,20},{18,... | collective-permute-start | bytes 6291464 | tf_op jit(solution)/shard_map/ppermute | solution.py:1395
  676.7 11.6 %copy-start.1 = (bf16[1536,512]{1,0:T(8,128)(2,1)S(1)}, bf16[1536,512]{1,0:T(8,128)(2,1)}, u32[]{:S(2)}) copy-start(bf16[1536,512]{1,0:T(8,128)(2,1)} %token_pull.2.refs_6_) | copy-start | bytes 4718596
  688.3 94.3 %collective-permute-start.14 = (bf16[1536,512]{1,0:T(8,128)(2,1)S(1)}, bf16[1536,512]{1,0:T(8,128)(2,1)}, u32[]{:S(2)}, u32[]{:S(2)}) collective-permute-start(bf16[1536,512]{1,0:T(8,128)(2,1)S(1)} %copy-done.1), channel_id=1, source_target_pairs={{0,1},{1,0},{2,3},{3,2},{4,5},{5,4},{6,7},{7,6},{8,9},{9,8},{10,11... | collective-permute-start | bytes 4718600 | tf_op jit(solution)/shard_map/ppermute | solution.py:1392
Sparse Core Ops, SparseCore 0:
  95.3 37.9 all-gather.3
  135.5 49.4 all-gather.5
  187.2 49.2 all-gather.7

commit v10 on v9

--- a/solution.py
+++ b/solution.py
@@ -494,14 +494,24 @@
     return jnp.where((lane & 32) == 0, pltpu.roll(block, 96, 1), pltpu.roll(block, 32, 1))
 
 
-def qkv_kernel(x_ref, w_ref, b_ref, cos_ref, sin_ref, out_ref):
+def qkv_kernel(slots, place_ref, *refs):
+    x_refs, (w_ref, b_ref, cos_ref, sin_ref, out_ref) = refs[:slots], refs[slots:]
     which = pl.program_id(0)
     bias = b_ref[pl.ds(QKV_BIAS + which, 1), :]
+    depth = x_refs[0].shape[1]
+
+    def mixed_rows(at):
+        total = bias
+        for k, x_ref in enumerate(x_refs):
+            place = (place_ref[0] + slots - k) % slots
+            rows = pl.ds(pl.multiple_of(place * depth, depth), depth)
+            total = total + mm(x_ref[at, :], w_ref[0, rows, :])
+        return total
 
     @pl.when(which < 2)
     def _():
-        for at in parts_of(x_ref.shape[0]):
-            mixed = mm(x_ref[at, :], w_ref[0]) + bias
+        for at in parts_of(out_ref.shape[1]):
+            mixed = mixed_rows(at)
             for first in range(0, mixed.shape[1], 128):
                 block = mixed[:, first : first + 128]
                 turned = block * cos_ref[at, :] + swap_halves(block) * sin_ref[at, :]
@@ -509,22 +519,23 @@
 
     @pl.when(which == 2)
     def _():
-        for at in parts_of(x_ref.shape[0]):
-            out_ref[0, at, :] = (mm(x_ref[at, :], w_ref[0]) + bias).astype(BF16)
-
-
-def project_qkv(x, weight, bias, cosine, sine, after=()):
-    n, D = x.shape
-    width = weight.shape[2]
+        for at in parts_of(out_ref.shape[1]):
+            out_ref[0, at, :] = mixed_rows(at).astype(BF16)
+
+
+def project_qkv(c, x_slots, weight, bias, cosine, sine, after=()):
+    n = x_slots[0].shape[0]
+    _, D, width = weight.shape
     return call(
-        qkv_kernel, "project_qkv", (3,),
-        [
-            held((n, D)), pl.BlockSpec((1, D, width), lambda j: (j, 0, 0)), held(bias.shape),
+        functools.partial(qkv_kernel, len(x_slots)), "project_qkv", (3,),
+        [held(x.shape) for x in x_slots] + [
+            pl.BlockSpec((1, D, width), lambda j, p: (j, 0, 0)), held(bias.shape),
             held((n, 128)), held((n, 128)),
         ],
-        [pl.BlockSpec((1, n, width), lambda j: (j, 0, 0))],
+        [pl.BlockSpec((1, n, width), lambda j, p: (j, 0, 0))],
         [shaped(BF16, 3, n, width)],
-        (x, weight, bias, cosine, sine), 6 * n * D * width, after=after,
+        (c.reshape(1), *x_slots, weight, bias, cosine, sine), 6 * n * D * width, after=after,
+        prefetch=1,
     )[0]
 
 
@@ -902,25 +913,6 @@
             body(place)
 
 
-def join_kernel(slots, place_ref, *refs):
-    out_ref = refs[-1]
-    width = refs[0].shape[1]
-    for k in range(slots):
-        at = pl.ds(pl.multiple_of((place_ref[0] + slots - k) % slots * width, width), width)
-        out_ref[:, at] = refs[k][...]
-
-
-def join(c, slots):
-    n, width = slots[0].shape
-    D = width * len(slots)
-    step = row_step(n)
-    return call(
-        functools.partial(join_kernel, len(slots)), "join", (n // step,),
-        [row_spec(step, width)] * len(slots),
-        [row_spec(step, D)], [shaped(BF16, n, D)], (c.reshape(1), *slots), 0, prefetch=1,
-    )[0]
-
-
 def assemble_kernel(place_ref, *refs):
     out_ref = refs[-1]
     slot = place_ref[1 + pl.program_id(0)]
@@ -959,11 +951,11 @@
     out_ref[...] = in_ref[...]
 
 
-def pass_on(array):
+def pass_on(array, after=()):
     spec = held(array.shape)
     return call(
         pass_on_kernel, "pass_on", (1,), [spec], [pl.BlockSpec(array.shape, lambda *_: (0,) * array.ndim)],
-        [shaped(array.dtype, *array.shape)], (array,), 0,
+        [shaped(array.dtype, *array.shape)], (array,), 0, after=after,
     )[0]
 
 
@@ -1437,15 +1429,15 @@
     doc_ends = jnp.cumsum(sizes, axis=1)
     begins = doc_ends - sizes
     cosine, sine, ext_k, ext_q, picks = prepare(n, Q, own_sizes, match_picks, begins, sizes)
-    wqkv_slots = [w_qkv]
-    for k in range(1, C):
-        if C == 2:
-            other = gather_rows(R, qkv_pieces[k - 1], 1)
-        else:
-            other = lax.all_gather(qkv_pieces[k - 1], "rows", axis=0, tiled=True)
-        wqkv_slots.append(other.reshape(w_qkv.shape))
-    x = join(c, token_slots)
-    behind, _ = lax.optimization_barrier(((w_proj, packed), x))
+    wqkv_slots = [w_qkv] + [
+        lax.all_gather(piece, "rows", axis=0, tiled=True).reshape(w_qkv.shape)
+        for piece in qkv_pieces
+    ]
+    x = jnp.concatenate(in_order(token_slots), axis=1)
+    flat = pass_on(
+        jnp.concatenate([piece.reshape(-1, D) for piece in late_pieces]), token_slots[1:]
+    )
+    behind, _ = lax.optimization_barrier(((w_proj, packed), flat))
     wproj = jnp.concatenate(
         in_order([w_proj] + [shift_cols(behind[0], k) for k in range(1, C)]), axis=0
     )
@@ -1475,10 +1467,8 @@
     qkv, attended, rests, exts = [], [], [], []
     for k in range(C):
         first = (lows, highs) if k == 0 else ()
-        qkv.append(project_qkv(x, wqkv_slots[k], packs[k], cosine, sine, first))
+        qkv.append(project_qkv(c, token_slots, wqkv_slots[k], packs[k], cosine, sine, first))
         if k == 0:
-            flat = jnp.concatenate([piece.reshape(-1, D) for piece in late_pieces])
-            flat, _ = lax.optimization_barrier((flat, x))
             arrived = [shift_cols(flat, j) for j in range(1, C)]
             arrived = [pass_on(a) for a in arrived]
             ends_of = [0]

time: 806 us -> 800 us (level)
  Pallas kernels: 639 us -> 599 us
  waiting for transfers between devices: 9.2 us -> 21.1 us
  other arithmetic: 13.5 us -> 22.1 us
    pallas_call x27 -> x26, Pallas kernels: 639 us -> 599 us  [call(): pl.pallas_call(wrapped, grid_spec=pltpu.PrefetchScalarGridSpec(num_scalar...]
    ppermute x11, waiting for transfers between devices: 8.46 us -> 20.7 us  [shift_cols(): return lax.ppermute(value, 'cols', [(i, (i + k) % C) for i in range(C)])]
  transfers between devices with their start and end apart: 19 -> 20, of which waited for: 4 -> 4; matrix products, arithmetic and copies ran while one was open for 12% -> 14% of each run, Pallas kernels for 63% -> 60%
where the time goes in v10:
time: 800 us; the launch traced here: 789 us
  Pallas kernels  599 us (75%)
  matrix products  58.3 us (7%)
  local copies, waits for them, and re-layouts  55.5 us (7%)
  other arithmetic  22.1 us (3%)
  waiting for transfers between devices  21.1 us (3%)
  starting transfers between devices  17.7 us (2%)
  between operations  15.5 us (2%)
    pallas_call x26, Pallas kernels, call(): pl.pallas_call(wrapped, grid_spec=pltpu.PrefetchScalarGridSpec(num_scalar...  599 us
    dot_general x9, matrix products, mm(): return lax.dot_general(left, right, dims, preferred_element_type=F32)  58.3 us
    ppermute x11, waiting for transfers between devices, shift_cols(): return lax.ppermute(value, 'cols', [(i, (i + k) % C) for i in range(C)])  20.7 us
  transfers between devices with their start and end apart: 20, of which 4 were waited for; matrix products, arithmetic and copies ran while one was open for 14% of the time, Pallas kernels for 60%

profile of v10, /device:TPU:0, one launch (start us, length us, event | category | flops | bytes accessed | tf_op | source)
XLA Modules:
  0.0 789.4 jit_solution(3845945076031816123)
XLA Ops:
  8.2 3.0 collective-permute-start.3
  11.2 4.9 collective-permute-done.3
  16.9 1.3 slice.162
  18.2 1.7 slice.163
  20.0 1.3 fusion.1
  21.3 1.7 collective-permute-start
  27.5 2.5 copy.72.refs_1_
  31.4 9.2 %prepare.1 = (f32[1536,128]{1,0:T(8,128)}, f32[1536,128]{1,0:T(8,128)}, bf16[1536,128]{1,0:T(8,128)(2,1)}, bf16[1536,128]{1,0:T(8,128)(2,1)}, s32[16,4,1024]{2,1,0:T(4,128)}) custom-call(s32[4]{0:T(128)} %fusion.4.refs_0_, s32[32,64,32]{2,1,0:T(8,128)} %copy.72.refs_1_, s32[64,2]{1,0:T(8,128)} %copy.73.refs_2_), custom_call_target="tpu_custom_call" | custom-call | bytes 1024 | tf_op jit(solution)/shard_map/prepare/pallas_call | solution.py:60
  43.3 13.9 %collective-permute-done.refs_1_.refs_2_ = bf16[1536,512]{1,0:T(8,128)(2,1)} collective-permute-done((bf16[1536,512]{1,0:T(8,128)(2,1)}, bf16[1536,512]{1,0:T(8,128)(2,1)}, u32[]{:S(2)}, u32[]{:S(2)}) %collective-permute-start) | collective-permute-done | bytes 1572896 | tf_op jit(solution)/shard_map/ppermute | solution.py:1384
  57.2 1.9 pass_on.2.refs_9_
  59.1 1.4 collective-permute-start.2
  60.5 2.2 broadcast_select_fusion.1
  62.7 9.9 %project_qkv.2.refs_1_ = bf16[3,1536,512]{2,1,0:T(8,128)(2,1)} custom-call(s32[1]{0:T(128)} %bitcast.19.refs_0_, bf16[1536,512]{1,0:T(8,128)(2,1)} %get-tuple-element.210.refs_1_, bf16[1536,512]{1,0:T(8,128)(2,1)} %collective-permute-done.refs_1_.refs_2_, bf16[3,1024,512]{2,1,0:T(8,128)(2,1)} %refs_4_.5, f32[16,512]{1,0:T(8,128)} %pad.8.refs_4_.refs_2_, ...), custom_call_target="tpu_custom_call" | custom-call | flops 4831838208 | bytes 12615684 | tf_op jit(solution)/shard_map/project_qkv/pallas_call | solution.py:60
  73.8 1.9 pass_on.3.refs_4_
  75.7 1.5 slice.203
  77.3 1.8 fusion.15
  82.7 1.6 collective-permute-start.1
  84.7 1.6 broadcast_select_fusion
  86.3 4.1 fusion.11
  91.9 32.9 %attention_forward.2 = (bf16[1536,512]{1,0:T(8,128)(2,1)}, bf16[1536,512]{1,0:T(8,128)(2,1)}, bf16[1536,512]{1,0:T(8,128)(2,1)}) custom-call(s32[12]{0:T(128)} %pad_add_fusion.1.refs_0_, bf16[3,1536,512]{2,1,0:T(8,128)(2,1)} %project_qkv.2.refs_1_, bf16[1536,128]{1,0:T(8,128)(2,1)} %get-tuple-element.73.refs_2_.refs_6_, ...), custom_call_target="tpu_custom_call" | custom-call | bytes 1024 | tf_op jit(solution)/shard_map/attention_forward/pallas_call | solution.py:60
  124.7 10.0 %project_qkv.3.refs_1_.refs_4_ = bf16[3,1536,512]{2,1,0:T(8,128)(2,1)} custom-call(s32[1]{0:T(128)} %bitcast.19.refs_0_, bf16[1536,512]{1,0:T(8,128)(2,1)} %get-tuple-element.210.refs_1_, bf16[1536,512]{1,0:T(8,128)(2,1)} %collective-permute-done.refs_1_.refs_2_, bf16[3,1024,512]{2,1,0:T(8,128)(2,1)} %bitcast.144, f32[16,512]{1,0:T(8,128)} %copy-done.17, ...), custom_call_target="tpu_custom_call" | custom-call | flops 4831838208 | bytes 12615684 | tf_op jit(solution)/shard_map/project_qkv/pallas_call | solution.py:60
  134.7 33.2 %attention_forward.3 = (bf16[1536,512]{1,0:T(8,128)(2,1)}, bf16[1536,512]{1,0:T(8,128)(2,1)}, bf16[1536,512]{1,0:T(8,128)(2,1)}) custom-call(s32[12]{0:T(128)} %pad_add_fusion.1.refs_0_, bf16[3,1536,512]{2,1,0:T(8,128)(2,1)} %project_qkv.3.refs_1_.refs_4_, bf16[1536,128]{1,0:T(8,128)(2,1)} %get-tuple-element.73.refs_2_.refs_6_, ...), custom_call_target="tpu_custom_call" | custom-call | bytes 1024 | tf_op jit(solution)/shard_map/attention_forward/pallas_call | solution.py:60
  168.0 11.3 %out_and_norm.1 = (f32[1536,1024]{1,0:T(8,128)}, f32[1536,1]{1,0:T(8,128)}, bf16[1536,1024]{1,0:T(8,128)(2,1)}, bf16[1024,1536]{1,0:T(8,128)(2,1)}) custom-call(bf16[1536,1024]{1,0:T(8,128)(2,1)} %get-tuple-element.212.refs_0_, f32[8,1024]{1,0:T(8,128)} %pad_maximum_fusion.5.refs_1_.refs_6_.refs_3_, ...), custom_call_target="tpu_custom_call" | custom-call | flops 3221225472 | bytes 21010432 | tf_op jit(solution)/shard_map/out_and_norm/pallas_call | solution.py:60
  179.2 22.7 %up_and_gelu.2 = (bf16[1536,2048]{1,0:T(8,128)(2,1)}, f32[1536,2048]{1,0:T(8,128)}) custom-call(bf16[1536,1024]{1,0:T(8,128)(2,1)} %get-tuple-element.79.refs_0_, bf16[1024,2048]{1,0:T(8,128)(2,1)} %refs_6_.1, f32[16,512]{1,0:T(8,128)} %pad.8.refs_4_.refs_2_, f32[1536,1]{1,0:T(8,128)} %get-tuple-element.80.refs_3_.refs_2_), custom_call_target="tpu_custom_call" | custom-call | flops 16106127360 | bytes 26247168 | tf_op jit(solution)/shard_map/up_and_gelu/pallas_call | solution.py:60
  202.0 22.6 %up_and_gelu.3 = (bf16[1536,2048]{1,0:T(8,128)(2,1)}, f32[1536,2048]{1,0:T(8,128)}) custom-call(bf16[1536,1024]{1,0:T(8,128)(2,1)} %get-tuple-element.79.refs_0_, bf16[1024,2048]{1,0:T(8,128)(2,1)} %all-gather.9.cloned.1.call-done.refs_1_.refs_7_, f32[16,512]{1,0:T(8,128)} %copy-done.17, bf16[1536,2048]{1,0:T(8,128)(2,1)} %get-tuple-element.81.refs_3_), custom_call_target="tpu_custom_call" | custom-call | flops 16106127360 | bytes 26247168 | tf_op jit(solution)/shard_map/up_and_gelu/pallas_call | solution.py:60
  224.5 24.8 %down_and_norm.1 = (f32[1536,1024]{1,0:T(8,128)}, f32[1536,1]{1,0:T(8,128)}, bf16[1536,1024]{1,0:T(8,128)(2,1)}, f32[1536,128]{1,0:T(8,128)}, bf16[1536,128]{1,0:T(8,128)(2,1)}, /*index=5*/f32[1536,1]{1,0:T(8,128)}) custom-call(f32[1536,1024]{1,0:T(8,128)} %get-tuple-element.77.refs_0_.refs_1_, f32[8,1024]{1,0:T(8,128)} %pad_maximum_fusion.5.refs_1_.refs_6_.refs_3_, ...), custom_call_target="tpu_custom_call" | custom-call | flops 12884901888 | bytes 38187008 | tf_op jit(solution)/shard_map/down_and_norm/pallas_call | solution.py:60
  250.6 1.7 slice.169.refs_0_
  252.3 33.5 %gather_rows.1.refs_5_ = bf16[16,1024,128]{2,1,0:T(8,128)(2,1)} custom-call(bf16[1024,128]{1,0:T(8,128)(2,1)} %slice.169.refs_0_, f32[1536,1]{1,0:T(8,128)} %get-tuple-element.84.refs_1_.refs_5_), custom_call_target="tpu_custom_call" | custom-call | bytes 1024 | tf_op jit(solution)/shard_map/gather_rows/pallas_call | solution.py:60
  287.4 34.3 %score_forward.1.refs_6_ = f32[64,32]{1,0:T(8,128)} custom-call(s32[512]{0:T(512)} %reshape.234.refs_7_.refs_0_, s32[512]{0:T(512)} %sub.97.refs_8_.refs_1_, bf16[16384,128]{1,0:T(8,128)(2,1)} %bitcast.153, bf16[1024,128]{1,0:T(8,128)(2,1)} %pad_maximum_fusion.4.refs_3_, s32[16,4,1024]{2,1,0:T(4,128)} %get-tuple-element.69.refs_2_.refs_4_, ...), custom_call_target="tpu_custom_call" | custom-call | flops 4294967296 | bytes 4730880 | tf_op jit(solution)/shard_map/score_forward/pallas_call | solution.py:60
  323.3 2.4 collective-permute-start.6
  325.7 1.6 collective-permute-done.6
  327.9 1.4 subtract_multiply_fusion.refs_5_
  329.3 34.5 %score_backward.1 = (f32[16384,128]{1,0:T(8,128)}, f32[128,1024]{1,0:T(8,128)}) custom-call(s32[512]{0:T(512)} %reshape.234.refs_7_.refs_0_, s32[512]{0:T(512)} %sub.97.refs_8_.refs_1_, bf16[16384,128]{1,0:T(8,128)(2,1)} %bitcast.154, bf16[1024,128]{1,0:T(8,128)(2,1)} %pad_maximum_fusion.4.refs_3_, s32[16,4,1024]{2,1,0:T(4,128)} %get-tuple-element.69.refs_2_.refs_4_, ...), custom_call_target="tpu_custom_call" | custom-call | flops 8589934592 | bytes 13643776 | tf_op jit(solution)/shard_map/score_backward/pallas_call | solution.py:60
  363.7 2.0 copy.78
  366.8 2.4 collective-permute-start.7
  369.1 3.8 constant_dynamic-slice_fusion.2
  373.0 35.0 %scatter_rows.1.refs_7_ = f32[1024,128]{1,0:T(8,128)} custom-call(f32[16,1024,128]{2,1,0:T(8,128)} %bitcast.149, f32[128,1024]{1,0:T(8,128)} %get-tuple-element.85.refs_1_), custom_call_target="tpu_custom_call" | custom-call | bytes 1024 | tf_op jit(solution)/shard_map/scatter_rows/pallas_call | solution.py:60
  408.0 2.0 pad_maximum_fusion.1.refs_0_
  410.0 12.5 %head_pull.1 = (bf16[1536,128]{1,0:T(8,128)(2,1)}, f32[1536,1024]{1,0:T(8,128)}, bf16[1536,1024]{1,0:T(8,128)(2,1)}, bf16[1024,1536]{1,0:T(8,128)(2,1)}, f32[8,1024]{1,0:T(8,128)}) custom-call(f32[1536,128]{1,0:T(8,128)} %pad_maximum_fusion.1.refs_0_, f32[1536,128]{1,0:T(8,128)} %get-tuple-element.87.refs_1_, f32[1536,1]{1,0:T(8,128)} %get-tuple-element.88.refs_2_, ...), custom_call_target="tpu_custom_call" | custom-call | flops 805306368 | bytes 21180416 | tf_op jit(solution)/shard_map/head_pull/pallas_call | solution.py:60
  422.5 3.5 constant_dynamic-slice_fusion.4
  426.0 6.5 convolution_convert_fusion.3.refs_4_
  432.7 4.6 convolution_convert_fusion.2.refs_5_
  437.8 13.6 %up_pull.2 = (bf16[1536,2048]{1,0:T(8,128)(2,1)}, f32[8,2048]{1,0:T(8,128)}) custom-call(bf16[1536,1024]{1,0:T(8,128)(2,1)} %get-tuple-element.91.refs_0_, bf16[2048,1024]{1,0:T(8,128)(2,1)} %all-gather.11.cloned.1.call-done.refs_6_.refs_1_, f32[1536,2048]{1,0:T(8,128)} %get-tuple-element.93.refs_2_, f32[8,1024]{1,0:T(8,128)} %get-tuple-element.94.refs_3_, ...), custom_call_target="tpu_custom_call" | custom-call | flops 6442450944 | bytes 26279936 | tf_op jit(solution)/shard_map/up_pull/pallas_call | solution.py:60
  451.3 6.8 convolution_convert_fusion.1.refs_11_
  458.3 8.3 %add_convert_fusion.1.refs_4_ = bf16[512,2048]{1,0:T(8,128)(2,1)} fusion(bf16[512,2048]{1,0:T(8,128)(2,1)} %collective-permute-done.8, bf16[512,1536]{1,0:T(8,128)(2,1)S(1)} %bitcast.165, bf16[1536,2048]{1,0:T(8,128)(2,1)} %get-tuple-element.82.refs_4_.refs_7_), kind=kOutput, calls=%fused_computation.3 | convolution fusion | flops 3224371200 | bytes 12058624 | tf_op jit(solution)/shard_map/dot_general | solution.py:23
  466.8 13.8 %up_pull.3 = (bf16[1536,2048]{1,0:T(8,128)(2,1)}, f32[8,2048]{1,0:T(8,128)}) custom-call(bf16[1536,1024]{1,0:T(8,128)(2,1)} %get-tuple-element.91.refs_0_, bf16[2048,1024]{1,0:T(8,128)(2,1)} %refs_1_.4, f32[1536,2048]{1,0:T(8,128)} %get-tuple-element.92.refs_2_, f32[8,2048]{1,0:T(8,128)} %get-tuple-element.96.refs_3_, ...), custom_call_target="tpu_custom_call" | custom-call | flops 6442450944 | bytes 26279936 | tf_op jit(solution)/shard_map/up_pull/pallas_call | solution.py:60
  480.6 8.2 %convolution_convert_fusion.refs_12_ = bf16[512,2048]{1,0:T(8,128)(2,1)} fusion(bf16[512,1536]{1,0:T(8,128)(2,1)} %bitcast.167, bf16[1536,2048]{1,0:T(8,128)(2,1)} %get-tuple-element.97.refs_4_), kind=kOutput, calls=%fused_computation.9 | convolution fusion | flops 3222274048 | bytes 9961472 | tf_op jit(solution)/shard_map/dot_general | solution.py:23
  488.9 5.8 add_convert_fusion.refs_14_
  494.7 1.8 collective-permute-start.13
  497.1 3.0 copy.76
  502.2 9.3 %convert_add_fusion.1.refs_13_ = f32[512,2048]{1,0:T(8,128)} fusion(bf16[512,2048]{1,0:T(8,128)(2,1)} %collective-permute-done.9, bf16[512,1536]{1,0:T(8,128)(2,1)} %bitcast.164, bf16[1536,2048]{1,0:T(8,128)(2,1)} %get-tuple-element.81.refs_3_), kind=kOutput, calls=%fused_computation.2 | convolution fusion | flops 3223322624 | bytes 14155776 | tf_op jit(solution)/shard_map/dot_general | solution.py:23
  511.6 29.7 %hidden_pull.1 = (f32[1536,1024]{1,0:T(8,128)}, bf16[1024,1536]{1,0:T(8,128)(2,1)}, f32[8,1024]{1,0:T(8,128)}, bf16[1536,512]{1,0:T(8,128)(2,1)}, bf16[1536,512]{1,0:T(8,128)(2,1)}) custom-call(f32[1536,1024]{1,0:T(8,128)} %get-tuple-element.90.refs_0_, f32[1536,1024]{1,0:T(8,128)} %get-tuple-element.77.refs_0_.refs_1_, ...), custom_call_target="tpu_custom_call" | custom-call | bytes 1024 | tf_op jit(solution)/shard_map/hidden_pull/pallas_call | solution.py:60
  541.3 8.1 %convert_add_fusion.refs_10_ = f32[512,2048]{1,0:T(8,128)} fusion(bf16[512,2048]{1,0:T(8,128)(2,1)} %collective-permute-done.11, bf16[512,1536]{1,0:T(8,128)(2,1)S(1)} %bitcast.163, bf16[1536,2048]{1,0:T(8,128)(2,1)} %get-tuple-element.97.refs_4_), kind=kOutput, calls=%fused_computation | convolution fusion | flops 3223322624 | bytes 14155776 | tf_op jit(solution)/shard_map/dot_general | solution.py:23
  549.4 46.7 %attention_backward.2 = (bf16[3,1536,512]{2,1,0:T(8,128)(2,1)}, f32[8,512]{1,0:T(8,128)}) custom-call(s32[12]{0:T(128)} %pad_add_fusion.1.refs_0_, bf16[3,1536,512]{2,1,0:T(8,128)(2,1)} %project_qkv.3.refs_1_.refs_4_, bf16[1536,512]{1,0:T(8,128)(2,1)} %get-tuple-element.105.refs_2_, bf16[1536,512]{1,0:T(8,128)(2,1)} %get-tuple-element.76.refs_3_.refs_6_.refs_5_, ...), custom_call_target="tpu_custom_call" | custom-call | bytes 1024 | tf_op jit(solution)/shard_map/attention_backward/pallas_call | solution.py:60
  596.1 8.8 %fold.1 = (bf16[2,256,2048]{2,1,0:T(8,128)(2,1)}, f32[2,256,2048]{2,1,0:T(8,128)}) custom-call(s32[1]{0:T(128)} %bitcast.43.refs_0_, f32[1,512,2048]{2,1,0:T(8,128)} %bitcast.141, f32[1,512,2048]{2,1,0:T(8,128)} %bitcast.142, bf16[1,512,2048]{2,1,0:T(8,128)(2,1)} %bitcast.46.refs_3_, bf16[1,512,2048]{2,1,0:T(8,128)(2,1)} %bitcast.47.refs_4_, ...), custom_call_target="tpu_custom_call" | custom-call | bytes 1024 | tf_op jit(solution)/shard_map/fold/pallas_call | solution.py:60
  610.2 46.5 %attention_backward.3 = (bf16[3,1536,512]{2,1,0:T(8,128)(2,1)}, f32[8,512]{1,0:T(8,128)}) custom-call(s32[12]{0:T(128)} %pad_add_fusion.1.refs_0_, bf16[3,1536,512]{2,1,0:T(8,128)(2,1)} %project_qkv.2.refs_1_, bf16[1536,512]{1,0:T(8,128)(2,1)} %get-tuple-element.102.refs_2_, bf16[1536,512]{1,0:T(8,128)(2,1)} %get-tuple-element.75.refs_7_.refs_2_.refs_3_.refs_4_, ...), custom_call_target="tpu_custom_call" | custom-call | bytes 1024 | tf_op jit(solution)/shard_map/attention_backward/pallas_call | solution.py:60
  656.8 10.9 %token_pull.2.refs_6_ = bf16[1536,512]{1,0:T(8,128)(2,1)} custom-call(s32[1]{0:T(128)} %bitcast.48.refs_0_, f32[1536,1024]{1,0:T(8,128)} %get-tuple-element.101.refs_1_, bf16[3,1536,512]{2,1,0:T(8,128)(2,1)} %get-tuple-element.111.refs_2_, bf16[3,1536,512]{2,1,0:T(8,128)(2,1)} %get-tuple-element.112.refs_3_, bf16[3,1024,512]{2,1,0:T(8,128)(2,1)} %refs_4_.5, ...), custom_call_target="tpu_custom_call" | custom-call | bytes 1024 | tf_op jit(solution)/shard_map/token_pull/pallas_call | solution.py:60
  667.7 11.6 %token_pull.3.refs_9_.refs_1_ = f32[1536,512]{1,0:T(8,128)} custom-call(s32[1]{0:T(128)} %bitcast.19.refs_0_, f32[1536,1024]{1,0:T(8,128)} %get-tuple-element.101.refs_1_, bf16[3,1536,512]{2,1,0:T(8,128)(2,1)} %get-tuple-element.111.refs_2_, bf16[3,1536,512]{2,1,0:T(8,128)(2,1)} %get-tuple-element.112.refs_3_, bf16[3,1024,512]{2,1,0:T(8,128)(2,1)} %refs_4_.5, ...), custom_call_target="tpu_custom_call" | custom-call | bytes 1024 | tf_op jit(solution)/shard_map/token_pull/pallas_call | solution.py:60
  683.7 1.4 reshape.264.refs_8_
  685.0 79.3 %late_sums.1 = (f32[4,64,512]{2,1,0:T(8,128)}, f32[2,64,2048]{2,1,0:T(8,128)}, f32[8,640]{1,0:T(8,128)}) custom-call(bf16[8,2,64,1536]{3,2,1,0:T(8,128)(2,1)} %bitcast.155, bf16[8,2,64,1536]{3,2,1,0:T(8,128)(2,1)} %bitcast.194, bf16[3,1536,512]{2,1,0:T(8,128)(2,1)} %get-tuple-element.111.refs_2_, bf16[3,1536,512]{2,1,0:T(8,128)(2,1)} %get-tuple-element.112.refs_3_, ...), custom_call_target="tpu_custom_call" | custom-call | flops 99999997952 | bytes 27414528 | tf_op jit(solution)/shard_map/late_sums/pallas_call | solution.py:60
  768.3 1.8 slice.188
  770.7 1.6 slice_bitcast_fusion.2
  772.3 2.3 slice_bitcast_fusion
  774.5 8.0 %assemble.1 = f32[3072,512]{1,0:T(8,128)} custom-call(s32[7]{0:T(128)} %pad_add_fusion.2.refs_0_, f32[1536,512]{1,0:T(8,128)} %token_pull.3.refs_9_.refs_1_, bf16[1536,512]{1,0:T(8,128)(2,1)} %collective-permute-done.14.refs_2_, f32[8,640]{1,0:T(8,128)} %get-tuple-element.118.refs_3_), custom_call_target="tpu_custom_call" | custom-call | bytes 1024 | tf_op jit(solution)/shard_map/assemble/pallas_call | solution.py:60
  (203 shorter events, 40.2 us)
Async XLA Ops:
  7.2 117.5 %all-gather.5.cloned.1.call-start = ((), (), s32[]{:S(2)}) async-start(), calls=%async_computation | async-start | bytes 3342336 | tf_op jit(solution)/shard_map/all_gather | solution.py:1433
  8.2 7.9 %collective-permute-start.3 = (bf16[192,512]{1,0:T(8,128)(2,1)S(1)}, bf16[192,512]{1,0:T(8,128)(2,1)S(1)}, u32[]{:S(2)}, u32[]{:S(2)}) collective-permute-start(bf16[192,512]{1,0:T(8,128)(2,1)S(1)} %dynamic-slice_bitcast_fusion.2), channel_id=1, source_target_pairs={{0,1},{1,0},{2,3},{3,2},{4,5},{5,4},{6,7},{7,6},{8,9},{9,8},{10,11... | collective-permute-start | bytes 589832 | tf_op jit(solution)/shard_map/ppermute | solution.py:1384
  16.1 0.7 copy-start.13
  16.8 151.1 %all-gather.7.cloned.1.call-start = ((), (), s32[]{:S(2)}) async-start(), calls=%async_computation.1 | async-start | bytes 1114112 | tf_op jit(solution)/shard_map/all_gather | solution.py:1406
  19.9 3.1 copy-start.16
  19.9 5.0 copy-start.19
  20.0 10.7 %copy-start.18 = (f32[3,512]{1,0:T(4,128)S(1)}, f32[3,512]{1,0:T(4,128)}, u32[]{:S(2)}) copy-start(f32[3,512]{1,0:T(4,128)} %param.24) | copy-start | bytes 18436
  20.0 10.7 %copy-start.21 = (f32[512]{0:T(512)S(1)}, f32[512]{0:T(512)}, u32[]{:S(2)}) copy-start(f32[512]{0:T(512)} %param.26) | copy-start | bytes 6148
  20.0 10.6 %copy-start.22 = (f32[512]{0:T(512)S(1)}, f32[512]{0:T(512)}, u32[]{:S(2)}) copy-start(f32[512]{0:T(512)} %param.27) | copy-start | bytes 6148
  20.0 10.6 %copy-start.23 = (f32[512]{0:T(512)S(1)}, f32[512]{0:T(512)}, u32[]{:S(2)}) copy-start(f32[512]{0:T(512)} %param.28) | copy-start | bytes 6148
  20.0 10.6 %copy-start.24 = (f32[512]{0:T(512)S(1)}, f32[512]{0:T(512)}, u32[]{:S(2)}) copy-start(f32[512]{0:T(512)} %param.32) | copy-start | bytes 6148
  20.0 10.6 %copy-start.25 = (f32[512]{0:T(512)S(1)}, f32[512]{0:T(512)}, u32[]{:S(2)}) copy-start(f32[512]{0:T(512)} %param.33) | copy-start | bytes 6148
  20.0 10.6 %copy-start.26 = (f32[512]{0:T(512)S(1)}, f32[512]{0:T(512)}, u32[]{:S(2)}) copy-start(f32[512]{0:T(512)} %param.34) | copy-start | bytes 6148
  21.3 35.9 %collective-permute-start = (bf16[1536,512]{1,0:T(8,128)(2,1)}, bf16[1536,512]{1,0:T(8,128)(2,1)}, u32[]{:S(2)}, u32[]{:S(2)}) collective-permute-start(bf16[1536,512]{1,0:T(8,128)(2,1)} %fusion.1), channel_id=1, source_target_pairs={{0,1},{1,0},{2,3},{3,2},{4,5},{5,4},{6,7},{7,6},{8,9},{9,8},{10,11... | collective-permute-start | bytes 4718600 | tf_op jit(solution)/shard_map/ppermute | solution.py:1384
  27.5 15.0 %copy-start.9 = (bf16[128,1024]{1,0:T(8,128)(2,1)S(1)}, bf16[128,1024]{1,0:T(8,128)(2,1)}, u32[]{:S(2)}) copy-start(bf16[128,1024]{1,0:T(8,128)(2,1)} %reshape.240) | copy-start | bytes 786436
  59.1 13.9 %collective-permute-start.2 = (bf16[288,1024]{1,0:T(8,128)(2,1)}, bf16[288,1024]{1,0:T(8,128)(2,1)S(1)}, u32[]{:S(2)}, u32[]{:S(2)}) collective-permute-start(bf16[288,1024]{1,0:T(8,128)(2,1)} %pass_on.2.refs_9_), channel_id=1, source_target_pairs={{0,1},{1,0},{2,3},{3,2},{4,5},{5,4},{6,7},{7,6},{8,9},{9,8},{10,11... | collective-permute-start | bytes 1769480 | tf_op jit(solution)/shard_map/ppermute | solution.py:1384
  72.6 8.6 %copy-start.20 = (s32[4]{0:T(128)S(1)}, s32[4]{0:T(128)}, u32[]{:S(2)}) copy-start(s32[4]{0:T(128)} %fusion.4.refs_0_) | copy-start | bytes 52
  72.6 9.6 %copy-start.28 = (s32[6]{0:T(128)S(1)}, s32[6]{0:T(128)}, u32[]{:S(2)}) copy-start(s32[6]{0:T(128)} %constant.238) | copy-start | bytes 76
  72.6 10.1 %copy-start.15 = (f32[16,512]{1,0:T(8,128)S(1)}, f32[16,512]{1,0:T(8,128)}, u32[]{:S(2)}) copy-start(f32[16,512]{1,0:T(8,128)} %pad.8.refs_4_.refs_2_) | copy-start | bytes 98308
  72.6 11.8 %copy-start.14 = (bf16[512,128]{1,0:T(8,128)(2,1)S(1)}, bf16[512,128]{1,0:T(8,128)(2,1)}, u32[]{:S(2)}) copy-start(bf16[512,128]{1,0:T(8,128)(2,1)} %param.35) | copy-start | bytes 393220
  72.6 12.2 %copy-start.1 = (bf16[1536,512]{1,0:T(8,128)(2,1)S(1)}, bf16[1536,512]{1,0:T(8,128)(2,1)}, u32[]{:S(2)}) copy-start(bf16[1536,512]{1,0:T(8,128)(2,1)} %get-tuple-element.210.refs_1_) | copy-start | bytes 4718596
  73.0 0.8 copy-start.11
  77.2 124.8 %all-gather.9.cloned.1.call-start = ((), (), s32[]{:S(2)}) async-start(), calls=%async_computation.2 | async-start | bytes 4456448 | tf_op jit(solution)/shard_map/all_gather | solution.py:1406
  79.9 144.7 %all-gather.11.cloned.1.call-start = ((), (), s32[]{:S(2)}) async-start(), calls=%async_computation.3 | async-start | bytes 4456448 | tf_op jit(solution)/shard_map/all_gather | solution.py:1406
  82.7 7.8 collective-permute-start.1
  84.3 6.8 collective-permute-start.4
  90.5 34.2 %copy-start.17 = (f32[16,512]{1,0:T(8,128)}, f32[16,512]{1,0:T(8,128)S(1)}, u32[]{:S(2)}) copy-start(f32[16,512]{1,0:T(8,128)S(1)} %collective-permute-done.1.refs_4_.refs_2_) | copy-start | bytes 98308
  224.5 26.1 %copy-start.27 = (s32[32]{0:T(128)S(1)}, s32[32]{0:T(128)}, u32[]{:S(2)}) copy-start(s32[32]{0:T(128)} %param.22) | copy-start | bytes 388
  250.3 35.5 %collective-permute-start.5 = (bf16[512,128]{1,0:T(8,128)(2,1)S(1)}, bf16[512,128]{1,0:T(8,128)(2,1)S(1)}, u32[]{:S(2)}, u32[]{:S(2)}) collective-permute-start(bf16[512,128]{1,0:T(8,128)(2,1)S(1)} %slice.170), channel_id=1, source_target_pairs={{0,1},{1,0},{2,3},{3,2},{4,5},{5,4},{6,7},{7,6},{8,9},{9,8},{10,11... | collective-permute-start | bytes 393224 | tf_op jit(solution)/shard_map/ppermute | solution.py:1384
  323.3 4.0 collective-permute-start.6
  366.8 41.2 %collective-permute-start.7 = (f32[512,128]{1,0:T(8,128)S(1)}, f32[512,128]{1,0:T(8,128)S(1)}, u32[]{:S(2)}, u32[]{:S(2)}) collective-permute-start(f32[512,128]{1,0:T(8,128)S(1)} %dynamic-slice_bitcast_fusion), channel_id=1, source_target_pairs={{0,1},{1,0},{2,3},{3,2},{4,5},{5,4},{6,7},{7,6},{8,9},{9,8},{10,11... | collective-permute-start | bytes 786440 | tf_op jit(solution)/shard_map/ppermute | solution.py:1384
  373.0 35.0 %copy-start.5 = (f32[1024,128]{1,0:T(8,128)S(1)}, f32[1024,128]{1,0:T(8,128)}, u32[]{:S(2)}) copy-start(f32[1024,128]{1,0:T(8,128)} %copy.78) | copy-start | bytes 1572868
  422.5 10.2 %slice-start.2 = ((s8[6291456]{0:T(1024)(128)(4,1)}), s8[4194304]{0:T(1024)(128)(4,1)S(1)}, s32[]{:S(2)}) async-start(s8[6291456]{0:T(1024)(128)(4,1)} %bitcast.195), calls=%async_computation.6 | async-start | bytes 8388608
  426.0 6.7 slice-start.3
  432.5 4.8 copy-start.4
  432.6 25.7 %collective-permute-start.8 = (bf16[512,2048]{1,0:T(8,128)(2,1)S(1)}, bf16[512,2048]{1,0:T(8,128)(2,1)}, u32[]{:S(2)}, u32[]{:S(2)}) collective-permute-start(bf16[512,2048]{1,0:T(8,128)(2,1)S(1)} %convolution_convert_fusion.3.refs_4_), channel_id=1, source_target_pairs={{0,2},{2,0},{4,6},{6,4},{8,10},{10,8},{12,14},{14,12},{16,18},{18,... | collective-permute-start | bytes 6291464 | tf_op jit(solution)/shard_map/ppermute | solution.py:1387
  437.4 64.9 %collective-permute-start.9 = (bf16[512,2048]{1,0:T(8,128)(2,1)}, bf16[512,2048]{1,0:T(8,128)(2,1)}, u32[]{:S(2)}, u32[]{:S(2)}) collective-permute-start(bf16[512,2048]{1,0:T(8,128)(2,1)} %convolution_convert_fusion.2.refs_5_), channel_id=1, source_target_pairs={{0,2},{2,0},{4,6},{6,4},{8,10},{10,8},{12,14},{14,12},{16,18},{18,... | collective-permute-start | bytes 6291464 | tf_op jit(solution)/shard_map/ppermute | solution.py:1387
  451.3 7.0 copy-start.8
  458.1 8.5 %copy-start.3 = (bf16[512,2048]{1,0:T(8,128)(2,1)}, bf16[512,2048]{1,0:T(8,128)(2,1)S(1)}, u32[]{:S(2)}) copy-start(bf16[512,2048]{1,0:T(8,128)(2,1)S(1)} %convolution_convert_fusion.1.refs_11_) | copy-start | bytes 6291460
  458.1 30.7 %collective-permute-start.10 = (bf16[512,2048]{1,0:T(8,128)(2,1)S(1)}, bf16[512,2048]{1,0:T(8,128)(2,1)}, u32[]{:S(2)}, u32[]{:S(2)}) collective-permute-start(bf16[512,2048]{1,0:T(8,128)(2,1)S(1)} %convolution_convert_fusion.1.refs_11_), channel_id=1, source_target_pairs={{0,2},{2,0},{4,6},{6,4},{8,10},{10,8},{12,14},{14,12},{16,18},{18,... | collective-permute-start | bytes 6291464 | tf_op jit(solution)/shard_map/ppermute | solution.py:1387
  466.6 129.5 %collective-permute-start.12 = (bf16[512,2048]{1,0:T(8,128)(2,1)}, bf16[512,2048]{1,0:T(8,128)(2,1)}, u32[]{:S(2)}, u32[]{:S(2)}) collective-permute-start(bf16[512,2048]{1,0:T(8,128)(2,1)} %add_convert_fusion.1.refs_4_), channel_id=1, source_target_pairs={{0,1},{1,0},{2,3},{3,2},{4,5},{5,4},{6,7},{7,6},{8,9},{9,8},{10,11... | collective-permute-start | bytes 6291464 | tf_op jit(solution)/shard_map/ppermute | solution.py:1384
  466.8 22.0 %slice-start = ((s8[6291456]{0:T(1024)(128)(4,1)}), s8[2097152]{0:T(1024)(128)(4,1)S(1)}, s32[]{:S(2)}) async-start(s8[6291456]{0:T(1024)(128)(4,1)} %bitcast.150), calls=%async_computation.4 | async-start | bytes 4194304
  480.6 8.2 %slice-start.1 = ((s8[6291456]{0:T(1024)(128)(4,1)}), s8[4194304]{0:T(1024)(128)(4,1)S(1)}, s32[]{:S(2)}) async-start(s8[6291456]{0:T(1024)(128)(4,1)} %bitcast.150), calls=%async_computation.5 | async-start | bytes 8388608
  480.6 8.2 %copy-start.6 = (bf16[8,1,64,1536]{3,2,1,0:T(8,128)(2,1)S(1)}, bf16[8,1,64,1536]{3,2,1,0:T(8,128)(2,1)}, u32[]{:S(2)}) copy-start(bf16[8,1,64,1536]{3,2,1,0:T(8,128)(2,1)} %get-tuple-element.213) | copy-start | bytes 4718596
  488.8 52.4 %collective-permute-start.11 = (bf16[512,2048]{1,0:T(8,128)(2,1)}, bf16[512,2048]{1,0:T(8,128)(2,1)}, u32[]{:S(2)}, u32[]{:S(2)}) collective-permute-start(bf16[512,2048]{1,0:T(8,128)(2,1)} %convolution_convert_fusion.refs_12_), channel_id=1, source_target_pairs={{0,2},{2,0},{4,6},{6,4},{8,10},{10,8},{12,14},{14,12},{16,18},{18,... | collective-permute-start | bytes 6291464 | tf_op jit(solution)/shard_map/ppermute | solution.py:1387
  488.9 7.6 copy-start.29
  494.7 101.3 %collective-permute-start.13 = (bf16[512,2048]{1,0:T(8,128)(2,1)}, bf16[512,2048]{1,0:T(8,128)(2,1)}, u32[]{:S(2)}, u32[]{:S(2)}) collective-permute-start(bf16[512,2048]{1,0:T(8,128)(2,1)} %add_convert_fusion.refs_14_), channel_id=1, source_target_pairs={{0,1},{1,0},{2,3},{3,2},{4,5},{5,4},{6,7},{7,6},{8,9},{9,8},{10,11... | collective-permute-start | bytes 6291464 | tf_op jit(solution)/shard_map/ppermute | solution.py:1384
  497.1 3.0 copy-start.10
  511.6 29.7 %copy-start.7 = (bf16[8,1,64,1536]{3,2,1,0:T(8,128)(2,1)S(1)}, bf16[8,1,64,1536]{3,2,1,0:T(8,128)(2,1)}, u32[]{:S(2)}) copy-start(bf16[8,1,64,1536]{3,2,1,0:T(8,128)(2,1)} %get-tuple-element.213) | copy-start | bytes 4718596
  596.1 10.0 %copy-start.2 = (bf16[1536,1024]{1,0:T(8,128)(2,1)S(1)}, bf16[1536,1024]{1,0:T(8,128)(2,1)}, u32[]{:S(2)}) copy-start(bf16[1536,1024]{1,0:T(8,128)(2,1)} %get-tuple-element.117) | copy-start | bytes 9437188
  596.1 10.0 %copy-start.12 = (bf16[1536,128]{1,0:T(8,128)(2,1)S(1)}, bf16[1536,128]{1,0:T(8,128)(2,1)}, u32[]{:S(2)}) copy-start(bf16[1536,128]{1,0:T(8,128)(2,1)} %get-tuple-element.116) | copy-start | bytes 1179652
  604.9 80.1 %collective-permute-start.15 = (bf16[2,256,2048]{2,1,0:T(8,128)(2,1)}, bf16[2,256,2048]{2,1,0:T(8,128)(2,1)}, u32[]{:S(2)}, u32[]{:S(2)}) collective-permute-start(bf16[2,256,2048]{2,1,0:T(8,128)(2,1)} %get-tuple-element.110.refs_9_), channel_id=1, source_target_pairs={{0,4},{2,6},{4,0},{6,2},{8,12},{10,14},{12,8},{14,10},{16,20},{18,... | collective-permute-start | bytes 6291464 | tf_op jit(solution)/shard_map/ppermute | solution.py:1387
  667.7 11.6 %copy-start = (bf16[1536,512]{1,0:T(8,128)(2,1)S(1)}, bf16[1536,512]{1,0:T(8,128)(2,1)}, u32[]{:S(2)}) copy-start(bf16[1536,512]{1,0:T(8,128)(2,1)} %token_pull.2.refs_6_) | copy-start | bytes 4718596
  679.4 95.1 %collective-permute-start.14 = (bf16[1536,512]{1,0:T(8,128)(2,1)S(1)}, bf16[1536,512]{1,0:T(8,128)(2,1)}, u32[]{:S(2)}, u32[]{:S(2)}) collective-permute-start(bf16[1536,512]{1,0:T(8,128)(2,1)S(1)} %copy-done), channel_id=1, source_target_pairs={{0,1},{1,0},{2,3},{3,2},{4,5},{5,4},{6,7},{7,6},{8,9},{9,8},{10,11... | collective-permute-start | bytes 4718600 | tf_op jit(solution)/shard_map/ppermute | solution.py:1384
Sparse Core Ops, SparseCore 0:
  16.9 46.8 all-gather.4
  77.3 39.2 all-gather.6
  118.8 49.8 all-gather.8
  170.7 49.2 all-gather.10
